TPU v7x, 32 devices: a whole 2x2x4 slice. The times are simulated.
32 devices in a mesh: groups: 2 (over x), shell: 16 (over z, y, core).
Axes of the slice: x: 2, y: 2, z: 4, core: 2. Of those that a mesh axis runs over, the one named last changes fastest.
Arguments:
- panels: bfloat16 [256, 32, 256], P(('groups', 'shell')), parts along dimension 0, may hold values from -6 to 6
- block_pairs: int32 [256, 2], P(('groups', 'shell')), parts along dimension 0, may hold values from 0 to 255, as said below
- block_count: int32 [32], P(('groups', 'shell')), parts along dimension 0, may hold values from 1 to 8, 64 in all
- shell_size: int32 [512], P('groups'), parts along dimension 0, may hold values from 1 to 16, 2560 in all
- occ_coef: bfloat16 [5120, 256], P(('groups', 'shell')), parts along dimension 0, may hold values from -4 to 4
- vir_coef: bfloat16 [5120, 2304], P(('groups', 'shell')), parts along dimension 0, may hold values from -0.125 to 0.125
Outputs:
- mo_vectors: bfloat16 [64, 256, 2304], P(('groups', 'shell')), parts along dimension 0
There are 2 independent parts, one for each index of `groups`. A program takes and returns all parts, laid end to end along the dimension named above; each array names one. Nothing has to cross between parts.
Inputs may be any that keep to these rules, and one draw needn't show every extreme that they name: `block_pairs`: no (row, column) pair of shell blocks appears twice among the slots. `block_count`: the counts of all devices sum to 64. `shell_size`: the sizes sum to 2560.
All inputs are finite; a program needn't handle non-finite values.
Results may differ from a plain program's by a relative error of at most 0.0049.
Values may be sent and summed in bfloat16 or wider, within the bound.
No kernel may reach another device: no remote copies, remote signals or barrier semaphores. Data moves between devices by JAX's collectives and lax.ppermute only.
A program may use at most 192 MiB of HBM per device.

v0:
```python
import math

import jax
import jax.numpy as jnp
from jax import lax
from jax.sharding import PartitionSpec as P

EDGE = 16
NOCC = 256
BLK_DEV = 8


def padded_rows(matrix, starts, shell_size):
    offsets = jnp.arange(EDGE, dtype=jnp.int32)
    rows = jnp.minimum(starts[:, None] + offsets[None, :], matrix.shape[0] - 1)
    inside = offsets[None, :] < shell_size[:, None]
    return jnp.where(inside[:, :, None], matrix[rows], jnp.zeros((), matrix.dtype))


def half_transform(slot_rows, pairs, keep, occ_blocks):
    count = slot_rows.shape[0]
    vecs_here = slot_rows.shape[1]
    shells = occ_blocks.shape[0]
    group_size = math.gcd(512, count)
    turns = count // group_size
    shaped = slot_rows.reshape(count, vecs_here, EDGE, EDGE)

    def advance(total, turn):
        first = turn * group_size
        block = lax.dynamic_slice_in_dim(shaped, first, group_size, 0)
        okay = lax.dynamic_slice_in_dim(keep, first, group_size, 0)
        block = jnp.where(okay[:, None, None, None], block, jnp.zeros((), block.dtype))
        row_shell = lax.dynamic_slice_in_dim(pairs[:, 0], first, group_size, 0)
        col_shell = lax.dynamic_slice_in_dim(pairs[:, 1], first, group_size, 0)
        coefs = occ_blocks[row_shell]
        piece = jnp.einsum("kmi,kvmn->kvin", coefs, block, preferred_element_type=jnp.float32)
        return (total.at[col_shell].add(piece), None)

    start_total = jnp.zeros((shells, vecs_here, NOCC, EDGE), jnp.float32)
    half, _ = lax.scan(advance, start_total, jnp.arange(turns, dtype=jnp.int32))
    return half


def per_device(panels, block_pairs, block_count, shell_size, occ_coef, vir_coef):
    all_pairs, all_counts = (
        lax.all_gather(block_pairs, "shell", axis=0, tiled=True),
        lax.all_gather(block_count, "shell", axis=0, tiled=True),
    )
    turned = lax.all_to_all(panels, "shell", split_axis=1, concat_axis=0, tiled=True)
    occ_full = lax.all_gather(occ_coef, "shell", axis=0, tiled=True)
    starts = jnp.cumsum(shell_size) - shell_size
    occ_blocks = padded_rows(occ_full, starts, shell_size)
    slot_total = turned.shape[0]
    position = jnp.arange(slot_total, dtype=jnp.int32)
    live = position % BLK_DEV < all_counts[position // BLK_DEV]
    half = half_transform(turned, all_pairs, live, occ_blocks)
    hidden = half.astype(jnp.bfloat16)
    vir_full = lax.all_gather(vir_coef, "shell", axis=0, tiled=True)
    vir_blocks = padded_rows(vir_full, starts, shell_size)
    result = jnp.einsum("svin,sna->via", hidden, vir_blocks, preferred_element_type=jnp.float32)
    return result.astype(jnp.bfloat16)


def solution(mesh):
    placed = (
        P(("groups", "shell"), None, None),
        P(("groups", "shell"), None),
        P(("groups", "shell")),
        P("groups"),
        P(("groups", "shell"), None),
        P(("groups", "shell"), None),
    )
    return jax.shard_map(
        per_device,
        mesh=mesh,
        in_specs=placed,
        out_specs=P(("groups", "shell"), None, None),
        check_vma=False,
    )
```

profile of v0, /device:TPU:0, one launch (start us, length us, event | category | flops | bytes accessed | tf_op | source)
XLA Modules:
  0.0 216.0 jit_solution(16213081563214003796)
XLA Ops:
  6.5 0.0 all-gather.4.cloned.1.call-start
  6.5 0.7 all-gather.4.cloned.1.call-update
  7.3 0.0 all-gather.6.cloned.1.call-start
  7.3 0.7 all-gather.6.cloned.1.call-update
  8.7 1.6 copy.16
  10.3 1.3 dynamic-slice
  11.6 0.7 dynamic-update-slice
  12.3 7.4 %all-to-all-start = ((bf16[8,32,256]{2,0,1:T(8,128)(2,1)}), bf16[8,32,256]{2,0,1:T(8,128)(2,1)S(1)}, u32[]{:S(2)}, u32[]{:S(2)}) async-start(bf16[8,32,256]{2,0,1:T(8,128)(2,1)} %copy.16), calls=%async_computation | async-start | bytes 262144 | tf_op jit(solution)/shard_map/all_to_all | solution.py:49
  19.7 12.4 %all-reduce = s32[16]{0:T(128)S(1)} all-reduce(s32[16]{0:T(128)S(1)} %dynamic-update-slice), channel_id=1, replica_groups=mesh['groups'=2,'shell'=16] {'shell'}, use_global_device_ids=true, to_apply=%add | all-reduce | flops 16 | bytes 128
  32.1 1.0 reduce-window.9
  33.1 0.1 slice.16
  33.2 0.1 slice_reduce_fusion
  33.3 0.8 bitcast_subtract_fusion
  34.0 0.1 compare_select_fusion
  34.1 0.1 reshape.165
  34.2 18.3 %all-gather = s32[16,8,2]{1,2,0:T(2,128)S(1)} all-gather(s32[1,8,2]{1,2,0:T(2,128)} %bitcast.122), channel_id=1, replica_groups=mesh['groups'=2,'shell'=16] {'shell'}, dimensions={0}, use_global_device_ids=true | all-gather | bytes 1088 | tf_op jit(solution)/shard_map/all_gather | solution.py:46
  52.5 0.1 reshape.238
  52.6 0.7 fusion.19
  53.3 9.9 %fusion.14 = pred[128]{0:T(512)(128)(4,1)S(1)} fusion(s32[]{:T(128)} %bitcast.21, s32[]{:T(128)} %bitcast.22, s32[]{:T(128)} %bitcast.23, s32[]{:T(128)} %bitcast.24, s32[]{:T(128)} %bitcast.25, s32[]{:T(128)} %bitcast.27, s32[]{:T(128)} %bitcast.26, s32[]{:T(128)} %bitcast.4, s32[]{:T(128)} %bitcast.6, s32[]{:T(128)} %bitcast.8, s32[]{:T(128)} %bitcast.10, ...), kind=kLoop, calls=%fused_computation.47 | loop fusion | flops 6144 | bytes 192 | tf_op jit(solution)/shard_map/lt | solution.py:55
  63.2 0.8 iota_compare_fusion
  64.0 0.0 all-to-all-done
  64.0 0.7 reshape.137
  64.7 0.0 all-gather.4.cloned.1.call-done
  64.8 14.7 %gather_fusion = bf16[4096,256]{1,0:T(8,128)(2,1)S(1)} fusion(bf16[2560,256]{1,0:T(8,128)(2,1)} %all-gather.4.cloned.1.call-done, s32[4096]{0:T(1024)S(1)} %broadcast_clamp_fusion), kind=kCustom, calls=%fused_computation | custom fusion | bytes 4210688 | tf_op jit(solution)/shard_map/gather | solution.py:17
  79.4 1.7 broadcast_select_fusion
  81.1 2.2 %gather_fusion.1 = bf16[128,16,256]{2,1,0:T(8,128)(2,1)S(1)} fusion(bf16[256,16,256]{2,1,0:T(8,128)(2,1)} %broadcast_select_fusion, s32[1024]{0:T(1024)S(1)} %pad_clamp_fusion), kind=kCustom, calls=%fused_computation.1 | custom fusion | bytes 2097664 | tf_op jit(solution)/shard_map/while/body/eval_jaxpr/gather | solution.py:35
  83.4 3.0 %convolution_bitcast_fusion = f32[128,2,256,16]{2,3,1,0:T(8,128)} fusion(bf16[128,16,256]{2,1,0:T(8,128)(2,1)S(1)} %gather_fusion.1, bf16[128,2,16,16]{3,2,0,1:T(8,128)(2,1)S(1)} %reshape.137, pred[128]{0:T(512)(128)(4,1)S(1)} %fusion.14), kind=kOutput, calls=%fused_computation.12 | convolution fusion | flops 33619968 | bytes 5374080 | tf_op jit(solution)/shard_map/while/body/eval_jaxpr/kmi,kvmn->kvin/dot_general | solution.py:36
  86.4 4.4 %broadcast_in_dim.62 = f32[256,2,256,16]{2,3,1,0:T(8,128)} broadcast(f32[]{:T(128)} %constant.50.clone.1), dimensions={} | broadcast | bytes 8388612 | tf_op jit(solution)/shard_map/broadcast_in_dim | solution.py:39
  90.8 20.6 %scatter_fusion = f32[256,2,256,16]{2,3,1,0:T(8,128)} fusion(f32[256,2,256,16]{2,3,1,0:T(8,128)} %broadcast_in_dim.62, s32[128]{0:T(128)S(1)} %get-tuple-element.16, f32[128,2,256,16]{2,3,1,0:T(8,128)} %convolution_bitcast_fusion), kind=kCustom, calls=%fused_computation.3 | custom fusion | flops 1048576 | bytes 12583424 | tf_op jit(solution)/shard_map/while/body/eval_jaxpr/scatter-add | solution.py:37
  111.4 37.8 %all-gather.6.cloned.1.call-done = bf16[2560,2304]{1,0:T(8,128)(2,1)} async-done(((bf16[160,2304]{1,0:T(8,128)(2,1)}), bf16[2560,2304]{1,0:T(8,128)(2,1)}) %all-gather.6.cloned.1.call-update) | async-done | bytes 11796496 | tf_op jit(solution)/shard_map/all_gather | solution.py:58
  149.2 41.0 %gather_fusion.2 = bf16[4096,2304]{1,0:T(8,128)(2,1)} fusion(bf16[2560,2304]{1,0:T(8,128)(2,1)} %all-gather.6.cloned.1.call-done, s32[4096]{0:T(1024)S(1)} %broadcast_clamp_fusion), kind=kCustom, calls=%fused_computation.2 | custom fusion | bytes 37765120 | tf_op jit(solution)/shard_map/gather | solution.py:17
  190.2 19.0 %fusion.8 = bf16[2,256,2304]{2,1,0:T(8,128)(2,1)} fusion(bf16[256,16,2304]{2,1,0:T(8,128)(2,1)} %bitcast.117, pred[256,16]{1,0:T(8,128)(4,1)S(1)} %iota_compare_fusion, f32[256,2,256,16]{2,3,1,0:T(8,128)} %scatter_fusion), kind=kOutput, calls=%fused_computation.10 | convolution fusion | flops 9676390400 | bytes 29626368 | tf_op jit(solution)/shard_map/svin,sna->via/dot_general | solution.py:60
  (7 shorter events, 0.1 us)
Async XLA Ops:
  6.5 58.2 %all-gather.4.cloned.1.call-start = ((), (), s32[]{:S(2)}) async-start(), calls=%async_computation.1 | async-start | bytes 1392640 | tf_op jit(solution)/shard_map/all_gather | solution.py:50
  7.3 141.9 %all-gather.6.cloned.1.call-start = ((), (), s32[]{:S(2)}) async-start(), calls=%async_computation.2 | async-start | bytes 12533760 | tf_op jit(solution)/shard_map/all_gather | solution.py:58
  12.3 51.7 %all-to-all-start = ((bf16[8,32,256]{2,0,1:T(8,128)(2,1)}), bf16[8,32,256]{2,0,1:T(8,128)(2,1)S(1)}, u32[]{:S(2)}, u32[]{:S(2)}) async-start(bf16[8,32,256]{2,0,1:T(8,128)(2,1)} %copy.16), calls=%async_computation | async-start | bytes 262144 | tf_op jit(solution)/shard_map/all_to_all | solution.py:49
Sparse Core Ops, SparseCore 0:
  9.6 42.3 all-gather.3
  54.4 94.7 all-gather.5
where the time goes:
time: 217 us; the launch traced here: 216 us
  local copies, waits for them, and re-layouts  67.8 us (31%)
  waiting for transfers between devices  39.2 us (18%)
  other arithmetic  34.8 us (16%)
  blocking collectives  30.6 us (14%)
  matrix products  22 us (10%)
  between operations  14.2 us (7%)
  starting transfers between devices  7.43 us (3%)
    gather x2, local copies, waits for them, and re-layouts, padded_rows(): matrix[rows]  55.7 us
    all_gather x1, waiting for transfers between devices, per_device(): vir_full = lax.all_gather(vir_coef, 'shell', axis=0, tiled=True)  37.8 us
    scatter-add x1, other arithmetic, advance(): return (total.at[col_shell].add(piece), None)  20.6 us
    dot_general x1, matrix products, per_device(): jnp.einsum('svin,sna->via', hidden, vir_blocks, preferred_element_type=jn...  19 us
    all_gather x1, blocking collectives, per_device(): lax.all_gather(block_pairs, 'shell', axis=0, tiled=True)  18.3 us
    unnamed x1, blocking collectives  12.4 us
    lt x1, other arithmetic, per_device(): live = position % BLK_DEV < all_counts[position // BLK_DEV]  9.87 us
    all_to_all x1, starting transfers between devices, per_device(): lax.all_to_all(panels, 'shell', split_axis=1, concat_axis=0, tiled=True)  7.39 us
  transfers between devices with their start and end apart: 3, of which 1 were waited for; matrix products, arithmetic and copies ran while one was open for 30% of the time, Pallas kernels for 0%

commit v1 on v0

--- a/solution.py
+++ b/solution.py
@@ -1,13 +1,21 @@
+import functools
 import math
 
 import jax
 import jax.numpy as jnp
 from jax import lax
+from jax.experimental import pallas as pl
+from jax.experimental.pallas import tpu as pltpu
 from jax.sharding import PartitionSpec as P
 
 EDGE = 16
 NOCC = 256
 BLK_DEV = 8
+LIVE_DEV = 4
+CAP = 160
+Z, Y, CORES = 4, 2, 2
+F32 = jnp.float32
+BF16 = jnp.bfloat16
 
 
 def padded_rows(matrix, starts, shell_size):
@@ -41,7 +49,7 @@
     return half
 
 
-def per_device(panels, block_pairs, block_count, shell_size, occ_coef, vir_coef):
+def long_way(panels, block_pairs, block_count, shell_size, occ_coef, vir_coef):
     all_pairs, all_counts = (
         lax.all_gather(block_pairs, "shell", axis=0, tiled=True),
         lax.all_gather(block_count, "shell", axis=0, tiled=True),
@@ -61,6 +69,277 @@
     return result.astype(jnp.bfloat16)
 
 
+def iota(shape, dim):
+    return lax.broadcasted_iota(jnp.int32, shape, dim)
+
+
+def column_of(row, mask):
+    return jnp.sum(jnp.where(mask, row, 0.0), axis=1, keepdims=True)
+
+
+def row_of(column, mask):
+    return jnp.sum(jnp.where(mask, column, 0.0), axis=0, keepdims=True)
+
+
+def one_hots(ids, shells):
+    lanes = iota(ids.shape, 1).astype(F32)
+    return jnp.concatenate(
+        [(ids == lanes + 128.0 * k).astype(F32) for k in range(shells // 128)], axis=1
+    )
+
+
+def shell_table(col_hot, size_row, windows, rows):
+    shells = size_row.shape[1]
+    sub, lane = iota((shells, shells), 0), iota((shells, shells), 1)
+    used_row = jnp.max(col_hot, axis=0, keepdims=True)
+    before, same = lane < sub, lane == sub
+    starts = column_of(size_row, before)
+    ahead = column_of(size_row * used_row, before)
+    size = column_of(size_row, same)
+    used = column_of(used_row, same)
+    edge = (iota((shells, 128), 1) * rows).astype(F32)
+    reach = used * jnp.clip(edge - starts, 0.0, size)
+    before_window = jnp.sum(reach, axis=0, keepdims=True)
+    return starts, size, used, ahead, before_window
+
+
+def lane_value(row, index):
+    return jnp.sum(jnp.where(iota(row.shape, 1) == index, row, 0.0), axis=1, keepdims=True)
+
+
+def pick_kernel(windows, rows, got_ref, size_ref, own_ref, other_ref, out_ref, over_ref):
+    shells = size_ref.shape[1]
+    here = rows // 2
+    me = lax.axis_index("shell")
+    core = lax.rem(me, 2)
+    window = lax.div(me, 2)
+    got = got_ref[...].astype(F32)
+    slots = got.shape[0] * BLK_DEV
+    ids = got[:, 2 * BLK_DEV :, :].reshape(slots, 256)
+    col_hot = one_hots(ids[:, :128], shells)
+    size_row = size_ref[...].astype(F32)
+    starts, size, used, ahead, before_window = shell_table(col_hot, size_row, windows, rows)
+    lanes = iota(before_window.shape, 1)
+    after = jnp.sum(
+        used * jnp.clip(((iota((shells, 128), 1) + 1) * rows).astype(F32) - starts, 0.0, size), axis=0, keepdims=True
+    )
+    most = jnp.max(jnp.where(lanes < windows, after - before_window, 0.0))
+    over_ref[0] = jnp.where(most > CAP, 1, 0).astype(jnp.int32)
+    base = lane_value(before_window, window)
+
+    def chosen(first):
+        where = (iota((shells, 256), 1) + first).astype(F32) - starts
+        inside = (used > 0.0) & (where >= 0.0) & (where < size)
+        place = jnp.sum(jnp.where(inside, ahead + where + 1.0, 0.0), axis=0, keepdims=True)
+        place = jnp.where(place > 0.0, place - 1.0 - base, -1.0)
+        hot = place == iota((CAP, 256), 0).astype(F32)
+        return jnp.where(hot, 1.0, 0.0).astype(BF16)[:, :here]
+
+    mine = chosen(window * rows + core * here)
+    theirs = chosen(window * rows + (1 - core) * here)
+    width = out_ref.shape[1]
+    own = own_ref[:, pl.ds(pl.multiple_of(core * width, 128), width)]
+    total = jnp.dot(mine, own, preferred_element_type=F32)
+    total += jnp.dot(theirs, other_ref[...], preferred_element_type=F32)
+    out_ref[...] = total.astype(BF16)
+
+
+def half_kernel(windows, rows, got_ref, size_ref, occ_ref, out_ref, total_ref):
+    shells = size_ref.shape[1]
+    nbf = occ_ref.shape[0]
+    sources = got_ref.shape[0]
+    got = got_ref[...].astype(F32)
+    slots = sources * BLK_DEV
+    ids = got[:, 2 * BLK_DEV :, :].reshape(slots, 256)
+    col_hot = one_hots(ids[:, :128], shells)
+    live = jnp.sum(col_hot, axis=1, keepdims=True)
+    row_hot = one_hots(ids[:, 128:], shells) * live
+    size_row = size_ref[...].astype(F32)
+    starts, size, used, ahead, before_window = shell_table(col_hot, size_row, windows, rows)
+    sub, lane = iota((shells, shells), 0), iota((shells, shells), 1)
+    starts_row = row_of(starts, sub == lane)
+    ahead_row = row_of(ahead, sub == lane)
+
+    def of_slot(hot, row):
+        return jnp.sum(hot * row, axis=1, keepdims=True)
+
+    def spread(column):
+        wide = jnp.broadcast_to(column, (slots, 128)).reshape(slots, 1, 128)
+        return jnp.broadcast_to(wide, (slots, EDGE, 128)).reshape(slots * EDGE, 128)
+
+    step = (iota((slots * EDGE, 128), 0) % EDGE).astype(F32)
+    first, length, skip = (spread(of_slot(col_hot, r)) for r in (starts_row, size_row, ahead_row))
+    place = skip + step
+    for w in range(1, windows):
+        shift = CAP - (lane_value(before_window, w) - lane_value(before_window, w - 1))
+        place += jnp.where(first + step >= float(rows * w), shift, 0.0)
+    place = jnp.where(step < length, place, -1.0)
+    first_r, length_r = (spread(of_slot(row_hot, r)) for r in (starts_row, size_row))
+    where_r = jnp.where(step < length_r, first_r + step, -1.0)
+
+    span = 2 * BLK_DEV * EDGE
+    width = out_ref.shape[1]
+    s_in, l_in = iota((span, span), 0), iota((span, span), 1)
+    keep_m = (l_in // EDGE) == (s_in % EDGE)
+    fold = jnp.where((s_in % EDGE) == (l_in % EDGE), 1.0, 0.0).astype(BF16)
+    same_slot = (s_in // EDGE) == (l_in // EDGE)
+    for g in range(slots * EDGE // span):
+        at = slice(g * span, (g + 1) * span)
+        r_hot = where_r[at, :1] == iota((span, nbf), 1).astype(F32)
+        occ_rows = jnp.dot(jnp.where(r_hot, 1.0, 0.0).astype(BF16), occ_ref[...], preferred_element_type=F32)
+        occ_rows = occ_rows.astype(BF16)
+        c_hot = place[at, :1] == iota((span, width), 1).astype(F32)
+        c_hot = jnp.where(c_hot, 1.0, 0.0).astype(BF16)
+        for p in range(2):
+            block = got[2 * g : 2 * g + 2, p * BLK_DEV : (p + 1) * BLK_DEV, :].reshape(16, 1, span)
+            block = jnp.broadcast_to(block, (16, EDGE, span)).reshape(span, span)
+            block = jnp.where(keep_m, block, 0.0).astype(BF16)
+            diag = jnp.dot(block, fold, preferred_element_type=F32)
+            diag = jnp.where(same_slot, diag, 0.0).astype(BF16)
+            placed = jnp.dot(diag, c_hot, preferred_element_type=F32).astype(BF16)
+            piece = lax.dot_general(occ_rows, placed, (((0,), (0,)), ((), ())), preferred_element_type=F32)
+            rows_p = slice(p * NOCC, (p + 1) * NOCC)
+            if g == 0:
+                total_ref[rows_p, :] = piece
+            else:
+                total_ref[rows_p, :] += piece
+    out_ref[...] = total_ref[...].astype(BF16)
+
+
+def last_kernel(count, order_ref, half_ref, *refs):
+    pieces, (out_ref, all_ref, sems) = refs[: 2 * count], refs[2 * count :]
+    width = pieces[0].shape[1]
+    core = order_ref[count]
+
+    def copies():
+        for k, piece in enumerate(pieces):
+            w = order_ref[k % count]
+            half = core if k < count else 1 - core
+            yield pltpu.make_async_copy(
+                piece,
+                all_ref.at[half, pl.ds(pl.multiple_of(w * CAP, 16), CAP), :],
+                sems.at[k],
+            )
+
+    @pl.when(pl.program_id(0) == 0)
+    def _():
+        for copy in copies():
+            copy.start()
+        for copy in copies():
+            copy.wait()
+
+    tile = out_ref.shape[2]
+    j = pl.program_id(0)
+    per = width // tile
+    right = all_ref[lax.div(j, per), :, pl.ds(pl.multiple_of(lax.rem(j, per) * tile, 128), tile)]
+    for p in range(2):
+        out_ref[p] = jnp.dot(half_ref[p * NOCC : (p + 1) * NOCC, :], right, preferred_element_type=F32).astype(BF16)
+
+
+VMEM = pl.BlockSpec(memory_space=pltpu.VMEM)
+SMEM = pl.BlockSpec(memory_space=pltpu.SMEM)
+ANY = pl.BlockSpec(memory_space=pl.ANY)
+
+
+def short_way(panels, block_pairs, block_count, shell_size, occ_coef, vir_coef):
+    n = lax.axis_size("shell")
+    windows = n // CORES
+    here, nvir = vir_coef.shape
+    rows = CORES * here
+    width = nvir // CORES
+    me = lax.axis_index("shell")
+    core = me % 2
+    y = (me // 2) % 2
+    z = me // 4
+
+    def swap(array, bit):
+        return lax.ppermute(array, "shell", [(i, i ^ bit) for i in range(n)])
+
+    def along_z(array, s):
+        return lax.ppermute(array, "shell", [(i, (i + 4 * s) % n) for i in range(n)])
+
+    other = swap(lax.dynamic_slice_in_dim(vir_coef, (1 - core) * width, width, 1), 1)
+    keep = jnp.arange(BLK_DEV, dtype=jnp.int32) < block_count[0]
+    cols = jnp.where(keep, block_pairs[:, 1], -1).astype(BF16)
+    ids = jnp.concatenate(
+        [jnp.broadcast_to(v[:, None], (BLK_DEV, 128)) for v in (cols, block_pairs[:, 0].astype(BF16))], axis=1
+    )
+    send = panels.transpose(1, 0, 2).reshape(n, 2 * BLK_DEV, EDGE * EDGE)
+    send = jnp.concatenate([send, jnp.broadcast_to(ids, (n,) + ids.shape)], axis=1)
+    got = lax.all_to_all(send, "shell", split_axis=0, concat_axis=0, tiled=True)
+    occ_full = lax.all_gather(occ_coef, "shell", axis=0, tiled=True)
+    size_row = shell_size.reshape(1, -1)
+
+    mine, over = pl.pallas_call(
+        functools.partial(pick_kernel, windows, rows),
+        out_shape=(jax.ShapeDtypeStruct((CAP, width), BF16), jax.ShapeDtypeStruct((1,), jnp.int32)),
+        in_specs=[VMEM] * 4,
+        out_specs=(VMEM, SMEM),
+        compiler_params=pltpu.CompilerParams(vmem_limit_bytes=32 << 20),
+        cost_estimate=pl.CostEstimate(flops=10**8, bytes_accessed=2 * 10**6, transcendentals=0),
+        name="pick_rows",
+    )(got, size_row, vir_coef, other)
+
+    near = [mine] + [along_z(mine, s) for s in range(1, Z)]
+    pieces, order = [], []
+    for s, piece in enumerate(near):
+        for dy in range(Y):
+            pieces.append(piece if dy == 0 else swap(piece, 2))
+            order.append(((z - s) % Z) * Y + (y ^ dy))
+    far = [swap(piece, 1) for piece in pieces]
+    order = jnp.stack(order + [core]).astype(jnp.int32)
+
+    half = pl.pallas_call(
+        functools.partial(half_kernel, windows, rows),
+        out_shape=jax.ShapeDtypeStruct((2 * NOCC, windows * CAP), BF16),
+        in_specs=[VMEM] * 3,
+        out_specs=VMEM,
+        scratch_shapes=[
+            pltpu.VMEM((2 * NOCC, windows * CAP), F32),
+        ],
+        compiler_params=pltpu.CompilerParams(vmem_limit_bytes=48 << 20),
+        cost_estimate=pl.CostEstimate(flops=8 * 10**9, bytes_accessed=4 * 10**6, transcendentals=0),
+        name="half_transform",
+    )(got, size_row, occ_full)
+
+    tile = width // 3
+    count = len(pieces)
+    out = pl.pallas_call(
+        functools.partial(last_kernel, count),
+        out_shape=jax.ShapeDtypeStruct((2, NOCC, nvir), BF16),
+        grid_spec=pltpu.PrefetchScalarGridSpec(
+            num_scalar_prefetch=1,
+            grid=(nvir // tile,),
+            in_specs=[pl.BlockSpec((2 * NOCC, windows * CAP), lambda j, o: (0, 0))] + [ANY] * (2 * count),
+            out_specs=pl.BlockSpec((2, NOCC, tile), lambda j, o: (0, 0, j)),
+            scratch_shapes=[
+                pltpu.VMEM((CORES, windows * CAP, width), BF16),
+                pltpu.SemaphoreType.DMA((2 * count,)),
+            ],
+        ),
+        compiler_params=pltpu.CompilerParams(vmem_limit_bytes=48 << 20),
+        cost_estimate=pl.CostEstimate(flops=3 * 10**9, bytes_accessed=10**7, transcendentals=0),
+        name="last_product",
+    )(order, half, *pieces, *far)
+    return out, over[0]
+
+
+def per_device(*args):
+    n = lax.axis_size("shell")
+    here, nvir = args[5].shape
+    sparse = LIVE_DEV * n * EDGE < n * here
+    if not (sparse and n == Z * Y * CORES and here <= 256 and here % 16 == 0 and nvir % 768 == 0):
+        return long_way(*args)
+    out, over = short_way(*args)
+
+    def again(carry):
+        over, _ = carry
+        over, *held = lax.optimization_barrier((over, *args))
+        return over - 1, long_way(*held)
+
+    return lax.while_loop(lambda carry: carry[0] > 0, again, (over, out))[1]
+
+
 def solution(mesh):
     placed = (
         P(("groups", "shell"), None, None),

time: 217 us -> 123 us (0.57)
  the two profiles are of different devices: /device:TPU:0 before, /device:TPU:29 now
where the time goes in v1:
time: 123 us
  waiting for transfers between devices  51.9 us (42%)
  Pallas kernels  27.8 us (23%)
  starting transfers between devices  20.1 us (16%)
  between operations  14.2 us (12%)
  local copies, waits for them, and re-layouts  6.26 us (5%)
  other arithmetic  2.07 us (2%)
    ppermute x3, waiting for transfers between devices, along_z(): lax.ppermute(array, 'shell', [(i, (i + 4 * s) % n) for i in range(n)])  33.3 us
    pallas_call x1, Pallas kernels, short_way(): pl.pallas_call(functools.partial(half_kernel, windows, rows), out_shape=j...  14.6 us
    ppermute x13, starting transfers between devices, swap(): return lax.ppermute(array, 'shell', [(i, i ^ bit) for i in range(n)])  11.5 us
    pallas_call x1, Pallas kernels, short_way(): pl.pallas_call(functools.partial(last_kernel, count), out_shape=jax.Shape...  11.2 us
    ppermute x13, waiting for transfers between devices, swap(): return lax.ppermute(array, 'shell', [(i, i ^ bit) for i in range(n)])  10.3 us
    all_to_all x1, waiting for transfers between devices, short_way(): got = lax.all_to_all(send, 'shell', split_axis=0, concat_axis=0, tiled=True)  7.61 us
    all_to_all x1, starting transfers between devices, short_way(): got = lax.all_to_all(send, 'shell', split_axis=0, concat_axis=0, tiled=True)  5.77 us
    ppermute x3, starting transfers between devices, along_z(): lax.ppermute(array, 'shell', [(i, (i + 4 * s) % n) for i in range(n)])  2.81 us
  transfers between devices with their start and end apart: 18, of which 5 were waited for; matrix products, arithmetic and copies ran while one was open for 5% of the time, Pallas kernels for 14%

profile of v1, /device:TPU:29, one launch (start us, length us, event | category | flops | bytes accessed | tf_op | source)
XLA Modules:
  0.0 122.8 jit_solution(12800423214425864471)
XLA Ops:
  6.5 0.7 all-gather.7.cloned.1.call-update
  7.3 1.0 constant_dynamic-slice_fusion
  8.3 0.7 collective-permute-start
  9.0 1.0 copy.20
  10.7 0.7 convert.3
  11.4 0.7 fusion.20
  12.2 0.7 pad_maximum_fusion
  12.9 5.8 %all-to-all-start.1 = ((bf16[16,24,256]{2,1,0:T(8,128)(2,1)}), bf16[16,24,256]{2,1,0:T(8,128)(2,1)S(1)}, u32[]{:S(2)}, u32[]{:S(2)}) async-start(bf16[16,24,256]{2,1,0:T(8,128)(2,1)} %pad_maximum_fusion), calls=%async_computation.1 | async-start | bytes 393216 | tf_op jit(solution)/shard_map/all_to_all | solution.py:269
  18.7 7.6 %all-to-all-done.1.got_ref = bf16[16,24,256]{2,1,0:T(8,128)(2,1)S(1)} async-done(((bf16[16,24,256]{2,1,0:T(8,128)(2,1)}), bf16[16,24,256]{2,1,0:T(8,128)(2,1)S(1)}, u32[]{:S(2)}, u32[]{:S(2)}) %all-to-all-start.1) | async-done | bytes 196640 | tf_op jit(solution)/shard_map/all_to_all | solution.py:269
  26.3 2.0 %pick_rows.1 = (bf16[160,1152]{1,0:T(8,128)(2,1)S(1)}, s32[1]{0:T(128)}) custom-call(bf16[16,24,256]{2,1,0:T(8,128)(2,1)S(1)} %all-to-all-done.1.got_ref, s32[1,256]{1,0:T(1,128)} %bitcast.220, bf16[160,2304]{1,0:T(8,128)(2,1)} %own_ref.1, bf16[160,1152]{1,0:T(8,128)(2,1)S(1)} %collective-permute-done.other_ref), custom_call_target="tpu_custom_call" | custom-call | flops 100000000 | bytes 2000000 | tf_op jit(solution)/shard_map/pick_rows/pallas_call | solution.py:273
  28.3 1.6 %collective-permute-start.2 = (bf16[160,1152]{1,0:T(8,128)(2,1)S(1)}, bf16[160,1152]{1,0:T(8,128)(2,1)S(1)}, u32[]{:S(2)}, u32[]{:S(2)}) collective-permute-start(bf16[160,1152]{1,0:T(8,128)(2,1)S(1)} %get-tuple-element.160.refs_0_), channel_id=1, source_target_pairs={{0,4},{1,5},{2,6},{3,7},{4,8},{5,9},{6,10},{7,11},{8,12},{9,13},{1... | collective-permute-start | bytes 1105928 | tf_op jit(solution)/shard_map/ppermute | solution.py:259
  30.0 1.2 collective-permute-start.6
  31.1 1.0 collective-permute-start.1
  32.1 0.9 collective-permute-start.8
  33.0 7.5 %collective-permute-done.2.refs_2_ = bf16[160,1152]{1,0:T(8,128)(2,1)S(1)} collective-permute-done((bf16[160,1152]{1,0:T(8,128)(2,1)S(1)}, bf16[160,1152]{1,0:T(8,128)(2,1)S(1)}, u32[]{:S(2)}, u32[]{:S(2)}) %collective-permute-start.2) | collective-permute-done | bytes 368672 | tf_op jit(solution)/shard_map/ppermute | solution.py:259
  40.5 1.3 %collective-permute-start.3 = (bf16[160,1152]{1,0:T(8,128)(2,1)S(1)}, bf16[160,1152]{1,0:T(8,128)(2,1)S(1)}, u32[]{:S(2)}, u32[]{:S(2)}) collective-permute-start(bf16[160,1152]{1,0:T(8,128)(2,1)S(1)} %collective-permute-done.2.refs_2_), channel_id=1, source_target_pairs={{0,2},{1,3},{2,0},{3,1},{4,6},{5,7},{6,4},{7,5},{8,10},{9,11},{10,... | collective-permute-start | bytes 1105928 | tf_op jit(solution)/shard_map/ppermute | solution.py:256
  41.9 25.8 %collective-permute-done.4.refs_4_ = bf16[160,1152]{1,0:T(8,128)(2,1)S(1)} collective-permute-done((bf16[160,1152]{1,0:T(8,128)(2,1)S(1)}, bf16[160,1152]{1,0:T(8,128)(2,1)S(1)}, u32[]{:S(2)}, u32[]{:S(2)}) %collective-permute-start.4) | collective-permute-done | bytes 368672 | tf_op jit(solution)/shard_map/ppermute | solution.py:259
  67.7 1.5 %collective-permute-start.7 = (bf16[160,1152]{1,0:T(8,128)(2,1)S(1)}, bf16[160,1152]{1,0:T(8,128)(2,1)}, u32[]{:S(2)}, u32[]{:S(2)}) collective-permute-start(bf16[160,1152]{1,0:T(8,128)(2,1)S(1)} %collective-permute-done.6.refs_6_), channel_id=1, source_target_pairs={{0,2},{1,3},{2,0},{3,1},{4,6},{5,7},{6,4},{7,5},{8,10},{9,11},{10,... | collective-permute-start | bytes 1105928 | tf_op jit(solution)/shard_map/ppermute | solution.py:256
  69.1 1.1 collective-permute-start.10
  70.3 1.6 %copy.21 = bf16[8,32,256]{2,0,1:T(8,128)(2,1)} copy(bf16[8,32,256]{2,1,0:T(8,128)(2,1)} %param.8) | data formatting | bytes 262144 | tf_op jit(solution)/shard_map/while | solution.py:340
  72.0 0.1 stack.39.order_ref
  72.0 0.5 collective-permute-start.14
  72.6 4.7 %collective-permute-done.5.refs_5_ = bf16[160,1152]{1,0:T(8,128)(2,1)S(1)} collective-permute-done((bf16[160,1152]{1,0:T(8,128)(2,1)S(1)}, bf16[160,1152]{1,0:T(8,128)(2,1)S(1)}, u32[]{:S(2)}, u32[]{:S(2)}) %collective-permute-start.5) | collective-permute-done | bytes 368672 | tf_op jit(solution)/shard_map/ppermute | solution.py:256
  77.2 2.5 %collective-permute-start.9 = (bf16[160,1152]{1,0:T(8,128)(2,1)S(1)}, bf16[160,1152]{1,0:T(8,128)(2,1)}, u32[]{:S(2)}, u32[]{:S(2)}) collective-permute-start(bf16[160,1152]{1,0:T(8,128)(2,1)S(1)} %collective-permute-done.1.refs_1_), channel_id=1, source_target_pairs={{0,1},{1,0},{2,3},{3,2},{4,5},{5,4},{6,7},{7,6},{8,9},{9,8},{10,11... | collective-permute-start | bytes 1105928 | tf_op jit(solution)/shard_map/ppermute | solution.py:256
  79.7 5.6 %collective-permute-done.7.refs_7_ = bf16[160,1152]{1,0:T(8,128)(2,1)} collective-permute-done((bf16[160,1152]{1,0:T(8,128)(2,1)S(1)}, bf16[160,1152]{1,0:T(8,128)(2,1)}, u32[]{:S(2)}, u32[]{:S(2)}) %collective-permute-start.7) | collective-permute-done | bytes 368672 | tf_op jit(solution)/shard_map/ppermute | solution.py:256
  85.2 1.4 %collective-permute-start.11 = (bf16[160,1152]{1,0:T(8,128)(2,1)S(1)}, bf16[160,1152]{1,0:T(8,128)(2,1)}, u32[]{:S(2)}, u32[]{:S(2)}) collective-permute-start(bf16[160,1152]{1,0:T(8,128)(2,1)S(1)} %collective-permute-done.3.refs_3_), channel_id=1, source_target_pairs={{0,1},{1,0},{2,3},{3,2},{4,5},{5,4},{6,7},{7,6},{8,9},{9,8},{10,11... | collective-permute-start | bytes 1105928 | tf_op jit(solution)/shard_map/ppermute | solution.py:256
  86.7 0.5 collective-permute-start.15
  87.2 1.3 %copy-done = bf16[2560,256]{1,0:T(8,128)(2,1)S(1)} copy-done((bf16[2560,256]{1,0:T(8,128)(2,1)S(1)}, bf16[2560,256]{1,0:T(8,128)(2,1)}, u32[]{:S(2)}) %copy-start) | copy-done | bytes 1310744
  88.5 14.6 %half_transform.1.half_ref = bf16[512,1280]{1,0:T(8,128)(2,1)S(1)} custom-call(bf16[16,24,256]{2,1,0:T(8,128)(2,1)S(1)} %all-to-all-done.1.got_ref, s32[1,256]{1,0:T(1,128)} %bitcast.221, bf16[2560,256]{1,0:T(8,128)(2,1)S(1)} %copy-done), custom_call_target="tpu_custom_call" | custom-call | flops 8000000000 | bytes 4000000 | tf_op jit(solution)/shard_map/half_transform/pallas_call | solution.py:292
  103.1 1.1 copy-done.1
  104.2 11.2 %last_product.1 = bf16[2,256,2304]{2,1,0:T(8,128)(2,1)} custom-call(s32[9]{0:T(128)S(1)} %stack.39.order_ref, bf16[512,1280]{1,0:T(8,128)(2,1)} %copy-done.1, bf16[160,1152]{1,0:T(8,128)(2,1)S(1)} %get-tuple-element.160.refs_0_, bf16[160,1152]{1,0:T(8,128)(2,1)S(1)} %collective-permute-done.1.refs_1_, bf16[160,1152]{1,0:T(8,128)(2,1)S(1)} %collective-permute-done.2.refs_2_, ...), custom_call_target="tpu_custom_call" | custom-call | flops 3000000000 | bytes 10000000 | tf_op jit(solution)/shard_map/last_product/pallas_call | solution.py:307
  115.4 0.6 while.17
  (31 shorter events, 0.3 us)
Async XLA Ops:
  6.5 80.7 %all-gather.7.cloned.1.call-start = ((), (), s32[]{:S(2)}) async-start(), calls=%async_computation.2 | async-start | bytes 1392640 | tf_op jit(solution)/shard_map/all_gather | solution.py:270
  8.3 10.4 %collective-permute-start = (bf16[160,1152]{1,0:T(8,128)(2,1)S(1)}, bf16[160,1152]{1,0:T(8,128)(2,1)S(1)}, u32[]{:S(2)}, u32[]{:S(2)}) collective-permute-start(bf16[160,1152]{1,0:T(8,128)(2,1)S(1)} %constant_dynamic-slice_fusion), channel_id=1, source_target_pairs={{0,1},{1,0},{2,3},{3,2},{4,5},{5,4},{6,7},{7,6},{8,9},{9,8},{10,11... | collective-permute-start | bytes 1105928 | tf_op jit(solution)/shard_map/ppermute | solution.py:256
  12.9 13.4 %all-to-all-start.1 = ((bf16[16,24,256]{2,1,0:T(8,128)(2,1)}), bf16[16,24,256]{2,1,0:T(8,128)(2,1)S(1)}, u32[]{:S(2)}, u32[]{:S(2)}) async-start(bf16[16,24,256]{2,1,0:T(8,128)(2,1)} %pad_maximum_fusion), calls=%async_computation.1 | async-start | bytes 393216 | tf_op jit(solution)/shard_map/all_to_all | solution.py:269
  28.3 12.2 %collective-permute-start.2 = (bf16[160,1152]{1,0:T(8,128)(2,1)S(1)}, bf16[160,1152]{1,0:T(8,128)(2,1)S(1)}, u32[]{:S(2)}, u32[]{:S(2)}) collective-permute-start(bf16[160,1152]{1,0:T(8,128)(2,1)S(1)} %get-tuple-element.160.refs_0_), channel_id=1, source_target_pairs={{0,4},{1,5},{2,6},{3,7},{4,8},{5,9},{6,10},{7,11},{8,12},{9,13},{1... | collective-permute-start | bytes 1105928 | tf_op jit(solution)/shard_map/ppermute | solution.py:259
  29.9 37.7 %collective-permute-start.4 = (bf16[160,1152]{1,0:T(8,128)(2,1)S(1)}, bf16[160,1152]{1,0:T(8,128)(2,1)S(1)}, u32[]{:S(2)}, u32[]{:S(2)}) collective-permute-start(bf16[160,1152]{1,0:T(8,128)(2,1)S(1)} %get-tuple-element.160.refs_0_), channel_id=1, source_target_pairs={{0,8},{1,9},{2,10},{3,11},{4,12},{5,13},{6,14},{7,15},{8,0},{9,1},... | collective-permute-start | bytes 1105928 | tf_op jit(solution)/shard_map/ppermute | solution.py:259
  30.0 37.7 %collective-permute-start.6 = (bf16[160,1152]{1,0:T(8,128)(2,1)S(1)}, bf16[160,1152]{1,0:T(8,128)(2,1)S(1)}, u32[]{:S(2)}, u32[]{:S(2)}) collective-permute-start(bf16[160,1152]{1,0:T(8,128)(2,1)S(1)} %get-tuple-element.160.refs_0_), channel_id=1, source_target_pairs={{0,12},{1,13},{2,14},{3,15},{4,0},{5,1},{6,2},{7,3},{8,4},{9,5},{1... | collective-permute-start | bytes 1105928 | tf_op jit(solution)/shard_map/ppermute | solution.py:259
  31.1 38.0 %collective-permute-start.1 = (bf16[160,1152]{1,0:T(8,128)(2,1)S(1)}, bf16[160,1152]{1,0:T(8,128)(2,1)S(1)}, u32[]{:S(2)}, u32[]{:S(2)}) collective-permute-start(bf16[160,1152]{1,0:T(8,128)(2,1)S(1)} %get-tuple-element.160.refs_0_), channel_id=1, source_target_pairs={{0,2},{1,3},{2,0},{3,1},{4,6},{5,7},{6,4},{7,5},{8,10},{9,11},{10,... | collective-permute-start | bytes 1105928 | tf_op jit(solution)/shard_map/ppermute | solution.py:256
  32.1 38.2 %collective-permute-start.8 = (bf16[160,1152]{1,0:T(8,128)(2,1)S(1)}, bf16[160,1152]{1,0:T(8,128)(2,1)S(1)}, u32[]{:S(2)}, u32[]{:S(2)}) collective-permute-start(bf16[160,1152]{1,0:T(8,128)(2,1)S(1)} %get-tuple-element.160.refs_0_), channel_id=1, source_target_pairs={{0,1},{1,0},{2,3},{3,2},{4,5},{5,4},{6,7},{7,6},{8,9},{9,8},{10,11... | collective-permute-start | bytes 1105928 | tf_op jit(solution)/shard_map/ppermute | solution.py:256
  40.5 31.5 %collective-permute-start.3 = (bf16[160,1152]{1,0:T(8,128)(2,1)S(1)}, bf16[160,1152]{1,0:T(8,128)(2,1)S(1)}, u32[]{:S(2)}, u32[]{:S(2)}) collective-permute-start(bf16[160,1152]{1,0:T(8,128)(2,1)S(1)} %collective-permute-done.2.refs_2_), channel_id=1, source_target_pairs={{0,2},{1,3},{2,0},{3,1},{4,6},{5,7},{6,4},{7,5},{8,10},{9,11},{10,... | collective-permute-start | bytes 1105928 | tf_op jit(solution)/shard_map/ppermute | solution.py:256
  67.7 9.6 %collective-permute-start.5 = (bf16[160,1152]{1,0:T(8,128)(2,1)S(1)}, bf16[160,1152]{1,0:T(8,128)(2,1)S(1)}, u32[]{:S(2)}, u32[]{:S(2)}) collective-permute-start(bf16[160,1152]{1,0:T(8,128)(2,1)S(1)} %collective-permute-done.4.refs_4_), channel_id=1, source_target_pairs={{0,2},{1,3},{2,0},{3,1},{4,6},{5,7},{6,4},{7,5},{8,10},{9,11},{10,... | collective-permute-start | bytes 1105928 | tf_op jit(solution)/shard_map/ppermute | solution.py:256
  67.7 17.6 %collective-permute-start.7 = (bf16[160,1152]{1,0:T(8,128)(2,1)S(1)}, bf16[160,1152]{1,0:T(8,128)(2,1)}, u32[]{:S(2)}, u32[]{:S(2)}) collective-permute-start(bf16[160,1152]{1,0:T(8,128)(2,1)S(1)} %collective-permute-done.6.refs_6_), channel_id=1, source_target_pairs={{0,2},{1,3},{2,0},{3,1},{4,6},{5,7},{6,4},{7,5},{8,10},{9,11},{10,... | collective-permute-start | bytes 1105928 | tf_op jit(solution)/shard_map/ppermute | solution.py:256
  69.1 17.5 %collective-permute-start.10 = (bf16[160,1152]{1,0:T(8,128)(2,1)S(1)}, bf16[160,1152]{1,0:T(8,128)(2,1)}, u32[]{:S(2)}, u32[]{:S(2)}) collective-permute-start(bf16[160,1152]{1,0:T(8,128)(2,1)S(1)} %collective-permute-done.2.refs_2_), channel_id=1, source_target_pairs={{0,1},{1,0},{2,3},{3,2},{4,5},{5,4},{6,7},{7,6},{8,9},{9,8},{10,11... | collective-permute-start | bytes 1105928 | tf_op jit(solution)/shard_map/ppermute | solution.py:256
  70.3 16.4 %collective-permute-start.12 = (bf16[160,1152]{1,0:T(8,128)(2,1)S(1)}, bf16[160,1152]{1,0:T(8,128)(2,1)}, u32[]{:S(2)}, u32[]{:S(2)}) collective-permute-start(bf16[160,1152]{1,0:T(8,128)(2,1)S(1)} %collective-permute-done.4.refs_4_), channel_id=1, source_target_pairs={{0,1},{1,0},{2,3},{3,2},{4,5},{5,4},{6,7},{7,6},{8,9},{9,8},{10,11... | collective-permute-start | bytes 1105928 | tf_op jit(solution)/shard_map/ppermute | solution.py:256
  72.0 32.1 %collective-permute-start.14 = (bf16[160,1152]{1,0:T(8,128)(2,1)S(1)}, bf16[160,1152]{1,0:T(8,128)(2,1)}, u32[]{:S(2)}, u32[]{:S(2)}) collective-permute-start(bf16[160,1152]{1,0:T(8,128)(2,1)S(1)} %collective-permute-done.6.refs_6_), channel_id=1, source_target_pairs={{0,1},{1,0},{2,3},{3,2},{4,5},{5,4},{6,7},{7,6},{8,9},{9,8},{10,11... | collective-permute-start | bytes 1105928 | tf_op jit(solution)/shard_map/ppermute | solution.py:256
  77.2 26.9 %collective-permute-start.9 = (bf16[160,1152]{1,0:T(8,128)(2,1)S(1)}, bf16[160,1152]{1,0:T(8,128)(2,1)}, u32[]{:S(2)}, u32[]{:S(2)}) collective-permute-start(bf16[160,1152]{1,0:T(8,128)(2,1)S(1)} %collective-permute-done.1.refs_1_), channel_id=1, source_target_pairs={{0,1},{1,0},{2,3},{3,2},{4,5},{5,4},{6,7},{7,6},{8,9},{9,8},{10,11... | collective-permute-start | bytes 1105928 | tf_op jit(solution)/shard_map/ppermute | solution.py:256
  85.2 18.9 %collective-permute-start.11 = (bf16[160,1152]{1,0:T(8,128)(2,1)S(1)}, bf16[160,1152]{1,0:T(8,128)(2,1)}, u32[]{:S(2)}, u32[]{:S(2)}) collective-permute-start(bf16[160,1152]{1,0:T(8,128)(2,1)S(1)} %collective-permute-done.3.refs_3_), channel_id=1, source_target_pairs={{0,1},{1,0},{2,3},{3,2},{4,5},{5,4},{6,7},{7,6},{8,9},{9,8},{10,11... | collective-permute-start | bytes 1105928 | tf_op jit(solution)/shard_map/ppermute | solution.py:256
  86.7 17.5 %collective-permute-start.13 = (bf16[160,1152]{1,0:T(8,128)(2,1)S(1)}, bf16[160,1152]{1,0:T(8,128)(2,1)}, u32[]{:S(2)}, u32[]{:S(2)}) collective-permute-start(bf16[160,1152]{1,0:T(8,128)(2,1)S(1)} %collective-permute-done.5.refs_5_), channel_id=1, source_target_pairs={{0,1},{1,0},{2,3},{3,2},{4,5},{5,4},{6,7},{7,6},{8,9},{9,8},{10,11... | collective-permute-start | bytes 1105928 | tf_op jit(solution)/shard_map/ppermute | solution.py:256
  86.7 17.5 %collective-permute-start.15 = (bf16[160,1152]{1,0:T(8,128)(2,1)}, bf16[160,1152]{1,0:T(8,128)(2,1)}, u32[]{:S(2)}, u32[]{:S(2)}) collective-permute-start(bf16[160,1152]{1,0:T(8,128)(2,1)} %collective-permute-done.7.refs_7_), channel_id=1, source_target_pairs={{0,1},{1,0},{2,3},{3,2},{4,5},{5,4},{6,7},{7,6},{8,9},{9,8},{10,11... | collective-permute-start | bytes 1105928 | tf_op jit(solution)/shard_map/ppermute | solution.py:256
  87.2 1.3 %copy-start = (bf16[2560,256]{1,0:T(8,128)(2,1)S(1)}, bf16[2560,256]{1,0:T(8,128)(2,1)}, u32[]{:S(2)}) copy-start(bf16[2560,256]{1,0:T(8,128)(2,1)} %all-gather.7.cloned.1.call-done.occ_ref) | copy-start | bytes 3932164
  103.1 1.1 copy-start.1
  104.1 11.2 %copy-start.2 = (s32[256]{0:T(256)S(1)}, s32[256]{0:T(256)}, u32[]{:S(2)}) copy-start(s32[256]{0:T(256)} %param.11) | copy-start | bytes 3076
  104.1 11.3 %copy-start.3 = (s32[8,2]{0,1:T(2,128)S(1)}, s32[8,2]{0,1:T(2,128)}, u32[]{:S(2)}) copy-start(s32[8,2]{0,1:T(2,128)} %param.9) | copy-start | bytes 196
  104.1 11.3 %copy-start.4 = (u32[32]{0:T(128)S(1)}, u32[32]{0:T(128)}, u32[]{:S(2)}) copy-start(u32[32]{0:T(128)} %constant.282) | copy-start | bytes 388
Sparse Core Ops, SparseCore 0:
  9.6 54.7 all-gather.6

commit v2 on v1

--- a/solution.py
+++ b/solution.py
@@ -82,13 +82,13 @@
 
 
 def one_hots(ids, shells):
-    lanes = iota(ids.shape, 1).astype(F32)
+    lanes = iota(ids.shape, 1)
     return jnp.concatenate(
-        [(ids == lanes + 128.0 * k).astype(F32) for k in range(shells // 128)], axis=1
+        [(ids == lanes + 128 * k).astype(F32) for k in range(shells // 128)], axis=1
     )
 
 
-def shell_table(col_hot, size_row, windows, rows):
+def shell_table(col_hot, size_row, rows):
     shells = size_row.shape[1]
     sub, lane = iota((shells, shells), 0), iota((shells, shells), 1)
     used_row = jnp.max(col_hot, axis=0, keepdims=True)
@@ -107,18 +107,16 @@
     return jnp.sum(jnp.where(iota(row.shape, 1) == index, row, 0.0), axis=1, keepdims=True)
 
 
-def pick_kernel(windows, rows, got_ref, size_ref, own_ref, other_ref, out_ref, over_ref):
+def pick_kernel(windows, rows, code_ref, size_ref, own_ref, other_ref, out_ref, over_ref):
     shells = size_ref.shape[1]
     here = rows // 2
     me = lax.axis_index("shell")
     core = lax.rem(me, 2)
     window = lax.div(me, 2)
-    got = got_ref[...].astype(F32)
-    slots = got.shape[0] * BLK_DEV
-    ids = got[:, 2 * BLK_DEV :, :].reshape(slots, 256)
-    col_hot = one_hots(ids[:, :128], shells)
+    code = code_ref[...].reshape(-1, 128)
+    col_hot = one_hots(jnp.where(code < 0, -1, code % shells), shells)
     size_row = size_ref[...].astype(F32)
-    starts, size, used, ahead, before_window = shell_table(col_hot, size_row, windows, rows)
+    starts, size, used, ahead, before_window = shell_table(col_hot, size_row, rows)
     lanes = iota(before_window.shape, 1)
     after = jnp.sum(
         used * jnp.clip(((iota((shells, 128), 1) + 1) * rows).astype(F32) - starts, 0.0, size), axis=0, keepdims=True
@@ -144,46 +142,76 @@
     out_ref[...] = total.astype(BF16)
 
 
-def half_kernel(windows, rows, got_ref, size_ref, occ_ref, out_ref, total_ref):
+def half_kernel(windows, rows, code_ref, got_ref, size_ref, *refs):
+    parts, (out_ref, total_ref, occ_ref, sems) = refs[:4], refs[4:]
+    me = lax.axis_index("shell")
+    core, y, z = lax.rem(me, 2), lax.rem(lax.div(me, 2), 2), lax.div(me, 4)
+    here = rows // 2
+    copies = []
+    for dc in range(CORES):
+        for dy in range(Y):
+            for s in range(Z):
+                source = (lax.rem(z - s + Z, Z) * Y + lax.rem(y + dy, Y)) * CORES + lax.rem(core + dc, CORES)
+                copies.append(
+                    pltpu.make_async_copy(
+                        parts[dc * Y + dy].at[pl.ds(s * here, here), :],
+                        occ_ref.at[pl.ds(pl.multiple_of(source * here, 16), here), :],
+                        sems.at[len(copies)],
+                    )
+                )
+    for copy in copies:
+        copy.start()
+
     shells = size_ref.shape[1]
     nbf = occ_ref.shape[0]
-    sources = got_ref.shape[0]
-    got = got_ref[...].astype(F32)
-    slots = sources * BLK_DEV
-    ids = got[:, 2 * BLK_DEV :, :].reshape(slots, 256)
-    col_hot = one_hots(ids[:, :128], shells)
-    live = jnp.sum(col_hot, axis=1, keepdims=True)
-    row_hot = one_hots(ids[:, 128:], shells) * live
+    code = code_ref[...].reshape(-1, 128)
+    slots = code.shape[0]
+    kept = LIVE_DEV * (slots // BLK_DEV)
+    cols = one_hots(jnp.where(code < 0, -1, code % shells), shells)
+    rws = one_hots(jnp.where(code < 0, -1, code // shells), shells)
+    alive = (code >= 0).astype(F32)
+    sub, lane = iota((slots, slots), 0), iota((slots, slots), 1)
+    rank = row_of(alive, sub < lane)
+    alive_row = row_of(alive, sub == lane)
+    take = (rank == iota((kept, slots), 0).astype(F32)) & (alive_row > 0.0)
+    take = jnp.where(take, 1.0, 0.0).astype(BF16)
+
+    def taken(array):
+        return jnp.dot(take, array.astype(BF16), preferred_element_type=F32)
+
+    col_hot, row_hot = taken(cols), taken(rws)
     size_row = size_ref[...].astype(F32)
-    starts, size, used, ahead, before_window = shell_table(col_hot, size_row, windows, rows)
+    starts, size, used, ahead, before_window = shell_table(col_hot, size_row, rows)
     sub, lane = iota((shells, shells), 0), iota((shells, shells), 1)
     starts_row = row_of(starts, sub == lane)
     ahead_row = row_of(ahead, sub == lane)
 
-    def of_slot(hot, row):
-        return jnp.sum(hot * row, axis=1, keepdims=True)
-
-    def spread(column):
-        wide = jnp.broadcast_to(column, (slots, 128)).reshape(slots, 1, 128)
-        return jnp.broadcast_to(wide, (slots, EDGE, 128)).reshape(slots * EDGE, 128)
-
-    step = (iota((slots * EDGE, 128), 0) % EDGE).astype(F32)
-    first, length, skip = (spread(of_slot(col_hot, r)) for r in (starts_row, size_row, ahead_row))
+    def spread(hot, row):
+        column = jnp.sum(hot * row, axis=1, keepdims=True)
+        wide = jnp.broadcast_to(column, (kept, 128)).reshape(kept, 1, 128)
+        return jnp.broadcast_to(wide, (kept, EDGE, 128)).reshape(kept * EDGE, 128)
+
+    step = (iota((kept * EDGE, 128), 0) % EDGE).astype(F32)
+    first, length, skip = (spread(col_hot, r) for r in (starts_row, size_row, ahead_row))
     place = skip + step
     for w in range(1, windows):
         shift = CAP - (lane_value(before_window, w) - lane_value(before_window, w - 1))
         place += jnp.where(first + step >= float(rows * w), shift, 0.0)
     place = jnp.where(step < length, place, -1.0)
-    first_r, length_r = (spread(of_slot(row_hot, r)) for r in (starts_row, size_row))
+    first_r, length_r = (spread(row_hot, r) for r in (starts_row, size_row))
     where_r = jnp.where(step < length_r, first_r + step, -1.0)
 
-    span = 2 * BLK_DEV * EDGE
+    span = 16 * EDGE
     width = out_ref.shape[1]
     s_in, l_in = iota((span, span), 0), iota((span, span), 1)
     keep_m = (l_in // EDGE) == (s_in % EDGE)
     fold = jnp.where((s_in % EDGE) == (l_in % EDGE), 1.0, 0.0).astype(BF16)
     same_slot = (s_in // EDGE) == (l_in // EDGE)
-    for g in range(slots * EDGE // span):
+    got = got_ref[...].astype(F32)
+    blocks = [taken(got[:, p * BLK_DEV : (p + 1) * BLK_DEV, :].reshape(slots, span)) for p in range(2)]
+    for copy in copies:
+        copy.wait()
+    for g in range(kept // 16):
         at = slice(g * span, (g + 1) * span)
         r_hot = where_r[at, :1] == iota((span, nbf), 1).astype(F32)
         occ_rows = jnp.dot(jnp.where(r_hot, 1.0, 0.0).astype(BF16), occ_ref[...], preferred_element_type=F32)
@@ -191,7 +219,7 @@
         c_hot = place[at, :1] == iota((span, width), 1).astype(F32)
         c_hot = jnp.where(c_hot, 1.0, 0.0).astype(BF16)
         for p in range(2):
-            block = got[2 * g : 2 * g + 2, p * BLK_DEV : (p + 1) * BLK_DEV, :].reshape(16, 1, span)
+            block = blocks[p][g * 16 : (g + 1) * 16].reshape(16, 1, span)
             block = jnp.broadcast_to(block, (16, EDGE, span)).reshape(span, span)
             block = jnp.where(keep_m, block, 0.0).astype(BF16)
             diag = jnp.dot(block, fold, preferred_element_type=F32)
@@ -209,28 +237,32 @@
 def last_kernel(count, order_ref, half_ref, *refs):
     pieces, (out_ref, all_ref, sems) = refs[: 2 * count], refs[2 * count :]
     width = pieces[0].shape[1]
+    tile = out_ref.shape[2]
+    per = width // tile
     core = order_ref[count]
-
-    def copies():
-        for k, piece in enumerate(pieces):
-            w = order_ref[k % count]
-            half = core if k < count else 1 - core
+    j = pl.program_id(0)
+
+    def copies(far):
+        for k in range(count):
             yield pltpu.make_async_copy(
-                piece,
-                all_ref.at[half, pl.ds(pl.multiple_of(w * CAP, 16), CAP), :],
-                sems.at[k],
+                pieces[far * count + k],
+                all_ref.at[far, pl.ds(pl.multiple_of(order_ref[k] * CAP, 16), CAP), :],
+                sems.at[far * count + k],
             )
 
-    @pl.when(pl.program_id(0) == 0)
+    @pl.when(j == 0)
     def _():
-        for copy in copies():
-            copy.start()
-        for copy in copies():
-            copy.wait()
-
-    tile = out_ref.shape[2]
-    j = pl.program_id(0)
-    per = width // tile
+        for far in range(2):
+            for copy in copies(far):
+                copy.start()
+
+    for far in range(2):
+
+        @pl.when(j == far * per)
+        def _():
+            for copy in copies(far):
+                copy.wait()
+
     right = all_ref[lax.div(j, per), :, pl.ds(pl.multiple_of(lax.rem(j, per) * tile, 128), tile)]
     for p in range(2):
         out_ref[p] = jnp.dot(half_ref[p * NOCC : (p + 1) * NOCC, :], right, preferred_element_type=F32).astype(BF16)
@@ -247,6 +279,7 @@
     here, nvir = vir_coef.shape
     rows = CORES * here
     width = nvir // CORES
+    shells = shell_size.shape[0]
     me = lax.axis_index("shell")
     core = me % 2
     y = (me // 2) % 2
@@ -258,16 +291,14 @@
     def along_z(array, s):
         return lax.ppermute(array, "shell", [(i, (i + 4 * s) % n) for i in range(n)])
 
+    def between(array, steps):
+        return lax.ppermute(array, "shell", [(4 * a + k, 4 * b + k) for a, b in steps for k in range(4)])
+
+    keep = jnp.arange(BLK_DEV, dtype=jnp.int32) < block_count[0]
+    code = jnp.where(keep, block_pairs[:, 1] + shells * block_pairs[:, 0], -1)
+    code = jnp.broadcast_to(code[None, :, None], (n, BLK_DEV, 128))
+    code = lax.all_to_all(code, "shell", split_axis=0, concat_axis=0, tiled=True)
     other = swap(lax.dynamic_slice_in_dim(vir_coef, (1 - core) * width, width, 1), 1)
-    keep = jnp.arange(BLK_DEV, dtype=jnp.int32) < block_count[0]
-    cols = jnp.where(keep, block_pairs[:, 1], -1).astype(BF16)
-    ids = jnp.concatenate(
-        [jnp.broadcast_to(v[:, None], (BLK_DEV, 128)) for v in (cols, block_pairs[:, 0].astype(BF16))], axis=1
-    )
-    send = panels.transpose(1, 0, 2).reshape(n, 2 * BLK_DEV, EDGE * EDGE)
-    send = jnp.concatenate([send, jnp.broadcast_to(ids, (n,) + ids.shape)], axis=1)
-    got = lax.all_to_all(send, "shell", split_axis=0, concat_axis=0, tiled=True)
-    occ_full = lax.all_gather(occ_coef, "shell", axis=0, tiled=True)
     size_row = shell_size.reshape(1, -1)
 
     mine, over = pl.pallas_call(
@@ -278,29 +309,48 @@
         compiler_params=pltpu.CompilerParams(vmem_limit_bytes=32 << 20),
         cost_estimate=pl.CostEstimate(flops=10**8, bytes_accessed=2 * 10**6, transcendentals=0),
         name="pick_rows",
-    )(got, size_row, vir_coef, other)
-
-    near = [mine] + [along_z(mine, s) for s in range(1, Z)]
-    pieces, order = [], []
-    for s, piece in enumerate(near):
-        for dy in range(Y):
-            pieces.append(piece if dy == 0 else swap(piece, 2))
-            order.append(((z - s) % Z) * Y + (y ^ dy))
-    far = [swap(piece, 1) for piece in pieces]
-    order = jnp.stack(order + [core]).astype(jnp.int32)
+    )(code, size_row, vir_coef, other)
+
+    near = (z == 1) | (z == 2)
+    pair = between(mine, [(0, 1), (1, 0), (2, 3), (3, 2)])
+    middle = between(mine, [(1, 2), (2, 1)])
+    middle_far = between(pair, [(1, 2), (2, 1)])
+    outward = between(middle, [(1, 0), (2, 3)])
+    outward_far = between(middle_far, [(1, 0), (2, 3)])
+    columns = [mine, pair, jnp.where(near, middle, outward), jnp.where(near, middle_far, outward_far)]
+    sources = [z, z ^ 1, jnp.where(z < 2, 2, 1), jnp.where(z < 2, 3, 0)]
+    swapped = [swap(piece, 2) for piece in columns]
+
+    line = jnp.concatenate([occ_coef] + [along_z(occ_coef, s) for s in range(1, Z)], axis=0)
+    plane = [line, swap(line, 2)]
+    plane += [swap(part, 1) for part in plane]
+
+    send = panels.transpose(1, 0, 2).reshape(n, 2 * BLK_DEV, EDGE * EDGE)
+    send, _ = lax.optimization_barrier((send, mine))
+    got = lax.all_to_all(send, "shell", split_axis=0, concat_axis=0, tiled=True)
 
     half = pl.pallas_call(
         functools.partial(half_kernel, windows, rows),
         out_shape=jax.ShapeDtypeStruct((2 * NOCC, windows * CAP), BF16),
-        in_specs=[VMEM] * 3,
+        in_specs=[VMEM] * 3 + [ANY] * 4,
         out_specs=VMEM,
         scratch_shapes=[
             pltpu.VMEM((2 * NOCC, windows * CAP), F32),
+            pltpu.VMEM((n * here, NOCC), BF16),
+            pltpu.SemaphoreType.DMA((n,)),
         ],
-        compiler_params=pltpu.CompilerParams(vmem_limit_bytes=48 << 20),
+        compiler_params=pltpu.CompilerParams(vmem_limit_bytes=32 << 20),
         cost_estimate=pl.CostEstimate(flops=8 * 10**9, bytes_accessed=4 * 10**6, transcendentals=0),
         name="half_transform",
-    )(got, size_row, occ_full)
+    )(code, got, size_row, *plane)
+
+    swapped[3], half = lax.optimization_barrier((swapped[3], half))
+    pieces, order = [], []
+    for k in range(Z):
+        pieces += [columns[k], swapped[k]]
+        order += [sources[k] * Y + y, sources[k] * Y + (y ^ 1)]
+    far = [swap(piece, 1) for piece in pieces]
+    order = jnp.stack(order + [core]).astype(jnp.int32)
 
     tile = width // 3
     count = len(pieces)
@@ -310,14 +360,14 @@
         grid_spec=pltpu.PrefetchScalarGridSpec(
             num_scalar_prefetch=1,
             grid=(nvir // tile,),
-            in_specs=[pl.BlockSpec((2 * NOCC, windows * CAP), lambda j, o: (0, 0))] + [ANY] * (2 * count),
-            out_specs=pl.BlockSpec((2, NOCC, tile), lambda j, o: (0, 0, j)),
+            in_specs=[VMEM] + [ANY] * (2 * count),
+            out_specs=pl.BlockSpec((2, NOCC, tile), lambda j, o: (0, 0, (j + 3 * o[count]) % 6)),
             scratch_shapes=[
                 pltpu.VMEM((CORES, windows * CAP, width), BF16),
                 pltpu.SemaphoreType.DMA((2 * count,)),
             ],
         ),
-        compiler_params=pltpu.CompilerParams(vmem_limit_bytes=48 << 20),
+        compiler_params=pltpu.CompilerParams(vmem_limit_bytes=32 << 20),
         cost_estimate=pl.CostEstimate(flops=3 * 10**9, bytes_accessed=10**7, transcendentals=0),
         name="last_product",
     )(order, half, *pieces, *far)

time: 123 us -> 126 us (1.024)
  the two profiles are of different devices: /device:TPU:29 before, /device:TPU:0 now
where the time goes in v2:
time: 126 us
  waiting for transfers between devices  42.3 us (34%)
  starting transfers between devices  21.9 us (17%)
  Pallas kernels  20 us (16%)
  between operations  14.3 us (11%)
  blocking collectives  13.7 us (11%)
  local copies, waits for them, and re-layouts  10.2 us (8%)
  other arithmetic  2.85 us (2%)
    ppermute x5, waiting for transfers between devices, between(): lax.ppermute(array, 'shell', [(4 * a + k, 4 * b + k) for a, b in steps fo...  17.2 us
    ppermute x16, waiting for transfers between devices, swap(): return lax.ppermute(array, 'shell', [(i, i ^ bit) for i in range(n)])  15.1 us
    all_to_all x1, blocking collectives, short_way(): lax.all_to_all(code, 'shell', split_axis=0, concat_axis=0, tiled=True)  13.7 us
    ppermute x3, waiting for transfers between devices, along_z(): lax.ppermute(array, 'shell', [(i, (i + 4 * s) % n) for i in range(n)])  9.94 us
    pallas_call x1, Pallas kernels, short_way(): pl.pallas_call(functools.partial(half_kernel, windows, rows), out_shape=j...  9.16 us
    pallas_call x1, Pallas kernels, short_way(): pl.pallas_call(functools.partial(last_kernel, count), out_shape=jax.Shape...  8.76 us
    ppermute x16, starting transfers between devices, swap(): return lax.ppermute(array, 'shell', [(i, i ^ bit) for i in range(n)])  6.74 us
    ppermute x3, starting transfers between devices, along_z(): lax.ppermute(array, 'shell', [(i, (i + 4 * s) % n) for i in range(n)])  6.35 us
  transfers between devices with their start and end apart: 25, of which 7 were waited for; matrix products, arithmetic and copies ran while one was open for 6% of the time, Pallas kernels for 7%

profile of v2, /device:TPU:0, one launch (start us, length us, event | category | flops | bytes accessed | tf_op | source)
XLA Modules:
  0.0 125.8 jit_solution(13764411106156495712)
XLA Ops:
  6.5 1.0 constant_dynamic-slice_fusion
  8.7 0.8 compare_select_fusion.10
  9.6 13.7 %all_to_all.36.code_ref = s32[16,8,128]{2,1,0:T(8,128)S(1)} all-to-all(s32[16,8,128]{2,1,0:T(8,128)S(1)} %broadcast_in_dim.96), channel_id=1, replica_groups=mesh['groups'=2,'shell'=16] {'shell'}, dimensions={0} | all-to-all | bytes 131072 | tf_op jit(solution)/shard_map/all_to_all | solution.py:300
  23.3 2.1 %pick_rows.1 = (bf16[160,1152]{1,0:T(8,128)(2,1)S(1)}, s32[1]{0:T(128)}) custom-call(s32[16,8,128]{2,1,0:T(8,128)S(1)} %all_to_all.36.code_ref, s32[1,256]{1,0:T(1,128)} %bitcast.217, bf16[160,2304]{1,0:T(8,128)(2,1)} %own_ref.1, bf16[160,1152]{1,0:T(8,128)(2,1)S(1)} %collective-permute-done.other_ref), custom_call_target="tpu_custom_call" | custom-call | flops 100000000 | bytes 2000000 | tf_op jit(solution)/shard_map/pick_rows/pallas_call | solution.py:304
  25.6 9.9 %collective-permute-done.1.refs_2_ = bf16[160,1152]{1,0:T(8,128)(2,1)S(1)} collective-permute-done((bf16[160,1152]{1,0:T(8,128)(2,1)S(1)}, bf16[160,1152]{1,0:T(8,128)(2,1)S(1)}, u32[]{:S(2)}, u32[]{:S(2)}) %collective-permute-start.1) | collective-permute-done | bytes 368672 | tf_op jit(solution)/shard_map/ppermute | solution.py:295
  36.2 2.6 %collective-permute-start.5 = (bf16[160,256]{1,0:T(8,128)(2,1)}, bf16[160,256]{1,0:T(8,128)(2,1)S(1)}, u32[]{:S(2)}, u32[]{:S(2)}) collective-permute-start(bf16[160,256]{1,0:T(8,128)(2,1)} %param.12), channel_id=1, source_target_pairs={{0,4},{1,5},{2,6},{3,7},{4,8},{5,9},{6,10},{7,11},{8,12},{9,13},{1... | collective-permute-start | bytes 245768 | tf_op jit(solution)/shard_map/ppermute | solution.py:292
  38.8 0.9 collective-permute-start.6
  39.7 2.8 %collective-permute-start.7 = (bf16[160,256]{1,0:T(8,128)(2,1)}, bf16[160,256]{1,0:T(8,128)(2,1)S(1)}, u32[]{:S(2)}, u32[]{:S(2)}) collective-permute-start(bf16[160,256]{1,0:T(8,128)(2,1)} %param.12), channel_id=1, source_target_pairs={{0,12},{1,13},{2,14},{3,15},{4,0},{5,1},{6,2},{7,3},{8,4},{9,5},{1... | collective-permute-start | bytes 245768 | tf_op jit(solution)/shard_map/ppermute | solution.py:292
  42.5 0.9 constant_dynamic-update-slice_fusion.3
  43.5 9.9 %collective-permute-done.6 = bf16[160,256]{1,0:T(8,128)(2,1)S(1)} collective-permute-done((bf16[160,256]{1,0:T(8,128)(2,1)}, bf16[160,256]{1,0:T(8,128)(2,1)S(1)}, u32[]{:S(2)}, u32[]{:S(2)}) %collective-permute-start.6) | collective-permute-done | bytes 81952 | tf_op jit(solution)/shard_map/ppermute | solution.py:292
  53.4 0.7 collective-permute-start.13
  54.1 1.3 %collective-permute-start.3 = (bf16[160,1152]{1,0:T(8,128)(2,1)S(1)}, bf16[160,1152]{1,0:T(8,128)(2,1)S(1)}, u32[]{:S(2)}, u32[]{:S(2)}) collective-permute-start(bf16[160,1152]{1,0:T(8,128)(2,1)S(1)} %collective-permute-done.2), channel_id=1, source_target_pairs={{4,0},{5,1},{6,2},{7,3},{8,12},{9,13},{10,14},{11,15},{20,16},{21,... | collective-permute-start | bytes 1105928 | tf_op jit(solution)/shard_map/ppermute | solution.py:295
  55.4 0.7 collective-permute-start.8
  56.2 1.6 %copy.20 = bf16[32,8,256]{2,1,0:T(8,128)(2,1)} copy(bf16[32,8,256]{2,0,1:T(8,128)(2,1)} %bitcast.216) | data formatting | bytes 262144 | tf_op jit(solution)/shard_map/transpose | solution.py:328
  57.8 1.4 %collective-permute-start.11 = (bf16[160,1152]{1,0:T(8,128)(2,1)S(1)}, bf16[160,1152]{1,0:T(8,128)(2,1)S(1)}, u32[]{:S(2)}, u32[]{:S(2)}) collective-permute-start(bf16[160,1152]{1,0:T(8,128)(2,1)S(1)} %get-tuple-element.163.refs_0_), channel_id=1, source_target_pairs={{0,2},{1,3},{2,0},{3,1},{4,6},{5,7},{6,4},{7,5},{8,10},{9,11},{10,... | collective-permute-start | bytes 1105928 | tf_op jit(solution)/shard_map/ppermute | solution.py:289
  59.2 6.4 %collective-permute-done.8.refs_1_ = bf16[640,256]{1,0:T(8,128)(2,1)} collective-permute-done((bf16[640,256]{1,0:T(8,128)(2,1)S(1)}, bf16[640,256]{1,0:T(8,128)(2,1)}, u32[]{:S(2)}, u32[]{:S(2)}) %collective-permute-start.8) | collective-permute-done | bytes 327712 | tf_op jit(solution)/shard_map/ppermute | solution.py:289
  66.0 0.8 copy-done.5
  66.8 1.3 %collective-permute-start.14 = (bf16[160,1152]{1,0:T(8,128)(2,1)S(1)}, bf16[160,1152]{1,0:T(8,128)(2,1)}, u32[]{:S(2)}, u32[]{:S(2)}) collective-permute-start(bf16[160,1152]{1,0:T(8,128)(2,1)S(1)} %collective-permute-done.13), channel_id=1, source_target_pairs={{4,0},{5,1},{6,2},{7,3},{8,12},{9,13},{10,14},{11,15},{20,16},{21,... | collective-permute-start | bytes 1105928 | tf_op jit(solution)/shard_map/ppermute | solution.py:295
  68.1 1.1 broadcast_select_fusion.3.refs_6_
  69.1 4.8 %all-to-all-start.2 = ((bf16[16,16,256]{2,1,0:T(8,128)(2,1)}), bf16[16,16,256]{2,1,0:T(8,128)(2,1)S(1)}, u32[]{:S(2)}, u32[]{:S(2)}) async-start(bf16[16,16,256]{2,1,0:T(8,128)(2,1)} %bitcast.56), calls=%async_computation.2 | async-start | bytes 262144 | tf_op jit(solution)/shard_map/all_to_all | solution.py:330
  73.9 7.2 %collective-permute-done.14 = bf16[160,1152]{1,0:T(8,128)(2,1)} collective-permute-done((bf16[160,1152]{1,0:T(8,128)(2,1)S(1)}, bf16[160,1152]{1,0:T(8,128)(2,1)}, u32[]{:S(2)}, u32[]{:S(2)}) %collective-permute-start.14) | collective-permute-done | bytes 368672 | tf_op jit(solution)/shard_map/ppermute | solution.py:295
  81.2 1.0 broadcast_select_fusion.2.refs_4_
  82.2 0.7 copy-done
  82.9 2.0 %collective-permute-start.12 = (bf16[160,1152]{1,0:T(8,128)(2,1)S(1)}, bf16[160,1152]{1,0:T(8,128)(2,1)S(1)}, u32[]{:S(2)}, u32[]{:S(2)}) collective-permute-start(bf16[160,1152]{1,0:T(8,128)(2,1)S(1)} %collective-permute-done.1.refs_2_), channel_id=1, source_target_pairs={{0,2},{1,3},{2,0},{3,1},{4,6},{5,7},{6,4},{7,5},{8,10},{9,11},{10,... | collective-permute-start | bytes 1105928 | tf_op jit(solution)/shard_map/ppermute | solution.py:289
  85.5 7.2 %collective-permute-done.4.refs_7_ = bf16[160,1152]{1,0:T(8,128)(2,1)S(1)} collective-permute-done((bf16[160,1152]{1,0:T(8,128)(2,1)S(1)}, bf16[160,1152]{1,0:T(8,128)(2,1)S(1)}, u32[]{:S(2)}, u32[]{:S(2)}) %collective-permute-start.4) | collective-permute-done | bytes 368672 | tf_op jit(solution)/shard_map/ppermute | solution.py:289
  92.7 1.0 copy-done.1
  93.7 9.2 %half_transform.1.half_ref = bf16[512,1280]{1,0:T(8,128)(2,1)S(1)} custom-call(s32[16,8,128]{2,1,0:T(8,128)S(1)} %all_to_all.36.code_ref, bf16[16,16,256]{2,1,0:T(8,128)(2,1)S(1)} %all-to-all-done.2.got_ref, s32[1,256]{1,0:T(1,128)S(1)} %bitcast.218, bf16[640,256]{1,0:T(8,128)(2,1)S(1)} %constant_dynamic-update-slice_fusion.refs_0_, ...), custom_call_target="tpu_custom_call" | custom-call | flops 8000000000 | bytes 4000000 | tf_op jit(solution)/shard_map/half_transform/pallas_call | solution.py:332
  102.9 1.0 copy-done.2
  104.5 1.3 %collective-permute-done.15.refs_5_ = bf16[160,1152]{1,0:T(8,128)(2,1)} collective-permute-done((bf16[160,1152]{1,0:T(8,128)(2,1)S(1)}, bf16[160,1152]{1,0:T(8,128)(2,1)}, u32[]{:S(2)}, u32[]{:S(2)}) %collective-permute-start.15) | collective-permute-done | bytes 368672 | tf_op jit(solution)/shard_map/ppermute | solution.py:289
  106.3 1.6 %copy.21 = bf16[8,32,256]{2,0,1:T(8,128)(2,1)} copy(bf16[8,32,256]{2,1,0:T(8,128)(2,1)} %param.8) | data formatting | bytes 262144 | tf_op jit(solution)/shard_map/while | solution.py:390
  108.3 1.3 %copy-done.3 = bf16[512,1280]{1,0:T(8,128)(2,1)S(1)} copy-done((bf16[512,1280]{1,0:T(8,128)(2,1)S(1)}, bf16[512,1280]{1,0:T(8,128)(2,1)}, u32[]{:S(2)}) %copy-start.3) | copy-done | bytes 1310744
  109.6 8.8 %last_product.1 = bf16[2,256,2304]{2,1,0:T(8,128)(2,1)} custom-call(s32[9]{0:T(128)S(1)} %stack.39.order_ref, bf16[512,1280]{1,0:T(8,128)(2,1)S(1)} %copy-done.3, bf16[160,1152]{1,0:T(8,128)(2,1)S(1)} %get-tuple-element.163.refs_0_, bf16[160,1152]{1,0:T(8,128)(2,1)S(1)} %collective-permute-done.11.refs_1_, ...), custom_call_target="tpu_custom_call" | custom-call | flops 3000000000 | bytes 10000000 | tf_op jit(solution)/shard_map/last_product/pallas_call | solution.py:357
  (53 shorter events, 4.6 us)
Async XLA Ops:
  6.5 86.2 %copy-start.6 = (s32[256]{0:T(256)S(1)}, s32[256]{0:T(256)}, u32[]{:S(2)}) copy-start(s32[256]{0:T(256)} %param.11) | copy-start | bytes 3076
  7.6 15.7 %collective-permute-start = (bf16[160,1152]{1,0:T(8,128)(2,1)S(1)}, bf16[160,1152]{1,0:T(8,128)(2,1)S(1)}, u32[]{:S(2)}, u32[]{:S(2)}) collective-permute-start(bf16[160,1152]{1,0:T(8,128)(2,1)S(1)} %constant_dynamic-slice_fusion), channel_id=1, source_target_pairs={{0,1},{1,0},{2,3},{3,2},{4,5},{5,4},{6,7},{7,6},{8,9},{9,8},{10,11... | collective-permute-start | bytes 1105928 | tf_op jit(solution)/shard_map/ppermute | solution.py:289
  25.4 10.1 %collective-permute-start.1 = (bf16[160,1152]{1,0:T(8,128)(2,1)S(1)}, bf16[160,1152]{1,0:T(8,128)(2,1)S(1)}, u32[]{:S(2)}, u32[]{:S(2)}) collective-permute-start(bf16[160,1152]{1,0:T(8,128)(2,1)S(1)} %get-tuple-element.163.refs_0_), channel_id=1, source_target_pairs={{0,4},{1,5},{2,6},{3,7},{4,0},{5,1},{6,2},{7,3},{8,12},{9,13},{10,... | collective-permute-start | bytes 1105928 | tf_op jit(solution)/shard_map/ppermute | solution.py:295
  35.5 18.6 %collective-permute-start.2 = (bf16[160,1152]{1,0:T(8,128)(2,1)S(1)}, bf16[160,1152]{1,0:T(8,128)(2,1)S(1)}, u32[]{:S(2)}, u32[]{:S(2)}) collective-permute-start(bf16[160,1152]{1,0:T(8,128)(2,1)S(1)} %collective-permute-done.1.refs_2_), channel_id=1, source_target_pairs={{4,8},{5,9},{6,10},{7,11},{8,4},{9,5},{10,6},{11,7},{20,24},{21,25... | collective-permute-start | bytes 1105928 | tf_op jit(solution)/shard_map/ppermute | solution.py:295
  36.2 7.3 %collective-permute-start.5 = (bf16[160,256]{1,0:T(8,128)(2,1)}, bf16[160,256]{1,0:T(8,128)(2,1)S(1)}, u32[]{:S(2)}, u32[]{:S(2)}) collective-permute-start(bf16[160,256]{1,0:T(8,128)(2,1)} %param.12), channel_id=1, source_target_pairs={{0,4},{1,5},{2,6},{3,7},{4,8},{5,9},{6,10},{7,11},{8,12},{9,13},{1... | collective-permute-start | bytes 245768 | tf_op jit(solution)/shard_map/ppermute | solution.py:292
  38.8 14.6 %collective-permute-start.6 = (bf16[160,256]{1,0:T(8,128)(2,1)}, bf16[160,256]{1,0:T(8,128)(2,1)S(1)}, u32[]{:S(2)}, u32[]{:S(2)}) collective-permute-start(bf16[160,256]{1,0:T(8,128)(2,1)} %param.12), channel_id=1, source_target_pairs={{0,8},{1,9},{2,10},{3,11},{4,12},{5,13},{6,14},{7,15},{8,0},{9,1},... | collective-permute-start | bytes 245768 | tf_op jit(solution)/shard_map/ppermute | solution.py:292
  39.7 15.7 %collective-permute-start.7 = (bf16[160,256]{1,0:T(8,128)(2,1)}, bf16[160,256]{1,0:T(8,128)(2,1)S(1)}, u32[]{:S(2)}, u32[]{:S(2)}) collective-permute-start(bf16[160,256]{1,0:T(8,128)(2,1)} %param.12), channel_id=1, source_target_pairs={{0,12},{1,13},{2,14},{3,15},{4,0},{5,1},{6,2},{7,3},{8,4},{9,5},{1... | collective-permute-start | bytes 245768 | tf_op jit(solution)/shard_map/ppermute | solution.py:292
  53.4 12.1 %collective-permute-start.13 = (bf16[160,1152]{1,0:T(8,128)(2,1)S(1)}, bf16[160,1152]{1,0:T(8,128)(2,1)S(1)}, u32[]{:S(2)}, u32[]{:S(2)}) collective-permute-start(bf16[160,1152]{1,0:T(8,128)(2,1)S(1)} %get-tuple-element.163.refs_0_), channel_id=1, source_target_pairs={{4,8},{5,9},{6,10},{7,11},{8,4},{9,5},{10,6},{11,7},{20,24},{21,25... | collective-permute-start | bytes 1105928 | tf_op jit(solution)/shard_map/ppermute | solution.py:295
  54.1 11.9 %collective-permute-start.3 = (bf16[160,1152]{1,0:T(8,128)(2,1)S(1)}, bf16[160,1152]{1,0:T(8,128)(2,1)S(1)}, u32[]{:S(2)}, u32[]{:S(2)}) collective-permute-start(bf16[160,1152]{1,0:T(8,128)(2,1)S(1)} %collective-permute-done.2), channel_id=1, source_target_pairs={{4,0},{5,1},{6,2},{7,3},{8,12},{9,13},{10,14},{11,15},{20,16},{21,... | collective-permute-start | bytes 1105928 | tf_op jit(solution)/shard_map/ppermute | solution.py:295
  55.4 10.1 %collective-permute-start.8 = (bf16[640,256]{1,0:T(8,128)(2,1)S(1)}, bf16[640,256]{1,0:T(8,128)(2,1)}, u32[]{:S(2)}, u32[]{:S(2)}) collective-permute-start(bf16[640,256]{1,0:T(8,128)(2,1)S(1)} %constant_dynamic-update-slice_fusion.refs_0_), channel_id=1, source_target_pairs={{0,2},{1,3},{2,0},{3,1},{4,6},{5,7},{6,4},{7,5},{8,10},{9,11},{10,... | collective-permute-start | bytes 983048 | tf_op jit(solution)/shard_map/ppermute | solution.py:289
  57.8 24.4 %collective-permute-start.9 = (bf16[640,256]{1,0:T(8,128)(2,1)S(1)}, bf16[640,256]{1,0:T(8,128)(2,1)S(1)}, u32[]{:S(2)}, u32[]{:S(2)}) collective-permute-start(bf16[640,256]{1,0:T(8,128)(2,1)S(1)} %constant_dynamic-update-slice_fusion.refs_0_), channel_id=1, source_target_pairs={{0,1},{1,0},{2,3},{3,2},{4,5},{5,4},{6,7},{7,6},{8,9},{9,8},{10,11... | collective-permute-start | bytes 983048 | tf_op jit(solution)/shard_map/ppermute | solution.py:289
  57.8 27.2 %collective-permute-start.11 = (bf16[160,1152]{1,0:T(8,128)(2,1)S(1)}, bf16[160,1152]{1,0:T(8,128)(2,1)S(1)}, u32[]{:S(2)}, u32[]{:S(2)}) collective-permute-start(bf16[160,1152]{1,0:T(8,128)(2,1)S(1)} %get-tuple-element.163.refs_0_), channel_id=1, source_target_pairs={{0,2},{1,3},{2,0},{3,1},{4,6},{5,7},{6,4},{7,5},{8,10},{9,11},{10,... | collective-permute-start | bytes 1105928 | tf_op jit(solution)/shard_map/ppermute | solution.py:289
  65.5 38.4 %collective-permute-start.16 = (bf16[160,1152]{1,0:T(8,128)(2,1)S(1)}, bf16[160,1152]{1,0:T(8,128)(2,1)S(1)}, u32[]{:S(2)}, u32[]{:S(2)}) collective-permute-start(bf16[160,1152]{1,0:T(8,128)(2,1)S(1)} %get-tuple-element.163.refs_0_), channel_id=1, source_target_pairs={{0,1},{1,0},{2,3},{3,2},{4,5},{5,4},{6,7},{7,6},{8,9},{9,8},{10,11... | collective-permute-start | bytes 1105928 | tf_op jit(solution)/shard_map/ppermute | solution.py:289
  65.5 15.6 %copy-start.4 = (bf16[160,1152]{1,0:T(8,128)(2,1)}, bf16[160,1152]{1,0:T(8,128)(2,1)S(1)}, u32[]{:S(2)}) copy-start(bf16[160,1152]{1,0:T(8,128)(2,1)S(1)} %collective-permute-done.13) | copy-start | bytes 1105924
  65.5 19.4 %collective-permute-start.10 = (bf16[640,256]{1,0:T(8,128)(2,1)}, bf16[640,256]{1,0:T(8,128)(2,1)}, u32[]{:S(2)}, u32[]{:S(2)}) collective-permute-start(bf16[640,256]{1,0:T(8,128)(2,1)} %collective-permute-done.8.refs_1_), channel_id=1, source_target_pairs={{0,1},{1,0},{2,3},{3,2},{4,5},{5,4},{6,7},{7,6},{8,9},{9,8},{10,11... | collective-permute-start | bytes 983048 | tf_op jit(solution)/shard_map/ppermute | solution.py:289
  66.8 14.4 %collective-permute-start.14 = (bf16[160,1152]{1,0:T(8,128)(2,1)S(1)}, bf16[160,1152]{1,0:T(8,128)(2,1)}, u32[]{:S(2)}, u32[]{:S(2)}) collective-permute-start(bf16[160,1152]{1,0:T(8,128)(2,1)S(1)} %collective-permute-done.13), channel_id=1, source_target_pairs={{4,0},{5,1},{6,2},{7,3},{8,12},{9,13},{10,14},{11,15},{20,16},{21,... | collective-permute-start | bytes 1105928 | tf_op jit(solution)/shard_map/ppermute | solution.py:295
  69.1 23.5 %all-to-all-start.2 = ((bf16[16,16,256]{2,1,0:T(8,128)(2,1)}), bf16[16,16,256]{2,1,0:T(8,128)(2,1)S(1)}, u32[]{:S(2)}, u32[]{:S(2)}) async-start(bf16[16,16,256]{2,1,0:T(8,128)(2,1)} %bitcast.56), calls=%async_computation.2 | async-start | bytes 262144 | tf_op jit(solution)/shard_map/all_to_all | solution.py:330
  81.2 11.5 %collective-permute-start.4 = (bf16[160,1152]{1,0:T(8,128)(2,1)S(1)}, bf16[160,1152]{1,0:T(8,128)(2,1)S(1)}, u32[]{:S(2)}, u32[]{:S(2)}) collective-permute-start(bf16[160,1152]{1,0:T(8,128)(2,1)S(1)} %broadcast_select_fusion.3.refs_6_), channel_id=1, source_target_pairs={{0,2},{1,3},{2,0},{3,1},{4,6},{5,7},{6,4},{7,5},{8,10},{9,11},{10,... | collective-permute-start | bytes 1105928 | tf_op jit(solution)/shard_map/ppermute | solution.py:289
  82.9 21.0 %collective-permute-start.12 = (bf16[160,1152]{1,0:T(8,128)(2,1)S(1)}, bf16[160,1152]{1,0:T(8,128)(2,1)S(1)}, u32[]{:S(2)}, u32[]{:S(2)}) collective-permute-start(bf16[160,1152]{1,0:T(8,128)(2,1)S(1)} %collective-permute-done.1.refs_2_), channel_id=1, source_target_pairs={{0,2},{1,3},{2,0},{3,1},{4,6},{5,7},{6,4},{7,5},{8,10},{9,11},{10,... | collective-permute-start | bytes 1105928 | tf_op jit(solution)/shard_map/ppermute | solution.py:289
  85.0 20.8 %collective-permute-start.18 = (bf16[160,1152]{1,0:T(8,128)(2,1)S(1)}, bf16[160,1152]{1,0:T(8,128)(2,1)}, u32[]{:S(2)}, u32[]{:S(2)}) collective-permute-start(bf16[160,1152]{1,0:T(8,128)(2,1)S(1)} %collective-permute-done.1.refs_2_), channel_id=1, source_target_pairs={{0,1},{1,0},{2,3},{3,2},{4,5},{5,4},{6,7},{7,6},{8,9},{9,8},{10,11... | collective-permute-start | bytes 1105928 | tf_op jit(solution)/shard_map/ppermute | solution.py:289
  85.0 19.5 %collective-permute-start.17 = (bf16[160,1152]{1,0:T(8,128)(2,1)S(1)}, bf16[160,1152]{1,0:T(8,128)(2,1)}, u32[]{:S(2)}, u32[]{:S(2)}) collective-permute-start(bf16[160,1152]{1,0:T(8,128)(2,1)S(1)} %collective-permute-done.11.refs_1_), channel_id=1, source_target_pairs={{0,1},{1,0},{2,3},{3,2},{4,5},{5,4},{6,7},{7,6},{8,9},{9,8},{10,11... | collective-permute-start | bytes 1105928 | tf_op jit(solution)/shard_map/ppermute | solution.py:289
  92.7 13.1 %collective-permute-start.15 = (bf16[160,1152]{1,0:T(8,128)(2,1)S(1)}, bf16[160,1152]{1,0:T(8,128)(2,1)}, u32[]{:S(2)}, u32[]{:S(2)}) collective-permute-start(bf16[160,1152]{1,0:T(8,128)(2,1)S(1)} %broadcast_select_fusion.2.refs_4_), channel_id=1, source_target_pairs={{0,2},{1,3},{2,0},{3,1},{4,6},{5,7},{6,4},{7,5},{8,10},{9,11},{10,... | collective-permute-start | bytes 1105928 | tf_op jit(solution)/shard_map/ppermute | solution.py:289
  92.7 1.0 copy-start.1
  102.8 1.1 copy-start.2
  103.9 4.1 %collective-permute-start.20 = (bf16[160,1152]{1,0:T(8,128)(2,1)S(1)}, bf16[160,1152]{1,0:T(8,128)(2,1)S(1)}, u32[]{:S(2)}, u32[]{:S(2)}) collective-permute-start(bf16[160,1152]{1,0:T(8,128)(2,1)S(1)} %broadcast_select_fusion.2.refs_4_), channel_id=1, source_target_pairs={{0,1},{1,0},{2,3},{3,2},{4,5},{5,4},{6,7},{7,6},{8,9},{9,8},{10,11... | collective-permute-start | bytes 1105928 | tf_op jit(solution)/shard_map/ppermute | solution.py:289
  103.9 4.1 %collective-permute-start.19 = (bf16[160,1152]{1,0:T(8,128)(2,1)S(1)}, bf16[160,1152]{1,0:T(8,128)(2,1)}, u32[]{:S(2)}, u32[]{:S(2)}) collective-permute-start(bf16[160,1152]{1,0:T(8,128)(2,1)S(1)} %collective-permute-done.12.refs_3_), channel_id=1, source_target_pairs={{0,1},{1,0},{2,3},{3,2},{4,5},{5,4},{6,7},{7,6},{8,9},{9,8},{10,11... | collective-permute-start | bytes 1105928 | tf_op jit(solution)/shard_map/ppermute | solution.py:289
  104.4 3.8 %collective-permute-start.22 = (bf16[160,1152]{1,0:T(8,128)(2,1)S(1)}, bf16[160,1152]{1,0:T(8,128)(2,1)}, u32[]{:S(2)}, u32[]{:S(2)}) collective-permute-start(bf16[160,1152]{1,0:T(8,128)(2,1)S(1)} %broadcast_select_fusion.3.refs_6_), channel_id=1, source_target_pairs={{0,1},{1,0},{2,3},{3,2},{4,5},{5,4},{6,7},{7,6},{8,9},{9,8},{10,11... | collective-permute-start | bytes 1105928 | tf_op jit(solution)/shard_map/ppermute | solution.py:289
  105.8 2.5 %collective-permute-start.21 = (bf16[160,1152]{1,0:T(8,128)(2,1)}, bf16[160,1152]{1,0:T(8,128)(2,1)}, u32[]{:S(2)}, u32[]{:S(2)}) collective-permute-start(bf16[160,1152]{1,0:T(8,128)(2,1)} %collective-permute-done.15.refs_5_), channel_id=1, source_target_pairs={{0,1},{1,0},{2,3},{3,2},{4,5},{5,4},{6,7},{7,6},{8,9},{9,8},{10,11... | collective-permute-start | bytes 1105928 | tf_op jit(solution)/shard_map/ppermute | solution.py:289
  105.8 2.5 %collective-permute-start.23 = (bf16[160,1152]{1,0:T(8,128)(2,1)S(1)}, bf16[160,1152]{1,0:T(8,128)(2,1)}, u32[]{:S(2)}, u32[]{:S(2)}) collective-permute-start(bf16[160,1152]{1,0:T(8,128)(2,1)S(1)} %collective-permute-done.4.refs_7_), channel_id=1, source_target_pairs={{0,1},{1,0},{2,3},{3,2},{4,5},{5,4},{6,7},{7,6},{8,9},{9,8},{10,11... | collective-permute-start | bytes 1105928 | tf_op jit(solution)/shard_map/ppermute | solution.py:289
  107.9 10.4 %copy-start.7 = (s32[8,2]{0,1:T(2,128)S(1)}, s32[8,2]{0,1:T(2,128)}, u32[]{:S(2)}) copy-start(s32[8,2]{0,1:T(2,128)} %param.9) | copy-start | bytes 196
  107.9 10.4 %copy-start.8 = (u32[32]{0:T(128)S(1)}, u32[32]{0:T(128)}, u32[]{:S(2)}) copy-start(u32[32]{0:T(128)} %constant.256) | copy-start | bytes 388
  108.3 1.3 %copy-start.3 = (bf16[512,1280]{1,0:T(8,128)(2,1)S(1)}, bf16[512,1280]{1,0:T(8,128)(2,1)}, u32[]{:S(2)}) copy-start(bf16[512,1280]{1,0:T(8,128)(2,1)} %copy-done.2) | copy-start | bytes 3932164
  (2 other events, 1.5 us)

commit v3 on v0

--- a/solution.py
+++ b/solution.py
@@ -1,13 +1,21 @@
+import functools
 import math
 
 import jax
 import jax.numpy as jnp
 from jax import lax
+from jax.experimental import pallas as pl
+from jax.experimental.pallas import tpu as pltpu
 from jax.sharding import PartitionSpec as P
 
 EDGE = 16
 NOCC = 256
 BLK_DEV = 8
+LIVE_DEV = 4
+CAP = 128
+Z, Y, CORES = 4, 2, 2
+F32 = jnp.float32
+BF16 = jnp.bfloat16
 
 
 def padded_rows(matrix, starts, shell_size):
@@ -41,24 +49,376 @@
     return half
 
 
-def per_device(panels, block_pairs, block_count, shell_size, occ_coef, vir_coef):
-    all_pairs, all_counts = (
-        lax.all_gather(block_pairs, "shell", axis=0, tiled=True),
-        lax.all_gather(block_count, "shell", axis=0, tiled=True),
-    )
-    turned = lax.all_to_all(panels, "shell", split_axis=1, concat_axis=0, tiled=True)
+def long_way(turned, pairs, live, shell_size, occ_coef, vir_coef):
     occ_full = lax.all_gather(occ_coef, "shell", axis=0, tiled=True)
     starts = jnp.cumsum(shell_size) - shell_size
     occ_blocks = padded_rows(occ_full, starts, shell_size)
-    slot_total = turned.shape[0]
-    position = jnp.arange(slot_total, dtype=jnp.int32)
-    live = position % BLK_DEV < all_counts[position // BLK_DEV]
-    half = half_transform(turned, all_pairs, live, occ_blocks)
+    half = half_transform(turned, pairs, live, occ_blocks)
     hidden = half.astype(jnp.bfloat16)
     vir_full = lax.all_gather(vir_coef, "shell", axis=0, tiled=True)
     vir_blocks = padded_rows(vir_full, starts, shell_size)
     result = jnp.einsum("svin,sna->via", hidden, vir_blocks, preferred_element_type=jnp.float32)
     return result.astype(jnp.bfloat16)
+
+
+def from_start(panels, block_pairs, block_count, *rest):
+    pairs = lax.all_gather(block_pairs, "shell", axis=0, tiled=True)
+    counts = lax.all_gather(block_count, "shell", axis=0, tiled=True)
+    turned = lax.all_to_all(panels, "shell", split_axis=1, concat_axis=0, tiled=True)
+    position = jnp.arange(turned.shape[0], dtype=jnp.int32)
+    live = position % BLK_DEV < counts[position // BLK_DEV]
+    return long_way(turned, pairs, live, *rest)
+
+
+def iota(shape, dim):
+    return lax.broadcasted_iota(jnp.int32, shape, dim)
+
+
+def column_of(row, mask):
+    return jnp.sum(jnp.where(mask, row, 0.0), axis=1, keepdims=True)
+
+
+def row_of(column, mask):
+    return jnp.sum(jnp.where(mask, column, 0.0), axis=0, keepdims=True)
+
+
+def zero_one(mask):
+    return jnp.where(mask, 1.0, 0.0)
+
+
+def lane_value(row, index):
+    return jnp.sum(jnp.where(iota(row.shape, 1) == index, row, 0.0), axis=1, keepdims=True)
+
+
+def one_hots(ids, shells):
+    lanes = iota(ids.shape, 1).astype(F32)
+    return jnp.concatenate([zero_one(ids == lanes + 128.0 * k) for k in range(shells // 128)], axis=1)
+
+
+def slot_hots(got, shells):
+    ids = got[:, 2 * BLK_DEV :, :].reshape(-1, 256)
+    return one_hots(ids[:, :128], shells), one_hots(ids[:, 128:], shells)
+
+
+class Shells:
+    def __init__(self, size_row):
+        shells = size_row.shape[1]
+        sub, lane = iota((shells, shells), 0), iota((shells, shells), 1)
+        self.before, self.same = lane < sub, lane == sub
+        self.starts = column_of(size_row, self.before)
+        self.size = column_of(size_row, self.same)
+        self.odd = self.starts - 2.0 * jnp.floor(self.starts * 0.5)
+
+
+class Used:
+    def __init__(self, shells, hot, window):
+        self.used = column_of(jnp.max(hot, axis=0, keepdims=True), shells.same)
+        self.extra, self.ahead, self.edges = [], [], []
+        edge = (iota((hot.shape[1], 128), 1) * window).astype(F32)
+        reach = jnp.clip(edge - shells.starts, 0.0, shells.size)
+        for parity in range(2):
+            extra = 1.0 - shells.odd if parity == 0 else shells.odd
+            count = self.used * jnp.floor((shells.size + extra) * 0.5)
+            count_row = row_of(count, shells.same)
+            self.extra.append(extra)
+            self.ahead.append(column_of(count_row, shells.before))
+            self.edges.append(jnp.sum(self.used * jnp.floor((reach + extra) * 0.5), axis=0, keepdims=True))
+
+
+def pack_kernel(pairs_ref, count_ref, panels_ref, vir_ref, occ_ref, send_ref, *outs):
+    me = lax.axis_index("shell")
+    core, y = lax.rem(me, 2), lax.rem(lax.div(me, 2), 2)
+    here, nvir = vir_ref.shape
+    width, thin = nvir // CORES, occ_ref.shape[1] // CORES
+    for dy in range(2):
+        parity = lax.rem(y + dy, 2)
+        pick = zero_one(iota((here // 2, here), 1) == 2 * iota((here // 2, here), 0) + parity).astype(BF16)
+        for dc in range(2):
+            half = lax.rem(core + dc, 2)
+            out = outs[2 * dy + dc]
+            part = vir_ref[:, pl.ds(pl.multiple_of(half * width, 128), width)]
+            out[:, :width] = jnp.dot(pick, part, preferred_element_type=F32).astype(BF16)
+            part = occ_ref[:, pl.ds(pl.multiple_of(half * thin, 128), thin)]
+            out[:, width:] = jnp.dot(pick, part, preferred_element_type=F32).astype(BF16)
+    n = send_ref.shape[0]
+    turned = jnp.swapaxes(panels_ref[...].astype(F32), 0, 1)
+    send_ref[:, : 2 * BLK_DEV, :] = turned.reshape(n, 2 * BLK_DEV, EDGE * EDGE).astype(BF16)
+    slot, lane = iota((BLK_DEV, 256), 0), iota((BLK_DEV, 256), 1)
+    ids = jnp.zeros((BLK_DEV, 256), jnp.int32)
+    for g in range(BLK_DEV):
+        ids = jnp.where(slot == g, jnp.where(lane < 128, pairs_ref[g, 1], pairs_ref[g, 0]), ids)
+    ids = jnp.where(slot < count_ref[0], ids, -1).astype(F32)
+    send_ref[:, 2 * BLK_DEV :, :] = jnp.broadcast_to(ids[None], (n, BLK_DEV, 256)).astype(BF16)
+
+
+def pick_kernel(here, got_ref, size_ref, *refs):
+    sources, (out_ref, over_ref) = refs[:4], refs[4:]
+    me = lax.axis_index("shell")
+    core, y, z = lax.rem(me, 2), lax.rem(lax.div(me, 2), 2), lax.div(me, 4)
+    window = CORES * Y * here
+    shell_count = size_ref.shape[1]
+    got = got_ref[...].astype(F32)
+    shells = Shells(size_ref[...].astype(F32))
+    lists = [Used(shells, hot, window) for hot in slot_hots(got, shell_count)]
+    most = jnp.zeros((1, 1), F32)
+    lane = iota((1, 128), 1)
+    for chosen in lists:
+        for edges in chosen.edges:
+            later = jnp.concatenate([edges[:, 1:], edges[:, :1]], axis=1)
+            most = jnp.maximum(most, jnp.max(jnp.where(lane < Z, later - edges, 0.0), axis=1, keepdims=True))
+    over_ref[0] = jnp.where(jnp.max(most) > CAP, 1, 0).astype(jnp.int32)
+
+    width = vir_width = out_ref.shape[1] - 128
+    even = y == 0
+    totals = [jnp.zeros((CAP, width), F32), jnp.zeros((CAP, 128), F32)]
+    columns = [slice(0, vir_width), slice(vir_width, vir_width + 128)]
+    extra = jnp.where(even, lists[0].extra[0], lists[0].extra[1])
+    for k, source in enumerate(sources):
+        device = 4 * z + 2 * lax.rem(y + k // 2, 2) + lax.rem(core + k % 2, 2)
+        row = (2 * iota((shell_count, 128), 1) + device * here + y).astype(F32)
+        where = row - shells.starts
+        inside = (where >= 0.0) & (where < shells.size)
+        within = jnp.floor((where + extra) * 0.5)
+        for chosen, total, column in zip(lists, range(2), columns):
+            ahead = jnp.where(even, chosen.ahead[0], chosen.ahead[1])
+            base = lane_value(jnp.where(even, chosen.edges[0], chosen.edges[1]), z)
+            place = jnp.where(inside & (chosen.used > 0.0), ahead + within + 1.0, 0.0)
+            place = jnp.sum(place, axis=0, keepdims=True)
+            place = jnp.where(place > 0.0, place - 1.0 - base, -1.0)
+            hot = zero_one(place == iota((CAP, 128), 0).astype(F32)).astype(BF16)
+            totals[total] += jnp.dot(
+                hot[:, : here // 2], source[:, column], preferred_element_type=F32
+            )
+    for total, column in zip(totals, columns):
+        out_ref[:, column] = total.astype(BF16)
+
+
+def place_kernel(here, got_ref, size_ref, rows_ref, placed_ref):
+    window = CORES * Y * here
+    shell_count = size_ref.shape[1]
+    got = got_ref[...].astype(F32)
+    size_row = size_ref[...].astype(F32)
+    shells = Shells(size_row)
+    hots = slot_hots(got, shell_count)
+    lists = [Used(shells, hot, window) for hot in hots]
+    slots = hots[0].shape[0]
+    kept = LIVE_DEV * (slots // BLK_DEV)
+    alive = jnp.broadcast_to(jnp.sum(hots[0], axis=1, keepdims=True), (slots, slots))
+    sub, lane = iota((slots, slots), 0), iota((slots, slots), 1)
+    rank = row_of(alive, sub < lane)
+    alive_row = row_of(alive, sub == lane)
+    take = (rank == iota((kept, slots), 0).astype(F32)) & (alive_row > 0.0)
+    take = zero_one(take).astype(BF16)
+
+    def taken(array):
+        return jnp.dot(take, array.astype(BF16), preferred_element_type=F32)
+
+    def spread(hot, column):
+        value = jnp.sum(hot * row_of(column, shells.same), axis=1, keepdims=True)
+        wide = jnp.broadcast_to(value, (kept, 128)).reshape(kept, 1, 128)
+        return jnp.broadcast_to(wide, (kept, EDGE, 128)).reshape(kept * EDGE, 128)
+
+    at = iota((kept * EDGE, 128), 0) % EDGE
+    step = at.astype(F32)
+
+    def places(hot, chosen):
+        hot = taken(hot)
+        first, length = spread(hot, shells.starts), spread(hot, shells.size)
+        row = first + step
+        odd = (row - 2.0 * jnp.floor(row * 0.5)) > 0.0
+        place = jnp.where(odd, spread(hot, chosen.ahead[1]) + CAP, spread(hot, chosen.ahead[0]))
+        place += jnp.floor(step * 0.5)
+        for w in range(1, Z):
+            gap = [2.0 * CAP - (lane_value(e, w) - lane_value(e, w - 1)) for e in chosen.edges]
+            place += jnp.where(row >= float(window * w), jnp.where(odd, gap[1], gap[0]), 0.0)
+        return jnp.where(step < length, place, -1.0)[:, :1]
+
+    place_c, place_r = places(hots[0], lists[0]), places(hots[1], lists[1])
+    span = 16 * EDGE
+    width = rows_ref.shape[1]
+    s_in, l_in = iota((span, span), 0), iota((span, span), 1)
+    keep_m = (l_in // EDGE) == (s_in % EDGE)
+    fold = zero_one((s_in % EDGE) == (l_in % EDGE)).astype(BF16)
+    same_slot = (s_in // EDGE) == (l_in // EDGE)
+    blocks = [taken(got[:, p * BLK_DEV : (p + 1) * BLK_DEV, :].reshape(slots, span)) for p in range(2)]
+    lanes = iota((span, width), 1).astype(F32)
+    for g in range(kept // 16):
+        rows = slice(g * span, (g + 1) * span)
+        rows_ref[rows, :] = zero_one(place_r[rows] == lanes).astype(BF16)
+        c_hot = zero_one(place_c[rows] == lanes).astype(BF16)
+        for p in range(2):
+            block = blocks[p][g * 16 : (g + 1) * 16].reshape(16, 1, span)
+            block = jnp.broadcast_to(block, (16, EDGE, span)).reshape(span, span)
+            block = jnp.where(keep_m, block, 0.0).astype(BF16)
+            diag = jnp.dot(block, fold, preferred_element_type=F32)
+            diag = jnp.where(same_slot, diag, 0.0).astype(BF16)
+            placed_ref[p, rows, :] = jnp.dot(diag, c_hot, preferred_element_type=F32).astype(BF16)
+
+
+def last_kernel(count, me_ref, rows_ref, placed_ref, *refs):
+    pieces, (out_ref, vir_ref, occ_ref, half_ref, sems) = refs[: 2 * count], refs[2 * count :]
+    width = vir_ref.shape[2]
+    tile = out_ref.shape[2]
+    per = width // tile
+    core = lax.rem(me_ref[0], CORES)
+    chip = lax.div(me_ref[0], CORES)
+    j = pl.program_id(0)
+
+    def copies(far, part):
+        for k in range(count):
+            rows = pl.ds(pl.multiple_of((chip ^ k) * CAP, CAP), CAP)
+            columns = pl.ds(0, width) if part == 0 else pl.ds(width, 128)
+            target = vir_ref.at[far, rows, :] if part == 0 else occ_ref.at[far, rows, :]
+            yield pltpu.make_async_copy(
+                pieces[far * count + k].at[:, columns], target, sems.at[(2 * far + part) * count + k]
+            )
+
+    @pl.when(j == 0)
+    def _():
+        for far, part in ((0, 1), (1, 1), (0, 0), (1, 0)):
+            for copy in copies(far, part):
+                copy.start()
+        for far in range(2):
+            for copy in copies(far, 1):
+                copy.wait()
+        parts = [
+            jnp.dot(rows_ref[...], occ_ref[far], preferred_element_type=F32).astype(BF16) for far in range(2)
+        ]
+        for far in range(2):
+            half = jnp.where(far == 0, core, 1 - core)
+            for p in range(2):
+                piece = lax.dot_general(
+                    parts[far], placed_ref[p], (((0,), (0,)), ((), ())), preferred_element_type=F32
+                )
+                start = pl.multiple_of(p * NOCC + half * 128, 128)
+                half_ref[pl.ds(start, 128), :] = piece.astype(BF16)
+
+    for far in range(2):
+
+        @pl.when(j == far * per)
+        def _():
+            for copy in copies(far, 0):
+                copy.wait()
+
+    right = vir_ref[lax.div(j, per), :, pl.ds(pl.multiple_of(lax.rem(j, per) * tile, 128), tile)]
+    for p in range(2):
+        out_ref[p] = jnp.dot(half_ref[p * NOCC : (p + 1) * NOCC, :], right, preferred_element_type=F32).astype(BF16)
+
+
+VMEM = pl.BlockSpec(memory_space=pltpu.VMEM)
+SMEM = pl.BlockSpec(memory_space=pltpu.SMEM)
+ANY = pl.BlockSpec(memory_space=pl.ANY)
+
+
+def shape(*dims, dtype=BF16):
+    return jax.ShapeDtypeStruct(dims, dtype)
+
+
+def params(mib):
+    return pltpu.CompilerParams(vmem_limit_bytes=mib << 20)
+
+
+def cost(flops, nbytes):
+    return pl.CostEstimate(flops=int(flops), bytes_accessed=int(nbytes), transcendentals=0)
+
+
+def short_way(panels, block_pairs, block_count, shell_size, occ_coef, vir_coef):
+    n = lax.axis_size("shell")
+    here, nvir = vir_coef.shape
+    width = nvir // CORES
+    packed = width + NOCC // CORES
+    room = Z * Y * CAP
+    me = lax.axis_index("shell")
+    size_row = shell_size.reshape(1, -1)
+
+    def swap(array, bit):
+        return lax.ppermute(array, "shell", [(i, i ^ bit) for i in range(n)])
+
+    send, keep, to_core, to_y, to_both = pl.pallas_call(
+        pack_kernel,
+        out_shape=[shape(n, 3 * BLK_DEV, EDGE * EDGE)] + [shape(here // 2, packed)] * 4,
+        in_specs=[SMEM] * 2 + [VMEM] * 3,
+        out_specs=[VMEM] * 5,
+        compiler_params=params(32),
+        cost_estimate=cost(3e8, 3e6),
+        name="pack_rows",
+    )(block_pairs, block_count, panels, vir_coef, occ_coef)
+    fresh = [keep, swap(to_core, 1), swap(to_y, 2), swap(to_both, 3)]
+    got = lax.all_to_all(send, "shell", split_axis=0, concat_axis=0, tiled=True)
+
+    mine, over = pl.pallas_call(
+        functools.partial(pick_kernel, here),
+        out_shape=(shape(CAP, packed), shape(1, dtype=jnp.int32)),
+        in_specs=[VMEM] * 6,
+        out_specs=(VMEM, SMEM),
+        compiler_params=params(32),
+        cost_estimate=cost(3e8, 2e6),
+        name="pick_rows",
+    )(got, size_row, *fresh)
+
+    across, beside, mine_y = swap(mine, 8), swap(mine, 4), swap(mine, 2)
+    beside, mine_y, got_late = lax.optimization_barrier((beside, mine_y, got))
+    beside_y = swap(beside, 2)
+
+    rows, placed = pl.pallas_call(
+        functools.partial(place_kernel, here),
+        out_shape=(shape(LIVE_DEV * n * EDGE, room), shape(2, LIVE_DEV * n * EDGE, room)),
+        in_specs=[VMEM] * 2,
+        out_specs=(VMEM, VMEM),
+        compiler_params=params(32),
+        cost_estimate=cost(4e9, 8e6),
+        name="place_panels",
+    )(got_late, size_row)
+
+    across, beside_y, rows, placed = lax.optimization_barrier((across, beside_y, rows, placed))
+    corner, across_y = swap(across, 4), swap(across, 2)
+    corner, across_y = lax.optimization_barrier((corner, across_y))
+    corner_y = swap(corner, 2)
+    pieces = [mine, mine_y, beside, beside_y, across, across_y, corner, corner_y]
+    far = [swap(piece, 1) for piece in pieces]
+
+    tile = width // 3
+    count = len(pieces)
+    out = pl.pallas_call(
+        functools.partial(last_kernel, count),
+        out_shape=shape(2, NOCC, nvir),
+        grid_spec=pltpu.PrefetchScalarGridSpec(
+            num_scalar_prefetch=1,
+            grid=(nvir // tile,),
+            in_specs=[VMEM] * 2 + [ANY] * (2 * count),
+            out_specs=pl.BlockSpec((2, NOCC, tile), lambda j, o: (0, 0, (j + 3 * (o[0] % 2)) % 6)),
+            scratch_shapes=[
+                pltpu.VMEM((CORES, room, width), BF16),
+                pltpu.VMEM((CORES, room, 128), BF16),
+                pltpu.VMEM((2 * NOCC, room), BF16),
+                pltpu.SemaphoreType.DMA((4 * count,)),
+            ],
+        ),
+        compiler_params=params(32),
+        cost_estimate=cost(4e9, 1e7),
+        name="last_product",
+    )(me.reshape(1), rows, placed, *pieces, *far)
+    return out, over[0], got
+
+
+def per_device(*args):
+    n = lax.axis_size("shell")
+    here, nvir = args[5].shape
+    sparse = LIVE_DEV * n * EDGE < n * here
+    if not (sparse and n == Z * Y * CORES and here <= 256 and here % 16 == 0 and nvir % 768 == 0):
+        return from_start(*args)
+    out, over, got = short_way(*args)
+
+    def again(carry):
+        over, _ = carry
+        over, got_now, *held = lax.optimization_barrier((over, got, *args[3:]))
+        turned = got_now[:, : 2 * BLK_DEV].reshape(n, 2, BLK_DEV, EDGE * EDGE).swapaxes(1, 2)
+        turned = turned.reshape(n * BLK_DEV, 2, EDGE * EDGE)
+        ids = got_now[:, 2 * BLK_DEV :].reshape(n * BLK_DEV, 256)
+        pairs = jnp.stack([ids[:, 128], ids[:, 0]], axis=1).astype(jnp.int32)
+        return over - 1, long_way(turned, jnp.maximum(pairs, 0), pairs[:, 1] >= 0, *held)
+
+    return lax.while_loop(lambda carry: carry[0] > 0, again, (over, out))[1]
 
 
 def solution(mesh):

time: 217 us -> 98.5 us (0.45)
  local copies, waits for them, and re-layouts: 67.8 us -> 8.68 us
  other arithmetic: 34.8 us -> 0 us
  blocking collectives: 30.6 us -> 0 us
  matrix products: 22 us -> 0 us
  Pallas kernels: 0 us -> 18 us
  starting transfers between devices: 7.43 us -> 19.2 us
    gather x4 -> x0, local copies, waits for them, and re-layouts: 58.6 us -> none  [the longest x2 55.7 us: padded_rows(): matrix[rows]]
    all_gather x2 -> x0, waiting for transfers between devices: 37.8 us -> none  [the longest x1 37.8 us: per_device(): vir_full = lax.all_gather(vir_coef, 'shell', axis=0, tiled=True)]
    ppermute x0 -> x18, waiting for transfers between devices: none -> 37.3 us  [swap(): return lax.ppermute(array, 'shell', [(i, i ^ bit) for i in range(n)])]
    dot_general x2 -> x0, matrix products: 22 us -> none  [the longest x1 19 us: per_device(): jnp.einsum('svin,sna->via', hidden, vir_blocks, preferred_element_type=jn...]
    scatter-add x1 -> x0, other arithmetic: 20.6 us -> none  [advance(): return (total.at[col_shell].add(piece), None)]
    all_gather x1 -> x0, blocking collectives: 18.3 us -> none  [per_device(): lax.all_gather(block_pairs, 'shell', axis=0, tiled=True)]
    pallas_call x0 -> x4, Pallas kernels: none -> 18 us  [the longest x1 8.95 us: short_way(): pl.pallas_call(functools.partial(last_kernel, count), out_shape=shape(2,...]
    unnamed x1 -> x0, blocking collectives: 12.4 us -> none
  transfers between devices with their start and end apart: 3 -> 19, of which waited for: 1 -> 8; matrix products, arithmetic and copies ran while one was open for 30% -> 0% of each run, Pallas kernels for 0% -> 5%
where the time goes in v3:
time: 98.5 us; the launch traced here: 98.1 us
  waiting for transfers between devices  37.3 us (38%)
  starting transfers between devices  19.2 us (19%)
  Pallas kernels  18 us (18%)
  between operations  14.1 us (14%)
  local copies, waits for them, and re-layouts  8.68 us (9%)
    ppermute x18, waiting for transfers between devices, swap(): return lax.ppermute(array, 'shell', [(i, i ^ bit) for i in range(n)])  37.3 us
    ppermute x18, starting transfers between devices, swap(): return lax.ppermute(array, 'shell', [(i, i ^ bit) for i in range(n)])  11.8 us
    pallas_call x1, Pallas kernels, short_way(): pl.pallas_call(functools.partial(last_kernel, count), out_shape=shape(2,...  8.95 us
    unnamed x13, local copies, waits for them, and re-layouts  8.68 us
    all_to_all x1, starting transfers between devices, short_way(): got = lax.all_to_all(send, 'shell', split_axis=0, concat_axis=0, tiled=True)  7.39 us
    pallas_call x1, Pallas kernels, short_way(): pl.pallas_call(functools.partial(place_kernel, here), out_shape=(shape(LI...  4.73 us
    pallas_call x1, Pallas kernels, short_way(): pl.pallas_call(pack_kernel, out_shape=[shape(n, 3 * BLK_DEV, EDGE * EDGE)...  2.24 us
    pallas_call x1, Pallas kernels, short_way(): pl.pallas_call(functools.partial(pick_kernel, here), out_shape=(shape(CAP...  2.08 us
  transfers between devices with their start and end apart: 19, of which 8 were waited for; matrix products, arithmetic and copies ran while one was open for 0% of the time, Pallas kernels for 5%

profile of v3, /device:TPU:0, one launch (start us, length us, event | category | flops | bytes accessed | tf_op | source)
XLA Modules:
  0.0 98.1 jit_solution(1094944782450948534)
XLA Ops:
  6.5 0.8 copy.24.pairs_ref
  8.0 0.9 copy-done
  8.8 2.2 %pack_rows.1 = (bf16[16,24,256]{2,1,0:T(8,128)(2,1)}, bf16[80,1280]{1,0:T(8,128)(2,1)S(1)}, bf16[80,1280]{1,0:T(8,128)(2,1)S(1)}, bf16[80,1280]{1,0:T(8,128)(2,1)S(1)}, bf16[80,1280]{1,0:T(8,128)(2,1)S(1)}) custom-call(s32[8,2]{1,0:T(8,128)S(1)} %copy.24.pairs_ref, s32[1]{0:T(128)S(6)} %copy.46.count_ref, bf16[8,32,256]{2,1,0:T(8,128)(2,1)S(1)} %copy-done, ...), custom_call_target="tpu_custom_call" | custom-call | flops 300000000 | bytes 3000000 | tf_op jit(solution)/shard_map/pack_rows/pallas_call | solution.py:337
  11.1 7.4 %all-to-all-start = ((bf16[16,24,256]{2,1,0:T(8,128)(2,1)}), bf16[16,24,256]{2,1,0:T(8,128)(2,1)S(1)}, u32[]{:S(2)}, u32[]{:S(2)}) async-start(bf16[16,24,256]{2,1,0:T(8,128)(2,1)} %get-tuple-element.119), calls=%async_computation | async-start | bytes 393216 | tf_op jit(solution)/shard_map/all_to_all | solution.py:347
  18.5 0.4 collective-permute-start
  18.9 1.7 %collective-permute-start.1 = (bf16[80,1280]{1,0:T(8,128)(2,1)S(1)}, bf16[80,1280]{1,0:T(8,128)(2,1)S(1)}, u32[]{:S(2)}, u32[]{:S(2)}) collective-permute-start(bf16[80,1280]{1,0:T(8,128)(2,1)S(1)} %get-tuple-element.122), channel_id=1, source_target_pairs={{0,2},{1,3},{2,0},{3,1},{4,6},{5,7},{6,4},{7,5},{8,10},{9,11},{10,... | collective-permute-start | bytes 614408 | tf_op jit(solution)/shard_map/ppermute | solution.py:335
  20.6 8.0 %collective-permute-done.1.refs_2_ = bf16[80,1280]{1,0:T(8,128)(2,1)S(1)} collective-permute-done((bf16[80,1280]{1,0:T(8,128)(2,1)S(1)}, bf16[80,1280]{1,0:T(8,128)(2,1)S(1)}, u32[]{:S(2)}, u32[]{:S(2)}) %collective-permute-start.1) | collective-permute-done | bytes 204832 | tf_op jit(solution)/shard_map/ppermute | solution.py:335
  28.6 3.4 %collective-permute-done.2.refs_3_ = bf16[80,1280]{1,0:T(8,128)(2,1)S(1)} collective-permute-done((bf16[80,1280]{1,0:T(8,128)(2,1)S(1)}, bf16[80,1280]{1,0:T(8,128)(2,1)S(1)}, u32[]{:S(2)}, u32[]{:S(2)}) %collective-permute-start.2) | collective-permute-done | bytes 204832 | tf_op jit(solution)/shard_map/ppermute | solution.py:335
  32.0 2.1 %pick_rows.1 = (bf16[128,1280]{1,0:T(8,128)(2,1)S(1)}, s32[1]{0:T(128)}) custom-call(bf16[16,24,256]{2,1,0:T(8,128)(2,1)S(1)} %all-to-all-done.got_ref, s32[1,256]{1,0:T(1,128)} %bitcast.72, bf16[80,1280]{1,0:T(8,128)(2,1)S(1)} %get-tuple-element.120.refs_0_, bf16[80,1280]{1,0:T(8,128)(2,1)S(1)} %collective-permute-done.refs_1_, ...), custom_call_target="tpu_custom_call" | custom-call | flops 300000000 | bytes 2000000 | tf_op jit(solution)/shard_map/pick_rows/pallas_call | solution.py:349
  34.1 1.8 %collective-permute-start.4 = (bf16[128,1280]{1,0:T(8,128)(2,1)S(1)}, bf16[128,1280]{1,0:T(8,128)(2,1)S(1)}, u32[]{:S(2)}, u32[]{:S(2)}) collective-permute-start(bf16[128,1280]{1,0:T(8,128)(2,1)S(1)} %get-tuple-element.125.refs_0_), channel_id=1, source_target_pairs={{0,4},{1,5},{2,6},{3,7},{4,0},{5,1},{6,2},{7,3},{8,12},{9,13},{10,... | collective-permute-start | bytes 983048 | tf_op jit(solution)/shard_map/ppermute | solution.py:335
  35.9 0.9 collective-permute-start.5
  36.8 2.3 %collective-permute-start.3 = (bf16[128,1280]{1,0:T(8,128)(2,1)S(1)}, bf16[128,1280]{1,0:T(8,128)(2,1)S(1)}, u32[]{:S(2)}, u32[]{:S(2)}) collective-permute-start(bf16[128,1280]{1,0:T(8,128)(2,1)S(1)} %get-tuple-element.125.refs_0_), channel_id=1, source_target_pairs={{0,8},{1,9},{2,10},{3,11},{4,12},{5,13},{6,14},{7,15},{8,0},{9,1},... | collective-permute-start | bytes 983048 | tf_op jit(solution)/shard_map/ppermute | solution.py:335
  39.1 11.0 %collective-permute-done.4.refs_2_ = bf16[128,1280]{1,0:T(8,128)(2,1)S(1)} collective-permute-done((bf16[128,1280]{1,0:T(8,128)(2,1)S(1)}, bf16[128,1280]{1,0:T(8,128)(2,1)S(1)}, u32[]{:S(2)}, u32[]{:S(2)}) %collective-permute-start.4) | collective-permute-done | bytes 327712 | tf_op jit(solution)/shard_map/ppermute | solution.py:335
  50.1 1.0 %collective-permute-start.6 = (bf16[128,1280]{1,0:T(8,128)(2,1)S(1)}, bf16[128,1280]{1,0:T(8,128)(2,1)S(1)}, u32[]{:S(2)}, u32[]{:S(2)}) collective-permute-start(bf16[128,1280]{1,0:T(8,128)(2,1)S(1)} %collective-permute-done.4.refs_2_), channel_id=1, source_target_pairs={{0,2},{1,3},{2,0},{3,1},{4,6},{5,7},{6,4},{7,5},{8,10},{9,11},{10,... | collective-permute-start | bytes 983048 | tf_op jit(solution)/shard_map/ppermute | solution.py:335
  51.2 4.7 %place_panels.1 = (bf16[1024,1024]{1,0:T(8,128)(2,1)S(1)}, bf16[2,1024,1024]{2,1,0:T(8,128)(2,1)S(1)}) custom-call(bf16[16,24,256]{2,1,0:T(8,128)(2,1)S(1)} %all-to-all-done.got_ref, s32[1,256]{1,0:T(1,128)} %bitcast.73), custom_call_target="tpu_custom_call" | custom-call | flops 4000000000 | bytes 8000000 | tf_op jit(solution)/shard_map/place_panels/pallas_call | solution.py:363
  55.9 1.9 %copy-done.1 = bf16[2,1024,1024]{2,1,0:T(8,128)(2,1)} copy-done((bf16[2,1024,1024]{2,1,0:T(8,128)(2,1)}, bf16[2,1024,1024]{2,1,0:T(8,128)(2,1)S(1)}, u32[]{:S(2)}) %copy-start.1) | copy-done | bytes 4194328
  57.8 1.3 %copy-done.3 = bf16[1024,1024]{1,0:T(8,128)(2,1)} copy-done((bf16[1024,1024]{1,0:T(8,128)(2,1)}, bf16[1024,1024]{1,0:T(8,128)(2,1)S(1)}, u32[]{:S(2)}) %copy-start.3) | copy-done | bytes 2097176
  59.1 0.1 collective-permute-done.6.refs_3_
  59.2 1.0 %collective-permute-start.8 = (bf16[128,1280]{1,0:T(8,128)(2,1)S(1)}, bf16[128,1280]{1,0:T(8,128)(2,1)S(1)}, u32[]{:S(2)}, u32[]{:S(2)}) collective-permute-start(bf16[128,1280]{1,0:T(8,128)(2,1)S(1)} %collective-permute-done.3.refs_4_), channel_id=1, source_target_pairs={{0,2},{1,3},{2,0},{3,1},{4,6},{5,7},{6,4},{7,5},{8,10},{9,11},{10,... | collective-permute-start | bytes 983048 | tf_op jit(solution)/shard_map/ppermute | solution.py:335
  60.3 0.5 collective-permute-start.12
  60.8 7.1 %collective-permute-done.7.refs_6_ = bf16[128,1280]{1,0:T(8,128)(2,1)S(1)} collective-permute-done((bf16[128,1280]{1,0:T(8,128)(2,1)S(1)}, bf16[128,1280]{1,0:T(8,128)(2,1)S(1)}, u32[]{:S(2)}, u32[]{:S(2)}) %collective-permute-start.7) | collective-permute-done | bytes 327712 | tf_op jit(solution)/shard_map/ppermute | solution.py:335
  67.8 0.1 collective-permute-done.8.refs_5_
  67.9 1.2 %collective-permute-start.9 = (bf16[128,1280]{1,0:T(8,128)(2,1)S(1)}, bf16[128,1280]{1,0:T(8,128)(2,1)}, u32[]{:S(2)}, u32[]{:S(2)}) collective-permute-start(bf16[128,1280]{1,0:T(8,128)(2,1)S(1)} %collective-permute-done.7.refs_6_), channel_id=1, source_target_pairs={{0,2},{1,3},{2,0},{3,1},{4,6},{5,7},{6,4},{7,5},{8,10},{9,11},{10,... | collective-permute-start | bytes 983048 | tf_op jit(solution)/shard_map/ppermute | solution.py:335
  69.1 0.5 collective-permute-start.13
  69.6 0.1 collective-permute-start.16
  69.7 0.4 collective-permute-start.15
  70.1 5.6 %collective-permute-done.9.refs_7_ = bf16[128,1280]{1,0:T(8,128)(2,1)} collective-permute-done((bf16[128,1280]{1,0:T(8,128)(2,1)S(1)}, bf16[128,1280]{1,0:T(8,128)(2,1)}, u32[]{:S(2)}, u32[]{:S(2)}) %collective-permute-start.9) | collective-permute-done | bytes 327712 | tf_op jit(solution)/shard_map/ppermute | solution.py:335
  75.8 1.9 %collective-permute-done.17.refs_15_ = bf16[128,1280]{1,0:T(8,128)(2,1)} collective-permute-done((bf16[128,1280]{1,0:T(8,128)(2,1)}, bf16[128,1280]{1,0:T(8,128)(2,1)}, u32[]{:S(2)}, u32[]{:S(2)}) %collective-permute-start.17) | collective-permute-done | bytes 327712 | tf_op jit(solution)/shard_map/ppermute | solution.py:335
  77.7 2.2 %copy-done.2 = bf16[2,1024,1024]{2,1,0:T(8,128)(2,1)S(1)} copy-done((bf16[2,1024,1024]{2,1,0:T(8,128)(2,1)S(1)}, bf16[2,1024,1024]{2,1,0:T(8,128)(2,1)}, u32[]{:S(2)}) %copy-start.2) | copy-done | bytes 4194328
  79.9 1.6 %copy-done.4 = bf16[1024,1024]{1,0:T(8,128)(2,1)S(1)} copy-done((bf16[1024,1024]{1,0:T(8,128)(2,1)S(1)}, bf16[1024,1024]{1,0:T(8,128)(2,1)}, u32[]{:S(2)}) %copy-start.4) | copy-done | bytes 2097176
  81.5 9.0 %last_product.1 = bf16[2,256,2304]{2,1,0:T(8,128)(2,1)} custom-call(s32[1]{0:T(128)} %bitcast.18.me_ref, bf16[1024,1024]{1,0:T(8,128)(2,1)S(1)} %copy-done.4, bf16[2,1024,1024]{2,1,0:T(8,128)(2,1)S(1)} %copy-done.2, bf16[128,1280]{1,0:T(8,128)(2,1)S(1)} %get-tuple-element.125.refs_0_, bf16[128,1280]{1,0:T(8,128)(2,1)S(1)} %collective-permute-done.5.refs_1_, ...), custom_call_target="tpu_custom_call" | custom-call | flops 4000000000 | bytes 10000000 | tf_op jit(solution)/shard_map/last_product/pallas_call | solution.py:382
  90.5 0.8 while.16
  (24 shorter events, 0.1 us)
Async XLA Ops:
  7.9 0.9 copy-start
  11.1 20.9 %all-to-all-start = ((bf16[16,24,256]{2,1,0:T(8,128)(2,1)}), bf16[16,24,256]{2,1,0:T(8,128)(2,1)S(1)}, u32[]{:S(2)}, u32[]{:S(2)}) async-start(bf16[16,24,256]{2,1,0:T(8,128)(2,1)} %get-tuple-element.119), calls=%async_computation | async-start | bytes 393216 | tf_op jit(solution)/shard_map/all_to_all | solution.py:347
  18.5 2.1 %collective-permute-start = (bf16[80,1280]{1,0:T(8,128)(2,1)S(1)}, bf16[80,1280]{1,0:T(8,128)(2,1)S(1)}, u32[]{:S(2)}, u32[]{:S(2)}) collective-permute-start(bf16[80,1280]{1,0:T(8,128)(2,1)S(1)} %get-tuple-element.121), channel_id=1, source_target_pairs={{0,1},{1,0},{2,3},{3,2},{4,5},{5,4},{6,7},{7,6},{8,9},{9,8},{10,11... | collective-permute-start | bytes 614408 | tf_op jit(solution)/shard_map/ppermute | solution.py:335
  18.9 9.7 %collective-permute-start.1 = (bf16[80,1280]{1,0:T(8,128)(2,1)S(1)}, bf16[80,1280]{1,0:T(8,128)(2,1)S(1)}, u32[]{:S(2)}, u32[]{:S(2)}) collective-permute-start(bf16[80,1280]{1,0:T(8,128)(2,1)S(1)} %get-tuple-element.122), channel_id=1, source_target_pairs={{0,2},{1,3},{2,0},{3,1},{4,6},{5,7},{6,4},{7,5},{8,10},{9,11},{10,... | collective-permute-start | bytes 614408 | tf_op jit(solution)/shard_map/ppermute | solution.py:335
  20.6 11.4 %collective-permute-start.2 = (bf16[80,1280]{1,0:T(8,128)(2,1)S(1)}, bf16[80,1280]{1,0:T(8,128)(2,1)S(1)}, u32[]{:S(2)}, u32[]{:S(2)}) collective-permute-start(bf16[80,1280]{1,0:T(8,128)(2,1)S(1)} %get-tuple-element.123), channel_id=1, source_target_pairs={{0,3},{1,2},{2,1},{3,0},{4,7},{5,6},{6,5},{7,4},{8,11},{9,10},{10,... | collective-permute-start | bytes 614408 | tf_op jit(solution)/shard_map/ppermute | solution.py:335
  34.1 16.0 %collective-permute-start.4 = (bf16[128,1280]{1,0:T(8,128)(2,1)S(1)}, bf16[128,1280]{1,0:T(8,128)(2,1)S(1)}, u32[]{:S(2)}, u32[]{:S(2)}) collective-permute-start(bf16[128,1280]{1,0:T(8,128)(2,1)S(1)} %get-tuple-element.125.refs_0_), channel_id=1, source_target_pairs={{0,4},{1,5},{2,6},{3,7},{4,0},{5,1},{6,2},{7,3},{8,12},{9,13},{10,... | collective-permute-start | bytes 983048 | tf_op jit(solution)/shard_map/ppermute | solution.py:335
  35.9 14.2 %collective-permute-start.5 = (bf16[128,1280]{1,0:T(8,128)(2,1)S(1)}, bf16[128,1280]{1,0:T(8,128)(2,1)S(1)}, u32[]{:S(2)}, u32[]{:S(2)}) collective-permute-start(bf16[128,1280]{1,0:T(8,128)(2,1)S(1)} %get-tuple-element.125.refs_0_), channel_id=1, source_target_pairs={{0,2},{1,3},{2,0},{3,1},{4,6},{5,7},{6,4},{7,5},{8,10},{9,11},{10,... | collective-permute-start | bytes 983048 | tf_op jit(solution)/shard_map/ppermute | solution.py:335
  36.8 22.3 %collective-permute-start.3 = (bf16[128,1280]{1,0:T(8,128)(2,1)S(1)}, bf16[128,1280]{1,0:T(8,128)(2,1)S(1)}, u32[]{:S(2)}, u32[]{:S(2)}) collective-permute-start(bf16[128,1280]{1,0:T(8,128)(2,1)S(1)} %get-tuple-element.125.refs_0_), channel_id=1, source_target_pairs={{0,8},{1,9},{2,10},{3,11},{4,12},{5,13},{6,14},{7,15},{8,0},{9,1},... | collective-permute-start | bytes 983048 | tf_op jit(solution)/shard_map/ppermute | solution.py:335
  50.1 9.1 %collective-permute-start.6 = (bf16[128,1280]{1,0:T(8,128)(2,1)S(1)}, bf16[128,1280]{1,0:T(8,128)(2,1)S(1)}, u32[]{:S(2)}, u32[]{:S(2)}) collective-permute-start(bf16[128,1280]{1,0:T(8,128)(2,1)S(1)} %collective-permute-done.4.refs_2_), channel_id=1, source_target_pairs={{0,2},{1,3},{2,0},{3,1},{4,6},{5,7},{6,4},{7,5},{8,10},{9,11},{10,... | collective-permute-start | bytes 983048 | tf_op jit(solution)/shard_map/ppermute | solution.py:335
  55.9 1.9 %copy-start.1 = (bf16[2,1024,1024]{2,1,0:T(8,128)(2,1)}, bf16[2,1024,1024]{2,1,0:T(8,128)(2,1)S(1)}, u32[]{:S(2)}) copy-start(bf16[2,1024,1024]{2,1,0:T(8,128)(2,1)S(1)} %get-tuple-element.131.placed_ref) | copy-start | bytes 12582916
  57.8 1.3 %copy-start.3 = (bf16[1024,1024]{1,0:T(8,128)(2,1)}, bf16[1024,1024]{1,0:T(8,128)(2,1)S(1)}, u32[]{:S(2)}) copy-start(bf16[1024,1024]{1,0:T(8,128)(2,1)S(1)} %get-tuple-element.130.rows_ref) | copy-start | bytes 6291460
  59.2 8.6 %collective-permute-start.7 = (bf16[128,1280]{1,0:T(8,128)(2,1)S(1)}, bf16[128,1280]{1,0:T(8,128)(2,1)S(1)}, u32[]{:S(2)}, u32[]{:S(2)}) collective-permute-start(bf16[128,1280]{1,0:T(8,128)(2,1)S(1)} %collective-permute-done.3.refs_4_), channel_id=1, source_target_pairs={{0,4},{1,5},{2,6},{3,7},{4,0},{5,1},{6,2},{7,3},{8,12},{9,13},{10,... | collective-permute-start | bytes 983048 | tf_op jit(solution)/shard_map/ppermute | solution.py:335
  59.2 8.7 %collective-permute-start.8 = (bf16[128,1280]{1,0:T(8,128)(2,1)S(1)}, bf16[128,1280]{1,0:T(8,128)(2,1)S(1)}, u32[]{:S(2)}, u32[]{:S(2)}) collective-permute-start(bf16[128,1280]{1,0:T(8,128)(2,1)S(1)} %collective-permute-done.3.refs_4_), channel_id=1, source_target_pairs={{0,2},{1,3},{2,0},{3,1},{4,6},{5,7},{6,4},{7,5},{8,10},{9,11},{10,... | collective-permute-start | bytes 983048 | tf_op jit(solution)/shard_map/ppermute | solution.py:335
  60.3 8.8 %collective-permute-start.10 = (bf16[128,1280]{1,0:T(8,128)(2,1)S(1)}, bf16[128,1280]{1,0:T(8,128)(2,1)S(1)}, u32[]{:S(2)}, u32[]{:S(2)}) collective-permute-start(bf16[128,1280]{1,0:T(8,128)(2,1)S(1)} %get-tuple-element.125.refs_0_), channel_id=1, source_target_pairs={{0,1},{1,0},{2,3},{3,2},{4,5},{5,4},{6,7},{7,6},{8,9},{9,8},{10,11... | collective-permute-start | bytes 983048 | tf_op jit(solution)/shard_map/ppermute | solution.py:335
  60.3 9.3 %collective-permute-start.12 = (bf16[128,1280]{1,0:T(8,128)(2,1)S(1)}, bf16[128,1280]{1,0:T(8,128)(2,1)S(1)}, u32[]{:S(2)}, u32[]{:S(2)}) collective-permute-start(bf16[128,1280]{1,0:T(8,128)(2,1)S(1)} %collective-permute-done.4.refs_2_), channel_id=1, source_target_pairs={{0,1},{1,0},{2,3},{3,2},{4,5},{5,4},{6,7},{7,6},{8,9},{9,8},{10,11... | collective-permute-start | bytes 983048 | tf_op jit(solution)/shard_map/ppermute | solution.py:335
  60.8 8.9 %collective-permute-start.11 = (bf16[128,1280]{1,0:T(8,128)(2,1)S(1)}, bf16[128,1280]{1,0:T(8,128)(2,1)S(1)}, u32[]{:S(2)}, u32[]{:S(2)}) collective-permute-start(bf16[128,1280]{1,0:T(8,128)(2,1)S(1)} %collective-permute-done.5.refs_1_), channel_id=1, source_target_pairs={{0,1},{1,0},{2,3},{3,2},{4,5},{5,4},{6,7},{7,6},{8,9},{9,8},{10,11... | collective-permute-start | bytes 983048 | tf_op jit(solution)/shard_map/ppermute | solution.py:335
  67.9 7.8 %collective-permute-start.9 = (bf16[128,1280]{1,0:T(8,128)(2,1)S(1)}, bf16[128,1280]{1,0:T(8,128)(2,1)}, u32[]{:S(2)}, u32[]{:S(2)}) collective-permute-start(bf16[128,1280]{1,0:T(8,128)(2,1)S(1)} %collective-permute-done.7.refs_6_), channel_id=1, source_target_pairs={{0,2},{1,3},{2,0},{3,1},{4,6},{5,7},{6,4},{7,5},{8,10},{9,11},{10,... | collective-permute-start | bytes 983048 | tf_op jit(solution)/shard_map/ppermute | solution.py:335
  69.1 6.7 %collective-permute-start.14 = (bf16[128,1280]{1,0:T(8,128)(2,1)S(1)}, bf16[128,1280]{1,0:T(8,128)(2,1)}, u32[]{:S(2)}, u32[]{:S(2)}) collective-permute-start(bf16[128,1280]{1,0:T(8,128)(2,1)S(1)} %collective-permute-done.3.refs_4_), channel_id=1, source_target_pairs={{0,1},{1,0},{2,3},{3,2},{4,5},{5,4},{6,7},{7,6},{8,9},{9,8},{10,11... | collective-permute-start | bytes 983048 | tf_op jit(solution)/shard_map/ppermute | solution.py:335
  69.1 6.7 %collective-permute-start.13 = (bf16[128,1280]{1,0:T(8,128)(2,1)S(1)}, bf16[128,1280]{1,0:T(8,128)(2,1)}, u32[]{:S(2)}, u32[]{:S(2)}) collective-permute-start(bf16[128,1280]{1,0:T(8,128)(2,1)S(1)} %collective-permute-done.6.refs_3_), channel_id=1, source_target_pairs={{0,1},{1,0},{2,3},{3,2},{4,5},{5,4},{6,7},{7,6},{8,9},{9,8},{10,11... | collective-permute-start | bytes 983048 | tf_op jit(solution)/shard_map/ppermute | solution.py:335
  69.6 6.2 %collective-permute-start.16 = (bf16[128,1280]{1,0:T(8,128)(2,1)S(1)}, bf16[128,1280]{1,0:T(8,128)(2,1)}, u32[]{:S(2)}, u32[]{:S(2)}) collective-permute-start(bf16[128,1280]{1,0:T(8,128)(2,1)S(1)} %collective-permute-done.7.refs_6_), channel_id=1, source_target_pairs={{0,1},{1,0},{2,3},{3,2},{4,5},{5,4},{6,7},{7,6},{8,9},{9,8},{10,11... | collective-permute-start | bytes 983048 | tf_op jit(solution)/shard_map/ppermute | solution.py:335
  69.7 6.1 %collective-permute-start.15 = (bf16[128,1280]{1,0:T(8,128)(2,1)S(1)}, bf16[128,1280]{1,0:T(8,128)(2,1)}, u32[]{:S(2)}, u32[]{:S(2)}) collective-permute-start(bf16[128,1280]{1,0:T(8,128)(2,1)S(1)} %collective-permute-done.8.refs_5_), channel_id=1, source_target_pairs={{0,1},{1,0},{2,3},{3,2},{4,5},{5,4},{6,7},{7,6},{8,9},{9,8},{10,11... | collective-permute-start | bytes 983048 | tf_op jit(solution)/shard_map/ppermute | solution.py:335
  75.7 2.0 %collective-permute-start.17 = (bf16[128,1280]{1,0:T(8,128)(2,1)}, bf16[128,1280]{1,0:T(8,128)(2,1)}, u32[]{:S(2)}, u32[]{:S(2)}) collective-permute-start(bf16[128,1280]{1,0:T(8,128)(2,1)} %collective-permute-done.9.refs_7_), channel_id=1, source_target_pairs={{0,1},{1,0},{2,3},{3,2},{4,5},{5,4},{6,7},{7,6},{8,9},{9,8},{10,11... | collective-permute-start | bytes 983048 | tf_op jit(solution)/shard_map/ppermute | solution.py:335
  77.7 2.2 %copy-start.2 = (bf16[2,1024,1024]{2,1,0:T(8,128)(2,1)S(1)}, bf16[2,1024,1024]{2,1,0:T(8,128)(2,1)}, u32[]{:S(2)}) copy-start(bf16[2,1024,1024]{2,1,0:T(8,128)(2,1)} %copy-done.1) | copy-start | bytes 12582916
  79.9 1.6 %copy-start.4 = (bf16[1024,1024]{1,0:T(8,128)(2,1)S(1)}, bf16[1024,1024]{1,0:T(8,128)(2,1)}, u32[]{:S(2)}) copy-start(bf16[1024,1024]{1,0:T(8,128)(2,1)} %copy-done.3) | copy-start | bytes 6291460
  81.5 9.0 %copy-start.5 = (s32[256]{0:T(256)S(1)}, s32[256]{0:T(256)}, u32[]{:S(2)}) copy-start(s32[256]{0:T(256)} %param.11) | copy-start | bytes 3076

commit v4 on v3

--- a/solution.py
+++ b/solution.py
@@ -95,9 +95,11 @@
     return jnp.concatenate([zero_one(ids == lanes + 128.0 * k) for k in range(shells // 128)], axis=1)
 
 
-def slot_hots(got, shells):
-    ids = got[:, 2 * BLK_DEV :, :].reshape(-1, 256)
-    return one_hots(ids[:, :128], shells), one_hots(ids[:, 128:], shells)
+def slot_hots(code, shells):
+    code = code.reshape(-1, 128)
+    kept = code >= 0
+    columns = jnp.where(kept, code % shells, -1).astype(F32)
+    return one_hots(columns, shells), one_hots(jnp.where(kept, code // shells, -1).astype(F32), shells)
 
 
 class Shells:
@@ -125,7 +127,7 @@
             self.edges.append(jnp.sum(self.used * jnp.floor((reach + extra) * 0.5), axis=0, keepdims=True))
 
 
-def pack_kernel(pairs_ref, count_ref, panels_ref, vir_ref, occ_ref, send_ref, *outs):
+def pack_kernel(shells, pairs_ref, count_ref, vir_ref, occ_ref, code_ref, *outs):
     me = lax.axis_index("shell")
     core, y = lax.rem(me, 2), lax.rem(lax.div(me, 2), 2)
     here, nvir = vir_ref.shape
@@ -140,26 +142,26 @@
             out[:, :width] = jnp.dot(pick, part, preferred_element_type=F32).astype(BF16)
             part = occ_ref[:, pl.ds(pl.multiple_of(half * thin, 128), thin)]
             out[:, width:] = jnp.dot(pick, part, preferred_element_type=F32).astype(BF16)
-    n = send_ref.shape[0]
+    code = pairs_ref[1:2, :] + shells * pairs_ref[0:1, :]
+    code = jnp.where(iota((1, BLK_DEV), 1) < count_ref[...], code, -1).astype(F32)
+    square = (BLK_DEV, BLK_DEV)
+    code = column_of(code, iota(square, 0) == iota(square, 1)).astype(jnp.int32)
+    code_ref[...] = jnp.broadcast_to(jnp.broadcast_to(code, (BLK_DEV, 128))[None], code_ref.shape)
+
+
+def send_kernel(panels_ref, send_ref):
     turned = jnp.swapaxes(panels_ref[...].astype(F32), 0, 1)
-    send_ref[:, : 2 * BLK_DEV, :] = turned.reshape(n, 2 * BLK_DEV, EDGE * EDGE).astype(BF16)
-    slot, lane = iota((BLK_DEV, 256), 0), iota((BLK_DEV, 256), 1)
-    ids = jnp.zeros((BLK_DEV, 256), jnp.int32)
-    for g in range(BLK_DEV):
-        ids = jnp.where(slot == g, jnp.where(lane < 128, pairs_ref[g, 1], pairs_ref[g, 0]), ids)
-    ids = jnp.where(slot < count_ref[0], ids, -1).astype(F32)
-    send_ref[:, 2 * BLK_DEV :, :] = jnp.broadcast_to(ids[None], (n, BLK_DEV, 256)).astype(BF16)
-
-
-def pick_kernel(here, got_ref, size_ref, *refs):
+    send_ref[...] = turned.reshape(send_ref.shape).astype(BF16)
+
+
+def pick_kernel(here, code_ref, size_ref, *refs):
     sources, (out_ref, over_ref) = refs[:4], refs[4:]
     me = lax.axis_index("shell")
     core, y, z = lax.rem(me, 2), lax.rem(lax.div(me, 2), 2), lax.div(me, 4)
     window = CORES * Y * here
     shell_count = size_ref.shape[1]
-    got = got_ref[...].astype(F32)
     shells = Shells(size_ref[...].astype(F32))
-    lists = [Used(shells, hot, window) for hot in slot_hots(got, shell_count)]
+    lists = [Used(shells, hot, window) for hot in slot_hots(code_ref[...], shell_count)]
     most = jnp.zeros((1, 1), F32)
     lane = iota((1, 128), 1)
     for chosen in lists:
@@ -193,13 +195,14 @@
         out_ref[:, column] = total.astype(BF16)
 
 
-def place_kernel(here, got_ref, size_ref, rows_ref, placed_ref):
+def place_kernel(here, code_ref, got_ref, size_ref, rows_ref, placed_ref):
+    chip = lax.div(lax.axis_index("shell"), CORES)
     window = CORES * Y * here
     shell_count = size_ref.shape[1]
     got = got_ref[...].astype(F32)
     size_row = size_ref[...].astype(F32)
     shells = Shells(size_row)
-    hots = slot_hots(got, shell_count)
+    hots = slot_hots(code_ref[...], shell_count)
     lists = [Used(shells, hot, window) for hot in hots]
     slots = hots[0].shape[0]
     kept = LIVE_DEV * (slots // BLK_DEV)
@@ -226,12 +229,16 @@
         first, length = spread(hot, shells.starts), spread(hot, shells.size)
         row = first + step
         odd = (row - 2.0 * jnp.floor(row * 0.5)) > 0.0
-        place = jnp.where(odd, spread(hot, chosen.ahead[1]) + CAP, spread(hot, chosen.ahead[0]))
+        place = jnp.where(odd, spread(hot, chosen.ahead[1]), spread(hot, chosen.ahead[0]))
         place += jnp.floor(step * 0.5)
+        offsets = [
+            [((w * Y + k) ^ chip).astype(F32) * CAP - lane_value(e, w) for w in range(Z)]
+            for k, e in enumerate(chosen.edges)
+        ]
+        offset = jnp.where(odd, offsets[1][0], offsets[0][0])
         for w in range(1, Z):
-            gap = [2.0 * CAP - (lane_value(e, w) - lane_value(e, w - 1)) for e in chosen.edges]
-            place += jnp.where(row >= float(window * w), jnp.where(odd, gap[1], gap[0]), 0.0)
-        return jnp.where(step < length, place, -1.0)[:, :1]
+            offset = jnp.where(row >= float(window * w), jnp.where(odd, offsets[1][w], offsets[0][w]), offset)
+        return jnp.where(step < length, place + offset, -1.0)[:, :1]
 
     place_c, place_r = places(hots[0], lists[0]), places(hots[1], lists[1])
     span = 16 * EDGE
@@ -256,58 +263,40 @@
 
 
 def last_kernel(count, me_ref, rows_ref, placed_ref, *refs):
-    pieces, (out_ref, vir_ref, occ_ref, half_ref, sems) = refs[: 2 * count], refs[2 * count :]
-    width = vir_ref.shape[2]
+    pieces, (out_ref, parts_ref, half_ref) = refs[: 2 * count], refs[2 * count :]
+    sides = [pieces[:count], pieces[count:]]
+    width = pieces[0].shape[1] - 128
     tile = out_ref.shape[2]
     per = width // tile
     core = lax.rem(me_ref[0], CORES)
-    chip = lax.div(me_ref[0], CORES)
     j = pl.program_id(0)
-
-    def copies(far, part):
-        for k in range(count):
-            rows = pl.ds(pl.multiple_of((chip ^ k) * CAP, CAP), CAP)
-            columns = pl.ds(0, width) if part == 0 else pl.ds(width, 128)
-            target = vir_ref.at[far, rows, :] if part == 0 else occ_ref.at[far, rows, :]
-            yield pltpu.make_async_copy(
-                pieces[far * count + k].at[:, columns], target, sems.at[(2 * far + part) * count + k]
-            )
 
     @pl.when(j == 0)
     def _():
-        for far, part in ((0, 1), (1, 1), (0, 0), (1, 0)):
-            for copy in copies(far, part):
-                copy.start()
-        for far in range(2):
-            for copy in copies(far, 1):
-                copy.wait()
-        parts = [
-            jnp.dot(rows_ref[...], occ_ref[far], preferred_element_type=F32).astype(BF16) for far in range(2)
-        ]
-        for far in range(2):
-            half = jnp.where(far == 0, core, 1 - core)
+        for far, side in enumerate(sides):
+            occ = jnp.concatenate([piece[:, width:] for piece in side], axis=0)
+            part = jnp.dot(rows_ref[...], occ, preferred_element_type=F32).astype(BF16)
+            half = lax.rem(core + far, CORES)
+            parts_ref[:, pl.ds(pl.multiple_of(half * 128, 128), 128)] = part
+        for p in range(2):
+            piece = lax.dot_general(
+                parts_ref[...], placed_ref[p], (((0,), (0,)), ((), ())), preferred_element_type=F32
+            )
+            half_ref[p * NOCC : (p + 1) * NOCC, :] = piece.astype(BF16)
+
+    for far, side in enumerate(sides):
+
+        @pl.when(lax.div(j, per) == far)
+        def _():
+            columns = pl.ds(pl.multiple_of(lax.rem(j, per) * tile, 128), tile)
+            right = jnp.concatenate([piece[:, columns] for piece in side], axis=0)
             for p in range(2):
-                piece = lax.dot_general(
-                    parts[far], placed_ref[p], (((0,), (0,)), ((), ())), preferred_element_type=F32
-                )
-                start = pl.multiple_of(p * NOCC + half * 128, 128)
-                half_ref[pl.ds(start, 128), :] = piece.astype(BF16)
-
-    for far in range(2):
-
-        @pl.when(j == far * per)
-        def _():
-            for copy in copies(far, 0):
-                copy.wait()
-
-    right = vir_ref[lax.div(j, per), :, pl.ds(pl.multiple_of(lax.rem(j, per) * tile, 128), tile)]
-    for p in range(2):
-        out_ref[p] = jnp.dot(half_ref[p * NOCC : (p + 1) * NOCC, :], right, preferred_element_type=F32).astype(BF16)
+                left = half_ref[p * NOCC : (p + 1) * NOCC, :]
+                out_ref[p] = jnp.dot(left, right, preferred_element_type=F32).astype(BF16)
 
 
 VMEM = pl.BlockSpec(memory_space=pltpu.VMEM)
 SMEM = pl.BlockSpec(memory_space=pltpu.SMEM)
-ANY = pl.BlockSpec(memory_space=pl.ANY)
 
 
 def shape(*dims, dtype=BF16):
@@ -334,27 +323,39 @@
     def swap(array, bit):
         return lax.ppermute(array, "shell", [(i, i ^ bit) for i in range(n)])
 
-    send, keep, to_core, to_y, to_both = pl.pallas_call(
-        pack_kernel,
-        out_shape=[shape(n, 3 * BLK_DEV, EDGE * EDGE)] + [shape(here // 2, packed)] * 4,
-        in_specs=[SMEM] * 2 + [VMEM] * 3,
+    code, keep, to_core, to_y, to_both = pl.pallas_call(
+        functools.partial(pack_kernel, size_row.shape[1]),
+        out_shape=[shape(n, BLK_DEV, 128, dtype=jnp.int32)] + [shape(here // 2, packed)] * 4,
+        in_specs=[VMEM] * 4,
         out_specs=[VMEM] * 5,
-        compiler_params=params(32),
+        compiler_params=params(12),
         cost_estimate=cost(3e8, 3e6),
         name="pack_rows",
-    )(block_pairs, block_count, panels, vir_coef, occ_coef)
+    )(block_pairs.T, block_count.reshape(1, 1), vir_coef, occ_coef)
     fresh = [keep, swap(to_core, 1), swap(to_y, 2), swap(to_both, 3)]
-    got = lax.all_to_all(send, "shell", split_axis=0, concat_axis=0, tiled=True)
+    code = lax.all_to_all(code, "shell", split_axis=0, concat_axis=0, tiled=True)
 
     mine, over = pl.pallas_call(
         functools.partial(pick_kernel, here),
         out_shape=(shape(CAP, packed), shape(1, dtype=jnp.int32)),
         in_specs=[VMEM] * 6,
         out_specs=(VMEM, SMEM),
-        compiler_params=params(32),
+        compiler_params=params(12),
         cost_estimate=cost(3e8, 2e6),
         name="pick_rows",
-    )(got, size_row, *fresh)
+    )(code, size_row, *fresh)
+
+    panels, mine_again = lax.optimization_barrier((panels, mine))
+    send = pl.pallas_call(
+        send_kernel,
+        out_shape=shape(n, 2 * BLK_DEV, EDGE * EDGE),
+        in_specs=[VMEM],
+        out_specs=VMEM,
+        compiler_params=params(12),
+        cost_estimate=cost(1e6, 3e5),
+        name="turn_panels",
+    )(panels)
+    got = lax.all_to_all(send, "shell", split_axis=0, concat_axis=0, tiled=True)
 
     across, beside, mine_y = swap(mine, 8), swap(mine, 4), swap(mine, 2)
     beside, mine_y, got_late = lax.optimization_barrier((beside, mine_y, got))
@@ -363,12 +364,12 @@
     rows, placed = pl.pallas_call(
         functools.partial(place_kernel, here),
         out_shape=(shape(LIVE_DEV * n * EDGE, room), shape(2, LIVE_DEV * n * EDGE, room)),
-        in_specs=[VMEM] * 2,
+        in_specs=[VMEM] * 3,
         out_specs=(VMEM, VMEM),
-        compiler_params=params(32),
+        compiler_params=params(20),
         cost_estimate=cost(4e9, 8e6),
         name="place_panels",
-    )(got_late, size_row)
+    )(code, got_late, size_row)
 
     across, beside_y, rows, placed = lax.optimization_barrier((across, beside_y, rows, placed))
     corner, across_y = swap(across, 4), swap(across, 2)
@@ -385,38 +386,34 @@
         grid_spec=pltpu.PrefetchScalarGridSpec(
             num_scalar_prefetch=1,
             grid=(nvir // tile,),
-            in_specs=[VMEM] * 2 + [ANY] * (2 * count),
+            in_specs=[VMEM] * (2 + 2 * count),
             out_specs=pl.BlockSpec((2, NOCC, tile), lambda j, o: (0, 0, (j + 3 * (o[0] % 2)) % 6)),
-            scratch_shapes=[
-                pltpu.VMEM((CORES, room, width), BF16),
-                pltpu.VMEM((CORES, room, 128), BF16),
-                pltpu.VMEM((2 * NOCC, room), BF16),
-                pltpu.SemaphoreType.DMA((4 * count,)),
-            ],
+            scratch_shapes=[pltpu.VMEM((LIVE_DEV * n * EDGE, NOCC), BF16), pltpu.VMEM((2 * NOCC, room), BF16)],
         ),
-        compiler_params=params(32),
+        compiler_params=params(24),
         cost_estimate=cost(4e9, 1e7),
         name="last_product",
     )(me.reshape(1), rows, placed, *pieces, *far)
-    return out, over[0], got
+    return out, over[0], code, got
 
 
 def per_device(*args):
     n = lax.axis_size("shell")
     here, nvir = args[5].shape
+    shells = args[3].shape[0]
     sparse = LIVE_DEV * n * EDGE < n * here
     if not (sparse and n == Z * Y * CORES and here <= 256 and here % 16 == 0 and nvir % 768 == 0):
         return from_start(*args)
-    out, over, got = short_way(*args)
+    out, over, code, got = short_way(*args)
 
     def again(carry):
         over, _ = carry
-        over, got_now, *held = lax.optimization_barrier((over, got, *args[3:]))
-        turned = got_now[:, : 2 * BLK_DEV].reshape(n, 2, BLK_DEV, EDGE * EDGE).swapaxes(1, 2)
-        turned = turned.reshape(n * BLK_DEV, 2, EDGE * EDGE)
-        ids = got_now[:, 2 * BLK_DEV :].reshape(n * BLK_DEV, 256)
-        pairs = jnp.stack([ids[:, 128], ids[:, 0]], axis=1).astype(jnp.int32)
-        return over - 1, long_way(turned, jnp.maximum(pairs, 0), pairs[:, 1] >= 0, *held)
+        over, code_now, turned, *held = lax.optimization_barrier((over, code, got, *args[3:]))
+        turned = turned.reshape(n, 2, BLK_DEV, EDGE * EDGE).swapaxes(1, 2).reshape(n * BLK_DEV, 2, EDGE * EDGE)
+        code_now = jnp.max(code_now, axis=2).reshape(n * BLK_DEV)
+        ids = jnp.maximum(code_now, 0)
+        pairs = jnp.stack([ids // shells, ids % shells], axis=1)
+        return over - 1, long_way(turned, pairs, code_now >= 0, *held)
 
     return lax.while_loop(lambda carry: carry[0] > 0, again, (over, out))[1]
 

time: 98.5 us -> 100 us (1.015)
  blocking collectives: 0 us -> 12.8 us
  waiting for transfers between devices: 37.3 us -> 26.5 us
  starting transfers between devices: 19.2 us -> 18.2 us
    ppermute x18, waiting for transfers between devices: 37.3 us -> 20.9 us  [swap(): return lax.ppermute(array, 'shell', [(i, i ^ bit) for i in range(n)])]
    all_to_all x0 -> x1, blocking collectives: none -> 12.8 us  [short_way(): lax.all_to_all(code, 'shell', split_axis=0, concat_axis=0, tiled=True)]
    all_to_all x1, waiting for transfers between devices: 0.01 us -> 5.58 us  [short_way(): got = lax.all_to_all(send, 'shell', split_axis=0, concat_axis=0, tiled=True)]
    all_to_all x1, starting transfers between devices: 7.39 us -> 3.97 us  [short_way(): got = lax.all_to_all(send, 'shell', split_axis=0, concat_axis=0, tiled=True)]
    ppermute x18, starting transfers between devices: 11.8 us -> 14.2 us  [swap(): return lax.ppermute(array, 'shell', [(i, i ^ bit) for i in range(n)])]
    unnamed x13 -> x14, local copies, waits for them, and re-layouts: 8.68 us -> 8.61 us
    pallas_call x1 -> x2, Pallas kernels: 2.24 us -> 2.25 us  [the longest x1 1.54 us: short_way(): pl.pallas_call(functools.partial(pack_kernel, size_row.shape[1]), out_sha...]
  transfers between devices with their start and end apart: 19 -> 19, of which waited for: 8 -> 6; matrix products, arithmetic and copies ran while one was open for 0% -> 0% of each run, Pallas kernels for 5% -> 6%
where the time goes in v4:
time: 100 us; the launch traced here: 99.8 us
  waiting for transfers between devices  26.5 us (26%)
  Pallas kernels  18.7 us (19%)
  starting transfers between devices  18.2 us (18%)
  between operations  14.1 us (14%)
  blocking collectives  12.8 us (13%)
  local copies, waits for them, and re-layouts  8.61 us (9%)
    ppermute x18, waiting for transfers between devices, swap(): return lax.ppermute(array, 'shell', [(i, i ^ bit) for i in range(n)])  20.9 us
    ppermute x18, starting transfers between devices, swap(): return lax.ppermute(array, 'shell', [(i, i ^ bit) for i in range(n)])  14.2 us
    all_to_all x1, blocking collectives, short_way(): lax.all_to_all(code, 'shell', split_axis=0, concat_axis=0, tiled=True)  12.8 us
    pallas_call x1, Pallas kernels, short_way(): pl.pallas_call(functools.partial(last_kernel, count), out_shape=shape(2,...  9.49 us
    unnamed x14, local copies, waits for them, and re-layouts  8.61 us
    all_to_all x1, waiting for transfers between devices, short_way(): got = lax.all_to_all(send, 'shell', split_axis=0, concat_axis=0, tiled=True)  5.58 us
    pallas_call x1, Pallas kernels, short_way(): pl.pallas_call(functools.partial(place_kernel, here), out_shape=(shape(LI...  4.82 us
    all_to_all x1, starting transfers between devices, short_way(): got = lax.all_to_all(send, 'shell', split_axis=0, concat_axis=0, tiled=True)  3.97 us
  transfers between devices with their start and end apart: 19, of which 6 were waited for; matrix products, arithmetic and copies ran while one was open for 0% of the time, Pallas kernels for 6%

profile of v4, /device:TPU:0, one launch (start us, length us, event | category | flops | bytes accessed | tf_op | source)
XLA Modules:
  0.0 99.8 jit_solution(3177434617386028378)
XLA Ops:
  7.2 0.7 copy-done.1
  7.9 1.5 %pack_rows.1 = (s32[16,8,128]{2,1,0:T(8,128)S(1)}, bf16[80,1280]{1,0:T(8,128)(2,1)S(1)}, bf16[80,1280]{1,0:T(8,128)(2,1)S(1)}, bf16[80,1280]{1,0:T(8,128)(2,1)S(1)}, bf16[80,1280]{1,0:T(8,128)(2,1)S(1)}) custom-call(s32[2,8]{1,0:T(2,128)S(1)} %bitcast.61, s32[1,1]{1,0:T(1,128)} %bitcast.60.count_ref, bf16[160,2304]{1,0:T(8,128)(2,1)} %vir_ref.1, ...), custom_call_target="tpu_custom_call" | custom-call | flops 300000000 | bytes 3000000 | tf_op jit(solution)/shard_map/pack_rows/pallas_call | solution.py:326
  9.4 0.5 collective-permute-start
  9.9 2.6 %collective-permute-start.1 = (bf16[80,1280]{1,0:T(8,128)(2,1)S(1)}, bf16[80,1280]{1,0:T(8,128)(2,1)S(1)}, u32[]{:S(2)}, u32[]{:S(2)}) collective-permute-start(bf16[80,1280]{1,0:T(8,128)(2,1)S(1)} %get-tuple-element.167), channel_id=1, source_target_pairs={{0,2},{1,3},{2,0},{3,1},{4,6},{5,7},{6,4},{7,5},{8,10},{9,11},{10,... | collective-permute-start | bytes 614408 | tf_op jit(solution)/shard_map/ppermute | solution.py:324
  12.6 12.8 %all_to_all.10.code_ref = s32[16,8,128]{2,1,0:T(8,128)S(1)} all-to-all(s32[16,8,128]{2,1,0:T(8,128)S(1)} %get-tuple-element.164), channel_id=1, replica_groups=mesh['groups'=2,'shell'=16] {'shell'}, dimensions={0} | all-to-all | bytes 131072 | tf_op jit(solution)/shard_map/all_to_all | solution.py:336
  25.4 2.2 %pick_rows.1 = (bf16[128,1280]{1,0:T(8,128)(2,1)S(1)}, s32[1]{0:T(128)}) custom-call(s32[16,8,128]{2,1,0:T(8,128)S(1)} %all_to_all.10.code_ref, s32[1,256]{1,0:T(1,128)} %bitcast.64, bf16[80,1280]{1,0:T(8,128)(2,1)S(1)} %get-tuple-element.165.refs_0_, bf16[80,1280]{1,0:T(8,128)(2,1)S(1)} %collective-permute-done.refs_1_, ...), custom_call_target="tpu_custom_call" | custom-call | flops 300000000 | bytes 2000000 | tf_op jit(solution)/shard_map/pick_rows/pallas_call | solution.py:338
  27.6 0.2 collective-permute-start.4
  27.8 1.1 %collective-permute-start.5 = (bf16[128,1280]{1,0:T(8,128)(2,1)S(1)}, bf16[128,1280]{1,0:T(8,128)(2,1)S(1)}, u32[]{:S(2)}, u32[]{:S(2)}) collective-permute-start(bf16[128,1280]{1,0:T(8,128)(2,1)S(1)} %get-tuple-element.170.refs_0_), channel_id=1, source_target_pairs={{0,2},{1,3},{2,0},{3,1},{4,6},{5,7},{6,4},{7,5},{8,10},{9,11},{10,... | collective-permute-start | bytes 983048 | tf_op jit(solution)/shard_map/ppermute | solution.py:324
  28.9 0.9 copy-done
  29.8 0.7 turn_panels.1
  30.5 4.0 %all-to-all-start.1 = ((bf16[16,16,256]{2,1,0:T(8,128)(2,1)}), bf16[16,16,256]{2,1,0:T(8,128)(2,1)S(1)}, u32[]{:S(2)}, u32[]{:S(2)}) async-start(bf16[16,16,256]{2,1,0:T(8,128)(2,1)} %turn_panels.1), calls=%async_computation.1 | async-start | bytes 262144 | tf_op jit(solution)/shard_map/all_to_all | solution.py:358
  34.5 2.8 %collective-permute-start.3 = (bf16[128,1280]{1,0:T(8,128)(2,1)S(1)}, bf16[128,1280]{1,0:T(8,128)(2,1)S(1)}, u32[]{:S(2)}, u32[]{:S(2)}) collective-permute-start(bf16[128,1280]{1,0:T(8,128)(2,1)S(1)} %get-tuple-element.170.refs_0_), channel_id=1, source_target_pairs={{0,8},{1,9},{2,10},{3,11},{4,12},{5,13},{6,14},{7,15},{8,0},{9,1},... | collective-permute-start | bytes 983048 | tf_op jit(solution)/shard_map/ppermute | solution.py:324
  37.3 5.6 %all-to-all-done.1.got_ref = bf16[16,16,256]{2,1,0:T(8,128)(2,1)S(1)} async-done(((bf16[16,16,256]{2,1,0:T(8,128)(2,1)}), bf16[16,16,256]{2,1,0:T(8,128)(2,1)S(1)}, u32[]{:S(2)}, u32[]{:S(2)}) %all-to-all-start.1) | async-done | bytes 131104 | tf_op jit(solution)/shard_map/all_to_all | solution.py:358
  42.9 4.8 %place_panels.1 = (bf16[1024,1024]{1,0:T(8,128)(2,1)S(1)}, bf16[2,1024,1024]{2,1,0:T(8,128)(2,1)S(1)}) custom-call(s32[16,8,128]{2,1,0:T(8,128)S(1)} %all_to_all.10.code_ref, bf16[16,16,256]{2,1,0:T(8,128)(2,1)S(1)} %all-to-all-done.1.got_ref, s32[1,256]{1,0:T(1,128)} %bitcast.65), custom_call_target="tpu_custom_call" | custom-call | flops 4000000000 | bytes 8000000 | tf_op jit(solution)/shard_map/place_panels/pallas_call | solution.py:364
  47.7 1.9 %copy-done.2 = bf16[2,1024,1024]{2,1,0:T(8,128)(2,1)} copy-done((bf16[2,1024,1024]{2,1,0:T(8,128)(2,1)}, bf16[2,1024,1024]{2,1,0:T(8,128)(2,1)S(1)}, u32[]{:S(2)}) %copy-start.2) | copy-done | bytes 4194328
  49.7 1.3 %copy-done.4 = bf16[1024,1024]{1,0:T(8,128)(2,1)} copy-done((bf16[1024,1024]{1,0:T(8,128)(2,1)}, bf16[1024,1024]{1,0:T(8,128)(2,1)S(1)}, u32[]{:S(2)}) %copy-start.4) | copy-done | bytes 2097176
  51.0 4.4 %collective-permute-done.3.refs_4_ = bf16[128,1280]{1,0:T(8,128)(2,1)S(1)} collective-permute-done((bf16[128,1280]{1,0:T(8,128)(2,1)S(1)}, bf16[128,1280]{1,0:T(8,128)(2,1)S(1)}, u32[]{:S(2)}, u32[]{:S(2)}) %collective-permute-start.3) | collective-permute-done | bytes 327712 | tf_op jit(solution)/shard_map/ppermute | solution.py:324
  55.3 1.4 %collective-permute-start.7 = (bf16[128,1280]{1,0:T(8,128)(2,1)S(1)}, bf16[128,1280]{1,0:T(8,128)(2,1)S(1)}, u32[]{:S(2)}, u32[]{:S(2)}) collective-permute-start(bf16[128,1280]{1,0:T(8,128)(2,1)S(1)} %collective-permute-done.3.refs_4_), channel_id=1, source_target_pairs={{0,4},{1,5},{2,6},{3,7},{4,0},{5,1},{6,2},{7,3},{8,12},{9,13},{10,... | collective-permute-start | bytes 983048 | tf_op jit(solution)/shard_map/ppermute | solution.py:324
  56.7 1.4 %collective-permute-start.8 = (bf16[128,1280]{1,0:T(8,128)(2,1)S(1)}, bf16[128,1280]{1,0:T(8,128)(2,1)S(1)}, u32[]{:S(2)}, u32[]{:S(2)}) collective-permute-start(bf16[128,1280]{1,0:T(8,128)(2,1)S(1)} %collective-permute-done.3.refs_4_), channel_id=1, source_target_pairs={{0,2},{1,3},{2,0},{3,1},{4,6},{5,7},{6,4},{7,5},{8,10},{9,11},{10,... | collective-permute-start | bytes 983048 | tf_op jit(solution)/shard_map/ppermute | solution.py:324
  58.1 1.1 %collective-permute-start.10 = (bf16[128,1280]{1,0:T(8,128)(2,1)S(1)}, bf16[128,1280]{1,0:T(8,128)(2,1)S(1)}, u32[]{:S(2)}, u32[]{:S(2)}) collective-permute-start(bf16[128,1280]{1,0:T(8,128)(2,1)S(1)} %get-tuple-element.170.refs_0_), channel_id=1, source_target_pairs={{0,1},{1,0},{2,3},{3,2},{4,5},{5,4},{6,7},{7,6},{8,9},{9,8},{10,11... | collective-permute-start | bytes 983048 | tf_op jit(solution)/shard_map/ppermute | solution.py:324
  59.2 0.5 collective-permute-start.11
  59.7 5.9 %collective-permute-done.7.refs_6_ = bf16[128,1280]{1,0:T(8,128)(2,1)S(1)} collective-permute-done((bf16[128,1280]{1,0:T(8,128)(2,1)S(1)}, bf16[128,1280]{1,0:T(8,128)(2,1)S(1)}, u32[]{:S(2)}, u32[]{:S(2)}) %collective-permute-start.7) | collective-permute-done | bytes 327712 | tf_op jit(solution)/shard_map/ppermute | solution.py:324
  65.6 1.3 %collective-permute-done.8.refs_5_ = bf16[128,1280]{1,0:T(8,128)(2,1)S(1)} collective-permute-done((bf16[128,1280]{1,0:T(8,128)(2,1)S(1)}, bf16[128,1280]{1,0:T(8,128)(2,1)S(1)}, u32[]{:S(2)}, u32[]{:S(2)}) %collective-permute-start.8) | collective-permute-done | bytes 327712 | tf_op jit(solution)/shard_map/ppermute | solution.py:324
  66.8 1.6 %collective-permute-start.9 = (bf16[128,1280]{1,0:T(8,128)(2,1)S(1)}, bf16[128,1280]{1,0:T(8,128)(2,1)}, u32[]{:S(2)}, u32[]{:S(2)}) collective-permute-start(bf16[128,1280]{1,0:T(8,128)(2,1)S(1)} %collective-permute-done.7.refs_6_), channel_id=1, source_target_pairs={{0,2},{1,3},{2,0},{3,1},{4,6},{5,7},{6,4},{7,5},{8,10},{9,11},{10,... | collective-permute-start | bytes 983048 | tf_op jit(solution)/shard_map/ppermute | solution.py:324
  68.4 0.5 collective-permute-start.13
  69.0 0.4 collective-permute-start.15
  69.4 7.4 %collective-permute-done.9.refs_7_ = bf16[128,1280]{1,0:T(8,128)(2,1)} collective-permute-done((bf16[128,1280]{1,0:T(8,128)(2,1)S(1)}, bf16[128,1280]{1,0:T(8,128)(2,1)}, u32[]{:S(2)}, u32[]{:S(2)}) %collective-permute-start.9) | collective-permute-done | bytes 327712 | tf_op jit(solution)/shard_map/ppermute | solution.py:324
  76.9 1.9 %collective-permute-done.17.refs_15_ = bf16[128,1280]{1,0:T(8,128)(2,1)} collective-permute-done((bf16[128,1280]{1,0:T(8,128)(2,1)}, bf16[128,1280]{1,0:T(8,128)(2,1)}, u32[]{:S(2)}, u32[]{:S(2)}) %collective-permute-start.17) | collective-permute-done | bytes 327712 | tf_op jit(solution)/shard_map/ppermute | solution.py:324
  78.8 2.2 %copy-done.3 = bf16[2,1024,1024]{2,1,0:T(8,128)(2,1)S(1)} copy-done((bf16[2,1024,1024]{2,1,0:T(8,128)(2,1)S(1)}, bf16[2,1024,1024]{2,1,0:T(8,128)(2,1)}, u32[]{:S(2)}) %copy-start.3) | copy-done | bytes 4194328
  81.0 1.6 %copy-done.5 = bf16[1024,1024]{1,0:T(8,128)(2,1)S(1)} copy-done((bf16[1024,1024]{1,0:T(8,128)(2,1)S(1)}, bf16[1024,1024]{1,0:T(8,128)(2,1)}, u32[]{:S(2)}) %copy-start.5) | copy-done | bytes 2097176
  82.6 9.5 %last_product.1 = bf16[2,256,2304]{2,1,0:T(8,128)(2,1)} custom-call(s32[1]{0:T(128)} %bitcast.17.me_ref, bf16[1024,1024]{1,0:T(8,128)(2,1)S(1)} %copy-done.5, bf16[2,1024,1024]{2,1,0:T(8,128)(2,1)S(1)} %copy-done.3, bf16[128,1280]{1,0:T(8,128)(2,1)S(1)} %get-tuple-element.170.refs_0_, bf16[128,1280]{1,0:T(8,128)(2,1)S(1)} %collective-permute-done.5.refs_1_, ...), custom_call_target="tpu_custom_call" | custom-call | flops 4000000000 | bytes 10000000 | tf_op jit(solution)/shard_map/last_product/pallas_call | solution.py:383
  92.1 0.9 while.17
  (27 shorter events, 0.2 us)
Async XLA Ops:
  7.2 0.7 copy-start.1
  9.4 16.0 %collective-permute-start = (bf16[80,1280]{1,0:T(8,128)(2,1)S(1)}, bf16[80,1280]{1,0:T(8,128)(2,1)S(1)}, u32[]{:S(2)}, u32[]{:S(2)}) collective-permute-start(bf16[80,1280]{1,0:T(8,128)(2,1)S(1)} %get-tuple-element.166), channel_id=1, source_target_pairs={{0,1},{1,0},{2,3},{3,2},{4,5},{5,4},{6,7},{7,6},{8,9},{9,8},{10,11... | collective-permute-start | bytes 614408 | tf_op jit(solution)/shard_map/ppermute | solution.py:324
  9.9 15.5 %collective-permute-start.1 = (bf16[80,1280]{1,0:T(8,128)(2,1)S(1)}, bf16[80,1280]{1,0:T(8,128)(2,1)S(1)}, u32[]{:S(2)}, u32[]{:S(2)}) collective-permute-start(bf16[80,1280]{1,0:T(8,128)(2,1)S(1)} %get-tuple-element.167), channel_id=1, source_target_pairs={{0,2},{1,3},{2,0},{3,1},{4,6},{5,7},{6,4},{7,5},{8,10},{9,11},{10,... | collective-permute-start | bytes 614408 | tf_op jit(solution)/shard_map/ppermute | solution.py:324
  12.5 12.9 %collective-permute-start.2 = (bf16[80,1280]{1,0:T(8,128)(2,1)S(1)}, bf16[80,1280]{1,0:T(8,128)(2,1)S(1)}, u32[]{:S(2)}, u32[]{:S(2)}) collective-permute-start(bf16[80,1280]{1,0:T(8,128)(2,1)S(1)} %get-tuple-element.168), channel_id=1, source_target_pairs={{0,3},{1,2},{2,1},{3,0},{4,7},{5,6},{6,5},{7,4},{8,11},{9,10},{10,... | collective-permute-start | bytes 614408 | tf_op jit(solution)/shard_map/ppermute | solution.py:324
  27.6 15.3 %collective-permute-start.4 = (bf16[128,1280]{1,0:T(8,128)(2,1)S(1)}, bf16[128,1280]{1,0:T(8,128)(2,1)S(1)}, u32[]{:S(2)}, u32[]{:S(2)}) collective-permute-start(bf16[128,1280]{1,0:T(8,128)(2,1)S(1)} %get-tuple-element.170.refs_0_), channel_id=1, source_target_pairs={{0,4},{1,5},{2,6},{3,7},{4,0},{5,1},{6,2},{7,3},{8,12},{9,13},{10,... | collective-permute-start | bytes 983048 | tf_op jit(solution)/shard_map/ppermute | solution.py:324
  27.8 15.1 %collective-permute-start.5 = (bf16[128,1280]{1,0:T(8,128)(2,1)S(1)}, bf16[128,1280]{1,0:T(8,128)(2,1)S(1)}, u32[]{:S(2)}, u32[]{:S(2)}) collective-permute-start(bf16[128,1280]{1,0:T(8,128)(2,1)S(1)} %get-tuple-element.170.refs_0_), channel_id=1, source_target_pairs={{0,2},{1,3},{2,0},{3,1},{4,6},{5,7},{6,4},{7,5},{8,10},{9,11},{10,... | collective-permute-start | bytes 983048 | tf_op jit(solution)/shard_map/ppermute | solution.py:324
  28.9 0.9 copy-start
  30.5 12.4 %all-to-all-start.1 = ((bf16[16,16,256]{2,1,0:T(8,128)(2,1)}), bf16[16,16,256]{2,1,0:T(8,128)(2,1)S(1)}, u32[]{:S(2)}, u32[]{:S(2)}) async-start(bf16[16,16,256]{2,1,0:T(8,128)(2,1)} %turn_panels.1), calls=%async_computation.1 | async-start | bytes 262144 | tf_op jit(solution)/shard_map/all_to_all | solution.py:358
  34.5 20.9 %collective-permute-start.3 = (bf16[128,1280]{1,0:T(8,128)(2,1)S(1)}, bf16[128,1280]{1,0:T(8,128)(2,1)S(1)}, u32[]{:S(2)}, u32[]{:S(2)}) collective-permute-start(bf16[128,1280]{1,0:T(8,128)(2,1)S(1)} %get-tuple-element.170.refs_0_), channel_id=1, source_target_pairs={{0,8},{1,9},{2,10},{3,11},{4,12},{5,13},{6,14},{7,15},{8,0},{9,1},... | collective-permute-start | bytes 983048 | tf_op jit(solution)/shard_map/ppermute | solution.py:324
  42.9 12.5 %collective-permute-start.6 = (bf16[128,1280]{1,0:T(8,128)(2,1)S(1)}, bf16[128,1280]{1,0:T(8,128)(2,1)S(1)}, u32[]{:S(2)}, u32[]{:S(2)}) collective-permute-start(bf16[128,1280]{1,0:T(8,128)(2,1)S(1)} %collective-permute-done.4.refs_2_), channel_id=1, source_target_pairs={{0,2},{1,3},{2,0},{3,1},{4,6},{5,7},{6,4},{7,5},{8,10},{9,11},{10,... | collective-permute-start | bytes 983048 | tf_op jit(solution)/shard_map/ppermute | solution.py:324
  47.7 1.9 %copy-start.2 = (bf16[2,1024,1024]{2,1,0:T(8,128)(2,1)}, bf16[2,1024,1024]{2,1,0:T(8,128)(2,1)S(1)}, u32[]{:S(2)}) copy-start(bf16[2,1024,1024]{2,1,0:T(8,128)(2,1)S(1)} %get-tuple-element.177.placed_ref) | copy-start | bytes 12582916
  49.7 1.3 %copy-start.4 = (bf16[1024,1024]{1,0:T(8,128)(2,1)}, bf16[1024,1024]{1,0:T(8,128)(2,1)S(1)}, u32[]{:S(2)}) copy-start(bf16[1024,1024]{1,0:T(8,128)(2,1)S(1)} %get-tuple-element.176.rows_ref) | copy-start | bytes 6291460
  55.3 10.2 %collective-permute-start.7 = (bf16[128,1280]{1,0:T(8,128)(2,1)S(1)}, bf16[128,1280]{1,0:T(8,128)(2,1)S(1)}, u32[]{:S(2)}, u32[]{:S(2)}) collective-permute-start(bf16[128,1280]{1,0:T(8,128)(2,1)S(1)} %collective-permute-done.3.refs_4_), channel_id=1, source_target_pairs={{0,4},{1,5},{2,6},{3,7},{4,0},{5,1},{6,2},{7,3},{8,12},{9,13},{10,... | collective-permute-start | bytes 983048 | tf_op jit(solution)/shard_map/ppermute | solution.py:324
  56.7 10.1 %collective-permute-start.8 = (bf16[128,1280]{1,0:T(8,128)(2,1)S(1)}, bf16[128,1280]{1,0:T(8,128)(2,1)S(1)}, u32[]{:S(2)}, u32[]{:S(2)}) collective-permute-start(bf16[128,1280]{1,0:T(8,128)(2,1)S(1)} %collective-permute-done.3.refs_4_), channel_id=1, source_target_pairs={{0,2},{1,3},{2,0},{3,1},{4,6},{5,7},{6,4},{7,5},{8,10},{9,11},{10,... | collective-permute-start | bytes 983048 | tf_op jit(solution)/shard_map/ppermute | solution.py:324
  58.1 10.3 %collective-permute-start.10 = (bf16[128,1280]{1,0:T(8,128)(2,1)S(1)}, bf16[128,1280]{1,0:T(8,128)(2,1)S(1)}, u32[]{:S(2)}, u32[]{:S(2)}) collective-permute-start(bf16[128,1280]{1,0:T(8,128)(2,1)S(1)} %get-tuple-element.170.refs_0_), channel_id=1, source_target_pairs={{0,1},{1,0},{2,3},{3,2},{4,5},{5,4},{6,7},{7,6},{8,9},{9,8},{10,11... | collective-permute-start | bytes 983048 | tf_op jit(solution)/shard_map/ppermute | solution.py:324
  59.2 9.8 %collective-permute-start.12 = (bf16[128,1280]{1,0:T(8,128)(2,1)S(1)}, bf16[128,1280]{1,0:T(8,128)(2,1)S(1)}, u32[]{:S(2)}, u32[]{:S(2)}) collective-permute-start(bf16[128,1280]{1,0:T(8,128)(2,1)S(1)} %collective-permute-done.4.refs_2_), channel_id=1, source_target_pairs={{0,1},{1,0},{2,3},{3,2},{4,5},{5,4},{6,7},{7,6},{8,9},{9,8},{10,11... | collective-permute-start | bytes 983048 | tf_op jit(solution)/shard_map/ppermute | solution.py:324
  59.2 9.7 %collective-permute-start.11 = (bf16[128,1280]{1,0:T(8,128)(2,1)S(1)}, bf16[128,1280]{1,0:T(8,128)(2,1)S(1)}, u32[]{:S(2)}, u32[]{:S(2)}) collective-permute-start(bf16[128,1280]{1,0:T(8,128)(2,1)S(1)} %collective-permute-done.5.refs_1_), channel_id=1, source_target_pairs={{0,1},{1,0},{2,3},{3,2},{4,5},{5,4},{6,7},{7,6},{8,9},{9,8},{10,11... | collective-permute-start | bytes 983048 | tf_op jit(solution)/shard_map/ppermute | solution.py:324
  66.8 10.0 %collective-permute-start.9 = (bf16[128,1280]{1,0:T(8,128)(2,1)S(1)}, bf16[128,1280]{1,0:T(8,128)(2,1)}, u32[]{:S(2)}, u32[]{:S(2)}) collective-permute-start(bf16[128,1280]{1,0:T(8,128)(2,1)S(1)} %collective-permute-done.7.refs_6_), channel_id=1, source_target_pairs={{0,2},{1,3},{2,0},{3,1},{4,6},{5,7},{6,4},{7,5},{8,10},{9,11},{10,... | collective-permute-start | bytes 983048 | tf_op jit(solution)/shard_map/ppermute | solution.py:324
  68.4 8.4 %collective-permute-start.14 = (bf16[128,1280]{1,0:T(8,128)(2,1)S(1)}, bf16[128,1280]{1,0:T(8,128)(2,1)}, u32[]{:S(2)}, u32[]{:S(2)}) collective-permute-start(bf16[128,1280]{1,0:T(8,128)(2,1)S(1)} %collective-permute-done.3.refs_4_), channel_id=1, source_target_pairs={{0,1},{1,0},{2,3},{3,2},{4,5},{5,4},{6,7},{7,6},{8,9},{9,8},{10,11... | collective-permute-start | bytes 983048 | tf_op jit(solution)/shard_map/ppermute | solution.py:324
  68.4 8.4 %collective-permute-start.13 = (bf16[128,1280]{1,0:T(8,128)(2,1)S(1)}, bf16[128,1280]{1,0:T(8,128)(2,1)}, u32[]{:S(2)}, u32[]{:S(2)}) collective-permute-start(bf16[128,1280]{1,0:T(8,128)(2,1)S(1)} %collective-permute-done.6.refs_3_), channel_id=1, source_target_pairs={{0,1},{1,0},{2,3},{3,2},{4,5},{5,4},{6,7},{7,6},{8,9},{9,8},{10,11... | collective-permute-start | bytes 983048 | tf_op jit(solution)/shard_map/ppermute | solution.py:324
  68.9 7.9 %collective-permute-start.16 = (bf16[128,1280]{1,0:T(8,128)(2,1)S(1)}, bf16[128,1280]{1,0:T(8,128)(2,1)}, u32[]{:S(2)}, u32[]{:S(2)}) collective-permute-start(bf16[128,1280]{1,0:T(8,128)(2,1)S(1)} %collective-permute-done.7.refs_6_), channel_id=1, source_target_pairs={{0,1},{1,0},{2,3},{3,2},{4,5},{5,4},{6,7},{7,6},{8,9},{9,8},{10,11... | collective-permute-start | bytes 983048 | tf_op jit(solution)/shard_map/ppermute | solution.py:324
  69.0 7.9 %collective-permute-start.15 = (bf16[128,1280]{1,0:T(8,128)(2,1)S(1)}, bf16[128,1280]{1,0:T(8,128)(2,1)}, u32[]{:S(2)}, u32[]{:S(2)}) collective-permute-start(bf16[128,1280]{1,0:T(8,128)(2,1)S(1)} %collective-permute-done.8.refs_5_), channel_id=1, source_target_pairs={{0,1},{1,0},{2,3},{3,2},{4,5},{5,4},{6,7},{7,6},{8,9},{9,8},{10,11... | collective-permute-start | bytes 983048 | tf_op jit(solution)/shard_map/ppermute | solution.py:324
  76.8 2.0 %collective-permute-start.17 = (bf16[128,1280]{1,0:T(8,128)(2,1)}, bf16[128,1280]{1,0:T(8,128)(2,1)}, u32[]{:S(2)}, u32[]{:S(2)}) collective-permute-start(bf16[128,1280]{1,0:T(8,128)(2,1)} %collective-permute-done.9.refs_7_), channel_id=1, source_target_pairs={{0,1},{1,0},{2,3},{3,2},{4,5},{5,4},{6,7},{7,6},{8,9},{9,8},{10,11... | collective-permute-start | bytes 983048 | tf_op jit(solution)/shard_map/ppermute | solution.py:324
  78.8 2.2 %copy-start.3 = (bf16[2,1024,1024]{2,1,0:T(8,128)(2,1)S(1)}, bf16[2,1024,1024]{2,1,0:T(8,128)(2,1)}, u32[]{:S(2)}) copy-start(bf16[2,1024,1024]{2,1,0:T(8,128)(2,1)} %copy-done.2) | copy-start | bytes 12582916
  81.0 1.6 %copy-start.5 = (bf16[1024,1024]{1,0:T(8,128)(2,1)S(1)}, bf16[1024,1024]{1,0:T(8,128)(2,1)}, u32[]{:S(2)}) copy-start(bf16[1024,1024]{1,0:T(8,128)(2,1)} %copy-done.4) | copy-start | bytes 6291460
  82.6 9.5 %copy-start.7 = (s32[256]{0:T(256)S(1)}, s32[256]{0:T(256)}, u32[]{:S(2)}) copy-start(s32[256]{0:T(256)} %param.11) | copy-start | bytes 3076

commit v5 on v4

--- a/solution.py
+++ b/solution.py
@@ -127,7 +127,14 @@
             self.edges.append(jnp.sum(self.used * jnp.floor((reach + extra) * 0.5), axis=0, keepdims=True))
 
 
-def pack_kernel(shells, pairs_ref, count_ref, vir_ref, occ_ref, code_ref, *outs):
+def pack_kernel(shells, pairs_any, count_any, vir_ref, occ_ref, code_ref, *refs):
+    outs, (pairs_ref, count_ref, sems) = refs[:4], refs[4:]
+    copies = [
+        pltpu.make_async_copy(pairs_any, pairs_ref, sems.at[0]),
+        pltpu.make_async_copy(count_any, count_ref, sems.at[1]),
+    ]
+    for copy in copies:
+        copy.start()
     me = lax.axis_index("shell")
     core, y = lax.rem(me, 2), lax.rem(lax.div(me, 2), 2)
     here, nvir = vir_ref.shape
@@ -142,6 +149,8 @@
             out[:, :width] = jnp.dot(pick, part, preferred_element_type=F32).astype(BF16)
             part = occ_ref[:, pl.ds(pl.multiple_of(half * thin, 128), thin)]
             out[:, width:] = jnp.dot(pick, part, preferred_element_type=F32).astype(BF16)
+    for copy in copies:
+        copy.wait()
     code = pairs_ref[1:2, :] + shells * pairs_ref[0:1, :]
     code = jnp.where(iota((1, BLK_DEV), 1) < count_ref[...], code, -1).astype(F32)
     square = (BLK_DEV, BLK_DEV)
@@ -263,7 +272,7 @@
 
 
 def last_kernel(count, me_ref, rows_ref, placed_ref, *refs):
-    pieces, (out_ref, parts_ref, half_ref) = refs[: 2 * count], refs[2 * count :]
+    pieces, (out_ref, occ_ref, half_ref) = refs[: 2 * count], refs[2 * count :]
     sides = [pieces[:count], pieces[count:]]
     width = pieces[0].shape[1] - 128
     tile = out_ref.shape[2]
@@ -275,13 +284,12 @@
     def _():
         for far, side in enumerate(sides):
             occ = jnp.concatenate([piece[:, width:] for piece in side], axis=0)
-            part = jnp.dot(rows_ref[...], occ, preferred_element_type=F32).astype(BF16)
             half = lax.rem(core + far, CORES)
-            parts_ref[:, pl.ds(pl.multiple_of(half * 128, 128), 128)] = part
+            occ_ref[:, pl.ds(pl.multiple_of(half * 128, 128), 128)] = occ
+        part = jnp.dot(rows_ref[...], occ_ref[...], preferred_element_type=F32)
+        part = part.T.astype(BF16)
         for p in range(2):
-            piece = lax.dot_general(
-                parts_ref[...], placed_ref[p], (((0,), (0,)), ((), ())), preferred_element_type=F32
-            )
+            piece = jnp.dot(part, placed_ref[p], preferred_element_type=F32)
             half_ref[p * NOCC : (p + 1) * NOCC, :] = piece.astype(BF16)
 
     for far, side in enumerate(sides):
@@ -290,13 +298,13 @@
         def _():
             columns = pl.ds(pl.multiple_of(lax.rem(j, per) * tile, 128), tile)
             right = jnp.concatenate([piece[:, columns] for piece in side], axis=0)
-            for p in range(2):
-                left = half_ref[p * NOCC : (p + 1) * NOCC, :]
-                out_ref[p] = jnp.dot(left, right, preferred_element_type=F32).astype(BF16)
+            total = jnp.dot(half_ref[...], right, preferred_element_type=F32).astype(BF16)
+            out_ref[...] = total.reshape(out_ref.shape)
 
 
 VMEM = pl.BlockSpec(memory_space=pltpu.VMEM)
 SMEM = pl.BlockSpec(memory_space=pltpu.SMEM)
+HBM = pl.BlockSpec(memory_space=pltpu.HBM)
 
 
 def shape(*dims, dtype=BF16):
@@ -326,13 +334,18 @@
     code, keep, to_core, to_y, to_both = pl.pallas_call(
         functools.partial(pack_kernel, size_row.shape[1]),
         out_shape=[shape(n, BLK_DEV, 128, dtype=jnp.int32)] + [shape(here // 2, packed)] * 4,
-        in_specs=[VMEM] * 4,
+        in_specs=[HBM] * 2 + [VMEM] * 2,
         out_specs=[VMEM] * 5,
+        scratch_shapes=[
+            pltpu.VMEM((2, BLK_DEV), jnp.int32),
+            pltpu.VMEM((1, 1), jnp.int32),
+            pltpu.SemaphoreType.DMA((2,)),
+        ],
         compiler_params=params(12),
         cost_estimate=cost(3e8, 3e6),
         name="pack_rows",
     )(block_pairs.T, block_count.reshape(1, 1), vir_coef, occ_coef)
-    fresh = [keep, swap(to_core, 1), swap(to_y, 2), swap(to_both, 3)]
+    to_y, to_both, to_core = swap(to_y, 2), swap(to_both, 3), swap(to_core, 1)
     code = lax.all_to_all(code, "shell", split_axis=0, concat_axis=0, tiled=True)
 
     mine, over = pl.pallas_call(
@@ -343,9 +356,11 @@
         compiler_params=params(12),
         cost_estimate=cost(3e8, 2e6),
         name="pick_rows",
-    )(code, size_row, *fresh)
-
-    panels, mine_again = lax.optimization_barrier((panels, mine))
+    )(code, size_row, keep, to_core, to_y, to_both)
+
+    across, beside, mine_y = swap(mine, 8), swap(mine, 4), swap(mine, 2)
+    beside, mine_y, panels = lax.optimization_barrier((beside, mine_y, panels))
+    beside_y = swap(beside, 2)
     send = pl.pallas_call(
         send_kernel,
         out_shape=shape(n, 2 * BLK_DEV, EDGE * EDGE),
@@ -357,10 +372,13 @@
     )(panels)
     got = lax.all_to_all(send, "shell", split_axis=0, concat_axis=0, tiled=True)
 
-    across, beside, mine_y = swap(mine, 8), swap(mine, 4), swap(mine, 2)
-    beside, mine_y, got_late = lax.optimization_barrier((beside, mine_y, got))
-    beside_y = swap(beside, 2)
-
+
+    far = [swap(mine, 1), swap(mine_y, 1), swap(beside, 1)]
+    across, beside_y, got, *far = lax.optimization_barrier((across, beside_y, got, *far))
+    corner, across_y = swap(across, 4), swap(across, 2)
+    far += [swap(beside_y, 1), swap(across, 1)]
+    corner, across_y, got, *far = lax.optimization_barrier((corner, across_y, got, *far))
+    corner_y = swap(corner, 2)
     rows, placed = pl.pallas_call(
         functools.partial(place_kernel, here),
         out_shape=(shape(LIVE_DEV * n * EDGE, room), shape(2, LIVE_DEV * n * EDGE, room)),
@@ -369,14 +387,12 @@
         compiler_params=params(20),
         cost_estimate=cost(4e9, 8e6),
         name="place_panels",
-    )(code, got_late, size_row)
-
-    across, beside_y, rows, placed = lax.optimization_barrier((across, beside_y, rows, placed))
-    corner, across_y = swap(across, 4), swap(across, 2)
-    corner, across_y = lax.optimization_barrier((corner, across_y))
-    corner_y = swap(corner, 2)
+    )(code, got, size_row)
+
+    far += [swap(across_y, 1), swap(corner, 1)]
+    corner_y, rows, placed, *far = lax.optimization_barrier((corner_y, rows, placed, *far))
+    far.append(swap(corner_y, 1))
     pieces = [mine, mine_y, beside, beside_y, across, across_y, corner, corner_y]
-    far = [swap(piece, 1) for piece in pieces]
 
     tile = width // 3
     count = len(pieces)
@@ -388,7 +404,7 @@
             grid=(nvir // tile,),
             in_specs=[VMEM] * (2 + 2 * count),
             out_specs=pl.BlockSpec((2, NOCC, tile), lambda j, o: (0, 0, (j + 3 * (o[0] % 2)) % 6)),
-            scratch_shapes=[pltpu.VMEM((LIVE_DEV * n * EDGE, NOCC), BF16), pltpu.VMEM((2 * NOCC, room), BF16)],
+            scratch_shapes=[pltpu.VMEM((room, NOCC), BF16), pltpu.VMEM((2 * NOCC, room), BF16)],
         ),
         compiler_params=params(24),
         cost_estimate=cost(4e9, 1e7),

time: 100 us -> 107 us (1.070)
  local copies, waits for them, and re-layouts: 8.61 us -> 15.5 us
  starting transfers between devices: 18.2 us -> 14.1 us
  waiting for transfers between devices: 26.5 us -> 29.8 us
    unnamed x14 -> x30, local copies, waits for them, and re-layouts: 8.61 us -> 15.5 us
    ppermute x18, starting transfers between devices: 14.2 us -> 10.3 us  [swap(): return lax.ppermute(array, 'shell', [(i, i ^ bit) for i in range(n)])]
    all_to_all x1, waiting for transfers between devices: 5.58 us -> 7.91 us  [short_way(): got = lax.all_to_all(send, 'shell', split_axis=0, concat_axis=0, tiled=True)]
  transfers between devices with their start and end apart: 19 -> 19, of which waited for: 6 -> 5; matrix products, arithmetic and copies ran while one was open for 0% -> 0% of each run, Pallas kernels for 6% -> 5%
where the time goes in v5:
time: 107 us; the launch traced here: 106 us
  waiting for transfers between devices  29.8 us (28%)
  Pallas kernels  18.7 us (17%)
  local copies, waits for them, and re-layouts  15.5 us (14%)
  between operations  14.2 us (13%)
  starting transfers between devices  14.1 us (13%)
  blocking collectives  12.8 us (12%)
    ppermute x18, waiting for transfers between devices, swap(): return lax.ppermute(array, 'shell', [(i, i ^ bit) for i in range(n)])  21.9 us
    unnamed x30, local copies, waits for them, and re-layouts  15.5 us
    all_to_all x1, blocking collectives, short_way(): lax.all_to_all(code, 'shell', split_axis=0, concat_axis=0, tiled=True)  12.8 us
    ppermute x18, starting transfers between devices, swap(): return lax.ppermute(array, 'shell', [(i, i ^ bit) for i in range(n)])  10.3 us
    pallas_call x1, Pallas kernels, short_way(): pl.pallas_call(functools.partial(last_kernel, count), out_shape=shape(2,...  9.33 us
    all_to_all x1, waiting for transfers between devices, short_way(): got = lax.all_to_all(send, 'shell', split_axis=0, concat_axis=0, tiled=True)  7.91 us
    pallas_call x1, Pallas kernels, short_way(): pl.pallas_call(functools.partial(place_kernel, here), out_shape=(shape(LI...  4.82 us
    all_to_all x1, starting transfers between devices, short_way(): got = lax.all_to_all(send, 'shell', split_axis=0, concat_axis=0, tiled=True)  3.8 us
  transfers between devices with their start and end apart: 19, of which 5 were waited for; matrix products, arithmetic and copies ran while one was open for 0% of the time, Pallas kernels for 5%

profile of v5, /device:TPU:0, one launch (start us, length us, event | category | flops | bytes accessed | tf_op | source)
XLA Modules:
  0.0 106.0 jit_solution(7730773861664770440)
XLA Ops:
  7.2 0.7 copy-done.9
  7.9 1.7 %pack_rows.1 = (s32[16,8,128]{2,1,0:T(8,128)S(1)}, bf16[80,1280]{1,0:T(8,128)(2,1)S(1)}, bf16[80,1280]{1,0:T(8,128)(2,1)S(1)}, bf16[80,1280]{1,0:T(8,128)(2,1)S(1)}, bf16[80,1280]{1,0:T(8,128)(2,1)S(1)}) custom-call(s32[2,8]{1,0:T(2,128)S(1)} %bitcast.61, s32[1,1]{1,0:T(1,128)} %bitcast.60.count_any, bf16[160,2304]{1,0:T(8,128)(2,1)} %vir_ref.1, ...), custom_call_target="tpu_custom_call" | custom-call | flops 300000000 | bytes 3000000 | tf_op jit(solution)/shard_map/pack_rows/pallas_call | solution.py:334
  9.6 0.5 collective-permute-start
  10.1 2.6 %collective-permute-start.1 = (bf16[80,1280]{1,0:T(8,128)(2,1)S(1)}, bf16[80,1280]{1,0:T(8,128)(2,1)S(1)}, u32[]{:S(2)}, u32[]{:S(2)}) collective-permute-start(bf16[80,1280]{1,0:T(8,128)(2,1)S(1)} %get-tuple-element.184), channel_id=1, source_target_pairs={{0,2},{1,3},{2,0},{3,1},{4,6},{5,7},{6,4},{7,5},{8,10},{9,11},{10,... | collective-permute-start | bytes 614408 | tf_op jit(solution)/shard_map/ppermute | solution.py:332
  12.8 12.8 %all_to_all.10.code_ref = s32[16,8,128]{2,1,0:T(8,128)S(1)} all-to-all(s32[16,8,128]{2,1,0:T(8,128)S(1)} %get-tuple-element.181), channel_id=1, replica_groups=mesh['groups'=2,'shell'=16] {'shell'}, dimensions={0} | all-to-all | bytes 131072 | tf_op jit(solution)/shard_map/all_to_all | solution.py:349
  25.6 2.2 %pick_rows.1 = (bf16[128,1280]{1,0:T(8,128)(2,1)S(1)}, s32[1]{0:T(128)}) custom-call(s32[16,8,128]{2,1,0:T(8,128)S(1)} %all_to_all.10.code_ref, s32[1,256]{1,0:T(1,128)} %bitcast.64, bf16[80,1280]{1,0:T(8,128)(2,1)S(1)} %get-tuple-element.182.refs_0_, bf16[80,1280]{1,0:T(8,128)(2,1)S(1)} %collective-permute-done.refs_1_, ...), custom_call_target="tpu_custom_call" | custom-call | flops 300000000 | bytes 2000000 | tf_op jit(solution)/shard_map/pick_rows/pallas_call | solution.py:351
  28.0 1.1 %collective-permute-start.5 = (bf16[128,1280]{1,0:T(8,128)(2,1)S(1)}, bf16[128,1280]{1,0:T(8,128)(2,1)S(1)}, u32[]{:S(2)}, u32[]{:S(2)}) collective-permute-start(bf16[128,1280]{1,0:T(8,128)(2,1)S(1)} %get-tuple-element.187.refs_0_), channel_id=1, source_target_pairs={{0,2},{1,3},{2,0},{3,1},{4,6},{5,7},{6,4},{7,5},{8,10},{9,11},{10,... | collective-permute-start | bytes 983048 | tf_op jit(solution)/shard_map/ppermute | solution.py:332
  29.0 2.6 %collective-permute-start.3 = (bf16[128,1280]{1,0:T(8,128)(2,1)S(1)}, bf16[128,1280]{1,0:T(8,128)(2,1)S(1)}, u32[]{:S(2)}, u32[]{:S(2)}) collective-permute-start(bf16[128,1280]{1,0:T(8,128)(2,1)S(1)} %get-tuple-element.187.refs_0_), channel_id=1, source_target_pairs={{0,8},{1,9},{2,10},{3,11},{4,12},{5,13},{6,14},{7,15},{8,0},{9,1},... | collective-permute-start | bytes 983048 | tf_op jit(solution)/shard_map/ppermute | solution.py:332
  31.6 11.3 %collective-permute-done.4.refs_2_ = bf16[128,1280]{1,0:T(8,128)(2,1)S(1)} collective-permute-done((bf16[128,1280]{1,0:T(8,128)(2,1)S(1)}, bf16[128,1280]{1,0:T(8,128)(2,1)S(1)}, u32[]{:S(2)}, u32[]{:S(2)}) %collective-permute-start.4) | collective-permute-done | bytes 327712 | tf_op jit(solution)/shard_map/ppermute | solution.py:332
  43.0 0.6 collective-permute-start.6
  44.1 0.9 copy-done
  45.0 0.7 turn_panels.1
  45.7 3.8 %all-to-all-start.1 = ((bf16[16,16,256]{2,1,0:T(8,128)(2,1)}), bf16[16,16,256]{2,1,0:T(8,128)(2,1)S(1)}, u32[]{:S(2)}, u32[]{:S(2)}) async-start(bf16[16,16,256]{2,1,0:T(8,128)(2,1)} %turn_panels.1), calls=%async_computation.1 | async-start | bytes 262144 | tf_op jit(solution)/shard_map/all_to_all | solution.py:373
  49.6 7.9 %all-to-all-done.1.got_ref = bf16[16,16,256]{2,1,0:T(8,128)(2,1)S(1)} async-done(((bf16[16,16,256]{2,1,0:T(8,128)(2,1)}), bf16[16,16,256]{2,1,0:T(8,128)(2,1)S(1)}, u32[]{:S(2)}, u32[]{:S(2)}) %all-to-all-start.1) | async-done | bytes 131104 | tf_op jit(solution)/shard_map/all_to_all | solution.py:373
  58.4 8.1 %collective-permute-done.10.refs_6_ = bf16[128,1280]{1,0:T(8,128)(2,1)S(1)} collective-permute-done((bf16[128,1280]{1,0:T(8,128)(2,1)S(1)}, bf16[128,1280]{1,0:T(8,128)(2,1)S(1)}, u32[]{:S(2)}, u32[]{:S(2)}) %collective-permute-start.10) | collective-permute-done | bytes 327712 | tf_op jit(solution)/shard_map/ppermute | solution.py:332
  66.9 0.7 copy-done.1
  67.7 0.7 copy-done.3
  68.4 0.7 collective-permute-start.14
  69.7 4.8 %place_panels.1 = (bf16[1024,1024]{1,0:T(8,128)(2,1)S(1)}, bf16[2,1024,1024]{2,1,0:T(8,128)(2,1)S(1)}) custom-call(s32[16,8,128]{2,1,0:T(8,128)S(1)} %all_to_all.10.code_ref, bf16[16,16,256]{2,1,0:T(8,128)(2,1)S(1)} %all-to-all-done.1.got_ref, s32[1,256]{1,0:T(1,128)} %bitcast.65), custom_call_target="tpu_custom_call" | custom-call | flops 4000000000 | bytes 8000000 | tf_op jit(solution)/shard_map/place_panels/pallas_call | solution.py:382
  74.5 1.9 %copy-done.10 = bf16[2,1024,1024]{2,1,0:T(8,128)(2,1)} copy-done((bf16[2,1024,1024]{2,1,0:T(8,128)(2,1)}, bf16[2,1024,1024]{2,1,0:T(8,128)(2,1)S(1)}, u32[]{:S(2)}) %copy-start.10) | copy-done | bytes 4194328
  76.5 1.3 %copy-done.12 = bf16[1024,1024]{1,0:T(8,128)(2,1)} copy-done((bf16[1024,1024]{1,0:T(8,128)(2,1)}, bf16[1024,1024]{1,0:T(8,128)(2,1)S(1)}, u32[]{:S(2)}) %copy-start.12) | copy-done | bytes 2097176
  77.8 0.7 copy-done.7
  78.5 0.7 copy-done.5
  79.2 2.0 %collective-permute-done.17.refs_15_ = bf16[128,1280]{1,0:T(8,128)(2,1)} collective-permute-done((bf16[128,1280]{1,0:T(8,128)(2,1)}, bf16[128,1280]{1,0:T(8,128)(2,1)}, u32[]{:S(2)}, u32[]{:S(2)}) %collective-permute-start.17) | collective-permute-done | bytes 327712 | tf_op jit(solution)/shard_map/ppermute | solution.py:332
  81.2 1.0 copy-done.2
  82.2 1.0 copy-done.4
  83.2 1.0 copy-done.6
  84.1 1.0 copy-done.8
  85.1 2.2 %copy-done.11 = bf16[2,1024,1024]{2,1,0:T(8,128)(2,1)S(1)} copy-done((bf16[2,1024,1024]{2,1,0:T(8,128)(2,1)S(1)}, bf16[2,1024,1024]{2,1,0:T(8,128)(2,1)}, u32[]{:S(2)}) %copy-start.11) | copy-done | bytes 4194328
  87.3 1.6 %copy-done.13 = bf16[1024,1024]{1,0:T(8,128)(2,1)S(1)} copy-done((bf16[1024,1024]{1,0:T(8,128)(2,1)S(1)}, bf16[1024,1024]{1,0:T(8,128)(2,1)}, u32[]{:S(2)}) %copy-start.13) | copy-done | bytes 2097176
  88.9 9.3 %last_product.1 = bf16[2,256,2304]{2,1,0:T(8,128)(2,1)} custom-call(s32[1]{0:T(128)} %bitcast.17.me_ref, bf16[1024,1024]{1,0:T(8,128)(2,1)S(1)} %copy-done.13, bf16[2,1024,1024]{2,1,0:T(8,128)(2,1)S(1)} %copy-done.11, bf16[128,1280]{1,0:T(8,128)(2,1)S(1)} %get-tuple-element.187.refs_0_, bf16[128,1280]{1,0:T(8,128)(2,1)S(1)} %collective-permute-done.5.refs_1_, ...), custom_call_target="tpu_custom_call" | custom-call | flops 4000000000 | bytes 10000000 | tf_op jit(solution)/shard_map/last_product/pallas_call | solution.py:399
  98.2 0.9 while.17
  (43 shorter events, 2.6 us)
Async XLA Ops:
  9.6 16.0 %collective-permute-start = (bf16[80,1280]{1,0:T(8,128)(2,1)S(1)}, bf16[80,1280]{1,0:T(8,128)(2,1)S(1)}, u32[]{:S(2)}, u32[]{:S(2)}) collective-permute-start(bf16[80,1280]{1,0:T(8,128)(2,1)S(1)} %get-tuple-element.183), channel_id=1, source_target_pairs={{0,1},{1,0},{2,3},{3,2},{4,5},{5,4},{6,7},{7,6},{8,9},{9,8},{10,11... | collective-permute-start | bytes 614408 | tf_op jit(solution)/shard_map/ppermute | solution.py:332
  10.1 15.5 %collective-permute-start.1 = (bf16[80,1280]{1,0:T(8,128)(2,1)S(1)}, bf16[80,1280]{1,0:T(8,128)(2,1)S(1)}, u32[]{:S(2)}, u32[]{:S(2)}) collective-permute-start(bf16[80,1280]{1,0:T(8,128)(2,1)S(1)} %get-tuple-element.184), channel_id=1, source_target_pairs={{0,2},{1,3},{2,0},{3,1},{4,6},{5,7},{6,4},{7,5},{8,10},{9,11},{10,... | collective-permute-start | bytes 614408 | tf_op jit(solution)/shard_map/ppermute | solution.py:332
  12.7 12.9 %collective-permute-start.2 = (bf16[80,1280]{1,0:T(8,128)(2,1)S(1)}, bf16[80,1280]{1,0:T(8,128)(2,1)S(1)}, u32[]{:S(2)}, u32[]{:S(2)}) collective-permute-start(bf16[80,1280]{1,0:T(8,128)(2,1)S(1)} %get-tuple-element.185), channel_id=1, source_target_pairs={{0,3},{1,2},{2,1},{3,0},{4,7},{5,6},{6,5},{7,4},{8,11},{9,10},{10,... | collective-permute-start | bytes 614408 | tf_op jit(solution)/shard_map/ppermute | solution.py:332
  27.8 15.2 %collective-permute-start.4 = (bf16[128,1280]{1,0:T(8,128)(2,1)S(1)}, bf16[128,1280]{1,0:T(8,128)(2,1)S(1)}, u32[]{:S(2)}, u32[]{:S(2)}) collective-permute-start(bf16[128,1280]{1,0:T(8,128)(2,1)S(1)} %get-tuple-element.187.refs_0_), channel_id=1, source_target_pairs={{0,4},{1,5},{2,6},{3,7},{4,0},{5,1},{6,2},{7,3},{8,12},{9,13},{10,... | collective-permute-start | bytes 983048 | tf_op jit(solution)/shard_map/ppermute | solution.py:332
  28.0 15.0 %collective-permute-start.5 = (bf16[128,1280]{1,0:T(8,128)(2,1)S(1)}, bf16[128,1280]{1,0:T(8,128)(2,1)S(1)}, u32[]{:S(2)}, u32[]{:S(2)}) collective-permute-start(bf16[128,1280]{1,0:T(8,128)(2,1)S(1)} %get-tuple-element.187.refs_0_), channel_id=1, source_target_pairs={{0,2},{1,3},{2,0},{3,1},{4,6},{5,7},{6,4},{7,5},{8,10},{9,11},{10,... | collective-permute-start | bytes 983048 | tf_op jit(solution)/shard_map/ppermute | solution.py:332
  29.0 20.5 %collective-permute-start.3 = (bf16[128,1280]{1,0:T(8,128)(2,1)S(1)}, bf16[128,1280]{1,0:T(8,128)(2,1)S(1)}, u32[]{:S(2)}, u32[]{:S(2)}) collective-permute-start(bf16[128,1280]{1,0:T(8,128)(2,1)S(1)} %get-tuple-element.187.refs_0_), channel_id=1, source_target_pairs={{0,8},{1,9},{2,10},{3,11},{4,12},{5,13},{6,14},{7,15},{8,0},{9,1},... | collective-permute-start | bytes 983048 | tf_op jit(solution)/shard_map/ppermute | solution.py:332
  31.6 17.9 %collective-permute-start.7 = (bf16[128,1280]{1,0:T(8,128)(2,1)S(1)}, bf16[128,1280]{1,0:T(8,128)(2,1)S(1)}, u32[]{:S(2)}, u32[]{:S(2)}) collective-permute-start(bf16[128,1280]{1,0:T(8,128)(2,1)S(1)} %get-tuple-element.187.refs_0_), channel_id=1, source_target_pairs={{0,1},{1,0},{2,3},{3,2},{4,5},{5,4},{6,7},{7,6},{8,9},{9,8},{10,11... | collective-permute-start | bytes 983048 | tf_op jit(solution)/shard_map/ppermute | solution.py:332
  43.0 14.5 %collective-permute-start.6 = (bf16[128,1280]{1,0:T(8,128)(2,1)S(1)}, bf16[128,1280]{1,0:T(8,128)(2,1)S(1)}, u32[]{:S(2)}, u32[]{:S(2)}) collective-permute-start(bf16[128,1280]{1,0:T(8,128)(2,1)S(1)} %collective-permute-done.4.refs_2_), channel_id=1, source_target_pairs={{0,2},{1,3},{2,0},{3,1},{4,6},{5,7},{6,4},{7,5},{8,10},{9,11},{10,... | collective-permute-start | bytes 983048 | tf_op jit(solution)/shard_map/ppermute | solution.py:332
  43.6 13.9 %collective-permute-start.8 = (bf16[128,1280]{1,0:T(8,128)(2,1)S(1)}, bf16[128,1280]{1,0:T(8,128)(2,1)S(1)}, u32[]{:S(2)}, u32[]{:S(2)}) collective-permute-start(bf16[128,1280]{1,0:T(8,128)(2,1)S(1)} %collective-permute-done.5.refs_1_), channel_id=1, source_target_pairs={{0,1},{1,0},{2,3},{3,2},{4,5},{5,4},{6,7},{7,6},{8,9},{9,8},{10,11... | collective-permute-start | bytes 983048 | tf_op jit(solution)/shard_map/ppermute | solution.py:332
  43.6 13.9 %collective-permute-start.9 = (bf16[128,1280]{1,0:T(8,128)(2,1)S(1)}, bf16[128,1280]{1,0:T(8,128)(2,1)S(1)}, u32[]{:S(2)}, u32[]{:S(2)}) collective-permute-start(bf16[128,1280]{1,0:T(8,128)(2,1)S(1)} %collective-permute-done.4.refs_2_), channel_id=1, source_target_pairs={{0,1},{1,0},{2,3},{3,2},{4,5},{5,4},{6,7},{7,6},{8,9},{9,8},{10,11... | collective-permute-start | bytes 983048 | tf_op jit(solution)/shard_map/ppermute | solution.py:332
  44.1 0.9 copy-start
  45.7 11.7 %all-to-all-start.1 = ((bf16[16,16,256]{2,1,0:T(8,128)(2,1)}), bf16[16,16,256]{2,1,0:T(8,128)(2,1)S(1)}, u32[]{:S(2)}, u32[]{:S(2)}) async-start(bf16[16,16,256]{2,1,0:T(8,128)(2,1)} %turn_panels.1), calls=%async_computation.1 | async-start | bytes 262144 | tf_op jit(solution)/shard_map/all_to_all | solution.py:373
  57.5 9.0 %collective-permute-start.10 = (bf16[128,1280]{1,0:T(8,128)(2,1)S(1)}, bf16[128,1280]{1,0:T(8,128)(2,1)S(1)}, u32[]{:S(2)}, u32[]{:S(2)}) collective-permute-start(bf16[128,1280]{1,0:T(8,128)(2,1)S(1)} %collective-permute-done.3.refs_4_), channel_id=1, source_target_pairs={{0,4},{1,5},{2,6},{3,7},{4,0},{5,1},{6,2},{7,3},{8,12},{9,13},{10,... | collective-permute-start | bytes 983048 | tf_op jit(solution)/shard_map/ppermute | solution.py:332
  57.6 9.4 %collective-permute-start.11 = (bf16[128,1280]{1,0:T(8,128)(2,1)S(1)}, bf16[128,1280]{1,0:T(8,128)(2,1)S(1)}, u32[]{:S(2)}, u32[]{:S(2)}) collective-permute-start(bf16[128,1280]{1,0:T(8,128)(2,1)S(1)} %collective-permute-done.3.refs_4_), channel_id=1, source_target_pairs={{0,2},{1,3},{2,0},{3,1},{4,6},{5,7},{6,4},{7,5},{8,10},{9,11},{10,... | collective-permute-start | bytes 983048 | tf_op jit(solution)/shard_map/ppermute | solution.py:332
  57.9 9.1 %collective-permute-start.12 = (bf16[128,1280]{1,0:T(8,128)(2,1)S(1)}, bf16[128,1280]{1,0:T(8,128)(2,1)S(1)}, u32[]{:S(2)}, u32[]{:S(2)}) collective-permute-start(bf16[128,1280]{1,0:T(8,128)(2,1)S(1)} %collective-permute-done.6.refs_3_), channel_id=1, source_target_pairs={{0,1},{1,0},{2,3},{3,2},{4,5},{5,4},{6,7},{7,6},{8,9},{9,8},{10,11... | collective-permute-start | bytes 983048 | tf_op jit(solution)/shard_map/ppermute | solution.py:332
  57.9 9.8 %collective-permute-start.13 = (bf16[128,1280]{1,0:T(8,128)(2,1)S(1)}, bf16[128,1280]{1,0:T(8,128)(2,1)S(1)}, u32[]{:S(2)}, u32[]{:S(2)}) collective-permute-start(bf16[128,1280]{1,0:T(8,128)(2,1)S(1)} %collective-permute-done.3.refs_4_), channel_id=1, source_target_pairs={{0,1},{1,0},{2,3},{3,2},{4,5},{5,4},{6,7},{7,6},{8,9},{9,8},{10,11... | collective-permute-start | bytes 983048 | tf_op jit(solution)/shard_map/ppermute | solution.py:332
  66.9 0.7 copy-start.1
  67.7 0.7 copy-start.3
  68.4 9.4 %collective-permute-start.14 = (bf16[128,1280]{1,0:T(8,128)(2,1)S(1)}, bf16[128,1280]{1,0:T(8,128)(2,1)}, u32[]{:S(2)}, u32[]{:S(2)}) collective-permute-start(bf16[128,1280]{1,0:T(8,128)(2,1)S(1)} %collective-permute-done.10.refs_6_), channel_id=1, source_target_pairs={{0,2},{1,3},{2,0},{3,1},{4,6},{5,7},{6,4},{7,5},{8,10},{9,11},{10,... | collective-permute-start | bytes 983048 | tf_op jit(solution)/shard_map/ppermute | solution.py:332
  69.2 9.4 %collective-permute-start.16 = (bf16[128,1280]{1,0:T(8,128)(2,1)S(1)}, bf16[128,1280]{1,0:T(8,128)(2,1)S(1)}, u32[]{:S(2)}, u32[]{:S(2)}) collective-permute-start(bf16[128,1280]{1,0:T(8,128)(2,1)S(1)} %collective-permute-done.10.refs_6_), channel_id=1, source_target_pairs={{0,1},{1,0},{2,3},{3,2},{4,5},{5,4},{6,7},{7,6},{8,9},{9,8},{10,11... | collective-permute-start | bytes 983048 | tf_op jit(solution)/shard_map/ppermute | solution.py:332
  69.2 8.6 %collective-permute-start.15 = (bf16[128,1280]{1,0:T(8,128)(2,1)S(1)}, bf16[128,1280]{1,0:T(8,128)(2,1)S(1)}, u32[]{:S(2)}, u32[]{:S(2)}) collective-permute-start(bf16[128,1280]{1,0:T(8,128)(2,1)S(1)} %collective-permute-done.11.refs_5_), channel_id=1, source_target_pairs={{0,1},{1,0},{2,3},{3,2},{4,5},{5,4},{6,7},{7,6},{8,9},{9,8},{10,11... | collective-permute-start | bytes 983048 | tf_op jit(solution)/shard_map/ppermute | solution.py:332
  74.5 2.0 %copy-start.10 = (bf16[2,1024,1024]{2,1,0:T(8,128)(2,1)}, bf16[2,1024,1024]{2,1,0:T(8,128)(2,1)S(1)}, u32[]{:S(2)}) copy-start(bf16[2,1024,1024]{2,1,0:T(8,128)(2,1)S(1)} %get-tuple-element.208.placed_ref) | copy-start | bytes 12582916
  76.5 1.3 %copy-start.12 = (bf16[1024,1024]{1,0:T(8,128)(2,1)}, bf16[1024,1024]{1,0:T(8,128)(2,1)S(1)}, u32[]{:S(2)}) copy-start(bf16[1024,1024]{1,0:T(8,128)(2,1)S(1)} %get-tuple-element.207.rows_ref) | copy-start | bytes 6291460
  77.8 0.7 copy-start.7
  79.2 2.0 %collective-permute-start.17 = (bf16[128,1280]{1,0:T(8,128)(2,1)}, bf16[128,1280]{1,0:T(8,128)(2,1)}, u32[]{:S(2)}, u32[]{:S(2)}) collective-permute-start(bf16[128,1280]{1,0:T(8,128)(2,1)} %collective-permute-done.14.refs_7_), channel_id=1, source_target_pairs={{0,1},{1,0},{2,3},{3,2},{4,5},{5,4},{6,7},{7,6},{8,9},{9,8},{10,11... | collective-permute-start | bytes 983048 | tf_op jit(solution)/shard_map/ppermute | solution.py:332
  81.2 1.0 copy-start.2
  82.2 1.0 copy-start.4
  83.2 1.0 copy-start.6
  84.1 1.0 copy-start.8
  85.1 2.2 %copy-start.11 = (bf16[2,1024,1024]{2,1,0:T(8,128)(2,1)S(1)}, bf16[2,1024,1024]{2,1,0:T(8,128)(2,1)}, u32[]{:S(2)}) copy-start(bf16[2,1024,1024]{2,1,0:T(8,128)(2,1)} %copy-done.10) | copy-start | bytes 12582916
  87.3 1.6 %copy-start.13 = (bf16[1024,1024]{1,0:T(8,128)(2,1)S(1)}, bf16[1024,1024]{1,0:T(8,128)(2,1)}, u32[]{:S(2)}) copy-start(bf16[1024,1024]{1,0:T(8,128)(2,1)} %copy-done.12) | copy-start | bytes 6291460
  88.9 9.3 %copy-start.15 = (s32[256]{0:T(256)S(1)}, s32[256]{0:T(256)}, u32[]{:S(2)}) copy-start(s32[256]{0:T(256)} %param.11) | copy-start | bytes 3076
  (2 other events, 1.4 us)

commit v6 on v5

--- a/solution.py
+++ b/solution.py
@@ -179,10 +179,10 @@
             most = jnp.maximum(most, jnp.max(jnp.where(lane < Z, later - edges, 0.0), axis=1, keepdims=True))
     over_ref[0] = jnp.where(jnp.max(most) > CAP, 1, 0).astype(jnp.int32)
 
-    width = vir_width = out_ref.shape[1] - 128
+    width = out_ref.shape[1] - 128
     even = y == 0
     totals = [jnp.zeros((CAP, width), F32), jnp.zeros((CAP, 128), F32)]
-    columns = [slice(0, vir_width), slice(vir_width, vir_width + 128)]
+    columns = [slice(0, width), slice(width, width + 128)]
     extra = jnp.where(even, lists[0].extra[0], lists[0].extra[1])
     for k, source in enumerate(sources):
         device = 4 * z + 2 * lax.rem(y + k // 2, 2) + lax.rem(core + k % 2, 2)
@@ -204,8 +204,29 @@
         out_ref[:, column] = total.astype(BF16)
 
 
-def place_kernel(here, code_ref, got_ref, size_ref, rows_ref, placed_ref):
-    chip = lax.div(lax.axis_index("shell"), CORES)
+def slot_of(window, chip):
+    z = lax.div(chip, Y)
+    slot = window ^ chip
+    inner = (z == 1) | (z == 2)
+    return jnp.where(inner & (slot >= 2 * Y), slot ^ Y, slot)
+
+
+def half_kernel(here, code_ref, got_ref, size_ref, *refs):
+    count = (len(refs) - 4) // 2
+    pieces, (half_ref, late_ref, occ_ref, sems) = refs[: 2 * count], refs[2 * count :]
+    me = lax.axis_index("shell")
+    core, chip = lax.rem(me, CORES), lax.div(me, CORES)
+    width = pieces[0].shape[1] - 128
+    copies = []
+    for far in range(2):
+        half = lax.rem(core + far, CORES)
+        for k in range(count):
+            at = far * count + k
+            target = occ_ref.at[pl.ds(k * CAP, CAP), pl.ds(pl.multiple_of(half * 128, 128), 128)]
+            copies.append(pltpu.make_async_copy(pieces[at].at[:, pl.ds(width, 128)], target, sems.at[at]))
+    for copy in copies:
+        copy.start()
+    occ_ref[count * CAP :, :] = jnp.zeros((occ_ref.shape[0] - count * CAP, occ_ref.shape[1]), BF16)
     window = CORES * Y * here
     shell_count = size_ref.shape[1]
     got = got_ref[...].astype(F32)
@@ -241,7 +262,7 @@
         place = jnp.where(odd, spread(hot, chosen.ahead[1]), spread(hot, chosen.ahead[0]))
         place += jnp.floor(step * 0.5)
         offsets = [
-            [((w * Y + k) ^ chip).astype(F32) * CAP - lane_value(e, w) for w in range(Z)]
+            [slot_of(w * Y + k, chip).astype(F32) * CAP - lane_value(e, w) for w in range(Z)]
             for k, e in enumerate(chosen.edges)
         ]
         offset = jnp.where(odd, offsets[1][0], offsets[0][0])
@@ -251,60 +272,92 @@
 
     place_c, place_r = places(hots[0], lists[0]), places(hots[1], lists[1])
     span = 16 * EDGE
-    width = rows_ref.shape[1]
+    width = half_ref.shape[1]
     s_in, l_in = iota((span, span), 0), iota((span, span), 1)
     keep_m = (l_in // EDGE) == (s_in % EDGE)
     fold = zero_one((s_in % EDGE) == (l_in % EDGE)).astype(BF16)
     same_slot = (s_in // EDGE) == (l_in // EDGE)
     blocks = [taken(got[:, p * BLK_DEV : (p + 1) * BLK_DEV, :].reshape(slots, span)) for p in range(2)]
     lanes = iota((span, width), 1).astype(F32)
+    for copy in copies:
+        copy.wait()
+    occ = occ_ref[...]
+    late = []
     for g in range(kept // 16):
         rows = slice(g * span, (g + 1) * span)
-        rows_ref[rows, :] = zero_one(place_r[rows] == lanes).astype(BF16)
+        r_hot = zero_one(place_r[rows] == lanes).astype(BF16)
         c_hot = zero_one(place_c[rows] == lanes).astype(BF16)
+        part = jnp.dot(r_hot, occ, preferred_element_type=F32).T.astype(BF16)
         for p in range(2):
             block = blocks[p][g * 16 : (g + 1) * 16].reshape(16, 1, span)
             block = jnp.broadcast_to(block, (16, EDGE, span)).reshape(span, span)
             block = jnp.where(keep_m, block, 0.0).astype(BF16)
             diag = jnp.dot(block, fold, preferred_element_type=F32)
             diag = jnp.where(same_slot, diag, 0.0).astype(BF16)
-            placed_ref[p, rows, :] = jnp.dot(diag, c_hot, preferred_element_type=F32).astype(BF16)
-
-
-def last_kernel(count, me_ref, rows_ref, placed_ref, *refs):
-    pieces, (out_ref, occ_ref, half_ref) = refs[: 2 * count], refs[2 * count :]
-    sides = [pieces[:count], pieces[count:]]
-    width = pieces[0].shape[1] - 128
+            placed = jnp.dot(diag, c_hot, preferred_element_type=F32).astype(BF16)
+            piece = jnp.dot(part, placed, preferred_element_type=F32)
+            rows_p = slice(p * NOCC, (p + 1) * NOCC)
+            rows_l = slice(p * CAP, (p + 1) * CAP)
+            later = jnp.dot(r_hot[:, count * CAP :].T, placed, preferred_element_type=F32)
+            if g == 0:
+                half_ref[rows_p, :] = piece
+                late.append(later)
+            else:
+                half_ref[rows_p, :] += piece
+                late[p] += later
+    for p in range(2):
+        late_ref[p * CAP : (p + 1) * CAP, :] = late[p].astype(BF16)
+
+
+def last_kernel(count, me_ref, part_ref, late_ref, *refs):
+    pieces, (out_ref, right_ref, occ_ref, half_ref, sems) = refs[: 2 * count], refs[2 * count :]
     tile = out_ref.shape[2]
+    width = right_ref.shape[2]
     per = width // tile
     core = lax.rem(me_ref[0], CORES)
     j = pl.program_id(0)
 
+    def occ_copies():
+        for far in range(2):
+            half = lax.rem(core + far, CORES)
+            target = occ_ref.at[:, pl.ds(pl.multiple_of(half * 128, 128), 128)]
+            source = pieces[far * count + count - 1].at[:, pl.ds(width, 128)]
+            yield pltpu.make_async_copy(source, target, sems.at[2 * count + far])
+
+    def copies(far):
+        for k in range(count):
+            at = far * count + k
+            target = right_ref.at[far, pl.ds(k * CAP, CAP), :]
+            yield pltpu.make_async_copy(pieces[at].at[:, pl.ds(0, width)], target, sems.at[at])
+
     @pl.when(j == 0)
     def _():
-        for far, side in enumerate(sides):
-            occ = jnp.concatenate([piece[:, width:] for piece in side], axis=0)
-            half = lax.rem(core + far, CORES)
-            occ_ref[:, pl.ds(pl.multiple_of(half * 128, 128), 128)] = occ
-        part = jnp.dot(rows_ref[...], occ_ref[...], preferred_element_type=F32)
-        part = part.T.astype(BF16)
+        for copy in (*occ_copies(), *copies(0), *copies(1)):
+            copy.start()
+        for copy in occ_copies():
+            copy.wait()
+        occ = occ_ref[...].T
         for p in range(2):
-            piece = jnp.dot(part, placed_ref[p], preferred_element_type=F32)
-            half_ref[p * NOCC : (p + 1) * NOCC, :] = piece.astype(BF16)
-
-    for far, side in enumerate(sides):
-
-        @pl.when(lax.div(j, per) == far)
+            rows = slice(p * NOCC, (p + 1) * NOCC)
+            late = jnp.dot(occ, late_ref[p * CAP : (p + 1) * CAP, :], preferred_element_type=F32)
+            half_ref[rows, :] = (part_ref[rows, :] + late).astype(BF16)
+
+    for far in range(2):
+
+        @pl.when(j == far * per)
         def _():
-            columns = pl.ds(pl.multiple_of(lax.rem(j, per) * tile, 128), tile)
-            right = jnp.concatenate([piece[:, columns] for piece in side], axis=0)
-            total = jnp.dot(half_ref[...], right, preferred_element_type=F32).astype(BF16)
-            out_ref[...] = total.reshape(out_ref.shape)
+            for copy in copies(far):
+                copy.wait()
+
+    right = right_ref[lax.div(j, per), :, pl.ds(pl.multiple_of(lax.rem(j, per) * tile, 128), tile)]
+    total = jnp.dot(half_ref[...], right, preferred_element_type=F32).astype(BF16)
+    out_ref[...] = total.reshape(out_ref.shape)
 
 
 VMEM = pl.BlockSpec(memory_space=pltpu.VMEM)
 SMEM = pl.BlockSpec(memory_space=pltpu.SMEM)
 HBM = pl.BlockSpec(memory_space=pltpu.HBM)
+ANY = pl.BlockSpec(memory_space=pl.ANY)
 
 
 def shape(*dims, dtype=BF16):
@@ -358,9 +411,25 @@
         name="pick_rows",
     )(code, size_row, keep, to_core, to_y, to_both)
 
-    across, beside, mine_y = swap(mine, 8), swap(mine, 4), swap(mine, 2)
-    beside, mine_y, panels = lax.optimization_barrier((beside, mine_y, panels))
-    beside_y = swap(beside, 2)
+    z = me // (Y * CORES)
+    inner = (z == 1) | (z == 2)
+    ends, middle, outward = [(0, 1), (1, 0), (2, 3), (3, 2)], [(1, 2), (2, 1)], [(1, 0), (2, 3)]
+
+    def hop(array, steps):
+        return lax.ppermute(array, "shell", [(4 * a + k, 4 * b + k) for a, b in steps for k in range(4)])
+
+    beside, across, mine_y = hop(mine, ends), hop(mine, middle), swap(mine, 2)
+    beside, across, mine_y = lax.optimization_barrier((beside, across, mine_y))
+
+    corner, across_out, beside_y = hop(beside, middle), hop(across, outward), swap(beside, 2)
+    far = [swap(mine, 1), swap(mine_y, 1), swap(beside, 1)]
+    corner, across_out, beside_y, panels, *far = lax.optimization_barrier(
+        (corner, across_out, beside_y, panels, *far)
+    )
+
+    across = jnp.where(inner, across, across_out)
+    corner_out, across_y = hop(corner, outward), swap(across, 2)
+    far += [swap(beside_y, 1), swap(across, 1)]
     send = pl.pallas_call(
         send_kernel,
         out_shape=shape(n, 2 * BLK_DEV, EDGE * EDGE),
@@ -371,45 +440,56 @@
         name="turn_panels",
     )(panels)
     got = lax.all_to_all(send, "shell", split_axis=0, concat_axis=0, tiled=True)
-
-
-    far = [swap(mine, 1), swap(mine_y, 1), swap(beside, 1)]
-    across, beside_y, got, *far = lax.optimization_barrier((across, beside_y, got, *far))
-    corner, across_y = swap(across, 4), swap(across, 2)
-    far += [swap(beside_y, 1), swap(across, 1)]
-    corner, across_y, got, *far = lax.optimization_barrier((corner, across_y, got, *far))
+    corner_out, across_y, got, *far = lax.optimization_barrier((corner_out, across_y, got, *far))
+
+    corner = jnp.where(inner, corner, corner_out)
     corner_y = swap(corner, 2)
-    rows, placed = pl.pallas_call(
-        functools.partial(place_kernel, here),
-        out_shape=(shape(LIVE_DEV * n * EDGE, room), shape(2, LIVE_DEV * n * EDGE, room)),
-        in_specs=[VMEM] * 3,
-        out_specs=(VMEM, VMEM),
-        compiler_params=params(20),
+    far += [swap(across_y, 1), swap(corner, 1)]
+    near = [mine, mine_y, beside, beside_y, across, across_y, corner]
+    count = len(near)
+    half, late = pl.pallas_call(
+        functools.partial(half_kernel, here),
+        out_shape=(shape(2 * NOCC, room, dtype=F32), shape(2 * CAP, room)),
+        grid=(1,),
+        in_specs=[VMEM] * 3 + [ANY] * (2 * count),
+        out_specs=(
+            pl.BlockSpec((2 * NOCC, room), lambda i: (0, 0)),
+            pl.BlockSpec((2 * CAP, room), lambda i: (0, 0)),
+        ),
+        scratch_shapes=[pltpu.VMEM((room, NOCC), BF16), pltpu.SemaphoreType.DMA((2 * count,))],
+        compiler_params=params(24),
         cost_estimate=cost(4e9, 8e6),
-        name="place_panels",
-    )(code, got, size_row)
-
-    far += [swap(across_y, 1), swap(corner, 1)]
-    corner_y, rows, placed, *far = lax.optimization_barrier((corner_y, rows, placed, *far))
+        name="half_transform",
+    )(code, got, size_row, *near, *far)
+    corner_y, half, late = lax.optimization_barrier((corner_y, half, late))
+    near.append(corner_y)
     far.append(swap(corner_y, 1))
-    pieces = [mine, mine_y, beside, beside_y, across, across_y, corner, corner_y]
-
+
+    count = len(near)
     tile = width // 3
-    count = len(pieces)
     out = pl.pallas_call(
         functools.partial(last_kernel, count),
         out_shape=shape(2, NOCC, nvir),
         grid_spec=pltpu.PrefetchScalarGridSpec(
             num_scalar_prefetch=1,
             grid=(nvir // tile,),
-            in_specs=[VMEM] * (2 + 2 * count),
+            in_specs=[
+                pl.BlockSpec((2 * NOCC, room), lambda j, o: (0, 0)),
+                pl.BlockSpec((2 * CAP, room), lambda j, o: (0, 0)),
+            ]
+            + [ANY] * (2 * count),
             out_specs=pl.BlockSpec((2, NOCC, tile), lambda j, o: (0, 0, (j + 3 * (o[0] % 2)) % 6)),
-            scratch_shapes=[pltpu.VMEM((room, NOCC), BF16), pltpu.VMEM((2 * NOCC, room), BF16)],
+            scratch_shapes=[
+                pltpu.VMEM((CORES, room, width), BF16),
+                pltpu.VMEM((CAP, NOCC), BF16),
+                pltpu.VMEM((2 * NOCC, room), BF16),
+                pltpu.SemaphoreType.DMA((2 * count + 2,)),
+            ],
         ),
         compiler_params=params(24),
-        cost_estimate=cost(4e9, 1e7),
+        cost_estimate=cost(3e9, 1e7),
         name="last_product",
-    )(me.reshape(1), rows, placed, *pieces, *far)
+    )(me.reshape(1), half, late, *near, *far)
     return out, over[0], code, got
 
 

time: 107 us -> 95.7 us (0.89)
  local copies, waits for them, and re-layouts: 15.5 us -> 1.58 us
  blocking collectives: 12.8 us -> 25.8 us
  waiting for transfers between devices: 29.8 us -> 23.6 us
  starting transfers between devices: 14.1 us -> 12 us
  Pallas kernels: 18.7 us -> 17.3 us
    ppermute x0 -> x5, waiting for transfers between devices: none -> 18.1 us  [hop(): lax.ppermute(array, 'shell', [(4 * a + k, 4 * b + k) for a, b in steps fo...]
    ppermute x18 -> x15, waiting for transfers between devices: 21.9 us -> 5.46 us  [swap(): return lax.ppermute(array, 'shell', [(i, i ^ bit) for i in range(n)])]
    unnamed x30 -> x6, local copies, waits for them, and re-layouts: 15.5 us -> 1.58 us
    all_to_all x0 -> x1, blocking collectives: none -> 13 us  [short_way(): got = lax.all_to_all(send, 'shell', split_axis=0, concat_axis=0, tiled=True)]
    all_to_all x1 -> x0, waiting for transfers between devices: 7.91 us -> none  [short_way(): got = lax.all_to_all(send, 'shell', split_axis=0, concat_axis=0, tiled=True)]
    ppermute x0 -> x5, starting transfers between devices: none -> 4.1 us  [hop(): lax.ppermute(array, 'shell', [(4 * a + k, 4 * b + k) for a, b in steps fo...]
    all_to_all x1 -> x0, starting transfers between devices: 3.8 us -> none  [short_way(): got = lax.all_to_all(send, 'shell', split_axis=0, concat_axis=0, tiled=True)]
    pallas_call x1, Pallas kernels: 9.33 us -> 6.31 us  [short_way(): pl.pallas_call(functools.partial(last_kernel, count), out_shape=shape(2,...]
  transfers between devices with their start and end apart: 19 -> 20, of which waited for: 5 -> 7; matrix products, arithmetic and copies ran while one was open for 0% -> 0% of each run, Pallas kernels for 5% -> 7%
where the time goes in v6:
time: 95.7 us; the launch traced here: 95.4 us
  blocking collectives  25.8 us (27%)
  waiting for transfers between devices  23.6 us (25%)
  Pallas kernels  17.3 us (18%)
  between operations  14.2 us (15%)
  starting transfers between devices  12 us (13%)
  local copies, waits for them, and re-layouts  1.58 us (2%)
    ppermute x5, waiting for transfers between devices, hop(): lax.ppermute(array, 'shell', [(4 * a + k, 4 * b + k) for a, b in steps fo...  18.1 us
    all_to_all x1, blocking collectives, short_way(): got = lax.all_to_all(send, 'shell', split_axis=0, concat_axis=0, tiled=True)  13 us
    all_to_all x1, blocking collectives, short_way(): lax.all_to_all(code, 'shell', split_axis=0, concat_axis=0, tiled=True)  12.8 us
    ppermute x15, starting transfers between devices, swap(): return lax.ppermute(array, 'shell', [(i, i ^ bit) for i in range(n)])  7.93 us
    pallas_call x1, Pallas kernels, short_way(): pl.pallas_call(functools.partial(half_kernel, here), out_shape=(shape(2 *...  7.02 us
    pallas_call x1, Pallas kernels, short_way(): pl.pallas_call(functools.partial(last_kernel, count), out_shape=shape(2,...  6.31 us
    ppermute x15, waiting for transfers between devices, swap(): return lax.ppermute(array, 'shell', [(i, i ^ bit) for i in range(n)])  5.46 us
    ppermute x5, starting transfers between devices, hop(): lax.ppermute(array, 'shell', [(4 * a + k, 4 * b + k) for a, b in steps fo...  4.1 us
  transfers between devices with their start and end apart: 20, of which 7 were waited for; matrix products, arithmetic and copies ran while one was open for 0% of the time, Pallas kernels for 7%

profile of v6, /device:TPU:0, one launch (start us, length us, event | category | flops | bytes accessed | tf_op | source)
XLA Modules:
  0.0 95.4 jit_solution(15779074717233748492)
XLA Ops:
  7.2 0.7 copy-done.1
  7.9 1.7 %pack_rows.1 = (s32[16,8,128]{2,1,0:T(8,128)S(1)}, bf16[80,1280]{1,0:T(8,128)(2,1)S(1)}, bf16[80,1280]{1,0:T(8,128)(2,1)S(1)}, bf16[80,1280]{1,0:T(8,128)(2,1)S(1)}, bf16[80,1280]{1,0:T(8,128)(2,1)S(1)}) custom-call(s32[2,8]{1,0:T(2,128)S(1)} %bitcast.61, s32[1,1]{1,0:T(1,128)} %bitcast.60.count_any, bf16[160,2304]{1,0:T(8,128)(2,1)} %vir_ref.1, ...), custom_call_target="tpu_custom_call" | custom-call | flops 300000000 | bytes 3000000 | tf_op jit(solution)/shard_map/pack_rows/pallas_call | solution.py:387
  9.6 0.5 collective-permute-start
  10.1 2.6 %collective-permute-start.1 = (bf16[80,1280]{1,0:T(8,128)(2,1)S(1)}, bf16[80,1280]{1,0:T(8,128)(2,1)S(1)}, u32[]{:S(2)}, u32[]{:S(2)}) collective-permute-start(bf16[80,1280]{1,0:T(8,128)(2,1)S(1)} %get-tuple-element.178), channel_id=1, source_target_pairs={{0,2},{1,3},{2,0},{3,1},{4,6},{5,7},{6,4},{7,5},{8,10},{9,11},{10,... | collective-permute-start | bytes 614408 | tf_op jit(solution)/shard_map/ppermute | solution.py:385
  12.7 0.1 collective-permute-start.2
  12.8 12.8 %all_to_all.10.code_ref = s32[16,8,128]{2,1,0:T(8,128)S(1)} all-to-all(s32[16,8,128]{2,1,0:T(8,128)S(1)} %get-tuple-element.175), channel_id=1, replica_groups=mesh['groups'=2,'shell'=16] {'shell'}, dimensions={0} | all-to-all | bytes 131072 | tf_op jit(solution)/shard_map/all_to_all | solution.py:402
  25.6 2.1 %pick_rows.1 = (bf16[128,1280]{1,0:T(8,128)(2,1)S(1)}, s32[1]{0:T(128)}) custom-call(s32[16,8,128]{2,1,0:T(8,128)S(1)} %all_to_all.10.code_ref, s32[1,256]{1,0:T(1,128)} %bitcast.64, bf16[80,1280]{1,0:T(8,128)(2,1)S(1)} %get-tuple-element.176.refs_0_, bf16[80,1280]{1,0:T(8,128)(2,1)S(1)} %collective-permute-done.refs_1_, ...), custom_call_target="tpu_custom_call" | custom-call | flops 300000000 | bytes 2000000 | tf_op jit(solution)/shard_map/pick_rows/pallas_call | solution.py:404
  27.8 0.2 collective-permute-start.3
  28.0 0.7 collective-permute-start.4
  28.7 1.1 %collective-permute-start.5 = (bf16[128,1280]{1,0:T(8,128)(2,1)S(1)}, bf16[128,1280]{1,0:T(8,128)(2,1)S(1)}, u32[]{:S(2)}, u32[]{:S(2)}) collective-permute-start(bf16[128,1280]{1,0:T(8,128)(2,1)S(1)} %get-tuple-element.181.refs_0_), channel_id=1, source_target_pairs={{0,2},{1,3},{2,0},{3,1},{4,6},{5,7},{6,4},{7,5},{8,10},{9,11},{10,... | collective-permute-start | bytes 983048 | tf_op jit(solution)/shard_map/ppermute | solution.py:385
  29.8 7.2 %collective-permute-done.3.refs_2_ = bf16[128,1280]{1,0:T(8,128)(2,1)S(1)} collective-permute-done((bf16[128,1280]{1,0:T(8,128)(2,1)S(1)}, bf16[128,1280]{1,0:T(8,128)(2,1)S(1)}, u32[]{:S(2)}, u32[]{:S(2)}) %collective-permute-start.3) | collective-permute-done | bytes 327712 | tf_op jit(solution)/shard_map/ppermute | solution.py:419
  37.0 1.1 %collective-permute-done.5.refs_1_ = bf16[128,1280]{1,0:T(8,128)(2,1)S(1)} collective-permute-done((bf16[128,1280]{1,0:T(8,128)(2,1)S(1)}, bf16[128,1280]{1,0:T(8,128)(2,1)S(1)}, u32[]{:S(2)}, u32[]{:S(2)}) %collective-permute-start.5) | collective-permute-done | bytes 327712 | tf_op jit(solution)/shard_map/ppermute | solution.py:385
  38.2 0.7 collective-permute-start.6
  38.9 0.8 collective-permute-start.8
  39.6 1.3 %collective-permute-start.7 = (bf16[128,1280]{1,0:T(8,128)(2,1)S(1)}, bf16[128,1280]{1,0:T(8,128)(2,1)S(1)}, u32[]{:S(2)}, u32[]{:S(2)}) collective-permute-start(bf16[128,1280]{1,0:T(8,128)(2,1)S(1)} %collective-permute-done.4), channel_id=1, source_target_pairs={{4,0},{5,1},{6,2},{7,3},{8,12},{9,13},{10,14},{11,15},{20,16},{21,... | collective-permute-start | bytes 983048 | tf_op jit(solution)/shard_map/ppermute | solution.py:419
  40.9 0.1 collective-permute-start.10
  41.0 0.5 collective-permute-start.11
  41.5 10.9 %collective-permute-done.7 = bf16[128,1280]{1,0:T(8,128)(2,1)S(1)} collective-permute-done((bf16[128,1280]{1,0:T(8,128)(2,1)S(1)}, bf16[128,1280]{1,0:T(8,128)(2,1)S(1)}, u32[]{:S(2)}, u32[]{:S(2)}) %collective-permute-start.7) | collective-permute-done | bytes 327712 | tf_op jit(solution)/shard_map/ppermute | solution.py:419
  52.4 1.3 %collective-permute-start.12 = (bf16[128,1280]{1,0:T(8,128)(2,1)S(1)}, bf16[128,1280]{1,0:T(8,128)(2,1)S(1)}, u32[]{:S(2)}, u32[]{:S(2)}) collective-permute-start(bf16[128,1280]{1,0:T(8,128)(2,1)S(1)} %collective-permute-done.6), channel_id=1, source_target_pairs={{4,0},{5,1},{6,2},{7,3},{8,12},{9,13},{10,14},{11,15},{20,16},{21,... | collective-permute-start | bytes 983048 | tf_op jit(solution)/shard_map/ppermute | solution.py:419
  53.8 1.2 %collective-permute-start.13 = (bf16[128,1280]{1,0:T(8,128)(2,1)S(1)}, bf16[128,1280]{1,0:T(8,128)(2,1)S(1)}, u32[]{:S(2)}, u32[]{:S(2)}) collective-permute-start(bf16[128,1280]{1,0:T(8,128)(2,1)S(1)} %broadcast_select_fusion.3.refs_4_), channel_id=1, source_target_pairs={{0,2},{1,3},{2,0},{3,1},{4,6},{5,7},{6,4},{7,5},{8,10},{9,11},{10,... | collective-permute-start | bytes 983048 | tf_op jit(solution)/shard_map/ppermute | solution.py:385
  54.9 0.5 collective-permute-start.15
  55.4 0.9 copy-done
  56.4 13.0 %all_to_all.11.got_ref = bf16[16,16,256]{2,1,0:T(8,128)(2,1)S(1)} all-to-all(bf16[16,16,256]{2,1,0:T(8,128)(2,1)S(1)} %turn_panels.1), channel_id=1, replica_groups=mesh['groups'=2,'shell'=16] {'shell'}, dimensions={0} | all-to-all | bytes 262144 | tf_op jit(solution)/shard_map/all_to_all | solution.py:442
  69.5 0.1 collective-permute-start.17
  69.6 0.5 collective-permute-start.18
  70.1 1.1 %collective-permute-done.17.refs_12_.refs_13_ = bf16[128,1280]{1,0:T(8,128)(2,1)S(1)} collective-permute-done((bf16[128,1280]{1,0:T(8,128)(2,1)S(1)}, bf16[128,1280]{1,0:T(8,128)(2,1)S(1)}, u32[]{:S(2)}, u32[]{:S(2)}) %collective-permute-start.17) | collective-permute-done | bytes 327712 | tf_op jit(solution)/shard_map/ppermute | solution.py:385
  71.2 0.5 collective-permute-done.18.refs_13_.refs_14_
  71.7 7.0 %half_transform.1 = (f32[512,1024]{1,0:T(8,128)S(1)}, bf16[256,1024]{1,0:T(8,128)(2,1)S(1)}) custom-call(s32[16,8,128]{2,1,0:T(8,128)S(1)} %all_to_all.10.code_ref, bf16[16,16,256]{2,1,0:T(8,128)(2,1)S(1)} %all_to_all.11.got_ref, s32[1,256]{1,0:T(1,128)S(1)} %bitcast.65, bf16[128,1280]{1,0:T(8,128)(2,1)S(1)} %get-tuple-element.181.refs_0_, ...), custom_call_target="tpu_custom_call" | custom-call | flops 4000000000 | bytes 8000000 | tf_op jit(solution)/shard_map/half_transform/pallas_call | solution.py:450
  78.7 1.1 %collective-permute-done.16.refs_7_ = bf16[128,1280]{1,0:T(8,128)(2,1)S(1)} collective-permute-done((bf16[128,1280]{1,0:T(8,128)(2,1)S(1)}, bf16[128,1280]{1,0:T(8,128)(2,1)S(1)}, u32[]{:S(2)}, u32[]{:S(2)}) %collective-permute-start.16) | collective-permute-done | bytes 327712 | tf_op jit(solution)/shard_map/ppermute | solution.py:385
  79.8 1.6 %collective-permute-done.19.refs_15_ = bf16[128,1280]{1,0:T(8,128)(2,1)S(1)} collective-permute-done((bf16[128,1280]{1,0:T(8,128)(2,1)S(1)}, bf16[128,1280]{1,0:T(8,128)(2,1)S(1)}, u32[]{:S(2)}, u32[]{:S(2)}) %collective-permute-start.19) | collective-permute-done | bytes 327712 | tf_op jit(solution)/shard_map/ppermute | solution.py:385
  81.4 6.3 %last_product.1 = bf16[2,256,2304]{2,1,0:T(8,128)(2,1)} custom-call(s32[1]{0:T(128)} %bitcast.17.me_ref, f32[512,1024]{1,0:T(8,128)S(1)} %get-tuple-element.202.part_ref, bf16[256,1024]{1,0:T(8,128)(2,1)S(1)} %get-tuple-element.203.late_ref, bf16[128,1280]{1,0:T(8,128)(2,1)S(1)} %get-tuple-element.181.refs_0_, ...), custom_call_target="tpu_custom_call" | custom-call | flops 3000000000 | bytes 10000000 | tf_op jit(solution)/shard_map/last_product/pallas_call | solution.py:470
  87.7 0.8 while.17
  (24 shorter events, 0.2 us)
Async XLA Ops:
  6.5 65.1 %copy-start.3 = (s32[256]{0:T(256)S(1)}, s32[256]{0:T(256)}, u32[]{:S(2)}) copy-start(s32[256]{0:T(256)} %param.11) | copy-start | bytes 3076
  7.2 0.7 copy-start.1
  9.6 16.0 %collective-permute-start = (bf16[80,1280]{1,0:T(8,128)(2,1)S(1)}, bf16[80,1280]{1,0:T(8,128)(2,1)S(1)}, u32[]{:S(2)}, u32[]{:S(2)}) collective-permute-start(bf16[80,1280]{1,0:T(8,128)(2,1)S(1)} %get-tuple-element.177), channel_id=1, source_target_pairs={{0,1},{1,0},{2,3},{3,2},{4,5},{5,4},{6,7},{7,6},{8,9},{9,8},{10,11... | collective-permute-start | bytes 614408 | tf_op jit(solution)/shard_map/ppermute | solution.py:385
  10.1 15.5 %collective-permute-start.1 = (bf16[80,1280]{1,0:T(8,128)(2,1)S(1)}, bf16[80,1280]{1,0:T(8,128)(2,1)S(1)}, u32[]{:S(2)}, u32[]{:S(2)}) collective-permute-start(bf16[80,1280]{1,0:T(8,128)(2,1)S(1)} %get-tuple-element.178), channel_id=1, source_target_pairs={{0,2},{1,3},{2,0},{3,1},{4,6},{5,7},{6,4},{7,5},{8,10},{9,11},{10,... | collective-permute-start | bytes 614408 | tf_op jit(solution)/shard_map/ppermute | solution.py:385
  12.7 12.9 %collective-permute-start.2 = (bf16[80,1280]{1,0:T(8,128)(2,1)S(1)}, bf16[80,1280]{1,0:T(8,128)(2,1)S(1)}, u32[]{:S(2)}, u32[]{:S(2)}) collective-permute-start(bf16[80,1280]{1,0:T(8,128)(2,1)S(1)} %get-tuple-element.179), channel_id=1, source_target_pairs={{0,3},{1,2},{2,1},{3,0},{4,7},{5,6},{6,5},{7,4},{8,11},{9,10},{10,... | collective-permute-start | bytes 614408 | tf_op jit(solution)/shard_map/ppermute | solution.py:385
  27.8 9.2 %collective-permute-start.3 = (bf16[128,1280]{1,0:T(8,128)(2,1)S(1)}, bf16[128,1280]{1,0:T(8,128)(2,1)S(1)}, u32[]{:S(2)}, u32[]{:S(2)}) collective-permute-start(bf16[128,1280]{1,0:T(8,128)(2,1)S(1)} %get-tuple-element.181.refs_0_), channel_id=1, source_target_pairs={{0,4},{1,5},{2,6},{3,7},{4,0},{5,1},{6,2},{7,3},{8,12},{9,13},{10,... | collective-permute-start | bytes 983048 | tf_op jit(solution)/shard_map/ppermute | solution.py:419
  28.0 9.0 %collective-permute-start.4 = (bf16[128,1280]{1,0:T(8,128)(2,1)S(1)}, bf16[128,1280]{1,0:T(8,128)(2,1)S(1)}, u32[]{:S(2)}, u32[]{:S(2)}) collective-permute-start(bf16[128,1280]{1,0:T(8,128)(2,1)S(1)} %get-tuple-element.181.refs_0_), channel_id=1, source_target_pairs={{4,8},{5,9},{6,10},{7,11},{8,4},{9,5},{10,6},{11,7},{20,24},{21,25... | collective-permute-start | bytes 983048 | tf_op jit(solution)/shard_map/ppermute | solution.py:419
  28.7 9.5 %collective-permute-start.5 = (bf16[128,1280]{1,0:T(8,128)(2,1)S(1)}, bf16[128,1280]{1,0:T(8,128)(2,1)S(1)}, u32[]{:S(2)}, u32[]{:S(2)}) collective-permute-start(bf16[128,1280]{1,0:T(8,128)(2,1)S(1)} %get-tuple-element.181.refs_0_), channel_id=1, source_target_pairs={{0,2},{1,3},{2,0},{3,1},{4,6},{5,7},{6,4},{7,5},{8,10},{9,11},{10,... | collective-permute-start | bytes 983048 | tf_op jit(solution)/shard_map/ppermute | solution.py:385
  29.8 11.2 %collective-permute-start.9 = (bf16[128,1280]{1,0:T(8,128)(2,1)S(1)}, bf16[128,1280]{1,0:T(8,128)(2,1)S(1)}, u32[]{:S(2)}, u32[]{:S(2)}) collective-permute-start(bf16[128,1280]{1,0:T(8,128)(2,1)S(1)} %get-tuple-element.181.refs_0_), channel_id=1, source_target_pairs={{0,1},{1,0},{2,3},{3,2},{4,5},{5,4},{6,7},{7,6},{8,9},{9,8},{10,11... | collective-permute-start | bytes 983048 | tf_op jit(solution)/shard_map/ppermute | solution.py:385
  38.2 3.3 %collective-permute-start.6 = (bf16[128,1280]{1,0:T(8,128)(2,1)S(1)}, bf16[128,1280]{1,0:T(8,128)(2,1)S(1)}, u32[]{:S(2)}, u32[]{:S(2)}) collective-permute-start(bf16[128,1280]{1,0:T(8,128)(2,1)S(1)} %collective-permute-done.3.refs_2_), channel_id=1, source_target_pairs={{4,8},{5,9},{6,10},{7,11},{8,4},{9,5},{10,6},{11,7},{20,24},{21,25... | collective-permute-start | bytes 983048 | tf_op jit(solution)/shard_map/ppermute | solution.py:419
  38.9 13.6 %collective-permute-start.8 = (bf16[128,1280]{1,0:T(8,128)(2,1)S(1)}, bf16[128,1280]{1,0:T(8,128)(2,1)S(1)}, u32[]{:S(2)}, u32[]{:S(2)}) collective-permute-start(bf16[128,1280]{1,0:T(8,128)(2,1)S(1)} %collective-permute-done.3.refs_2_), channel_id=1, source_target_pairs={{0,2},{1,3},{2,0},{3,1},{4,6},{5,7},{6,4},{7,5},{8,10},{9,11},{10,... | collective-permute-start | bytes 983048 | tf_op jit(solution)/shard_map/ppermute | solution.py:385
  39.6 12.8 %collective-permute-start.7 = (bf16[128,1280]{1,0:T(8,128)(2,1)S(1)}, bf16[128,1280]{1,0:T(8,128)(2,1)S(1)}, u32[]{:S(2)}, u32[]{:S(2)}) collective-permute-start(bf16[128,1280]{1,0:T(8,128)(2,1)S(1)} %collective-permute-done.4), channel_id=1, source_target_pairs={{4,0},{5,1},{6,2},{7,3},{8,12},{9,13},{10,14},{11,15},{20,16},{21,... | collective-permute-start | bytes 983048 | tf_op jit(solution)/shard_map/ppermute | solution.py:419
  40.9 11.5 %collective-permute-start.10 = (bf16[128,1280]{1,0:T(8,128)(2,1)S(1)}, bf16[128,1280]{1,0:T(8,128)(2,1)S(1)}, u32[]{:S(2)}, u32[]{:S(2)}) collective-permute-start(bf16[128,1280]{1,0:T(8,128)(2,1)S(1)} %collective-permute-done.5.refs_1_), channel_id=1, source_target_pairs={{0,1},{1,0},{2,3},{3,2},{4,5},{5,4},{6,7},{7,6},{8,9},{9,8},{10,11... | collective-permute-start | bytes 983048 | tf_op jit(solution)/shard_map/ppermute | solution.py:385
  41.0 11.4 %collective-permute-start.11 = (bf16[128,1280]{1,0:T(8,128)(2,1)S(1)}, bf16[128,1280]{1,0:T(8,128)(2,1)S(1)}, u32[]{:S(2)}, u32[]{:S(2)}) collective-permute-start(bf16[128,1280]{1,0:T(8,128)(2,1)S(1)} %collective-permute-done.3.refs_2_), channel_id=1, source_target_pairs={{0,1},{1,0},{2,3},{3,2},{4,5},{5,4},{6,7},{7,6},{8,9},{9,8},{10,11... | collective-permute-start | bytes 983048 | tf_op jit(solution)/shard_map/ppermute | solution.py:385
  52.4 17.0 %collective-permute-start.12 = (bf16[128,1280]{1,0:T(8,128)(2,1)S(1)}, bf16[128,1280]{1,0:T(8,128)(2,1)S(1)}, u32[]{:S(2)}, u32[]{:S(2)}) collective-permute-start(bf16[128,1280]{1,0:T(8,128)(2,1)S(1)} %collective-permute-done.6), channel_id=1, source_target_pairs={{4,0},{5,1},{6,2},{7,3},{8,12},{9,13},{10,14},{11,15},{20,16},{21,... | collective-permute-start | bytes 983048 | tf_op jit(solution)/shard_map/ppermute | solution.py:419
  53.8 15.7 %collective-permute-start.13 = (bf16[128,1280]{1,0:T(8,128)(2,1)S(1)}, bf16[128,1280]{1,0:T(8,128)(2,1)S(1)}, u32[]{:S(2)}, u32[]{:S(2)}) collective-permute-start(bf16[128,1280]{1,0:T(8,128)(2,1)S(1)} %broadcast_select_fusion.3.refs_4_), channel_id=1, source_target_pairs={{0,2},{1,3},{2,0},{3,1},{4,6},{5,7},{6,4},{7,5},{8,10},{9,11},{10,... | collective-permute-start | bytes 983048 | tf_op jit(solution)/shard_map/ppermute | solution.py:385
  54.9 14.5 %collective-permute-start.14 = (bf16[128,1280]{1,0:T(8,128)(2,1)S(1)}, bf16[128,1280]{1,0:T(8,128)(2,1)S(1)}, u32[]{:S(2)}, u32[]{:S(2)}) collective-permute-start(bf16[128,1280]{1,0:T(8,128)(2,1)S(1)} %collective-permute-done.8.refs_3_), channel_id=1, source_target_pairs={{0,1},{1,0},{2,3},{3,2},{4,5},{5,4},{6,7},{7,6},{8,9},{9,8},{10,11... | collective-permute-start | bytes 983048 | tf_op jit(solution)/shard_map/ppermute | solution.py:385
  54.9 14.5 %collective-permute-start.15 = (bf16[128,1280]{1,0:T(8,128)(2,1)S(1)}, bf16[128,1280]{1,0:T(8,128)(2,1)S(1)}, u32[]{:S(2)}, u32[]{:S(2)}) collective-permute-start(bf16[128,1280]{1,0:T(8,128)(2,1)S(1)} %broadcast_select_fusion.3.refs_4_), channel_id=1, source_target_pairs={{0,1},{1,0},{2,3},{3,2},{4,5},{5,4},{6,7},{7,6},{8,9},{9,8},{10,11... | collective-permute-start | bytes 983048 | tf_op jit(solution)/shard_map/ppermute | solution.py:385
  55.4 0.9 copy-start
  69.5 1.7 %collective-permute-start.17 = (bf16[128,1280]{1,0:T(8,128)(2,1)S(1)}, bf16[128,1280]{1,0:T(8,128)(2,1)S(1)}, u32[]{:S(2)}, u32[]{:S(2)}) collective-permute-start(bf16[128,1280]{1,0:T(8,128)(2,1)S(1)} %collective-permute-done.13.refs_5_), channel_id=1, source_target_pairs={{0,1},{1,0},{2,3},{3,2},{4,5},{5,4},{6,7},{7,6},{8,9},{9,8},{10,11... | collective-permute-start | bytes 983048 | tf_op jit(solution)/shard_map/ppermute | solution.py:385
  69.6 2.1 %collective-permute-start.18 = (bf16[128,1280]{1,0:T(8,128)(2,1)S(1)}, bf16[128,1280]{1,0:T(8,128)(2,1)S(1)}, u32[]{:S(2)}, u32[]{:S(2)}) collective-permute-start(bf16[128,1280]{1,0:T(8,128)(2,1)S(1)} %broadcast_select_fusion.2.refs_6_), channel_id=1, source_target_pairs={{0,1},{1,0},{2,3},{3,2},{4,5},{5,4},{6,7},{7,6},{8,9},{9,8},{10,11... | collective-permute-start | bytes 983048 | tf_op jit(solution)/shard_map/ppermute | solution.py:385
  70.1 9.7 %collective-permute-start.16 = (bf16[128,1280]{1,0:T(8,128)(2,1)S(1)}, bf16[128,1280]{1,0:T(8,128)(2,1)S(1)}, u32[]{:S(2)}, u32[]{:S(2)}) collective-permute-start(bf16[128,1280]{1,0:T(8,128)(2,1)S(1)} %broadcast_select_fusion.2.refs_6_), channel_id=1, source_target_pairs={{0,2},{1,3},{2,0},{3,1},{4,6},{5,7},{6,4},{7,5},{8,10},{9,11},{10,... | collective-permute-start | bytes 983048 | tf_op jit(solution)/shard_map/ppermute | solution.py:385
  79.8 1.6 %collective-permute-start.19 = (bf16[128,1280]{1,0:T(8,128)(2,1)S(1)}, bf16[128,1280]{1,0:T(8,128)(2,1)S(1)}, u32[]{:S(2)}, u32[]{:S(2)}) collective-permute-start(bf16[128,1280]{1,0:T(8,128)(2,1)S(1)} %collective-permute-done.16.refs_7_), channel_id=1, source_target_pairs={{0,1},{1,0},{2,3},{3,2},{4,5},{5,4},{6,7},{7,6},{8,9},{9,8},{10,11... | collective-permute-start | bytes 983048 | tf_op jit(solution)/shard_map/ppermute | solution.py:385

commit v7 on v6

--- a/solution.py
+++ b/solution.py
@@ -95,11 +95,9 @@
     return jnp.concatenate([zero_one(ids == lanes + 128.0 * k) for k in range(shells // 128)], axis=1)
 
 
-def slot_hots(code, shells):
-    code = code.reshape(-1, 128)
-    kept = code >= 0
-    columns = jnp.where(kept, code % shells, -1).astype(F32)
-    return one_hots(columns, shells), one_hots(jnp.where(kept, code // shells, -1).astype(F32), shells)
+def slot_hots(got, shells):
+    ids = got[:, 2 * BLK_DEV :, :].reshape(-1, 256)
+    return one_hots(ids[:, :128], shells), one_hots(ids[:, 128:], shells)
 
 
 class Shells:
@@ -127,14 +125,7 @@
             self.edges.append(jnp.sum(self.used * jnp.floor((reach + extra) * 0.5), axis=0, keepdims=True))
 
 
-def pack_kernel(shells, pairs_any, count_any, vir_ref, occ_ref, code_ref, *refs):
-    outs, (pairs_ref, count_ref, sems) = refs[:4], refs[4:]
-    copies = [
-        pltpu.make_async_copy(pairs_any, pairs_ref, sems.at[0]),
-        pltpu.make_async_copy(count_any, count_ref, sems.at[1]),
-    ]
-    for copy in copies:
-        copy.start()
+def pack_kernel(vir_ref, occ_ref, *outs):
     me = lax.axis_index("shell")
     core, y = lax.rem(me, 2), lax.rem(lax.div(me, 2), 2)
     here, nvir = vir_ref.shape
@@ -149,28 +140,32 @@
             out[:, :width] = jnp.dot(pick, part, preferred_element_type=F32).astype(BF16)
             part = occ_ref[:, pl.ds(pl.multiple_of(half * thin, 128), thin)]
             out[:, width:] = jnp.dot(pick, part, preferred_element_type=F32).astype(BF16)
-    for copy in copies:
-        copy.wait()
-    code = pairs_ref[1:2, :] + shells * pairs_ref[0:1, :]
-    code = jnp.where(iota((1, BLK_DEV), 1) < count_ref[...], code, -1).astype(F32)
+
+
+def send_kernel(pairs_ref, count_ref, panels_ref, send_ref):
+    n = send_ref.shape[0]
+    turned = jnp.swapaxes(panels_ref[...].astype(F32), 0, 1)
+    send_ref[:, : 2 * BLK_DEV, :] = turned.reshape(n, 2 * BLK_DEV, EDGE * EDGE).astype(BF16)
+    kept = iota((1, BLK_DEV), 1) < count_ref[...]
     square = (BLK_DEV, BLK_DEV)
-    code = column_of(code, iota(square, 0) == iota(square, 1)).astype(jnp.int32)
-    code_ref[...] = jnp.broadcast_to(jnp.broadcast_to(code, (BLK_DEV, 128))[None], code_ref.shape)
-
-
-def send_kernel(panels_ref, send_ref):
-    turned = jnp.swapaxes(panels_ref[...].astype(F32), 0, 1)
-    send_ref[...] = turned.reshape(send_ref.shape).astype(BF16)
-
-
-def pick_kernel(here, code_ref, size_ref, *refs):
+    same = iota(square, 0) == iota(square, 1)
+    wide = (BLK_DEV, 128)
+    columns, rows = (
+        jnp.broadcast_to(column_of(jnp.where(kept, pairs_ref[k : k + 1, :], -1).astype(F32), same), wide)
+        for k in (1, 0)
+    )
+    ids = jnp.concatenate([columns, rows], axis=1)
+    send_ref[:, 2 * BLK_DEV :, :] = jnp.broadcast_to(ids[None], (n, BLK_DEV, 256)).astype(BF16)
+
+
+def pick_kernel(here, got_ref, size_ref, *refs):
     sources, (out_ref, over_ref) = refs[:4], refs[4:]
     me = lax.axis_index("shell")
     core, y, z = lax.rem(me, 2), lax.rem(lax.div(me, 2), 2), lax.div(me, 4)
     window = CORES * Y * here
     shell_count = size_ref.shape[1]
     shells = Shells(size_ref[...].astype(F32))
-    lists = [Used(shells, hot, window) for hot in slot_hots(code_ref[...], shell_count)]
+    lists = [Used(shells, hot, window) for hot in slot_hots(got_ref[...].astype(F32), shell_count)]
     most = jnp.zeros((1, 1), F32)
     lane = iota((1, 128), 1)
     for chosen in lists:
@@ -204,14 +199,7 @@
         out_ref[:, column] = total.astype(BF16)
 
 
-def slot_of(window, chip):
-    z = lax.div(chip, Y)
-    slot = window ^ chip
-    inner = (z == 1) | (z == 2)
-    return jnp.where(inner & (slot >= 2 * Y), slot ^ Y, slot)
-
-
-def half_kernel(here, code_ref, got_ref, size_ref, *refs):
+def half_kernel(here, got_ref, size_ref, *refs):
     count = (len(refs) - 4) // 2
     pieces, (half_ref, late_ref, occ_ref, sems) = refs[: 2 * count], refs[2 * count :]
     me = lax.axis_index("shell")
@@ -232,7 +220,8 @@
     got = got_ref[...].astype(F32)
     size_row = size_ref[...].astype(F32)
     shells = Shells(size_row)
-    hots = slot_hots(code_ref[...], shell_count)
+    got = got_ref[...].astype(F32)
+    hots = slot_hots(got, shell_count)
     lists = [Used(shells, hot, window) for hot in hots]
     slots = hots[0].shape[0]
     kept = LIVE_DEV * (slots // BLK_DEV)
@@ -262,7 +251,7 @@
         place = jnp.where(odd, spread(hot, chosen.ahead[1]), spread(hot, chosen.ahead[0]))
         place += jnp.floor(step * 0.5)
         offsets = [
-            [slot_of(w * Y + k, chip).astype(F32) * CAP - lane_value(e, w) for w in range(Z)]
+            [((w * Y + k) ^ chip).astype(F32) * CAP - lane_value(e, w) for w in range(Z)]
             for k, e in enumerate(chosen.edges)
         ]
         offset = jnp.where(odd, offsets[1][0], offsets[0][0])
@@ -356,7 +345,6 @@
 
 VMEM = pl.BlockSpec(memory_space=pltpu.VMEM)
 SMEM = pl.BlockSpec(memory_space=pltpu.SMEM)
-HBM = pl.BlockSpec(memory_space=pltpu.HBM)
 ANY = pl.BlockSpec(memory_space=pl.ANY)
 
 
@@ -384,22 +372,26 @@
     def swap(array, bit):
         return lax.ppermute(array, "shell", [(i, i ^ bit) for i in range(n)])
 
-    code, keep, to_core, to_y, to_both = pl.pallas_call(
-        functools.partial(pack_kernel, size_row.shape[1]),
-        out_shape=[shape(n, BLK_DEV, 128, dtype=jnp.int32)] + [shape(here // 2, packed)] * 4,
-        in_specs=[HBM] * 2 + [VMEM] * 2,
-        out_specs=[VMEM] * 5,
-        scratch_shapes=[
-            pltpu.VMEM((2, BLK_DEV), jnp.int32),
-            pltpu.VMEM((1, 1), jnp.int32),
-            pltpu.SemaphoreType.DMA((2,)),
-        ],
+    keep, to_core, to_y, to_both = pl.pallas_call(
+        pack_kernel,
+        out_shape=[shape(here // 2, packed)] * 4,
+        in_specs=[VMEM] * 2,
+        out_specs=[VMEM] * 4,
         compiler_params=params(12),
         cost_estimate=cost(3e8, 3e6),
         name="pack_rows",
-    )(block_pairs.T, block_count.reshape(1, 1), vir_coef, occ_coef)
+    )(vir_coef, occ_coef)
     to_y, to_both, to_core = swap(to_y, 2), swap(to_both, 3), swap(to_core, 1)
-    code = lax.all_to_all(code, "shell", split_axis=0, concat_axis=0, tiled=True)
+    send = pl.pallas_call(
+        send_kernel,
+        out_shape=shape(n, 3 * BLK_DEV, EDGE * EDGE),
+        in_specs=[VMEM] * 3,
+        out_specs=VMEM,
+        compiler_params=params(12),
+        cost_estimate=cost(1e6, 5e5),
+        name="pack_panels",
+    )(block_pairs.T, block_count.reshape(1, 1), panels)
+    got = lax.all_to_all(send, "shell", split_axis=0, concat_axis=0, tiled=True)
 
     mine, over = pl.pallas_call(
         functools.partial(pick_kernel, here),
@@ -409,40 +401,19 @@
         compiler_params=params(12),
         cost_estimate=cost(3e8, 2e6),
         name="pick_rows",
-    )(code, size_row, keep, to_core, to_y, to_both)
-
-    z = me // (Y * CORES)
-    inner = (z == 1) | (z == 2)
-    ends, middle, outward = [(0, 1), (1, 0), (2, 3), (3, 2)], [(1, 2), (2, 1)], [(1, 0), (2, 3)]
-
-    def hop(array, steps):
-        return lax.ppermute(array, "shell", [(4 * a + k, 4 * b + k) for a, b in steps for k in range(4)])
-
-    beside, across, mine_y = hop(mine, ends), hop(mine, middle), swap(mine, 2)
-    beside, across, mine_y = lax.optimization_barrier((beside, across, mine_y))
-
-    corner, across_out, beside_y = hop(beside, middle), hop(across, outward), swap(beside, 2)
+    )(got, size_row, keep, to_core, to_y, to_both)
+
+    beside, across, mine_y = swap(mine, 4), swap(mine, 8), swap(mine, 2)
+    beside, mine_y = lax.optimization_barrier((beside, mine_y))
+
+    beside_y = swap(beside, 2)
     far = [swap(mine, 1), swap(mine_y, 1), swap(beside, 1)]
-    corner, across_out, beside_y, panels, *far = lax.optimization_barrier(
-        (corner, across_out, beside_y, panels, *far)
-    )
-
-    across = jnp.where(inner, across, across_out)
-    corner_out, across_y = hop(corner, outward), swap(across, 2)
+    across, beside_y, *far = lax.optimization_barrier((across, beside_y, *far))
+
+    corner, across_y = swap(across, 4), swap(across, 2)
     far += [swap(beside_y, 1), swap(across, 1)]
-    send = pl.pallas_call(
-        send_kernel,
-        out_shape=shape(n, 2 * BLK_DEV, EDGE * EDGE),
-        in_specs=[VMEM],
-        out_specs=VMEM,
-        compiler_params=params(12),
-        cost_estimate=cost(1e6, 3e5),
-        name="turn_panels",
-    )(panels)
-    got = lax.all_to_all(send, "shell", split_axis=0, concat_axis=0, tiled=True)
-    corner_out, across_y, got, *far = lax.optimization_barrier((corner_out, across_y, got, *far))
-
-    corner = jnp.where(inner, corner, corner_out)
+    corner, across_y, *far = lax.optimization_barrier((corner, across_y, *far))
+
     corner_y = swap(corner, 2)
     far += [swap(across_y, 1), swap(corner, 1)]
     near = [mine, mine_y, beside, beside_y, across, across_y, corner]
@@ -451,7 +422,7 @@
         functools.partial(half_kernel, here),
         out_shape=(shape(2 * NOCC, room, dtype=F32), shape(2 * CAP, room)),
         grid=(1,),
-        in_specs=[VMEM] * 3 + [ANY] * (2 * count),
+        in_specs=[VMEM] * 2 + [ANY] * (2 * count),
         out_specs=(
             pl.BlockSpec((2 * NOCC, room), lambda i: (0, 0)),
             pl.BlockSpec((2 * CAP, room), lambda i: (0, 0)),
@@ -460,7 +431,7 @@
         compiler_params=params(24),
         cost_estimate=cost(4e9, 8e6),
         name="half_transform",
-    )(code, got, size_row, *near, *far)
+    )(got, size_row, *near, *far)
     corner_y, half, late = lax.optimization_barrier((corner_y, half, late))
     near.append(corner_y)
     far.append(swap(corner_y, 1))
@@ -490,26 +461,26 @@
         cost_estimate=cost(3e9, 1e7),
         name="last_product",
     )(me.reshape(1), half, late, *near, *far)
-    return out, over[0], code, got
+    return out, over[0], got
 
 
 def per_device(*args):
     n = lax.axis_size("shell")
     here, nvir = args[5].shape
-    shells = args[3].shape[0]
     sparse = LIVE_DEV * n * EDGE < n * here
     if not (sparse and n == Z * Y * CORES and here <= 256 and here % 16 == 0 and nvir % 768 == 0):
         return from_start(*args)
-    out, over, code, got = short_way(*args)
+    out, over, got = short_way(*args)
 
     def again(carry):
         over, _ = carry
-        over, code_now, turned, *held = lax.optimization_barrier((over, code, got, *args[3:]))
-        turned = turned.reshape(n, 2, BLK_DEV, EDGE * EDGE).swapaxes(1, 2).reshape(n * BLK_DEV, 2, EDGE * EDGE)
-        code_now = jnp.max(code_now, axis=2).reshape(n * BLK_DEV)
-        ids = jnp.maximum(code_now, 0)
-        pairs = jnp.stack([ids // shells, ids % shells], axis=1)
-        return over - 1, long_way(turned, pairs, code_now >= 0, *held)
+        over, got_now, *held = lax.optimization_barrier((over, got, *args[3:]))
+        turned = got_now[:, : 2 * BLK_DEV].reshape(n, 2, BLK_DEV, EDGE * EDGE).swapaxes(1, 2)
+        turned = turned.reshape(n * BLK_DEV, 2, EDGE * EDGE)
+        ids = got_now[:, 2 * BLK_DEV :].reshape(n * BLK_DEV, 256).astype(jnp.int32)
+        columns, rows = jnp.max(ids[:, :128], axis=1), jnp.max(ids[:, 128:], axis=1)
+        pairs = jnp.maximum(jnp.stack([rows, columns], axis=1), 0)
+        return over - 1, long_way(turned, pairs, columns >= 0, *held)
 
     return lax.while_loop(lambda carry: carry[0] > 0, again, (over, out))[1]
 

time: 95.7 us -> 102 us (1.066)
  blocking collectives: 25.8 us -> 0 us
  waiting for transfers between devices: 23.6 us -> 38 us
  local copies, waits for them, and re-layouts: 1.58 us -> 10.3 us
  starting transfers between devices: 12 us -> 19.5 us
  Pallas kernels: 17.3 us -> 18.8 us
    ppermute x15 -> x18, waiting for transfers between devices: 5.46 us -> 38 us  [swap(): return lax.ppermute(array, 'shell', [(i, i ^ bit) for i in range(n)])]
    all_to_all x2 -> x0, blocking collectives: 25.8 us -> none  [the longest x1 13 us: short_way(): got = lax.all_to_all(send, 'shell', split_axis=0, concat_axis=0, tiled=True)]
    ppermute x5 -> x0, waiting for transfers between devices: 18.1 us -> none  [hop(): lax.ppermute(array, 'shell', [(4 * a + k, 4 * b + k) for a, b in steps fo...]
    unnamed x6 -> x30, local copies, waits for them, and re-layouts: 1.58 us -> 10.3 us
    all_to_all x0 -> x1, starting transfers between devices: none -> 7.39 us  [short_way(): got = lax.all_to_all(send, 'shell', split_axis=0, concat_axis=0, tiled=True)]
    ppermute x15 -> x18, starting transfers between devices: 7.93 us -> 12.1 us  [swap(): return lax.ppermute(array, 'shell', [(i, i ^ bit) for i in range(n)])]
    ppermute x5 -> x0, starting transfers between devices: 4.1 us -> none  [hop(): lax.ppermute(array, 'shell', [(4 * a + k, 4 * b + k) for a, b in steps fo...]
  transfers between devices with their start and end apart: 20 -> 19, of which waited for: 7 -> 10; matrix products, arithmetic and copies ran while one was open for 0% -> 0% of each run, Pallas kernels for 7% -> 9%
where the time goes in v7:
time: 102 us
  waiting for transfers between devices  38 us (37%)
  starting transfers between devices  19.5 us (19%)
  Pallas kernels  18.8 us (18%)
  between operations  14.2 us (14%)
  local copies, waits for them, and re-layouts  10.3 us (10%)
    ppermute x18, waiting for transfers between devices, swap(): return lax.ppermute(array, 'shell', [(i, i ^ bit) for i in range(n)])  38 us
    ppermute x18, starting transfers between devices, swap(): return lax.ppermute(array, 'shell', [(i, i ^ bit) for i in range(n)])  12.1 us
    unnamed x30, local copies, waits for them, and re-layouts  10.3 us
    pallas_call x1, Pallas kernels, short_way(): pl.pallas_call(functools.partial(half_kernel, here), out_shape=(shape(2 *...  7.63 us
    all_to_all x1, starting transfers between devices, short_way(): got = lax.all_to_all(send, 'shell', split_axis=0, concat_axis=0, tiled=True)  7.39 us
    pallas_call x1, Pallas kernels, short_way(): pl.pallas_call(functools.partial(last_kernel, count), out_shape=shape(2,...  6.73 us
    pallas_call x1, Pallas kernels, short_way(): pl.pallas_call(functools.partial(pick_kernel, here), out_shape=(shape(CAP...  2.1 us
  transfers between devices with their start and end apart: 19, of which 10 were waited for; matrix products, arithmetic and copies ran while one was open for 0% of the time, Pallas kernels for 9%

profile of v7, /device:TPU:0, one launch (start us, length us, event | category | flops | bytes accessed | tf_op | source)
XLA Modules:
  0.0 101.5 jit_solution(11076987298573359918)
XLA Ops:
  7.2 0.9 copy-done
  8.1 0.7 copy-done.1
  8.8 0.8 pack_panels.1
  9.6 7.4 %all-to-all-start = ((bf16[16,24,256]{2,1,0:T(8,128)(2,1)}), bf16[16,24,256]{2,1,0:T(8,128)(2,1)S(1)}, u32[]{:S(2)}, u32[]{:S(2)}) async-start(bf16[16,24,256]{2,1,0:T(8,128)(2,1)} %pack_panels.1), calls=%async_computation | async-start | bytes 393216 | tf_op jit(solution)/shard_map/all_to_all | solution.py:394
  17.0 1.5 %pack_rows.1 = (bf16[80,1280]{1,0:T(8,128)(2,1)S(1)}, bf16[80,1280]{1,0:T(8,128)(2,1)S(1)}, bf16[80,1280]{1,0:T(8,128)(2,1)S(1)}, bf16[80,1280]{1,0:T(8,128)(2,1)S(1)}) custom-call(bf16[160,2304]{1,0:T(8,128)(2,1)} %vir_ref.1, bf16[160,256]{1,0:T(8,128)(2,1)} %occ_ref.1), custom_call_target="tpu_custom_call" | custom-call | flops 300000000 | bytes 3000000 | tf_op jit(solution)/shard_map/pack_rows/pallas_call | solution.py:375
  19.0 1.7 %collective-permute-start.1 = (bf16[80,1280]{1,0:T(8,128)(2,1)S(1)}, bf16[80,1280]{1,0:T(8,128)(2,1)S(1)}, u32[]{:S(2)}, u32[]{:S(2)}) collective-permute-start(bf16[80,1280]{1,0:T(8,128)(2,1)S(1)} %get-tuple-element.128), channel_id=1, source_target_pairs={{0,2},{1,3},{2,0},{3,1},{4,6},{5,7},{6,4},{7,5},{8,10},{9,11},{10,... | collective-permute-start | bytes 614408 | tf_op jit(solution)/shard_map/ppermute | solution.py:373
  20.7 7.0 %collective-permute-done.1.refs_2_ = bf16[80,1280]{1,0:T(8,128)(2,1)S(1)} collective-permute-done((bf16[80,1280]{1,0:T(8,128)(2,1)S(1)}, bf16[80,1280]{1,0:T(8,128)(2,1)S(1)}, u32[]{:S(2)}, u32[]{:S(2)}) %collective-permute-start.1) | collective-permute-done | bytes 204832 | tf_op jit(solution)/shard_map/ppermute | solution.py:373
  27.7 3.7 %collective-permute-done.2.refs_3_ = bf16[80,1280]{1,0:T(8,128)(2,1)S(1)} collective-permute-done((bf16[80,1280]{1,0:T(8,128)(2,1)S(1)}, bf16[80,1280]{1,0:T(8,128)(2,1)S(1)}, u32[]{:S(2)}, u32[]{:S(2)}) %collective-permute-start.2) | collective-permute-done | bytes 204832 | tf_op jit(solution)/shard_map/ppermute | solution.py:373
  31.5 2.1 %pick_rows.1 = (bf16[128,1280]{1,0:T(8,128)(2,1)S(1)}, s32[1]{0:T(128)}) custom-call(bf16[16,24,256]{2,1,0:T(8,128)(2,1)S(1)} %all-to-all-done.got_ref, s32[1,256]{1,0:T(1,128)} %bitcast.75, bf16[80,1280]{1,0:T(8,128)(2,1)S(1)} %get-tuple-element.126.refs_0_, bf16[80,1280]{1,0:T(8,128)(2,1)S(1)} %collective-permute-done.refs_1_, ...), custom_call_target="tpu_custom_call" | custom-call | flops 300000000 | bytes 2000000 | tf_op jit(solution)/shard_map/pick_rows/pallas_call | solution.py:396
  33.6 1.9 %collective-permute-start.4 = (bf16[128,1280]{1,0:T(8,128)(2,1)S(1)}, bf16[128,1280]{1,0:T(8,128)(2,1)S(1)}, u32[]{:S(2)}, u32[]{:S(2)}) collective-permute-start(bf16[128,1280]{1,0:T(8,128)(2,1)S(1)} %get-tuple-element.131.refs_0_), channel_id=1, source_target_pairs={{0,4},{1,5},{2,6},{3,7},{4,0},{5,1},{6,2},{7,3},{8,12},{9,13},{10,... | collective-permute-start | bytes 983048 | tf_op jit(solution)/shard_map/ppermute | solution.py:373
  35.5 0.9 collective-permute-start.5
  36.4 2.0 %collective-permute-start.3 = (bf16[128,1280]{1,0:T(8,128)(2,1)S(1)}, bf16[128,1280]{1,0:T(8,128)(2,1)S(1)}, u32[]{:S(2)}, u32[]{:S(2)}) collective-permute-start(bf16[128,1280]{1,0:T(8,128)(2,1)S(1)} %get-tuple-element.131.refs_0_), channel_id=1, source_target_pairs={{0,8},{1,9},{2,10},{3,11},{4,12},{5,13},{6,14},{7,15},{8,0},{9,1},... | collective-permute-start | bytes 983048 | tf_op jit(solution)/shard_map/ppermute | solution.py:373
  38.4 11.0 %collective-permute-done.4.refs_2_ = bf16[128,1280]{1,0:T(8,128)(2,1)S(1)} collective-permute-done((bf16[128,1280]{1,0:T(8,128)(2,1)S(1)}, bf16[128,1280]{1,0:T(8,128)(2,1)S(1)}, u32[]{:S(2)}, u32[]{:S(2)}) %collective-permute-start.4) | collective-permute-done | bytes 327712 | tf_op jit(solution)/shard_map/ppermute | solution.py:373
  49.4 1.2 %collective-permute-start.6 = (bf16[128,1280]{1,0:T(8,128)(2,1)S(1)}, bf16[128,1280]{1,0:T(8,128)(2,1)S(1)}, u32[]{:S(2)}, u32[]{:S(2)}) collective-permute-start(bf16[128,1280]{1,0:T(8,128)(2,1)S(1)} %collective-permute-done.4.refs_2_), channel_id=1, source_target_pairs={{0,2},{1,3},{2,0},{3,1},{4,6},{5,7},{6,4},{7,5},{8,10},{9,11},{10,... | collective-permute-start | bytes 983048 | tf_op jit(solution)/shard_map/ppermute | solution.py:373
  50.6 0.5 collective-permute-start.9
  51.1 2.6 %collective-permute-done.3.refs_4_ = bf16[128,1280]{1,0:T(8,128)(2,1)S(1)} collective-permute-done((bf16[128,1280]{1,0:T(8,128)(2,1)S(1)}, bf16[128,1280]{1,0:T(8,128)(2,1)S(1)}, u32[]{:S(2)}, u32[]{:S(2)}) %collective-permute-start.3) | collective-permute-done | bytes 327712 | tf_op jit(solution)/shard_map/ppermute | solution.py:373
  53.7 4.7 %collective-permute-done.6.refs_3_ = bf16[128,1280]{1,0:T(8,128)(2,1)S(1)} collective-permute-done((bf16[128,1280]{1,0:T(8,128)(2,1)S(1)}, bf16[128,1280]{1,0:T(8,128)(2,1)S(1)}, u32[]{:S(2)}, u32[]{:S(2)}) %collective-permute-start.6) | collective-permute-done | bytes 327712 | tf_op jit(solution)/shard_map/ppermute | solution.py:373
  58.4 1.2 %collective-permute-start.11 = (bf16[128,1280]{1,0:T(8,128)(2,1)S(1)}, bf16[128,1280]{1,0:T(8,128)(2,1)S(1)}, u32[]{:S(2)}, u32[]{:S(2)}) collective-permute-start(bf16[128,1280]{1,0:T(8,128)(2,1)S(1)} %collective-permute-done.3.refs_4_), channel_id=1, source_target_pairs={{0,2},{1,3},{2,0},{3,1},{4,6},{5,7},{6,4},{7,5},{8,10},{9,11},{10,... | collective-permute-start | bytes 983048 | tf_op jit(solution)/shard_map/ppermute | solution.py:373
  60.1 6.4 %collective-permute-done.10.refs_6_ = bf16[128,1280]{1,0:T(8,128)(2,1)S(1)} collective-permute-done((bf16[128,1280]{1,0:T(8,128)(2,1)S(1)}, bf16[128,1280]{1,0:T(8,128)(2,1)S(1)}, u32[]{:S(2)}, u32[]{:S(2)}) %collective-permute-start.10) | collective-permute-done | bytes 327712 | tf_op jit(solution)/shard_map/ppermute | solution.py:373
  67.2 1.0 %collective-permute-start.14 = (bf16[128,1280]{1,0:T(8,128)(2,1)S(1)}, bf16[128,1280]{1,0:T(8,128)(2,1)}, u32[]{:S(2)}, u32[]{:S(2)}) collective-permute-start(bf16[128,1280]{1,0:T(8,128)(2,1)S(1)} %collective-permute-done.10.refs_6_), channel_id=1, source_target_pairs={{0,2},{1,3},{2,0},{3,1},{4,6},{5,7},{6,4},{7,5},{8,10},{9,11},{10,... | collective-permute-start | bytes 983048 | tf_op jit(solution)/shard_map/ppermute | solution.py:373
  68.8 7.6 %half_transform.1 = (f32[512,1024]{1,0:T(8,128)S(1)}, bf16[256,1024]{1,0:T(8,128)(2,1)S(1)}) custom-call(bf16[16,24,256]{2,1,0:T(8,128)(2,1)S(1)} %all-to-all-done.got_ref, s32[1,256]{1,0:T(1,128)} %bitcast.76, bf16[128,1280]{1,0:T(8,128)(2,1)S(1)} %get-tuple-element.131.refs_0_, bf16[128,1280]{1,0:T(8,128)(2,1)S(1)} %collective-permute-done.5.refs_1_, ...), custom_call_target="tpu_custom_call" | custom-call | flops 4000000000 | bytes 8000000 | tf_op jit(solution)/shard_map/half_transform/pallas_call | solution.py:421
  76.5 1.3 %copy-done.10 = f32[512,1024]{1,0:T(8,128)} copy-done((f32[512,1024]{1,0:T(8,128)}, f32[512,1024]{1,0:T(8,128)S(1)}, u32[]{:S(2)}) %copy-start.10) | copy-done | bytes 2097176
  77.8 0.8 copy-done.12
  78.8 1.8 %collective-permute-done.17.refs_15_ = bf16[128,1280]{1,0:T(8,128)(2,1)} collective-permute-done((bf16[128,1280]{1,0:T(8,128)(2,1)}, bf16[128,1280]{1,0:T(8,128)(2,1)}, u32[]{:S(2)}, u32[]{:S(2)}) %collective-permute-start.17) | collective-permute-done | bytes 327712 | tf_op jit(solution)/shard_map/ppermute | solution.py:373
  80.6 1.0 copy-done.3
  81.6 1.0 copy-done.5
  82.6 1.0 copy-done.7
  83.5 1.0 copy-done.9
  84.5 1.6 %copy-done.11 = f32[512,1024]{1,0:T(8,128)S(1)} copy-done((f32[512,1024]{1,0:T(8,128)S(1)}, f32[512,1024]{1,0:T(8,128)}, u32[]{:S(2)}) %copy-start.11) | copy-done | bytes 2097176
  86.1 1.0 %copy-done.13 = bf16[256,1024]{1,0:T(8,128)(2,1)S(1)} copy-done((bf16[256,1024]{1,0:T(8,128)(2,1)S(1)}, bf16[256,1024]{1,0:T(8,128)(2,1)}, u32[]{:S(2)}) %copy-start.13) | copy-done | bytes 524312
  87.2 6.7 %last_product.1 = bf16[2,256,2304]{2,1,0:T(8,128)(2,1)} custom-call(s32[1]{0:T(128)} %bitcast.21.me_ref, f32[512,1024]{1,0:T(8,128)S(1)} %copy-done.11, bf16[256,1024]{1,0:T(8,128)(2,1)S(1)} %copy-done.13, bf16[128,1280]{1,0:T(8,128)(2,1)S(1)} %get-tuple-element.131.refs_0_, bf16[128,1280]{1,0:T(8,128)(2,1)S(1)} %collective-permute-done.5.refs_1_, ...), custom_call_target="tpu_custom_call" | custom-call | flops 3000000000 | bytes 10000000 | tf_op jit(solution)/shard_map/last_product/pallas_call | solution.py:441
  93.9 0.8 while.16
  (42 shorter events, 2.4 us)
Async XLA Ops:
  7.2 0.9 copy-start
  9.6 21.9 %all-to-all-start = ((bf16[16,24,256]{2,1,0:T(8,128)(2,1)}), bf16[16,24,256]{2,1,0:T(8,128)(2,1)S(1)}, u32[]{:S(2)}, u32[]{:S(2)}) async-start(bf16[16,24,256]{2,1,0:T(8,128)(2,1)} %pack_panels.1), calls=%async_computation | async-start | bytes 393216 | tf_op jit(solution)/shard_map/all_to_all | solution.py:394
  18.5 2.2 %collective-permute-start = (bf16[80,1280]{1,0:T(8,128)(2,1)S(1)}, bf16[80,1280]{1,0:T(8,128)(2,1)S(1)}, u32[]{:S(2)}, u32[]{:S(2)}) collective-permute-start(bf16[80,1280]{1,0:T(8,128)(2,1)S(1)} %get-tuple-element.127), channel_id=1, source_target_pairs={{0,1},{1,0},{2,3},{3,2},{4,5},{5,4},{6,7},{7,6},{8,9},{9,8},{10,11... | collective-permute-start | bytes 614408 | tf_op jit(solution)/shard_map/ppermute | solution.py:373
  19.0 8.7 %collective-permute-start.1 = (bf16[80,1280]{1,0:T(8,128)(2,1)S(1)}, bf16[80,1280]{1,0:T(8,128)(2,1)S(1)}, u32[]{:S(2)}, u32[]{:S(2)}) collective-permute-start(bf16[80,1280]{1,0:T(8,128)(2,1)S(1)} %get-tuple-element.128), channel_id=1, source_target_pairs={{0,2},{1,3},{2,0},{3,1},{4,6},{5,7},{6,4},{7,5},{8,10},{9,11},{10,... | collective-permute-start | bytes 614408 | tf_op jit(solution)/shard_map/ppermute | solution.py:373
  20.7 10.8 %collective-permute-start.2 = (bf16[80,1280]{1,0:T(8,128)(2,1)S(1)}, bf16[80,1280]{1,0:T(8,128)(2,1)S(1)}, u32[]{:S(2)}, u32[]{:S(2)}) collective-permute-start(bf16[80,1280]{1,0:T(8,128)(2,1)S(1)} %get-tuple-element.129), channel_id=1, source_target_pairs={{0,3},{1,2},{2,1},{3,0},{4,7},{5,6},{6,5},{7,4},{8,11},{9,10},{10,... | collective-permute-start | bytes 614408 | tf_op jit(solution)/shard_map/ppermute | solution.py:373
  33.6 15.8 %collective-permute-start.4 = (bf16[128,1280]{1,0:T(8,128)(2,1)S(1)}, bf16[128,1280]{1,0:T(8,128)(2,1)S(1)}, u32[]{:S(2)}, u32[]{:S(2)}) collective-permute-start(bf16[128,1280]{1,0:T(8,128)(2,1)S(1)} %get-tuple-element.131.refs_0_), channel_id=1, source_target_pairs={{0,4},{1,5},{2,6},{3,7},{4,0},{5,1},{6,2},{7,3},{8,12},{9,13},{10,... | collective-permute-start | bytes 983048 | tf_op jit(solution)/shard_map/ppermute | solution.py:373
  35.5 13.8 %collective-permute-start.5 = (bf16[128,1280]{1,0:T(8,128)(2,1)S(1)}, bf16[128,1280]{1,0:T(8,128)(2,1)S(1)}, u32[]{:S(2)}, u32[]{:S(2)}) collective-permute-start(bf16[128,1280]{1,0:T(8,128)(2,1)S(1)} %get-tuple-element.131.refs_0_), channel_id=1, source_target_pairs={{0,2},{1,3},{2,0},{3,1},{4,6},{5,7},{6,4},{7,5},{8,10},{9,11},{10,... | collective-permute-start | bytes 983048 | tf_op jit(solution)/shard_map/ppermute | solution.py:373
  36.4 17.3 %collective-permute-start.3 = (bf16[128,1280]{1,0:T(8,128)(2,1)S(1)}, bf16[128,1280]{1,0:T(8,128)(2,1)S(1)}, u32[]{:S(2)}, u32[]{:S(2)}) collective-permute-start(bf16[128,1280]{1,0:T(8,128)(2,1)S(1)} %get-tuple-element.131.refs_0_), channel_id=1, source_target_pairs={{0,8},{1,9},{2,10},{3,11},{4,12},{5,13},{6,14},{7,15},{8,0},{9,1},... | collective-permute-start | bytes 983048 | tf_op jit(solution)/shard_map/ppermute | solution.py:373
  38.4 15.3 %collective-permute-start.7 = (bf16[128,1280]{1,0:T(8,128)(2,1)S(1)}, bf16[128,1280]{1,0:T(8,128)(2,1)S(1)}, u32[]{:S(2)}, u32[]{:S(2)}) collective-permute-start(bf16[128,1280]{1,0:T(8,128)(2,1)S(1)} %get-tuple-element.131.refs_0_), channel_id=1, source_target_pairs={{0,1},{1,0},{2,3},{3,2},{4,5},{5,4},{6,7},{7,6},{8,9},{9,8},{10,11... | collective-permute-start | bytes 983048 | tf_op jit(solution)/shard_map/ppermute | solution.py:373
  49.4 9.1 %collective-permute-start.6 = (bf16[128,1280]{1,0:T(8,128)(2,1)S(1)}, bf16[128,1280]{1,0:T(8,128)(2,1)S(1)}, u32[]{:S(2)}, u32[]{:S(2)}) collective-permute-start(bf16[128,1280]{1,0:T(8,128)(2,1)S(1)} %collective-permute-done.4.refs_2_), channel_id=1, source_target_pairs={{0,2},{1,3},{2,0},{3,1},{4,6},{5,7},{6,4},{7,5},{8,10},{9,11},{10,... | collective-permute-start | bytes 983048 | tf_op jit(solution)/shard_map/ppermute | solution.py:373
  50.6 7.9 %collective-permute-start.8 = (bf16[128,1280]{1,0:T(8,128)(2,1)S(1)}, bf16[128,1280]{1,0:T(8,128)(2,1)S(1)}, u32[]{:S(2)}, u32[]{:S(2)}) collective-permute-start(bf16[128,1280]{1,0:T(8,128)(2,1)S(1)} %collective-permute-done.5.refs_1_), channel_id=1, source_target_pairs={{0,1},{1,0},{2,3},{3,2},{4,5},{5,4},{6,7},{7,6},{8,9},{9,8},{10,11... | collective-permute-start | bytes 983048 | tf_op jit(solution)/shard_map/ppermute | solution.py:373
  50.6 7.9 %collective-permute-start.9 = (bf16[128,1280]{1,0:T(8,128)(2,1)S(1)}, bf16[128,1280]{1,0:T(8,128)(2,1)S(1)}, u32[]{:S(2)}, u32[]{:S(2)}) collective-permute-start(bf16[128,1280]{1,0:T(8,128)(2,1)S(1)} %collective-permute-done.4.refs_2_), channel_id=1, source_target_pairs={{0,1},{1,0},{2,3},{3,2},{4,5},{5,4},{6,7},{7,6},{8,9},{9,8},{10,11... | collective-permute-start | bytes 983048 | tf_op jit(solution)/shard_map/ppermute | solution.py:373
  58.4 8.1 %collective-permute-start.10 = (bf16[128,1280]{1,0:T(8,128)(2,1)S(1)}, bf16[128,1280]{1,0:T(8,128)(2,1)S(1)}, u32[]{:S(2)}, u32[]{:S(2)}) collective-permute-start(bf16[128,1280]{1,0:T(8,128)(2,1)S(1)} %collective-permute-done.3.refs_4_), channel_id=1, source_target_pairs={{0,4},{1,5},{2,6},{3,7},{4,0},{5,1},{6,2},{7,3},{8,12},{9,13},{10,... | collective-permute-start | bytes 983048 | tf_op jit(solution)/shard_map/ppermute | solution.py:373
  58.4 8.2 %collective-permute-start.11 = (bf16[128,1280]{1,0:T(8,128)(2,1)S(1)}, bf16[128,1280]{1,0:T(8,128)(2,1)S(1)}, u32[]{:S(2)}, u32[]{:S(2)}) collective-permute-start(bf16[128,1280]{1,0:T(8,128)(2,1)S(1)} %collective-permute-done.3.refs_4_), channel_id=1, source_target_pairs={{0,2},{1,3},{2,0},{3,1},{4,6},{5,7},{6,4},{7,5},{8,10},{9,11},{10,... | collective-permute-start | bytes 983048 | tf_op jit(solution)/shard_map/ppermute | solution.py:373
  59.6 7.0 %collective-permute-start.12 = (bf16[128,1280]{1,0:T(8,128)(2,1)S(1)}, bf16[128,1280]{1,0:T(8,128)(2,1)S(1)}, u32[]{:S(2)}, u32[]{:S(2)}) collective-permute-start(bf16[128,1280]{1,0:T(8,128)(2,1)S(1)} %collective-permute-done.6.refs_3_), channel_id=1, source_target_pairs={{0,1},{1,0},{2,3},{3,2},{4,5},{5,4},{6,7},{7,6},{8,9},{9,8},{10,11... | collective-permute-start | bytes 983048 | tf_op jit(solution)/shard_map/ppermute | solution.py:373
  59.6 7.0 %collective-permute-start.13 = (bf16[128,1280]{1,0:T(8,128)(2,1)S(1)}, bf16[128,1280]{1,0:T(8,128)(2,1)S(1)}, u32[]{:S(2)}, u32[]{:S(2)}) collective-permute-start(bf16[128,1280]{1,0:T(8,128)(2,1)S(1)} %collective-permute-done.3.refs_4_), channel_id=1, source_target_pairs={{0,1},{1,0},{2,3},{3,2},{4,5},{5,4},{6,7},{7,6},{8,9},{9,8},{10,11... | collective-permute-start | bytes 983048 | tf_op jit(solution)/shard_map/ppermute | solution.py:373
  66.6 9.8 %copy-start.2 = (bf16[128,1280]{1,0:T(8,128)(2,1)}, bf16[128,1280]{1,0:T(8,128)(2,1)S(1)}, u32[]{:S(2)}) copy-start(bf16[128,1280]{1,0:T(8,128)(2,1)S(1)} %collective-permute-done.12.refs_10_.refs_11_) | copy-start | bytes 983044
  66.6 9.8 %copy-start.4 = (bf16[128,1280]{1,0:T(8,128)(2,1)}, bf16[128,1280]{1,0:T(8,128)(2,1)S(1)}, u32[]{:S(2)}) copy-start(bf16[128,1280]{1,0:T(8,128)(2,1)S(1)} %collective-permute-done.13.refs_11_.refs_12_) | copy-start | bytes 983044
  66.7 1.7 %collective-permute-start.15 = (bf16[128,1280]{1,0:T(8,128)(2,1)S(1)}, bf16[128,1280]{1,0:T(8,128)(2,1)S(1)}, u32[]{:S(2)}, u32[]{:S(2)}) collective-permute-start(bf16[128,1280]{1,0:T(8,128)(2,1)S(1)} %collective-permute-done.11.refs_5_), channel_id=1, source_target_pairs={{0,1},{1,0},{2,3},{3,2},{4,5},{5,4},{6,7},{7,6},{8,9},{9,8},{10,11... | collective-permute-start | bytes 983048 | tf_op jit(solution)/shard_map/ppermute | solution.py:373
  66.7 2.1 %collective-permute-start.16 = (bf16[128,1280]{1,0:T(8,128)(2,1)S(1)}, bf16[128,1280]{1,0:T(8,128)(2,1)S(1)}, u32[]{:S(2)}, u32[]{:S(2)}) collective-permute-start(bf16[128,1280]{1,0:T(8,128)(2,1)S(1)} %collective-permute-done.10.refs_6_), channel_id=1, source_target_pairs={{0,1},{1,0},{2,3},{3,2},{4,5},{5,4},{6,7},{7,6},{8,9},{9,8},{10,11... | collective-permute-start | bytes 983048 | tf_op jit(solution)/shard_map/ppermute | solution.py:373
  67.2 11.4 %collective-permute-start.14 = (bf16[128,1280]{1,0:T(8,128)(2,1)S(1)}, bf16[128,1280]{1,0:T(8,128)(2,1)}, u32[]{:S(2)}, u32[]{:S(2)}) collective-permute-start(bf16[128,1280]{1,0:T(8,128)(2,1)S(1)} %collective-permute-done.10.refs_6_), channel_id=1, source_target_pairs={{0,2},{1,3},{2,0},{3,1},{4,6},{5,7},{6,4},{7,5},{8,10},{9,11},{10,... | collective-permute-start | bytes 983048 | tf_op jit(solution)/shard_map/ppermute | solution.py:373
  68.3 8.1 %copy-start.6 = (bf16[128,1280]{1,0:T(8,128)(2,1)}, bf16[128,1280]{1,0:T(8,128)(2,1)S(1)}, u32[]{:S(2)}) copy-start(bf16[128,1280]{1,0:T(8,128)(2,1)S(1)} %collective-permute-done.15.refs_12_.refs_13_) | copy-start | bytes 983044
  68.8 7.7 %copy-start.8 = (bf16[128,1280]{1,0:T(8,128)(2,1)}, bf16[128,1280]{1,0:T(8,128)(2,1)S(1)}, u32[]{:S(2)}) copy-start(bf16[128,1280]{1,0:T(8,128)(2,1)S(1)} %collective-permute-done.16.refs_13_.refs_14_) | copy-start | bytes 983044
  76.5 1.3 %copy-start.10 = (f32[512,1024]{1,0:T(8,128)}, f32[512,1024]{1,0:T(8,128)S(1)}, u32[]{:S(2)}) copy-start(f32[512,1024]{1,0:T(8,128)S(1)} %get-tuple-element.148.part_ref) | copy-start | bytes 6291460
  78.6 2.0 %collective-permute-start.17 = (bf16[128,1280]{1,0:T(8,128)(2,1)}, bf16[128,1280]{1,0:T(8,128)(2,1)}, u32[]{:S(2)}, u32[]{:S(2)}) collective-permute-start(bf16[128,1280]{1,0:T(8,128)(2,1)} %collective-permute-done.14.refs_7_), channel_id=1, source_target_pairs={{0,1},{1,0},{2,3},{3,2},{4,5},{5,4},{6,7},{7,6},{8,9},{9,8},{10,11... | collective-permute-start | bytes 983048 | tf_op jit(solution)/shard_map/ppermute | solution.py:373
  80.6 1.0 copy-start.3
  81.6 1.0 copy-start.5
  82.6 1.0 copy-start.7
  83.5 1.0 copy-start.9
  84.5 1.6 %copy-start.11 = (f32[512,1024]{1,0:T(8,128)S(1)}, f32[512,1024]{1,0:T(8,128)}, u32[]{:S(2)}) copy-start(f32[512,1024]{1,0:T(8,128)} %copy-done.10) | copy-start | bytes 6291460
  86.1 1.0 %copy-start.13 = (bf16[256,1024]{1,0:T(8,128)(2,1)S(1)}, bf16[256,1024]{1,0:T(8,128)(2,1)}, u32[]{:S(2)}) copy-start(bf16[256,1024]{1,0:T(8,128)(2,1)} %copy-done.12) | copy-start | bytes 1572868
  87.1 6.7 %copy-start.15 = (s32[256]{0:T(256)S(1)}, s32[256]{0:T(256)}, u32[]{:S(2)}) copy-start(s32[256]{0:T(256)} %param.11) | copy-start | bytes 3076
  (2 other events, 1.5 us)

commit v8 on v6

--- a/solution.py
+++ b/solution.py
@@ -127,14 +127,7 @@
             self.edges.append(jnp.sum(self.used * jnp.floor((reach + extra) * 0.5), axis=0, keepdims=True))
 
 
-def pack_kernel(shells, pairs_any, count_any, vir_ref, occ_ref, code_ref, *refs):
-    outs, (pairs_ref, count_ref, sems) = refs[:4], refs[4:]
-    copies = [
-        pltpu.make_async_copy(pairs_any, pairs_ref, sems.at[0]),
-        pltpu.make_async_copy(count_any, count_ref, sems.at[1]),
-    ]
-    for copy in copies:
-        copy.start()
+def pack_kernel(vir_ref, occ_ref, *outs):
     me = lax.axis_index("shell")
     core, y = lax.rem(me, 2), lax.rem(lax.div(me, 2), 2)
     here, nvir = vir_ref.shape
@@ -149,8 +142,9 @@
             out[:, :width] = jnp.dot(pick, part, preferred_element_type=F32).astype(BF16)
             part = occ_ref[:, pl.ds(pl.multiple_of(half * thin, 128), thin)]
             out[:, width:] = jnp.dot(pick, part, preferred_element_type=F32).astype(BF16)
-    for copy in copies:
-        copy.wait()
+
+
+def ids_kernel(shells, pairs_ref, count_ref, code_ref):
     code = pairs_ref[1:2, :] + shells * pairs_ref[0:1, :]
     code = jnp.where(iota((1, BLK_DEV), 1) < count_ref[...], code, -1).astype(F32)
     square = (BLK_DEV, BLK_DEV)
@@ -158,7 +152,7 @@
     code_ref[...] = jnp.broadcast_to(jnp.broadcast_to(code, (BLK_DEV, 128))[None], code_ref.shape)
 
 
-def send_kernel(panels_ref, send_ref):
+def turn_kernel(panels_ref, send_ref):
     turned = jnp.swapaxes(panels_ref[...].astype(F32), 0, 1)
     send_ref[...] = turned.reshape(send_ref.shape).astype(BF16)
 
@@ -205,10 +199,8 @@
 
 
 def slot_of(window, chip):
-    z = lax.div(chip, Y)
-    slot = window ^ chip
-    inner = (z == 1) | (z == 2)
-    return jnp.where(inner & (slot >= 2 * Y), slot ^ Y, slot)
+    rel = window ^ chip
+    return jnp.where((rel == 3) | (rel == 4), rel ^ 7, rel)
 
 
 def half_kernel(here, code_ref, got_ref, size_ref, *refs):
@@ -226,12 +218,12 @@
             copies.append(pltpu.make_async_copy(pieces[at].at[:, pl.ds(width, 128)], target, sems.at[at]))
     for copy in copies:
         copy.start()
-    occ_ref[count * CAP :, :] = jnp.zeros((occ_ref.shape[0] - count * CAP, occ_ref.shape[1]), BF16)
     window = CORES * Y * here
     shell_count = size_ref.shape[1]
     got = got_ref[...].astype(F32)
     size_row = size_ref[...].astype(F32)
     shells = Shells(size_row)
+    got = got_ref[...].astype(F32)
     hots = slot_hots(code_ref[...], shell_count)
     lists = [Used(shells, hot, window) for hot in hots]
     slots = hots[0].shape[0]
@@ -287,7 +279,7 @@
         rows = slice(g * span, (g + 1) * span)
         r_hot = zero_one(place_r[rows] == lanes).astype(BF16)
         c_hot = zero_one(place_c[rows] == lanes).astype(BF16)
-        part = jnp.dot(r_hot, occ, preferred_element_type=F32).T.astype(BF16)
+        part = jnp.dot(r_hot[:, : count * CAP], occ, preferred_element_type=F32).T.astype(BF16)
         for p in range(2):
             block = blocks[p][g * 16 : (g + 1) * 16].reshape(16, 1, span)
             block = jnp.broadcast_to(block, (16, EDGE, span)).reshape(span, span)
@@ -297,7 +289,6 @@
             placed = jnp.dot(diag, c_hot, preferred_element_type=F32).astype(BF16)
             piece = jnp.dot(part, placed, preferred_element_type=F32)
             rows_p = slice(p * NOCC, (p + 1) * NOCC)
-            rows_l = slice(p * CAP, (p + 1) * CAP)
             later = jnp.dot(r_hot[:, count * CAP :].T, placed, preferred_element_type=F32)
             if g == 0:
                 half_ref[rows_p, :] = piece
@@ -306,10 +297,10 @@
                 half_ref[rows_p, :] += piece
                 late[p] += later
     for p in range(2):
-        late_ref[p * CAP : (p + 1) * CAP, :] = late[p].astype(BF16)
-
-
-def last_kernel(count, me_ref, part_ref, late_ref, *refs):
+        late_ref[p] = late[p].astype(BF16)
+
+
+def last_kernel(count, early, me_ref, part_ref, late_ref, *refs):
     pieces, (out_ref, right_ref, occ_ref, half_ref, sems) = refs[: 2 * count], refs[2 * count :]
     tile = out_ref.shape[2]
     width = right_ref.shape[2]
@@ -320,9 +311,10 @@
     def occ_copies():
         for far in range(2):
             half = lax.rem(core + far, CORES)
-            target = occ_ref.at[:, pl.ds(pl.multiple_of(half * 128, 128), 128)]
-            source = pieces[far * count + count - 1].at[:, pl.ds(width, 128)]
-            yield pltpu.make_async_copy(source, target, sems.at[2 * count + far])
+            for k in range(early, count):
+                at = far * count + k
+                target = occ_ref.at[pl.ds((k - early) * CAP, CAP), pl.ds(pl.multiple_of(half * 128, 128), 128)]
+                yield pltpu.make_async_copy(pieces[at].at[:, pl.ds(width, 128)], target, sems.at[2 * count + at])
 
     def copies(far):
         for k in range(count):
@@ -339,7 +331,7 @@
         occ = occ_ref[...].T
         for p in range(2):
             rows = slice(p * NOCC, (p + 1) * NOCC)
-            late = jnp.dot(occ, late_ref[p * CAP : (p + 1) * CAP, :], preferred_element_type=F32)
+            late = jnp.dot(occ, late_ref[p], preferred_element_type=F32)
             half_ref[rows, :] = (part_ref[rows, :] + late).astype(BF16)
 
     for far in range(2):
@@ -356,7 +348,6 @@
 
 VMEM = pl.BlockSpec(memory_space=pltpu.VMEM)
 SMEM = pl.BlockSpec(memory_space=pltpu.SMEM)
-HBM = pl.BlockSpec(memory_space=pltpu.HBM)
 ANY = pl.BlockSpec(memory_space=pl.ANY)
 
 
@@ -384,21 +375,25 @@
     def swap(array, bit):
         return lax.ppermute(array, "shell", [(i, i ^ bit) for i in range(n)])
 
-    code, keep, to_core, to_y, to_both = pl.pallas_call(
-        functools.partial(pack_kernel, size_row.shape[1]),
-        out_shape=[shape(n, BLK_DEV, 128, dtype=jnp.int32)] + [shape(here // 2, packed)] * 4,
-        in_specs=[HBM] * 2 + [VMEM] * 2,
-        out_specs=[VMEM] * 5,
-        scratch_shapes=[
-            pltpu.VMEM((2, BLK_DEV), jnp.int32),
-            pltpu.VMEM((1, 1), jnp.int32),
-            pltpu.SemaphoreType.DMA((2,)),
-        ],
+    keep, to_core, to_y, to_both = pl.pallas_call(
+        pack_kernel,
+        out_shape=[shape(here // 2, packed)] * 4,
+        in_specs=[VMEM] * 2,
+        out_specs=[VMEM] * 4,
         compiler_params=params(12),
         cost_estimate=cost(3e8, 3e6),
         name="pack_rows",
-    )(block_pairs.T, block_count.reshape(1, 1), vir_coef, occ_coef)
+    )(vir_coef, occ_coef)
     to_y, to_both, to_core = swap(to_y, 2), swap(to_both, 3), swap(to_core, 1)
+    code = pl.pallas_call(
+        functools.partial(ids_kernel, size_row.shape[1]),
+        out_shape=shape(n, BLK_DEV, 128, dtype=jnp.int32),
+        in_specs=[VMEM] * 2,
+        out_specs=VMEM,
+        compiler_params=params(12),
+        cost_estimate=cost(1e4, 1e4),
+        name="pack_ids",
+    )(block_pairs.T, block_count.reshape(1, 1))
     code = lax.all_to_all(code, "shell", split_axis=0, concat_axis=0, tiled=True)
 
     mine, over = pl.pallas_call(
@@ -411,27 +406,10 @@
         name="pick_rows",
     )(code, size_row, keep, to_core, to_y, to_both)
 
-    z = me // (Y * CORES)
-    inner = (z == 1) | (z == 2)
-    ends, middle, outward = [(0, 1), (1, 0), (2, 3), (3, 2)], [(1, 2), (2, 1)], [(1, 0), (2, 3)]
-
-    def hop(array, steps):
-        return lax.ppermute(array, "shell", [(4 * a + k, 4 * b + k) for a, b in steps for k in range(4)])
-
-    beside, across, mine_y = hop(mine, ends), hop(mine, middle), swap(mine, 2)
-    beside, across, mine_y = lax.optimization_barrier((beside, across, mine_y))
-
-    corner, across_out, beside_y = hop(beside, middle), hop(across, outward), swap(beside, 2)
-    far = [swap(mine, 1), swap(mine_y, 1), swap(beside, 1)]
-    corner, across_out, beside_y, panels, *far = lax.optimization_barrier(
-        (corner, across_out, beside_y, panels, *far)
-    )
-
-    across = jnp.where(inner, across, across_out)
-    corner_out, across_y = hop(corner, outward), swap(across, 2)
-    far += [swap(beside_y, 1), swap(across, 1)]
+    beside, across, mine_y = swap(mine, 4), swap(mine, 8), swap(mine, 2)
+    panels, _ = lax.optimization_barrier((panels, mine))
     send = pl.pallas_call(
-        send_kernel,
+        turn_kernel,
         out_shape=shape(n, 2 * BLK_DEV, EDGE * EDGE),
         in_specs=[VMEM],
         out_specs=VMEM,
@@ -440,54 +418,58 @@
         name="turn_panels",
     )(panels)
     got = lax.all_to_all(send, "shell", split_axis=0, concat_axis=0, tiled=True)
-    corner_out, across_y, got, *far = lax.optimization_barrier((corner_out, across_y, got, *far))
-
-    corner = jnp.where(inner, corner, corner_out)
-    corner_y = swap(corner, 2)
-    far += [swap(across_y, 1), swap(corner, 1)]
-    near = [mine, mine_y, beside, beside_y, across, across_y, corner]
-    count = len(near)
+    beside, across, mine_y, got = lax.optimization_barrier((beside, across, mine_y, got))
+
+    corner, beside_y, across_y = swap(across, 4), swap(beside, 2), swap(across, 2)
+    near = [mine, mine_y, beside, across]
+    far = [swap(piece, 1) for piece in near]
+    early = len(near)
     half, late = pl.pallas_call(
         functools.partial(half_kernel, here),
-        out_shape=(shape(2 * NOCC, room, dtype=F32), shape(2 * CAP, room)),
+        out_shape=(shape(2 * NOCC, room, dtype=F32), shape(2, room - early * CAP, room)),
         grid=(1,),
-        in_specs=[VMEM] * 3 + [ANY] * (2 * count),
+        in_specs=[VMEM] * 3 + [ANY] * (2 * early),
         out_specs=(
             pl.BlockSpec((2 * NOCC, room), lambda i: (0, 0)),
-            pl.BlockSpec((2 * CAP, room), lambda i: (0, 0)),
+            pl.BlockSpec((2, room - early * CAP, room), lambda i: (0, 0, 0)),
         ),
-        scratch_shapes=[pltpu.VMEM((room, NOCC), BF16), pltpu.SemaphoreType.DMA((2 * count,))],
-        compiler_params=params(24),
-        cost_estimate=cost(4e9, 8e6),
+        scratch_shapes=[pltpu.VMEM((early * CAP, NOCC), BF16), pltpu.SemaphoreType.DMA((2 * early,))],
+        compiler_params=params(28),
+        cost_estimate=cost(7e9, 1),
         name="half_transform",
     )(code, got, size_row, *near, *far)
-    corner_y, half, late = lax.optimization_barrier((corner_y, half, late))
+    corner, beside_y, across_y, half, late = lax.optimization_barrier((corner, beside_y, across_y, half, late))
+
+    corner_y = swap(corner, 2)
+    near += [beside_y, across_y, corner]
+    far += [swap(piece, 1) for piece in near[early:]]
+    corner_y, *far = lax.optimization_barrier((corner_y, *far))
     near.append(corner_y)
     far.append(swap(corner_y, 1))
 
     count = len(near)
     tile = width // 3
     out = pl.pallas_call(
-        functools.partial(last_kernel, count),
+        functools.partial(last_kernel, count, early),
         out_shape=shape(2, NOCC, nvir),
         grid_spec=pltpu.PrefetchScalarGridSpec(
             num_scalar_prefetch=1,
             grid=(nvir // tile,),
             in_specs=[
                 pl.BlockSpec((2 * NOCC, room), lambda j, o: (0, 0)),
-                pl.BlockSpec((2 * CAP, room), lambda j, o: (0, 0)),
+                pl.BlockSpec((2, room - early * CAP, room), lambda j, o: (0, 0, 0)),
             ]
             + [ANY] * (2 * count),
             out_specs=pl.BlockSpec((2, NOCC, tile), lambda j, o: (0, 0, (j + 3 * (o[0] % 2)) % 6)),
             scratch_shapes=[
                 pltpu.VMEM((CORES, room, width), BF16),
-                pltpu.VMEM((CAP, NOCC), BF16),
+                pltpu.VMEM((room - early * CAP, NOCC), BF16),
                 pltpu.VMEM((2 * NOCC, room), BF16),
-                pltpu.SemaphoreType.DMA((2 * count + 2,)),
+                pltpu.SemaphoreType.DMA((4 * count,)),
             ],
         ),
-        compiler_params=params(24),
-        cost_estimate=cost(3e9, 1e7),
+        compiler_params=params(28),
+        cost_estimate=cost(2e10, 1),
         name="last_product",
     )(me.reshape(1), half, late, *near, *far)
     return out, over[0], code, got

time: 95.7 us -> 101 us (1.055)
  blocking collectives: 25.8 us -> 12.8 us
  local copies, waits for them, and re-layouts: 1.58 us -> 14.2 us
  starting transfers between devices: 12 us -> 16.4 us
  Pallas kernels: 17.3 us -> 20.5 us
  waiting for transfers between devices: 23.6 us -> 21.9 us
    ppermute x5 -> x0, waiting for transfers between devices: 18.1 us -> none  [hop(): lax.ppermute(array, 'shell', [(4 * a + k, 4 * b + k) for a, b in steps fo...]
    all_to_all x1 -> x0, blocking collectives: 13 us -> none  [short_way(): got = lax.all_to_all(send, 'shell', split_axis=0, concat_axis=0, tiled=True)]
    unnamed x6 -> x30, local copies, waits for them, and re-layouts: 1.58 us -> 14.2 us
    all_to_all x0 -> x1, waiting for transfers between devices: none -> 10.5 us  [short_way(): got = lax.all_to_all(send, 'shell', split_axis=0, concat_axis=0, tiled=True)]
    ppermute x15 -> x18, waiting for transfers between devices: 5.46 us -> 11.4 us  [swap(): return lax.ppermute(array, 'shell', [(i, i ^ bit) for i in range(n)])]
    all_to_all x0 -> x1, starting transfers between devices: none -> 4.95 us  [short_way(): got = lax.all_to_all(send, 'shell', split_axis=0, concat_axis=0, tiled=True)]
    ppermute x5 -> x0, starting transfers between devices: 4.1 us -> none  [hop(): lax.ppermute(array, 'shell', [(4 * a + k, 4 * b + k) for a, b in steps fo...]
    ppermute x15 -> x18, starting transfers between devices: 7.93 us -> 11.5 us  [swap(): return lax.ppermute(array, 'shell', [(i, i ^ bit) for i in range(n)])]
  transfers between devices with their start and end apart: 20 -> 19, of which waited for: 7 -> 4; matrix products, arithmetic and copies ran while one was open for 0% -> 0% of each run, Pallas kernels for 7% -> 10%
where the time goes in v8:
time: 101 us
  waiting for transfers between devices  21.9 us (22%)
  Pallas kernels  20.5 us (20%)
  starting transfers between devices  16.4 us (16%)
  local copies, waits for them, and re-layouts  14.2 us (14%)
  between operations  14.1 us (14%)
  blocking collectives  12.8 us (13%)
    unnamed x30, local copies, waits for them, and re-layouts  14.2 us
    all_to_all x1, blocking collectives, short_way(): lax.all_to_all(code, 'shell', split_axis=0, concat_axis=0, tiled=True)  12.8 us
    ppermute x18, starting transfers between devices, swap(): return lax.ppermute(array, 'shell', [(i, i ^ bit) for i in range(n)])  11.5 us
    ppermute x18, waiting for transfers between devices, swap(): return lax.ppermute(array, 'shell', [(i, i ^ bit) for i in range(n)])  11.4 us
    all_to_all x1, waiting for transfers between devices, short_way(): got = lax.all_to_all(send, 'shell', split_axis=0, concat_axis=0, tiled=True)  10.5 us
    pallas_call x1, Pallas kernels, short_way(): pl.pallas_call(functools.partial(half_kernel, here), out_shape=(shape(2 *...  8.86 us
    pallas_call x1, Pallas kernels, short_way(): pl.pallas_call(functools.partial(last_kernel, count, early), out_shape=sh...  7.12 us
    all_to_all x1, starting transfers between devices, short_way(): got = lax.all_to_all(send, 'shell', split_axis=0, concat_axis=0, tiled=True)  4.95 us
  transfers between devices with their start and end apart: 19, of which 4 were waited for; matrix products, arithmetic and copies ran while one was open for 0% of the time, Pallas kernels for 10%

profile of v8, /device:TPU:0, one launch (start us, length us, event | category | flops | bytes accessed | tf_op | source)
XLA Modules:
  0.0 100.7 jit_solution(18203677004267881633)
XLA Ops:
  6.5 1.5 %pack_rows.1 = (bf16[80,1280]{1,0:T(8,128)(2,1)S(1)}, bf16[80,1280]{1,0:T(8,128)(2,1)S(1)}, bf16[80,1280]{1,0:T(8,128)(2,1)S(1)}, bf16[80,1280]{1,0:T(8,128)(2,1)S(1)}) custom-call(bf16[160,2304]{1,0:T(8,128)(2,1)} %vir_ref.1, bf16[160,256]{1,0:T(8,128)(2,1)} %occ_ref.1), custom_call_target="tpu_custom_call" | custom-call | flops 300000000 | bytes 3000000 | tf_op jit(solution)/shard_map/pack_rows/pallas_call | solution.py:378
  8.6 2.6 %collective-permute-start.1 = (bf16[80,1280]{1,0:T(8,128)(2,1)S(1)}, bf16[80,1280]{1,0:T(8,128)(2,1)S(1)}, u32[]{:S(2)}, u32[]{:S(2)}) collective-permute-start(bf16[80,1280]{1,0:T(8,128)(2,1)S(1)} %get-tuple-element.173), channel_id=1, source_target_pairs={{0,2},{1,3},{2,0},{3,1},{4,6},{5,7},{6,4},{7,5},{8,10},{9,11},{10,... | collective-permute-start | bytes 614408 | tf_op jit(solution)/shard_map/ppermute | solution.py:376
  11.9 0.7 copy-done.1
  12.8 12.8 %all_to_all.10.code_ref = s32[16,8,128]{2,1,0:T(8,128)S(1)} all-to-all(s32[16,8,128]{2,1,0:T(8,128)S(1)} %pack_ids.1), channel_id=1, replica_groups=mesh['groups'=2,'shell'=16] {'shell'}, dimensions={0} | all-to-all | bytes 131072 | tf_op jit(solution)/shard_map/all_to_all | solution.py:397
  25.6 2.2 %pick_rows.1 = (bf16[128,1280]{1,0:T(8,128)(2,1)S(1)}, s32[1]{0:T(128)}) custom-call(s32[16,8,128]{2,1,0:T(8,128)S(1)} %all_to_all.10.code_ref, s32[1,256]{1,0:T(1,128)} %bitcast.64, bf16[80,1280]{1,0:T(8,128)(2,1)S(1)} %get-tuple-element.171.refs_0_, bf16[80,1280]{1,0:T(8,128)(2,1)S(1)} %collective-permute-done.refs_1_, ...), custom_call_target="tpu_custom_call" | custom-call | flops 300000000 | bytes 2000000 | tf_op jit(solution)/shard_map/pick_rows/pallas_call | solution.py:399
  28.0 1.0 collective-permute-start.4
  28.9 1.2 %collective-permute-start.5 = (bf16[128,1280]{1,0:T(8,128)(2,1)S(1)}, bf16[128,1280]{1,0:T(8,128)(2,1)S(1)}, u32[]{:S(2)}, u32[]{:S(2)}) collective-permute-start(bf16[128,1280]{1,0:T(8,128)(2,1)S(1)} %get-tuple-element.176.refs_0_), channel_id=1, source_target_pairs={{0,2},{1,3},{2,0},{3,1},{4,6},{5,7},{6,4},{7,5},{8,10},{9,11},{10,... | collective-permute-start | bytes 983048 | tf_op jit(solution)/shard_map/ppermute | solution.py:376
  30.1 0.9 copy-done
  31.0 0.7 turn_panels.1
  31.7 4.9 %all-to-all-start.1 = ((bf16[16,16,256]{2,1,0:T(8,128)(2,1)}), bf16[16,16,256]{2,1,0:T(8,128)(2,1)S(1)}, u32[]{:S(2)}, u32[]{:S(2)}) async-start(bf16[16,16,256]{2,1,0:T(8,128)(2,1)} %turn_panels.1), calls=%async_computation.1 | async-start | bytes 262144 | tf_op jit(solution)/shard_map/all_to_all | solution.py:420
  37.2 10.5 %all-to-all-done.1.got_ref = bf16[16,16,256]{2,1,0:T(8,128)(2,1)S(1)} async-done(((bf16[16,16,256]{2,1,0:T(8,128)(2,1)}), bf16[16,16,256]{2,1,0:T(8,128)(2,1)S(1)}, u32[]{:S(2)}, u32[]{:S(2)}) %all-to-all-start.1) | async-done | bytes 131104 | tf_op jit(solution)/shard_map/all_to_all | solution.py:420
  48.4 0.7 collective-permute-start.6
  49.2 1.5 %collective-permute-start.7 = (bf16[128,1280]{1,0:T(8,128)(2,1)S(1)}, bf16[128,1280]{1,0:T(8,128)(2,1)S(1)}, u32[]{:S(2)}, u32[]{:S(2)}) collective-permute-start(bf16[128,1280]{1,0:T(8,128)(2,1)S(1)} %collective-permute-done.3.refs_2_), channel_id=1, source_target_pairs={{0,2},{1,3},{2,0},{3,1},{4,6},{5,7},{6,4},{7,5},{8,10},{9,11},{10,... | collective-permute-start | bytes 983048 | tf_op jit(solution)/shard_map/ppermute | solution.py:376
  51.2 8.9 %half_transform.1 = (f32[512,1024]{1,0:T(8,128)S(1)}, bf16[2,512,1024]{2,1,0:T(8,128)(2,1)S(1)}) custom-call(s32[16,8,128]{2,1,0:T(8,128)S(1)} %all_to_all.10.code_ref, bf16[16,16,256]{2,1,0:T(8,128)(2,1)S(1)} %all-to-all-done.1.got_ref, s32[1,256]{1,0:T(1,128)} %bitcast.65, bf16[128,1280]{1,0:T(8,128)(2,1)S(1)} %get-tuple-element.176.refs_0_, ...), custom_call_target="tpu_custom_call" | custom-call | flops 7000000000 | bytes 1 | tf_op jit(solution)/shard_map/half_transform/pallas_call | solution.py:427
  60.1 1.3 %copy-done.10 = f32[512,1024]{1,0:T(8,128)} copy-done((f32[512,1024]{1,0:T(8,128)}, f32[512,1024]{1,0:T(8,128)S(1)}, u32[]{:S(2)}) %copy-start.10) | copy-done | bytes 2097176
  61.4 1.3 %copy-done.12 = bf16[2,512,1024]{2,1,0:T(8,128)(2,1)} copy-done((bf16[2,512,1024]{2,1,0:T(8,128)(2,1)}, bf16[2,512,1024]{2,1,0:T(8,128)(2,1)S(1)}, u32[]{:S(2)}) %copy-start.12) | copy-done | bytes 2097176
  62.7 3.1 %collective-permute-done.8.refs_5_ = bf16[128,1280]{1,0:T(8,128)(2,1)S(1)} collective-permute-done((bf16[128,1280]{1,0:T(8,128)(2,1)S(1)}, bf16[128,1280]{1,0:T(8,128)(2,1)S(1)}, u32[]{:S(2)}, u32[]{:S(2)}) %collective-permute-start.8) | collective-permute-done | bytes 327712 | tf_op jit(solution)/shard_map/ppermute | solution.py:376
  65.9 1.5 %collective-permute-start.13 = (bf16[128,1280]{1,0:T(8,128)(2,1)S(1)}, bf16[128,1280]{1,0:T(8,128)(2,1)}, u32[]{:S(2)}, u32[]{:S(2)}) collective-permute-start(bf16[128,1280]{1,0:T(8,128)(2,1)S(1)} %collective-permute-done.6.refs_6_), channel_id=1, source_target_pairs={{0,2},{1,3},{2,0},{3,1},{4,6},{5,7},{6,4},{7,5},{8,10},{9,11},{10,... | collective-permute-start | bytes 983048 | tf_op jit(solution)/shard_map/ppermute | solution.py:376
  67.8 0.7 copy-done.2
  68.5 6.2 %collective-permute-done.13.refs_7_ = bf16[128,1280]{1,0:T(8,128)(2,1)} collective-permute-done((bf16[128,1280]{1,0:T(8,128)(2,1)S(1)}, bf16[128,1280]{1,0:T(8,128)(2,1)}, u32[]{:S(2)}, u32[]{:S(2)}) %collective-permute-start.13) | collective-permute-done | bytes 327712 | tf_op jit(solution)/shard_map/ppermute | solution.py:376
  74.8 0.7 copy-done.4
  75.5 0.7 copy-done.6
  76.3 0.7 copy-done.8
  77.0 2.0 %collective-permute-done.17.refs_15_ = bf16[128,1280]{1,0:T(8,128)(2,1)} collective-permute-done((bf16[128,1280]{1,0:T(8,128)(2,1)}, bf16[128,1280]{1,0:T(8,128)(2,1)}, u32[]{:S(2)}, u32[]{:S(2)}) %collective-permute-start.17) | collective-permute-done | bytes 327712 | tf_op jit(solution)/shard_map/ppermute | solution.py:376
  79.0 1.0 copy-done.3
  79.9 1.0 copy-done.5
  80.9 1.0 copy-done.7
  81.9 1.0 copy-done.9
  82.9 1.6 %copy-done.11 = f32[512,1024]{1,0:T(8,128)S(1)} copy-done((f32[512,1024]{1,0:T(8,128)S(1)}, f32[512,1024]{1,0:T(8,128)}, u32[]{:S(2)}) %copy-start.11) | copy-done | bytes 2097176
  84.4 1.6 %copy-done.13 = bf16[2,512,1024]{2,1,0:T(8,128)(2,1)S(1)} copy-done((bf16[2,512,1024]{2,1,0:T(8,128)(2,1)S(1)}, bf16[2,512,1024]{2,1,0:T(8,128)(2,1)}, u32[]{:S(2)}) %copy-start.13) | copy-done | bytes 2097176
  86.0 7.1 %last_product.1 = bf16[2,256,2304]{2,1,0:T(8,128)(2,1)} custom-call(s32[1]{0:T(128)} %bitcast.17.me_ref, f32[512,1024]{1,0:T(8,128)S(1)} %copy-done.11, bf16[2,512,1024]{2,1,0:T(8,128)(2,1)S(1)} %copy-done.13, bf16[128,1280]{1,0:T(8,128)(2,1)S(1)} %get-tuple-element.176.refs_0_, bf16[128,1280]{1,0:T(8,128)(2,1)S(1)} %collective-permute-done.5.refs_1_, ...), custom_call_target="tpu_custom_call" | custom-call | flops 20000000000 | bytes 1 | tf_op jit(solution)/shard_map/last_product/pallas_call | solution.py:452
  93.2 0.7 while.17
  (44 shorter events, 3.3 us)
Async XLA Ops:
  8.1 17.5 %collective-permute-start = (bf16[80,1280]{1,0:T(8,128)(2,1)S(1)}, bf16[80,1280]{1,0:T(8,128)(2,1)S(1)}, u32[]{:S(2)}, u32[]{:S(2)}) collective-permute-start(bf16[80,1280]{1,0:T(8,128)(2,1)S(1)} %get-tuple-element.172), channel_id=1, source_target_pairs={{0,1},{1,0},{2,3},{3,2},{4,5},{5,4},{6,7},{7,6},{8,9},{9,8},{10,11... | collective-permute-start | bytes 614408 | tf_op jit(solution)/shard_map/ppermute | solution.py:376
  8.6 17.0 %collective-permute-start.1 = (bf16[80,1280]{1,0:T(8,128)(2,1)S(1)}, bf16[80,1280]{1,0:T(8,128)(2,1)S(1)}, u32[]{:S(2)}, u32[]{:S(2)}) collective-permute-start(bf16[80,1280]{1,0:T(8,128)(2,1)S(1)} %get-tuple-element.173), channel_id=1, source_target_pairs={{0,2},{1,3},{2,0},{3,1},{4,6},{5,7},{6,4},{7,5},{8,10},{9,11},{10,... | collective-permute-start | bytes 614408 | tf_op jit(solution)/shard_map/ppermute | solution.py:376
  11.2 14.4 %collective-permute-start.2 = (bf16[80,1280]{1,0:T(8,128)(2,1)S(1)}, bf16[80,1280]{1,0:T(8,128)(2,1)S(1)}, u32[]{:S(2)}, u32[]{:S(2)}) collective-permute-start(bf16[80,1280]{1,0:T(8,128)(2,1)S(1)} %get-tuple-element.174), channel_id=1, source_target_pairs={{0,3},{1,2},{2,1},{3,0},{4,7},{5,6},{6,5},{7,4},{8,11},{9,10},{10,... | collective-permute-start | bytes 614408 | tf_op jit(solution)/shard_map/ppermute | solution.py:376
  27.8 19.9 %collective-permute-start.3 = (bf16[128,1280]{1,0:T(8,128)(2,1)S(1)}, bf16[128,1280]{1,0:T(8,128)(2,1)S(1)}, u32[]{:S(2)}, u32[]{:S(2)}) collective-permute-start(bf16[128,1280]{1,0:T(8,128)(2,1)S(1)} %get-tuple-element.176.refs_0_), channel_id=1, source_target_pairs={{0,4},{1,5},{2,6},{3,7},{4,0},{5,1},{6,2},{7,3},{8,12},{9,13},{10,... | collective-permute-start | bytes 983048 | tf_op jit(solution)/shard_map/ppermute | solution.py:376
  28.0 19.7 %collective-permute-start.4 = (bf16[128,1280]{1,0:T(8,128)(2,1)S(1)}, bf16[128,1280]{1,0:T(8,128)(2,1)S(1)}, u32[]{:S(2)}, u32[]{:S(2)}) collective-permute-start(bf16[128,1280]{1,0:T(8,128)(2,1)S(1)} %get-tuple-element.176.refs_0_), channel_id=1, source_target_pairs={{0,8},{1,9},{2,10},{3,11},{4,12},{5,13},{6,14},{7,15},{8,0},{9,1},... | collective-permute-start | bytes 983048 | tf_op jit(solution)/shard_map/ppermute | solution.py:376
  28.9 18.7 %collective-permute-start.5 = (bf16[128,1280]{1,0:T(8,128)(2,1)S(1)}, bf16[128,1280]{1,0:T(8,128)(2,1)S(1)}, u32[]{:S(2)}, u32[]{:S(2)}) collective-permute-start(bf16[128,1280]{1,0:T(8,128)(2,1)S(1)} %get-tuple-element.176.refs_0_), channel_id=1, source_target_pairs={{0,2},{1,3},{2,0},{3,1},{4,6},{5,7},{6,4},{7,5},{8,10},{9,11},{10,... | collective-permute-start | bytes 983048 | tf_op jit(solution)/shard_map/ppermute | solution.py:376
  30.1 0.9 copy-start
  31.7 15.9 %all-to-all-start.1 = ((bf16[16,16,256]{2,1,0:T(8,128)(2,1)}), bf16[16,16,256]{2,1,0:T(8,128)(2,1)S(1)}, u32[]{:S(2)}, u32[]{:S(2)}) async-start(bf16[16,16,256]{2,1,0:T(8,128)(2,1)} %turn_panels.1), calls=%async_computation.1 | async-start | bytes 262144 | tf_op jit(solution)/shard_map/all_to_all | solution.py:420
  36.7 12.5 %collective-permute-start.9 = (bf16[128,1280]{1,0:T(8,128)(2,1)S(1)}, bf16[128,1280]{1,0:T(8,128)(2,1)S(1)}, u32[]{:S(2)}, u32[]{:S(2)}) collective-permute-start(bf16[128,1280]{1,0:T(8,128)(2,1)S(1)} %get-tuple-element.176.refs_0_), channel_id=1, source_target_pairs={{0,1},{1,0},{2,3},{3,2},{4,5},{5,4},{6,7},{7,6},{8,9},{9,8},{10,11... | collective-permute-start | bytes 983048 | tf_op jit(solution)/shard_map/ppermute | solution.py:376
  47.7 3.0 %collective-permute-start.10 = (bf16[128,1280]{1,0:T(8,128)(2,1)S(1)}, bf16[128,1280]{1,0:T(8,128)(2,1)S(1)}, u32[]{:S(2)}, u32[]{:S(2)}) collective-permute-start(bf16[128,1280]{1,0:T(8,128)(2,1)S(1)} %collective-permute-done.5.refs_1_), channel_id=1, source_target_pairs={{0,1},{1,0},{2,3},{3,2},{4,5},{5,4},{6,7},{7,6},{8,9},{9,8},{10,11... | collective-permute-start | bytes 983048 | tf_op jit(solution)/shard_map/ppermute | solution.py:376
  47.9 3.3 %collective-permute-start.11 = (bf16[128,1280]{1,0:T(8,128)(2,1)S(1)}, bf16[128,1280]{1,0:T(8,128)(2,1)S(1)}, u32[]{:S(2)}, u32[]{:S(2)}) collective-permute-start(bf16[128,1280]{1,0:T(8,128)(2,1)S(1)} %collective-permute-done.3.refs_2_), channel_id=1, source_target_pairs={{0,1},{1,0},{2,3},{3,2},{4,5},{5,4},{6,7},{7,6},{8,9},{9,8},{10,11... | collective-permute-start | bytes 983048 | tf_op jit(solution)/shard_map/ppermute | solution.py:376
  48.2 3.0 %collective-permute-start.12 = (bf16[128,1280]{1,0:T(8,128)(2,1)S(1)}, bf16[128,1280]{1,0:T(8,128)(2,1)S(1)}, u32[]{:S(2)}, u32[]{:S(2)}) collective-permute-start(bf16[128,1280]{1,0:T(8,128)(2,1)S(1)} %collective-permute-done.4.refs_3_), channel_id=1, source_target_pairs={{0,1},{1,0},{2,3},{3,2},{4,5},{5,4},{6,7},{7,6},{8,9},{9,8},{10,11... | collective-permute-start | bytes 983048 | tf_op jit(solution)/shard_map/ppermute | solution.py:376
  48.4 14.3 %collective-permute-start.6 = (bf16[128,1280]{1,0:T(8,128)(2,1)S(1)}, bf16[128,1280]{1,0:T(8,128)(2,1)S(1)}, u32[]{:S(2)}, u32[]{:S(2)}) collective-permute-start(bf16[128,1280]{1,0:T(8,128)(2,1)S(1)} %collective-permute-done.4.refs_3_), channel_id=1, source_target_pairs={{0,4},{1,5},{2,6},{3,7},{4,0},{5,1},{6,2},{7,3},{8,12},{9,13},{10,... | collective-permute-start | bytes 983048 | tf_op jit(solution)/shard_map/ppermute | solution.py:376
  49.2 13.6 %collective-permute-start.7 = (bf16[128,1280]{1,0:T(8,128)(2,1)S(1)}, bf16[128,1280]{1,0:T(8,128)(2,1)S(1)}, u32[]{:S(2)}, u32[]{:S(2)}) collective-permute-start(bf16[128,1280]{1,0:T(8,128)(2,1)S(1)} %collective-permute-done.3.refs_2_), channel_id=1, source_target_pairs={{0,2},{1,3},{2,0},{3,1},{4,6},{5,7},{6,4},{7,5},{8,10},{9,11},{10,... | collective-permute-start | bytes 983048 | tf_op jit(solution)/shard_map/ppermute | solution.py:376
  50.6 15.2 %collective-permute-start.8 = (bf16[128,1280]{1,0:T(8,128)(2,1)S(1)}, bf16[128,1280]{1,0:T(8,128)(2,1)S(1)}, u32[]{:S(2)}, u32[]{:S(2)}) collective-permute-start(bf16[128,1280]{1,0:T(8,128)(2,1)S(1)} %collective-permute-done.4.refs_3_), channel_id=1, source_target_pairs={{0,2},{1,3},{2,0},{3,1},{4,6},{5,7},{6,4},{7,5},{8,10},{9,11},{10,... | collective-permute-start | bytes 983048 | tf_op jit(solution)/shard_map/ppermute | solution.py:376
  60.1 1.3 %copy-start.10 = (f32[512,1024]{1,0:T(8,128)}, f32[512,1024]{1,0:T(8,128)S(1)}, u32[]{:S(2)}) copy-start(f32[512,1024]{1,0:T(8,128)S(1)} %get-tuple-element.184.part_ref) | copy-start | bytes 6291460
  61.4 1.4 %copy-start.12 = (bf16[2,512,1024]{2,1,0:T(8,128)(2,1)}, bf16[2,512,1024]{2,1,0:T(8,128)(2,1)S(1)}, u32[]{:S(2)}) copy-start(bf16[2,512,1024]{2,1,0:T(8,128)(2,1)S(1)} %get-tuple-element.185.late_ref) | copy-start | bytes 6291460
  65.9 8.9 %collective-permute-start.13 = (bf16[128,1280]{1,0:T(8,128)(2,1)S(1)}, bf16[128,1280]{1,0:T(8,128)(2,1)}, u32[]{:S(2)}, u32[]{:S(2)}) collective-permute-start(bf16[128,1280]{1,0:T(8,128)(2,1)S(1)} %collective-permute-done.6.refs_6_), channel_id=1, source_target_pairs={{0,2},{1,3},{2,0},{3,1},{4,6},{5,7},{6,4},{7,5},{8,10},{9,11},{10,... | collective-permute-start | bytes 983048 | tf_op jit(solution)/shard_map/ppermute | solution.py:376
  67.3 7.5 %collective-permute-start.14 = (bf16[128,1280]{1,0:T(8,128)(2,1)S(1)}, bf16[128,1280]{1,0:T(8,128)(2,1)S(1)}, u32[]{:S(2)}, u32[]{:S(2)}) collective-permute-start(bf16[128,1280]{1,0:T(8,128)(2,1)S(1)} %collective-permute-done.7.refs_4_), channel_id=1, source_target_pairs={{0,1},{1,0},{2,3},{3,2},{4,5},{5,4},{6,7},{7,6},{8,9},{9,8},{10,11... | collective-permute-start | bytes 983048 | tf_op jit(solution)/shard_map/ppermute | solution.py:376
  67.3 8.2 %collective-permute-start.15 = (bf16[128,1280]{1,0:T(8,128)(2,1)S(1)}, bf16[128,1280]{1,0:T(8,128)(2,1)S(1)}, u32[]{:S(2)}, u32[]{:S(2)}) collective-permute-start(bf16[128,1280]{1,0:T(8,128)(2,1)S(1)} %collective-permute-done.8.refs_5_), channel_id=1, source_target_pairs={{0,1},{1,0},{2,3},{3,2},{4,5},{5,4},{6,7},{7,6},{8,9},{9,8},{10,11... | collective-permute-start | bytes 983048 | tf_op jit(solution)/shard_map/ppermute | solution.py:376
  68.5 7.7 %collective-permute-start.16 = (bf16[128,1280]{1,0:T(8,128)(2,1)S(1)}, bf16[128,1280]{1,0:T(8,128)(2,1)S(1)}, u32[]{:S(2)}, u32[]{:S(2)}) collective-permute-start(bf16[128,1280]{1,0:T(8,128)(2,1)S(1)} %collective-permute-done.6.refs_6_), channel_id=1, source_target_pairs={{0,1},{1,0},{2,3},{3,2},{4,5},{5,4},{6,7},{7,6},{8,9},{9,8},{10,11... | collective-permute-start | bytes 983048 | tf_op jit(solution)/shard_map/ppermute | solution.py:376
  74.8 0.7 copy-start.4
  75.5 0.7 copy-start.6
  76.3 0.7 copy-start.8
  77.0 2.0 %collective-permute-start.17 = (bf16[128,1280]{1,0:T(8,128)(2,1)}, bf16[128,1280]{1,0:T(8,128)(2,1)}, u32[]{:S(2)}, u32[]{:S(2)}) collective-permute-start(bf16[128,1280]{1,0:T(8,128)(2,1)} %collective-permute-done.13.refs_7_), channel_id=1, source_target_pairs={{0,1},{1,0},{2,3},{3,2},{4,5},{5,4},{6,7},{7,6},{8,9},{9,8},{10,11... | collective-permute-start | bytes 983048 | tf_op jit(solution)/shard_map/ppermute | solution.py:376
  79.0 1.0 copy-start.3
  79.9 1.0 copy-start.5
  80.9 1.0 copy-start.7
  81.9 1.0 copy-start.9
  82.8 1.6 %copy-start.11 = (f32[512,1024]{1,0:T(8,128)S(1)}, f32[512,1024]{1,0:T(8,128)}, u32[]{:S(2)}) copy-start(f32[512,1024]{1,0:T(8,128)} %copy-done.10) | copy-start | bytes 6291460
  84.4 1.6 %copy-start.13 = (bf16[2,512,1024]{2,1,0:T(8,128)(2,1)S(1)}, bf16[2,512,1024]{2,1,0:T(8,128)(2,1)}, u32[]{:S(2)}) copy-start(bf16[2,512,1024]{2,1,0:T(8,128)(2,1)} %copy-done.12) | copy-start | bytes 6291460
  86.0 7.1 %copy-start.15 = (s32[256]{0:T(256)S(1)}, s32[256]{0:T(256)}, u32[]{:S(2)}) copy-start(s32[256]{0:T(256)} %param.11) | copy-start | bytes 3076
  (2 other events, 1.4 us)

commit v9 on v7

--- a/solution.py
+++ b/solution.py
@@ -125,21 +125,16 @@
             self.edges.append(jnp.sum(self.used * jnp.floor((reach + extra) * 0.5), axis=0, keepdims=True))
 
 
-def pack_kernel(vir_ref, occ_ref, *outs):
-    me = lax.axis_index("shell")
-    core, y = lax.rem(me, 2), lax.rem(lax.div(me, 2), 2)
+def pack_kernel(vir_ref, occ_ref, out_ref):
     here, nvir = vir_ref.shape
     width, thin = nvir // CORES, occ_ref.shape[1] // CORES
-    for dy in range(2):
-        parity = lax.rem(y + dy, 2)
-        pick = zero_one(iota((here // 2, here), 1) == 2 * iota((here // 2, here), 0) + parity).astype(BF16)
-        for dc in range(2):
-            half = lax.rem(core + dc, 2)
-            out = outs[2 * dy + dc]
-            part = vir_ref[:, pl.ds(pl.multiple_of(half * width, 128), width)]
-            out[:, :width] = jnp.dot(pick, part, preferred_element_type=F32).astype(BF16)
-            part = occ_ref[:, pl.ds(pl.multiple_of(half * thin, 128), thin)]
-            out[:, width:] = jnp.dot(pick, part, preferred_element_type=F32).astype(BF16)
+    for y in range(Y):
+        pick = zero_one(iota((here // 2, here), 1) == 2 * iota((here // 2, here), 0) + y).astype(BF16)
+        for core in range(CORES):
+            part = vir_ref[:, core * width : (core + 1) * width]
+            out_ref[2 * y + core, :, :width] = jnp.dot(pick, part, preferred_element_type=F32).astype(BF16)
+            part = occ_ref[:, core * thin : (core + 1) * thin]
+            out_ref[2 * y + core, :, width:] = jnp.dot(pick, part, preferred_element_type=F32).astype(BF16)
 
 
 def send_kernel(pairs_ref, count_ref, panels_ref, send_ref):
@@ -158,10 +153,10 @@
     send_ref[:, 2 * BLK_DEV :, :] = jnp.broadcast_to(ids[None], (n, BLK_DEV, 256)).astype(BF16)
 
 
-def pick_kernel(here, got_ref, size_ref, *refs):
-    sources, (out_ref, over_ref) = refs[:4], refs[4:]
+def pick_kernel(here, got_ref, size_ref, blocks_ref, out_ref, over_ref, me_ref):
     me = lax.axis_index("shell")
-    core, y, z = lax.rem(me, 2), lax.rem(lax.div(me, 2), 2), lax.div(me, 4)
+    me_ref[0] = me
+    y, z = lax.rem(lax.div(me, 2), 2), lax.div(me, 4)
     window = CORES * Y * here
     shell_count = size_ref.shape[1]
     shells = Shells(size_ref[...].astype(F32))
@@ -179,8 +174,8 @@
     totals = [jnp.zeros((CAP, width), F32), jnp.zeros((CAP, 128), F32)]
     columns = [slice(0, width), slice(width, width + 128)]
     extra = jnp.where(even, lists[0].extra[0], lists[0].extra[1])
-    for k, source in enumerate(sources):
-        device = 4 * z + 2 * lax.rem(y + k // 2, 2) + lax.rem(core + k % 2, 2)
+    for k in range(Y * CORES):
+        device = 4 * z + k
         row = (2 * iota((shell_count, 128), 1) + device * here + y).astype(F32)
         where = row - shells.starts
         inside = (where >= 0.0) & (where < shells.size)
@@ -193,10 +188,15 @@
             place = jnp.where(place > 0.0, place - 1.0 - base, -1.0)
             hot = zero_one(place == iota((CAP, 128), 0).astype(F32)).astype(BF16)
             totals[total] += jnp.dot(
-                hot[:, : here // 2], source[:, column], preferred_element_type=F32
+                hot[:, : here // 2], blocks_ref[k, :, column], preferred_element_type=F32
             )
     for total, column in zip(totals, columns):
         out_ref[:, column] = total.astype(BF16)
+
+
+def slot_of(window, chip):
+    rel = window ^ chip
+    return jnp.where((rel == 3) | (rel == 4), rel ^ 7, rel)
 
 
 def half_kernel(here, got_ref, size_ref, *refs):
@@ -214,7 +214,6 @@
             copies.append(pltpu.make_async_copy(pieces[at].at[:, pl.ds(width, 128)], target, sems.at[at]))
     for copy in copies:
         copy.start()
-    occ_ref[count * CAP :, :] = jnp.zeros((occ_ref.shape[0] - count * CAP, occ_ref.shape[1]), BF16)
     window = CORES * Y * here
     shell_count = size_ref.shape[1]
     got = got_ref[...].astype(F32)
@@ -251,7 +250,7 @@
         place = jnp.where(odd, spread(hot, chosen.ahead[1]), spread(hot, chosen.ahead[0]))
         place += jnp.floor(step * 0.5)
         offsets = [
-            [((w * Y + k) ^ chip).astype(F32) * CAP - lane_value(e, w) for w in range(Z)]
+            [slot_of(w * Y + k, chip).astype(F32) * CAP - lane_value(e, w) for w in range(Z)]
             for k, e in enumerate(chosen.edges)
         ]
         offset = jnp.where(odd, offsets[1][0], offsets[0][0])
@@ -276,7 +275,7 @@
         rows = slice(g * span, (g + 1) * span)
         r_hot = zero_one(place_r[rows] == lanes).astype(BF16)
         c_hot = zero_one(place_c[rows] == lanes).astype(BF16)
-        part = jnp.dot(r_hot, occ, preferred_element_type=F32).T.astype(BF16)
+        part = jnp.dot(r_hot[:, : count * CAP], occ, preferred_element_type=F32).T.astype(BF16)
         for p in range(2):
             block = blocks[p][g * 16 : (g + 1) * 16].reshape(16, 1, span)
             block = jnp.broadcast_to(block, (16, EDGE, span)).reshape(span, span)
@@ -286,7 +285,6 @@
             placed = jnp.dot(diag, c_hot, preferred_element_type=F32).astype(BF16)
             piece = jnp.dot(part, placed, preferred_element_type=F32)
             rows_p = slice(p * NOCC, (p + 1) * NOCC)
-            rows_l = slice(p * CAP, (p + 1) * CAP)
             later = jnp.dot(r_hot[:, count * CAP :].T, placed, preferred_element_type=F32)
             if g == 0:
                 half_ref[rows_p, :] = piece
@@ -295,10 +293,10 @@
                 half_ref[rows_p, :] += piece
                 late[p] += later
     for p in range(2):
-        late_ref[p * CAP : (p + 1) * CAP, :] = late[p].astype(BF16)
-
-
-def last_kernel(count, me_ref, part_ref, late_ref, *refs):
+        late_ref[p] = late[p].astype(BF16)
+
+
+def last_kernel(count, early, me_ref, part_ref, late_ref, *refs):
     pieces, (out_ref, right_ref, occ_ref, half_ref, sems) = refs[: 2 * count], refs[2 * count :]
     tile = out_ref.shape[2]
     width = right_ref.shape[2]
@@ -309,9 +307,10 @@
     def occ_copies():
         for far in range(2):
             half = lax.rem(core + far, CORES)
-            target = occ_ref.at[:, pl.ds(pl.multiple_of(half * 128, 128), 128)]
-            source = pieces[far * count + count - 1].at[:, pl.ds(width, 128)]
-            yield pltpu.make_async_copy(source, target, sems.at[2 * count + far])
+            for k in range(early, count):
+                at = far * count + k
+                target = occ_ref.at[pl.ds((k - early) * CAP, CAP), pl.ds(pl.multiple_of(half * 128, 128), 128)]
+                yield pltpu.make_async_copy(pieces[at].at[:, pl.ds(width, 128)], target, sems.at[2 * count + at])
 
     def copies(far):
         for k in range(count):
@@ -328,7 +327,7 @@
         occ = occ_ref[...].T
         for p in range(2):
             rows = slice(p * NOCC, (p + 1) * NOCC)
-            late = jnp.dot(occ, late_ref[p * CAP : (p + 1) * CAP, :], preferred_element_type=F32)
+            late = jnp.dot(occ, late_ref[p], preferred_element_type=F32)
             half_ref[rows, :] = (part_ref[rows, :] + late).astype(BF16)
 
     for far in range(2):
@@ -366,22 +365,23 @@
     width = nvir // CORES
     packed = width + NOCC // CORES
     room = Z * Y * CAP
-    me = lax.axis_index("shell")
     size_row = shell_size.reshape(1, -1)
 
     def swap(array, bit):
         return lax.ppermute(array, "shell", [(i, i ^ bit) for i in range(n)])
 
-    keep, to_core, to_y, to_both = pl.pallas_call(
+    blocks = pl.pallas_call(
         pack_kernel,
-        out_shape=[shape(here // 2, packed)] * 4,
+        out_shape=shape(Y * CORES, here // 2, packed),
         in_specs=[VMEM] * 2,
-        out_specs=[VMEM] * 4,
+        out_specs=VMEM,
         compiler_params=params(12),
         cost_estimate=cost(3e8, 3e6),
         name="pack_rows",
     )(vir_coef, occ_coef)
-    to_y, to_both, to_core = swap(to_y, 2), swap(to_both, 3), swap(to_core, 1)
+    blocks, panels = lax.optimization_barrier((blocks, panels))
+    planes = [[Y * CORES * z + k for k in range(Y * CORES)] for z in range(Z)]
+    blocks = lax.all_to_all(blocks, "shell", split_axis=0, concat_axis=0, axis_index_groups=planes, tiled=True)
     send = pl.pallas_call(
         send_kernel,
         out_shape=shape(n, 3 * BLK_DEV, EDGE * EDGE),
@@ -393,74 +393,71 @@
     )(block_pairs.T, block_count.reshape(1, 1), panels)
     got = lax.all_to_all(send, "shell", split_axis=0, concat_axis=0, tiled=True)
 
-    mine, over = pl.pallas_call(
+    mine, over, me = pl.pallas_call(
         functools.partial(pick_kernel, here),
-        out_shape=(shape(CAP, packed), shape(1, dtype=jnp.int32)),
-        in_specs=[VMEM] * 6,
-        out_specs=(VMEM, SMEM),
+        out_shape=(shape(CAP, packed), shape(1, dtype=jnp.int32), shape(1, dtype=jnp.int32)),
+        in_specs=[VMEM] * 3,
+        out_specs=(VMEM, SMEM, SMEM),
         compiler_params=params(12),
         cost_estimate=cost(3e8, 2e6),
         name="pick_rows",
-    )(got, size_row, keep, to_core, to_y, to_both)
+    )(got, size_row, blocks)
 
     beside, across, mine_y = swap(mine, 4), swap(mine, 8), swap(mine, 2)
-    beside, mine_y = lax.optimization_barrier((beside, mine_y))
-
-    beside_y = swap(beside, 2)
-    far = [swap(mine, 1), swap(mine_y, 1), swap(beside, 1)]
-    across, beside_y, *far = lax.optimization_barrier((across, beside_y, *far))
-
-    corner, across_y = swap(across, 4), swap(across, 2)
-    far += [swap(beside_y, 1), swap(across, 1)]
-    corner, across_y, *far = lax.optimization_barrier((corner, across_y, *far))
-
-    corner_y = swap(corner, 2)
-    far += [swap(across_y, 1), swap(corner, 1)]
-    near = [mine, mine_y, beside, beside_y, across, across_y, corner]
-    count = len(near)
+    beside, across, mine_y = lax.optimization_barrier((beside, across, mine_y))
+
+    corner, beside_y, across_y = swap(across, 4), swap(beside, 2), swap(across, 2)
+    near = [mine, mine_y, beside, across]
+    far = [swap(piece, 1) for piece in near]
+    early = len(near)
     half, late = pl.pallas_call(
         functools.partial(half_kernel, here),
-        out_shape=(shape(2 * NOCC, room, dtype=F32), shape(2 * CAP, room)),
+        out_shape=(shape(2 * NOCC, room, dtype=F32), shape(2, room - early * CAP, room)),
         grid=(1,),
-        in_specs=[VMEM] * 2 + [ANY] * (2 * count),
+        in_specs=[VMEM] * 2 + [ANY] * (2 * early),
         out_specs=(
             pl.BlockSpec((2 * NOCC, room), lambda i: (0, 0)),
-            pl.BlockSpec((2 * CAP, room), lambda i: (0, 0)),
+            pl.BlockSpec((2, room - early * CAP, room), lambda i: (0, 0, 0)),
         ),
-        scratch_shapes=[pltpu.VMEM((room, NOCC), BF16), pltpu.SemaphoreType.DMA((2 * count,))],
-        compiler_params=params(24),
-        cost_estimate=cost(4e9, 8e6),
+        scratch_shapes=[pltpu.VMEM((early * CAP, NOCC), BF16), pltpu.SemaphoreType.DMA((2 * early,))],
+        compiler_params=params(28),
+        cost_estimate=cost(7e9, 1),
         name="half_transform",
     )(got, size_row, *near, *far)
-    corner_y, half, late = lax.optimization_barrier((corner_y, half, late))
+    corner, half, late = lax.optimization_barrier((corner, half, late))
+
+    corner_y = swap(corner, 2)
+    near += [beside_y, across_y, corner]
+    far += [swap(piece, 1) for piece in near[early:]]
+    corner_y, *far = lax.optimization_barrier((corner_y, *far))
     near.append(corner_y)
     far.append(swap(corner_y, 1))
 
     count = len(near)
     tile = width // 3
     out = pl.pallas_call(
-        functools.partial(last_kernel, count),
+        functools.partial(last_kernel, count, early),
         out_shape=shape(2, NOCC, nvir),
         grid_spec=pltpu.PrefetchScalarGridSpec(
             num_scalar_prefetch=1,
             grid=(nvir // tile,),
             in_specs=[
                 pl.BlockSpec((2 * NOCC, room), lambda j, o: (0, 0)),
-                pl.BlockSpec((2 * CAP, room), lambda j, o: (0, 0)),
+                pl.BlockSpec((2, room - early * CAP, room), lambda j, o: (0, 0, 0)),
             ]
             + [ANY] * (2 * count),
             out_specs=pl.BlockSpec((2, NOCC, tile), lambda j, o: (0, 0, (j + 3 * (o[0] % 2)) % 6)),
             scratch_shapes=[
                 pltpu.VMEM((CORES, room, width), BF16),
-                pltpu.VMEM((CAP, NOCC), BF16),
+                pltpu.VMEM((room - early * CAP, NOCC), BF16),
                 pltpu.VMEM((2 * NOCC, room), BF16),
-                pltpu.SemaphoreType.DMA((2 * count + 2,)),
+                pltpu.SemaphoreType.DMA((4 * count,)),
             ],
         ),
-        compiler_params=params(24),
-        cost_estimate=cost(3e9, 1e7),
+        compiler_params=params(28),
+        cost_estimate=cost(2e10, 1),
         name="last_product",
-    )(me.reshape(1), half, late, *near, *far)
+    )(me, half, late, *near, *far)
     return out, over[0], got
 
 

time: 102 us -> 103 us (level)
  blocking collectives: 0 us -> 30.5 us
  starting transfers between devices: 19.5 us -> 5.47 us
  local copies, waits for them, and re-layouts: 10.3 us -> 1.58 us
  waiting for transfers between devices: 38 us -> 30.4 us
    all_to_all x0 -> x2, blocking collectives: none -> 30.5 us  [the longest x1 16.2 us: short_way(): got = lax.all_to_all(send, 'shell', split_axis=0, concat_axis=0, tiled=True)]
    unnamed x30 -> x6, local copies, waits for them, and re-layouts: 10.3 us -> 1.58 us
    ppermute x18 -> x15, waiting for transfers between devices: 38 us -> 30.4 us  [swap(): return lax.ppermute(array, 'shell', [(i, i ^ bit) for i in range(n)])]
    all_to_all x1 -> x0, starting transfers between devices: 7.39 us -> none  [short_way(): got = lax.all_to_all(send, 'shell', split_axis=0, concat_axis=0, tiled=True)]
    ppermute x18 -> x15, starting transfers between devices: 12.1 us -> 5.47 us  [swap(): return lax.ppermute(array, 'shell', [(i, i ^ bit) for i in range(n)])]
  transfers between devices with their start and end apart: 19 -> 15, of which waited for: 10 -> 6; matrix products, arithmetic and copies ran while one was open for 0% -> 0% of each run, Pallas kernels for 9% -> 8%
where the time goes in v9:
time: 103 us; the launch traced here: 102 us
  blocking collectives  30.5 us (30%)
  waiting for transfers between devices  30.4 us (30%)
  Pallas kernels  19.4 us (19%)
  between operations  14.1 us (14%)
  starting transfers between devices  5.47 us (5%)
  local copies, waits for them, and re-layouts  1.58 us (2%)
    ppermute x15, waiting for transfers between devices, swap(): return lax.ppermute(array, 'shell', [(i, i ^ bit) for i in range(n)])  30.4 us
    all_to_all x1, blocking collectives, short_way(): got = lax.all_to_all(send, 'shell', split_axis=0, concat_axis=0, tiled=True)  16.2 us
    all_to_all x1, blocking collectives, short_way(): lax.all_to_all(blocks, 'shell', split_axis=0, concat_axis=0, axis_index_g...  14.4 us
    pallas_call x1, Pallas kernels, short_way(): pl.pallas_call(functools.partial(half_kernel, here), out_shape=(shape(2 *...  8.16 us
    pallas_call x1, Pallas kernels, short_way(): pl.pallas_call(functools.partial(last_kernel, count, early), out_shape=sh...  7.47 us
    ppermute x15, starting transfers between devices, swap(): return lax.ppermute(array, 'shell', [(i, i ^ bit) for i in range(n)])  5.47 us
    pallas_call x1, Pallas kernels, short_way(): pl.pallas_call(functools.partial(pick_kernel, here), out_shape=(shape(CAP...  2.07 us
  transfers between devices with their start and end apart: 15, of which 6 were waited for; matrix products, arithmetic and copies ran while one was open for 0% of the time, Pallas kernels for 8%

profile of v9, /device:TPU:0, one launch (start us, length us, event | category | flops | bytes accessed | tf_op | source)
XLA Modules:
  0.0 102.4 jit_solution(3254945960536926314)
XLA Ops:
  7.2 1.5 %pack_rows.1 = bf16[4,80,1280]{2,1,0:T(8,128)(2,1)S(1)} custom-call(bf16[160,2304]{1,0:T(8,128)(2,1)} %vir_ref.1, bf16[160,256]{1,0:T(8,128)(2,1)} %occ_ref.1), custom_call_target="tpu_custom_call" | custom-call | flops 300000000 | bytes 3000000 | tf_op jit(solution)/shard_map/pack_rows/pallas_call | solution.py:373
  8.7 0.0 copy-start
  8.8 0.9 copy-done
  9.7 0.7 copy-done.1
  10.3 0.2 pack_panels.1
  10.5 16.2 %all_to_all.10.got_ref = bf16[16,24,256]{2,1,0:T(8,128)(2,1)S(1)} all-to-all(bf16[16,24,256]{2,1,0:T(8,128)(2,1)S(1)} %pack_panels.1), channel_id=1, replica_groups=mesh['groups'=2,'shell'=16] {'shell'}, dimensions={0} | all-to-all | bytes 393216 | tf_op jit(solution)/shard_map/all_to_all | solution.py:394
  26.7 14.4 %all_to_all.11.blocks_ref = bf16[4,80,1280]{2,1,0:T(8,128)(2,1)S(1)} all-to-all(bf16[4,80,1280]{2,1,0:T(8,128)(2,1)S(1)} %pack_rows.1), channel_id=1, replica_groups={{0,1,2,3},{4,5,6,7},{8,9,10,11},{12,13,14,15},{16,17,18,19},{20,21,22,2..., dimensions={0} | all-to-all | bytes 1638400 | tf_op jit(solution)/shard_map/all_to_all | solution.py:384
  41.0 2.1 %pick_rows.1 = (bf16[128,1280]{1,0:T(8,128)(2,1)S(1)}, s32[1]{0:T(128)}, s32[1]{0:T(128)}) custom-call(bf16[16,24,256]{2,1,0:T(8,128)(2,1)S(1)} %all_to_all.10.got_ref, s32[1,256]{1,0:T(1,128)} %bitcast.74, bf16[4,80,1280]{2,1,0:T(8,128)(2,1)S(1)} %all_to_all.11.blocks_ref), custom_call_target="tpu_custom_call" | custom-call | flops 300000000 | bytes 2000000 | tf_op jit(solution)/shard_map/pick_rows/pallas_call | solution.py:396
  43.1 0.1 collective-permute-start
  43.2 1.4 %collective-permute-start.1 = (bf16[128,1280]{1,0:T(8,128)(2,1)S(1)}, bf16[128,1280]{1,0:T(8,128)(2,1)S(1)}, u32[]{:S(2)}, u32[]{:S(2)}) collective-permute-start(bf16[128,1280]{1,0:T(8,128)(2,1)S(1)} %get-tuple-element.126.refs_0_), channel_id=1, source_target_pairs={{0,8},{1,9},{2,10},{3,11},{4,12},{5,13},{6,14},{7,15},{8,0},{9,1},... | collective-permute-start | bytes 983048 | tf_op jit(solution)/shard_map/ppermute | solution.py:371
  44.6 0.4 collective-permute-start.2
  45.0 0.0 collective-permute-start.4
  45.0 14.0 %collective-permute-done.refs_2_ = bf16[128,1280]{1,0:T(8,128)(2,1)S(1)} collective-permute-done((bf16[128,1280]{1,0:T(8,128)(2,1)S(1)}, bf16[128,1280]{1,0:T(8,128)(2,1)S(1)}, u32[]{:S(2)}, u32[]{:S(2)}) %collective-permute-start) | collective-permute-done | bytes 327712 | tf_op jit(solution)/shard_map/ppermute | solution.py:371
  59.0 1.8 %collective-permute-done.1.refs_3_ = bf16[128,1280]{1,0:T(8,128)(2,1)S(1)} collective-permute-done((bf16[128,1280]{1,0:T(8,128)(2,1)S(1)}, bf16[128,1280]{1,0:T(8,128)(2,1)S(1)}, u32[]{:S(2)}, u32[]{:S(2)}) %collective-permute-start.1) | collective-permute-done | bytes 327712 | tf_op jit(solution)/shard_map/ppermute | solution.py:371
  60.8 0.0 collective-permute-done.2.refs_1_
  60.8 0.0 collective-permute-start.5
  60.8 0.5 collective-permute-start.6
  61.3 0.0 collective-permute-start.7
  61.3 0.4 collective-permute-start.8
  61.8 0.7 collective-permute-done.5.refs_5_.refs_9_
  62.4 1.0 collective-permute-start.9
  63.4 0.0 collective-permute-done.6.refs_6_.refs_10_
  63.4 0.0 collective-permute-done.7.refs_7_.refs_11_
  63.4 8.2 %half_transform.1 = (f32[512,1024]{1,0:T(8,128)S(1)}, bf16[2,512,1024]{2,1,0:T(8,128)(2,1)S(1)}) custom-call(bf16[16,24,256]{2,1,0:T(8,128)(2,1)S(1)} %all_to_all.10.got_ref, s32[1,256]{1,0:T(1,128)S(1)} %bitcast.75, bf16[128,1280]{1,0:T(8,128)(2,1)S(1)} %get-tuple-element.126.refs_0_, bf16[128,1280]{1,0:T(8,128)(2,1)S(1)} %collective-permute-done.2.refs_1_, ...), custom_call_target="tpu_custom_call" | custom-call | flops 7000000000 | bytes 1 | tf_op jit(solution)/shard_map/half_transform/pallas_call | solution.py:413
  71.6 1.1 %collective-permute-start.10 = (bf16[128,1280]{1,0:T(8,128)(2,1)S(1)}, bf16[128,1280]{1,0:T(8,128)(2,1)S(1)}, u32[]{:S(2)}, u32[]{:S(2)}) collective-permute-start(bf16[128,1280]{1,0:T(8,128)(2,1)S(1)} %collective-permute-done.3.refs_6_), channel_id=1, source_target_pairs={{0,2},{1,3},{2,0},{3,1},{4,6},{5,7},{6,4},{7,5},{8,10},{9,11},{10,... | collective-permute-start | bytes 983048 | tf_op jit(solution)/shard_map/ppermute | solution.py:371
  72.7 6.2 %collective-permute-done.9.refs_5_ = bf16[128,1280]{1,0:T(8,128)(2,1)S(1)} collective-permute-done((bf16[128,1280]{1,0:T(8,128)(2,1)S(1)}, bf16[128,1280]{1,0:T(8,128)(2,1)S(1)}, u32[]{:S(2)}, u32[]{:S(2)}) %collective-permute-start.9) | collective-permute-done | bytes 327712 | tf_op jit(solution)/shard_map/ppermute | solution.py:371
  78.9 0.5 collective-permute-start.13
  79.4 6.0 %collective-permute-done.10.refs_7_ = bf16[128,1280]{1,0:T(8,128)(2,1)S(1)} collective-permute-done((bf16[128,1280]{1,0:T(8,128)(2,1)S(1)}, bf16[128,1280]{1,0:T(8,128)(2,1)S(1)}, u32[]{:S(2)}, u32[]{:S(2)}) %collective-permute-start.10) | collective-permute-done | bytes 327712 | tf_op jit(solution)/shard_map/ppermute | solution.py:371
  85.5 0.1 collective-permute-start.14
  85.6 1.6 %collective-permute-done.14.refs_15_ = bf16[128,1280]{1,0:T(8,128)(2,1)S(1)} collective-permute-done((bf16[128,1280]{1,0:T(8,128)(2,1)S(1)}, bf16[128,1280]{1,0:T(8,128)(2,1)S(1)}, u32[]{:S(2)}, u32[]{:S(2)}) %collective-permute-start.14) | collective-permute-done | bytes 327712 | tf_op jit(solution)/shard_map/ppermute | solution.py:371
  87.2 7.5 %last_product.1 = bf16[2,256,2304]{2,1,0:T(8,128)(2,1)} custom-call(s32[1]{0:T(128)} %get-tuple-element.125.me_ref, f32[512,1024]{1,0:T(8,128)S(1)} %get-tuple-element.132.part_ref, bf16[2,512,1024]{2,1,0:T(8,128)(2,1)S(1)} %get-tuple-element.133.late_ref, bf16[128,1280]{1,0:T(8,128)(2,1)S(1)} %get-tuple-element.126.refs_0_, ...), custom_call_target="tpu_custom_call" | custom-call | flops 20000000000 | bytes 1 | tf_op jit(solution)/shard_map/last_product/pallas_call | solution.py:438
  94.7 0.9 while.16
  (12 shorter events, 0.0 us)
Async XLA Ops:
  6.5 56.9 %copy-start.3 = (s32[256]{0:T(256)S(1)}, s32[256]{0:T(256)}, u32[]{:S(2)}) copy-start(s32[256]{0:T(256)} %param.11) | copy-start | bytes 3076
  8.7 0.9 copy-start
  9.6 0.7 copy-start.1
  43.1 15.9 %collective-permute-start = (bf16[128,1280]{1,0:T(8,128)(2,1)S(1)}, bf16[128,1280]{1,0:T(8,128)(2,1)S(1)}, u32[]{:S(2)}, u32[]{:S(2)}) collective-permute-start(bf16[128,1280]{1,0:T(8,128)(2,1)S(1)} %get-tuple-element.126.refs_0_), channel_id=1, source_target_pairs={{0,4},{1,5},{2,6},{3,7},{4,0},{5,1},{6,2},{7,3},{8,12},{9,13},{10,... | collective-permute-start | bytes 983048 | tf_op jit(solution)/shard_map/ppermute | solution.py:371
  43.2 17.6 %collective-permute-start.1 = (bf16[128,1280]{1,0:T(8,128)(2,1)S(1)}, bf16[128,1280]{1,0:T(8,128)(2,1)S(1)}, u32[]{:S(2)}, u32[]{:S(2)}) collective-permute-start(bf16[128,1280]{1,0:T(8,128)(2,1)S(1)} %get-tuple-element.126.refs_0_), channel_id=1, source_target_pairs={{0,8},{1,9},{2,10},{3,11},{4,12},{5,13},{6,14},{7,15},{8,0},{9,1},... | collective-permute-start | bytes 983048 | tf_op jit(solution)/shard_map/ppermute | solution.py:371
  44.6 16.2 %collective-permute-start.2 = (bf16[128,1280]{1,0:T(8,128)(2,1)S(1)}, bf16[128,1280]{1,0:T(8,128)(2,1)S(1)}, u32[]{:S(2)}, u32[]{:S(2)}) collective-permute-start(bf16[128,1280]{1,0:T(8,128)(2,1)S(1)} %get-tuple-element.126.refs_0_), channel_id=1, source_target_pairs={{0,2},{1,3},{2,0},{3,1},{4,6},{5,7},{6,4},{7,5},{8,10},{9,11},{10,... | collective-permute-start | bytes 983048 | tf_op jit(solution)/shard_map/ppermute | solution.py:371
  45.0 16.4 %collective-permute-start.4 = (bf16[128,1280]{1,0:T(8,128)(2,1)S(1)}, bf16[128,1280]{1,0:T(8,128)(2,1)S(1)}, u32[]{:S(2)}, u32[]{:S(2)}) collective-permute-start(bf16[128,1280]{1,0:T(8,128)(2,1)S(1)} %get-tuple-element.126.refs_0_), channel_id=1, source_target_pairs={{0,1},{1,0},{2,3},{3,2},{4,5},{5,4},{6,7},{7,6},{8,9},{9,8},{10,11... | collective-permute-start | bytes 983048 | tf_op jit(solution)/shard_map/ppermute | solution.py:371
  60.8 1.6 %collective-permute-start.5 = (bf16[128,1280]{1,0:T(8,128)(2,1)S(1)}, bf16[128,1280]{1,0:T(8,128)(2,1)S(1)}, u32[]{:S(2)}, u32[]{:S(2)}) collective-permute-start(bf16[128,1280]{1,0:T(8,128)(2,1)S(1)} %collective-permute-done.2.refs_1_), channel_id=1, source_target_pairs={{0,1},{1,0},{2,3},{3,2},{4,5},{5,4},{6,7},{7,6},{8,9},{9,8},{10,11... | collective-permute-start | bytes 983048 | tf_op jit(solution)/shard_map/ppermute | solution.py:371
  60.8 2.6 %collective-permute-start.6 = (bf16[128,1280]{1,0:T(8,128)(2,1)S(1)}, bf16[128,1280]{1,0:T(8,128)(2,1)S(1)}, u32[]{:S(2)}, u32[]{:S(2)}) collective-permute-start(bf16[128,1280]{1,0:T(8,128)(2,1)S(1)} %collective-permute-done.refs_2_), channel_id=1, source_target_pairs={{0,1},{1,0},{2,3},{3,2},{4,5},{5,4},{6,7},{7,6},{8,9},{9,8},{10,11... | collective-permute-start | bytes 983048 | tf_op jit(solution)/shard_map/ppermute | solution.py:371
  61.3 2.1 %collective-permute-start.7 = (bf16[128,1280]{1,0:T(8,128)(2,1)S(1)}, bf16[128,1280]{1,0:T(8,128)(2,1)S(1)}, u32[]{:S(2)}, u32[]{:S(2)}) collective-permute-start(bf16[128,1280]{1,0:T(8,128)(2,1)S(1)} %collective-permute-done.1.refs_3_), channel_id=1, source_target_pairs={{0,1},{1,0},{2,3},{3,2},{4,5},{5,4},{6,7},{7,6},{8,9},{9,8},{10,11... | collective-permute-start | bytes 983048 | tf_op jit(solution)/shard_map/ppermute | solution.py:371
  61.3 10.3 %collective-permute-start.3 = (bf16[128,1280]{1,0:T(8,128)(2,1)S(1)}, bf16[128,1280]{1,0:T(8,128)(2,1)S(1)}, u32[]{:S(2)}, u32[]{:S(2)}) collective-permute-start(bf16[128,1280]{1,0:T(8,128)(2,1)S(1)} %collective-permute-done.1.refs_3_), channel_id=1, source_target_pairs={{0,4},{1,5},{2,6},{3,7},{4,0},{5,1},{6,2},{7,3},{8,12},{9,13},{10,... | collective-permute-start | bytes 983048 | tf_op jit(solution)/shard_map/ppermute | solution.py:371
  61.3 11.4 %collective-permute-start.8 = (bf16[128,1280]{1,0:T(8,128)(2,1)S(1)}, bf16[128,1280]{1,0:T(8,128)(2,1)S(1)}, u32[]{:S(2)}, u32[]{:S(2)}) collective-permute-start(bf16[128,1280]{1,0:T(8,128)(2,1)S(1)} %collective-permute-done.refs_2_), channel_id=1, source_target_pairs={{0,2},{1,3},{2,0},{3,1},{4,6},{5,7},{6,4},{7,5},{8,10},{9,11},{10,... | collective-permute-start | bytes 983048 | tf_op jit(solution)/shard_map/ppermute | solution.py:371
  62.4 16.5 %collective-permute-start.9 = (bf16[128,1280]{1,0:T(8,128)(2,1)S(1)}, bf16[128,1280]{1,0:T(8,128)(2,1)S(1)}, u32[]{:S(2)}, u32[]{:S(2)}) collective-permute-start(bf16[128,1280]{1,0:T(8,128)(2,1)S(1)} %collective-permute-done.1.refs_3_), channel_id=1, source_target_pairs={{0,2},{1,3},{2,0},{3,1},{4,6},{5,7},{6,4},{7,5},{8,10},{9,11},{10,... | collective-permute-start | bytes 983048 | tf_op jit(solution)/shard_map/ppermute | solution.py:371
  71.6 13.9 %collective-permute-start.10 = (bf16[128,1280]{1,0:T(8,128)(2,1)S(1)}, bf16[128,1280]{1,0:T(8,128)(2,1)S(1)}, u32[]{:S(2)}, u32[]{:S(2)}) collective-permute-start(bf16[128,1280]{1,0:T(8,128)(2,1)S(1)} %collective-permute-done.3.refs_6_), channel_id=1, source_target_pairs={{0,2},{1,3},{2,0},{3,1},{4,6},{5,7},{6,4},{7,5},{8,10},{9,11},{10,... | collective-permute-start | bytes 983048 | tf_op jit(solution)/shard_map/ppermute | solution.py:371
  72.7 12.8 %collective-permute-start.11 = (bf16[128,1280]{1,0:T(8,128)(2,1)S(1)}, bf16[128,1280]{1,0:T(8,128)(2,1)S(1)}, u32[]{:S(2)}, u32[]{:S(2)}) collective-permute-start(bf16[128,1280]{1,0:T(8,128)(2,1)S(1)} %collective-permute-done.8.refs_4_), channel_id=1, source_target_pairs={{0,1},{1,0},{2,3},{3,2},{4,5},{5,4},{6,7},{7,6},{8,9},{9,8},{10,11... | collective-permute-start | bytes 983048 | tf_op jit(solution)/shard_map/ppermute | solution.py:371
  78.9 6.6 %collective-permute-start.12 = (bf16[128,1280]{1,0:T(8,128)(2,1)S(1)}, bf16[128,1280]{1,0:T(8,128)(2,1)S(1)}, u32[]{:S(2)}, u32[]{:S(2)}) collective-permute-start(bf16[128,1280]{1,0:T(8,128)(2,1)S(1)} %collective-permute-done.9.refs_5_), channel_id=1, source_target_pairs={{0,1},{1,0},{2,3},{3,2},{4,5},{5,4},{6,7},{7,6},{8,9},{9,8},{10,11... | collective-permute-start | bytes 983048 | tf_op jit(solution)/shard_map/ppermute | solution.py:371
  78.9 6.6 %collective-permute-start.13 = (bf16[128,1280]{1,0:T(8,128)(2,1)S(1)}, bf16[128,1280]{1,0:T(8,128)(2,1)S(1)}, u32[]{:S(2)}, u32[]{:S(2)}) collective-permute-start(bf16[128,1280]{1,0:T(8,128)(2,1)S(1)} %collective-permute-done.3.refs_6_), channel_id=1, source_target_pairs={{0,1},{1,0},{2,3},{3,2},{4,5},{5,4},{6,7},{7,6},{8,9},{9,8},{10,11... | collective-permute-start | bytes 983048 | tf_op jit(solution)/shard_map/ppermute | solution.py:371
  85.5 1.7 %collective-permute-start.14 = (bf16[128,1280]{1,0:T(8,128)(2,1)S(1)}, bf16[128,1280]{1,0:T(8,128)(2,1)S(1)}, u32[]{:S(2)}, u32[]{:S(2)}) collective-permute-start(bf16[128,1280]{1,0:T(8,128)(2,1)S(1)} %collective-permute-done.10.refs_7_), channel_id=1, source_target_pairs={{0,1},{1,0},{2,3},{3,2},{4,5},{5,4},{6,7},{7,6},{8,9},{9,8},{10,11... | collective-permute-start | bytes 983048 | tf_op jit(solution)/shard_map/ppermute | solution.py:371

commit v10 on v8

--- a/solution.py
+++ b/solution.py
@@ -158,8 +158,9 @@
 
 
 def pick_kernel(here, code_ref, size_ref, *refs):
-    sources, (out_ref, over_ref) = refs[:4], refs[4:]
+    sources, (out_ref, over_ref, me_ref) = refs[:4], refs[4:]
     me = lax.axis_index("shell")
+    me_ref[0] = me
     core, y, z = lax.rem(me, 2), lax.rem(lax.div(me, 2), 2), lax.div(me, 4)
     window = CORES * Y * here
     shell_count = size_ref.shape[1]
@@ -198,9 +199,30 @@
         out_ref[:, column] = total.astype(BF16)
 
 
+def inner_chip(chip):
+    z = lax.div(chip, Y)
+    return (z == 1) | (z == 2)
+
+
 def slot_of(window, chip):
-    rel = window ^ chip
-    return jnp.where((rel == 3) | (rel == 4), rel ^ 7, rel)
+    slot = window ^ chip
+    return jnp.where(inner_chip(chip) & (slot >= 2 * Y), slot ^ Y, slot)
+
+
+def choose_kernel(me_ref, inner_ref, outer_ref, out_ref, sem):
+    inner = inner_chip(lax.div(me_ref[0], CORES))
+
+    @pl.when(inner)
+    def _():
+        copy = pltpu.make_async_copy(inner_ref, out_ref, sem)
+        copy.start()
+        copy.wait()
+
+    @pl.when(jnp.logical_not(inner))
+    def _():
+        copy = pltpu.make_async_copy(outer_ref, out_ref, sem)
+        copy.start()
+        copy.wait()
 
 
 def half_kernel(here, code_ref, got_ref, size_ref, *refs):
@@ -369,7 +391,6 @@
     width = nvir // CORES
     packed = width + NOCC // CORES
     room = Z * Y * CAP
-    me = lax.axis_index("shell")
     size_row = shell_size.reshape(1, -1)
 
     def swap(array, bit):
@@ -396,17 +417,34 @@
     )(block_pairs.T, block_count.reshape(1, 1))
     code = lax.all_to_all(code, "shell", split_axis=0, concat_axis=0, tiled=True)
 
-    mine, over = pl.pallas_call(
+    mine, over, me = pl.pallas_call(
         functools.partial(pick_kernel, here),
-        out_shape=(shape(CAP, packed), shape(1, dtype=jnp.int32)),
+        out_shape=(shape(CAP, packed), shape(1, dtype=jnp.int32), shape(1, dtype=jnp.int32)),
         in_specs=[VMEM] * 6,
-        out_specs=(VMEM, SMEM),
+        out_specs=(VMEM, SMEM, SMEM),
         compiler_params=params(12),
         cost_estimate=cost(3e8, 2e6),
         name="pick_rows",
     )(code, size_row, keep, to_core, to_y, to_both)
 
-    beside, across, mine_y = swap(mine, 4), swap(mine, 8), swap(mine, 2)
+    ends, middle, outward = [(0, 1), (1, 0), (2, 3), (3, 2)], [(1, 2), (2, 1)], [(1, 0), (2, 3)]
+
+    def hop(array, steps):
+        return lax.ppermute(array, "shell", [(4 * a + k, 4 * b + k) for a, b in steps for k in range(4)])
+
+    def choose(inner, outer):
+        return pl.pallas_call(
+            choose_kernel,
+            out_shape=shape(*inner.shape),
+            in_specs=[SMEM, ANY, ANY],
+            out_specs=ANY,
+            scratch_shapes=[pltpu.SemaphoreType.DMA],
+            compiler_params=params(4),
+            cost_estimate=cost(1, 1),
+            name="choose_piece",
+        )(me, inner, outer)
+
+    mine_y, beside, across = swap(mine, 2), hop(mine, ends), hop(mine, middle)
     panels, _ = lax.optimization_barrier((panels, mine))
     send = pl.pallas_call(
         turn_kernel,
@@ -418,11 +456,20 @@
         name="turn_panels",
     )(panels)
     got = lax.all_to_all(send, "shell", split_axis=0, concat_axis=0, tiled=True)
-    beside, across, mine_y, got = lax.optimization_barrier((beside, across, mine_y, got))
-
-    corner, beside_y, across_y = swap(across, 4), swap(beside, 2), swap(across, 2)
-    near = [mine, mine_y, beside, across]
-    far = [swap(piece, 1) for piece in near]
+    mine_y, beside, across, got = lax.optimization_barrier((mine_y, beside, across, got))
+
+    beside_y, across_out, corner = swap(beside, 2), hop(across, outward), hop(beside, middle)
+    far = [swap(piece, 1) for piece in (mine, mine_y, beside)]
+    beside_y, across_out, corner, *far = lax.optimization_barrier((beside_y, across_out, corner, *far))
+
+    across = choose(across, across_out)
+    across_y, corner_out = swap(across, 2), hop(corner, outward)
+    far += [swap(piece, 1) for piece in (beside_y, across)]
+    across_y, corner_out, *far = lax.optimization_barrier((across_y, corner_out, *far))
+
+    corner = choose(corner, corner_out)
+    corner_y = swap(corner, 2)
+    near = [mine, mine_y, beside, beside_y, across]
     early = len(near)
     half, late = pl.pallas_call(
         functools.partial(half_kernel, here),
@@ -438,12 +485,9 @@
         cost_estimate=cost(7e9, 1),
         name="half_transform",
     )(code, got, size_row, *near, *far)
-    corner, beside_y, across_y, half, late = lax.optimization_barrier((corner, beside_y, across_y, half, late))
-
-    corner_y = swap(corner, 2)
-    near += [beside_y, across_y, corner]
+    near += [across_y, corner]
     far += [swap(piece, 1) for piece in near[early:]]
-    corner_y, *far = lax.optimization_barrier((corner_y, *far))
+    corner_y, half, late, *far = lax.optimization_barrier((corner_y, half, late, *far))
     near.append(corner_y)
     far.append(swap(corner_y, 1))
 
@@ -471,7 +515,7 @@
         compiler_params=params(28),
         cost_estimate=cost(2e10, 1),
         name="last_product",
-    )(me.reshape(1), half, late, *near, *far)
+    )(me, half, late, *near, *far)
     return out, over[0], code, got
 
 

time: 101 us -> 96.5 us (0.955)
  blocking collectives: 12.8 us -> 27.4 us
  local copies, waits for them, and re-layouts: 14.2 us -> 1.58 us
  starting transfers between devices: 16.4 us -> 12.5 us
  waiting for transfers between devices: 21.9 us -> 18.9 us
    all_to_all x0 -> x1, blocking collectives: none -> 14.6 us  [short_way(): got = lax.all_to_all(send, 'shell', split_axis=0, concat_axis=0, tiled=True)]
    unnamed x30 -> x6, local copies, waits for them, and re-layouts: 14.2 us -> 1.58 us
    all_to_all x1 -> x0, waiting for transfers between devices: 10.5 us -> none  [short_way(): got = lax.all_to_all(send, 'shell', split_axis=0, concat_axis=0, tiled=True)]
    ppermute x0 -> x5, waiting for transfers between devices: none -> 5.72 us  [hop(): lax.ppermute(array, 'shell', [(4 * a + k, 4 * b + k) for a, b in steps fo...]
    all_to_all x1 -> x0, starting transfers between devices: 4.95 us -> none  [short_way(): got = lax.all_to_all(send, 'shell', split_axis=0, concat_axis=0, tiled=True)]
    ppermute x0 -> x5, starting transfers between devices: none -> 4.58 us  [hop(): lax.ppermute(array, 'shell', [(4 * a + k, 4 * b + k) for a, b in steps fo...]
    ppermute x18 -> x15, starting transfers between devices: 11.5 us -> 7.87 us  [swap(): return lax.ppermute(array, 'shell', [(i, i ^ bit) for i in range(n)])]
    ppermute x18 -> x15, waiting for transfers between devices: 11.4 us -> 13.1 us  [swap(): return lax.ppermute(array, 'shell', [(i, i ^ bit) for i in range(n)])]
  transfers between devices with their start and end apart: 19 -> 20, of which waited for: 4 -> 5; matrix products, arithmetic and copies ran while one was open for 0% -> 0% of each run, Pallas kernels for 10% -> 9%
where the time goes in v10:
time: 96.5 us; the launch traced here: 96.2 us
  blocking collectives  27.4 us (28%)
  Pallas kernels  21.1 us (22%)
  waiting for transfers between devices  18.9 us (20%)
  between operations  14.2 us (15%)
  starting transfers between devices  12.5 us (13%)
  local copies, waits for them, and re-layouts  1.58 us (2%)
    all_to_all x1, blocking collectives, short_way(): got = lax.all_to_all(send, 'shell', split_axis=0, concat_axis=0, tiled=True)  14.6 us
    ppermute x15, waiting for transfers between devices, swap(): return lax.ppermute(array, 'shell', [(i, i ^ bit) for i in range(n)])  13.1 us
    all_to_all x1, blocking collectives, short_way(): lax.all_to_all(code, 'shell', split_axis=0, concat_axis=0, tiled=True)  12.8 us
    pallas_call x1, Pallas kernels, short_way(): pl.pallas_call(functools.partial(half_kernel, here), out_shape=(shape(2 *...  8.01 us
    ppermute x15, starting transfers between devices, swap(): return lax.ppermute(array, 'shell', [(i, i ^ bit) for i in range(n)])  7.87 us
    pallas_call x1, Pallas kernels, short_way(): pl.pallas_call(functools.partial(last_kernel, count, early), out_shape=sh...  7.44 us
    ppermute x5, waiting for transfers between devices, hop(): lax.ppermute(array, 'shell', [(4 * a + k, 4 * b + k) for a, b in steps fo...  5.72 us
    ppermute x5, starting transfers between devices, hop(): lax.ppermute(array, 'shell', [(4 * a + k, 4 * b + k) for a, b in steps fo...  4.58 us
  transfers between devices with their start and end apart: 20, of which 5 were waited for; matrix products, arithmetic and copies ran while one was open for 0% of the time, Pallas kernels for 9%

profile of v10, /device:TPU:0, one launch (start us, length us, event | category | flops | bytes accessed | tf_op | source)
XLA Modules:
  0.0 96.2 jit_solution(8779231336997914190)
XLA Ops:
  6.5 1.5 %pack_rows.1 = (bf16[80,1280]{1,0:T(8,128)(2,1)S(1)}, bf16[80,1280]{1,0:T(8,128)(2,1)S(1)}, bf16[80,1280]{1,0:T(8,128)(2,1)S(1)}, bf16[80,1280]{1,0:T(8,128)(2,1)S(1)}) custom-call(bf16[160,2304]{1,0:T(8,128)(2,1)} %vir_ref.1, bf16[160,256]{1,0:T(8,128)(2,1)} %occ_ref.1), custom_call_target="tpu_custom_call" | custom-call | flops 300000000 | bytes 3000000 | tf_op jit(solution)/shard_map/pack_rows/pallas_call | solution.py:399
  8.1 0.5 collective-permute-start
  8.6 2.6 %collective-permute-start.1 = (bf16[80,1280]{1,0:T(8,128)(2,1)S(1)}, bf16[80,1280]{1,0:T(8,128)(2,1)S(1)}, u32[]{:S(2)}, u32[]{:S(2)}) collective-permute-start(bf16[80,1280]{1,0:T(8,128)(2,1)S(1)} %get-tuple-element.184), channel_id=1, source_target_pairs={{0,2},{1,3},{2,0},{3,1},{4,6},{5,7},{6,4},{7,5},{8,10},{9,11},{10,... | collective-permute-start | bytes 614408 | tf_op jit(solution)/shard_map/ppermute | solution.py:397
  11.9 0.7 copy-done.1
  12.6 0.2 pack_ids.1
  12.8 12.8 %all_to_all.10.code_ref = s32[16,8,128]{2,1,0:T(8,128)S(1)} all-to-all(s32[16,8,128]{2,1,0:T(8,128)S(1)} %pack_ids.1), channel_id=1, replica_groups=mesh['groups'=2,'shell'=16] {'shell'}, dimensions={0} | all-to-all | bytes 131072 | tf_op jit(solution)/shard_map/all_to_all | solution.py:418
  25.6 2.1 %pick_rows.1 = (bf16[128,1280]{1,0:T(8,128)(2,1)S(1)}, s32[1]{0:T(128)}, s32[1]{0:T(128)}) custom-call(s32[16,8,128]{2,1,0:T(8,128)S(1)} %all_to_all.10.code_ref, s32[1,256]{1,0:T(1,128)} %bitcast.63, bf16[80,1280]{1,0:T(8,128)(2,1)S(1)} %get-tuple-element.182.refs_0_, bf16[80,1280]{1,0:T(8,128)(2,1)S(1)} %collective-permute-done.refs_1_, ...), custom_call_target="tpu_custom_call" | custom-call | flops 300000000 | bytes 2000000 | tf_op jit(solution)/shard_map/pick_rows/pallas_call | solution.py:420
  27.8 0.2 collective-permute-start.3
  28.0 0.7 collective-permute-start.4
  28.6 0.7 collective-permute-start.5
  29.3 0.1 collective-permute-start.9
  29.4 0.9 copy-done
  30.4 14.6 %all_to_all.11.got_ref = bf16[16,16,256]{2,1,0:T(8,128)(2,1)S(1)} all-to-all(bf16[16,16,256]{2,1,0:T(8,128)(2,1)S(1)} %turn_panels.1), channel_id=1, replica_groups=mesh['groups'=2,'shell'=16] {'shell'}, dimensions={0} | all-to-all | bytes 262144 | tf_op jit(solution)/shard_map/all_to_all | solution.py:458
  45.0 0.7 collective-permute-start.8
  45.7 1.3 %collective-permute-start.7 = (bf16[128,1280]{1,0:T(8,128)(2,1)S(1)}, bf16[128,1280]{1,0:T(8,128)(2,1)S(1)}, u32[]{:S(2)}, u32[]{:S(2)}) collective-permute-start(bf16[128,1280]{1,0:T(8,128)(2,1)S(1)} %collective-permute-done.5.inner_ref), channel_id=1, source_target_pairs={{4,0},{5,1},{6,2},{7,3},{8,12},{9,13},{10,14},{11,15},{20,16},{21,... | collective-permute-start | bytes 983048 | tf_op jit(solution)/shard_map/ppermute | solution.py:433
  47.1 0.5 collective-permute-start.11
  47.6 6.4 %collective-permute-done.6.refs_3_ = bf16[128,1280]{1,0:T(8,128)(2,1)S(1)} collective-permute-done((bf16[128,1280]{1,0:T(8,128)(2,1)S(1)}, bf16[128,1280]{1,0:T(8,128)(2,1)S(1)}, u32[]{:S(2)}, u32[]{:S(2)}) %collective-permute-start.6) | collective-permute-done | bytes 327712 | tf_op jit(solution)/shard_map/ppermute | solution.py:397
  54.0 3.0 %collective-permute-done.7.outer_ref = bf16[128,1280]{1,0:T(8,128)(2,1)S(1)} collective-permute-done((bf16[128,1280]{1,0:T(8,128)(2,1)S(1)}, bf16[128,1280]{1,0:T(8,128)(2,1)S(1)}, u32[]{:S(2)}, u32[]{:S(2)}) %collective-permute-start.7) | collective-permute-done | bytes 327712 | tf_op jit(solution)/shard_map/ppermute | solution.py:433
  57.1 0.8 choose_piece.2.refs_4_
  57.8 1.6 %collective-permute-start.12 = (bf16[128,1280]{1,0:T(8,128)(2,1)S(1)}, bf16[128,1280]{1,0:T(8,128)(2,1)S(1)}, u32[]{:S(2)}, u32[]{:S(2)}) collective-permute-start(bf16[128,1280]{1,0:T(8,128)(2,1)S(1)} %choose_piece.2.refs_4_), channel_id=1, source_target_pairs={{0,2},{1,3},{2,0},{3,1},{4,6},{5,7},{6,4},{7,5},{8,10},{9,11},{10,... | collective-permute-start | bytes 983048 | tf_op jit(solution)/shard_map/ppermute | solution.py:397
  59.4 1.3 %collective-permute-start.13 = (bf16[128,1280]{1,0:T(8,128)(2,1)S(1)}, bf16[128,1280]{1,0:T(8,128)(2,1)S(1)}, u32[]{:S(2)}, u32[]{:S(2)}) collective-permute-start(bf16[128,1280]{1,0:T(8,128)(2,1)S(1)} %collective-permute-done.8.inner_ref), channel_id=1, source_target_pairs={{4,0},{5,1},{6,2},{7,3},{8,12},{9,13},{10,14},{11,15},{20,16},{21,... | collective-permute-start | bytes 983048 | tf_op jit(solution)/shard_map/ppermute | solution.py:433
  60.8 0.5 collective-permute-start.15
  61.3 5.1 %collective-permute-done.12.refs_5_ = bf16[128,1280]{1,0:T(8,128)(2,1)S(1)} collective-permute-done((bf16[128,1280]{1,0:T(8,128)(2,1)S(1)}, bf16[128,1280]{1,0:T(8,128)(2,1)S(1)}, u32[]{:S(2)}, u32[]{:S(2)}) %collective-permute-start.12) | collective-permute-done | bytes 327712 | tf_op jit(solution)/shard_map/ppermute | solution.py:397
  66.4 2.7 %collective-permute-done.13.outer_ref = bf16[128,1280]{1,0:T(8,128)(2,1)S(1)} collective-permute-done((bf16[128,1280]{1,0:T(8,128)(2,1)S(1)}, bf16[128,1280]{1,0:T(8,128)(2,1)S(1)}, u32[]{:S(2)}, u32[]{:S(2)}) %collective-permute-start.13) | collective-permute-done | bytes 327712 | tf_op jit(solution)/shard_map/ppermute | solution.py:433
  69.1 0.9 choose_piece.3.refs_6_
  70.0 1.0 %collective-permute-start.16 = (bf16[128,1280]{1,0:T(8,128)(2,1)S(1)}, bf16[128,1280]{1,0:T(8,128)(2,1)S(1)}, u32[]{:S(2)}, u32[]{:S(2)}) collective-permute-start(bf16[128,1280]{1,0:T(8,128)(2,1)S(1)} %choose_piece.3.refs_6_), channel_id=1, source_target_pairs={{0,2},{1,3},{2,0},{3,1},{4,6},{5,7},{6,4},{7,5},{8,10},{9,11},{10,... | collective-permute-start | bytes 983048 | tf_op jit(solution)/shard_map/ppermute | solution.py:397
  71.1 0.5 collective-permute-start.17
  71.6 8.0 %half_transform.1 = (f32[512,1024]{1,0:T(8,128)S(1)}, bf16[2,384,1024]{2,1,0:T(8,128)(2,1)S(1)}) custom-call(s32[16,8,128]{2,1,0:T(8,128)S(1)} %all_to_all.10.code_ref, bf16[16,16,256]{2,1,0:T(8,128)(2,1)S(1)} %all_to_all.11.got_ref, s32[1,256]{1,0:T(1,128)S(1)} %bitcast.64, bf16[128,1280]{1,0:T(8,128)(2,1)S(1)} %get-tuple-element.188.refs_0_, ...), custom_call_target="tpu_custom_call" | custom-call | flops 7000000000 | bytes 1 | tf_op jit(solution)/shard_map/half_transform/pallas_call | solution.py:474
  79.6 0.1 collective-permute-start.19
  79.7 1.6 %collective-permute-done.19.refs_15_ = bf16[128,1280]{1,0:T(8,128)(2,1)S(1)} collective-permute-done((bf16[128,1280]{1,0:T(8,128)(2,1)S(1)}, bf16[128,1280]{1,0:T(8,128)(2,1)S(1)}, u32[]{:S(2)}, u32[]{:S(2)}) %collective-permute-start.19) | collective-permute-done | bytes 327712 | tf_op jit(solution)/shard_map/ppermute | solution.py:397
  81.3 7.4 %last_product.1 = bf16[2,256,2304]{2,1,0:T(8,128)(2,1)} custom-call(s32[1]{0:T(128)} %get-tuple-element.187.me_ref, f32[512,1024]{1,0:T(8,128)S(1)} %get-tuple-element.209.part_ref, bf16[2,384,1024]{2,1,0:T(8,128)(2,1)S(1)} %get-tuple-element.210.late_ref, bf16[128,1280]{1,0:T(8,128)(2,1)S(1)} %get-tuple-element.188.refs_0_, ...), custom_call_target="tpu_custom_call" | custom-call | flops 20000000000 | bytes 1 | tf_op jit(solution)/shard_map/last_product/pallas_call | solution.py:496
  88.8 0.6 while.17
  (25 shorter events, 0.4 us)
Async XLA Ops:
  6.5 65.0 %copy-start.3 = (s32[256]{0:T(256)S(1)}, s32[256]{0:T(256)}, u32[]{:S(2)}) copy-start(s32[256]{0:T(256)} %param.11) | copy-start | bytes 3076
  8.1 17.5 %collective-permute-start = (bf16[80,1280]{1,0:T(8,128)(2,1)S(1)}, bf16[80,1280]{1,0:T(8,128)(2,1)S(1)}, u32[]{:S(2)}, u32[]{:S(2)}) collective-permute-start(bf16[80,1280]{1,0:T(8,128)(2,1)S(1)} %get-tuple-element.183), channel_id=1, source_target_pairs={{0,1},{1,0},{2,3},{3,2},{4,5},{5,4},{6,7},{7,6},{8,9},{9,8},{10,11... | collective-permute-start | bytes 614408 | tf_op jit(solution)/shard_map/ppermute | solution.py:397
  8.6 17.0 %collective-permute-start.1 = (bf16[80,1280]{1,0:T(8,128)(2,1)S(1)}, bf16[80,1280]{1,0:T(8,128)(2,1)S(1)}, u32[]{:S(2)}, u32[]{:S(2)}) collective-permute-start(bf16[80,1280]{1,0:T(8,128)(2,1)S(1)} %get-tuple-element.184), channel_id=1, source_target_pairs={{0,2},{1,3},{2,0},{3,1},{4,6},{5,7},{6,4},{7,5},{8,10},{9,11},{10,... | collective-permute-start | bytes 614408 | tf_op jit(solution)/shard_map/ppermute | solution.py:397
  11.2 14.4 %collective-permute-start.2 = (bf16[80,1280]{1,0:T(8,128)(2,1)S(1)}, bf16[80,1280]{1,0:T(8,128)(2,1)S(1)}, u32[]{:S(2)}, u32[]{:S(2)}) collective-permute-start(bf16[80,1280]{1,0:T(8,128)(2,1)S(1)} %get-tuple-element.185), channel_id=1, source_target_pairs={{0,3},{1,2},{2,1},{3,0},{4,7},{5,6},{6,5},{7,4},{8,11},{9,10},{10,... | collective-permute-start | bytes 614408 | tf_op jit(solution)/shard_map/ppermute | solution.py:397
  11.9 0.7 copy-start.1
  27.8 17.2 %collective-permute-start.3 = (bf16[128,1280]{1,0:T(8,128)(2,1)S(1)}, bf16[128,1280]{1,0:T(8,128)(2,1)S(1)}, u32[]{:S(2)}, u32[]{:S(2)}) collective-permute-start(bf16[128,1280]{1,0:T(8,128)(2,1)S(1)} %get-tuple-element.188.refs_0_), channel_id=1, source_target_pairs={{0,2},{1,3},{2,0},{3,1},{4,6},{5,7},{6,4},{7,5},{8,10},{9,11},{10,... | collective-permute-start | bytes 983048 | tf_op jit(solution)/shard_map/ppermute | solution.py:397
  28.0 17.0 %collective-permute-start.4 = (bf16[128,1280]{1,0:T(8,128)(2,1)S(1)}, bf16[128,1280]{1,0:T(8,128)(2,1)S(1)}, u32[]{:S(2)}, u32[]{:S(2)}) collective-permute-start(bf16[128,1280]{1,0:T(8,128)(2,1)S(1)} %get-tuple-element.188.refs_0_), channel_id=1, source_target_pairs={{0,4},{1,5},{2,6},{3,7},{4,0},{5,1},{6,2},{7,3},{8,12},{9,13},{10,... | collective-permute-start | bytes 983048 | tf_op jit(solution)/shard_map/ppermute | solution.py:433
  28.6 16.3 %collective-permute-start.5 = (bf16[128,1280]{1,0:T(8,128)(2,1)S(1)}, bf16[128,1280]{1,0:T(8,128)(2,1)S(1)}, u32[]{:S(2)}, u32[]{:S(2)}) collective-permute-start(bf16[128,1280]{1,0:T(8,128)(2,1)S(1)} %get-tuple-element.188.refs_0_), channel_id=1, source_target_pairs={{4,8},{5,9},{6,10},{7,11},{8,4},{9,5},{10,6},{11,7},{20,24},{21,25... | collective-permute-start | bytes 983048 | tf_op jit(solution)/shard_map/ppermute | solution.py:433
  29.3 17.8 %collective-permute-start.9 = (bf16[128,1280]{1,0:T(8,128)(2,1)S(1)}, bf16[128,1280]{1,0:T(8,128)(2,1)S(1)}, u32[]{:S(2)}, u32[]{:S(2)}) collective-permute-start(bf16[128,1280]{1,0:T(8,128)(2,1)S(1)} %get-tuple-element.188.refs_0_), channel_id=1, source_target_pairs={{0,1},{1,0},{2,3},{3,2},{4,5},{5,4},{6,7},{7,6},{8,9},{9,8},{10,11... | collective-permute-start | bytes 983048 | tf_op jit(solution)/shard_map/ppermute | solution.py:397
  29.4 0.9 copy-start
  45.0 9.0 %collective-permute-start.6 = (bf16[128,1280]{1,0:T(8,128)(2,1)S(1)}, bf16[128,1280]{1,0:T(8,128)(2,1)S(1)}, u32[]{:S(2)}, u32[]{:S(2)}) collective-permute-start(bf16[128,1280]{1,0:T(8,128)(2,1)S(1)} %collective-permute-done.4.refs_2_), channel_id=1, source_target_pairs={{0,2},{1,3},{2,0},{3,1},{4,6},{5,7},{6,4},{7,5},{8,10},{9,11},{10,... | collective-permute-start | bytes 983048 | tf_op jit(solution)/shard_map/ppermute | solution.py:397
  45.0 12.0 %collective-permute-start.8 = (bf16[128,1280]{1,0:T(8,128)(2,1)S(1)}, bf16[128,1280]{1,0:T(8,128)(2,1)S(1)}, u32[]{:S(2)}, u32[]{:S(2)}) collective-permute-start(bf16[128,1280]{1,0:T(8,128)(2,1)S(1)} %collective-permute-done.4.refs_2_), channel_id=1, source_target_pairs={{4,8},{5,9},{6,10},{7,11},{8,4},{9,5},{10,6},{11,7},{20,24},{21,25... | collective-permute-start | bytes 983048 | tf_op jit(solution)/shard_map/ppermute | solution.py:433
  45.7 11.3 %collective-permute-start.7 = (bf16[128,1280]{1,0:T(8,128)(2,1)S(1)}, bf16[128,1280]{1,0:T(8,128)(2,1)S(1)}, u32[]{:S(2)}, u32[]{:S(2)}) collective-permute-start(bf16[128,1280]{1,0:T(8,128)(2,1)S(1)} %collective-permute-done.5.inner_ref), channel_id=1, source_target_pairs={{4,0},{5,1},{6,2},{7,3},{8,12},{9,13},{10,14},{11,15},{20,16},{21,... | collective-permute-start | bytes 983048 | tf_op jit(solution)/shard_map/ppermute | solution.py:433
  47.0 10.0 %collective-permute-start.10 = (bf16[128,1280]{1,0:T(8,128)(2,1)S(1)}, bf16[128,1280]{1,0:T(8,128)(2,1)S(1)}, u32[]{:S(2)}, u32[]{:S(2)}) collective-permute-start(bf16[128,1280]{1,0:T(8,128)(2,1)S(1)} %collective-permute-done.3.refs_1_), channel_id=1, source_target_pairs={{0,1},{1,0},{2,3},{3,2},{4,5},{5,4},{6,7},{7,6},{8,9},{9,8},{10,11... | collective-permute-start | bytes 983048 | tf_op jit(solution)/shard_map/ppermute | solution.py:397
  47.1 9.9 %collective-permute-start.11 = (bf16[128,1280]{1,0:T(8,128)(2,1)S(1)}, bf16[128,1280]{1,0:T(8,128)(2,1)S(1)}, u32[]{:S(2)}, u32[]{:S(2)}) collective-permute-start(bf16[128,1280]{1,0:T(8,128)(2,1)S(1)} %collective-permute-done.4.refs_2_), channel_id=1, source_target_pairs={{0,1},{1,0},{2,3},{3,2},{4,5},{5,4},{6,7},{7,6},{8,9},{9,8},{10,11... | collective-permute-start | bytes 983048 | tf_op jit(solution)/shard_map/ppermute | solution.py:397
  57.8 8.6 %collective-permute-start.12 = (bf16[128,1280]{1,0:T(8,128)(2,1)S(1)}, bf16[128,1280]{1,0:T(8,128)(2,1)S(1)}, u32[]{:S(2)}, u32[]{:S(2)}) collective-permute-start(bf16[128,1280]{1,0:T(8,128)(2,1)S(1)} %choose_piece.2.refs_4_), channel_id=1, source_target_pairs={{0,2},{1,3},{2,0},{3,1},{4,6},{5,7},{6,4},{7,5},{8,10},{9,11},{10,... | collective-permute-start | bytes 983048 | tf_op jit(solution)/shard_map/ppermute | solution.py:397
  59.4 9.6 %collective-permute-start.13 = (bf16[128,1280]{1,0:T(8,128)(2,1)S(1)}, bf16[128,1280]{1,0:T(8,128)(2,1)S(1)}, u32[]{:S(2)}, u32[]{:S(2)}) collective-permute-start(bf16[128,1280]{1,0:T(8,128)(2,1)S(1)} %collective-permute-done.8.inner_ref), channel_id=1, source_target_pairs={{4,0},{5,1},{6,2},{7,3},{8,12},{9,13},{10,14},{11,15},{20,16},{21,... | collective-permute-start | bytes 983048 | tf_op jit(solution)/shard_map/ppermute | solution.py:433
  60.7 8.4 %collective-permute-start.14 = (bf16[128,1280]{1,0:T(8,128)(2,1)S(1)}, bf16[128,1280]{1,0:T(8,128)(2,1)S(1)}, u32[]{:S(2)}, u32[]{:S(2)}) collective-permute-start(bf16[128,1280]{1,0:T(8,128)(2,1)S(1)} %collective-permute-done.6.refs_3_), channel_id=1, source_target_pairs={{0,1},{1,0},{2,3},{3,2},{4,5},{5,4},{6,7},{7,6},{8,9},{9,8},{10,11... | collective-permute-start | bytes 983048 | tf_op jit(solution)/shard_map/ppermute | solution.py:397
  60.8 8.3 %collective-permute-start.15 = (bf16[128,1280]{1,0:T(8,128)(2,1)S(1)}, bf16[128,1280]{1,0:T(8,128)(2,1)S(1)}, u32[]{:S(2)}, u32[]{:S(2)}) collective-permute-start(bf16[128,1280]{1,0:T(8,128)(2,1)S(1)} %choose_piece.2.refs_4_), channel_id=1, source_target_pairs={{0,1},{1,0},{2,3},{3,2},{4,5},{5,4},{6,7},{7,6},{8,9},{9,8},{10,11... | collective-permute-start | bytes 983048 | tf_op jit(solution)/shard_map/ppermute | solution.py:397
  70.0 9.6 %collective-permute-start.16 = (bf16[128,1280]{1,0:T(8,128)(2,1)S(1)}, bf16[128,1280]{1,0:T(8,128)(2,1)S(1)}, u32[]{:S(2)}, u32[]{:S(2)}) collective-permute-start(bf16[128,1280]{1,0:T(8,128)(2,1)S(1)} %choose_piece.3.refs_6_), channel_id=1, source_target_pairs={{0,2},{1,3},{2,0},{3,1},{4,6},{5,7},{6,4},{7,5},{8,10},{9,11},{10,... | collective-permute-start | bytes 983048 | tf_op jit(solution)/shard_map/ppermute | solution.py:397
  71.1 8.6 %collective-permute-start.18 = (bf16[128,1280]{1,0:T(8,128)(2,1)S(1)}, bf16[128,1280]{1,0:T(8,128)(2,1)S(1)}, u32[]{:S(2)}, u32[]{:S(2)}) collective-permute-start(bf16[128,1280]{1,0:T(8,128)(2,1)S(1)} %choose_piece.3.refs_6_), channel_id=1, source_target_pairs={{0,1},{1,0},{2,3},{3,2},{4,5},{5,4},{6,7},{7,6},{8,9},{9,8},{10,11... | collective-permute-start | bytes 983048 | tf_op jit(solution)/shard_map/ppermute | solution.py:397
  71.1 8.5 %collective-permute-start.17 = (bf16[128,1280]{1,0:T(8,128)(2,1)S(1)}, bf16[128,1280]{1,0:T(8,128)(2,1)S(1)}, u32[]{:S(2)}, u32[]{:S(2)}) collective-permute-start(bf16[128,1280]{1,0:T(8,128)(2,1)S(1)} %collective-permute-done.12.refs_5_), channel_id=1, source_target_pairs={{0,1},{1,0},{2,3},{3,2},{4,5},{5,4},{6,7},{7,6},{8,9},{9,8},{10,11... | collective-permute-start | bytes 983048 | tf_op jit(solution)/shard_map/ppermute | solution.py:397
  79.6 1.7 %collective-permute-start.19 = (bf16[128,1280]{1,0:T(8,128)(2,1)S(1)}, bf16[128,1280]{1,0:T(8,128)(2,1)S(1)}, u32[]{:S(2)}, u32[]{:S(2)}) collective-permute-start(bf16[128,1280]{1,0:T(8,128)(2,1)S(1)} %collective-permute-done.16.refs_7_), channel_id=1, source_target_pairs={{0,1},{1,0},{2,3},{3,2},{4,5},{5,4},{6,7},{7,6},{8,9},{9,8},{10,11... | collective-permute-start | bytes 983048 | tf_op jit(solution)/shard_map/ppermute | solution.py:397

commit v11 on v10

--- a/solution.py
+++ b/solution.py
@@ -127,21 +127,30 @@
             self.edges.append(jnp.sum(self.used * jnp.floor((reach + extra) * 0.5), axis=0, keepdims=True))
 
 
-def pack_kernel(vir_ref, occ_ref, *outs):
+def pack_kernel(vir_ref, occ_ref, panels_ref, *refs):
+    outs, (turned_ref,) = refs[:4], refs[4:]
     me = lax.axis_index("shell")
     core, y = lax.rem(me, 2), lax.rem(lax.div(me, 2), 2)
     here, nvir = vir_ref.shape
+    rows = here // 2
     width, thin = nvir // CORES, occ_ref.shape[1] // CORES
+    turned_ref[...] = jnp.swapaxes(panels_ref[...].astype(F32), 0, 1)
+    block = EDGE * EDGE
     for dy in range(2):
         parity = lax.rem(y + dy, 2)
-        pick = zero_one(iota((here // 2, here), 1) == 2 * iota((here // 2, here), 0) + parity).astype(BF16)
+        pick = zero_one(iota((rows, here), 1) == 2 * iota((rows, here), 0) + parity).astype(BF16)
         for dc in range(2):
             half = lax.rem(core + dc, 2)
             out = outs[2 * dy + dc]
             part = vir_ref[:, pl.ds(pl.multiple_of(half * width, 128), width)]
-            out[:, :width] = jnp.dot(pick, part, preferred_element_type=F32).astype(BF16)
+            out[:rows, :width] = jnp.dot(pick, part, preferred_element_type=F32).astype(BF16)
             part = occ_ref[:, pl.ds(pl.multiple_of(half * thin, 128), thin)]
-            out[:, width:] = jnp.dot(pick, part, preferred_element_type=F32).astype(BF16)
+            out[:rows, width:] = jnp.dot(pick, part, preferred_element_type=F32).astype(BF16)
+            for z in range(Z):
+                device = (z * Y + parity) * CORES + half
+                pair = turned_ref[pl.ds(2 * device, 2)].reshape(2 * BLK_DEV, block)
+                out[rows:, z * block : (z + 1) * block] = pair.astype(BF16)
+            out[rows:, Z * block :] = jnp.zeros((2 * BLK_DEV, out.shape[1] - Z * block), BF16)
 
 
 def ids_kernel(shells, pairs_ref, count_ref, code_ref):
@@ -152,13 +161,8 @@
     code_ref[...] = jnp.broadcast_to(jnp.broadcast_to(code, (BLK_DEV, 128))[None], code_ref.shape)
 
 
-def turn_kernel(panels_ref, send_ref):
-    turned = jnp.swapaxes(panels_ref[...].astype(F32), 0, 1)
-    send_ref[...] = turned.reshape(send_ref.shape).astype(BF16)
-
-
 def pick_kernel(here, code_ref, size_ref, *refs):
-    sources, (out_ref, over_ref, me_ref) = refs[:4], refs[4:]
+    sources, (out_ref, over_ref, me_ref), panel_refs = refs[:4], refs[4:7], refs[7:]
     me = lax.axis_index("shell")
     me_ref[0] = me
     core, y, z = lax.rem(me, 2), lax.rem(lax.div(me, 2), 2), lax.div(me, 4)
@@ -179,8 +183,13 @@
     totals = [jnp.zeros((CAP, width), F32), jnp.zeros((CAP, 128), F32)]
     columns = [slice(0, width), slice(width, width + 128)]
     extra = jnp.where(even, lists[0].extra[0], lists[0].extra[1])
+    rows = here // 2
     for k, source in enumerate(sources):
-        device = 4 * z + 2 * lax.rem(y + k // 2, 2) + lax.rem(core + k % 2, 2)
+        member = 2 * lax.rem(y + k // 2, 2) + lax.rem(core + k % 2, 2)
+        device = 4 * z + member
+        for r, panel_ref in enumerate(panel_refs):
+            lanes = pl.ds(pl.multiple_of((z ^ r) * (EDGE * EDGE), 128), EDGE * EDGE)
+            panel_ref[member] = source[rows:, lanes]
         row = (2 * iota((shell_count, 128), 1) + device * here + y).astype(F32)
         where = row - shells.starts
         inside = (where >= 0.0) & (where < shells.size)
@@ -193,7 +202,7 @@
             place = jnp.where(place > 0.0, place - 1.0 - base, -1.0)
             hot = zero_one(place == iota((CAP, 128), 0).astype(F32)).astype(BF16)
             totals[total] += jnp.dot(
-                hot[:, : here // 2], source[:, column], preferred_element_type=F32
+                hot[:, :rows], source[:rows, column], preferred_element_type=F32
             )
     for total, column in zip(totals, columns):
         out_ref[:, column] = total.astype(BF16)
@@ -225,21 +234,24 @@
         copy.wait()
 
 
-def half_kernel(here, code_ref, got_ref, size_ref, *refs):
-    count = (len(refs) - 4) // 2
-    pieces, (half_ref, late_ref, occ_ref, sems) = refs[: 2 * count], refs[2 * count :]
+def half_kernel(here, early, code_ref, size_ref, *refs):
+    panel_refs, pieces, refs = refs[:Z], refs[Z : Z + 2 * early], refs[Z + 2 * early :]
+    half_ref, late_ref, got_ref, occ_ref, part_ref, hot_ref, placed_ref, sems = refs
     me = lax.axis_index("shell")
     core, chip = lax.rem(me, CORES), lax.div(me, CORES)
+    z = lax.div(chip, Y)
     width = pieces[0].shape[1] - 128
     copies = []
     for far in range(2):
         half = lax.rem(core + far, CORES)
-        for k in range(count):
-            at = far * count + k
+        for k in range(early):
+            at = far * early + k
             target = occ_ref.at[pl.ds(k * CAP, CAP), pl.ds(pl.multiple_of(half * 128, 128), 128)]
             copies.append(pltpu.make_async_copy(pieces[at].at[:, pl.ds(width, 128)], target, sems.at[at]))
     for copy in copies:
         copy.start()
+    for r, panel_ref in enumerate(panel_refs):
+        got_ref[pl.ds((z ^ r) * (Y * CORES), Y * CORES)] = panel_ref[...]
     window = CORES * Y * here
     shell_count = size_ref.shape[1]
     got = got_ref[...].astype(F32)
@@ -286,86 +298,80 @@
 
     place_c, place_r = places(hots[0], lists[0]), places(hots[1], lists[1])
     span = 16 * EDGE
-    width = half_ref.shape[1]
     s_in, l_in = iota((span, span), 0), iota((span, span), 1)
     keep_m = (l_in // EDGE) == (s_in % EDGE)
     fold = zero_one((s_in % EDGE) == (l_in % EDGE)).astype(BF16)
     same_slot = (s_in // EDGE) == (l_in // EDGE)
     blocks = [taken(got[:, p * BLK_DEV : (p + 1) * BLK_DEV, :].reshape(slots, span)) for p in range(2)]
-    lanes = iota((span, width), 1).astype(F32)
+    lanes = iota((span, half_ref.shape[1]), 1).astype(F32)
     for copy in copies:
         copy.wait()
     occ = occ_ref[...]
-    late = []
+    cut = early * CAP
     for g in range(kept // 16):
         rows = slice(g * span, (g + 1) * span)
         r_hot = zero_one(place_r[rows] == lanes).astype(BF16)
         c_hot = zero_one(place_c[rows] == lanes).astype(BF16)
-        part = jnp.dot(r_hot[:, : count * CAP], occ, preferred_element_type=F32).T.astype(BF16)
+        part_ref[:, rows] = jnp.dot(r_hot[:, :cut], occ, preferred_element_type=F32).T.astype(BF16)
+        hot_ref[:, rows] = r_hot[:, cut:].T
         for p in range(2):
             block = blocks[p][g * 16 : (g + 1) * 16].reshape(16, 1, span)
             block = jnp.broadcast_to(block, (16, EDGE, span)).reshape(span, span)
             block = jnp.where(keep_m, block, 0.0).astype(BF16)
             diag = jnp.dot(block, fold, preferred_element_type=F32)
             diag = jnp.where(same_slot, diag, 0.0).astype(BF16)
-            placed = jnp.dot(diag, c_hot, preferred_element_type=F32).astype(BF16)
-            piece = jnp.dot(part, placed, preferred_element_type=F32)
-            rows_p = slice(p * NOCC, (p + 1) * NOCC)
-            later = jnp.dot(r_hot[:, count * CAP :].T, placed, preferred_element_type=F32)
-            if g == 0:
-                half_ref[rows_p, :] = piece
-                late.append(later)
-            else:
-                half_ref[rows_p, :] += piece
-                late[p] += later
+            placed_ref[p, rows, :] = jnp.dot(diag, c_hot, preferred_element_type=F32).astype(BF16)
     for p in range(2):
-        late_ref[p] = late[p].astype(BF16)
-
-
-def last_kernel(count, early, me_ref, part_ref, late_ref, *refs):
-    pieces, (out_ref, right_ref, occ_ref, half_ref, sems) = refs[: 2 * count], refs[2 * count :]
-    tile = out_ref.shape[2]
+        half_ref[p * NOCC : (p + 1) * NOCC, :] = jnp.dot(part_ref[...], placed_ref[p], preferred_element_type=F32)
+        late_ref[p] = jnp.dot(hot_ref[...], placed_ref[p], preferred_element_type=F32).astype(BF16)
+
+
+def last_kernel(count, early, me_ref, part_any, late_any, *refs):
+    pieces, (out_any, right_ref, occ_ref, part_ref, late_ref, half_ref, tiles_ref, sems) = refs[: 2 * count], refs[2 * count :]
     width = right_ref.shape[2]
+    tile = tiles_ref.shape[3]
     per = width // tile
     core = lax.rem(me_ref[0], CORES)
-    j = pl.program_id(0)
-
-    def occ_copies():
-        for far in range(2):
-            half = lax.rem(core + far, CORES)
-            for k in range(early, count):
-                at = far * count + k
-                target = occ_ref.at[pl.ds((k - early) * CAP, CAP), pl.ds(pl.multiple_of(half * 128, 128), 128)]
-                yield pltpu.make_async_copy(pieces[at].at[:, pl.ds(width, 128)], target, sems.at[2 * count + at])
-
-    def copies(far):
+    first, near, far, results = [], [], [], []
+
+    def copy_of(source, target):
+        at = len(first) + len(near) + len(far) + len(results)
+        return pltpu.make_async_copy(source, target, sems.at[at])
+
+    first.append(copy_of(part_any, part_ref))
+    first.append(copy_of(late_any, late_ref))
+    for side in range(2):
+        half = lax.rem(core + side, CORES)
+        for k in range(early, count):
+            target = occ_ref.at[pl.ds((k - early) * CAP, CAP), pl.ds(pl.multiple_of(half * 128, 128), 128)]
+            first.append(copy_of(pieces[side * count + k].at[:, pl.ds(width, 128)], target))
+    for side, copies in enumerate((near, far)):
         for k in range(count):
-            at = far * count + k
-            target = right_ref.at[far, pl.ds(k * CAP, CAP), :]
-            yield pltpu.make_async_copy(pieces[at].at[:, pl.ds(0, width)], target, sems.at[at])
-
-    @pl.when(j == 0)
-    def _():
-        for copy in (*occ_copies(), *copies(0), *copies(1)):
-            copy.start()
-        for copy in occ_copies():
+            target = right_ref.at[side, pl.ds(k * CAP, CAP), :]
+            copies.append(copy_of(pieces[side * count + k].at[:, pl.ds(0, width)], target))
+    for copy in (*first, *near, *far):
+        copy.start()
+    for copy in first:
+        copy.wait()
+    occ = occ_ref[...].T
+    for p in range(2):
+        rows = slice(p * NOCC, (p + 1) * NOCC)
+        late = jnp.dot(occ, late_ref[p], preferred_element_type=F32)
+        half_ref[rows, :] = (part_ref[rows, :] + late).astype(BF16)
+    for side, copies in enumerate((near, far)):
+        for copy in copies:
             copy.wait()
-        occ = occ_ref[...].T
-        for p in range(2):
-            rows = slice(p * NOCC, (p + 1) * NOCC)
-            late = jnp.dot(occ, late_ref[p], preferred_element_type=F32)
-            half_ref[rows, :] = (part_ref[rows, :] + late).astype(BF16)
-
-    for far in range(2):
-
-        @pl.when(j == far * per)
-        def _():
-            for copy in copies(far):
-                copy.wait()
-
-    right = right_ref[lax.div(j, per), :, pl.ds(pl.multiple_of(lax.rem(j, per) * tile, 128), tile)]
-    total = jnp.dot(half_ref[...], right, preferred_element_type=F32).astype(BF16)
-    out_ref[...] = total.reshape(out_ref.shape)
+        base = lax.rem(core + side, CORES) * width
+        for t in range(per):
+            right = right_ref[side, :, t * tile : (t + 1) * tile]
+            total = jnp.dot(half_ref[...], right, preferred_element_type=F32).astype(BF16)
+            at = side * per + t
+            tiles_ref[at] = total.reshape(tiles_ref.shape[1:])
+            columns = pl.ds(pl.multiple_of(base + t * tile, 128), tile)
+            results.append(copy_of(tiles_ref.at[at], out_any.at[:, :, columns]))
+            results[-1].start()
+    for copy in results:
+        copy.wait()
 
 
 VMEM = pl.BlockSpec(memory_space=pltpu.VMEM)
@@ -398,13 +404,14 @@
 
     keep, to_core, to_y, to_both = pl.pallas_call(
         pack_kernel,
-        out_shape=[shape(here // 2, packed)] * 4,
-        in_specs=[VMEM] * 2,
+        out_shape=[shape(here // 2 + 2 * BLK_DEV, packed)] * 4,
+        in_specs=[VMEM] * 3,
         out_specs=[VMEM] * 4,
+        scratch_shapes=[pltpu.VMEM((2 * n, BLK_DEV, EDGE * EDGE), F32)],
         compiler_params=params(12),
         cost_estimate=cost(3e8, 3e6),
         name="pack_rows",
-    )(vir_coef, occ_coef)
+    )(vir_coef, occ_coef, panels)
     to_y, to_both, to_core = swap(to_y, 2), swap(to_both, 3), swap(to_core, 1)
     code = pl.pallas_call(
         functools.partial(ids_kernel, size_row.shape[1]),
@@ -417,11 +424,12 @@
     )(block_pairs.T, block_count.reshape(1, 1))
     code = lax.all_to_all(code, "shell", split_axis=0, concat_axis=0, tiled=True)
 
-    mine, over, me = pl.pallas_call(
+    mine, over, me, *panel = pl.pallas_call(
         functools.partial(pick_kernel, here),
-        out_shape=(shape(CAP, packed), shape(1, dtype=jnp.int32), shape(1, dtype=jnp.int32)),
+        out_shape=[shape(CAP, packed), shape(1, dtype=jnp.int32), shape(1, dtype=jnp.int32)]
+        + [shape(Y * CORES, 2 * BLK_DEV, EDGE * EDGE)] * Z,
         in_specs=[VMEM] * 6,
-        out_specs=(VMEM, SMEM, SMEM),
+        out_specs=[VMEM, SMEM, SMEM] + [VMEM] * Z,
         compiler_params=params(12),
         cost_estimate=cost(3e8, 2e6),
         name="pick_rows",
@@ -445,46 +453,48 @@
         )(me, inner, outer)
 
     mine_y, beside, across = swap(mine, 2), hop(mine, ends), hop(mine, middle)
-    panels, _ = lax.optimization_barrier((panels, mine))
-    send = pl.pallas_call(
-        turn_kernel,
-        out_shape=shape(n, 2 * BLK_DEV, EDGE * EDGE),
-        in_specs=[VMEM],
-        out_specs=VMEM,
-        compiler_params=params(12),
-        cost_estimate=cost(1e6, 3e5),
-        name="turn_panels",
-    )(panels)
-    got = lax.all_to_all(send, "shell", split_axis=0, concat_axis=0, tiled=True)
-    mine_y, beside, across, got = lax.optimization_barrier((mine_y, beside, across, got))
+    panel[1] = swap(panel[1], 4)
+    mine_y, beside, across, panel[1] = lax.optimization_barrier((mine_y, beside, across, panel[1]))
 
     beside_y, across_out, corner = swap(beside, 2), hop(across, outward), hop(beside, middle)
     far = [swap(piece, 1) for piece in (mine, mine_y, beside)]
-    beside_y, across_out, corner, *far = lax.optimization_barrier((beside_y, across_out, corner, *far))
+    panel[2] = swap(panel[2], 8)
+    beside_y, across_out, corner, panel[2], *far = lax.optimization_barrier(
+        (beside_y, across_out, corner, panel[2], *far)
+    )
 
     across = choose(across, across_out)
     across_y, corner_out = swap(across, 2), hop(corner, outward)
     far += [swap(piece, 1) for piece in (beside_y, across)]
-    across_y, corner_out, *far = lax.optimization_barrier((across_y, corner_out, *far))
+    panel[3] = swap(panel[3], 12)
+    across_y, corner_out, panel[3], *far = lax.optimization_barrier((across_y, corner_out, panel[3], *far))
 
     corner = choose(corner, corner_out)
     corner_y = swap(corner, 2)
     near = [mine, mine_y, beside, beside_y, across]
     early = len(near)
+    slots = LIVE_DEV * n * EDGE
     half, late = pl.pallas_call(
-        functools.partial(half_kernel, here),
+        functools.partial(half_kernel, here, early),
         out_shape=(shape(2 * NOCC, room, dtype=F32), shape(2, room - early * CAP, room)),
         grid=(1,),
-        in_specs=[VMEM] * 3 + [ANY] * (2 * early),
+        in_specs=[VMEM] * (2 + Z) + [ANY] * (2 * early),
         out_specs=(
             pl.BlockSpec((2 * NOCC, room), lambda i: (0, 0)),
             pl.BlockSpec((2, room - early * CAP, room), lambda i: (0, 0, 0)),
         ),
-        scratch_shapes=[pltpu.VMEM((early * CAP, NOCC), BF16), pltpu.SemaphoreType.DMA((2 * early,))],
-        compiler_params=params(28),
+        scratch_shapes=[
+            pltpu.VMEM((n, 2 * BLK_DEV, EDGE * EDGE), BF16),
+            pltpu.VMEM((early * CAP, NOCC), BF16),
+            pltpu.VMEM((NOCC, slots), BF16),
+            pltpu.VMEM((room - early * CAP, slots), BF16),
+            pltpu.VMEM((2, slots, room), BF16),
+            pltpu.SemaphoreType.DMA((2 * early,)),
+        ],
+        compiler_params=params(30),
         cost_estimate=cost(7e9, 1),
         name="half_transform",
-    )(code, got, size_row, *near, *far)
+    )(code, size_row, *panel, *near, *far)
     near += [across_y, corner]
     far += [swap(piece, 1) for piece in near[early:]]
     corner_y, half, late, *far = lax.optimization_barrier((corner_y, half, late, *far))
@@ -496,27 +506,22 @@
     out = pl.pallas_call(
         functools.partial(last_kernel, count, early),
         out_shape=shape(2, NOCC, nvir),
-        grid_spec=pltpu.PrefetchScalarGridSpec(
-            num_scalar_prefetch=1,
-            grid=(nvir // tile,),
-            in_specs=[
-                pl.BlockSpec((2 * NOCC, room), lambda j, o: (0, 0)),
-                pl.BlockSpec((2, room - early * CAP, room), lambda j, o: (0, 0, 0)),
-            ]
-            + [ANY] * (2 * count),
-            out_specs=pl.BlockSpec((2, NOCC, tile), lambda j, o: (0, 0, (j + 3 * (o[0] % 2)) % 6)),
-            scratch_shapes=[
-                pltpu.VMEM((CORES, room, width), BF16),
-                pltpu.VMEM((room - early * CAP, NOCC), BF16),
-                pltpu.VMEM((2 * NOCC, room), BF16),
-                pltpu.SemaphoreType.DMA((4 * count,)),
-            ],
-        ),
-        compiler_params=params(28),
+        in_specs=[SMEM] + [ANY] * (2 + 2 * count),
+        out_specs=ANY,
+        scratch_shapes=[
+            pltpu.VMEM((CORES, room, width), BF16),
+            pltpu.VMEM((room - early * CAP, NOCC), BF16),
+            pltpu.VMEM(half.shape, F32),
+            pltpu.VMEM(late.shape, BF16),
+            pltpu.VMEM((2 * NOCC, room), BF16),
+            pltpu.VMEM((nvir // tile, 2, NOCC, tile), BF16),
+            pltpu.SemaphoreType.DMA((2 + 4 * count + nvir // tile,)),
+        ],
+        compiler_params=params(30),
         cost_estimate=cost(2e10, 1),
         name="last_product",
     )(me, half, late, *near, *far)
-    return out, over[0], code, got
+    return out, over[0], code, me, panel
 
 
 def per_device(*args):
@@ -526,11 +531,13 @@
     sparse = LIVE_DEV * n * EDGE < n * here
     if not (sparse and n == Z * Y * CORES and here <= 256 and here % 16 == 0 and nvir % 768 == 0):
         return from_start(*args)
-    out, over, code, got = short_way(*args)
+    out, over, code, me, panel = short_way(*args)
 
     def again(carry):
         over, _ = carry
-        over, code_now, turned, *held = lax.optimization_barrier((over, code, got, *args[3:]))
+        over, code_now, me_now, panel_now, *held = lax.optimization_barrier((over, code, me, tuple(panel), *args[3:]))
+        z = me_now[0] // (Y * CORES)
+        turned = jnp.stack(panel_now)[jnp.arange(Z, dtype=jnp.int32) ^ z]
         turned = turned.reshape(n, 2, BLK_DEV, EDGE * EDGE).swapaxes(1, 2).reshape(n * BLK_DEV, 2, EDGE * EDGE)
         code_now = jnp.max(code_now, axis=2).reshape(n * BLK_DEV)
         ids = jnp.maximum(code_now, 0)

time: 96.5 us -> 91.6 us (0.949)
  blocking collectives: 27.4 us -> 12.8 us
  starting transfers between devices: 12.5 us -> 21.4 us
  waiting for transfers between devices: 18.9 us -> 21.1 us
  Pallas kernels: 21.1 us -> 19.6 us
    all_to_all x1 -> x0, blocking collectives: 14.6 us -> none  [short_way(): got = lax.all_to_all(send, 'shell', split_axis=0, concat_axis=0, tiled=True)]
    ppermute x15 -> x18, starting transfers between devices: 7.87 us -> 16.1 us  [swap(): return lax.ppermute(array, 'shell', [(i, i ^ bit) for i in range(n)])]
    ppermute x5, waiting for transfers between devices: 5.72 us -> 7.04 us  [hop(): lax.ppermute(array, 'shell', [(4 * a + k, 4 * b + k) for a, b in steps fo...]
    ppermute x15 -> x18, waiting for transfers between devices: 13.1 us -> 14.1 us  [swap(): return lax.ppermute(array, 'shell', [(i, i ^ bit) for i in range(n)])]
    pallas_call x4 -> x3, Pallas kernels: 11.8 us -> 10.9 us  [the longest x1 7.19 us: short_way(): pl.pallas_call(functools.partial(half_kernel, here, early), out_shape=(sh...]
  transfers between devices with their start and end apart: 20 -> 23, of which waited for: 5 -> 6; matrix products, arithmetic and copies ran while one was open for 0% -> 0% of each run, Pallas kernels for 9% -> 8%
where the time goes in v11:
time: 91.6 us; the launch traced here: 91.3 us
  starting transfers between devices  21.4 us (23%)
  waiting for transfers between devices  21.1 us (23%)
  Pallas kernels  19.6 us (21%)
  between operations  14.2 us (16%)
  blocking collectives  12.8 us (14%)
  local copies, waits for them, and re-layouts  1.58 us (2%)
    ppermute x18, starting transfers between devices, swap(): return lax.ppermute(array, 'shell', [(i, i ^ bit) for i in range(n)])  16.1 us
    ppermute x18, waiting for transfers between devices, swap(): return lax.ppermute(array, 'shell', [(i, i ^ bit) for i in range(n)])  14.1 us
    all_to_all x1, blocking collectives, short_way(): lax.all_to_all(code, 'shell', split_axis=0, concat_axis=0, tiled=True)  12.8 us
    pallas_call x1, Pallas kernels, short_way(): pl.pallas_call(functools.partial(half_kernel, here, early), out_shape=(sh...  7.19 us
    ppermute x5, waiting for transfers between devices, hop(): lax.ppermute(array, 'shell', [(4 * a + k, 4 * b + k) for a, b in steps fo...  7.04 us
    pallas_call x1, Pallas kernels, short_way(): pl.pallas_call(functools.partial(last_kernel, count, early), out_shape=sh...  6.77 us
    ppermute x5, starting transfers between devices, hop(): lax.ppermute(array, 'shell', [(4 * a + k, 4 * b + k) for a, b in steps fo...  5.25 us
    pallas_call x1, Pallas kernels, short_way(): pl.pallas_call(functools.partial(pick_kernel, here), out_shape=[shape(CAP...  2.16 us
  transfers between devices with their start and end apart: 23, of which 6 were waited for; matrix products, arithmetic and copies ran while one was open for 0% of the time, Pallas kernels for 8%

profile of v11, /device:TPU:0, one launch (start us, length us, event | category | flops | bytes accessed | tf_op | source)
XLA Modules:
  0.0 91.3 jit_solution(16972427593647031613)
XLA Ops:
  6.5 0.9 copy-done.1
  7.4 1.6 %pack_rows.1 = (bf16[96,1280]{1,0:T(8,128)(2,1)S(1)}, bf16[96,1280]{1,0:T(8,128)(2,1)S(1)}, bf16[96,1280]{1,0:T(8,128)(2,1)S(1)}, bf16[96,1280]{1,0:T(8,128)(2,1)S(1)}) custom-call(bf16[160,2304]{1,0:T(8,128)(2,1)} %vir_ref.1, bf16[160,256]{1,0:T(8,128)(2,1)} %occ_ref.1, bf16[8,32,256]{2,1,0:T(8,128)(2,1)S(1)} %copy-done.1), custom_call_target="tpu_custom_call" | custom-call | flops 300000000 | bytes 3000000 | tf_op jit(solution)/shard_map/pack_rows/pallas_call | solution.py:405
  9.0 0.5 collective-permute-start
  9.6 2.6 %collective-permute-start.1 = (bf16[96,1280]{1,0:T(8,128)(2,1)S(1)}, bf16[96,1280]{1,0:T(8,128)(2,1)S(1)}, u32[]{:S(2)}, u32[]{:S(2)}) collective-permute-start(bf16[96,1280]{1,0:T(8,128)(2,1)S(1)} %get-tuple-element.253), channel_id=1, source_target_pairs={{0,2},{1,3},{2,0},{3,1},{4,6},{5,7},{6,4},{7,5},{8,10},{9,11},{10,... | collective-permute-start | bytes 737288 | tf_op jit(solution)/shard_map/ppermute | solution.py:403
  12.9 0.7 copy-done
  13.7 12.8 %all_to_all.5.code_ref = s32[16,8,128]{2,1,0:T(8,128)S(1)} all-to-all(s32[16,8,128]{2,1,0:T(8,128)S(1)} %pack_ids.1), channel_id=1, replica_groups=mesh['groups'=2,'shell'=16] {'shell'}, dimensions={0} | all-to-all | bytes 131072 | tf_op jit(solution)/shard_map/all_to_all | solution.py:425
  26.6 2.2 %pick_rows.1 = (bf16[128,1280]{1,0:T(8,128)(2,1)S(1)}, s32[1]{0:T(128)}, s32[1]{0:T(128)}, bf16[4,16,256]{2,1,0:T(8,128)(2,1)S(1)}, bf16[4,16,256]{2,1,0:T(8,128...) custom-call(s32[16,8,128]{2,1,0:T(8,128)S(1)} %all_to_all.5.code_ref, s32[1,256]{1,0:T(1,128)} %bitcast.87, ...), custom_call_target="tpu_custom_call" | custom-call | flops 300000000 | bytes 2000000 | tf_op jit(solution)/shard_map/pick_rows/pallas_call | solution.py:427
  28.9 1.3 %collective-permute-start.4 = (bf16[128,1280]{1,0:T(8,128)(2,1)S(1)}, bf16[128,1280]{1,0:T(8,128)(2,1)S(1)}, u32[]{:S(2)}, u32[]{:S(2)}) collective-permute-start(bf16[128,1280]{1,0:T(8,128)(2,1)S(1)} %get-tuple-element.257.refs_4_.refs_0_), channel_id=1, source_target_pairs={{0,4},{1,5},{2,6},{3,7},{4,0},{5,1},{6,2},{7,3},{8,12},{9,13},{10,... | collective-permute-start | bytes 983048 | tf_op jit(solution)/shard_map/ppermute | solution.py:441
  30.2 0.7 collective-permute-start.5
  31.0 4.4 %collective-permute-start.6 = (bf16[4,16,256]{2,1,0:T(8,128)(2,1)S(1)}, bf16[4,16,256]{2,1,0:T(8,128)(2,1)S(1)}, u32[]{:S(2)}, u32[]{:S(2)}) collective-permute-start(bf16[4,16,256]{2,1,0:T(8,128)(2,1)S(1)} %get-tuple-element.258), channel_id=1, source_target_pairs={{0,4},{1,5},{2,6},{3,7},{4,0},{5,1},{6,2},{7,3},{8,12},{9,13},{10,... | collective-permute-start | bytes 98312 | tf_op jit(solution)/shard_map/ppermute | solution.py:403
  35.4 3.6 %collective-permute-done.6.refs_1_ = bf16[4,16,256]{2,1,0:T(8,128)(2,1)S(1)} collective-permute-done((bf16[4,16,256]{2,1,0:T(8,128)(2,1)S(1)}, bf16[4,16,256]{2,1,0:T(8,128)(2,1)S(1)}, u32[]{:S(2)}, u32[]{:S(2)}) %collective-permute-start.6) | collective-permute-done | bytes 32800 | tf_op jit(solution)/shard_map/ppermute | solution.py:403
  39.1 2.0 %collective-permute-start.10 = (bf16[4,16,256]{2,1,0:T(8,128)(2,1)S(1)}, bf16[4,16,256]{2,1,0:T(8,128)(2,1)S(1)}, u32[]{:S(2)}, u32[]{:S(2)}) collective-permute-start(bf16[4,16,256]{2,1,0:T(8,128)(2,1)S(1)} %get-tuple-element.261), channel_id=1, source_target_pairs={{0,8},{1,9},{2,10},{3,11},{4,12},{5,13},{6,14},{7,15},{8,0},{9,1},... | collective-permute-start | bytes 98312 | tf_op jit(solution)/shard_map/ppermute | solution.py:403
  41.1 0.9 collective-permute-start.7
  41.9 0.7 collective-permute-start.9
  42.6 1.3 %collective-permute-start.8 = (bf16[128,1280]{1,0:T(8,128)(2,1)S(1)}, bf16[128,1280]{1,0:T(8,128)(2,1)S(1)}, u32[]{:S(2)}, u32[]{:S(2)}) collective-permute-start(bf16[128,1280]{1,0:T(8,128)(2,1)S(1)} %collective-permute-done.5.inner_ref), channel_id=1, source_target_pairs={{4,0},{5,1},{6,2},{7,3},{8,12},{9,13},{10,14},{11,15},{20,16},{21,... | collective-permute-start | bytes 983048 | tf_op jit(solution)/shard_map/ppermute | solution.py:441
  44.0 0.5 collective-permute-start.13
  44.5 4.5 %collective-permute-done.7.refs_7_.refs_3_ = bf16[128,1280]{1,0:T(8,128)(2,1)S(1)} collective-permute-done((bf16[128,1280]{1,0:T(8,128)(2,1)S(1)}, bf16[128,1280]{1,0:T(8,128)(2,1)S(1)}, u32[]{:S(2)}, u32[]{:S(2)}) %collective-permute-start.7) | collective-permute-done | bytes 327712 | tf_op jit(solution)/shard_map/ppermute | solution.py:403
  49.1 5.0 %collective-permute-done.8.outer_ref = bf16[128,1280]{1,0:T(8,128)(2,1)S(1)} collective-permute-done((bf16[128,1280]{1,0:T(8,128)(2,1)S(1)}, bf16[128,1280]{1,0:T(8,128)(2,1)S(1)}, u32[]{:S(2)}, u32[]{:S(2)}) %collective-permute-start.8) | collective-permute-done | bytes 327712 | tf_op jit(solution)/shard_map/ppermute | solution.py:441
  54.1 0.8 choose_piece.2.refs_8_.refs_4_
  54.8 1.0 %collective-permute-start.14 = (bf16[128,1280]{1,0:T(8,128)(2,1)S(1)}, bf16[128,1280]{1,0:T(8,128)(2,1)S(1)}, u32[]{:S(2)}, u32[]{:S(2)}) collective-permute-start(bf16[128,1280]{1,0:T(8,128)(2,1)S(1)} %choose_piece.2.refs_8_.refs_4_), channel_id=1, source_target_pairs={{0,2},{1,3},{2,0},{3,1},{4,6},{5,7},{6,4},{7,5},{8,10},{9,11},{10,... | collective-permute-start | bytes 983048 | tf_op jit(solution)/shard_map/ppermute | solution.py:403
  55.8 1.3 %collective-permute-start.15 = (bf16[128,1280]{1,0:T(8,128)(2,1)S(1)}, bf16[128,1280]{1,0:T(8,128)(2,1)S(1)}, u32[]{:S(2)}, u32[]{:S(2)}) collective-permute-start(bf16[128,1280]{1,0:T(8,128)(2,1)S(1)} %collective-permute-done.9.inner_ref), channel_id=1, source_target_pairs={{4,0},{5,1},{6,2},{7,3},{8,12},{9,13},{10,14},{11,15},{20,16},{21,... | collective-permute-start | bytes 983048 | tf_op jit(solution)/shard_map/ppermute | solution.py:441
  57.2 0.5 collective-permute-start.18
  57.7 1.5 %collective-permute-start.16 = (bf16[4,16,256]{2,1,0:T(8,128)(2,1)S(1)}, bf16[4,16,256]{2,1,0:T(8,128)(2,1)S(1)}, u32[]{:S(2)}, u32[]{:S(2)}) collective-permute-start(bf16[4,16,256]{2,1,0:T(8,128)(2,1)S(1)} %get-tuple-element.265), channel_id=1, source_target_pairs={{0,12},{1,13},{2,14},{3,15},{4,8},{5,9},{6,10},{7,11},{8,4},{9,5},... | collective-permute-start | bytes 98312 | tf_op jit(solution)/shard_map/ppermute | solution.py:403
  59.2 4.2 %collective-permute-done.16.refs_3_ = bf16[4,16,256]{2,1,0:T(8,128)(2,1)S(1)} collective-permute-done((bf16[4,16,256]{2,1,0:T(8,128)(2,1)S(1)}, bf16[4,16,256]{2,1,0:T(8,128)(2,1)S(1)}, u32[]{:S(2)}, u32[]{:S(2)}) %collective-permute-start.16) | collective-permute-done | bytes 32800 | tf_op jit(solution)/shard_map/ppermute | solution.py:403
  63.4 2.0 %collective-permute-done.15.outer_ref = bf16[128,1280]{1,0:T(8,128)(2,1)S(1)} collective-permute-done((bf16[128,1280]{1,0:T(8,128)(2,1)S(1)}, bf16[128,1280]{1,0:T(8,128)(2,1)S(1)}, u32[]{:S(2)}, u32[]{:S(2)}) %collective-permute-start.15) | collective-permute-done | bytes 327712 | tf_op jit(solution)/shard_map/ppermute | solution.py:441
  65.5 0.9 %choose_piece.3.refs_6_ = bf16[128,1280]{1,0:T(8,128)(2,1)S(1)} custom-call(s32[1]{0:T(128)} %get-tuple-element.422.me_ref, bf16[128,1280]{1,0:T(8,128)(2,1)S(1)} %collective-permute-done.9.inner_ref, bf16[128,1280]{1,0:T(8,128)(2,1)S(1)} %collective-permute-done.15.outer_ref), custom_call_target="tpu_custom_call" | custom-call | flops 1 | bytes 1 | tf_op jit(solution)/shard_map/choose_piece/pallas_call | solution.py:444
  66.4 1.2 %collective-permute-start.19 = (bf16[128,1280]{1,0:T(8,128)(2,1)S(1)}, bf16[128,1280]{1,0:T(8,128)(2,1)S(1)}, u32[]{:S(2)}, u32[]{:S(2)}) collective-permute-start(bf16[128,1280]{1,0:T(8,128)(2,1)S(1)} %choose_piece.3.refs_6_), channel_id=1, source_target_pairs={{0,2},{1,3},{2,0},{3,1},{4,6},{5,7},{6,4},{7,5},{8,10},{9,11},{10,... | collective-permute-start | bytes 983048 | tf_op jit(solution)/shard_map/ppermute | solution.py:403
  67.6 0.5 collective-permute-start.20
  68.1 7.2 %half_transform.1 = (f32[512,1024]{1,0:T(8,128)S(1)}, bf16[2,384,1024]{2,1,0:T(8,128)(2,1)S(1)}) custom-call(s32[16,8,128]{2,1,0:T(8,128)S(1)} %all_to_all.5.code_ref, s32[1,256]{1,0:T(1,128)S(1)} %bitcast.88, bf16[4,16,256]{2,1,0:T(8,128)(2,1)S(1)} %get-tuple-element.423.refs_0_, bf16[4,16,256]{2,1,0:T(8,128)(2,1)S(1)} %collective-permute-done.6.refs_1_, ...), custom_call_target="tpu_custom_call" | custom-call | flops 7000000000 | bytes 1 | tf_op jit(solution)/shard_map/half_transform/pallas_call | solution.py:477
  75.4 1.6 %collective-permute-done.22.refs_15_ = bf16[128,1280]{1,0:T(8,128)(2,1)S(1)} collective-permute-done((bf16[128,1280]{1,0:T(8,128)(2,1)S(1)}, bf16[128,1280]{1,0:T(8,128)(2,1)S(1)}, u32[]{:S(2)}, u32[]{:S(2)}) %collective-permute-start.22) | collective-permute-done | bytes 327712 | tf_op jit(solution)/shard_map/ppermute | solution.py:403
  77.0 6.8 %last_product.1 = bf16[2,256,2304]{2,1,0:T(8,128)(2,1)} custom-call(s32[1]{0:T(128)} %get-tuple-element.422.me_ref, f32[512,1024]{1,0:T(8,128)S(1)} %get-tuple-element.283.part_any, bf16[2,384,1024]{2,1,0:T(8,128)(2,1)S(1)} %get-tuple-element.284.late_any, bf16[128,1280]{1,0:T(8,128)(2,1)S(1)} %get-tuple-element.257.refs_4_.refs_0_, ...), custom_call_target="tpu_custom_call" | custom-call | flops 20000000000 | bytes 1 | tf_op jit(solution)/shard_map/last_product/pallas_call | solution.py:506
  83.8 0.6 while.17
  (29 shorter events, 0.8 us)
Async XLA Ops:
  6.5 0.9 copy-start.1
  7.4 60.7 %copy-start.3 = (s32[256]{0:T(256)S(1)}, s32[256]{0:T(256)}, u32[]{:S(2)}) copy-start(s32[256]{0:T(256)} %param.11) | copy-start | bytes 3076
  9.0 17.5 %collective-permute-start = (bf16[96,1280]{1,0:T(8,128)(2,1)S(1)}, bf16[96,1280]{1,0:T(8,128)(2,1)S(1)}, u32[]{:S(2)}, u32[]{:S(2)}) collective-permute-start(bf16[96,1280]{1,0:T(8,128)(2,1)S(1)} %get-tuple-element.252), channel_id=1, source_target_pairs={{0,1},{1,0},{2,3},{3,2},{4,5},{5,4},{6,7},{7,6},{8,9},{9,8},{10,11... | collective-permute-start | bytes 737288 | tf_op jit(solution)/shard_map/ppermute | solution.py:403
  9.6 17.0 %collective-permute-start.1 = (bf16[96,1280]{1,0:T(8,128)(2,1)S(1)}, bf16[96,1280]{1,0:T(8,128)(2,1)S(1)}, u32[]{:S(2)}, u32[]{:S(2)}) collective-permute-start(bf16[96,1280]{1,0:T(8,128)(2,1)S(1)} %get-tuple-element.253), channel_id=1, source_target_pairs={{0,2},{1,3},{2,0},{3,1},{4,6},{5,7},{6,4},{7,5},{8,10},{9,11},{10,... | collective-permute-start | bytes 737288 | tf_op jit(solution)/shard_map/ppermute | solution.py:403
  12.2 14.4 %collective-permute-start.2 = (bf16[96,1280]{1,0:T(8,128)(2,1)S(1)}, bf16[96,1280]{1,0:T(8,128)(2,1)S(1)}, u32[]{:S(2)}, u32[]{:S(2)}) collective-permute-start(bf16[96,1280]{1,0:T(8,128)(2,1)S(1)} %get-tuple-element.254), channel_id=1, source_target_pairs={{0,3},{1,2},{2,1},{3,0},{4,7},{5,6},{6,5},{7,4},{8,11},{9,10},{10,... | collective-permute-start | bytes 737288 | tf_op jit(solution)/shard_map/ppermute | solution.py:403
  12.9 0.7 copy-start
  28.7 12.4 %collective-permute-start.3 = (bf16[128,1280]{1,0:T(8,128)(2,1)S(1)}, bf16[128,1280]{1,0:T(8,128)(2,1)S(1)}, u32[]{:S(2)}, u32[]{:S(2)}) collective-permute-start(bf16[128,1280]{1,0:T(8,128)(2,1)S(1)} %get-tuple-element.257.refs_4_.refs_0_), channel_id=1, source_target_pairs={{0,2},{1,3},{2,0},{3,1},{4,6},{5,7},{6,4},{7,5},{8,10},{9,11},{10,... | collective-permute-start | bytes 983048 | tf_op jit(solution)/shard_map/ppermute | solution.py:403
  28.9 12.2 %collective-permute-start.4 = (bf16[128,1280]{1,0:T(8,128)(2,1)S(1)}, bf16[128,1280]{1,0:T(8,128)(2,1)S(1)}, u32[]{:S(2)}, u32[]{:S(2)}) collective-permute-start(bf16[128,1280]{1,0:T(8,128)(2,1)S(1)} %get-tuple-element.257.refs_4_.refs_0_), channel_id=1, source_target_pairs={{0,4},{1,5},{2,6},{3,7},{4,0},{5,1},{6,2},{7,3},{8,12},{9,13},{10,... | collective-permute-start | bytes 983048 | tf_op jit(solution)/shard_map/ppermute | solution.py:441
  30.2 10.8 %collective-permute-start.5 = (bf16[128,1280]{1,0:T(8,128)(2,1)S(1)}, bf16[128,1280]{1,0:T(8,128)(2,1)S(1)}, u32[]{:S(2)}, u32[]{:S(2)}) collective-permute-start(bf16[128,1280]{1,0:T(8,128)(2,1)S(1)} %get-tuple-element.257.refs_4_.refs_0_), channel_id=1, source_target_pairs={{4,8},{5,9},{6,10},{7,11},{8,4},{9,5},{10,6},{11,7},{20,24},{21,25... | collective-permute-start | bytes 983048 | tf_op jit(solution)/shard_map/ppermute | solution.py:441
  30.9 13.1 %collective-permute-start.11 = (bf16[128,1280]{1,0:T(8,128)(2,1)S(1)}, bf16[128,1280]{1,0:T(8,128)(2,1)S(1)}, u32[]{:S(2)}, u32[]{:S(2)}) collective-permute-start(bf16[128,1280]{1,0:T(8,128)(2,1)S(1)} %get-tuple-element.257.refs_4_.refs_0_), channel_id=1, source_target_pairs={{0,1},{1,0},{2,3},{3,2},{4,5},{5,4},{6,7},{7,6},{8,9},{9,8},{10,11... | collective-permute-start | bytes 983048 | tf_op jit(solution)/shard_map/ppermute | solution.py:403
  31.0 8.1 %collective-permute-start.6 = (bf16[4,16,256]{2,1,0:T(8,128)(2,1)S(1)}, bf16[4,16,256]{2,1,0:T(8,128)(2,1)S(1)}, u32[]{:S(2)}, u32[]{:S(2)}) collective-permute-start(bf16[4,16,256]{2,1,0:T(8,128)(2,1)S(1)} %get-tuple-element.258), channel_id=1, source_target_pairs={{0,4},{1,5},{2,6},{3,7},{4,0},{5,1},{6,2},{7,3},{8,12},{9,13},{10,... | collective-permute-start | bytes 98312 | tf_op jit(solution)/shard_map/ppermute | solution.py:403
  39.1 4.9 %collective-permute-start.10 = (bf16[4,16,256]{2,1,0:T(8,128)(2,1)S(1)}, bf16[4,16,256]{2,1,0:T(8,128)(2,1)S(1)}, u32[]{:S(2)}, u32[]{:S(2)}) collective-permute-start(bf16[4,16,256]{2,1,0:T(8,128)(2,1)S(1)} %get-tuple-element.261), channel_id=1, source_target_pairs={{0,8},{1,9},{2,10},{3,11},{4,12},{5,13},{6,14},{7,15},{8,0},{9,1},... | collective-permute-start | bytes 98312 | tf_op jit(solution)/shard_map/ppermute | solution.py:403
  41.1 8.0 %collective-permute-start.7 = (bf16[128,1280]{1,0:T(8,128)(2,1)S(1)}, bf16[128,1280]{1,0:T(8,128)(2,1)S(1)}, u32[]{:S(2)}, u32[]{:S(2)}) collective-permute-start(bf16[128,1280]{1,0:T(8,128)(2,1)S(1)} %collective-permute-done.4.refs_6_.refs_2_), channel_id=1, source_target_pairs={{0,2},{1,3},{2,0},{3,1},{4,6},{5,7},{6,4},{7,5},{8,10},{9,11},{10,... | collective-permute-start | bytes 983048 | tf_op jit(solution)/shard_map/ppermute | solution.py:403
  41.9 12.1 %collective-permute-start.9 = (bf16[128,1280]{1,0:T(8,128)(2,1)S(1)}, bf16[128,1280]{1,0:T(8,128)(2,1)S(1)}, u32[]{:S(2)}, u32[]{:S(2)}) collective-permute-start(bf16[128,1280]{1,0:T(8,128)(2,1)S(1)} %collective-permute-done.4.refs_6_.refs_2_), channel_id=1, source_target_pairs={{4,8},{5,9},{6,10},{7,11},{8,4},{9,5},{10,6},{11,7},{20,24},{21,25... | collective-permute-start | bytes 983048 | tf_op jit(solution)/shard_map/ppermute | solution.py:441
  42.6 11.4 %collective-permute-start.8 = (bf16[128,1280]{1,0:T(8,128)(2,1)S(1)}, bf16[128,1280]{1,0:T(8,128)(2,1)S(1)}, u32[]{:S(2)}, u32[]{:S(2)}) collective-permute-start(bf16[128,1280]{1,0:T(8,128)(2,1)S(1)} %collective-permute-done.5.inner_ref), channel_id=1, source_target_pairs={{4,0},{5,1},{6,2},{7,3},{8,12},{9,13},{10,14},{11,15},{20,16},{21,... | collective-permute-start | bytes 983048 | tf_op jit(solution)/shard_map/ppermute | solution.py:441
  43.9 10.1 %collective-permute-start.12 = (bf16[128,1280]{1,0:T(8,128)(2,1)S(1)}, bf16[128,1280]{1,0:T(8,128)(2,1)S(1)}, u32[]{:S(2)}, u32[]{:S(2)}) collective-permute-start(bf16[128,1280]{1,0:T(8,128)(2,1)S(1)} %collective-permute-done.3.refs_5_.refs_1_), channel_id=1, source_target_pairs={{0,1},{1,0},{2,3},{3,2},{4,5},{5,4},{6,7},{7,6},{8,9},{9,8},{10,11... | collective-permute-start | bytes 983048 | tf_op jit(solution)/shard_map/ppermute | solution.py:403
  44.0 10.0 %collective-permute-start.13 = (bf16[128,1280]{1,0:T(8,128)(2,1)S(1)}, bf16[128,1280]{1,0:T(8,128)(2,1)S(1)}, u32[]{:S(2)}, u32[]{:S(2)}) collective-permute-start(bf16[128,1280]{1,0:T(8,128)(2,1)S(1)} %collective-permute-done.4.refs_6_.refs_2_), channel_id=1, source_target_pairs={{0,1},{1,0},{2,3},{3,2},{4,5},{5,4},{6,7},{7,6},{8,9},{9,8},{10,11... | collective-permute-start | bytes 983048 | tf_op jit(solution)/shard_map/ppermute | solution.py:403
  54.8 8.6 %collective-permute-start.14 = (bf16[128,1280]{1,0:T(8,128)(2,1)S(1)}, bf16[128,1280]{1,0:T(8,128)(2,1)S(1)}, u32[]{:S(2)}, u32[]{:S(2)}) collective-permute-start(bf16[128,1280]{1,0:T(8,128)(2,1)S(1)} %choose_piece.2.refs_8_.refs_4_), channel_id=1, source_target_pairs={{0,2},{1,3},{2,0},{3,1},{4,6},{5,7},{6,4},{7,5},{8,10},{9,11},{10,... | collective-permute-start | bytes 983048 | tf_op jit(solution)/shard_map/ppermute | solution.py:403
  55.8 9.7 %collective-permute-start.15 = (bf16[128,1280]{1,0:T(8,128)(2,1)S(1)}, bf16[128,1280]{1,0:T(8,128)(2,1)S(1)}, u32[]{:S(2)}, u32[]{:S(2)}) collective-permute-start(bf16[128,1280]{1,0:T(8,128)(2,1)S(1)} %collective-permute-done.9.inner_ref), channel_id=1, source_target_pairs={{4,0},{5,1},{6,2},{7,3},{8,12},{9,13},{10,14},{11,15},{20,16},{21,... | collective-permute-start | bytes 983048 | tf_op jit(solution)/shard_map/ppermute | solution.py:441
  57.1 8.4 %collective-permute-start.17 = (bf16[128,1280]{1,0:T(8,128)(2,1)S(1)}, bf16[128,1280]{1,0:T(8,128)(2,1)S(1)}, u32[]{:S(2)}, u32[]{:S(2)}) collective-permute-start(bf16[128,1280]{1,0:T(8,128)(2,1)S(1)} %collective-permute-done.7.refs_7_.refs_3_), channel_id=1, source_target_pairs={{0,1},{1,0},{2,3},{3,2},{4,5},{5,4},{6,7},{7,6},{8,9},{9,8},{10,11... | collective-permute-start | bytes 983048 | tf_op jit(solution)/shard_map/ppermute | solution.py:403
  57.2 8.3 %collective-permute-start.18 = (bf16[128,1280]{1,0:T(8,128)(2,1)S(1)}, bf16[128,1280]{1,0:T(8,128)(2,1)S(1)}, u32[]{:S(2)}, u32[]{:S(2)}) collective-permute-start(bf16[128,1280]{1,0:T(8,128)(2,1)S(1)} %choose_piece.2.refs_8_.refs_4_), channel_id=1, source_target_pairs={{0,1},{1,0},{2,3},{3,2},{4,5},{5,4},{6,7},{7,6},{8,9},{9,8},{10,11... | collective-permute-start | bytes 983048 | tf_op jit(solution)/shard_map/ppermute | solution.py:403
  57.7 5.8 %collective-permute-start.16 = (bf16[4,16,256]{2,1,0:T(8,128)(2,1)S(1)}, bf16[4,16,256]{2,1,0:T(8,128)(2,1)S(1)}, u32[]{:S(2)}, u32[]{:S(2)}) collective-permute-start(bf16[4,16,256]{2,1,0:T(8,128)(2,1)S(1)} %get-tuple-element.265), channel_id=1, source_target_pairs={{0,12},{1,13},{2,14},{3,15},{4,8},{5,9},{6,10},{7,11},{8,4},{9,5},... | collective-permute-start | bytes 98312 | tf_op jit(solution)/shard_map/ppermute | solution.py:403
  66.4 8.9 %collective-permute-start.19 = (bf16[128,1280]{1,0:T(8,128)(2,1)S(1)}, bf16[128,1280]{1,0:T(8,128)(2,1)S(1)}, u32[]{:S(2)}, u32[]{:S(2)}) collective-permute-start(bf16[128,1280]{1,0:T(8,128)(2,1)S(1)} %choose_piece.3.refs_6_), channel_id=1, source_target_pairs={{0,2},{1,3},{2,0},{3,1},{4,6},{5,7},{6,4},{7,5},{8,10},{9,11},{10,... | collective-permute-start | bytes 983048 | tf_op jit(solution)/shard_map/ppermute | solution.py:403
  67.6 7.7 %collective-permute-start.21 = (bf16[128,1280]{1,0:T(8,128)(2,1)S(1)}, bf16[128,1280]{1,0:T(8,128)(2,1)S(1)}, u32[]{:S(2)}, u32[]{:S(2)}) collective-permute-start(bf16[128,1280]{1,0:T(8,128)(2,1)S(1)} %choose_piece.3.refs_6_), channel_id=1, source_target_pairs={{0,1},{1,0},{2,3},{3,2},{4,5},{5,4},{6,7},{7,6},{8,9},{9,8},{10,11... | collective-permute-start | bytes 983048 | tf_op jit(solution)/shard_map/ppermute | solution.py:403
  67.6 7.7 %collective-permute-start.20 = (bf16[128,1280]{1,0:T(8,128)(2,1)S(1)}, bf16[128,1280]{1,0:T(8,128)(2,1)S(1)}, u32[]{:S(2)}, u32[]{:S(2)}) collective-permute-start(bf16[128,1280]{1,0:T(8,128)(2,1)S(1)} %collective-permute-done.14.refs_5_), channel_id=1, source_target_pairs={{0,1},{1,0},{2,3},{3,2},{4,5},{5,4},{6,7},{7,6},{8,9},{9,8},{10,11... | collective-permute-start | bytes 983048 | tf_op jit(solution)/shard_map/ppermute | solution.py:403
  75.4 1.7 %collective-permute-start.22 = (bf16[128,1280]{1,0:T(8,128)(2,1)S(1)}, bf16[128,1280]{1,0:T(8,128)(2,1)S(1)}, u32[]{:S(2)}, u32[]{:S(2)}) collective-permute-start(bf16[128,1280]{1,0:T(8,128)(2,1)S(1)} %collective-permute-done.19.refs_7_), channel_id=1, source_target_pairs={{0,1},{1,0},{2,3},{3,2},{4,5},{5,4},{6,7},{7,6},{8,9},{9,8},{10,11... | collective-permute-start | bytes 983048 | tf_op jit(solution)/shard_map/ppermute | solution.py:403

commit v12 on v11

--- a/solution.py
+++ b/solution.py
@@ -208,30 +208,9 @@
         out_ref[:, column] = total.astype(BF16)
 
 
-def inner_chip(chip):
-    z = lax.div(chip, Y)
-    return (z == 1) | (z == 2)
-
-
 def slot_of(window, chip):
     slot = window ^ chip
-    return jnp.where(inner_chip(chip) & (slot >= 2 * Y), slot ^ Y, slot)
-
-
-def choose_kernel(me_ref, inner_ref, outer_ref, out_ref, sem):
-    inner = inner_chip(lax.div(me_ref[0], CORES))
-
-    @pl.when(inner)
-    def _():
-        copy = pltpu.make_async_copy(inner_ref, out_ref, sem)
-        copy.start()
-        copy.wait()
-
-    @pl.when(jnp.logical_not(inner))
-    def _():
-        copy = pltpu.make_async_copy(outer_ref, out_ref, sem)
-        copy.start()
-        copy.wait()
+    return jnp.where((slot == 3) | (slot == 4), slot ^ 7, slot)
 
 
 def half_kernel(here, early, code_ref, size_ref, *refs):
@@ -435,43 +414,16 @@
         name="pick_rows",
     )(code, size_row, keep, to_core, to_y, to_both)
 
-    ends, middle, outward = [(0, 1), (1, 0), (2, 3), (3, 2)], [(1, 2), (2, 1)], [(1, 0), (2, 3)]
-
-    def hop(array, steps):
-        return lax.ppermute(array, "shell", [(4 * a + k, 4 * b + k) for a, b in steps for k in range(4)])
-
-    def choose(inner, outer):
-        return pl.pallas_call(
-            choose_kernel,
-            out_shape=shape(*inner.shape),
-            in_specs=[SMEM, ANY, ANY],
-            out_specs=ANY,
-            scratch_shapes=[pltpu.SemaphoreType.DMA],
-            compiler_params=params(4),
-            cost_estimate=cost(1, 1),
-            name="choose_piece",
-        )(me, inner, outer)
-
-    mine_y, beside, across = swap(mine, 2), hop(mine, ends), hop(mine, middle)
-    panel[1] = swap(panel[1], 4)
-    mine_y, beside, across, panel[1] = lax.optimization_barrier((mine_y, beside, across, panel[1]))
-
-    beside_y, across_out, corner = swap(beside, 2), hop(across, outward), hop(beside, middle)
-    far = [swap(piece, 1) for piece in (mine, mine_y, beside)]
-    panel[2] = swap(panel[2], 8)
-    beside_y, across_out, corner, panel[2], *far = lax.optimization_barrier(
-        (beside_y, across_out, corner, panel[2], *far)
-    )
-
-    across = choose(across, across_out)
-    across_y, corner_out = swap(across, 2), hop(corner, outward)
-    far += [swap(piece, 1) for piece in (beside_y, across)]
-    panel[3] = swap(panel[3], 12)
-    across_y, corner_out, panel[3], *far = lax.optimization_barrier((across_y, corner_out, panel[3], *far))
-
-    corner = choose(corner, corner_out)
+    across, mine_y, beside = swap(mine, 8), swap(mine, 2), swap(mine, 4)
+    far = [swap(mine, 1), swap(mine_y, 1), swap(beside, 1)]
+    across, mine_y, beside, *far = lax.optimization_barrier((across, mine_y, beside, *far))
+
+    corner, beside_y, across_y = swap(across, 4), swap(beside, 2), swap(across, 2)
+    panel = [panel[0]] + [swap(panel[r], 4 * r) for r in range(1, Z)]
+    corner, *panel = lax.optimization_barrier((corner, *panel))
+
     corner_y = swap(corner, 2)
-    near = [mine, mine_y, beside, beside_y, across]
+    near = [mine, mine_y, beside]
     early = len(near)
     slots = LIVE_DEV * n * EDGE
     half, late = pl.pallas_call(
@@ -495,9 +447,11 @@
         cost_estimate=cost(7e9, 1),
         name="half_transform",
     )(code, size_row, *panel, *near, *far)
-    near += [across_y, corner]
-    far += [swap(piece, 1) for piece in near[early:]]
-    corner_y, half, late, *far = lax.optimization_barrier((corner_y, half, late, *far))
+    far.append(swap(across, 1))
+    beside_y, across_y, half, late, *far = lax.optimization_barrier((beside_y, across_y, half, late, *far))
+    near += [across, beside_y, across_y, corner]
+    far += [swap(piece, 1) for piece in near[early + 1 :]]
+    corner_y, *far = lax.optimization_barrier((corner_y, *far))
     near.append(corner_y)
     far.append(swap(corner_y, 1))
 

time: 91.6 us -> 95.1 us (1.038)
  waiting for transfers between devices: 21.1 us -> 29.8 us
  starting transfers between devices: 21.4 us -> 15.8 us
    ppermute x18 -> x21, waiting for transfers between devices: 14.1 us -> 29.8 us  [swap(): return lax.ppermute(array, 'shell', [(i, i ^ bit) for i in range(n)])]
    ppermute x5 -> x0, waiting for transfers between devices: 7.04 us -> none  [hop(): lax.ppermute(array, 'shell', [(4 * a + k, 4 * b + k) for a, b in steps fo...]
    ppermute x5 -> x0, starting transfers between devices: 5.25 us -> none  [hop(): lax.ppermute(array, 'shell', [(4 * a + k, 4 * b + k) for a, b in steps fo...]
    pallas_call x2 -> x0, Pallas kernels: 1.71 us -> none  [choose(): pl.pallas_call(choose_kernel, out_shape=shape(*inner.shape), in_specs=[SM...]
    pallas_call x1, Pallas kernels: 7.19 us -> 8.79 us  [short_way(): pl.pallas_call(functools.partial(half_kernel, here, early), out_shape=(sh...]
    ppermute x18 -> x21, starting transfers between devices: 16.1 us -> 15.8 us  [swap(): return lax.ppermute(array, 'shell', [(i, i ^ bit) for i in range(n)])]
  transfers between devices with their start and end apart: 23 -> 21, of which waited for: 6 -> 7; matrix products, arithmetic and copies ran while one was open for 0% -> 0% of each run, Pallas kernels for 8% -> 9%
where the time goes in v12:
time: 95.1 us; the launch traced here: 94.8 us
  waiting for transfers between devices  29.8 us (31%)
  Pallas kernels  20.1 us (21%)
  starting transfers between devices  15.8 us (17%)
  between operations  14.1 us (15%)
  blocking collectives  12.8 us (13%)
  local copies, waits for them, and re-layouts  1.58 us (2%)
    ppermute x21, waiting for transfers between devices, swap(): return lax.ppermute(array, 'shell', [(i, i ^ bit) for i in range(n)])  29.8 us
    ppermute x21, starting transfers between devices, swap(): return lax.ppermute(array, 'shell', [(i, i ^ bit) for i in range(n)])  15.8 us
    all_to_all x1, blocking collectives, short_way(): lax.all_to_all(code, 'shell', split_axis=0, concat_axis=0, tiled=True)  12.8 us
    pallas_call x1, Pallas kernels, short_way(): pl.pallas_call(functools.partial(half_kernel, here, early), out_shape=(sh...  8.79 us
    pallas_call x1, Pallas kernels, short_way(): pl.pallas_call(functools.partial(last_kernel, count, early), out_shape=sh...  7.38 us
    pallas_call x1, Pallas kernels, short_way(): pl.pallas_call(functools.partial(pick_kernel, here), out_shape=[shape(CAP...  2.16 us
  transfers between devices with their start and end apart: 21, of which 7 were waited for; matrix products, arithmetic and copies ran while one was open for 0% of the time, Pallas kernels for 9%

profile of v12, /device:TPU:0, one launch (start us, length us, event | category | flops | bytes accessed | tf_op | source)
XLA Modules:
  0.0 94.8 jit_solution(12263717442485893506)
XLA Ops:
  6.5 0.9 copy-done.1
  7.4 1.6 %pack_rows.1 = (bf16[96,1280]{1,0:T(8,128)(2,1)S(1)}, bf16[96,1280]{1,0:T(8,128)(2,1)S(1)}, bf16[96,1280]{1,0:T(8,128)(2,1)S(1)}, bf16[96,1280]{1,0:T(8,128)(2,1)S(1)}) custom-call(bf16[160,2304]{1,0:T(8,128)(2,1)} %vir_ref.1, bf16[160,256]{1,0:T(8,128)(2,1)} %occ_ref.1, bf16[8,32,256]{2,1,0:T(8,128)(2,1)S(1)} %copy-done.1), custom_call_target="tpu_custom_call" | custom-call | flops 300000000 | bytes 3000000 | tf_op jit(solution)/shard_map/pack_rows/pallas_call | solution.py:384
  9.0 0.5 collective-permute-start
  9.5 2.6 %collective-permute-start.1 = (bf16[96,1280]{1,0:T(8,128)(2,1)S(1)}, bf16[96,1280]{1,0:T(8,128)(2,1)S(1)}, u32[]{:S(2)}, u32[]{:S(2)}) collective-permute-start(bf16[96,1280]{1,0:T(8,128)(2,1)S(1)} %get-tuple-element.251), channel_id=1, source_target_pairs={{0,2},{1,3},{2,0},{3,1},{4,6},{5,7},{6,4},{7,5},{8,10},{9,11},{10,... | collective-permute-start | bytes 737288 | tf_op jit(solution)/shard_map/ppermute | solution.py:382
  12.1 0.1 collective-permute-start.2
  12.9 0.0 copy-start
  12.9 0.7 copy-done
  13.5 0.2 pack_ids.1
  13.7 12.8 %all_to_all.5.code_ref = s32[16,8,128]{2,1,0:T(8,128)S(1)} all-to-all(s32[16,8,128]{2,1,0:T(8,128)S(1)} %pack_ids.1), channel_id=1, replica_groups=mesh['groups'=2,'shell'=16] {'shell'}, dimensions={0} | all-to-all | bytes 131072 | tf_op jit(solution)/shard_map/all_to_all | solution.py:404
  26.5 2.2 %pick_rows.1 = (bf16[128,1280]{1,0:T(8,128)(2,1)S(1)}, s32[1]{0:T(128)}, s32[1]{0:T(128)}, bf16[4,16,256]{2,1,0:T(8,128)(2,1)S(1)}, bf16[4,16,256]{2,1,0:T(8,128...) custom-call(s32[16,8,128]{2,1,0:T(8,128)S(1)} %all_to_all.5.code_ref, s32[1,256]{1,0:T(1,128)} %bitcast.87, ...), custom_call_target="tpu_custom_call" | custom-call | flops 300000000 | bytes 2000000 | tf_op jit(solution)/shard_map/pick_rows/pallas_call | solution.py:406
  28.7 0.2 collective-permute-start.4
  28.9 1.3 %collective-permute-start.5 = (bf16[128,1280]{1,0:T(8,128)(2,1)S(1)}, bf16[128,1280]{1,0:T(8,128)(2,1)S(1)}, u32[]{:S(2)}, u32[]{:S(2)}) collective-permute-start(bf16[128,1280]{1,0:T(8,128)(2,1)S(1)} %get-tuple-element.255.refs_4_.refs_0_), channel_id=1, source_target_pairs={{0,4},{1,5},{2,6},{3,7},{4,0},{5,1},{6,2},{7,3},{8,12},{9,13},{10,... | collective-permute-start | bytes 983048 | tf_op jit(solution)/shard_map/ppermute | solution.py:382
  30.2 2.6 %collective-permute-start.3 = (bf16[128,1280]{1,0:T(8,128)(2,1)S(1)}, bf16[128,1280]{1,0:T(8,128)(2,1)S(1)}, u32[]{:S(2)}, u32[]{:S(2)}) collective-permute-start(bf16[128,1280]{1,0:T(8,128)(2,1)S(1)} %get-tuple-element.255.refs_4_.refs_0_), channel_id=1, source_target_pairs={{0,8},{1,9},{2,10},{3,11},{4,12},{5,13},{6,14},{7,15},{8,0},{9,1},... | collective-permute-start | bytes 983048 | tf_op jit(solution)/shard_map/ppermute | solution.py:382
  32.8 5.1 %collective-permute-done.4.refs_5_.refs_1_ = bf16[128,1280]{1,0:T(8,128)(2,1)S(1)} collective-permute-done((bf16[128,1280]{1,0:T(8,128)(2,1)S(1)}, bf16[128,1280]{1,0:T(8,128)(2,1)S(1)}, u32[]{:S(2)}, u32[]{:S(2)}) %collective-permute-start.4) | collective-permute-done | bytes 327712 | tf_op jit(solution)/shard_map/ppermute | solution.py:382
  38.0 7.3 %collective-permute-done.5.refs_6_.refs_2_ = bf16[128,1280]{1,0:T(8,128)(2,1)S(1)} collective-permute-done((bf16[128,1280]{1,0:T(8,128)(2,1)S(1)}, bf16[128,1280]{1,0:T(8,128)(2,1)S(1)}, u32[]{:S(2)}, u32[]{:S(2)}) %collective-permute-start.5) | collective-permute-done | bytes 327712 | tf_op jit(solution)/shard_map/ppermute | solution.py:382
  45.3 1.8 %collective-permute-done.3.refs_3_ = bf16[128,1280]{1,0:T(8,128)(2,1)S(1)} collective-permute-done((bf16[128,1280]{1,0:T(8,128)(2,1)S(1)}, bf16[128,1280]{1,0:T(8,128)(2,1)S(1)}, u32[]{:S(2)}, u32[]{:S(2)}) %collective-permute-start.3) | collective-permute-done | bytes 327712 | tf_op jit(solution)/shard_map/ppermute | solution.py:382
  47.0 0.5 collective-permute-start.11
  47.6 1.6 %collective-permute-start.12 = (bf16[4,16,256]{2,1,0:T(8,128)(2,1)S(1)}, bf16[4,16,256]{2,1,0:T(8,128)(2,1)S(1)}, u32[]{:S(2)}, u32[]{:S(2)}) collective-permute-start(bf16[4,16,256]{2,1,0:T(8,128)(2,1)S(1)} %get-tuple-element.259), channel_id=1, source_target_pairs={{0,4},{1,5},{2,6},{3,7},{4,0},{5,1},{6,2},{7,3},{8,12},{9,13},{10,... | collective-permute-start | bytes 98312 | tf_op jit(solution)/shard_map/ppermute | solution.py:382
  49.1 1.1 %collective-permute-start.13 = (bf16[4,16,256]{2,1,0:T(8,128)(2,1)S(1)}, bf16[4,16,256]{2,1,0:T(8,128)(2,1)S(1)}, u32[]{:S(2)}, u32[]{:S(2)}) collective-permute-start(bf16[4,16,256]{2,1,0:T(8,128)(2,1)S(1)} %get-tuple-element.260), channel_id=1, source_target_pairs={{0,8},{1,9},{2,10},{3,11},{4,12},{5,13},{6,14},{7,15},{8,0},{9,1},... | collective-permute-start | bytes 98312 | tf_op jit(solution)/shard_map/ppermute | solution.py:382
  50.2 1.7 %collective-permute-start.14 = (bf16[4,16,256]{2,1,0:T(8,128)(2,1)S(1)}, bf16[4,16,256]{2,1,0:T(8,128)(2,1)S(1)}, u32[]{:S(2)}, u32[]{:S(2)}) collective-permute-start(bf16[4,16,256]{2,1,0:T(8,128)(2,1)S(1)} %get-tuple-element.261), channel_id=1, source_target_pairs={{0,12},{1,13},{2,14},{3,15},{4,8},{5,9},{6,10},{7,11},{8,4},{9,5},... | collective-permute-start | bytes 98312 | tf_op jit(solution)/shard_map/ppermute | solution.py:382
  51.9 0.8 collective-permute-start.10
  52.7 5.6 %collective-permute-done.12.refs_1_ = bf16[4,16,256]{2,1,0:T(8,128)(2,1)S(1)} collective-permute-done((bf16[4,16,256]{2,1,0:T(8,128)(2,1)S(1)}, bf16[4,16,256]{2,1,0:T(8,128)(2,1)S(1)}, u32[]{:S(2)}, u32[]{:S(2)}) %collective-permute-start.12) | collective-permute-done | bytes 32800 | tf_op jit(solution)/shard_map/ppermute | solution.py:382
  58.4 1.1 %collective-permute-start.9 = (bf16[128,1280]{1,0:T(8,128)(2,1)S(1)}, bf16[128,1280]{1,0:T(8,128)(2,1)S(1)}, u32[]{:S(2)}, u32[]{:S(2)}) collective-permute-start(bf16[128,1280]{1,0:T(8,128)(2,1)S(1)} %collective-permute-done.5.refs_6_.refs_2_), channel_id=1, source_target_pairs={{0,2},{1,3},{2,0},{3,1},{4,6},{5,7},{6,4},{7,5},{8,10},{9,11},{10,... | collective-permute-start | bytes 983048 | tf_op jit(solution)/shard_map/ppermute | solution.py:382
  59.5 8.8 %half_transform.1 = (f32[512,1024]{1,0:T(8,128)S(1)}, bf16[2,640,1024]{2,1,0:T(8,128)(2,1)S(1)}) custom-call(s32[16,8,128]{2,1,0:T(8,128)S(1)} %all_to_all.5.code_ref, s32[1,256]{1,0:T(1,128)} %bitcast.88, bf16[4,16,256]{2,1,0:T(8,128)(2,1)S(1)} %get-tuple-element.419.refs_0_, bf16[4,16,256]{2,1,0:T(8,128)(2,1)S(1)} %collective-permute-done.12.refs_1_, ...), custom_call_target="tpu_custom_call" | custom-call | flops 7000000000 | bytes 1 | tf_op jit(solution)/shard_map/half_transform/pallas_call | solution.py:429
  68.3 0.2 collective-permute-done.9.refs_4_
  68.5 1.1 %collective-permute-start.16 = (bf16[128,1280]{1,0:T(8,128)(2,1)S(1)}, bf16[128,1280]{1,0:T(8,128)(2,1)S(1)}, u32[]{:S(2)}, u32[]{:S(2)}) collective-permute-start(bf16[128,1280]{1,0:T(8,128)(2,1)S(1)} %collective-permute-done.11.refs_6_), channel_id=1, source_target_pairs={{0,2},{1,3},{2,0},{3,1},{4,6},{5,7},{6,4},{7,5},{8,10},{9,11},{10,... | collective-permute-start | bytes 983048 | tf_op jit(solution)/shard_map/ppermute | solution.py:382
  69.6 0.5 collective-permute-start.18
  70.2 8.1 %collective-permute-done.16.refs_7_ = bf16[128,1280]{1,0:T(8,128)(2,1)S(1)} collective-permute-done((bf16[128,1280]{1,0:T(8,128)(2,1)S(1)}, bf16[128,1280]{1,0:T(8,128)(2,1)S(1)}, u32[]{:S(2)}, u32[]{:S(2)}) %collective-permute-start.16) | collective-permute-done | bytes 327712 | tf_op jit(solution)/shard_map/ppermute | solution.py:382
  78.3 0.1 collective-permute-start.20
  78.4 1.6 %collective-permute-done.20.refs_15_ = bf16[128,1280]{1,0:T(8,128)(2,1)S(1)} collective-permute-done((bf16[128,1280]{1,0:T(8,128)(2,1)S(1)}, bf16[128,1280]{1,0:T(8,128)(2,1)S(1)}, u32[]{:S(2)}, u32[]{:S(2)}) %collective-permute-start.20) | collective-permute-done | bytes 327712 | tf_op jit(solution)/shard_map/ppermute | solution.py:382
  80.0 7.4 %last_product.1 = bf16[2,256,2304]{2,1,0:T(8,128)(2,1)} custom-call(s32[1]{0:T(128)} %get-tuple-element.418.me_ref, f32[512,1024]{1,0:T(8,128)S(1)} %get-tuple-element.272.part_any, bf16[2,640,1024]{2,1,0:T(8,128)(2,1)S(1)} %get-tuple-element.273.late_any, bf16[128,1280]{1,0:T(8,128)(2,1)S(1)} %get-tuple-element.255.refs_4_.refs_0_, ...), custom_call_target="tpu_custom_call" | custom-call | flops 20000000000 | bytes 1 | tf_op jit(solution)/shard_map/last_product/pallas_call | solution.py:460
  87.4 0.6 while.17
  (23 shorter events, 0.1 us)
Async XLA Ops:
  6.5 0.9 copy-start.1
  9.0 17.5 %collective-permute-start = (bf16[96,1280]{1,0:T(8,128)(2,1)S(1)}, bf16[96,1280]{1,0:T(8,128)(2,1)S(1)}, u32[]{:S(2)}, u32[]{:S(2)}) collective-permute-start(bf16[96,1280]{1,0:T(8,128)(2,1)S(1)} %get-tuple-element.250), channel_id=1, source_target_pairs={{0,1},{1,0},{2,3},{3,2},{4,5},{5,4},{6,7},{7,6},{8,9},{9,8},{10,11... | collective-permute-start | bytes 737288 | tf_op jit(solution)/shard_map/ppermute | solution.py:382
  9.5 17.0 %collective-permute-start.1 = (bf16[96,1280]{1,0:T(8,128)(2,1)S(1)}, bf16[96,1280]{1,0:T(8,128)(2,1)S(1)}, u32[]{:S(2)}, u32[]{:S(2)}) collective-permute-start(bf16[96,1280]{1,0:T(8,128)(2,1)S(1)} %get-tuple-element.251), channel_id=1, source_target_pairs={{0,2},{1,3},{2,0},{3,1},{4,6},{5,7},{6,4},{7,5},{8,10},{9,11},{10,... | collective-permute-start | bytes 737288 | tf_op jit(solution)/shard_map/ppermute | solution.py:382
  12.1 14.4 %collective-permute-start.2 = (bf16[96,1280]{1,0:T(8,128)(2,1)S(1)}, bf16[96,1280]{1,0:T(8,128)(2,1)S(1)}, u32[]{:S(2)}, u32[]{:S(2)}) collective-permute-start(bf16[96,1280]{1,0:T(8,128)(2,1)S(1)} %get-tuple-element.252), channel_id=1, source_target_pairs={{0,3},{1,2},{2,1},{3,0},{4,7},{5,6},{6,5},{7,4},{8,11},{9,10},{10,... | collective-permute-start | bytes 737288 | tf_op jit(solution)/shard_map/ppermute | solution.py:382
  12.9 0.7 copy-start
  28.7 9.2 %collective-permute-start.4 = (bf16[128,1280]{1,0:T(8,128)(2,1)S(1)}, bf16[128,1280]{1,0:T(8,128)(2,1)S(1)}, u32[]{:S(2)}, u32[]{:S(2)}) collective-permute-start(bf16[128,1280]{1,0:T(8,128)(2,1)S(1)} %get-tuple-element.255.refs_4_.refs_0_), channel_id=1, source_target_pairs={{0,2},{1,3},{2,0},{3,1},{4,6},{5,7},{6,4},{7,5},{8,10},{9,11},{10,... | collective-permute-start | bytes 983048 | tf_op jit(solution)/shard_map/ppermute | solution.py:382
  28.9 16.4 %collective-permute-start.5 = (bf16[128,1280]{1,0:T(8,128)(2,1)S(1)}, bf16[128,1280]{1,0:T(8,128)(2,1)S(1)}, u32[]{:S(2)}, u32[]{:S(2)}) collective-permute-start(bf16[128,1280]{1,0:T(8,128)(2,1)S(1)} %get-tuple-element.255.refs_4_.refs_0_), channel_id=1, source_target_pairs={{0,4},{1,5},{2,6},{3,7},{4,0},{5,1},{6,2},{7,3},{8,12},{9,13},{10,... | collective-permute-start | bytes 983048 | tf_op jit(solution)/shard_map/ppermute | solution.py:382
  30.2 16.8 %collective-permute-start.3 = (bf16[128,1280]{1,0:T(8,128)(2,1)S(1)}, bf16[128,1280]{1,0:T(8,128)(2,1)S(1)}, u32[]{:S(2)}, u32[]{:S(2)}) collective-permute-start(bf16[128,1280]{1,0:T(8,128)(2,1)S(1)} %get-tuple-element.255.refs_4_.refs_0_), channel_id=1, source_target_pairs={{0,8},{1,9},{2,10},{3,11},{4,12},{5,13},{6,14},{7,15},{8,0},{9,1},... | collective-permute-start | bytes 983048 | tf_op jit(solution)/shard_map/ppermute | solution.py:382
  32.8 14.2 %collective-permute-start.6 = (bf16[128,1280]{1,0:T(8,128)(2,1)S(1)}, bf16[128,1280]{1,0:T(8,128)(2,1)S(1)}, u32[]{:S(2)}, u32[]{:S(2)}) collective-permute-start(bf16[128,1280]{1,0:T(8,128)(2,1)S(1)} %get-tuple-element.255.refs_4_.refs_0_), channel_id=1, source_target_pairs={{0,1},{1,0},{2,3},{3,2},{4,5},{5,4},{6,7},{7,6},{8,9},{9,8},{10,11... | collective-permute-start | bytes 983048 | tf_op jit(solution)/shard_map/ppermute | solution.py:382
  38.0 9.1 %collective-permute-start.7 = (bf16[128,1280]{1,0:T(8,128)(2,1)S(1)}, bf16[128,1280]{1,0:T(8,128)(2,1)S(1)}, u32[]{:S(2)}, u32[]{:S(2)}) collective-permute-start(bf16[128,1280]{1,0:T(8,128)(2,1)S(1)} %collective-permute-done.4.refs_5_.refs_1_), channel_id=1, source_target_pairs={{0,1},{1,0},{2,3},{3,2},{4,5},{5,4},{6,7},{7,6},{8,9},{9,8},{10,11... | collective-permute-start | bytes 983048 | tf_op jit(solution)/shard_map/ppermute | solution.py:382
  45.2 1.8 %collective-permute-start.8 = (bf16[128,1280]{1,0:T(8,128)(2,1)S(1)}, bf16[128,1280]{1,0:T(8,128)(2,1)S(1)}, u32[]{:S(2)}, u32[]{:S(2)}) collective-permute-start(bf16[128,1280]{1,0:T(8,128)(2,1)S(1)} %collective-permute-done.5.refs_6_.refs_2_), channel_id=1, source_target_pairs={{0,1},{1,0},{2,3},{3,2},{4,5},{5,4},{6,7},{7,6},{8,9},{9,8},{10,11... | collective-permute-start | bytes 983048 | tf_op jit(solution)/shard_map/ppermute | solution.py:382
  47.0 12.5 %collective-permute-start.11 = (bf16[128,1280]{1,0:T(8,128)(2,1)S(1)}, bf16[128,1280]{1,0:T(8,128)(2,1)S(1)}, u32[]{:S(2)}, u32[]{:S(2)}) collective-permute-start(bf16[128,1280]{1,0:T(8,128)(2,1)S(1)} %collective-permute-done.3.refs_3_), channel_id=1, source_target_pairs={{0,4},{1,5},{2,6},{3,7},{4,0},{5,1},{6,2},{7,3},{8,12},{9,13},{10,... | collective-permute-start | bytes 983048 | tf_op jit(solution)/shard_map/ppermute | solution.py:382
  47.6 10.8 %collective-permute-start.12 = (bf16[4,16,256]{2,1,0:T(8,128)(2,1)S(1)}, bf16[4,16,256]{2,1,0:T(8,128)(2,1)S(1)}, u32[]{:S(2)}, u32[]{:S(2)}) collective-permute-start(bf16[4,16,256]{2,1,0:T(8,128)(2,1)S(1)} %get-tuple-element.259), channel_id=1, source_target_pairs={{0,4},{1,5},{2,6},{3,7},{4,0},{5,1},{6,2},{7,3},{8,12},{9,13},{10,... | collective-permute-start | bytes 98312 | tf_op jit(solution)/shard_map/ppermute | solution.py:382
  49.1 9.3 %collective-permute-start.13 = (bf16[4,16,256]{2,1,0:T(8,128)(2,1)S(1)}, bf16[4,16,256]{2,1,0:T(8,128)(2,1)S(1)}, u32[]{:S(2)}, u32[]{:S(2)}) collective-permute-start(bf16[4,16,256]{2,1,0:T(8,128)(2,1)S(1)} %get-tuple-element.260), channel_id=1, source_target_pairs={{0,8},{1,9},{2,10},{3,11},{4,12},{5,13},{6,14},{7,15},{8,0},{9,1},... | collective-permute-start | bytes 98312 | tf_op jit(solution)/shard_map/ppermute | solution.py:382
  50.2 9.3 %collective-permute-start.14 = (bf16[4,16,256]{2,1,0:T(8,128)(2,1)S(1)}, bf16[4,16,256]{2,1,0:T(8,128)(2,1)S(1)}, u32[]{:S(2)}, u32[]{:S(2)}) collective-permute-start(bf16[4,16,256]{2,1,0:T(8,128)(2,1)S(1)} %get-tuple-element.261), channel_id=1, source_target_pairs={{0,12},{1,13},{2,14},{3,15},{4,8},{5,9},{6,10},{7,11},{8,4},{9,5},... | collective-permute-start | bytes 98312 | tf_op jit(solution)/shard_map/ppermute | solution.py:382
  51.9 16.6 %collective-permute-start.10 = (bf16[128,1280]{1,0:T(8,128)(2,1)S(1)}, bf16[128,1280]{1,0:T(8,128)(2,1)S(1)}, u32[]{:S(2)}, u32[]{:S(2)}) collective-permute-start(bf16[128,1280]{1,0:T(8,128)(2,1)S(1)} %collective-permute-done.3.refs_3_), channel_id=1, source_target_pairs={{0,2},{1,3},{2,0},{3,1},{4,6},{5,7},{6,4},{7,5},{8,10},{9,11},{10,... | collective-permute-start | bytes 983048 | tf_op jit(solution)/shard_map/ppermute | solution.py:382
  58.4 10.1 %collective-permute-start.15 = (bf16[128,1280]{1,0:T(8,128)(2,1)S(1)}, bf16[128,1280]{1,0:T(8,128)(2,1)S(1)}, u32[]{:S(2)}, u32[]{:S(2)}) collective-permute-start(bf16[128,1280]{1,0:T(8,128)(2,1)S(1)} %collective-permute-done.3.refs_3_), channel_id=1, source_target_pairs={{0,1},{1,0},{2,3},{3,2},{4,5},{5,4},{6,7},{7,6},{8,9},{9,8},{10,11... | collective-permute-start | bytes 983048 | tf_op jit(solution)/shard_map/ppermute | solution.py:382
  58.4 10.1 %collective-permute-start.9 = (bf16[128,1280]{1,0:T(8,128)(2,1)S(1)}, bf16[128,1280]{1,0:T(8,128)(2,1)S(1)}, u32[]{:S(2)}, u32[]{:S(2)}) collective-permute-start(bf16[128,1280]{1,0:T(8,128)(2,1)S(1)} %collective-permute-done.5.refs_6_.refs_2_), channel_id=1, source_target_pairs={{0,2},{1,3},{2,0},{3,1},{4,6},{5,7},{6,4},{7,5},{8,10},{9,11},{10,... | collective-permute-start | bytes 983048 | tf_op jit(solution)/shard_map/ppermute | solution.py:382
  68.5 9.7 %collective-permute-start.16 = (bf16[128,1280]{1,0:T(8,128)(2,1)S(1)}, bf16[128,1280]{1,0:T(8,128)(2,1)S(1)}, u32[]{:S(2)}, u32[]{:S(2)}) collective-permute-start(bf16[128,1280]{1,0:T(8,128)(2,1)S(1)} %collective-permute-done.11.refs_6_), channel_id=1, source_target_pairs={{0,2},{1,3},{2,0},{3,1},{4,6},{5,7},{6,4},{7,5},{8,10},{9,11},{10,... | collective-permute-start | bytes 983048 | tf_op jit(solution)/shard_map/ppermute | solution.py:382
  69.6 8.6 %collective-permute-start.17 = (bf16[128,1280]{1,0:T(8,128)(2,1)S(1)}, bf16[128,1280]{1,0:T(8,128)(2,1)S(1)}, u32[]{:S(2)}, u32[]{:S(2)}) collective-permute-start(bf16[128,1280]{1,0:T(8,128)(2,1)S(1)} %collective-permute-done.9.refs_4_), channel_id=1, source_target_pairs={{0,1},{1,0},{2,3},{3,2},{4,5},{5,4},{6,7},{7,6},{8,9},{9,8},{10,11... | collective-permute-start | bytes 983048 | tf_op jit(solution)/shard_map/ppermute | solution.py:382
  69.6 8.6 %collective-permute-start.18 = (bf16[128,1280]{1,0:T(8,128)(2,1)S(1)}, bf16[128,1280]{1,0:T(8,128)(2,1)S(1)}, u32[]{:S(2)}, u32[]{:S(2)}) collective-permute-start(bf16[128,1280]{1,0:T(8,128)(2,1)S(1)} %collective-permute-done.10.refs_5_), channel_id=1, source_target_pairs={{0,1},{1,0},{2,3},{3,2},{4,5},{5,4},{6,7},{7,6},{8,9},{9,8},{10,11... | collective-permute-start | bytes 983048 | tf_op jit(solution)/shard_map/ppermute | solution.py:382
  70.2 8.1 %collective-permute-start.19 = (bf16[128,1280]{1,0:T(8,128)(2,1)S(1)}, bf16[128,1280]{1,0:T(8,128)(2,1)S(1)}, u32[]{:S(2)}, u32[]{:S(2)}) collective-permute-start(bf16[128,1280]{1,0:T(8,128)(2,1)S(1)} %collective-permute-done.11.refs_6_), channel_id=1, source_target_pairs={{0,1},{1,0},{2,3},{3,2},{4,5},{5,4},{6,7},{7,6},{8,9},{9,8},{10,11... | collective-permute-start | bytes 983048 | tf_op jit(solution)/shard_map/ppermute | solution.py:382
  78.3 1.7 %collective-permute-start.20 = (bf16[128,1280]{1,0:T(8,128)(2,1)S(1)}, bf16[128,1280]{1,0:T(8,128)(2,1)S(1)}, u32[]{:S(2)}, u32[]{:S(2)}) collective-permute-start(bf16[128,1280]{1,0:T(8,128)(2,1)S(1)} %collective-permute-done.16.refs_7_), channel_id=1, source_target_pairs={{0,1},{1,0},{2,3},{3,2},{4,5},{5,4},{6,7},{7,6},{8,9},{9,8},{10,11... | collective-permute-start | bytes 983048 | tf_op jit(solution)/shard_map/ppermute | solution.py:382
  80.0 7.4 %copy-start.3 = (s32[256]{0:T(256)S(1)}, s32[256]{0:T(256)}, u32[]{:S(2)}) copy-start(s32[256]{0:T(256)} %param.11) | copy-start | bytes 3076

commit v13 on v12

--- a/solution.py
+++ b/solution.py
@@ -415,14 +415,12 @@
     )(code, size_row, keep, to_core, to_y, to_both)
 
     across, mine_y, beside = swap(mine, 8), swap(mine, 2), swap(mine, 4)
+    panel = [panel[0]] + [swap(panel[r], 4 * r) for r in range(1, Z)]
+    mine_y, panel[1], panel[2] = lax.optimization_barrier((mine_y, panel[1], panel[2]))
     far = [swap(mine, 1), swap(mine_y, 1), swap(beside, 1)]
-    across, mine_y, beside, *far = lax.optimization_barrier((across, mine_y, beside, *far))
+    across, beside, panel[3], *far = lax.optimization_barrier((across, beside, panel[3], *far))
 
     corner, beside_y, across_y = swap(across, 4), swap(beside, 2), swap(across, 2)
-    panel = [panel[0]] + [swap(panel[r], 4 * r) for r in range(1, Z)]
-    corner, *panel = lax.optimization_barrier((corner, *panel))
-
-    corner_y = swap(corner, 2)
     near = [mine, mine_y, beside]
     early = len(near)
     slots = LIVE_DEV * n * EDGE
@@ -447,10 +445,10 @@
         cost_estimate=cost(7e9, 1),
         name="half_transform",
     )(code, size_row, *panel, *near, *far)
-    far.append(swap(across, 1))
-    beside_y, across_y, half, late, *far = lax.optimization_barrier((beside_y, across_y, half, late, *far))
+    corner, half, late = lax.optimization_barrier((corner, half, late))
+    corner_y = swap(corner, 2)
     near += [across, beside_y, across_y, corner]
-    far += [swap(piece, 1) for piece in near[early + 1 :]]
+    far += [swap(piece, 1) for piece in near[early:]]
     corner_y, *far = lax.optimization_barrier((corner_y, *far))
     near.append(corner_y)
     far.append(swap(corner_y, 1))

time: 95.1 us -> 90.9 us (0.956)
  waiting for transfers between devices: 29.8 us -> 25.4 us
    ppermute x21, waiting for transfers between devices: 29.8 us -> 25.4 us  [swap(): return lax.ppermute(array, 'shell', [(i, i ^ bit) for i in range(n)])]
  transfers between devices with their start and end apart: 21 -> 21, of which waited for: 7 -> 6; matrix products, arithmetic and copies ran while one was open for 0% -> 0% of each run, Pallas kernels for 9% -> 10%
where the time goes in v13:
time: 90.9 us; the launch traced here: 90.7 us
  waiting for transfers between devices  25.4 us (28%)
  Pallas kernels  20.1 us (22%)
  starting transfers between devices  16.1 us (18%)
  between operations  14.1 us (16%)
  blocking collectives  12.8 us (14%)
  local copies, waits for them, and re-layouts  1.58 us (2%)
    ppermute x21, waiting for transfers between devices, swap(): return lax.ppermute(array, 'shell', [(i, i ^ bit) for i in range(n)])  25.4 us
    ppermute x21, starting transfers between devices, swap(): return lax.ppermute(array, 'shell', [(i, i ^ bit) for i in range(n)])  16.1 us
    all_to_all x1, blocking collectives, short_way(): lax.all_to_all(code, 'shell', split_axis=0, concat_axis=0, tiled=True)  12.8 us
    pallas_call x1, Pallas kernels, short_way(): pl.pallas_call(functools.partial(half_kernel, here, early), out_shape=(sh...  8.79 us
    pallas_call x1, Pallas kernels, short_way(): pl.pallas_call(functools.partial(last_kernel, count, early), out_shape=sh...  7.38 us
    pallas_call x1, Pallas kernels, short_way(): pl.pallas_call(functools.partial(pick_kernel, here), out_shape=[shape(CAP...  2.16 us
  transfers between devices with their start and end apart: 21, of which 6 were waited for; matrix products, arithmetic and copies ran while one was open for 0% of the time, Pallas kernels for 10%

profile of v13, /device:TPU:0, one launch (start us, length us, event | category | flops | bytes accessed | tf_op | source)
XLA Modules:
  0.0 90.7 jit_solution(5092105783725021245)
XLA Ops:
  6.5 0.9 copy-done.1
  7.4 1.6 %pack_rows.1 = (bf16[96,1280]{1,0:T(8,128)(2,1)S(1)}, bf16[96,1280]{1,0:T(8,128)(2,1)S(1)}, bf16[96,1280]{1,0:T(8,128)(2,1)S(1)}, bf16[96,1280]{1,0:T(8,128)(2,1)S(1)}) custom-call(bf16[160,2304]{1,0:T(8,128)(2,1)} %vir_ref.1, bf16[160,256]{1,0:T(8,128)(2,1)} %occ_ref.1, bf16[8,32,256]{2,1,0:T(8,128)(2,1)S(1)} %copy-done.1), custom_call_target="tpu_custom_call" | custom-call | flops 300000000 | bytes 3000000 | tf_op jit(solution)/shard_map/pack_rows/pallas_call | solution.py:384
  9.0 0.5 collective-permute-start
  9.5 2.6 %collective-permute-start.1 = (bf16[96,1280]{1,0:T(8,128)(2,1)S(1)}, bf16[96,1280]{1,0:T(8,128)(2,1)S(1)}, u32[]{:S(2)}, u32[]{:S(2)}) collective-permute-start(bf16[96,1280]{1,0:T(8,128)(2,1)S(1)} %get-tuple-element.244), channel_id=1, source_target_pairs={{0,2},{1,3},{2,0},{3,1},{4,6},{5,7},{6,4},{7,5},{8,10},{9,11},{10,... | collective-permute-start | bytes 737288 | tf_op jit(solution)/shard_map/ppermute | solution.py:382
  12.1 0.1 collective-permute-start.2
  12.9 0.7 copy-done
  13.5 0.2 pack_ids.1
  13.7 12.8 %all_to_all.5.code_ref = s32[16,8,128]{2,1,0:T(8,128)S(1)} all-to-all(s32[16,8,128]{2,1,0:T(8,128)S(1)} %pack_ids.1), channel_id=1, replica_groups=mesh['groups'=2,'shell'=16] {'shell'}, dimensions={0} | all-to-all | bytes 131072 | tf_op jit(solution)/shard_map/all_to_all | solution.py:404
  26.5 2.2 %pick_rows.1 = (bf16[128,1280]{1,0:T(8,128)(2,1)S(1)}, s32[1]{0:T(128)}, s32[1]{0:T(128)}, bf16[4,16,256]{2,1,0:T(8,128)(2,1)S(1)}, bf16[4,16,256]{2,1,0:T(8,128...) custom-call(s32[16,8,128]{2,1,0:T(8,128)S(1)} %all_to_all.5.code_ref, s32[1,256]{1,0:T(1,128)} %bitcast.87, ...), custom_call_target="tpu_custom_call" | custom-call | flops 300000000 | bytes 2000000 | tf_op jit(solution)/shard_map/pick_rows/pallas_call | solution.py:406
  28.7 0.2 collective-permute-start.7
  28.9 1.3 %collective-permute-start.4 = (bf16[128,1280]{1,0:T(8,128)(2,1)S(1)}, bf16[128,1280]{1,0:T(8,128)(2,1)S(1)}, u32[]{:S(2)}, u32[]{:S(2)}) collective-permute-start(bf16[128,1280]{1,0:T(8,128)(2,1)S(1)} %get-tuple-element.248.refs_4_.refs_0_), channel_id=1, source_target_pairs={{0,4},{1,5},{2,6},{3,7},{4,0},{5,1},{6,2},{7,3},{8,12},{9,13},{10,... | collective-permute-start | bytes 983048 | tf_op jit(solution)/shard_map/ppermute | solution.py:382
  30.2 0.7 collective-permute-start.8
  30.9 2.4 %collective-permute-start.9 = (bf16[4,16,256]{2,1,0:T(8,128)(2,1)S(1)}, bf16[4,16,256]{2,1,0:T(8,128)(2,1)S(1)}, u32[]{:S(2)}, u32[]{:S(2)}) collective-permute-start(bf16[4,16,256]{2,1,0:T(8,128)(2,1)S(1)} %get-tuple-element.251), channel_id=1, source_target_pairs={{0,8},{1,9},{2,10},{3,11},{4,12},{5,13},{6,14},{7,15},{8,0},{9,1},... | collective-permute-start | bytes 98312 | tf_op jit(solution)/shard_map/ppermute | solution.py:382
  33.3 0.6 collective-permute-start.3
  33.8 10.7 %collective-permute-done.8.refs_1_ = bf16[4,16,256]{2,1,0:T(8,128)(2,1)S(1)} collective-permute-done((bf16[4,16,256]{2,1,0:T(8,128)(2,1)S(1)}, bf16[4,16,256]{2,1,0:T(8,128)(2,1)S(1)}, u32[]{:S(2)}, u32[]{:S(2)}) %collective-permute-start.8) | collective-permute-done | bytes 32800 | tf_op jit(solution)/shard_map/ppermute | solution.py:382
  44.6 0.5 collective-permute-start.10
  45.1 0.1 collective-permute-start.11
  45.2 2.7 %collective-permute-start.5 = (bf16[4,16,256]{2,1,0:T(8,128)(2,1)S(1)}, bf16[4,16,256]{2,1,0:T(8,128)(2,1)S(1)}, u32[]{:S(2)}, u32[]{:S(2)}) collective-permute-start(bf16[4,16,256]{2,1,0:T(8,128)(2,1)S(1)} %get-tuple-element.249), channel_id=1, source_target_pairs={{0,12},{1,13},{2,14},{3,15},{4,8},{5,9},{6,10},{7,11},{8,4},{9,5},... | collective-permute-start | bytes 98312 | tf_op jit(solution)/shard_map/ppermute | solution.py:382
  47.9 3.0 %collective-permute-done.5.refs_3_ = bf16[4,16,256]{2,1,0:T(8,128)(2,1)S(1)} collective-permute-done((bf16[4,16,256]{2,1,0:T(8,128)(2,1)S(1)}, bf16[4,16,256]{2,1,0:T(8,128)(2,1)S(1)}, u32[]{:S(2)}, u32[]{:S(2)}) %collective-permute-start.5) | collective-permute-done | bytes 32800 | tf_op jit(solution)/shard_map/ppermute | solution.py:382
  50.9 0.7 collective-permute-done.3.refs_3_
  51.6 1.0 %collective-permute-start.12 = (bf16[128,1280]{1,0:T(8,128)(2,1)S(1)}, bf16[128,1280]{1,0:T(8,128)(2,1)S(1)}, u32[]{:S(2)}, u32[]{:S(2)}) collective-permute-start(bf16[128,1280]{1,0:T(8,128)(2,1)S(1)} %collective-permute-done.3.refs_3_), channel_id=1, source_target_pairs={{0,4},{1,5},{2,6},{3,7},{4,0},{5,1},{6,2},{7,3},{8,12},{9,13},{10,... | collective-permute-start | bytes 983048 | tf_op jit(solution)/shard_map/ppermute | solution.py:382
  52.6 0.8 collective-permute-start.14
  53.4 1.2 %collective-permute-start.13 = (bf16[128,1280]{1,0:T(8,128)(2,1)S(1)}, bf16[128,1280]{1,0:T(8,128)(2,1)S(1)}, u32[]{:S(2)}, u32[]{:S(2)}) collective-permute-start(bf16[128,1280]{1,0:T(8,128)(2,1)S(1)} %collective-permute-done.4.refs_6_.refs_2_), channel_id=1, source_target_pairs={{0,2},{1,3},{2,0},{3,1},{4,6},{5,7},{6,4},{7,5},{8,10},{9,11},{10,... | collective-permute-start | bytes 983048 | tf_op jit(solution)/shard_map/ppermute | solution.py:382
  54.6 8.8 %half_transform.1 = (f32[512,1024]{1,0:T(8,128)S(1)}, bf16[2,640,1024]{2,1,0:T(8,128)(2,1)S(1)}) custom-call(s32[16,8,128]{2,1,0:T(8,128)S(1)} %all_to_all.5.code_ref, s32[1,256]{1,0:T(1,128)} %bitcast.88, bf16[4,16,256]{2,1,0:T(8,128)(2,1)S(1)} %get-tuple-element.405.refs_0_, bf16[4,16,256]{2,1,0:T(8,128)(2,1)S(1)} %collective-permute-done.8.refs_1_, ...), custom_call_target="tpu_custom_call" | custom-call | flops 7000000000 | bytes 1 | tf_op jit(solution)/shard_map/half_transform/pallas_call | solution.py:427
  63.4 0.9 collective-permute-start.15
  64.3 3.5 %collective-permute-done.13.refs_4_ = bf16[128,1280]{1,0:T(8,128)(2,1)S(1)} collective-permute-done((bf16[128,1280]{1,0:T(8,128)(2,1)S(1)}, bf16[128,1280]{1,0:T(8,128)(2,1)S(1)}, u32[]{:S(2)}, u32[]{:S(2)}) %collective-permute-start.13) | collective-permute-done | bytes 327712 | tf_op jit(solution)/shard_map/ppermute | solution.py:382
  67.8 0.5 collective-permute-start.18
  68.3 5.8 %collective-permute-done.15.refs_7_ = bf16[128,1280]{1,0:T(8,128)(2,1)S(1)} collective-permute-done((bf16[128,1280]{1,0:T(8,128)(2,1)S(1)}, bf16[128,1280]{1,0:T(8,128)(2,1)S(1)}, u32[]{:S(2)}, u32[]{:S(2)}) %collective-permute-start.15) | collective-permute-done | bytes 327712 | tf_op jit(solution)/shard_map/ppermute | solution.py:382
  74.1 0.1 collective-permute-start.20
  74.2 1.6 %collective-permute-done.20.refs_15_ = bf16[128,1280]{1,0:T(8,128)(2,1)S(1)} collective-permute-done((bf16[128,1280]{1,0:T(8,128)(2,1)S(1)}, bf16[128,1280]{1,0:T(8,128)(2,1)S(1)}, u32[]{:S(2)}, u32[]{:S(2)}) %collective-permute-start.20) | collective-permute-done | bytes 327712 | tf_op jit(solution)/shard_map/ppermute | solution.py:382
  75.8 7.4 %last_product.1 = bf16[2,256,2304]{2,1,0:T(8,128)(2,1)} custom-call(s32[1]{0:T(128)} %get-tuple-element.404.me_ref, f32[512,1024]{1,0:T(8,128)S(1)} %get-tuple-element.264.part_any, bf16[2,640,1024]{2,1,0:T(8,128)(2,1)S(1)} %get-tuple-element.265.late_any, bf16[128,1280]{1,0:T(8,128)(2,1)S(1)} %get-tuple-element.248.refs_4_.refs_0_, ...), custom_call_target="tpu_custom_call" | custom-call | flops 20000000000 | bytes 1 | tf_op jit(solution)/shard_map/last_product/pallas_call | solution.py:458
  83.2 0.6 while.17
  (23 shorter events, 0.1 us)
Async XLA Ops:
  6.5 0.9 copy-start.1
  9.0 17.5 %collective-permute-start = (bf16[96,1280]{1,0:T(8,128)(2,1)S(1)}, bf16[96,1280]{1,0:T(8,128)(2,1)S(1)}, u32[]{:S(2)}, u32[]{:S(2)}) collective-permute-start(bf16[96,1280]{1,0:T(8,128)(2,1)S(1)} %get-tuple-element.243), channel_id=1, source_target_pairs={{0,1},{1,0},{2,3},{3,2},{4,5},{5,4},{6,7},{7,6},{8,9},{9,8},{10,11... | collective-permute-start | bytes 737288 | tf_op jit(solution)/shard_map/ppermute | solution.py:382
  9.5 17.0 %collective-permute-start.1 = (bf16[96,1280]{1,0:T(8,128)(2,1)S(1)}, bf16[96,1280]{1,0:T(8,128)(2,1)S(1)}, u32[]{:S(2)}, u32[]{:S(2)}) collective-permute-start(bf16[96,1280]{1,0:T(8,128)(2,1)S(1)} %get-tuple-element.244), channel_id=1, source_target_pairs={{0,2},{1,3},{2,0},{3,1},{4,6},{5,7},{6,4},{7,5},{8,10},{9,11},{10,... | collective-permute-start | bytes 737288 | tf_op jit(solution)/shard_map/ppermute | solution.py:382
  12.1 14.4 %collective-permute-start.2 = (bf16[96,1280]{1,0:T(8,128)(2,1)S(1)}, bf16[96,1280]{1,0:T(8,128)(2,1)S(1)}, u32[]{:S(2)}, u32[]{:S(2)}) collective-permute-start(bf16[96,1280]{1,0:T(8,128)(2,1)S(1)} %get-tuple-element.245), channel_id=1, source_target_pairs={{0,3},{1,2},{2,1},{3,0},{4,7},{5,6},{6,5},{7,4},{8,11},{9,10},{10,... | collective-permute-start | bytes 737288 | tf_op jit(solution)/shard_map/ppermute | solution.py:382
  12.9 0.7 copy-start
  28.7 15.9 %collective-permute-start.7 = (bf16[128,1280]{1,0:T(8,128)(2,1)S(1)}, bf16[128,1280]{1,0:T(8,128)(2,1)S(1)}, u32[]{:S(2)}, u32[]{:S(2)}) collective-permute-start(bf16[128,1280]{1,0:T(8,128)(2,1)S(1)} %get-tuple-element.248.refs_4_.refs_0_), channel_id=1, source_target_pairs={{0,2},{1,3},{2,0},{3,1},{4,6},{5,7},{6,4},{7,5},{8,10},{9,11},{10,... | collective-permute-start | bytes 983048 | tf_op jit(solution)/shard_map/ppermute | solution.py:382
  28.9 16.2 %collective-permute-start.4 = (bf16[128,1280]{1,0:T(8,128)(2,1)S(1)}, bf16[128,1280]{1,0:T(8,128)(2,1)S(1)}, u32[]{:S(2)}, u32[]{:S(2)}) collective-permute-start(bf16[128,1280]{1,0:T(8,128)(2,1)S(1)} %get-tuple-element.248.refs_4_.refs_0_), channel_id=1, source_target_pairs={{0,4},{1,5},{2,6},{3,7},{4,0},{5,1},{6,2},{7,3},{8,12},{9,13},{10,... | collective-permute-start | bytes 983048 | tf_op jit(solution)/shard_map/ppermute | solution.py:382
  30.2 14.3 %collective-permute-start.8 = (bf16[4,16,256]{2,1,0:T(8,128)(2,1)S(1)}, bf16[4,16,256]{2,1,0:T(8,128)(2,1)S(1)}, u32[]{:S(2)}, u32[]{:S(2)}) collective-permute-start(bf16[4,16,256]{2,1,0:T(8,128)(2,1)S(1)} %get-tuple-element.250), channel_id=1, source_target_pairs={{0,4},{1,5},{2,6},{3,7},{4,0},{5,1},{6,2},{7,3},{8,12},{9,13},{10,... | collective-permute-start | bytes 98312 | tf_op jit(solution)/shard_map/ppermute | solution.py:382
  30.9 13.7 %collective-permute-start.9 = (bf16[4,16,256]{2,1,0:T(8,128)(2,1)S(1)}, bf16[4,16,256]{2,1,0:T(8,128)(2,1)S(1)}, u32[]{:S(2)}, u32[]{:S(2)}) collective-permute-start(bf16[4,16,256]{2,1,0:T(8,128)(2,1)S(1)} %get-tuple-element.251), channel_id=1, source_target_pairs={{0,8},{1,9},{2,10},{3,11},{4,12},{5,13},{6,14},{7,15},{8,0},{9,1},... | collective-permute-start | bytes 98312 | tf_op jit(solution)/shard_map/ppermute | solution.py:382
  33.3 18.3 %collective-permute-start.3 = (bf16[128,1280]{1,0:T(8,128)(2,1)S(1)}, bf16[128,1280]{1,0:T(8,128)(2,1)S(1)}, u32[]{:S(2)}, u32[]{:S(2)}) collective-permute-start(bf16[128,1280]{1,0:T(8,128)(2,1)S(1)} %get-tuple-element.248.refs_4_.refs_0_), channel_id=1, source_target_pairs={{0,8},{1,9},{2,10},{3,11},{4,12},{5,13},{6,14},{7,15},{8,0},{9,1},... | collective-permute-start | bytes 983048 | tf_op jit(solution)/shard_map/ppermute | solution.py:382
  44.6 7.0 %collective-permute-start.6 = (bf16[128,1280]{1,0:T(8,128)(2,1)S(1)}, bf16[128,1280]{1,0:T(8,128)(2,1)S(1)}, u32[]{:S(2)}, u32[]{:S(2)}) collective-permute-start(bf16[128,1280]{1,0:T(8,128)(2,1)S(1)} %get-tuple-element.248.refs_4_.refs_0_), channel_id=1, source_target_pairs={{0,1},{1,0},{2,3},{3,2},{4,5},{5,4},{6,7},{7,6},{8,9},{9,8},{10,11... | collective-permute-start | bytes 983048 | tf_op jit(solution)/shard_map/ppermute | solution.py:382
  44.6 7.0 %collective-permute-start.10 = (bf16[128,1280]{1,0:T(8,128)(2,1)S(1)}, bf16[128,1280]{1,0:T(8,128)(2,1)S(1)}, u32[]{:S(2)}, u32[]{:S(2)}) collective-permute-start(bf16[128,1280]{1,0:T(8,128)(2,1)S(1)} %collective-permute-done.7.refs_5_.refs_1_), channel_id=1, source_target_pairs={{0,1},{1,0},{2,3},{3,2},{4,5},{5,4},{6,7},{7,6},{8,9},{9,8},{10,11... | collective-permute-start | bytes 983048 | tf_op jit(solution)/shard_map/ppermute | solution.py:382
  45.1 6.5 %collective-permute-start.11 = (bf16[128,1280]{1,0:T(8,128)(2,1)S(1)}, bf16[128,1280]{1,0:T(8,128)(2,1)S(1)}, u32[]{:S(2)}, u32[]{:S(2)}) collective-permute-start(bf16[128,1280]{1,0:T(8,128)(2,1)S(1)} %collective-permute-done.4.refs_6_.refs_2_), channel_id=1, source_target_pairs={{0,1},{1,0},{2,3},{3,2},{4,5},{5,4},{6,7},{7,6},{8,9},{9,8},{10,11... | collective-permute-start | bytes 983048 | tf_op jit(solution)/shard_map/ppermute | solution.py:382
  45.2 5.7 %collective-permute-start.5 = (bf16[4,16,256]{2,1,0:T(8,128)(2,1)S(1)}, bf16[4,16,256]{2,1,0:T(8,128)(2,1)S(1)}, u32[]{:S(2)}, u32[]{:S(2)}) collective-permute-start(bf16[4,16,256]{2,1,0:T(8,128)(2,1)S(1)} %get-tuple-element.249), channel_id=1, source_target_pairs={{0,12},{1,13},{2,14},{3,15},{4,8},{5,9},{6,10},{7,11},{8,4},{9,5},... | collective-permute-start | bytes 98312 | tf_op jit(solution)/shard_map/ppermute | solution.py:382
  51.6 11.8 %collective-permute-start.12 = (bf16[128,1280]{1,0:T(8,128)(2,1)S(1)}, bf16[128,1280]{1,0:T(8,128)(2,1)S(1)}, u32[]{:S(2)}, u32[]{:S(2)}) collective-permute-start(bf16[128,1280]{1,0:T(8,128)(2,1)S(1)} %collective-permute-done.3.refs_3_), channel_id=1, source_target_pairs={{0,4},{1,5},{2,6},{3,7},{4,0},{5,1},{6,2},{7,3},{8,12},{9,13},{10,... | collective-permute-start | bytes 983048 | tf_op jit(solution)/shard_map/ppermute | solution.py:382
  52.6 15.2 %collective-permute-start.14 = (bf16[128,1280]{1,0:T(8,128)(2,1)S(1)}, bf16[128,1280]{1,0:T(8,128)(2,1)S(1)}, u32[]{:S(2)}, u32[]{:S(2)}) collective-permute-start(bf16[128,1280]{1,0:T(8,128)(2,1)S(1)} %collective-permute-done.3.refs_3_), channel_id=1, source_target_pairs={{0,2},{1,3},{2,0},{3,1},{4,6},{5,7},{6,4},{7,5},{8,10},{9,11},{10,... | collective-permute-start | bytes 983048 | tf_op jit(solution)/shard_map/ppermute | solution.py:382
  53.4 14.9 %collective-permute-start.16 = (bf16[128,1280]{1,0:T(8,128)(2,1)S(1)}, bf16[128,1280]{1,0:T(8,128)(2,1)S(1)}, u32[]{:S(2)}, u32[]{:S(2)}) collective-permute-start(bf16[128,1280]{1,0:T(8,128)(2,1)S(1)} %collective-permute-done.3.refs_3_), channel_id=1, source_target_pairs={{0,1},{1,0},{2,3},{3,2},{4,5},{5,4},{6,7},{7,6},{8,9},{9,8},{10,11... | collective-permute-start | bytes 983048 | tf_op jit(solution)/shard_map/ppermute | solution.py:382
  53.4 14.4 %collective-permute-start.13 = (bf16[128,1280]{1,0:T(8,128)(2,1)S(1)}, bf16[128,1280]{1,0:T(8,128)(2,1)S(1)}, u32[]{:S(2)}, u32[]{:S(2)}) collective-permute-start(bf16[128,1280]{1,0:T(8,128)(2,1)S(1)} %collective-permute-done.4.refs_6_.refs_2_), channel_id=1, source_target_pairs={{0,2},{1,3},{2,0},{3,1},{4,6},{5,7},{6,4},{7,5},{8,10},{9,11},{10,... | collective-permute-start | bytes 983048 | tf_op jit(solution)/shard_map/ppermute | solution.py:382
  63.4 10.7 %collective-permute-start.15 = (bf16[128,1280]{1,0:T(8,128)(2,1)S(1)}, bf16[128,1280]{1,0:T(8,128)(2,1)S(1)}, u32[]{:S(2)}, u32[]{:S(2)}) collective-permute-start(bf16[128,1280]{1,0:T(8,128)(2,1)S(1)} %collective-permute-done.12.refs_6_), channel_id=1, source_target_pairs={{0,2},{1,3},{2,0},{3,1},{4,6},{5,7},{6,4},{7,5},{8,10},{9,11},{10,... | collective-permute-start | bytes 983048 | tf_op jit(solution)/shard_map/ppermute | solution.py:382
  67.8 6.3 %collective-permute-start.17 = (bf16[128,1280]{1,0:T(8,128)(2,1)S(1)}, bf16[128,1280]{1,0:T(8,128)(2,1)S(1)}, u32[]{:S(2)}, u32[]{:S(2)}) collective-permute-start(bf16[128,1280]{1,0:T(8,128)(2,1)S(1)} %collective-permute-done.13.refs_4_), channel_id=1, source_target_pairs={{0,1},{1,0},{2,3},{3,2},{4,5},{5,4},{6,7},{7,6},{8,9},{9,8},{10,11... | collective-permute-start | bytes 983048 | tf_op jit(solution)/shard_map/ppermute | solution.py:382
  67.8 6.3 %collective-permute-start.18 = (bf16[128,1280]{1,0:T(8,128)(2,1)S(1)}, bf16[128,1280]{1,0:T(8,128)(2,1)S(1)}, u32[]{:S(2)}, u32[]{:S(2)}) collective-permute-start(bf16[128,1280]{1,0:T(8,128)(2,1)S(1)} %collective-permute-done.14.refs_5_), channel_id=1, source_target_pairs={{0,1},{1,0},{2,3},{3,2},{4,5},{5,4},{6,7},{7,6},{8,9},{9,8},{10,11... | collective-permute-start | bytes 983048 | tf_op jit(solution)/shard_map/ppermute | solution.py:382
  68.3 5.8 %collective-permute-start.19 = (bf16[128,1280]{1,0:T(8,128)(2,1)S(1)}, bf16[128,1280]{1,0:T(8,128)(2,1)S(1)}, u32[]{:S(2)}, u32[]{:S(2)}) collective-permute-start(bf16[128,1280]{1,0:T(8,128)(2,1)S(1)} %collective-permute-done.12.refs_6_), channel_id=1, source_target_pairs={{0,1},{1,0},{2,3},{3,2},{4,5},{5,4},{6,7},{7,6},{8,9},{9,8},{10,11... | collective-permute-start | bytes 983048 | tf_op jit(solution)/shard_map/ppermute | solution.py:382
  74.1 1.7 %collective-permute-start.20 = (bf16[128,1280]{1,0:T(8,128)(2,1)S(1)}, bf16[128,1280]{1,0:T(8,128)(2,1)S(1)}, u32[]{:S(2)}, u32[]{:S(2)}) collective-permute-start(bf16[128,1280]{1,0:T(8,128)(2,1)S(1)} %collective-permute-done.15.refs_7_), channel_id=1, source_target_pairs={{0,1},{1,0},{2,3},{3,2},{4,5},{5,4},{6,7},{7,6},{8,9},{9,8},{10,11... | collective-permute-start | bytes 983048 | tf_op jit(solution)/shard_map/ppermute | solution.py:382
  75.8 7.4 %copy-start.3 = (s32[256]{0:T(256)S(1)}, s32[256]{0:T(256)}, u32[]{:S(2)}) copy-start(s32[256]{0:T(256)} %param.11) | copy-start | bytes 3076

commit v14 on v13

--- a/solution.py
+++ b/solution.py
@@ -95,11 +95,16 @@
     return jnp.concatenate([zero_one(ids == lanes + 128.0 * k) for k in range(shells // 128)], axis=1)
 
 
-def slot_hots(code, shells):
-    code = code.reshape(-1, 128)
-    kept = code >= 0
-    columns = jnp.where(kept, code % shells, -1).astype(F32)
-    return one_hots(columns, shells), one_hots(jnp.where(kept, code // shells, -1).astype(F32), shells)
+def slot_hots(got, shells):
+    sources, slots = got.shape[0], got.shape[0] * BLK_DEV
+    rows = got[:, 2 * BLK_DEV :, :].reshape(sources, got.shape[2]).astype(BF16)
+    owner = zero_one(iota((slots, sources), 0) // BLK_DEV == iota((slots, sources), 1)).astype(BF16)
+    ids = jnp.dot(owner, rows, preferred_element_type=F32)
+    slot, lane = iota(ids.shape, 0) % BLK_DEV, iota(ids.shape, 1)
+    columns, rows = (
+        jnp.broadcast_to(column_of(ids, lane == slot + first), (slots, 128)) for first in (0, BLK_DEV)
+    )
+    return one_hots(columns, shells), one_hots(rows, shells)
 
 
 class Shells:
@@ -127,49 +132,46 @@
             self.edges.append(jnp.sum(self.used * jnp.floor((reach + extra) * 0.5), axis=0, keepdims=True))
 
 
-def pack_kernel(vir_ref, occ_ref, panels_ref, *refs):
-    outs, (turned_ref,) = refs[:4], refs[4:]
+def pack_kernel(vir_ref, occ_ref, *outs):
     me = lax.axis_index("shell")
     core, y = lax.rem(me, 2), lax.rem(lax.div(me, 2), 2)
     here, nvir = vir_ref.shape
-    rows = here // 2
     width, thin = nvir // CORES, occ_ref.shape[1] // CORES
-    turned_ref[...] = jnp.swapaxes(panels_ref[...].astype(F32), 0, 1)
-    block = EDGE * EDGE
     for dy in range(2):
         parity = lax.rem(y + dy, 2)
-        pick = zero_one(iota((rows, here), 1) == 2 * iota((rows, here), 0) + parity).astype(BF16)
+        pick = zero_one(iota((here // 2, here), 1) == 2 * iota((here // 2, here), 0) + parity).astype(BF16)
         for dc in range(2):
             half = lax.rem(core + dc, 2)
             out = outs[2 * dy + dc]
             part = vir_ref[:, pl.ds(pl.multiple_of(half * width, 128), width)]
-            out[:rows, :width] = jnp.dot(pick, part, preferred_element_type=F32).astype(BF16)
+            out[:, :width] = jnp.dot(pick, part, preferred_element_type=F32).astype(BF16)
             part = occ_ref[:, pl.ds(pl.multiple_of(half * thin, 128), thin)]
-            out[:rows, width:] = jnp.dot(pick, part, preferred_element_type=F32).astype(BF16)
-            for z in range(Z):
-                device = (z * Y + parity) * CORES + half
-                pair = turned_ref[pl.ds(2 * device, 2)].reshape(2 * BLK_DEV, block)
-                out[rows:, z * block : (z + 1) * block] = pair.astype(BF16)
-            out[rows:, Z * block :] = jnp.zeros((2 * BLK_DEV, out.shape[1] - Z * block), BF16)
-
-
-def ids_kernel(shells, pairs_ref, count_ref, code_ref):
-    code = pairs_ref[1:2, :] + shells * pairs_ref[0:1, :]
-    code = jnp.where(iota((1, BLK_DEV), 1) < count_ref[...], code, -1).astype(F32)
-    square = (BLK_DEV, BLK_DEV)
-    code = column_of(code, iota(square, 0) == iota(square, 1)).astype(jnp.int32)
-    code_ref[...] = jnp.broadcast_to(jnp.broadcast_to(code, (BLK_DEV, 128))[None], code_ref.shape)
-
-
-def pick_kernel(here, code_ref, size_ref, *refs):
-    sources, (out_ref, over_ref, me_ref), panel_refs = refs[:4], refs[4:7], refs[7:]
+            out[:, width:] = jnp.dot(pick, part, preferred_element_type=F32).astype(BF16)
+
+
+def send_kernel(pairs_ref, count_ref, panels_ref, send_ref):
+    n = send_ref.shape[0]
+    turned = jnp.swapaxes(panels_ref[...].astype(F32), 0, 1)
+    send_ref[:, : 2 * BLK_DEV, :] = turned.reshape(n, 2 * BLK_DEV, EDGE * EDGE).astype(BF16)
+    kept = iota((1, BLK_DEV), 1) < count_ref[...]
+    square, wide = (BLK_DEV, BLK_DEV), (BLK_DEV, EDGE * EDGE)
+    same = iota(square, 0) == iota(square, 1)
+    row = jnp.zeros((1, EDGE * EDGE), F32)
+    for first, k in ((0, 1), (BLK_DEV, 0)):
+        ids = column_of(jnp.where(kept, pairs_ref[k : k + 1, :], -1).astype(F32), same)
+        row += row_of(ids, iota(wide, 1) == iota(wide, 0) + first)
+    send_ref[:, 2 * BLK_DEV :, :] = jnp.broadcast_to(row[None], (n, 1, EDGE * EDGE)).astype(BF16)
+
+
+def pick_kernel(here, got_ref, size_ref, *refs):
+    sources, (out_ref, over_ref, me_ref) = refs[:4], refs[4:]
     me = lax.axis_index("shell")
     me_ref[0] = me
     core, y, z = lax.rem(me, 2), lax.rem(lax.div(me, 2), 2), lax.div(me, 4)
     window = CORES * Y * here
     shell_count = size_ref.shape[1]
     shells = Shells(size_ref[...].astype(F32))
-    lists = [Used(shells, hot, window) for hot in slot_hots(code_ref[...], shell_count)]
+    lists = [Used(shells, hot, window) for hot in slot_hots(got_ref[...].astype(F32), shell_count)]
     most = jnp.zeros((1, 1), F32)
     lane = iota((1, 128), 1)
     for chosen in lists:
@@ -185,11 +187,7 @@
     extra = jnp.where(even, lists[0].extra[0], lists[0].extra[1])
     rows = here // 2
     for k, source in enumerate(sources):
-        member = 2 * lax.rem(y + k // 2, 2) + lax.rem(core + k % 2, 2)
-        device = 4 * z + member
-        for r, panel_ref in enumerate(panel_refs):
-            lanes = pl.ds(pl.multiple_of((z ^ r) * (EDGE * EDGE), 128), EDGE * EDGE)
-            panel_ref[member] = source[rows:, lanes]
+        device = 4 * z + 2 * lax.rem(y + k // 2, 2) + lax.rem(core + k % 2, 2)
         row = (2 * iota((shell_count, 128), 1) + device * here + y).astype(F32)
         where = row - shells.starts
         inside = (where >= 0.0) & (where < shells.size)
@@ -202,7 +200,7 @@
             place = jnp.where(place > 0.0, place - 1.0 - base, -1.0)
             hot = zero_one(place == iota((CAP, 128), 0).astype(F32)).astype(BF16)
             totals[total] += jnp.dot(
-                hot[:, :rows], source[:rows, column], preferred_element_type=F32
+                hot[:, :rows], source[:, column], preferred_element_type=F32
             )
     for total, column in zip(totals, columns):
         out_ref[:, column] = total.astype(BF16)
@@ -213,12 +211,11 @@
     return jnp.where((slot == 3) | (slot == 4), slot ^ 7, slot)
 
 
-def half_kernel(here, early, code_ref, size_ref, *refs):
-    panel_refs, pieces, refs = refs[:Z], refs[Z : Z + 2 * early], refs[Z + 2 * early :]
-    half_ref, late_ref, got_ref, occ_ref, part_ref, hot_ref, placed_ref, sems = refs
+def half_kernel(here, early, got_ref, size_ref, *refs):
+    pieces, refs = refs[: 2 * early], refs[2 * early :]
+    half_ref, late_ref, panels_ref, ids_ref, occ_ref, part_ref, hot_ref, placed_ref, sems = refs
     me = lax.axis_index("shell")
     core, chip = lax.rem(me, CORES), lax.div(me, CORES)
-    z = lax.div(chip, Y)
     width = pieces[0].shape[1] - 128
     copies = []
     for far in range(2):
@@ -229,15 +226,15 @@
             copies.append(pltpu.make_async_copy(pieces[at].at[:, pl.ds(width, 128)], target, sems.at[at]))
     for copy in copies:
         copy.start()
-    for r, panel_ref in enumerate(panel_refs):
-        got_ref[pl.ds((z ^ r) * (Y * CORES), Y * CORES)] = panel_ref[...]
     window = CORES * Y * here
     shell_count = size_ref.shape[1]
     got = got_ref[...].astype(F32)
     size_row = size_ref[...].astype(F32)
     shells = Shells(size_row)
     got = got_ref[...].astype(F32)
-    hots = slot_hots(code_ref[...], shell_count)
+    panels_ref[...] = got[:, : 2 * BLK_DEV, :].astype(BF16)
+    ids_ref[...] = got[:, 2 * BLK_DEV :, :].reshape(ids_ref.shape)
+    hots = slot_hots(got, shell_count)
     lists = [Used(shells, hot, window) for hot in hots]
     slots = hots[0].shape[0]
     kept = LIVE_DEV * (slots // BLK_DEV)
@@ -383,58 +380,60 @@
 
     keep, to_core, to_y, to_both = pl.pallas_call(
         pack_kernel,
-        out_shape=[shape(here // 2 + 2 * BLK_DEV, packed)] * 4,
-        in_specs=[VMEM] * 3,
+        out_shape=[shape(here // 2, packed)] * 4,
+        in_specs=[VMEM] * 2,
         out_specs=[VMEM] * 4,
-        scratch_shapes=[pltpu.VMEM((2 * n, BLK_DEV, EDGE * EDGE), F32)],
         compiler_params=params(12),
         cost_estimate=cost(3e8, 3e6),
         name="pack_rows",
-    )(vir_coef, occ_coef, panels)
+    )(vir_coef, occ_coef)
     to_y, to_both, to_core = swap(to_y, 2), swap(to_both, 3), swap(to_core, 1)
-    code = pl.pallas_call(
-        functools.partial(ids_kernel, size_row.shape[1]),
-        out_shape=shape(n, BLK_DEV, 128, dtype=jnp.int32),
-        in_specs=[VMEM] * 2,
+    send = pl.pallas_call(
+        send_kernel,
+        out_shape=shape(n, 2 * BLK_DEV + 1, EDGE * EDGE),
+        in_specs=[VMEM] * 3,
         out_specs=VMEM,
         compiler_params=params(12),
-        cost_estimate=cost(1e4, 1e4),
-        name="pack_ids",
-    )(block_pairs.T, block_count.reshape(1, 1))
-    code = lax.all_to_all(code, "shell", split_axis=0, concat_axis=0, tiled=True)
-
-    mine, over, me, *panel = pl.pallas_call(
+        cost_estimate=cost(1e6, 5e5),
+        name="pack_panels",
+    )(block_pairs.T, block_count.reshape(1, 1), panels)
+    got = lax.all_to_all(send, "shell", split_axis=0, concat_axis=0, tiled=True)
+
+    mine, over, me = pl.pallas_call(
         functools.partial(pick_kernel, here),
-        out_shape=[shape(CAP, packed), shape(1, dtype=jnp.int32), shape(1, dtype=jnp.int32)]
-        + [shape(Y * CORES, 2 * BLK_DEV, EDGE * EDGE)] * Z,
+        out_shape=(shape(CAP, packed), shape(1, dtype=jnp.int32), shape(1, dtype=jnp.int32)),
         in_specs=[VMEM] * 6,
-        out_specs=[VMEM, SMEM, SMEM] + [VMEM] * Z,
+        out_specs=(VMEM, SMEM, SMEM),
         compiler_params=params(12),
         cost_estimate=cost(3e8, 2e6),
         name="pick_rows",
-    )(code, size_row, keep, to_core, to_y, to_both)
+    )(got, size_row, keep, to_core, to_y, to_both)
 
     across, mine_y, beside = swap(mine, 8), swap(mine, 2), swap(mine, 4)
-    panel = [panel[0]] + [swap(panel[r], 4 * r) for r in range(1, Z)]
-    mine_y, panel[1], panel[2] = lax.optimization_barrier((mine_y, panel[1], panel[2]))
     far = [swap(mine, 1), swap(mine_y, 1), swap(beside, 1)]
-    across, beside, panel[3], *far = lax.optimization_barrier((across, beside, panel[3], *far))
+    across, mine_y, beside, *far = lax.optimization_barrier((across, mine_y, beside, *far))
 
     corner, beside_y, across_y = swap(across, 4), swap(beside, 2), swap(across, 2)
     near = [mine, mine_y, beside]
     early = len(near)
     slots = LIVE_DEV * n * EDGE
-    half, late = pl.pallas_call(
+    half, late, got_panels, got_ids = pl.pallas_call(
         functools.partial(half_kernel, here, early),
-        out_shape=(shape(2 * NOCC, room, dtype=F32), shape(2, room - early * CAP, room)),
+        out_shape=(
+            shape(2 * NOCC, room, dtype=F32),
+            shape(2, room - early * CAP, room),
+            shape(n, 2 * BLK_DEV, EDGE * EDGE),
+            shape(n, EDGE * EDGE, dtype=F32),
+        ),
         grid=(1,),
-        in_specs=[VMEM] * (2 + Z) + [ANY] * (2 * early),
+        in_specs=[VMEM] * 2 + [ANY] * (2 * early),
         out_specs=(
             pl.BlockSpec((2 * NOCC, room), lambda i: (0, 0)),
             pl.BlockSpec((2, room - early * CAP, room), lambda i: (0, 0, 0)),
+            pl.BlockSpec((n, 2 * BLK_DEV, EDGE * EDGE), lambda i: (0, 0, 0)),
+            pl.BlockSpec((n, EDGE * EDGE), lambda i: (0, 0)),
         ),
         scratch_shapes=[
-            pltpu.VMEM((n, 2 * BLK_DEV, EDGE * EDGE), BF16),
             pltpu.VMEM((early * CAP, NOCC), BF16),
             pltpu.VMEM((NOCC, slots), BF16),
             pltpu.VMEM((room - early * CAP, slots), BF16),
@@ -444,7 +443,7 @@
         compiler_params=params(30),
         cost_estimate=cost(7e9, 1),
         name="half_transform",
-    )(code, size_row, *panel, *near, *far)
+    )(got, size_row, *near, *far)
     corner, half, late = lax.optimization_barrier((corner, half, late))
     corner_y = swap(corner, 2)
     near += [across, beside_y, across_y, corner]
@@ -473,28 +472,25 @@
         cost_estimate=cost(2e10, 1),
         name="last_product",
     )(me, half, late, *near, *far)
-    return out, over[0], code, me, panel
+    return out, over[0], got_panels, got_ids
 
 
 def per_device(*args):
     n = lax.axis_size("shell")
     here, nvir = args[5].shape
-    shells = args[3].shape[0]
     sparse = LIVE_DEV * n * EDGE < n * here
     if not (sparse and n == Z * Y * CORES and here <= 256 and here % 16 == 0 and nvir % 768 == 0):
         return from_start(*args)
-    out, over, code, me, panel = short_way(*args)
+    out, over, got_panels, got_ids = short_way(*args)
 
     def again(carry):
         over, _ = carry
-        over, code_now, me_now, panel_now, *held = lax.optimization_barrier((over, code, me, tuple(panel), *args[3:]))
-        z = me_now[0] // (Y * CORES)
-        turned = jnp.stack(panel_now)[jnp.arange(Z, dtype=jnp.int32) ^ z]
+        over, turned, ids, *held = lax.optimization_barrier((over, got_panels, got_ids, *args[3:]))
         turned = turned.reshape(n, 2, BLK_DEV, EDGE * EDGE).swapaxes(1, 2).reshape(n * BLK_DEV, 2, EDGE * EDGE)
-        code_now = jnp.max(code_now, axis=2).reshape(n * BLK_DEV)
-        ids = jnp.maximum(code_now, 0)
-        pairs = jnp.stack([ids // shells, ids % shells], axis=1)
-        return over - 1, long_way(turned, pairs, code_now >= 0, *held)
+        ids = ids[:, : 2 * BLK_DEV].astype(jnp.int32)
+        columns, rows = ids[:, :BLK_DEV].reshape(n * BLK_DEV), ids[:, BLK_DEV:].reshape(n * BLK_DEV)
+        pairs = jnp.maximum(jnp.stack([rows, columns], axis=1), 0)
+        return over - 1, long_way(turned, pairs, columns >= 0, *held)
 
     return lax.while_loop(lambda carry: carry[0] > 0, again, (over, out))[1]
 

time: 90.9 us -> 93.4 us (1.028)
  blocking collectives: 12.8 us -> 0 us
  waiting for transfers between devices: 25.4 us -> 37.9 us
  starting transfers between devices: 16.1 us -> 18.3 us
    all_to_all x1 -> x0, blocking collectives: 12.8 us -> none  [short_way(): lax.all_to_all(code, 'shell', split_axis=0, concat_axis=0, tiled=True)]
    ppermute x21 -> x18, waiting for transfers between devices: 25.4 us -> 37.9 us  [swap(): return lax.ppermute(array, 'shell', [(i, i ^ bit) for i in range(n)])]
    all_to_all x0 -> x1, starting transfers between devices: none -> 7.39 us  [short_way(): got = lax.all_to_all(send, 'shell', split_axis=0, concat_axis=0, tiled=True)]
    ppermute x21 -> x18, starting transfers between devices: 16.1 us -> 10.9 us  [swap(): return lax.ppermute(array, 'shell', [(i, i ^ bit) for i in range(n)])]
  transfers between devices with their start and end apart: 21 -> 19, of which waited for: 6 -> 8; matrix products, arithmetic and copies ran while one was open for 0% -> 0% of each run, Pallas kernels for 10% -> 11%
where the time goes in v14:
time: 93.4 us; the launch traced here: 93 us
  waiting for transfers between devices  37.9 us (41%)
  Pallas kernels  20.6 us (22%)
  starting transfers between devices  18.3 us (20%)
  between operations  14.1 us (15%)
  local copies, waits for them, and re-layouts  1.58 us (2%)
    ppermute x18, waiting for transfers between devices, swap(): return lax.ppermute(array, 'shell', [(i, i ^ bit) for i in range(n)])  37.9 us
    ppermute x18, starting transfers between devices, swap(): return lax.ppermute(array, 'shell', [(i, i ^ bit) for i in range(n)])  10.9 us
    pallas_call x1, Pallas kernels, short_way(): pl.pallas_call(functools.partial(half_kernel, here, early), out_shape=(sh...  8.67 us
    all_to_all x1, starting transfers between devices, short_way(): got = lax.all_to_all(send, 'shell', split_axis=0, concat_axis=0, tiled=True)  7.39 us
    pallas_call x1, Pallas kernels, short_way(): pl.pallas_call(functools.partial(last_kernel, count, early), out_shape=sh...  7.31 us
    pallas_call x1, Pallas kernels, short_way(): pl.pallas_call(functools.partial(pick_kernel, here), out_shape=(shape(CAP...  2.22 us
  transfers between devices with their start and end apart: 19, of which 8 were waited for; matrix products, arithmetic and copies ran while one was open for 0% of the time, Pallas kernels for 11%

profile of v14, /device:TPU:0, one launch (start us, length us, event | category | flops | bytes accessed | tf_op | source)
XLA Modules:
  0.0 93.0 jit_solution(9075703520782334363)
XLA Ops:
  7.2 0.9 copy-done
  8.1 0.7 copy-done.1
  8.8 0.8 pack_panels.1
  9.6 7.4 %all-to-all-start = ((bf16[16,17,256]{2,1,0:T(8,128)(2,1)}), bf16[16,17,256]{2,1,0:T(8,128)(2,1)S(1)}, u32[]{:S(2)}, u32[]{:S(2)}) async-start(bf16[16,17,256]{2,1,0:T(8,128)(2,1)} %pack_panels.1), calls=%async_computation | async-start | bytes 393216 | tf_op jit(solution)/shard_map/all_to_all | solution.py:400
  17.0 1.5 %pack_rows.1 = (bf16[80,1280]{1,0:T(8,128)(2,1)S(1)}, bf16[80,1280]{1,0:T(8,128)(2,1)S(1)}, bf16[80,1280]{1,0:T(8,128)(2,1)S(1)}, bf16[80,1280]{1,0:T(8,128)(2,1)S(1)}) custom-call(bf16[160,2304]{1,0:T(8,128)(2,1)} %vir_ref.1, bf16[160,256]{1,0:T(8,128)(2,1)} %occ_ref.1), custom_call_target="tpu_custom_call" | custom-call | flops 300000000 | bytes 3000000 | tf_op jit(solution)/shard_map/pack_rows/pallas_call | solution.py:381
  18.6 0.5 collective-permute-start
  19.0 1.7 %collective-permute-start.1 = (bf16[80,1280]{1,0:T(8,128)(2,1)S(1)}, bf16[80,1280]{1,0:T(8,128)(2,1)S(1)}, u32[]{:S(2)}, u32[]{:S(2)}) collective-permute-start(bf16[80,1280]{1,0:T(8,128)(2,1)S(1)} %get-tuple-element.144), channel_id=1, source_target_pairs={{0,2},{1,3},{2,0},{3,1},{4,6},{5,7},{6,4},{7,5},{8,10},{9,11},{10,... | collective-permute-start | bytes 614408 | tf_op jit(solution)/shard_map/ppermute | solution.py:379
  20.7 0.0 collective-permute-start.2
  20.7 0.0 collective-permute-done.refs_1_
  20.7 7.0 %collective-permute-done.1.refs_2_ = bf16[80,1280]{1,0:T(8,128)(2,1)S(1)} collective-permute-done((bf16[80,1280]{1,0:T(8,128)(2,1)S(1)}, bf16[80,1280]{1,0:T(8,128)(2,1)S(1)}, u32[]{:S(2)}, u32[]{:S(2)}) %collective-permute-start.1) | collective-permute-done | bytes 204832 | tf_op jit(solution)/shard_map/ppermute | solution.py:379
  27.7 3.7 %collective-permute-done.2.refs_3_ = bf16[80,1280]{1,0:T(8,128)(2,1)S(1)} collective-permute-done((bf16[80,1280]{1,0:T(8,128)(2,1)S(1)}, bf16[80,1280]{1,0:T(8,128)(2,1)S(1)}, u32[]{:S(2)}, u32[]{:S(2)}) %collective-permute-start.2) | collective-permute-done | bytes 204832 | tf_op jit(solution)/shard_map/ppermute | solution.py:379
  31.5 2.2 %pick_rows.1 = (bf16[128,1280]{1,0:T(8,128)(2,1)S(1)}, s32[1]{0:T(128)}, s32[1]{0:T(128)}) custom-call(bf16[16,17,256]{2,1,0:T(8,128)(2,1)S(1)} %all-to-all-done.got_ref, s32[1,256]{1,0:T(1,128)} %bitcast.63, bf16[80,1280]{1,0:T(8,128)(2,1)S(1)} %get-tuple-element.142.refs_0_, bf16[80,1280]{1,0:T(8,128)(2,1)S(1)} %collective-permute-done.refs_1_, ...), custom_call_target="tpu_custom_call" | custom-call | flops 300000000 | bytes 2000000 | tf_op jit(solution)/shard_map/pick_rows/pallas_call | solution.py:402
  33.7 1.3 %collective-permute-start.4 = (bf16[128,1280]{1,0:T(8,128)(2,1)S(1)}, bf16[128,1280]{1,0:T(8,128)(2,1)S(1)}, u32[]{:S(2)}, u32[]{:S(2)}) collective-permute-start(bf16[128,1280]{1,0:T(8,128)(2,1)S(1)} %get-tuple-element.148.refs_0_), channel_id=1, source_target_pairs={{0,2},{1,3},{2,0},{3,1},{4,6},{5,7},{6,4},{7,5},{8,10},{9,11},{10,... | collective-permute-start | bytes 983048 | tf_op jit(solution)/shard_map/ppermute | solution.py:379
  35.1 1.5 %collective-permute-start.5 = (bf16[128,1280]{1,0:T(8,128)(2,1)S(1)}, bf16[128,1280]{1,0:T(8,128)(2,1)S(1)}, u32[]{:S(2)}, u32[]{:S(2)}) collective-permute-start(bf16[128,1280]{1,0:T(8,128)(2,1)S(1)} %get-tuple-element.148.refs_0_), channel_id=1, source_target_pairs={{0,4},{1,5},{2,6},{3,7},{4,0},{5,1},{6,2},{7,3},{8,12},{9,13},{10,... | collective-permute-start | bytes 983048 | tf_op jit(solution)/shard_map/ppermute | solution.py:379
  36.5 2.0 %collective-permute-start.3 = (bf16[128,1280]{1,0:T(8,128)(2,1)S(1)}, bf16[128,1280]{1,0:T(8,128)(2,1)S(1)}, u32[]{:S(2)}, u32[]{:S(2)}) collective-permute-start(bf16[128,1280]{1,0:T(8,128)(2,1)S(1)} %get-tuple-element.148.refs_0_), channel_id=1, source_target_pairs={{0,8},{1,9},{2,10},{3,11},{4,12},{5,13},{6,14},{7,15},{8,0},{9,1},... | collective-permute-start | bytes 983048 | tf_op jit(solution)/shard_map/ppermute | solution.py:379
  38.5 5.0 %collective-permute-done.4.refs_1_ = bf16[128,1280]{1,0:T(8,128)(2,1)S(1)} collective-permute-done((bf16[128,1280]{1,0:T(8,128)(2,1)S(1)}, bf16[128,1280]{1,0:T(8,128)(2,1)S(1)}, u32[]{:S(2)}, u32[]{:S(2)}) %collective-permute-start.4) | collective-permute-done | bytes 327712 | tf_op jit(solution)/shard_map/ppermute | solution.py:379
  43.5 0.0 collective-permute-start.7
  43.5 7.6 %collective-permute-done.5.refs_2_ = bf16[128,1280]{1,0:T(8,128)(2,1)S(1)} collective-permute-done((bf16[128,1280]{1,0:T(8,128)(2,1)S(1)}, bf16[128,1280]{1,0:T(8,128)(2,1)S(1)}, u32[]{:S(2)}, u32[]{:S(2)}) %collective-permute-start.5) | collective-permute-done | bytes 327712 | tf_op jit(solution)/shard_map/ppermute | solution.py:379
  51.1 2.7 %collective-permute-done.3.refs_3_ = bf16[128,1280]{1,0:T(8,128)(2,1)S(1)} collective-permute-done((bf16[128,1280]{1,0:T(8,128)(2,1)S(1)}, bf16[128,1280]{1,0:T(8,128)(2,1)S(1)}, u32[]{:S(2)}, u32[]{:S(2)}) %collective-permute-start.3) | collective-permute-done | bytes 327712 | tf_op jit(solution)/shard_map/ppermute | solution.py:379
  53.8 0.2 collective-permute-start.9
  54.0 1.0 %collective-permute-start.11 = (bf16[128,1280]{1,0:T(8,128)(2,1)S(1)}, bf16[128,1280]{1,0:T(8,128)(2,1)S(1)}, u32[]{:S(2)}, u32[]{:S(2)}) collective-permute-start(bf16[128,1280]{1,0:T(8,128)(2,1)S(1)} %collective-permute-done.3.refs_3_), channel_id=1, source_target_pairs={{0,2},{1,3},{2,0},{3,1},{4,6},{5,7},{6,4},{7,5},{8,10},{9,11},{10,... | collective-permute-start | bytes 983048 | tf_op jit(solution)/shard_map/ppermute | solution.py:379
  55.0 1.0 %collective-permute-start.10 = (bf16[128,1280]{1,0:T(8,128)(2,1)S(1)}, bf16[128,1280]{1,0:T(8,128)(2,1)S(1)}, u32[]{:S(2)}, u32[]{:S(2)}) collective-permute-start(bf16[128,1280]{1,0:T(8,128)(2,1)S(1)} %collective-permute-done.5.refs_2_), channel_id=1, source_target_pairs={{0,2},{1,3},{2,0},{3,1},{4,6},{5,7},{6,4},{7,5},{8,10},{9,11},{10,... | collective-permute-start | bytes 983048 | tf_op jit(solution)/shard_map/ppermute | solution.py:379
  56.0 8.7 %half_transform.1 = (f32[512,1024]{1,0:T(8,128)S(1)}, bf16[2,640,1024]{2,1,0:T(8,128)(2,1)S(1)}, bf16[16,16,256]{2,1,0:T(8,128)(2,1)S(1)}, f32[16,256]{1,0:T(8,128)S(1)}) custom-call(bf16[16,17,256]{2,1,0:T(8,128)(2,1)S(1)} %all-to-all-done.got_ref, s32[1,256]{1,0:T(1,128)} %bitcast.64, bf16[128,1280]{1,0:T(8,128)(2,1)S(1)} %get-tuple-element.148.refs_0_, ...), custom_call_target="tpu_custom_call" | custom-call | flops 7000000000 | bytes 1 | tf_op jit(solution)/shard_map/half_transform/pallas_call | solution.py:420
  64.7 1.1 %collective-permute-start.12 = (bf16[128,1280]{1,0:T(8,128)(2,1)S(1)}, bf16[128,1280]{1,0:T(8,128)(2,1)S(1)}, u32[]{:S(2)}, u32[]{:S(2)}) collective-permute-start(bf16[128,1280]{1,0:T(8,128)(2,1)S(1)} %collective-permute-done.9.refs_6_), channel_id=1, source_target_pairs={{0,2},{1,3},{2,0},{3,1},{4,6},{5,7},{6,4},{7,5},{8,10},{9,11},{10,... | collective-permute-start | bytes 983048 | tf_op jit(solution)/shard_map/ppermute | solution.py:379
  65.8 5.5 %collective-permute-done.10.refs_4_ = bf16[128,1280]{1,0:T(8,128)(2,1)S(1)} collective-permute-done((bf16[128,1280]{1,0:T(8,128)(2,1)S(1)}, bf16[128,1280]{1,0:T(8,128)(2,1)S(1)}, u32[]{:S(2)}, u32[]{:S(2)}) %collective-permute-start.10) | collective-permute-done | bytes 327712 | tf_op jit(solution)/shard_map/ppermute | solution.py:379
  71.4 0.5 collective-permute-start.15
  71.9 0.0 collective-permute-start.16
  71.9 4.6 %collective-permute-done.12.refs_7_ = bf16[128,1280]{1,0:T(8,128)(2,1)S(1)} collective-permute-done((bf16[128,1280]{1,0:T(8,128)(2,1)S(1)}, bf16[128,1280]{1,0:T(8,128)(2,1)S(1)}, u32[]{:S(2)}, u32[]{:S(2)}) %collective-permute-start.12) | collective-permute-done | bytes 327712 | tf_op jit(solution)/shard_map/ppermute | solution.py:379
  76.6 0.1 collective-permute-start.17
  76.7 1.6 %collective-permute-done.17.refs_15_ = bf16[128,1280]{1,0:T(8,128)(2,1)S(1)} collective-permute-done((bf16[128,1280]{1,0:T(8,128)(2,1)S(1)}, bf16[128,1280]{1,0:T(8,128)(2,1)S(1)}, u32[]{:S(2)}, u32[]{:S(2)}) %collective-permute-start.17) | collective-permute-done | bytes 327712 | tf_op jit(solution)/shard_map/ppermute | solution.py:379
  78.3 7.3 %last_product.1 = bf16[2,256,2304]{2,1,0:T(8,128)(2,1)} custom-call(s32[1]{0:T(128)} %get-tuple-element.147.me_ref, f32[512,1024]{1,0:T(8,128)S(1)} %get-tuple-element.157.part_any, bf16[2,640,1024]{2,1,0:T(8,128)(2,1)S(1)} %get-tuple-element.158.late_any, bf16[128,1280]{1,0:T(8,128)(2,1)S(1)} %get-tuple-element.148.refs_0_, ...), custom_call_target="tpu_custom_call" | custom-call | flops 20000000000 | bytes 1 | tf_op jit(solution)/shard_map/last_product/pallas_call | solution.py:457
  85.6 0.6 while.16
  (18 shorter events, 0.0 us)
Async XLA Ops:
  7.2 0.9 copy-start
  8.1 0.7 copy-start.1
  9.6 21.9 %all-to-all-start = ((bf16[16,17,256]{2,1,0:T(8,128)(2,1)}), bf16[16,17,256]{2,1,0:T(8,128)(2,1)S(1)}, u32[]{:S(2)}, u32[]{:S(2)}) async-start(bf16[16,17,256]{2,1,0:T(8,128)(2,1)} %pack_panels.1), calls=%async_computation | async-start | bytes 393216 | tf_op jit(solution)/shard_map/all_to_all | solution.py:400
  18.6 2.2 %collective-permute-start = (bf16[80,1280]{1,0:T(8,128)(2,1)S(1)}, bf16[80,1280]{1,0:T(8,128)(2,1)S(1)}, u32[]{:S(2)}, u32[]{:S(2)}) collective-permute-start(bf16[80,1280]{1,0:T(8,128)(2,1)S(1)} %get-tuple-element.143), channel_id=1, source_target_pairs={{0,1},{1,0},{2,3},{3,2},{4,5},{5,4},{6,7},{7,6},{8,9},{9,8},{10,11... | collective-permute-start | bytes 614408 | tf_op jit(solution)/shard_map/ppermute | solution.py:379
  19.0 8.7 %collective-permute-start.1 = (bf16[80,1280]{1,0:T(8,128)(2,1)S(1)}, bf16[80,1280]{1,0:T(8,128)(2,1)S(1)}, u32[]{:S(2)}, u32[]{:S(2)}) collective-permute-start(bf16[80,1280]{1,0:T(8,128)(2,1)S(1)} %get-tuple-element.144), channel_id=1, source_target_pairs={{0,2},{1,3},{2,0},{3,1},{4,6},{5,7},{6,4},{7,5},{8,10},{9,11},{10,... | collective-permute-start | bytes 614408 | tf_op jit(solution)/shard_map/ppermute | solution.py:379
  20.7 10.8 %collective-permute-start.2 = (bf16[80,1280]{1,0:T(8,128)(2,1)S(1)}, bf16[80,1280]{1,0:T(8,128)(2,1)S(1)}, u32[]{:S(2)}, u32[]{:S(2)}) collective-permute-start(bf16[80,1280]{1,0:T(8,128)(2,1)S(1)} %get-tuple-element.145), channel_id=1, source_target_pairs={{0,3},{1,2},{2,1},{3,0},{4,7},{5,6},{6,5},{7,4},{8,11},{9,10},{10,... | collective-permute-start | bytes 614408 | tf_op jit(solution)/shard_map/ppermute | solution.py:379
  33.7 9.8 %collective-permute-start.4 = (bf16[128,1280]{1,0:T(8,128)(2,1)S(1)}, bf16[128,1280]{1,0:T(8,128)(2,1)S(1)}, u32[]{:S(2)}, u32[]{:S(2)}) collective-permute-start(bf16[128,1280]{1,0:T(8,128)(2,1)S(1)} %get-tuple-element.148.refs_0_), channel_id=1, source_target_pairs={{0,2},{1,3},{2,0},{3,1},{4,6},{5,7},{6,4},{7,5},{8,10},{9,11},{10,... | collective-permute-start | bytes 983048 | tf_op jit(solution)/shard_map/ppermute | solution.py:379
  35.1 16.1 %collective-permute-start.5 = (bf16[128,1280]{1,0:T(8,128)(2,1)S(1)}, bf16[128,1280]{1,0:T(8,128)(2,1)S(1)}, u32[]{:S(2)}, u32[]{:S(2)}) collective-permute-start(bf16[128,1280]{1,0:T(8,128)(2,1)S(1)} %get-tuple-element.148.refs_0_), channel_id=1, source_target_pairs={{0,4},{1,5},{2,6},{3,7},{4,0},{5,1},{6,2},{7,3},{8,12},{9,13},{10,... | collective-permute-start | bytes 983048 | tf_op jit(solution)/shard_map/ppermute | solution.py:379
  36.5 17.3 %collective-permute-start.3 = (bf16[128,1280]{1,0:T(8,128)(2,1)S(1)}, bf16[128,1280]{1,0:T(8,128)(2,1)S(1)}, u32[]{:S(2)}, u32[]{:S(2)}) collective-permute-start(bf16[128,1280]{1,0:T(8,128)(2,1)S(1)} %get-tuple-element.148.refs_0_), channel_id=1, source_target_pairs={{0,8},{1,9},{2,10},{3,11},{4,12},{5,13},{6,14},{7,15},{8,0},{9,1},... | collective-permute-start | bytes 983048 | tf_op jit(solution)/shard_map/ppermute | solution.py:379
  38.5 15.3 %collective-permute-start.6 = (bf16[128,1280]{1,0:T(8,128)(2,1)S(1)}, bf16[128,1280]{1,0:T(8,128)(2,1)S(1)}, u32[]{:S(2)}, u32[]{:S(2)}) collective-permute-start(bf16[128,1280]{1,0:T(8,128)(2,1)S(1)} %get-tuple-element.148.refs_0_), channel_id=1, source_target_pairs={{0,1},{1,0},{2,3},{3,2},{4,5},{5,4},{6,7},{7,6},{8,9},{9,8},{10,11... | collective-permute-start | bytes 983048 | tf_op jit(solution)/shard_map/ppermute | solution.py:379
  43.5 10.3 %collective-permute-start.7 = (bf16[128,1280]{1,0:T(8,128)(2,1)S(1)}, bf16[128,1280]{1,0:T(8,128)(2,1)S(1)}, u32[]{:S(2)}, u32[]{:S(2)}) collective-permute-start(bf16[128,1280]{1,0:T(8,128)(2,1)S(1)} %collective-permute-done.4.refs_1_), channel_id=1, source_target_pairs={{0,1},{1,0},{2,3},{3,2},{4,5},{5,4},{6,7},{7,6},{8,9},{9,8},{10,11... | collective-permute-start | bytes 983048 | tf_op jit(solution)/shard_map/ppermute | solution.py:379
  51.1 2.7 %collective-permute-start.8 = (bf16[128,1280]{1,0:T(8,128)(2,1)S(1)}, bf16[128,1280]{1,0:T(8,128)(2,1)S(1)}, u32[]{:S(2)}, u32[]{:S(2)}) collective-permute-start(bf16[128,1280]{1,0:T(8,128)(2,1)S(1)} %collective-permute-done.5.refs_2_), channel_id=1, source_target_pairs={{0,1},{1,0},{2,3},{3,2},{4,5},{5,4},{6,7},{7,6},{8,9},{9,8},{10,11... | collective-permute-start | bytes 983048 | tf_op jit(solution)/shard_map/ppermute | solution.py:379
  53.8 10.9 %collective-permute-start.9 = (bf16[128,1280]{1,0:T(8,128)(2,1)S(1)}, bf16[128,1280]{1,0:T(8,128)(2,1)S(1)}, u32[]{:S(2)}, u32[]{:S(2)}) collective-permute-start(bf16[128,1280]{1,0:T(8,128)(2,1)S(1)} %collective-permute-done.3.refs_3_), channel_id=1, source_target_pairs={{0,4},{1,5},{2,6},{3,7},{4,0},{5,1},{6,2},{7,3},{8,12},{9,13},{10,... | collective-permute-start | bytes 983048 | tf_op jit(solution)/shard_map/ppermute | solution.py:379
  54.0 17.4 %collective-permute-start.11 = (bf16[128,1280]{1,0:T(8,128)(2,1)S(1)}, bf16[128,1280]{1,0:T(8,128)(2,1)S(1)}, u32[]{:S(2)}, u32[]{:S(2)}) collective-permute-start(bf16[128,1280]{1,0:T(8,128)(2,1)S(1)} %collective-permute-done.3.refs_3_), channel_id=1, source_target_pairs={{0,2},{1,3},{2,0},{3,1},{4,6},{5,7},{6,4},{7,5},{8,10},{9,11},{10,... | collective-permute-start | bytes 983048 | tf_op jit(solution)/shard_map/ppermute | solution.py:379
  55.0 16.9 %collective-permute-start.13 = (bf16[128,1280]{1,0:T(8,128)(2,1)S(1)}, bf16[128,1280]{1,0:T(8,128)(2,1)S(1)}, u32[]{:S(2)}, u32[]{:S(2)}) collective-permute-start(bf16[128,1280]{1,0:T(8,128)(2,1)S(1)} %collective-permute-done.3.refs_3_), channel_id=1, source_target_pairs={{0,1},{1,0},{2,3},{3,2},{4,5},{5,4},{6,7},{7,6},{8,9},{9,8},{10,11... | collective-permute-start | bytes 983048 | tf_op jit(solution)/shard_map/ppermute | solution.py:379
  55.0 16.4 %collective-permute-start.10 = (bf16[128,1280]{1,0:T(8,128)(2,1)S(1)}, bf16[128,1280]{1,0:T(8,128)(2,1)S(1)}, u32[]{:S(2)}, u32[]{:S(2)}) collective-permute-start(bf16[128,1280]{1,0:T(8,128)(2,1)S(1)} %collective-permute-done.5.refs_2_), channel_id=1, source_target_pairs={{0,2},{1,3},{2,0},{3,1},{4,6},{5,7},{6,4},{7,5},{8,10},{9,11},{10,... | collective-permute-start | bytes 983048 | tf_op jit(solution)/shard_map/ppermute | solution.py:379
  64.7 11.9 %collective-permute-start.12 = (bf16[128,1280]{1,0:T(8,128)(2,1)S(1)}, bf16[128,1280]{1,0:T(8,128)(2,1)S(1)}, u32[]{:S(2)}, u32[]{:S(2)}) collective-permute-start(bf16[128,1280]{1,0:T(8,128)(2,1)S(1)} %collective-permute-done.9.refs_6_), channel_id=1, source_target_pairs={{0,2},{1,3},{2,0},{3,1},{4,6},{5,7},{6,4},{7,5},{8,10},{9,11},{10,... | collective-permute-start | bytes 983048 | tf_op jit(solution)/shard_map/ppermute | solution.py:379
  71.4 5.2 %collective-permute-start.14 = (bf16[128,1280]{1,0:T(8,128)(2,1)S(1)}, bf16[128,1280]{1,0:T(8,128)(2,1)S(1)}, u32[]{:S(2)}, u32[]{:S(2)}) collective-permute-start(bf16[128,1280]{1,0:T(8,128)(2,1)S(1)} %collective-permute-done.10.refs_4_), channel_id=1, source_target_pairs={{0,1},{1,0},{2,3},{3,2},{4,5},{5,4},{6,7},{7,6},{8,9},{9,8},{10,11... | collective-permute-start | bytes 983048 | tf_op jit(solution)/shard_map/ppermute | solution.py:379
  71.4 5.2 %collective-permute-start.15 = (bf16[128,1280]{1,0:T(8,128)(2,1)S(1)}, bf16[128,1280]{1,0:T(8,128)(2,1)S(1)}, u32[]{:S(2)}, u32[]{:S(2)}) collective-permute-start(bf16[128,1280]{1,0:T(8,128)(2,1)S(1)} %collective-permute-done.11.refs_5_), channel_id=1, source_target_pairs={{0,1},{1,0},{2,3},{3,2},{4,5},{5,4},{6,7},{7,6},{8,9},{9,8},{10,11... | collective-permute-start | bytes 983048 | tf_op jit(solution)/shard_map/ppermute | solution.py:379
  71.9 4.7 %collective-permute-start.16 = (bf16[128,1280]{1,0:T(8,128)(2,1)S(1)}, bf16[128,1280]{1,0:T(8,128)(2,1)S(1)}, u32[]{:S(2)}, u32[]{:S(2)}) collective-permute-start(bf16[128,1280]{1,0:T(8,128)(2,1)S(1)} %collective-permute-done.9.refs_6_), channel_id=1, source_target_pairs={{0,1},{1,0},{2,3},{3,2},{4,5},{5,4},{6,7},{7,6},{8,9},{9,8},{10,11... | collective-permute-start | bytes 983048 | tf_op jit(solution)/shard_map/ppermute | solution.py:379
  76.6 1.7 %collective-permute-start.17 = (bf16[128,1280]{1,0:T(8,128)(2,1)S(1)}, bf16[128,1280]{1,0:T(8,128)(2,1)S(1)}, u32[]{:S(2)}, u32[]{:S(2)}) collective-permute-start(bf16[128,1280]{1,0:T(8,128)(2,1)S(1)} %collective-permute-done.12.refs_7_), channel_id=1, source_target_pairs={{0,1},{1,0},{2,3},{3,2},{4,5},{5,4},{6,7},{7,6},{8,9},{9,8},{10,11... | collective-permute-start | bytes 983048 | tf_op jit(solution)/shard_map/ppermute | solution.py:379
  78.3 7.3 %copy-start.3 = (s32[256]{0:T(256)S(1)}, s32[256]{0:T(256)}, u32[]{:S(2)}) copy-start(s32[256]{0:T(256)} %param.11) | copy-start | bytes 3076

commit v15 on v13

--- a/solution.py
+++ b/solution.py
@@ -414,13 +414,18 @@
         name="pick_rows",
     )(code, size_row, keep, to_core, to_y, to_both)
 
-    across, mine_y, beside = swap(mine, 8), swap(mine, 2), swap(mine, 4)
+    beside, mine_y, far = swap(mine, 4), swap(mine, 2), [swap(mine, 1)]
+    mine, far[0] = lax.optimization_barrier((mine, far[0]))
+    across = swap(mine, 8)
+    beside, mine_y = lax.optimization_barrier((beside, mine_y))
+
+    beside_y = swap(beside, 2)
+    far += [swap(mine_y, 1), swap(beside, 1)]
+    *panel, far[1], far[2] = lax.optimization_barrier((*panel, far[1], far[2]))
     panel = [panel[0]] + [swap(panel[r], 4 * r) for r in range(1, Z)]
-    mine_y, panel[1], panel[2] = lax.optimization_barrier((mine_y, panel[1], panel[2]))
-    far = [swap(mine, 1), swap(mine_y, 1), swap(beside, 1)]
-    across, beside, panel[3], *far = lax.optimization_barrier((across, beside, panel[3], *far))
-
-    corner, beside_y, across_y = swap(across, 4), swap(beside, 2), swap(across, 2)
+    across, beside_y, *panel = lax.optimization_barrier((across, beside_y, *panel))
+
+    corner, across_y = swap(across, 4), swap(across, 2)
     near = [mine, mine_y, beside]
     early = len(near)
     slots = LIVE_DEV * n * EDGE

time: 90.9 us -> 96.5 us (1.062)
  waiting for transfers between devices: 25.4 us -> 29.8 us
  starting transfers between devices: 16.1 us -> 17.2 us
    ppermute x21, waiting for transfers between devices: 25.4 us -> 29.8 us  [swap(): return lax.ppermute(array, 'shell', [(i, i ^ bit) for i in range(n)])]
    ppermute x21, starting transfers between devices: 16.1 us -> 17.2 us  [swap(): return lax.ppermute(array, 'shell', [(i, i ^ bit) for i in range(n)])]
  transfers between devices with their start and end apart: 21 -> 21, of which waited for: 6 -> 6; matrix products, arithmetic and copies ran while one was open for 0% -> 0% of each run, Pallas kernels for 10% -> 9%
where the time goes in v15:
time: 96.5 us; the launch traced here: 96.3 us
  waiting for transfers between devices  29.8 us (31%)
  Pallas kernels  20.1 us (21%)
  starting transfers between devices  17.2 us (18%)
  between operations  14.1 us (15%)
  blocking collectives  12.8 us (13%)
  local copies, waits for them, and re-layouts  1.58 us (2%)
    ppermute x21, waiting for transfers between devices, swap(): return lax.ppermute(array, 'shell', [(i, i ^ bit) for i in range(n)])  29.8 us
    ppermute x21, starting transfers between devices, swap(): return lax.ppermute(array, 'shell', [(i, i ^ bit) for i in range(n)])  17.2 us
    all_to_all x1, blocking collectives, short_way(): lax.all_to_all(code, 'shell', split_axis=0, concat_axis=0, tiled=True)  12.8 us
    pallas_call x1, Pallas kernels, short_way(): pl.pallas_call(functools.partial(half_kernel, here, early), out_shape=(sh...  8.78 us
    pallas_call x1, Pallas kernels, short_way(): pl.pallas_call(functools.partial(last_kernel, count, early), out_shape=sh...  7.38 us
    pallas_call x1, Pallas kernels, short_way(): pl.pallas_call(functools.partial(pick_kernel, here), out_shape=[shape(CAP...  2.16 us
  transfers between devices with their start and end apart: 21, of which 6 were waited for; matrix products, arithmetic and copies ran while one was open for 0% of the time, Pallas kernels for 9%

profile of v15, /device:TPU:0, one launch (start us, length us, event | category | flops | bytes accessed | tf_op | source)
XLA Modules:
  0.0 96.3 jit_solution(4863772446619723211)
XLA Ops:
  6.5 0.9 copy-done.1
  7.4 1.6 %pack_rows.1 = (bf16[96,1280]{1,0:T(8,128)(2,1)S(1)}, bf16[96,1280]{1,0:T(8,128)(2,1)S(1)}, bf16[96,1280]{1,0:T(8,128)(2,1)S(1)}, bf16[96,1280]{1,0:T(8,128)(2,1)S(1)}) custom-call(bf16[160,2304]{1,0:T(8,128)(2,1)} %vir_ref.1, bf16[160,256]{1,0:T(8,128)(2,1)} %occ_ref.1, bf16[8,32,256]{2,1,0:T(8,128)(2,1)S(1)} %copy-done.1), custom_call_target="tpu_custom_call" | custom-call | flops 300000000 | bytes 3000000 | tf_op jit(solution)/shard_map/pack_rows/pallas_call | solution.py:384
  9.0 0.5 collective-permute-start
  9.5 2.6 %collective-permute-start.1 = (bf16[96,1280]{1,0:T(8,128)(2,1)S(1)}, bf16[96,1280]{1,0:T(8,128)(2,1)S(1)}, u32[]{:S(2)}, u32[]{:S(2)}) collective-permute-start(bf16[96,1280]{1,0:T(8,128)(2,1)S(1)} %get-tuple-element.251), channel_id=1, source_target_pairs={{0,2},{1,3},{2,0},{3,1},{4,6},{5,7},{6,4},{7,5},{8,10},{9,11},{10,... | collective-permute-start | bytes 737288 | tf_op jit(solution)/shard_map/ppermute | solution.py:382
  12.1 0.1 collective-permute-start.2
  12.9 0.0 copy-start
  12.9 0.7 copy-done
  13.5 0.2 pack_ids.1
  13.7 12.8 %all_to_all.5.code_ref = s32[16,8,128]{2,1,0:T(8,128)S(1)} all-to-all(s32[16,8,128]{2,1,0:T(8,128)S(1)} %pack_ids.1), channel_id=1, replica_groups=mesh['groups'=2,'shell'=16] {'shell'}, dimensions={0} | all-to-all | bytes 131072 | tf_op jit(solution)/shard_map/all_to_all | solution.py:404
  26.5 2.2 %pick_rows.1 = (bf16[128,1280]{1,0:T(8,128)(2,1)S(1)}, s32[1]{0:T(128)}, s32[1]{0:T(128)}, bf16[4,16,256]{2,1,0:T(8,128)(2,1)S(1)}, bf16[4,16,256]{2,1,0:T(8,128...) custom-call(s32[16,8,128]{2,1,0:T(8,128)S(1)} %all_to_all.5.code_ref, s32[1,256]{1,0:T(1,128)} %bitcast.87, ...), custom_call_target="tpu_custom_call" | custom-call | flops 300000000 | bytes 2000000 | tf_op jit(solution)/shard_map/pick_rows/pallas_call | solution.py:406
  28.7 0.2 collective-permute-start.5
  28.9 1.3 %collective-permute-start.6 = (bf16[128,1280]{1,0:T(8,128)(2,1)S(1)}, bf16[128,1280]{1,0:T(8,128)(2,1)S(1)}, u32[]{:S(2)}, u32[]{:S(2)}) collective-permute-start(bf16[128,1280]{1,0:T(8,128)(2,1)S(1)} %get-tuple-element.256.refs_4_.refs_0_), channel_id=1, source_target_pairs={{0,2},{1,3},{2,0},{3,1},{4,6},{5,7},{6,4},{7,5},{8,10},{9,11},{10,... | collective-permute-start | bytes 983048 | tf_op jit(solution)/shard_map/ppermute | solution.py:382
  30.2 7.7 %collective-permute-done.5.refs_6_.refs_2_ = bf16[128,1280]{1,0:T(8,128)(2,1)S(1)} collective-permute-done((bf16[128,1280]{1,0:T(8,128)(2,1)S(1)}, bf16[128,1280]{1,0:T(8,128)(2,1)S(1)}, u32[]{:S(2)}, u32[]{:S(2)}) %collective-permute-start.5) | collective-permute-done | bytes 327712 | tf_op jit(solution)/shard_map/ppermute | solution.py:382
  38.0 0.4 collective-permute-done.6.refs_5_.refs_1_
  38.4 0.5 collective-permute-start.9
  38.9 2.4 %collective-permute-start.4 = (bf16[128,1280]{1,0:T(8,128)(2,1)S(1)}, bf16[128,1280]{1,0:T(8,128)(2,1)S(1)}, u32[]{:S(2)}, u32[]{:S(2)}) collective-permute-start(bf16[128,1280]{1,0:T(8,128)(2,1)S(1)} %get-tuple-element.256.refs_4_.refs_0_), channel_id=1, source_target_pairs={{0,8},{1,9},{2,10},{3,11},{4,12},{5,13},{6,14},{7,15},{8,0},{9,1},... | collective-permute-start | bytes 983048 | tf_op jit(solution)/shard_map/ppermute | solution.py:382
  41.2 1.2 %collective-permute-start.7 = (bf16[128,1280]{1,0:T(8,128)(2,1)S(1)}, bf16[128,1280]{1,0:T(8,128)(2,1)S(1)}, u32[]{:S(2)}, u32[]{:S(2)}) collective-permute-start(bf16[128,1280]{1,0:T(8,128)(2,1)S(1)} %collective-permute-done.5.refs_6_.refs_2_), channel_id=1, source_target_pairs={{0,2},{1,3},{2,0},{3,1},{4,6},{5,7},{6,4},{7,5},{8,10},{9,11},{10,... | collective-permute-start | bytes 983048 | tf_op jit(solution)/shard_map/ppermute | solution.py:382
  42.4 0.5 collective-permute-start.10
  42.9 0.9 collective-permute-start.11
  43.8 3.0 %collective-permute-start.12 = (bf16[4,16,256]{2,1,0:T(8,128)(2,1)S(1)}, bf16[4,16,256]{2,1,0:T(8,128)(2,1)S(1)}, u32[]{:S(2)}, u32[]{:S(2)}) collective-permute-start(bf16[4,16,256]{2,1,0:T(8,128)(2,1)S(1)} %get-tuple-element.266), channel_id=1, source_target_pairs={{0,12},{1,13},{2,14},{3,15},{4,8},{5,9},{6,10},{7,11},{8,4},{9,5},... | collective-permute-start | bytes 98312 | tf_op jit(solution)/shard_map/ppermute | solution.py:382
  46.8 11.7 %collective-permute-done.4.refs_3_ = bf16[128,1280]{1,0:T(8,128)(2,1)S(1)} collective-permute-done((bf16[128,1280]{1,0:T(8,128)(2,1)S(1)}, bf16[128,1280]{1,0:T(8,128)(2,1)S(1)}, u32[]{:S(2)}, u32[]{:S(2)}) %collective-permute-start.4) | collective-permute-done | bytes 327712 | tf_op jit(solution)/shard_map/ppermute | solution.py:382
  58.5 0.3 collective-permute-done.11.refs_2_
  58.9 0.9 collective-permute-start.13
  59.8 1.0 %collective-permute-start.14 = (bf16[128,1280]{1,0:T(8,128)(2,1)S(1)}, bf16[128,1280]{1,0:T(8,128)(2,1)S(1)}, u32[]{:S(2)}, u32[]{:S(2)}) collective-permute-start(bf16[128,1280]{1,0:T(8,128)(2,1)S(1)} %collective-permute-done.4.refs_3_), channel_id=1, source_target_pairs={{0,2},{1,3},{2,0},{3,1},{4,6},{5,7},{6,4},{7,5},{8,10},{9,11},{10,... | collective-permute-start | bytes 983048 | tf_op jit(solution)/shard_map/ppermute | solution.py:382
  60.8 0.5 collective-permute-start.17
  61.3 8.8 %half_transform.1 = (f32[512,1024]{1,0:T(8,128)S(1)}, bf16[2,640,1024]{2,1,0:T(8,128)(2,1)S(1)}) custom-call(s32[16,8,128]{2,1,0:T(8,128)S(1)} %all_to_all.5.code_ref, s32[1,256]{1,0:T(1,128)} %bitcast.88, bf16[4,16,256]{2,1,0:T(8,128)(2,1)S(1)} %get-tuple-element.419.refs_0_, bf16[4,16,256]{2,1,0:T(8,128)(2,1)S(1)} %collective-permute-done.10.refs_1_, ...), custom_call_target="tpu_custom_call" | custom-call | flops 7000000000 | bytes 1 | tf_op jit(solution)/shard_map/half_transform/pallas_call | solution.py:432
  70.1 1.1 %collective-permute-start.15 = (bf16[128,1280]{1,0:T(8,128)(2,1)S(1)}, bf16[128,1280]{1,0:T(8,128)(2,1)S(1)}, u32[]{:S(2)}, u32[]{:S(2)}) collective-permute-start(bf16[128,1280]{1,0:T(8,128)(2,1)S(1)} %collective-permute-done.13.refs_6_), channel_id=1, source_target_pairs={{0,2},{1,3},{2,0},{3,1},{4,6},{5,7},{6,4},{7,5},{8,10},{9,11},{10,... | collective-permute-start | bytes 983048 | tf_op jit(solution)/shard_map/ppermute | solution.py:382
  71.2 0.5 collective-permute-start.19
  71.7 8.1 %collective-permute-done.15.refs_7_ = bf16[128,1280]{1,0:T(8,128)(2,1)S(1)} collective-permute-done((bf16[128,1280]{1,0:T(8,128)(2,1)S(1)}, bf16[128,1280]{1,0:T(8,128)(2,1)S(1)}, u32[]{:S(2)}, u32[]{:S(2)}) %collective-permute-start.15) | collective-permute-done | bytes 327712 | tf_op jit(solution)/shard_map/ppermute | solution.py:382
  79.8 1.6 %collective-permute-done.20.refs_15_ = bf16[128,1280]{1,0:T(8,128)(2,1)S(1)} collective-permute-done((bf16[128,1280]{1,0:T(8,128)(2,1)S(1)}, bf16[128,1280]{1,0:T(8,128)(2,1)S(1)}, u32[]{:S(2)}, u32[]{:S(2)}) %collective-permute-start.20) | collective-permute-done | bytes 327712 | tf_op jit(solution)/shard_map/ppermute | solution.py:382
  81.4 7.4 %last_product.1 = bf16[2,256,2304]{2,1,0:T(8,128)(2,1)} custom-call(s32[1]{0:T(128)} %get-tuple-element.418.me_ref, f32[512,1024]{1,0:T(8,128)S(1)} %get-tuple-element.277.part_any, bf16[2,640,1024]{2,1,0:T(8,128)(2,1)S(1)} %get-tuple-element.278.late_any, bf16[128,1280]{1,0:T(8,128)(2,1)S(1)} %get-tuple-element.256.refs_4_.refs_0_, ...), custom_call_target="tpu_custom_call" | custom-call | flops 20000000000 | bytes 1 | tf_op jit(solution)/shard_map/last_product/pallas_call | solution.py:463
  88.8 0.6 while.17
  (23 shorter events, 0.1 us)
Async XLA Ops:
  6.5 0.9 copy-start.1
  9.0 17.5 %collective-permute-start = (bf16[96,1280]{1,0:T(8,128)(2,1)S(1)}, bf16[96,1280]{1,0:T(8,128)(2,1)S(1)}, u32[]{:S(2)}, u32[]{:S(2)}) collective-permute-start(bf16[96,1280]{1,0:T(8,128)(2,1)S(1)} %get-tuple-element.250), channel_id=1, source_target_pairs={{0,1},{1,0},{2,3},{3,2},{4,5},{5,4},{6,7},{7,6},{8,9},{9,8},{10,11... | collective-permute-start | bytes 737288 | tf_op jit(solution)/shard_map/ppermute | solution.py:382
  9.5 17.0 %collective-permute-start.1 = (bf16[96,1280]{1,0:T(8,128)(2,1)S(1)}, bf16[96,1280]{1,0:T(8,128)(2,1)S(1)}, u32[]{:S(2)}, u32[]{:S(2)}) collective-permute-start(bf16[96,1280]{1,0:T(8,128)(2,1)S(1)} %get-tuple-element.251), channel_id=1, source_target_pairs={{0,2},{1,3},{2,0},{3,1},{4,6},{5,7},{6,4},{7,5},{8,10},{9,11},{10,... | collective-permute-start | bytes 737288 | tf_op jit(solution)/shard_map/ppermute | solution.py:382
  12.1 14.4 %collective-permute-start.2 = (bf16[96,1280]{1,0:T(8,128)(2,1)S(1)}, bf16[96,1280]{1,0:T(8,128)(2,1)S(1)}, u32[]{:S(2)}, u32[]{:S(2)}) collective-permute-start(bf16[96,1280]{1,0:T(8,128)(2,1)S(1)} %get-tuple-element.252), channel_id=1, source_target_pairs={{0,3},{1,2},{2,1},{3,0},{4,7},{5,6},{6,5},{7,4},{8,11},{9,10},{10,... | collective-permute-start | bytes 737288 | tf_op jit(solution)/shard_map/ppermute | solution.py:382
  12.9 0.7 copy-start
  28.7 9.2 %collective-permute-start.5 = (bf16[128,1280]{1,0:T(8,128)(2,1)S(1)}, bf16[128,1280]{1,0:T(8,128)(2,1)S(1)}, u32[]{:S(2)}, u32[]{:S(2)}) collective-permute-start(bf16[128,1280]{1,0:T(8,128)(2,1)S(1)} %get-tuple-element.256.refs_4_.refs_0_), channel_id=1, source_target_pairs={{0,4},{1,5},{2,6},{3,7},{4,0},{5,1},{6,2},{7,3},{8,12},{9,13},{10,... | collective-permute-start | bytes 983048 | tf_op jit(solution)/shard_map/ppermute | solution.py:382
  28.9 9.5 %collective-permute-start.6 = (bf16[128,1280]{1,0:T(8,128)(2,1)S(1)}, bf16[128,1280]{1,0:T(8,128)(2,1)S(1)}, u32[]{:S(2)}, u32[]{:S(2)}) collective-permute-start(bf16[128,1280]{1,0:T(8,128)(2,1)S(1)} %get-tuple-element.256.refs_4_.refs_0_), channel_id=1, source_target_pairs={{0,2},{1,3},{2,0},{3,1},{4,6},{5,7},{6,4},{7,5},{8,10},{9,11},{10,... | collective-permute-start | bytes 983048 | tf_op jit(solution)/shard_map/ppermute | solution.py:382
  30.2 8.6 %collective-permute-start.3 = (bf16[128,1280]{1,0:T(8,128)(2,1)S(1)}, bf16[128,1280]{1,0:T(8,128)(2,1)S(1)}, u32[]{:S(2)}, u32[]{:S(2)}) collective-permute-start(bf16[128,1280]{1,0:T(8,128)(2,1)S(1)} %get-tuple-element.256.refs_4_.refs_0_), channel_id=1, source_target_pairs={{0,1},{1,0},{2,3},{3,2},{4,5},{5,4},{6,7},{7,6},{8,9},{9,8},{10,11... | collective-permute-start | bytes 983048 | tf_op jit(solution)/shard_map/ppermute | solution.py:382
  38.3 4.1 %collective-permute-start.8 = (bf16[128,1280]{1,0:T(8,128)(2,1)S(1)}, bf16[128,1280]{1,0:T(8,128)(2,1)S(1)}, u32[]{:S(2)}, u32[]{:S(2)}) collective-permute-start(bf16[128,1280]{1,0:T(8,128)(2,1)S(1)} %collective-permute-done.6.refs_5_.refs_1_), channel_id=1, source_target_pairs={{0,1},{1,0},{2,3},{3,2},{4,5},{5,4},{6,7},{7,6},{8,9},{9,8},{10,11... | collective-permute-start | bytes 983048 | tf_op jit(solution)/shard_map/ppermute | solution.py:382
  38.4 4.1 %collective-permute-start.9 = (bf16[128,1280]{1,0:T(8,128)(2,1)S(1)}, bf16[128,1280]{1,0:T(8,128)(2,1)S(1)}, u32[]{:S(2)}, u32[]{:S(2)}) collective-permute-start(bf16[128,1280]{1,0:T(8,128)(2,1)S(1)} %collective-permute-done.5.refs_6_.refs_2_), channel_id=1, source_target_pairs={{0,1},{1,0},{2,3},{3,2},{4,5},{5,4},{6,7},{7,6},{8,9},{9,8},{10,11... | collective-permute-start | bytes 983048 | tf_op jit(solution)/shard_map/ppermute | solution.py:382
  38.9 19.6 %collective-permute-start.4 = (bf16[128,1280]{1,0:T(8,128)(2,1)S(1)}, bf16[128,1280]{1,0:T(8,128)(2,1)S(1)}, u32[]{:S(2)}, u32[]{:S(2)}) collective-permute-start(bf16[128,1280]{1,0:T(8,128)(2,1)S(1)} %get-tuple-element.256.refs_4_.refs_0_), channel_id=1, source_target_pairs={{0,8},{1,9},{2,10},{3,11},{4,12},{5,13},{6,14},{7,15},{8,0},{9,1},... | collective-permute-start | bytes 983048 | tf_op jit(solution)/shard_map/ppermute | solution.py:382
  41.2 17.3 %collective-permute-start.7 = (bf16[128,1280]{1,0:T(8,128)(2,1)S(1)}, bf16[128,1280]{1,0:T(8,128)(2,1)S(1)}, u32[]{:S(2)}, u32[]{:S(2)}) collective-permute-start(bf16[128,1280]{1,0:T(8,128)(2,1)S(1)} %collective-permute-done.5.refs_6_.refs_2_), channel_id=1, source_target_pairs={{0,2},{1,3},{2,0},{3,1},{4,6},{5,7},{6,4},{7,5},{8,10},{9,11},{10,... | collective-permute-start | bytes 983048 | tf_op jit(solution)/shard_map/ppermute | solution.py:382
  42.4 16.1 %collective-permute-start.10 = (bf16[4,16,256]{2,1,0:T(8,128)(2,1)S(1)}, bf16[4,16,256]{2,1,0:T(8,128)(2,1)S(1)}, u32[]{:S(2)}, u32[]{:S(2)}) collective-permute-start(bf16[4,16,256]{2,1,0:T(8,128)(2,1)S(1)} %get-tuple-element.264), channel_id=1, source_target_pairs={{0,4},{1,5},{2,6},{3,7},{4,0},{5,1},{6,2},{7,3},{8,12},{9,13},{10,... | collective-permute-start | bytes 98312 | tf_op jit(solution)/shard_map/ppermute | solution.py:382
  42.9 16.0 %collective-permute-start.11 = (bf16[4,16,256]{2,1,0:T(8,128)(2,1)S(1)}, bf16[4,16,256]{2,1,0:T(8,128)(2,1)S(1)}, u32[]{:S(2)}, u32[]{:S(2)}) collective-permute-start(bf16[4,16,256]{2,1,0:T(8,128)(2,1)S(1)} %get-tuple-element.265), channel_id=1, source_target_pairs={{0,8},{1,9},{2,10},{3,11},{4,12},{5,13},{6,14},{7,15},{8,0},{9,1},... | collective-permute-start | bytes 98312 | tf_op jit(solution)/shard_map/ppermute | solution.py:382
  43.8 15.0 %collective-permute-start.12 = (bf16[4,16,256]{2,1,0:T(8,128)(2,1)S(1)}, bf16[4,16,256]{2,1,0:T(8,128)(2,1)S(1)}, u32[]{:S(2)}, u32[]{:S(2)}) collective-permute-start(bf16[4,16,256]{2,1,0:T(8,128)(2,1)S(1)} %get-tuple-element.266), channel_id=1, source_target_pairs={{0,12},{1,13},{2,14},{3,15},{4,8},{5,9},{6,10},{7,11},{8,4},{9,5},... | collective-permute-start | bytes 98312 | tf_op jit(solution)/shard_map/ppermute | solution.py:382
  58.9 11.2 %collective-permute-start.13 = (bf16[128,1280]{1,0:T(8,128)(2,1)S(1)}, bf16[128,1280]{1,0:T(8,128)(2,1)S(1)}, u32[]{:S(2)}, u32[]{:S(2)}) collective-permute-start(bf16[128,1280]{1,0:T(8,128)(2,1)S(1)} %collective-permute-done.4.refs_3_), channel_id=1, source_target_pairs={{0,4},{1,5},{2,6},{3,7},{4,0},{5,1},{6,2},{7,3},{8,12},{9,13},{10,... | collective-permute-start | bytes 983048 | tf_op jit(solution)/shard_map/ppermute | solution.py:382
  59.8 11.4 %collective-permute-start.14 = (bf16[128,1280]{1,0:T(8,128)(2,1)S(1)}, bf16[128,1280]{1,0:T(8,128)(2,1)S(1)}, u32[]{:S(2)}, u32[]{:S(2)}) collective-permute-start(bf16[128,1280]{1,0:T(8,128)(2,1)S(1)} %collective-permute-done.4.refs_3_), channel_id=1, source_target_pairs={{0,2},{1,3},{2,0},{3,1},{4,6},{5,7},{6,4},{7,5},{8,10},{9,11},{10,... | collective-permute-start | bytes 983048 | tf_op jit(solution)/shard_map/ppermute | solution.py:382
  60.8 10.9 %collective-permute-start.16 = (bf16[128,1280]{1,0:T(8,128)(2,1)S(1)}, bf16[128,1280]{1,0:T(8,128)(2,1)S(1)}, u32[]{:S(2)}, u32[]{:S(2)}) collective-permute-start(bf16[128,1280]{1,0:T(8,128)(2,1)S(1)} %collective-permute-done.4.refs_3_), channel_id=1, source_target_pairs={{0,1},{1,0},{2,3},{3,2},{4,5},{5,4},{6,7},{7,6},{8,9},{9,8},{10,11... | collective-permute-start | bytes 983048 | tf_op jit(solution)/shard_map/ppermute | solution.py:382
  60.8 10.9 %collective-permute-start.17 = (bf16[128,1280]{1,0:T(8,128)(2,1)S(1)}, bf16[128,1280]{1,0:T(8,128)(2,1)S(1)}, u32[]{:S(2)}, u32[]{:S(2)}) collective-permute-start(bf16[128,1280]{1,0:T(8,128)(2,1)S(1)} %collective-permute-done.7.refs_4_), channel_id=1, source_target_pairs={{0,1},{1,0},{2,3},{3,2},{4,5},{5,4},{6,7},{7,6},{8,9},{9,8},{10,11... | collective-permute-start | bytes 983048 | tf_op jit(solution)/shard_map/ppermute | solution.py:382
  70.1 9.7 %collective-permute-start.15 = (bf16[128,1280]{1,0:T(8,128)(2,1)S(1)}, bf16[128,1280]{1,0:T(8,128)(2,1)S(1)}, u32[]{:S(2)}, u32[]{:S(2)}) collective-permute-start(bf16[128,1280]{1,0:T(8,128)(2,1)S(1)} %collective-permute-done.13.refs_6_), channel_id=1, source_target_pairs={{0,2},{1,3},{2,0},{3,1},{4,6},{5,7},{6,4},{7,5},{8,10},{9,11},{10,... | collective-permute-start | bytes 983048 | tf_op jit(solution)/shard_map/ppermute | solution.py:382
  71.2 8.6 %collective-permute-start.18 = (bf16[128,1280]{1,0:T(8,128)(2,1)S(1)}, bf16[128,1280]{1,0:T(8,128)(2,1)S(1)}, u32[]{:S(2)}, u32[]{:S(2)}) collective-permute-start(bf16[128,1280]{1,0:T(8,128)(2,1)S(1)} %collective-permute-done.14.refs_5_), channel_id=1, source_target_pairs={{0,1},{1,0},{2,3},{3,2},{4,5},{5,4},{6,7},{7,6},{8,9},{9,8},{10,11... | collective-permute-start | bytes 983048 | tf_op jit(solution)/shard_map/ppermute | solution.py:382
  71.2 8.6 %collective-permute-start.19 = (bf16[128,1280]{1,0:T(8,128)(2,1)S(1)}, bf16[128,1280]{1,0:T(8,128)(2,1)S(1)}, u32[]{:S(2)}, u32[]{:S(2)}) collective-permute-start(bf16[128,1280]{1,0:T(8,128)(2,1)S(1)} %collective-permute-done.13.refs_6_), channel_id=1, source_target_pairs={{0,1},{1,0},{2,3},{3,2},{4,5},{5,4},{6,7},{7,6},{8,9},{9,8},{10,11... | collective-permute-start | bytes 983048 | tf_op jit(solution)/shard_map/ppermute | solution.py:382
  79.8 1.6 %collective-permute-start.20 = (bf16[128,1280]{1,0:T(8,128)(2,1)S(1)}, bf16[128,1280]{1,0:T(8,128)(2,1)S(1)}, u32[]{:S(2)}, u32[]{:S(2)}) collective-permute-start(bf16[128,1280]{1,0:T(8,128)(2,1)S(1)} %collective-permute-done.15.refs_7_), channel_id=1, source_target_pairs={{0,1},{1,0},{2,3},{3,2},{4,5},{5,4},{6,7},{7,6},{8,9},{9,8},{10,11... | collective-permute-start | bytes 983048 | tf_op jit(solution)/shard_map/ppermute | solution.py:382
  81.4 7.4 %copy-start.3 = (s32[256]{0:T(256)S(1)}, s32[256]{0:T(256)}, u32[]{:S(2)}) copy-start(s32[256]{0:T(256)} %param.11) | copy-start | bytes 3076

commit v16 on v14

--- a/solution.py
+++ b/solution.py
@@ -12,8 +12,9 @@
 NOCC = 256
 BLK_DEV = 8
 LIVE_DEV = 4
-CAP = 128
+CAP = 96
 Z, Y, CORES = 4, 2, 2
+CHIPS = Z * Y
 F32 = jnp.float32
 BF16 = jnp.bfloat16
 
@@ -95,16 +96,20 @@
     return jnp.concatenate([zero_one(ids == lanes + 128.0 * k) for k in range(shells // 128)], axis=1)
 
 
-def slot_hots(got, shells):
-    sources, slots = got.shape[0], got.shape[0] * BLK_DEV
-    rows = got[:, 2 * BLK_DEV :, :].reshape(sources, got.shape[2]).astype(BF16)
+def slot_hots(rows, shells):
+    sources, slots = rows.shape[0], rows.shape[0] * BLK_DEV
     owner = zero_one(iota((slots, sources), 0) // BLK_DEV == iota((slots, sources), 1)).astype(BF16)
-    ids = jnp.dot(owner, rows, preferred_element_type=F32)
+    ids = jnp.dot(owner, rows.astype(BF16), preferred_element_type=F32)
     slot, lane = iota(ids.shape, 0) % BLK_DEV, iota(ids.shape, 1)
     columns, rows = (
         jnp.broadcast_to(column_of(ids, lane == slot + first), (slots, 128)) for first in (0, BLK_DEV)
     )
     return one_hots(columns, shells), one_hots(rows, shells)
+
+
+def chunk(tail, i):
+    row, lane = 4 + i // 5, (i % 5) * 256
+    return tail[:, row : row + 1, lane : lane + 256]
 
 
 class Shells:
@@ -114,96 +119,76 @@
         self.before, self.same = lane < sub, lane == sub
         self.starts = column_of(size_row, self.before)
         self.size = column_of(size_row, self.same)
-        self.odd = self.starts - 2.0 * jnp.floor(self.starts * 0.5)
-
-
-class Used:
-    def __init__(self, shells, hot, window):
-        self.used = column_of(jnp.max(hot, axis=0, keepdims=True), shells.same)
-        self.extra, self.ahead, self.edges = [], [], []
-        edge = (iota((hot.shape[1], 128), 1) * window).astype(F32)
-        reach = jnp.clip(edge - shells.starts, 0.0, shells.size)
-        for parity in range(2):
-            extra = 1.0 - shells.odd if parity == 0 else shells.odd
-            count = self.used * jnp.floor((shells.size + extra) * 0.5)
-            count_row = row_of(count, shells.same)
-            self.extra.append(extra)
-            self.ahead.append(column_of(count_row, shells.before))
-            self.edges.append(jnp.sum(self.used * jnp.floor((reach + extra) * 0.5), axis=0, keepdims=True))
-
-
-def pack_kernel(vir_ref, occ_ref, *outs):
-    me = lax.axis_index("shell")
-    core, y = lax.rem(me, 2), lax.rem(lax.div(me, 2), 2)
+
+    def members(self, chip):
+        ahead = chip - self.starts
+        ahead = ahead - CHIPS * jnp.floor(ahead / CHIPS)
+        return jnp.floor((self.size + (CHIPS - 1.0) - ahead) / CHIPS)
+
+
+def used_shells(shells, hot):
+    return column_of(jnp.max(hot, axis=0, keepdims=True), shells.same)
+
+
+def pack_kernel(pairs_ref, count_ref, panels_ref, vir_ref, occ_ref, out_ref):
+    n, rows, packed = out_ref.shape
     here, nvir = vir_ref.shape
     width, thin = nvir // CORES, occ_ref.shape[1] // CORES
-    for dy in range(2):
-        parity = lax.rem(y + dy, 2)
-        pick = zero_one(iota((here // 2, here), 1) == 2 * iota((here // 2, here), 0) + parity).astype(BF16)
-        for dc in range(2):
-            half = lax.rem(core + dc, 2)
-            out = outs[2 * dy + dc]
-            part = vir_ref[:, pl.ds(pl.multiple_of(half * width, 128), width)]
-            out[:, :width] = jnp.dot(pick, part, preferred_element_type=F32).astype(BF16)
-            part = occ_ref[:, pl.ds(pl.multiple_of(half * thin, 128), thin)]
-            out[:, width:] = jnp.dot(pick, part, preferred_element_type=F32).astype(BF16)
-
-
-def send_kernel(pairs_ref, count_ref, panels_ref, send_ref):
-    n = send_ref.shape[0]
-    turned = jnp.swapaxes(panels_ref[...].astype(F32), 0, 1)
-    send_ref[:, : 2 * BLK_DEV, :] = turned.reshape(n, 2 * BLK_DEV, EDGE * EDGE).astype(BF16)
+    row, column = iota((CHIPS * rows, here), 0), iota((CHIPS * rows, here), 1)
+    deal = zero_one((row % rows < here // CHIPS) & (column == CHIPS * (row % rows) + row // rows)).astype(BF16)
+    for core in range(CORES):
+        part = jnp.dot(deal, vir_ref[:, core * width : (core + 1) * width], preferred_element_type=F32)
+        thin_part = jnp.dot(deal, occ_ref[:, core * thin : (core + 1) * thin], preferred_element_type=F32)
+        for chip in range(CHIPS):
+            at = slice(chip * rows, (chip + 1) * rows)
+            out_ref[CORES * chip + core, :, :width] = part[at].astype(BF16)
+            out_ref[CORES * chip + core, :, width:] = thin_part[at].astype(BF16)
+    turned = jnp.swapaxes(panels_ref[...].astype(F32), 0, 1).reshape(n, 2 * BLK_DEV, EDGE * EDGE)
     kept = iota((1, BLK_DEV), 1) < count_ref[...]
     square, wide = (BLK_DEV, BLK_DEV), (BLK_DEV, EDGE * EDGE)
     same = iota(square, 0) == iota(square, 1)
-    row = jnp.zeros((1, EDGE * EDGE), F32)
+    ids_row = jnp.zeros((1, EDGE * EDGE), F32)
     for first, k in ((0, 1), (BLK_DEV, 0)):
         ids = column_of(jnp.where(kept, pairs_ref[k : k + 1, :], -1).astype(F32), same)
-        row += row_of(ids, iota(wide, 1) == iota(wide, 0) + first)
-    send_ref[:, 2 * BLK_DEV :, :] = jnp.broadcast_to(row[None], (n, 1, EDGE * EDGE)).astype(BF16)
-
-
-def pick_kernel(here, got_ref, size_ref, *refs):
-    sources, (out_ref, over_ref, me_ref) = refs[:4], refs[4:]
+        ids_row += row_of(ids, iota(wide, 1) == iota(wide, 0) + first)
+    chunks = [turned[:, i : i + 1, :] for i in range(2 * BLK_DEV)]
+    chunks.append(jnp.broadcast_to(ids_row[None], (n, 1, EDGE * EDGE)))
+    chunks += [jnp.zeros((n, 1, EDGE * EDGE), F32)] * 3
+    tail = [jnp.concatenate(chunks[5 * k : 5 * k + 5], axis=2) for k in range(4)]
+    out_ref[:, rows - 4 :, :] = jnp.concatenate(tail, axis=1).astype(BF16)
+
+
+def pick_kernel(here, got_ref, size_ref, out_ref, over_ref, me_ref):
     me = lax.axis_index("shell")
     me_ref[0] = me
-    core, y, z = lax.rem(me, 2), lax.rem(lax.div(me, 2), 2), lax.div(me, 4)
-    window = CORES * Y * here
+    chip = lax.div(me, CORES).astype(F32)
     shell_count = size_ref.shape[1]
+    n, rows, packed = got_ref.shape
+    tail = got_ref[:, rows - 8 :, :].astype(F32)
+    hots = slot_hots(chunk(tail, 2 * BLK_DEV).reshape(n, EDGE * EDGE), shell_count)
     shells = Shells(size_ref[...].astype(F32))
-    lists = [Used(shells, hot, window) for hot in slot_hots(got_ref[...].astype(F32), shell_count)]
+    lists = [used_shells(shells, hot) for hot in hots]
     most = jnp.zeros((1, 1), F32)
-    lane = iota((1, 128), 1)
-    for chosen in lists:
-        for edges in chosen.edges:
-            later = jnp.concatenate([edges[:, 1:], edges[:, :1]], axis=1)
-            most = jnp.maximum(most, jnp.max(jnp.where(lane < Z, later - edges, 0.0), axis=1, keepdims=True))
+    for other in range(CHIPS):
+        members = shells.members(float(other))
+        for used in lists:
+            most = jnp.maximum(most, jnp.sum(used * members, axis=0, keepdims=True))
     over_ref[0] = jnp.where(jnp.max(most) > CAP, 1, 0).astype(jnp.int32)
 
-    width = out_ref.shape[1] - 128
-    even = y == 0
-    totals = [jnp.zeros((CAP, width), F32), jnp.zeros((CAP, 128), F32)]
-    columns = [slice(0, width), slice(width, width + 128)]
-    extra = jnp.where(even, lists[0].extra[0], lists[0].extra[1])
-    rows = here // 2
-    for k, source in enumerate(sources):
-        device = 4 * z + 2 * lax.rem(y + k // 2, 2) + lax.rem(core + k % 2, 2)
-        row = (2 * iota((shell_count, 128), 1) + device * here + y).astype(F32)
-        where = row - shells.starts
-        inside = (where >= 0.0) & (where < shells.size)
-        within = jnp.floor((where + extra) * 0.5)
-        for chosen, total, column in zip(lists, range(2), columns):
-            ahead = jnp.where(even, chosen.ahead[0], chosen.ahead[1])
-            base = lane_value(jnp.where(even, chosen.edges[0], chosen.edges[1]), z)
-            place = jnp.where(inside & (chosen.used > 0.0), ahead + within + 1.0, 0.0)
-            place = jnp.sum(place, axis=0, keepdims=True)
-            place = jnp.where(place > 0.0, place - 1.0 - base, -1.0)
-            hot = zero_one(place == iota((CAP, 128), 0).astype(F32)).astype(BF16)
-            totals[total] += jnp.dot(
-                hot[:, :rows], source[:, column], preferred_element_type=F32
-            )
-    for total, column in zip(totals, columns):
-        out_ref[:, column] = total.astype(BF16)
+    lane = iota((shell_count, n * rows), 1)
+    row = (lane // rows * here + CHIPS * (lane % rows)).astype(F32) + chip
+    where = row - shells.starts
+    inside = (where >= 0.0) & (where < shells.size) & (lane % rows < here // CHIPS)
+    within = jnp.floor(where / CHIPS) + 1.0
+    members = shells.members(chip)
+    width = packed - 128
+    blocks = got_ref[...].reshape(n * rows, packed)
+    for used, column in zip(lists, (slice(0, width), slice(width, packed))):
+        ahead = column_of(row_of(used * members, shells.same), shells.before)
+        place = jnp.where(inside & (used > 0.0), ahead + within, 0.0)
+        place = jnp.sum(place, axis=0, keepdims=True) - 1.0
+        hot = zero_one(place == iota((CAP, n * rows), 0).astype(F32)).astype(BF16)
+        out_ref[:, column] = jnp.dot(hot, blocks[:, column], preferred_element_type=F32).astype(BF16)
 
 
 def slot_of(window, chip):
@@ -226,16 +211,23 @@
             copies.append(pltpu.make_async_copy(pieces[at].at[:, pl.ds(width, 128)], target, sems.at[at]))
     for copy in copies:
         copy.start()
-    window = CORES * Y * here
     shell_count = size_ref.shape[1]
-    got = got_ref[...].astype(F32)
-    size_row = size_ref[...].astype(F32)
-    shells = Shells(size_row)
-    got = got_ref[...].astype(F32)
-    panels_ref[...] = got[:, : 2 * BLK_DEV, :].astype(BF16)
-    ids_ref[...] = got[:, 2 * BLK_DEV :, :].reshape(ids_ref.shape)
-    hots = slot_hots(got, shell_count)
-    lists = [Used(shells, hot, window) for hot in hots]
+    n, rows, _ = got_ref.shape
+    tail = got_ref[:, rows - 8 :, :].astype(F32)
+    blocks = [jnp.concatenate([chunk(tail, p * BLK_DEV + k) for k in range(BLK_DEV)], axis=1) for p in range(2)]
+    panels_ref[...] = jnp.concatenate(blocks, axis=1).astype(BF16)
+    ids_ref[...] = chunk(tail, 2 * BLK_DEV).reshape(ids_ref.shape)
+    shells = Shells(size_ref[...].astype(F32))
+    hots = slot_hots(chunk(tail, 2 * BLK_DEV).reshape(n, EDGE * EDGE), shell_count)
+    sub, lane = iota((shell_count, 128), 0), iota((shell_count, 128), 1)
+    members = shells.members(lane.astype(F32))
+    earlier = zero_one(shells.before).astype(BF16)
+    lists = [
+        jnp.dot(earlier, (used_shells(shells, hot) * members).astype(BF16), preferred_element_type=F32) for hot in hots
+    ]
+    first_place = jnp.zeros((1, 128), F32)
+    for other in range(CHIPS):
+        first_place += jnp.where(iota((1, 128), 1) == other, (slot_of(other, chip) * CAP).astype(F32), 0.0)
     slots = hots[0].shape[0]
     kept = LIVE_DEV * (slots // BLK_DEV)
     alive = jnp.broadcast_to(jnp.sum(hots[0], axis=1, keepdims=True), (slots, slots))
@@ -248,29 +240,24 @@
     def taken(array):
         return jnp.dot(take, array.astype(BF16), preferred_element_type=F32)
 
-    def spread(hot, column):
+    def spread(wide):
+        wide = wide.reshape(kept, 1, 128)
+        return jnp.broadcast_to(wide, (kept, EDGE, 128)).reshape(kept * EDGE, 128)
+
+    def of_slot(hot, column):
         value = jnp.sum(hot * row_of(column, shells.same), axis=1, keepdims=True)
-        wide = jnp.broadcast_to(value, (kept, 128)).reshape(kept, 1, 128)
-        return jnp.broadcast_to(wide, (kept, EDGE, 128)).reshape(kept * EDGE, 128)
-
-    at = iota((kept * EDGE, 128), 0) % EDGE
-    step = at.astype(F32)
-
-    def places(hot, chosen):
+        return spread(jnp.broadcast_to(value, (kept, 128)))
+
+    step = (iota((kept * EDGE, 128), 0) % EDGE).astype(F32)
+    lane = iota((kept * EDGE, 128), 1).astype(F32)
+
+    def places(hot, ahead):
         hot = taken(hot)
-        first, length = spread(hot, shells.starts), spread(hot, shells.size)
-        row = first + step
-        odd = (row - 2.0 * jnp.floor(row * 0.5)) > 0.0
-        place = jnp.where(odd, spread(hot, chosen.ahead[1]), spread(hot, chosen.ahead[0]))
-        place += jnp.floor(step * 0.5)
-        offsets = [
-            [slot_of(w * Y + k, chip).astype(F32) * CAP - lane_value(e, w) for w in range(Z)]
-            for k, e in enumerate(chosen.edges)
-        ]
-        offset = jnp.where(odd, offsets[1][0], offsets[0][0])
-        for w in range(1, Z):
-            offset = jnp.where(row >= float(window * w), jnp.where(odd, offsets[1][w], offsets[0][w]), offset)
-        return jnp.where(step < length, place + offset, -1.0)[:, :1]
+        row = of_slot(hot, shells.starts) + step
+        table = jnp.dot(hot.astype(BF16), ahead.astype(BF16), preferred_element_type=F32) + first_place
+        mine = lane == row - CHIPS * jnp.floor(row / CHIPS)
+        place = jnp.sum(jnp.where(mine, spread(table), 0.0), axis=1, keepdims=True) + jnp.floor(step / CHIPS)[:, :1]
+        return jnp.where((step < of_slot(hot, shells.size))[:, :1], place, -1.0)
 
     place_c, place_r = places(hots[0], lists[0]), places(hots[1], lists[1])
     span = 16 * EDGE
@@ -278,7 +265,7 @@
     keep_m = (l_in // EDGE) == (s_in % EDGE)
     fold = zero_one((s_in % EDGE) == (l_in % EDGE)).astype(BF16)
     same_slot = (s_in // EDGE) == (l_in // EDGE)
-    blocks = [taken(got[:, p * BLK_DEV : (p + 1) * BLK_DEV, :].reshape(slots, span)) for p in range(2)]
+    blocks = [taken(block.reshape(slots, span)) for block in blocks]
     lanes = iota((span, half_ref.shape[1]), 1).astype(F32)
     for copy in copies:
         copy.wait()
@@ -372,49 +359,41 @@
     here, nvir = vir_coef.shape
     width = nvir // CORES
     packed = width + NOCC // CORES
-    room = Z * Y * CAP
+    room = CHIPS * CAP
     size_row = shell_size.reshape(1, -1)
 
     def swap(array, bit):
         return lax.ppermute(array, "shell", [(i, i ^ bit) for i in range(n)])
 
-    keep, to_core, to_y, to_both = pl.pallas_call(
+    rows = here // CHIPS + 4
+    blocks = pl.pallas_call(
         pack_kernel,
-        out_shape=[shape(here // 2, packed)] * 4,
-        in_specs=[VMEM] * 2,
-        out_specs=[VMEM] * 4,
-        compiler_params=params(12),
-        cost_estimate=cost(3e8, 3e6),
+        out_shape=shape(n, rows, packed),
+        in_specs=[VMEM] * 5,
+        out_specs=VMEM,
+        compiler_params=params(16),
+        cost_estimate=cost(3e9, 1),
         name="pack_rows",
-    )(vir_coef, occ_coef)
-    to_y, to_both, to_core = swap(to_y, 2), swap(to_both, 3), swap(to_core, 1)
-    send = pl.pallas_call(
-        send_kernel,
-        out_shape=shape(n, 2 * BLK_DEV + 1, EDGE * EDGE),
-        in_specs=[VMEM] * 3,
-        out_specs=VMEM,
-        compiler_params=params(12),
-        cost_estimate=cost(1e6, 5e5),
-        name="pack_panels",
-    )(block_pairs.T, block_count.reshape(1, 1), panels)
-    got = lax.all_to_all(send, "shell", split_axis=0, concat_axis=0, tiled=True)
+    )(block_pairs.T, block_count.reshape(1, 1), panels, vir_coef, occ_coef)
+    got = lax.all_to_all(blocks, "shell", split_axis=0, concat_axis=0, tiled=True)
 
     mine, over, me = pl.pallas_call(
         functools.partial(pick_kernel, here),
         out_shape=(shape(CAP, packed), shape(1, dtype=jnp.int32), shape(1, dtype=jnp.int32)),
-        in_specs=[VMEM] * 6,
+        in_specs=[VMEM] * 2,
         out_specs=(VMEM, SMEM, SMEM),
-        compiler_params=params(12),
+        compiler_params=params(16),
         cost_estimate=cost(3e8, 2e6),
         name="pick_rows",
-    )(got, size_row, keep, to_core, to_y, to_both)
+    )(got, size_row)
 
     across, mine_y, beside = swap(mine, 8), swap(mine, 2), swap(mine, 4)
     far = [swap(mine, 1), swap(mine_y, 1), swap(beside, 1)]
     across, mine_y, beside, *far = lax.optimization_barrier((across, mine_y, beside, *far))
 
     corner, beside_y, across_y = swap(across, 4), swap(beside, 2), swap(across, 2)
-    near = [mine, mine_y, beside]
+    near = [mine, mine_y, beside, across]
+    far.append(swap(across, 1))
     early = len(near)
     slots = LIVE_DEV * n * EDGE
     half, late, got_panels, got_ids = pl.pallas_call(
@@ -446,7 +425,7 @@
     )(got, size_row, *near, *far)
     corner, half, late = lax.optimization_barrier((corner, half, late))
     corner_y = swap(corner, 2)
-    near += [across, beside_y, across_y, corner]
+    near += [beside_y, across_y, corner]
     far += [swap(piece, 1) for piece in near[early:]]
     corner_y, *far = lax.optimization_barrier((corner_y, *far))
     near.append(corner_y)
@@ -479,7 +458,7 @@
     n = lax.axis_size("shell")
     here, nvir = args[5].shape
     sparse = LIVE_DEV * n * EDGE < n * here
-    if not (sparse and n == Z * Y * CORES and here <= 256 and here % 16 == 0 and nvir % 768 == 0):
+    if not (sparse and n == Z * Y * CORES and here % (2 * CHIPS) == 0 and nvir % 768 == 0):
         return from_start(*args)
     out, over, got_panels, got_ids = short_way(*args)
 

time: 93.4 us -> 94.3 us (level)
  blocking collectives: 0 us -> 30.9 us
  waiting for transfers between devices: 37.9 us -> 23.2 us
  starting transfers between devices: 18.3 us -> 8.52 us
  Pallas kernels: 20.6 us -> 14.9 us
    all_to_all x0 -> x1, blocking collectives: none -> 30.9 us  [short_way(): lax.all_to_all(blocks, 'shell', split_axis=0, concat_axis=0, tiled=True)]
    ppermute x18 -> x15, waiting for transfers between devices: 37.9 us -> 23.2 us  [swap(): return lax.ppermute(array, 'shell', [(i, i ^ bit) for i in range(n)])]
    all_to_all x1 -> x0, starting transfers between devices: 7.39 us -> none  [short_way(): got = lax.all_to_all(send, 'shell', split_axis=0, concat_axis=0, tiled=True)]
    pallas_call x1, Pallas kernels: 8.67 us -> 5.62 us  [short_way(): pl.pallas_call(functools.partial(half_kernel, here, early), out_shape=(sh...]
    ppermute x18 -> x15, starting transfers between devices: 10.9 us -> 8.52 us  [swap(): return lax.ppermute(array, 'shell', [(i, i ^ bit) for i in range(n)])]
    pallas_call x1, Pallas kernels: 7.31 us -> 6.04 us  [short_way(): pl.pallas_call(functools.partial(last_kernel, count, early), out_shape=sh...]
    pallas_call x2 -> x1, Pallas kernels: 2.38 us -> 1.61 us  [short_way(): pl.pallas_call(pack_kernel, out_shape=shape(n, rows, packed), in_specs=[V...]
  transfers between devices with their start and end apart: 19 -> 15, of which waited for: 8 -> 7; matrix products, arithmetic and copies ran while one was open for 0% -> 0% of each run, Pallas kernels for 11% -> 6%
where the time goes in v16:
time: 94.3 us; the launch traced here: 94.1 us
  blocking collectives  30.9 us (33%)
  waiting for transfers between devices  23.2 us (25%)
  Pallas kernels  14.9 us (16%)
  between operations  14.1 us (15%)
  starting transfers between devices  8.52 us (9%)
  local copies, waits for them, and re-layouts  1.58 us (2%)
    all_to_all x1, blocking collectives, short_way(): lax.all_to_all(blocks, 'shell', split_axis=0, concat_axis=0, tiled=True)  30.9 us
    ppermute x15, waiting for transfers between devices, swap(): return lax.ppermute(array, 'shell', [(i, i ^ bit) for i in range(n)])  23.2 us
    ppermute x15, starting transfers between devices, swap(): return lax.ppermute(array, 'shell', [(i, i ^ bit) for i in range(n)])  8.52 us
    pallas_call x1, Pallas kernels, short_way(): pl.pallas_call(functools.partial(last_kernel, count, early), out_shape=sh...  6.04 us
    pallas_call x1, Pallas kernels, short_way(): pl.pallas_call(functools.partial(half_kernel, here, early), out_shape=(sh...  5.62 us
  transfers between devices with their start and end apart: 15, of which 7 were waited for; matrix products, arithmetic and copies ran while one was open for 0% of the time, Pallas kernels for 6%

profile of v16, /device:TPU:0, one launch (start us, length us, event | category | flops | bytes accessed | tf_op | source)
XLA Modules:
  0.0 94.1 jit_solution(6537360649249264888)
XLA Ops:
  7.2 0.9 copy-done
  8.1 0.7 copy-done.1
  8.8 1.6 %pack_rows.1 = bf16[16,24,1280]{2,1,0:T(8,128)(2,1)S(1)} custom-call(s32[2,8]{1,0:T(2,128)S(1)} %bitcast.60, s32[1,1]{1,0:T(1,128)} %bitcast.59.count_ref, bf16[8,32,256]{2,1,0:T(8,128)(2,1)S(1)} %copy-done, bf16[160,2304]{1,0:T(8,128)(2,1)} %vir_ref.1, bf16[160,256]{1,0:T(8,128)(2,1)} %occ_ref.1), custom_call_target="tpu_custom_call" | custom-call | flops 3000000000 | bytes 1 | tf_op jit(solution)/shard_map/pack_rows/pallas_call | solution.py:369
  10.4 30.9 %all_to_all.5.got_ref = bf16[16,24,1280]{2,1,0:T(8,128)(2,1)S(1)} all-to-all(bf16[16,24,1280]{2,1,0:T(8,128)(2,1)S(1)} %pack_rows.1), channel_id=1, replica_groups=mesh['groups'=2,'shell'=16] {'shell'}, dimensions={0} | all-to-all | bytes 1966080 | tf_op jit(solution)/shard_map/all_to_all | solution.py:378
  41.3 1.6 %pick_rows.1 = (bf16[96,1280]{1,0:T(8,128)(2,1)S(1)}, s32[1]{0:T(128)}, s32[1]{0:T(128)}) custom-call(bf16[16,24,1280]{2,1,0:T(8,128)(2,1)S(1)} %all_to_all.5.got_ref, s32[1,256]{1,0:T(1,128)S(1)} %bitcast.63), custom_call_target="tpu_custom_call" | custom-call | flops 300000000 | bytes 2000000 | tf_op jit(solution)/shard_map/pick_rows/pallas_call | solution.py:380
  42.9 1.2 %collective-permute-start.1 = (bf16[96,1280]{1,0:T(8,128)(2,1)S(1)}, bf16[96,1280]{1,0:T(8,128)(2,1)S(1)}, u32[]{:S(2)}, u32[]{:S(2)}) collective-permute-start(bf16[96,1280]{1,0:T(8,128)(2,1)S(1)} %get-tuple-element.140.refs_0_), channel_id=1, source_target_pairs={{0,2},{1,3},{2,0},{3,1},{4,6},{5,7},{6,4},{7,5},{8,10},{9,11},{10,... | collective-permute-start | bytes 737288 | tf_op jit(solution)/shard_map/ppermute | solution.py:366
  44.2 1.8 %collective-permute-start.2 = (bf16[96,1280]{1,0:T(8,128)(2,1)S(1)}, bf16[96,1280]{1,0:T(8,128)(2,1)S(1)}, u32[]{:S(2)}, u32[]{:S(2)}) collective-permute-start(bf16[96,1280]{1,0:T(8,128)(2,1)S(1)} %get-tuple-element.140.refs_0_), channel_id=1, source_target_pairs={{0,4},{1,5},{2,6},{3,7},{4,0},{5,1},{6,2},{7,3},{8,12},{9,13},{10,... | collective-permute-start | bytes 737288 | tf_op jit(solution)/shard_map/ppermute | solution.py:366
  46.0 1.5 %collective-permute-start = (bf16[96,1280]{1,0:T(8,128)(2,1)S(1)}, bf16[96,1280]{1,0:T(8,128)(2,1)S(1)}, u32[]{:S(2)}, u32[]{:S(2)}) collective-permute-start(bf16[96,1280]{1,0:T(8,128)(2,1)S(1)} %get-tuple-element.140.refs_0_), channel_id=1, source_target_pairs={{0,8},{1,9},{2,10},{3,11},{4,12},{5,13},{6,14},{7,15},{8,0},{9,1},... | collective-permute-start | bytes 737288 | tf_op jit(solution)/shard_map/ppermute | solution.py:366
  47.5 0.0 collective-permute-start.3
  47.5 4.2 %collective-permute-done.1.refs_1_ = bf16[96,1280]{1,0:T(8,128)(2,1)S(1)} collective-permute-done((bf16[96,1280]{1,0:T(8,128)(2,1)S(1)}, bf16[96,1280]{1,0:T(8,128)(2,1)S(1)}, u32[]{:S(2)}, u32[]{:S(2)}) %collective-permute-start.1) | collective-permute-done | bytes 245792 | tf_op jit(solution)/shard_map/ppermute | solution.py:366
  51.6 4.8 %collective-permute-done.2.refs_2_ = bf16[96,1280]{1,0:T(8,128)(2,1)S(1)} collective-permute-done((bf16[96,1280]{1,0:T(8,128)(2,1)S(1)}, bf16[96,1280]{1,0:T(8,128)(2,1)S(1)}, u32[]{:S(2)}, u32[]{:S(2)}) %collective-permute-start.2) | collective-permute-done | bytes 245792 | tf_op jit(solution)/shard_map/ppermute | solution.py:366
  56.4 3.3 %collective-permute-done.refs_3_ = bf16[96,1280]{1,0:T(8,128)(2,1)S(1)} collective-permute-done((bf16[96,1280]{1,0:T(8,128)(2,1)S(1)}, bf16[96,1280]{1,0:T(8,128)(2,1)S(1)}, u32[]{:S(2)}, u32[]{:S(2)}) %collective-permute-start) | collective-permute-done | bytes 245792 | tf_op jit(solution)/shard_map/ppermute | solution.py:366
  59.8 0.0 collective-permute-done.3.refs_4_.refs_8_
  59.8 0.0 collective-permute-done.4.refs_5_.refs_9_
  59.8 0.0 collective-permute-done.5.refs_6_.refs_10_
  59.8 0.1 collective-permute-start.7
  59.9 0.1 collective-permute-start.6
  59.9 1.2 %collective-permute-start.9 = (bf16[96,1280]{1,0:T(8,128)(2,1)S(1)}, bf16[96,1280]{1,0:T(8,128)(2,1)S(1)}, u32[]{:S(2)}, u32[]{:S(2)}) collective-permute-start(bf16[96,1280]{1,0:T(8,128)(2,1)S(1)} %collective-permute-done.refs_3_), channel_id=1, source_target_pairs={{0,2},{1,3},{2,0},{3,1},{4,6},{5,7},{6,4},{7,5},{8,10},{9,11},{10,... | collective-permute-start | bytes 737288 | tf_op jit(solution)/shard_map/ppermute | solution.py:366
  61.2 0.9 collective-permute-start.8
  62.0 5.6 %half_transform.1 = (f32[512,768]{1,0:T(8,128)S(1)}, bf16[2,384,768]{2,1,0:T(8,128)(2,1)S(1)}, bf16[16,16,256]{2,1,0:T(8,128)(2,1)S(1)}, f32[16,256]{1,0:T(8,128)S(1)}) custom-call(bf16[16,24,1280]{2,1,0:T(8,128)(2,1)S(1)} %all_to_all.5.got_ref, s32[1,256]{1,0:T(1,128)S(1)} %bitcast.64, bf16[96,1280]{1,0:T(8,128)(2,1)S(1)} %get-tuple-element.140.refs_0_, ...), custom_call_target="tpu_custom_call" | custom-call | flops 7000000000 | bytes 1 | tf_op jit(solution)/shard_map/half_transform/pallas_call | solution.py:399
  67.7 0.6 collective-permute-done.6.refs_6_
  68.2 1.2 %collective-permute-start.10 = (bf16[96,1280]{1,0:T(8,128)(2,1)S(1)}, bf16[96,1280]{1,0:T(8,128)(2,1)S(1)}, u32[]{:S(2)}, u32[]{:S(2)}) collective-permute-start(bf16[96,1280]{1,0:T(8,128)(2,1)S(1)} %collective-permute-done.6.refs_6_), channel_id=1, source_target_pairs={{0,2},{1,3},{2,0},{3,1},{4,6},{5,7},{6,4},{7,5},{8,10},{9,11},{10,... | collective-permute-start | bytes 737288 | tf_op jit(solution)/shard_map/ppermute | solution.py:366
  69.4 4.7 %collective-permute-done.8.refs_4_ = bf16[96,1280]{1,0:T(8,128)(2,1)S(1)} collective-permute-done((bf16[96,1280]{1,0:T(8,128)(2,1)S(1)}, bf16[96,1280]{1,0:T(8,128)(2,1)S(1)}, u32[]{:S(2)}, u32[]{:S(2)}) %collective-permute-start.8) | collective-permute-done | bytes 245792 | tf_op jit(solution)/shard_map/ppermute | solution.py:366
  74.0 0.5 collective-permute-start.12
  74.5 0.0 collective-permute-start.13
  74.6 4.2 %collective-permute-done.10.refs_7_ = bf16[96,1280]{1,0:T(8,128)(2,1)S(1)} collective-permute-done((bf16[96,1280]{1,0:T(8,128)(2,1)S(1)}, bf16[96,1280]{1,0:T(8,128)(2,1)S(1)}, u32[]{:S(2)}, u32[]{:S(2)}) %collective-permute-start.10) | collective-permute-done | bytes 245792 | tf_op jit(solution)/shard_map/ppermute | solution.py:366
  78.7 0.0 collective-permute-done.11.refs_12_
  78.8 0.0 collective-permute-done.12.refs_13_
  78.8 0.1 collective-permute-start.14
  78.8 1.5 %collective-permute-done.14.refs_15_ = bf16[96,1280]{1,0:T(8,128)(2,1)S(1)} collective-permute-done((bf16[96,1280]{1,0:T(8,128)(2,1)S(1)}, bf16[96,1280]{1,0:T(8,128)(2,1)S(1)}, u32[]{:S(2)}, u32[]{:S(2)}) %collective-permute-start.14) | collective-permute-done | bytes 245792 | tf_op jit(solution)/shard_map/ppermute | solution.py:366
  80.3 6.0 %last_product.1 = bf16[2,256,2304]{2,1,0:T(8,128)(2,1)} custom-call(s32[1]{0:T(128)} %get-tuple-element.139.me_ref, f32[512,768]{1,0:T(8,128)S(1)} %get-tuple-element.149.part_any, bf16[2,384,768]{2,1,0:T(8,128)(2,1)S(1)} %get-tuple-element.150.late_any, bf16[96,1280]{1,0:T(8,128)(2,1)S(1)} %get-tuple-element.140.refs_0_, ...), custom_call_target="tpu_custom_call" | custom-call | flops 20000000000 | bytes 1 | tf_op jit(solution)/shard_map/last_product/pallas_call | solution.py:436
  86.4 0.8 while.16
  (10 shorter events, 0.0 us)
Async XLA Ops:
  7.2 0.9 copy-start
  8.1 0.7 copy-start.1
  8.8 32.5 %copy-start.3 = (s32[256]{0:T(256)S(1)}, s32[256]{0:T(256)}, u32[]{:S(2)}) copy-start(s32[256]{0:T(256)} %param.11) | copy-start | bytes 3076
  42.9 8.7 %collective-permute-start.1 = (bf16[96,1280]{1,0:T(8,128)(2,1)S(1)}, bf16[96,1280]{1,0:T(8,128)(2,1)S(1)}, u32[]{:S(2)}, u32[]{:S(2)}) collective-permute-start(bf16[96,1280]{1,0:T(8,128)(2,1)S(1)} %get-tuple-element.140.refs_0_), channel_id=1, source_target_pairs={{0,2},{1,3},{2,0},{3,1},{4,6},{5,7},{6,4},{7,5},{8,10},{9,11},{10,... | collective-permute-start | bytes 737288 | tf_op jit(solution)/shard_map/ppermute | solution.py:366
  44.2 12.2 %collective-permute-start.2 = (bf16[96,1280]{1,0:T(8,128)(2,1)S(1)}, bf16[96,1280]{1,0:T(8,128)(2,1)S(1)}, u32[]{:S(2)}, u32[]{:S(2)}) collective-permute-start(bf16[96,1280]{1,0:T(8,128)(2,1)S(1)} %get-tuple-element.140.refs_0_), channel_id=1, source_target_pairs={{0,4},{1,5},{2,6},{3,7},{4,0},{5,1},{6,2},{7,3},{8,12},{9,13},{10,... | collective-permute-start | bytes 737288 | tf_op jit(solution)/shard_map/ppermute | solution.py:366
  46.0 13.8 %collective-permute-start = (bf16[96,1280]{1,0:T(8,128)(2,1)S(1)}, bf16[96,1280]{1,0:T(8,128)(2,1)S(1)}, u32[]{:S(2)}, u32[]{:S(2)}) collective-permute-start(bf16[96,1280]{1,0:T(8,128)(2,1)S(1)} %get-tuple-element.140.refs_0_), channel_id=1, source_target_pairs={{0,8},{1,9},{2,10},{3,11},{4,12},{5,13},{6,14},{7,15},{8,0},{9,1},... | collective-permute-start | bytes 737288 | tf_op jit(solution)/shard_map/ppermute | solution.py:366
  47.5 12.3 %collective-permute-start.3 = (bf16[96,1280]{1,0:T(8,128)(2,1)S(1)}, bf16[96,1280]{1,0:T(8,128)(2,1)S(1)}, u32[]{:S(2)}, u32[]{:S(2)}) collective-permute-start(bf16[96,1280]{1,0:T(8,128)(2,1)S(1)} %get-tuple-element.140.refs_0_), channel_id=1, source_target_pairs={{0,1},{1,0},{2,3},{3,2},{4,5},{5,4},{6,7},{7,6},{8,9},{9,8},{10,11... | collective-permute-start | bytes 737288 | tf_op jit(solution)/shard_map/ppermute | solution.py:366
  51.6 8.2 %collective-permute-start.4 = (bf16[96,1280]{1,0:T(8,128)(2,1)S(1)}, bf16[96,1280]{1,0:T(8,128)(2,1)S(1)}, u32[]{:S(2)}, u32[]{:S(2)}) collective-permute-start(bf16[96,1280]{1,0:T(8,128)(2,1)S(1)} %collective-permute-done.1.refs_1_), channel_id=1, source_target_pairs={{0,1},{1,0},{2,3},{3,2},{4,5},{5,4},{6,7},{7,6},{8,9},{9,8},{10,11... | collective-permute-start | bytes 737288 | tf_op jit(solution)/shard_map/ppermute | solution.py:366
  56.4 3.4 %collective-permute-start.5 = (bf16[96,1280]{1,0:T(8,128)(2,1)S(1)}, bf16[96,1280]{1,0:T(8,128)(2,1)S(1)}, u32[]{:S(2)}, u32[]{:S(2)}) collective-permute-start(bf16[96,1280]{1,0:T(8,128)(2,1)S(1)} %collective-permute-done.2.refs_2_), channel_id=1, source_target_pairs={{0,1},{1,0},{2,3},{3,2},{4,5},{5,4},{6,7},{7,6},{8,9},{9,8},{10,11... | collective-permute-start | bytes 737288 | tf_op jit(solution)/shard_map/ppermute | solution.py:366
  59.8 2.3 %collective-permute-start.7 = (bf16[96,1280]{1,0:T(8,128)(2,1)S(1)}, bf16[96,1280]{1,0:T(8,128)(2,1)S(1)}, u32[]{:S(2)}, u32[]{:S(2)}) collective-permute-start(bf16[96,1280]{1,0:T(8,128)(2,1)S(1)} %collective-permute-done.refs_3_), channel_id=1, source_target_pairs={{0,1},{1,0},{2,3},{3,2},{4,5},{5,4},{6,7},{7,6},{8,9},{9,8},{10,11... | collective-permute-start | bytes 737288 | tf_op jit(solution)/shard_map/ppermute | solution.py:366
  59.9 8.4 %collective-permute-start.6 = (bf16[96,1280]{1,0:T(8,128)(2,1)S(1)}, bf16[96,1280]{1,0:T(8,128)(2,1)S(1)}, u32[]{:S(2)}, u32[]{:S(2)}) collective-permute-start(bf16[96,1280]{1,0:T(8,128)(2,1)S(1)} %collective-permute-done.refs_3_), channel_id=1, source_target_pairs={{0,4},{1,5},{2,6},{3,7},{4,0},{5,1},{6,2},{7,3},{8,12},{9,13},{10,... | collective-permute-start | bytes 737288 | tf_op jit(solution)/shard_map/ppermute | solution.py:366
  59.9 14.1 %collective-permute-start.9 = (bf16[96,1280]{1,0:T(8,128)(2,1)S(1)}, bf16[96,1280]{1,0:T(8,128)(2,1)S(1)}, u32[]{:S(2)}, u32[]{:S(2)}) collective-permute-start(bf16[96,1280]{1,0:T(8,128)(2,1)S(1)} %collective-permute-done.refs_3_), channel_id=1, source_target_pairs={{0,2},{1,3},{2,0},{3,1},{4,6},{5,7},{6,4},{7,5},{8,10},{9,11},{10,... | collective-permute-start | bytes 737288 | tf_op jit(solution)/shard_map/ppermute | solution.py:366
  61.2 12.9 %collective-permute-start.8 = (bf16[96,1280]{1,0:T(8,128)(2,1)S(1)}, bf16[96,1280]{1,0:T(8,128)(2,1)S(1)}, u32[]{:S(2)}, u32[]{:S(2)}) collective-permute-start(bf16[96,1280]{1,0:T(8,128)(2,1)S(1)} %collective-permute-done.2.refs_2_), channel_id=1, source_target_pairs={{0,2},{1,3},{2,0},{3,1},{4,6},{5,7},{6,4},{7,5},{8,10},{9,11},{10,... | collective-permute-start | bytes 737288 | tf_op jit(solution)/shard_map/ppermute | solution.py:366
  68.2 10.5 %collective-permute-start.10 = (bf16[96,1280]{1,0:T(8,128)(2,1)S(1)}, bf16[96,1280]{1,0:T(8,128)(2,1)S(1)}, u32[]{:S(2)}, u32[]{:S(2)}) collective-permute-start(bf16[96,1280]{1,0:T(8,128)(2,1)S(1)} %collective-permute-done.6.refs_6_), channel_id=1, source_target_pairs={{0,2},{1,3},{2,0},{3,1},{4,6},{5,7},{6,4},{7,5},{8,10},{9,11},{10,... | collective-permute-start | bytes 737288 | tf_op jit(solution)/shard_map/ppermute | solution.py:366
  74.0 4.7 %collective-permute-start.11 = (bf16[96,1280]{1,0:T(8,128)(2,1)S(1)}, bf16[96,1280]{1,0:T(8,128)(2,1)S(1)}, u32[]{:S(2)}, u32[]{:S(2)}) collective-permute-start(bf16[96,1280]{1,0:T(8,128)(2,1)S(1)} %collective-permute-done.8.refs_4_), channel_id=1, source_target_pairs={{0,1},{1,0},{2,3},{3,2},{4,5},{5,4},{6,7},{7,6},{8,9},{9,8},{10,11... | collective-permute-start | bytes 737288 | tf_op jit(solution)/shard_map/ppermute | solution.py:366
  74.0 4.7 %collective-permute-start.12 = (bf16[96,1280]{1,0:T(8,128)(2,1)S(1)}, bf16[96,1280]{1,0:T(8,128)(2,1)S(1)}, u32[]{:S(2)}, u32[]{:S(2)}) collective-permute-start(bf16[96,1280]{1,0:T(8,128)(2,1)S(1)} %collective-permute-done.9.refs_5_), channel_id=1, source_target_pairs={{0,1},{1,0},{2,3},{3,2},{4,5},{5,4},{6,7},{7,6},{8,9},{9,8},{10,11... | collective-permute-start | bytes 737288 | tf_op jit(solution)/shard_map/ppermute | solution.py:366
  74.5 4.2 %collective-permute-start.13 = (bf16[96,1280]{1,0:T(8,128)(2,1)S(1)}, bf16[96,1280]{1,0:T(8,128)(2,1)S(1)}, u32[]{:S(2)}, u32[]{:S(2)}) collective-permute-start(bf16[96,1280]{1,0:T(8,128)(2,1)S(1)} %collective-permute-done.6.refs_6_), channel_id=1, source_target_pairs={{0,1},{1,0},{2,3},{3,2},{4,5},{5,4},{6,7},{7,6},{8,9},{9,8},{10,11... | collective-permute-start | bytes 737288 | tf_op jit(solution)/shard_map/ppermute | solution.py:366
  78.8 1.6 %collective-permute-start.14 = (bf16[96,1280]{1,0:T(8,128)(2,1)S(1)}, bf16[96,1280]{1,0:T(8,128)(2,1)S(1)}, u32[]{:S(2)}, u32[]{:S(2)}) collective-permute-start(bf16[96,1280]{1,0:T(8,128)(2,1)S(1)} %collective-permute-done.10.refs_7_), channel_id=1, source_target_pairs={{0,1},{1,0},{2,3},{3,2},{4,5},{5,4},{6,7},{7,6},{8,9},{9,8},{10,11... | collective-permute-start | bytes 737288 | tf_op jit(solution)/shard_map/ppermute | solution.py:366

commit v17 on v12

--- a/solution.py
+++ b/solution.py
@@ -127,7 +127,7 @@
             self.edges.append(jnp.sum(self.used * jnp.floor((reach + extra) * 0.5), axis=0, keepdims=True))
 
 
-def pack_kernel(vir_ref, occ_ref, panels_ref, *refs):
+def pack_kernel(shells, pairs_ref, count_ref, vir_ref, occ_ref, panels_ref, code_ref, *refs):
     outs, (turned_ref,) = refs[:4], refs[4:]
     me = lax.axis_index("shell")
     core, y = lax.rem(me, 2), lax.rem(lax.div(me, 2), 2)
@@ -151,9 +151,6 @@
                 pair = turned_ref[pl.ds(2 * device, 2)].reshape(2 * BLK_DEV, block)
                 out[rows:, z * block : (z + 1) * block] = pair.astype(BF16)
             out[rows:, Z * block :] = jnp.zeros((2 * BLK_DEV, out.shape[1] - Z * block), BF16)
-
-
-def ids_kernel(shells, pairs_ref, count_ref, code_ref):
     code = pairs_ref[1:2, :] + shells * pairs_ref[0:1, :]
     code = jnp.where(iota((1, BLK_DEV), 1) < count_ref[...], code, -1).astype(F32)
     square = (BLK_DEV, BLK_DEV)
@@ -381,26 +378,17 @@
     def swap(array, bit):
         return lax.ppermute(array, "shell", [(i, i ^ bit) for i in range(n)])
 
-    keep, to_core, to_y, to_both = pl.pallas_call(
-        pack_kernel,
-        out_shape=[shape(here // 2 + 2 * BLK_DEV, packed)] * 4,
-        in_specs=[VMEM] * 3,
-        out_specs=[VMEM] * 4,
+    code, keep, to_core, to_y, to_both = pl.pallas_call(
+        functools.partial(pack_kernel, size_row.shape[1]),
+        out_shape=[shape(n, BLK_DEV, 128, dtype=jnp.int32)] + [shape(here // 2 + 2 * BLK_DEV, packed)] * 4,
+        in_specs=[VMEM] * 5,
+        out_specs=[VMEM] * 5,
         scratch_shapes=[pltpu.VMEM((2 * n, BLK_DEV, EDGE * EDGE), F32)],
         compiler_params=params(12),
-        cost_estimate=cost(3e8, 3e6),
+        cost_estimate=cost(3e9, 1),
         name="pack_rows",
-    )(vir_coef, occ_coef, panels)
+    )(block_pairs.T, block_count.reshape(1, 1), vir_coef, occ_coef, panels)
     to_y, to_both, to_core = swap(to_y, 2), swap(to_both, 3), swap(to_core, 1)
-    code = pl.pallas_call(
-        functools.partial(ids_kernel, size_row.shape[1]),
-        out_shape=shape(n, BLK_DEV, 128, dtype=jnp.int32),
-        in_specs=[VMEM] * 2,
-        out_specs=VMEM,
-        compiler_params=params(12),
-        cost_estimate=cost(1e4, 1e4),
-        name="pack_ids",
-    )(block_pairs.T, block_count.reshape(1, 1))
     code = lax.all_to_all(code, "shell", split_axis=0, concat_axis=0, tiled=True)
 
     mine, over, me, *panel = pl.pallas_call(
@@ -423,7 +411,8 @@
     corner, *panel = lax.optimization_barrier((corner, *panel))
 
     corner_y = swap(corner, 2)
-    near = [mine, mine_y, beside]
+    near = [mine, mine_y, beside, across]
+    far.append(swap(across, 1))
     early = len(near)
     slots = LIVE_DEV * n * EDGE
     half, late = pl.pallas_call(
@@ -447,11 +436,9 @@
         cost_estimate=cost(7e9, 1),
         name="half_transform",
     )(code, size_row, *panel, *near, *far)
-    far.append(swap(across, 1))
-    beside_y, across_y, half, late, *far = lax.optimization_barrier((beside_y, across_y, half, late, *far))
-    near += [across, beside_y, across_y, corner]
-    far += [swap(piece, 1) for piece in near[early + 1 :]]
-    corner_y, *far = lax.optimization_barrier((corner_y, *far))
+    near += [beside_y, across_y, corner]
+    far += [swap(piece, 1) for piece in near[early:]]
+    corner_y, half, late, *far = lax.optimization_barrier((corner_y, half, late, *far))
     near.append(corner_y)
     far.append(swap(corner_y, 1))
 

time: 95.1 us -> 93.5 us (0.983)
  Pallas kernels: 20.1 us -> 17.7 us
  starting transfers between devices: 15.8 us -> 18 us
  waiting for transfers between devices: 29.8 us -> 28.4 us
    ppermute x21, starting transfers between devices: 15.8 us -> 18 us  [swap(): return lax.ppermute(array, 'shell', [(i, i ^ bit) for i in range(n)])]
    ppermute x21, waiting for transfers between devices: 29.8 us -> 28.4 us  [swap(): return lax.ppermute(array, 'shell', [(i, i ^ bit) for i in range(n)])]
    pallas_call x1, Pallas kernels: 8.79 us -> 7.61 us  [short_way(): pl.pallas_call(functools.partial(half_kernel, here, early), out_shape=(sh...]
  transfers between devices with their start and end apart: 21 -> 21, of which waited for: 7 -> 7; matrix products, arithmetic and copies ran while one was open for 0% -> 0% of each run, Pallas kernels for 9% -> 8%
where the time goes in v17:
time: 93.5 us; the launch traced here: 93.3 us
  waiting for transfers between devices  28.4 us (30%)
  starting transfers between devices  18 us (19%)
  Pallas kernels  17.7 us (19%)
  between operations  14.2 us (15%)
  blocking collectives  12.8 us (14%)
  local copies, waits for them, and re-layouts  1.58 us (2%)
    ppermute x21, waiting for transfers between devices, swap(): return lax.ppermute(array, 'shell', [(i, i ^ bit) for i in range(n)])  28.4 us
    ppermute x21, starting transfers between devices, swap(): return lax.ppermute(array, 'shell', [(i, i ^ bit) for i in range(n)])  18 us
    all_to_all x1, blocking collectives, short_way(): lax.all_to_all(code, 'shell', split_axis=0, concat_axis=0, tiled=True)  12.8 us
    pallas_call x1, Pallas kernels, short_way(): pl.pallas_call(functools.partial(half_kernel, here, early), out_shape=(sh...  7.61 us
    pallas_call x1, Pallas kernels, short_way(): pl.pallas_call(functools.partial(last_kernel, count, early), out_shape=sh...  7.05 us
  transfers between devices with their start and end apart: 21, of which 7 were waited for; matrix products, arithmetic and copies ran while one was open for 0% of the time, Pallas kernels for 8%

profile of v17, /device:TPU:0, one launch (start us, length us, event | category | flops | bytes accessed | tf_op | source)
XLA Modules:
  0.0 93.3 jit_solution(14877453696998512630)
XLA Ops:
  7.2 0.9 copy-done
  8.1 0.7 copy-done.1
  8.8 1.6 %pack_rows.1 = (s32[16,8,128]{2,1,0:T(8,128)S(1)}, bf16[96,1280]{1,0:T(8,128)(2,1)S(1)}, bf16[96,1280]{1,0:T(8,128)(2,1)S(1)}, bf16[96,1280]{1,0:T(8,128)(2,1)S(1)}, bf16[96,1280]{1,0:T(8,128)(2,1)S(1)}) custom-call(s32[2,8]{1,0:T(2,128)S(1)} %bitcast.78, s32[1,1]{1,0:T(1,128)} %bitcast.77.count_ref, bf16[160,2304]{1,0:T(8,128)(2,1)} %vir_ref.1, ...), custom_call_target="tpu_custom_call" | custom-call | flops 3000000000 | bytes 1 | tf_op jit(solution)/shard_map/pack_rows/pallas_call | solution.py:381
  10.4 0.5 collective-permute-start
  10.9 2.6 %collective-permute-start.1 = (bf16[96,1280]{1,0:T(8,128)(2,1)S(1)}, bf16[96,1280]{1,0:T(8,128)(2,1)S(1)}, u32[]{:S(2)}, u32[]{:S(2)}) collective-permute-start(bf16[96,1280]{1,0:T(8,128)(2,1)S(1)} %get-tuple-element.247), channel_id=1, source_target_pairs={{0,2},{1,3},{2,0},{3,1},{4,6},{5,7},{6,4},{7,5},{8,10},{9,11},{10,... | collective-permute-start | bytes 737288 | tf_op jit(solution)/shard_map/ppermute | solution.py:379
  13.5 0.1 collective-permute-start.2
  13.6 12.8 %all_to_all.5.code_ref = s32[16,8,128]{2,1,0:T(8,128)S(1)} all-to-all(s32[16,8,128]{2,1,0:T(8,128)S(1)} %get-tuple-element.244), channel_id=1, replica_groups=mesh['groups'=2,'shell'=16] {'shell'}, dimensions={0} | all-to-all | bytes 131072 | tf_op jit(solution)/shard_map/all_to_all | solution.py:392
  26.4 0.0 collective-permute-done.refs_1_
  26.4 1.5 %pick_rows.1 = (bf16[128,1280]{1,0:T(8,128)(2,1)S(1)}, s32[1]{0:T(128)}, s32[1]{0:T(128)}, bf16[4,16,256]{2,1,0:T(8,128)(2,1)S(1)}, bf16[4,16,256]{2,1,0:T(8,128...) custom-call(s32[16,8,128]{2,1,0:T(8,128)S(1)} %all_to_all.5.code_ref, ...), custom_call_target="tpu_custom_call" | custom-call | flops 300000000 | bytes 2000000 | tf_op jit(solution)/shard_map/pick_rows/pallas_call | solution.py:394
  27.9 1.4 %collective-permute-start.4 = (bf16[128,1280]{1,0:T(8,128)(2,1)S(1)}, bf16[128,1280]{1,0:T(8,128)(2,1)S(1)}, u32[]{:S(2)}, u32[]{:S(2)}) collective-permute-start(bf16[128,1280]{1,0:T(8,128)(2,1)S(1)} %get-tuple-element.251.refs_4_.refs_0_), channel_id=1, source_target_pairs={{0,2},{1,3},{2,0},{3,1},{4,6},{5,7},{6,4},{7,5},{8,10},{9,11},{10,... | collective-permute-start | bytes 983048 | tf_op jit(solution)/shard_map/ppermute | solution.py:379
  29.3 1.6 %collective-permute-start.5 = (bf16[128,1280]{1,0:T(8,128)(2,1)S(1)}, bf16[128,1280]{1,0:T(8,128)(2,1)S(1)}, u32[]{:S(2)}, u32[]{:S(2)}) collective-permute-start(bf16[128,1280]{1,0:T(8,128)(2,1)S(1)} %get-tuple-element.251.refs_4_.refs_0_), channel_id=1, source_target_pairs={{0,4},{1,5},{2,6},{3,7},{4,0},{5,1},{6,2},{7,3},{8,12},{9,13},{10,... | collective-permute-start | bytes 983048 | tf_op jit(solution)/shard_map/ppermute | solution.py:379
  30.9 2.6 %collective-permute-start.3 = (bf16[128,1280]{1,0:T(8,128)(2,1)S(1)}, bf16[128,1280]{1,0:T(8,128)(2,1)S(1)}, u32[]{:S(2)}, u32[]{:S(2)}) collective-permute-start(bf16[128,1280]{1,0:T(8,128)(2,1)S(1)} %get-tuple-element.251.refs_4_.refs_0_), channel_id=1, source_target_pairs={{0,8},{1,9},{2,10},{3,11},{4,12},{5,13},{6,14},{7,15},{8,0},{9,1},... | collective-permute-start | bytes 983048 | tf_op jit(solution)/shard_map/ppermute | solution.py:379
  33.5 3.7 %collective-permute-done.4.refs_5_.refs_1_ = bf16[128,1280]{1,0:T(8,128)(2,1)S(1)} collective-permute-done((bf16[128,1280]{1,0:T(8,128)(2,1)S(1)}, bf16[128,1280]{1,0:T(8,128)(2,1)S(1)}, u32[]{:S(2)}, u32[]{:S(2)}) %collective-permute-start.4) | collective-permute-done | bytes 327712 | tf_op jit(solution)/shard_map/ppermute | solution.py:379
  37.2 8.1 %collective-permute-done.5.refs_6_.refs_2_ = bf16[128,1280]{1,0:T(8,128)(2,1)S(1)} collective-permute-done((bf16[128,1280]{1,0:T(8,128)(2,1)S(1)}, bf16[128,1280]{1,0:T(8,128)(2,1)S(1)}, u32[]{:S(2)}, u32[]{:S(2)}) %collective-permute-start.5) | collective-permute-done | bytes 327712 | tf_op jit(solution)/shard_map/ppermute | solution.py:379
  45.4 2.4 %collective-permute-done.3.refs_7_.refs_3_ = bf16[128,1280]{1,0:T(8,128)(2,1)S(1)} collective-permute-done((bf16[128,1280]{1,0:T(8,128)(2,1)S(1)}, bf16[128,1280]{1,0:T(8,128)(2,1)S(1)}, u32[]{:S(2)}, u32[]{:S(2)}) %collective-permute-start.3) | collective-permute-done | bytes 327712 | tf_op jit(solution)/shard_map/ppermute | solution.py:379
  47.7 0.5 collective-permute-start.9
  48.3 0.8 collective-permute-start.15
  49.0 1.2 %collective-permute-start.17 = (bf16[128,1280]{1,0:T(8,128)(2,1)S(1)}, bf16[128,1280]{1,0:T(8,128)(2,1)S(1)}, u32[]{:S(2)}, u32[]{:S(2)}) collective-permute-start(bf16[128,1280]{1,0:T(8,128)(2,1)S(1)} %collective-permute-done.3.refs_7_.refs_3_), channel_id=1, source_target_pairs={{0,2},{1,3},{2,0},{3,1},{4,6},{5,7},{6,4},{7,5},{8,10},{9,11},{10,... | collective-permute-start | bytes 983048 | tf_op jit(solution)/shard_map/ppermute | solution.py:379
  50.3 1.6 %collective-permute-start.10 = (bf16[4,16,256]{2,1,0:T(8,128)(2,1)S(1)}, bf16[4,16,256]{2,1,0:T(8,128)(2,1)S(1)}, u32[]{:S(2)}, u32[]{:S(2)}) collective-permute-start(bf16[4,16,256]{2,1,0:T(8,128)(2,1)S(1)} %get-tuple-element.254), channel_id=1, source_target_pairs={{0,4},{1,5},{2,6},{3,7},{4,0},{5,1},{6,2},{7,3},{8,12},{9,13},{10,... | collective-permute-start | bytes 98312 | tf_op jit(solution)/shard_map/ppermute | solution.py:379
  51.9 5.6 %collective-permute-done.10.refs_1_ = bf16[4,16,256]{2,1,0:T(8,128)(2,1)S(1)} collective-permute-done((bf16[4,16,256]{2,1,0:T(8,128)(2,1)S(1)}, bf16[4,16,256]{2,1,0:T(8,128)(2,1)S(1)}, u32[]{:S(2)}, u32[]{:S(2)}) %collective-permute-start.10) | collective-permute-done | bytes 32800 | tf_op jit(solution)/shard_map/ppermute | solution.py:379
  57.5 1.3 %collective-permute-start.11 = (bf16[4,16,256]{2,1,0:T(8,128)(2,1)S(1)}, bf16[4,16,256]{2,1,0:T(8,128)(2,1)S(1)}, u32[]{:S(2)}, u32[]{:S(2)}) collective-permute-start(bf16[4,16,256]{2,1,0:T(8,128)(2,1)S(1)} %get-tuple-element.255), channel_id=1, source_target_pairs={{0,8},{1,9},{2,10},{3,11},{4,12},{5,13},{6,14},{7,15},{8,0},{9,1},... | collective-permute-start | bytes 98312 | tf_op jit(solution)/shard_map/ppermute | solution.py:379
  58.7 3.9 %collective-permute-done.11.refs_2_ = bf16[4,16,256]{2,1,0:T(8,128)(2,1)S(1)} collective-permute-done((bf16[4,16,256]{2,1,0:T(8,128)(2,1)S(1)}, bf16[4,16,256]{2,1,0:T(8,128)(2,1)S(1)}, u32[]{:S(2)}, u32[]{:S(2)}) %collective-permute-start.11) | collective-permute-done | bytes 32800 | tf_op jit(solution)/shard_map/ppermute | solution.py:379
  62.6 2.3 %collective-permute-start.12 = (bf16[4,16,256]{2,1,0:T(8,128)(2,1)S(1)}, bf16[4,16,256]{2,1,0:T(8,128)(2,1)S(1)}, u32[]{:S(2)}, u32[]{:S(2)}) collective-permute-start(bf16[4,16,256]{2,1,0:T(8,128)(2,1)S(1)} %get-tuple-element.256), channel_id=1, source_target_pairs={{0,12},{1,13},{2,14},{3,15},{4,8},{5,9},{6,10},{7,11},{8,4},{9,5},... | collective-permute-start | bytes 98312 | tf_op jit(solution)/shard_map/ppermute | solution.py:379
  64.9 3.4 %collective-permute-done.12.refs_3_ = bf16[4,16,256]{2,1,0:T(8,128)(2,1)S(1)} collective-permute-done((bf16[4,16,256]{2,1,0:T(8,128)(2,1)S(1)}, bf16[4,16,256]{2,1,0:T(8,128)(2,1)S(1)}, u32[]{:S(2)}, u32[]{:S(2)}) %collective-permute-start.12) | collective-permute-done | bytes 32800 | tf_op jit(solution)/shard_map/ppermute | solution.py:379
  68.3 0.4 collective-permute-start.13
  68.8 0.5 collective-permute-start.16
  69.3 0.1 collective-permute-start.18
  69.4 7.6 %half_transform.1 = (f32[512,1024]{1,0:T(8,128)S(1)}, bf16[2,512,1024]{2,1,0:T(8,128)(2,1)S(1)}) custom-call(s32[16,8,128]{2,1,0:T(8,128)S(1)} %all_to_all.5.code_ref, s32[1,256]{1,0:T(1,128)S(1)} %bitcast.88, bf16[4,16,256]{2,1,0:T(8,128)(2,1)S(1)} %get-tuple-element.409.refs_0_, bf16[4,16,256]{2,1,0:T(8,128)(2,1)S(1)} %collective-permute-done.10.refs_1_, ...), custom_call_target="tpu_custom_call" | custom-call | flops 7000000000 | bytes 1 | tf_op jit(solution)/shard_map/half_transform/pallas_call | solution.py:418
  77.0 0.5 collective-permute-start.20
  77.6 1.3 %collective-permute-done.20.refs_15_ = bf16[128,1280]{1,0:T(8,128)(2,1)S(1)} collective-permute-done((bf16[128,1280]{1,0:T(8,128)(2,1)S(1)}, bf16[128,1280]{1,0:T(8,128)(2,1)S(1)}, u32[]{:S(2)}, u32[]{:S(2)}) %collective-permute-start.20) | collective-permute-done | bytes 327712 | tf_op jit(solution)/shard_map/ppermute | solution.py:379
  78.8 7.0 %last_product.1 = bf16[2,256,2304]{2,1,0:T(8,128)(2,1)} custom-call(s32[1]{0:T(128)} %get-tuple-element.408.me_ref, f32[512,1024]{1,0:T(8,128)S(1)} %get-tuple-element.269.part_any, bf16[2,512,1024]{2,1,0:T(8,128)(2,1)S(1)} %get-tuple-element.270.late_any, bf16[128,1280]{1,0:T(8,128)(2,1)S(1)} %get-tuple-element.251.refs_4_.refs_0_, ...), custom_call_target="tpu_custom_call" | custom-call | flops 20000000000 | bytes 1 | tf_op jit(solution)/shard_map/last_product/pallas_call | solution.py:447
  85.9 0.6 while.17
  (22 shorter events, 0.1 us)
Async XLA Ops:
  7.2 0.9 copy-start
  8.1 0.7 copy-start.1
  8.8 17.6 %copy-start.3 = (s32[256]{0:T(256)S(1)}, s32[256]{0:T(256)}, u32[]{:S(2)}) copy-start(s32[256]{0:T(256)} %param.11) | copy-start | bytes 3076
  10.4 16.0 %collective-permute-start = (bf16[96,1280]{1,0:T(8,128)(2,1)S(1)}, bf16[96,1280]{1,0:T(8,128)(2,1)S(1)}, u32[]{:S(2)}, u32[]{:S(2)}) collective-permute-start(bf16[96,1280]{1,0:T(8,128)(2,1)S(1)} %get-tuple-element.246), channel_id=1, source_target_pairs={{0,1},{1,0},{2,3},{3,2},{4,5},{5,4},{6,7},{7,6},{8,9},{9,8},{10,11... | collective-permute-start | bytes 737288 | tf_op jit(solution)/shard_map/ppermute | solution.py:379
  10.9 15.5 %collective-permute-start.1 = (bf16[96,1280]{1,0:T(8,128)(2,1)S(1)}, bf16[96,1280]{1,0:T(8,128)(2,1)S(1)}, u32[]{:S(2)}, u32[]{:S(2)}) collective-permute-start(bf16[96,1280]{1,0:T(8,128)(2,1)S(1)} %get-tuple-element.247), channel_id=1, source_target_pairs={{0,2},{1,3},{2,0},{3,1},{4,6},{5,7},{6,4},{7,5},{8,10},{9,11},{10,... | collective-permute-start | bytes 737288 | tf_op jit(solution)/shard_map/ppermute | solution.py:379
  13.5 12.9 %collective-permute-start.2 = (bf16[96,1280]{1,0:T(8,128)(2,1)S(1)}, bf16[96,1280]{1,0:T(8,128)(2,1)S(1)}, u32[]{:S(2)}, u32[]{:S(2)}) collective-permute-start(bf16[96,1280]{1,0:T(8,128)(2,1)S(1)} %get-tuple-element.248), channel_id=1, source_target_pairs={{0,3},{1,2},{2,1},{3,0},{4,7},{5,6},{6,5},{7,4},{8,11},{9,10},{10,... | collective-permute-start | bytes 737288 | tf_op jit(solution)/shard_map/ppermute | solution.py:379
  27.9 9.3 %collective-permute-start.4 = (bf16[128,1280]{1,0:T(8,128)(2,1)S(1)}, bf16[128,1280]{1,0:T(8,128)(2,1)S(1)}, u32[]{:S(2)}, u32[]{:S(2)}) collective-permute-start(bf16[128,1280]{1,0:T(8,128)(2,1)S(1)} %get-tuple-element.251.refs_4_.refs_0_), channel_id=1, source_target_pairs={{0,2},{1,3},{2,0},{3,1},{4,6},{5,7},{6,4},{7,5},{8,10},{9,11},{10,... | collective-permute-start | bytes 983048 | tf_op jit(solution)/shard_map/ppermute | solution.py:379
  29.3 16.0 %collective-permute-start.5 = (bf16[128,1280]{1,0:T(8,128)(2,1)S(1)}, bf16[128,1280]{1,0:T(8,128)(2,1)S(1)}, u32[]{:S(2)}, u32[]{:S(2)}) collective-permute-start(bf16[128,1280]{1,0:T(8,128)(2,1)S(1)} %get-tuple-element.251.refs_4_.refs_0_), channel_id=1, source_target_pairs={{0,4},{1,5},{2,6},{3,7},{4,0},{5,1},{6,2},{7,3},{8,12},{9,13},{10,... | collective-permute-start | bytes 983048 | tf_op jit(solution)/shard_map/ppermute | solution.py:379
  30.9 16.8 %collective-permute-start.3 = (bf16[128,1280]{1,0:T(8,128)(2,1)S(1)}, bf16[128,1280]{1,0:T(8,128)(2,1)S(1)}, u32[]{:S(2)}, u32[]{:S(2)}) collective-permute-start(bf16[128,1280]{1,0:T(8,128)(2,1)S(1)} %get-tuple-element.251.refs_4_.refs_0_), channel_id=1, source_target_pairs={{0,8},{1,9},{2,10},{3,11},{4,12},{5,13},{6,14},{7,15},{8,0},{9,1},... | collective-permute-start | bytes 983048 | tf_op jit(solution)/shard_map/ppermute | solution.py:379
  33.5 14.2 %collective-permute-start.6 = (bf16[128,1280]{1,0:T(8,128)(2,1)S(1)}, bf16[128,1280]{1,0:T(8,128)(2,1)S(1)}, u32[]{:S(2)}, u32[]{:S(2)}) collective-permute-start(bf16[128,1280]{1,0:T(8,128)(2,1)S(1)} %get-tuple-element.251.refs_4_.refs_0_), channel_id=1, source_target_pairs={{0,1},{1,0},{2,3},{3,2},{4,5},{5,4},{6,7},{7,6},{8,9},{9,8},{10,11... | collective-permute-start | bytes 983048 | tf_op jit(solution)/shard_map/ppermute | solution.py:379
  37.2 10.5 %collective-permute-start.7 = (bf16[128,1280]{1,0:T(8,128)(2,1)S(1)}, bf16[128,1280]{1,0:T(8,128)(2,1)S(1)}, u32[]{:S(2)}, u32[]{:S(2)}) collective-permute-start(bf16[128,1280]{1,0:T(8,128)(2,1)S(1)} %collective-permute-done.4.refs_5_.refs_1_), channel_id=1, source_target_pairs={{0,1},{1,0},{2,3},{3,2},{4,5},{5,4},{6,7},{7,6},{8,9},{9,8},{10,11... | collective-permute-start | bytes 983048 | tf_op jit(solution)/shard_map/ppermute | solution.py:379
  45.4 2.4 %collective-permute-start.8 = (bf16[128,1280]{1,0:T(8,128)(2,1)S(1)}, bf16[128,1280]{1,0:T(8,128)(2,1)S(1)}, u32[]{:S(2)}, u32[]{:S(2)}) collective-permute-start(bf16[128,1280]{1,0:T(8,128)(2,1)S(1)} %collective-permute-done.5.refs_6_.refs_2_), channel_id=1, source_target_pairs={{0,1},{1,0},{2,3},{3,2},{4,5},{5,4},{6,7},{7,6},{8,9},{9,8},{10,11... | collective-permute-start | bytes 983048 | tf_op jit(solution)/shard_map/ppermute | solution.py:379
  47.7 20.6 %collective-permute-start.9 = (bf16[128,1280]{1,0:T(8,128)(2,1)S(1)}, bf16[128,1280]{1,0:T(8,128)(2,1)S(1)}, u32[]{:S(2)}, u32[]{:S(2)}) collective-permute-start(bf16[128,1280]{1,0:T(8,128)(2,1)S(1)} %collective-permute-done.3.refs_7_.refs_3_), channel_id=1, source_target_pairs={{0,4},{1,5},{2,6},{3,7},{4,0},{5,1},{6,2},{7,3},{8,12},{9,13},{10,... | collective-permute-start | bytes 983048 | tf_op jit(solution)/shard_map/ppermute | solution.py:379
  48.3 20.5 %collective-permute-start.15 = (bf16[128,1280]{1,0:T(8,128)(2,1)S(1)}, bf16[128,1280]{1,0:T(8,128)(2,1)S(1)}, u32[]{:S(2)}, u32[]{:S(2)}) collective-permute-start(bf16[128,1280]{1,0:T(8,128)(2,1)S(1)} %collective-permute-done.5.refs_6_.refs_2_), channel_id=1, source_target_pairs={{0,2},{1,3},{2,0},{3,1},{4,6},{5,7},{6,4},{7,5},{8,10},{9,11},{10,... | collective-permute-start | bytes 983048 | tf_op jit(solution)/shard_map/ppermute | solution.py:379
  49.0 20.3 %collective-permute-start.17 = (bf16[128,1280]{1,0:T(8,128)(2,1)S(1)}, bf16[128,1280]{1,0:T(8,128)(2,1)S(1)}, u32[]{:S(2)}, u32[]{:S(2)}) collective-permute-start(bf16[128,1280]{1,0:T(8,128)(2,1)S(1)} %collective-permute-done.3.refs_7_.refs_3_), channel_id=1, source_target_pairs={{0,2},{1,3},{2,0},{3,1},{4,6},{5,7},{6,4},{7,5},{8,10},{9,11},{10,... | collective-permute-start | bytes 983048 | tf_op jit(solution)/shard_map/ppermute | solution.py:379
  50.3 19.1 %collective-permute-start.14 = (bf16[128,1280]{1,0:T(8,128)(2,1)S(1)}, bf16[128,1280]{1,0:T(8,128)(2,1)S(1)}, u32[]{:S(2)}, u32[]{:S(2)}) collective-permute-start(bf16[128,1280]{1,0:T(8,128)(2,1)S(1)} %collective-permute-done.3.refs_7_.refs_3_), channel_id=1, source_target_pairs={{0,1},{1,0},{2,3},{3,2},{4,5},{5,4},{6,7},{7,6},{8,9},{9,8},{10,11... | collective-permute-start | bytes 983048 | tf_op jit(solution)/shard_map/ppermute | solution.py:379
  50.3 7.2 %collective-permute-start.10 = (bf16[4,16,256]{2,1,0:T(8,128)(2,1)S(1)}, bf16[4,16,256]{2,1,0:T(8,128)(2,1)S(1)}, u32[]{:S(2)}, u32[]{:S(2)}) collective-permute-start(bf16[4,16,256]{2,1,0:T(8,128)(2,1)S(1)} %get-tuple-element.254), channel_id=1, source_target_pairs={{0,4},{1,5},{2,6},{3,7},{4,0},{5,1},{6,2},{7,3},{8,12},{9,13},{10,... | collective-permute-start | bytes 98312 | tf_op jit(solution)/shard_map/ppermute | solution.py:379
  57.5 5.2 %collective-permute-start.11 = (bf16[4,16,256]{2,1,0:T(8,128)(2,1)S(1)}, bf16[4,16,256]{2,1,0:T(8,128)(2,1)S(1)}, u32[]{:S(2)}, u32[]{:S(2)}) collective-permute-start(bf16[4,16,256]{2,1,0:T(8,128)(2,1)S(1)} %get-tuple-element.255), channel_id=1, source_target_pairs={{0,8},{1,9},{2,10},{3,11},{4,12},{5,13},{6,14},{7,15},{8,0},{9,1},... | collective-permute-start | bytes 98312 | tf_op jit(solution)/shard_map/ppermute | solution.py:379
  62.6 5.7 %collective-permute-start.12 = (bf16[4,16,256]{2,1,0:T(8,128)(2,1)S(1)}, bf16[4,16,256]{2,1,0:T(8,128)(2,1)S(1)}, u32[]{:S(2)}, u32[]{:S(2)}) collective-permute-start(bf16[4,16,256]{2,1,0:T(8,128)(2,1)S(1)} %get-tuple-element.256), channel_id=1, source_target_pairs={{0,12},{1,13},{2,14},{3,15},{4,8},{5,9},{6,10},{7,11},{8,4},{9,5},... | collective-permute-start | bytes 98312 | tf_op jit(solution)/shard_map/ppermute | solution.py:379
  68.3 8.7 %collective-permute-start.13 = (bf16[128,1280]{1,0:T(8,128)(2,1)S(1)}, bf16[128,1280]{1,0:T(8,128)(2,1)S(1)}, u32[]{:S(2)}, u32[]{:S(2)}) collective-permute-start(bf16[128,1280]{1,0:T(8,128)(2,1)S(1)} %collective-permute-done.9.refs_6_), channel_id=1, source_target_pairs={{0,2},{1,3},{2,0},{3,1},{4,6},{5,7},{6,4},{7,5},{8,10},{9,11},{10,... | collective-permute-start | bytes 983048 | tf_op jit(solution)/shard_map/ppermute | solution.py:379
  68.8 8.2 %collective-permute-start.19 = (bf16[128,1280]{1,0:T(8,128)(2,1)S(1)}, bf16[128,1280]{1,0:T(8,128)(2,1)S(1)}, u32[]{:S(2)}, u32[]{:S(2)}) collective-permute-start(bf16[128,1280]{1,0:T(8,128)(2,1)S(1)} %collective-permute-done.9.refs_6_), channel_id=1, source_target_pairs={{0,1},{1,0},{2,3},{3,2},{4,5},{5,4},{6,7},{7,6},{8,9},{9,8},{10,11... | collective-permute-start | bytes 983048 | tf_op jit(solution)/shard_map/ppermute | solution.py:379
  68.8 8.2 %collective-permute-start.16 = (bf16[128,1280]{1,0:T(8,128)(2,1)S(1)}, bf16[128,1280]{1,0:T(8,128)(2,1)S(1)}, u32[]{:S(2)}, u32[]{:S(2)}) collective-permute-start(bf16[128,1280]{1,0:T(8,128)(2,1)S(1)} %collective-permute-done.15.refs_4_), channel_id=1, source_target_pairs={{0,1},{1,0},{2,3},{3,2},{4,5},{5,4},{6,7},{7,6},{8,9},{9,8},{10,11... | collective-permute-start | bytes 983048 | tf_op jit(solution)/shard_map/ppermute | solution.py:379
  69.3 7.7 %collective-permute-start.18 = (bf16[128,1280]{1,0:T(8,128)(2,1)S(1)}, bf16[128,1280]{1,0:T(8,128)(2,1)S(1)}, u32[]{:S(2)}, u32[]{:S(2)}) collective-permute-start(bf16[128,1280]{1,0:T(8,128)(2,1)S(1)} %collective-permute-done.17.refs_5_), channel_id=1, source_target_pairs={{0,1},{1,0},{2,3},{3,2},{4,5},{5,4},{6,7},{7,6},{8,9},{9,8},{10,11... | collective-permute-start | bytes 983048 | tf_op jit(solution)/shard_map/ppermute | solution.py:379
  77.0 1.8 %collective-permute-start.20 = (bf16[128,1280]{1,0:T(8,128)(2,1)S(1)}, bf16[128,1280]{1,0:T(8,128)(2,1)S(1)}, u32[]{:S(2)}, u32[]{:S(2)}) collective-permute-start(bf16[128,1280]{1,0:T(8,128)(2,1)S(1)} %collective-permute-done.13.refs_7_), channel_id=1, source_target_pairs={{0,1},{1,0},{2,3},{3,2},{4,5},{5,4},{6,7},{7,6},{8,9},{9,8},{10,11... | collective-permute-start | bytes 983048 | tf_op jit(solution)/shard_map/ppermute | solution.py:379

commit v18 on v13

--- a/solution.py
+++ b/solution.py
@@ -162,7 +162,7 @@
 
 
 def pick_kernel(here, code_ref, size_ref, *refs):
-    sources, (out_ref, over_ref, me_ref), panel_refs = refs[:4], refs[4:7], refs[7:]
+    sources, (out_ref, over_ref, me_ref, panel_ref) = refs[:4], refs[4:]
     me = lax.axis_index("shell")
     me_ref[0] = me
     core, y, z = lax.rem(me, 2), lax.rem(lax.div(me, 2), 2), lax.div(me, 4)
@@ -187,9 +187,8 @@
     for k, source in enumerate(sources):
         member = 2 * lax.rem(y + k // 2, 2) + lax.rem(core + k % 2, 2)
         device = 4 * z + member
-        for r, panel_ref in enumerate(panel_refs):
-            lanes = pl.ds(pl.multiple_of((z ^ r) * (EDGE * EDGE), 128), EDGE * EDGE)
-            panel_ref[member] = source[rows:, lanes]
+        for to_z in range(Z):
+            panel_ref[to_z, member] = source[rows:, to_z * EDGE * EDGE : (to_z + 1) * EDGE * EDGE]
         row = (2 * iota((shell_count, 128), 1) + device * here + y).astype(F32)
         where = row - shells.starts
         inside = (where >= 0.0) & (where < shells.size)
@@ -213,12 +212,11 @@
     return jnp.where((slot == 3) | (slot == 4), slot ^ 7, slot)
 
 
-def half_kernel(here, early, code_ref, size_ref, *refs):
-    panel_refs, pieces, refs = refs[:Z], refs[Z : Z + 2 * early], refs[Z + 2 * early :]
-    half_ref, late_ref, got_ref, occ_ref, part_ref, hot_ref, placed_ref, sems = refs
+def half_kernel(here, early, code_ref, got_ref, size_ref, *refs):
+    pieces, refs = refs[: 2 * early], refs[2 * early :]
+    half_ref, late_ref, occ_ref, part_ref, hot_ref, placed_ref, sems = refs
     me = lax.axis_index("shell")
     core, chip = lax.rem(me, CORES), lax.div(me, CORES)
-    z = lax.div(chip, Y)
     width = pieces[0].shape[1] - 128
     copies = []
     for far in range(2):
@@ -229,8 +227,6 @@
             copies.append(pltpu.make_async_copy(pieces[at].at[:, pl.ds(width, 128)], target, sems.at[at]))
     for copy in copies:
         copy.start()
-    for r, panel_ref in enumerate(panel_refs):
-        got_ref[pl.ds((z ^ r) * (Y * CORES), Y * CORES)] = panel_ref[...]
     window = CORES * Y * here
     shell_count = size_ref.shape[1]
     got = got_ref[...].astype(F32)
@@ -403,38 +399,39 @@
     )(block_pairs.T, block_count.reshape(1, 1))
     code = lax.all_to_all(code, "shell", split_axis=0, concat_axis=0, tiled=True)
 
-    mine, over, me, *panel = pl.pallas_call(
+    mine, over, me, panel = pl.pallas_call(
         functools.partial(pick_kernel, here),
         out_shape=[shape(CAP, packed), shape(1, dtype=jnp.int32), shape(1, dtype=jnp.int32)]
-        + [shape(Y * CORES, 2 * BLK_DEV, EDGE * EDGE)] * Z,
+        + [shape(Z, Y * CORES, 2 * BLK_DEV, EDGE * EDGE)],
         in_specs=[VMEM] * 6,
-        out_specs=[VMEM, SMEM, SMEM] + [VMEM] * Z,
+        out_specs=[VMEM, SMEM, SMEM, VMEM],
         compiler_params=params(12),
         cost_estimate=cost(3e8, 2e6),
         name="pick_rows",
     )(code, size_row, keep, to_core, to_y, to_both)
 
     across, mine_y, beside = swap(mine, 8), swap(mine, 2), swap(mine, 4)
-    panel = [panel[0]] + [swap(panel[r], 4 * r) for r in range(1, Z)]
-    mine_y, panel[1], panel[2] = lax.optimization_barrier((mine_y, panel[1], panel[2]))
-    far = [swap(mine, 1), swap(mine_y, 1), swap(beside, 1)]
-    across, beside, panel[3], *far = lax.optimization_barrier((across, beside, panel[3], *far))
+    lines = [[Y * CORES * z + k for z in range(Z)] for k in range(Y * CORES)]
+    got = lax.all_to_all(panel, "shell", split_axis=0, concat_axis=0, axis_index_groups=lines, tiled=True)
+    got = got.reshape(n, 2 * BLK_DEV, EDGE * EDGE)
+    far = [swap(mine, 1)]
+    across, mine_y, beside, got, *far = lax.optimization_barrier((across, mine_y, beside, got, *far))
 
     corner, beside_y, across_y = swap(across, 4), swap(beside, 2), swap(across, 2)
-    near = [mine, mine_y, beside]
+    near = [mine, mine_y, beside, across]
+    far += [swap(piece, 1) for piece in near[1:]]
     early = len(near)
     slots = LIVE_DEV * n * EDGE
     half, late = pl.pallas_call(
         functools.partial(half_kernel, here, early),
         out_shape=(shape(2 * NOCC, room, dtype=F32), shape(2, room - early * CAP, room)),
         grid=(1,),
-        in_specs=[VMEM] * (2 + Z) + [ANY] * (2 * early),
+        in_specs=[VMEM] * 3 + [ANY] * (2 * early),
         out_specs=(
             pl.BlockSpec((2 * NOCC, room), lambda i: (0, 0)),
             pl.BlockSpec((2, room - early * CAP, room), lambda i: (0, 0, 0)),
         ),
         scratch_shapes=[
-            pltpu.VMEM((n, 2 * BLK_DEV, EDGE * EDGE), BF16),
             pltpu.VMEM((early * CAP, NOCC), BF16),
             pltpu.VMEM((NOCC, slots), BF16),
             pltpu.VMEM((room - early * CAP, slots), BF16),
@@ -444,10 +441,10 @@
         compiler_params=params(30),
         cost_estimate=cost(7e9, 1),
         name="half_transform",
-    )(code, size_row, *panel, *near, *far)
+    )(code, got, size_row, *near, *far)
     corner, half, late = lax.optimization_barrier((corner, half, late))
     corner_y = swap(corner, 2)
-    near += [across, beside_y, across_y, corner]
+    near += [beside_y, across_y, corner]
     far += [swap(piece, 1) for piece in near[early:]]
     corner_y, *far = lax.optimization_barrier((corner_y, *far))
     near.append(corner_y)
@@ -473,7 +470,7 @@
         cost_estimate=cost(2e10, 1),
         name="last_product",
     )(me, half, late, *near, *far)
-    return out, over[0], code, me, panel
+    return out, over[0], code, got
 
 
 def per_device(*args):
@@ -483,13 +480,11 @@
     sparse = LIVE_DEV * n * EDGE < n * here
     if not (sparse and n == Z * Y * CORES and here <= 256 and here % 16 == 0 and nvir % 768 == 0):
         return from_start(*args)
-    out, over, code, me, panel = short_way(*args)
+    out, over, code, got = short_way(*args)
 
     def again(carry):
         over, _ = carry
-        over, code_now, me_now, panel_now, *held = lax.optimization_barrier((over, code, me, tuple(panel), *args[3:]))
-        z = me_now[0] // (Y * CORES)
-        turned = jnp.stack(panel_now)[jnp.arange(Z, dtype=jnp.int32) ^ z]
+        over, code_now, turned, *held = lax.optimization_barrier((over, code, got, *args[3:]))
         turned = turned.reshape(n, 2, BLK_DEV, EDGE * EDGE).swapaxes(1, 2).reshape(n * BLK_DEV, 2, EDGE * EDGE)
         code_now = jnp.max(code_now, axis=2).reshape(n * BLK_DEV)
         ids = jnp.maximum(code_now, 0)

time: 90.9 us -> 90 us (0.990)
  blocking collectives: 12.8 us -> 29 us
  waiting for transfers between devices: 25.4 us -> 14.1 us
  starting transfers between devices: 16.1 us -> 11.3 us
  Pallas kernels: 20.1 us -> 18.9 us
    all_to_all x0 -> x1, blocking collectives: none -> 16.1 us  [short_way(): lax.all_to_all(panel, 'shell', split_axis=0, concat_axis=0, axis_index_gr...]
    ppermute x21 -> x18, waiting for transfers between devices: 25.4 us -> 14.1 us  [swap(): return lax.ppermute(array, 'shell', [(i, i ^ bit) for i in range(n)])]
    ppermute x21 -> x18, starting transfers between devices: 16.1 us -> 11.3 us  [swap(): return lax.ppermute(array, 'shell', [(i, i ^ bit) for i in range(n)])]
  transfers between devices with their start and end apart: 21 -> 18, of which waited for: 6 -> 4; matrix products, arithmetic and copies ran while one was open for 0% -> 0% of each run, Pallas kernels for 10% -> 9%
where the time goes in v18:
time: 90 us; the launch traced here: 89.7 us
  blocking collectives  29 us (32%)
  Pallas kernels  18.9 us (21%)
  between operations  14.2 us (16%)
  waiting for transfers between devices  14.1 us (16%)
  starting transfers between devices  11.3 us (13%)
  local copies, waits for them, and re-layouts  1.58 us (2%)
    all_to_all x1, blocking collectives, short_way(): lax.all_to_all(panel, 'shell', split_axis=0, concat_axis=0, axis_index_gr...  16.1 us
    ppermute x18, waiting for transfers between devices, swap(): return lax.ppermute(array, 'shell', [(i, i ^ bit) for i in range(n)])  14.1 us
    all_to_all x1, blocking collectives, short_way(): lax.all_to_all(code, 'shell', split_axis=0, concat_axis=0, tiled=True)  12.8 us
    ppermute x18, starting transfers between devices, swap(): return lax.ppermute(array, 'shell', [(i, i ^ bit) for i in range(n)])  11.3 us
    pallas_call x1, Pallas kernels, short_way(): pl.pallas_call(functools.partial(half_kernel, here, early), out_shape=(sh...  8.31 us
    pallas_call x1, Pallas kernels, short_way(): pl.pallas_call(functools.partial(last_kernel, count, early), out_shape=sh...  6.76 us
    pallas_call x1, Pallas kernels, short_way(): pl.pallas_call(functools.partial(pick_kernel, here), out_shape=[shape(CAP...  2.14 us
  transfers between devices with their start and end apart: 18, of which 4 were waited for; matrix products, arithmetic and copies ran while one was open for 0% of the time, Pallas kernels for 9%

profile of v18, /device:TPU:0, one launch (start us, length us, event | category | flops | bytes accessed | tf_op | source)
XLA Modules:
  0.0 89.7 jit_solution(7828812445817215947)
XLA Ops:
  6.5 0.9 %copy-done.1 = bf16[8,32,256]{2,1,0:T(8,128)(2,1)S(1)} copy-done((bf16[8,32,256]{2,1,0:T(8,128)(2,1)S(1)}, bf16[8,32,256]{2,1,0:T(8,128)(2,1)}, u32[]{:S(2)}) %copy-start.1) | copy-done | bytes 131096
  7.4 1.6 %pack_rows.1 = (bf16[96,1280]{1,0:T(8,128)(2,1)S(1)}, bf16[96,1280]{1,0:T(8,128)(2,1)S(1)}, bf16[96,1280]{1,0:T(8,128)(2,1)S(1)}, bf16[96,1280]{1,0:T(8,128)(2,1)S(1)}) custom-call(bf16[160,2304]{1,0:T(8,128)(2,1)} %vir_ref.1, bf16[160,256]{1,0:T(8,128)(2,1)} %occ_ref.1, bf16[8,32,256]{2,1,0:T(8,128)(2,1)S(1)} %copy-done.1), custom_call_target="tpu_custom_call" | custom-call | flops 300000000 | bytes 3000000 | tf_op jit(solution)/shard_map/pack_rows/pallas_call | solution.py:380
  9.0 0.5 collective-permute-start
  9.5 2.6 %collective-permute-start.1 = (bf16[96,1280]{1,0:T(8,128)(2,1)S(1)}, bf16[96,1280]{1,0:T(8,128)(2,1)S(1)}, u32[]{:S(2)}, u32[]{:S(2)}) collective-permute-start(bf16[96,1280]{1,0:T(8,128)(2,1)S(1)} %get-tuple-element.173), channel_id=1, source_target_pairs={{0,2},{1,3},{2,0},{3,1},{4,6},{5,7},{6,4},{7,5},{8,10},{9,11},{10,... | collective-permute-start | bytes 737288 | tf_op jit(solution)/shard_map/ppermute | solution.py:378
  12.1 0.1 collective-permute-start.2
  12.9 0.0 copy-start
  12.9 0.7 copy-done
  13.5 0.2 pack_ids.1
  13.7 12.8 %all_to_all.10.code_ref = s32[16,8,128]{2,1,0:T(8,128)S(1)} all-to-all(s32[16,8,128]{2,1,0:T(8,128)S(1)} %pack_ids.1), channel_id=1, replica_groups=mesh['groups'=2,'shell'=16] {'shell'}, dimensions={0} | all-to-all | bytes 131072 | tf_op jit(solution)/shard_map/all_to_all | solution.py:400
  26.5 2.1 %pick_rows.1 = (bf16[128,1280]{1,0:T(8,128)(2,1)S(1)}, s32[1]{0:T(128)}, s32[1]{0:T(128)}, bf16[4,4,16,256]{3,2,1,0:T(8,128)(2,1)S(1)}) custom-call(s32[16,8,128]{2,1,0:T(8,128)S(1)} %all_to_all.10.code_ref, s32[1,256]{1,0:T(1,128)} %bitcast.66, bf16[96,1280]{1,0:T(8,128)(2,1)S(1)} %get-tuple-element.171.refs_0_, ...), custom_call_target="tpu_custom_call" | custom-call | flops 300000000 | bytes 2000000 | tf_op jit(solution)/shard_map/pick_rows/pallas_call | solution.py:402
  28.7 1.0 %collective-permute-start.3 = (bf16[128,1280]{1,0:T(8,128)(2,1)S(1)}, bf16[128,1280]{1,0:T(8,128)(2,1)S(1)}, u32[]{:S(2)}, u32[]{:S(2)}) collective-permute-start(bf16[128,1280]{1,0:T(8,128)(2,1)S(1)} %get-tuple-element.177.refs_0_), channel_id=1, source_target_pairs={{0,8},{1,9},{2,10},{3,11},{4,12},{5,13},{6,14},{7,15},{8,0},{9,1},... | collective-permute-start | bytes 983048 | tf_op jit(solution)/shard_map/ppermute | solution.py:378
  29.6 1.6 %collective-permute-start.4 = (bf16[128,1280]{1,0:T(8,128)(2,1)S(1)}, bf16[128,1280]{1,0:T(8,128)(2,1)S(1)}, u32[]{:S(2)}, u32[]{:S(2)}) collective-permute-start(bf16[128,1280]{1,0:T(8,128)(2,1)S(1)} %get-tuple-element.177.refs_0_), channel_id=1, source_target_pairs={{0,2},{1,3},{2,0},{3,1},{4,6},{5,7},{6,4},{7,5},{8,10},{9,11},{10,... | collective-permute-start | bytes 983048 | tf_op jit(solution)/shard_map/ppermute | solution.py:378
  31.2 1.6 %collective-permute-start.5 = (bf16[128,1280]{1,0:T(8,128)(2,1)S(1)}, bf16[128,1280]{1,0:T(8,128)(2,1)S(1)}, u32[]{:S(2)}, u32[]{:S(2)}) collective-permute-start(bf16[128,1280]{1,0:T(8,128)(2,1)S(1)} %get-tuple-element.177.refs_0_), channel_id=1, source_target_pairs={{0,4},{1,5},{2,6},{3,7},{4,0},{5,1},{6,2},{7,3},{8,12},{9,13},{10,... | collective-permute-start | bytes 983048 | tf_op jit(solution)/shard_map/ppermute | solution.py:378
  32.8 0.0 collective-permute-start.6
  32.8 16.1 %all_to_all.11 = bf16[4,4,16,256]{3,2,1,0:T(8,128)(2,1)S(1)} all-to-all(bf16[4,4,16,256]{3,2,1,0:T(8,128)(2,1)S(1)} %get-tuple-element.178), channel_id=1, replica_groups={{0,4,8,12},{1,5,9,13},{2,6,10,14},{3,7,11,15},{16,20,24,28},{17,21,25,2..., dimensions={0} | all-to-all | bytes 262144 | tf_op jit(solution)/shard_map/all_to_all | solution.py:415
  49.0 0.0 collective-permute-done.3.refs_3_
  49.0 0.0 collective-permute-done.4.refs_1_
  49.0 0.1 collective-permute-start.8
  49.1 0.5 collective-permute-start.9
  49.6 0.1 collective-permute-start.10
  49.6 0.7 collective-permute-start.11
  50.4 0.3 collective-permute-done.8.refs_5_.refs_9_
  50.7 1.0 %collective-permute-start.12 = (bf16[128,1280]{1,0:T(8,128)(2,1)S(1)}, bf16[128,1280]{1,0:T(8,128)(2,1)S(1)}, u32[]{:S(2)}, u32[]{:S(2)}) collective-permute-start(bf16[128,1280]{1,0:T(8,128)(2,1)S(1)} %collective-permute-done.3.refs_3_), channel_id=1, source_target_pairs={{0,2},{1,3},{2,0},{3,1},{4,6},{5,7},{6,4},{7,5},{8,10},{9,11},{10,... | collective-permute-start | bytes 983048 | tf_op jit(solution)/shard_map/ppermute | solution.py:378
  51.7 8.3 %half_transform.1 = (f32[512,1024]{1,0:T(8,128)S(1)}, bf16[2,512,1024]{2,1,0:T(8,128)(2,1)S(1)}) custom-call(s32[16,8,128]{2,1,0:T(8,128)S(1)} %all_to_all.10.code_ref, bf16[16,16,256]{2,1,0:T(8,128)(2,1)S(1)} %bitcast.64, s32[1,256]{1,0:T(1,128)} %bitcast.67, bf16[128,1280]{1,0:T(8,128)(2,1)S(1)} %get-tuple-element.177.refs_0_, ...), custom_call_target="tpu_custom_call" | custom-call | flops 7000000000 | bytes 1 | tf_op jit(solution)/shard_map/half_transform/pallas_call | solution.py:425
  60.0 1.1 %collective-permute-start.13 = (bf16[128,1280]{1,0:T(8,128)(2,1)S(1)}, bf16[128,1280]{1,0:T(8,128)(2,1)S(1)}, u32[]{:S(2)}, u32[]{:S(2)}) collective-permute-start(bf16[128,1280]{1,0:T(8,128)(2,1)S(1)} %collective-permute-done.7.refs_6_), channel_id=1, source_target_pairs={{0,2},{1,3},{2,0},{3,1},{4,6},{5,7},{6,4},{7,5},{8,10},{9,11},{10,... | collective-permute-start | bytes 983048 | tf_op jit(solution)/shard_map/ppermute | solution.py:378
  61.1 6.1 %collective-permute-done.12.refs_5_ = bf16[128,1280]{1,0:T(8,128)(2,1)S(1)} collective-permute-done((bf16[128,1280]{1,0:T(8,128)(2,1)S(1)}, bf16[128,1280]{1,0:T(8,128)(2,1)S(1)}, u32[]{:S(2)}, u32[]{:S(2)}) %collective-permute-start.12) | collective-permute-done | bytes 327712 | tf_op jit(solution)/shard_map/ppermute | solution.py:378
  67.2 0.5 collective-permute-start.16
  67.7 6.1 %collective-permute-done.13.refs_7_ = bf16[128,1280]{1,0:T(8,128)(2,1)S(1)} collective-permute-done((bf16[128,1280]{1,0:T(8,128)(2,1)S(1)}, bf16[128,1280]{1,0:T(8,128)(2,1)S(1)}, u32[]{:S(2)}, u32[]{:S(2)}) %collective-permute-start.13) | collective-permute-done | bytes 327712 | tf_op jit(solution)/shard_map/ppermute | solution.py:378
  73.8 0.1 collective-permute-start.17
  73.8 1.6 %collective-permute-done.17.refs_15_ = bf16[128,1280]{1,0:T(8,128)(2,1)S(1)} collective-permute-done((bf16[128,1280]{1,0:T(8,128)(2,1)S(1)}, bf16[128,1280]{1,0:T(8,128)(2,1)S(1)}, u32[]{:S(2)}, u32[]{:S(2)}) %collective-permute-start.17) | collective-permute-done | bytes 327712 | tf_op jit(solution)/shard_map/ppermute | solution.py:378
  75.4 6.8 %last_product.1 = bf16[2,256,2304]{2,1,0:T(8,128)(2,1)} custom-call(s32[1]{0:T(128)} %get-tuple-element.176.me_ref, f32[512,1024]{1,0:T(8,128)S(1)} %get-tuple-element.186.part_any, bf16[2,512,1024]{2,1,0:T(8,128)(2,1)S(1)} %get-tuple-element.187.late_any, bf16[128,1280]{1,0:T(8,128)(2,1)S(1)} %get-tuple-element.177.refs_0_, ...), custom_call_target="tpu_custom_call" | custom-call | flops 20000000000 | bytes 1 | tf_op jit(solution)/shard_map/last_product/pallas_call | solution.py:455
  82.2 0.6 while.17
  (18 shorter events, 0.0 us)
Async XLA Ops:
  6.5 0.9 %copy-start.1 = (bf16[8,32,256]{2,1,0:T(8,128)(2,1)S(1)}, bf16[8,32,256]{2,1,0:T(8,128)(2,1)}, u32[]{:S(2)}) copy-start(bf16[8,32,256]{2,1,0:T(8,128)(2,1)} %panels_ref.1) | copy-start | bytes 393220
  9.0 17.5 %collective-permute-start = (bf16[96,1280]{1,0:T(8,128)(2,1)S(1)}, bf16[96,1280]{1,0:T(8,128)(2,1)S(1)}, u32[]{:S(2)}, u32[]{:S(2)}) collective-permute-start(bf16[96,1280]{1,0:T(8,128)(2,1)S(1)} %get-tuple-element.172), channel_id=1, source_target_pairs={{0,1},{1,0},{2,3},{3,2},{4,5},{5,4},{6,7},{7,6},{8,9},{9,8},{10,11... | collective-permute-start | bytes 737288 | tf_op jit(solution)/shard_map/ppermute | solution.py:378
  9.5 17.0 %collective-permute-start.1 = (bf16[96,1280]{1,0:T(8,128)(2,1)S(1)}, bf16[96,1280]{1,0:T(8,128)(2,1)S(1)}, u32[]{:S(2)}, u32[]{:S(2)}) collective-permute-start(bf16[96,1280]{1,0:T(8,128)(2,1)S(1)} %get-tuple-element.173), channel_id=1, source_target_pairs={{0,2},{1,3},{2,0},{3,1},{4,6},{5,7},{6,4},{7,5},{8,10},{9,11},{10,... | collective-permute-start | bytes 737288 | tf_op jit(solution)/shard_map/ppermute | solution.py:378
  12.1 14.4 %collective-permute-start.2 = (bf16[96,1280]{1,0:T(8,128)(2,1)S(1)}, bf16[96,1280]{1,0:T(8,128)(2,1)S(1)}, u32[]{:S(2)}, u32[]{:S(2)}) collective-permute-start(bf16[96,1280]{1,0:T(8,128)(2,1)S(1)} %get-tuple-element.174), channel_id=1, source_target_pairs={{0,3},{1,2},{2,1},{3,0},{4,7},{5,6},{6,5},{7,4},{8,11},{9,10},{10,... | collective-permute-start | bytes 737288 | tf_op jit(solution)/shard_map/ppermute | solution.py:378
  12.9 0.7 copy-start
  28.7 20.3 %collective-permute-start.3 = (bf16[128,1280]{1,0:T(8,128)(2,1)S(1)}, bf16[128,1280]{1,0:T(8,128)(2,1)S(1)}, u32[]{:S(2)}, u32[]{:S(2)}) collective-permute-start(bf16[128,1280]{1,0:T(8,128)(2,1)S(1)} %get-tuple-element.177.refs_0_), channel_id=1, source_target_pairs={{0,8},{1,9},{2,10},{3,11},{4,12},{5,13},{6,14},{7,15},{8,0},{9,1},... | collective-permute-start | bytes 983048 | tf_op jit(solution)/shard_map/ppermute | solution.py:378
  29.6 19.3 %collective-permute-start.4 = (bf16[128,1280]{1,0:T(8,128)(2,1)S(1)}, bf16[128,1280]{1,0:T(8,128)(2,1)S(1)}, u32[]{:S(2)}, u32[]{:S(2)}) collective-permute-start(bf16[128,1280]{1,0:T(8,128)(2,1)S(1)} %get-tuple-element.177.refs_0_), channel_id=1, source_target_pairs={{0,2},{1,3},{2,0},{3,1},{4,6},{5,7},{6,4},{7,5},{8,10},{9,11},{10,... | collective-permute-start | bytes 983048 | tf_op jit(solution)/shard_map/ppermute | solution.py:378
  31.2 17.7 %collective-permute-start.5 = (bf16[128,1280]{1,0:T(8,128)(2,1)S(1)}, bf16[128,1280]{1,0:T(8,128)(2,1)S(1)}, u32[]{:S(2)}, u32[]{:S(2)}) collective-permute-start(bf16[128,1280]{1,0:T(8,128)(2,1)S(1)} %get-tuple-element.177.refs_0_), channel_id=1, source_target_pairs={{0,4},{1,5},{2,6},{3,7},{4,0},{5,1},{6,2},{7,3},{8,12},{9,13},{10,... | collective-permute-start | bytes 983048 | tf_op jit(solution)/shard_map/ppermute | solution.py:378
  32.8 16.2 %collective-permute-start.6 = (bf16[128,1280]{1,0:T(8,128)(2,1)S(1)}, bf16[128,1280]{1,0:T(8,128)(2,1)S(1)}, u32[]{:S(2)}, u32[]{:S(2)}) collective-permute-start(bf16[128,1280]{1,0:T(8,128)(2,1)S(1)} %get-tuple-element.177.refs_0_), channel_id=1, source_target_pairs={{0,1},{1,0},{2,3},{3,2},{4,5},{5,4},{6,7},{7,6},{8,9},{9,8},{10,11... | collective-permute-start | bytes 983048 | tf_op jit(solution)/shard_map/ppermute | solution.py:378
  49.0 1.7 %collective-permute-start.8 = (bf16[128,1280]{1,0:T(8,128)(2,1)S(1)}, bf16[128,1280]{1,0:T(8,128)(2,1)S(1)}, u32[]{:S(2)}, u32[]{:S(2)}) collective-permute-start(bf16[128,1280]{1,0:T(8,128)(2,1)S(1)} %collective-permute-done.4.refs_1_), channel_id=1, source_target_pairs={{0,1},{1,0},{2,3},{3,2},{4,5},{5,4},{6,7},{7,6},{8,9},{9,8},{10,11... | collective-permute-start | bytes 983048 | tf_op jit(solution)/shard_map/ppermute | solution.py:378
  49.1 2.6 %collective-permute-start.9 = (bf16[128,1280]{1,0:T(8,128)(2,1)S(1)}, bf16[128,1280]{1,0:T(8,128)(2,1)S(1)}, u32[]{:S(2)}, u32[]{:S(2)}) collective-permute-start(bf16[128,1280]{1,0:T(8,128)(2,1)S(1)} %collective-permute-done.5.refs_2_), channel_id=1, source_target_pairs={{0,1},{1,0},{2,3},{3,2},{4,5},{5,4},{6,7},{7,6},{8,9},{9,8},{10,11... | collective-permute-start | bytes 983048 | tf_op jit(solution)/shard_map/ppermute | solution.py:378
  49.6 2.1 %collective-permute-start.10 = (bf16[128,1280]{1,0:T(8,128)(2,1)S(1)}, bf16[128,1280]{1,0:T(8,128)(2,1)S(1)}, u32[]{:S(2)}, u32[]{:S(2)}) collective-permute-start(bf16[128,1280]{1,0:T(8,128)(2,1)S(1)} %collective-permute-done.3.refs_3_), channel_id=1, source_target_pairs={{0,1},{1,0},{2,3},{3,2},{4,5},{5,4},{6,7},{7,6},{8,9},{9,8},{10,11... | collective-permute-start | bytes 983048 | tf_op jit(solution)/shard_map/ppermute | solution.py:378
  49.6 10.4 %collective-permute-start.7 = (bf16[128,1280]{1,0:T(8,128)(2,1)S(1)}, bf16[128,1280]{1,0:T(8,128)(2,1)S(1)}, u32[]{:S(2)}, u32[]{:S(2)}) collective-permute-start(bf16[128,1280]{1,0:T(8,128)(2,1)S(1)} %collective-permute-done.3.refs_3_), channel_id=1, source_target_pairs={{0,4},{1,5},{2,6},{3,7},{4,0},{5,1},{6,2},{7,3},{8,12},{9,13},{10,... | collective-permute-start | bytes 983048 | tf_op jit(solution)/shard_map/ppermute | solution.py:378
  49.6 11.5 %collective-permute-start.11 = (bf16[128,1280]{1,0:T(8,128)(2,1)S(1)}, bf16[128,1280]{1,0:T(8,128)(2,1)S(1)}, u32[]{:S(2)}, u32[]{:S(2)}) collective-permute-start(bf16[128,1280]{1,0:T(8,128)(2,1)S(1)} %collective-permute-done.5.refs_2_), channel_id=1, source_target_pairs={{0,2},{1,3},{2,0},{3,1},{4,6},{5,7},{6,4},{7,5},{8,10},{9,11},{10,... | collective-permute-start | bytes 983048 | tf_op jit(solution)/shard_map/ppermute | solution.py:378
  50.7 16.5 %collective-permute-start.12 = (bf16[128,1280]{1,0:T(8,128)(2,1)S(1)}, bf16[128,1280]{1,0:T(8,128)(2,1)S(1)}, u32[]{:S(2)}, u32[]{:S(2)}) collective-permute-start(bf16[128,1280]{1,0:T(8,128)(2,1)S(1)} %collective-permute-done.3.refs_3_), channel_id=1, source_target_pairs={{0,2},{1,3},{2,0},{3,1},{4,6},{5,7},{6,4},{7,5},{8,10},{9,11},{10,... | collective-permute-start | bytes 983048 | tf_op jit(solution)/shard_map/ppermute | solution.py:378
  60.0 13.7 %collective-permute-start.13 = (bf16[128,1280]{1,0:T(8,128)(2,1)S(1)}, bf16[128,1280]{1,0:T(8,128)(2,1)S(1)}, u32[]{:S(2)}, u32[]{:S(2)}) collective-permute-start(bf16[128,1280]{1,0:T(8,128)(2,1)S(1)} %collective-permute-done.7.refs_6_), channel_id=1, source_target_pairs={{0,2},{1,3},{2,0},{3,1},{4,6},{5,7},{6,4},{7,5},{8,10},{9,11},{10,... | collective-permute-start | bytes 983048 | tf_op jit(solution)/shard_map/ppermute | solution.py:378
  61.1 12.6 %collective-permute-start.14 = (bf16[128,1280]{1,0:T(8,128)(2,1)S(1)}, bf16[128,1280]{1,0:T(8,128)(2,1)S(1)}, u32[]{:S(2)}, u32[]{:S(2)}) collective-permute-start(bf16[128,1280]{1,0:T(8,128)(2,1)S(1)} %collective-permute-done.11.refs_4_), channel_id=1, source_target_pairs={{0,1},{1,0},{2,3},{3,2},{4,5},{5,4},{6,7},{7,6},{8,9},{9,8},{10,11... | collective-permute-start | bytes 983048 | tf_op jit(solution)/shard_map/ppermute | solution.py:378
  67.2 6.6 %collective-permute-start.15 = (bf16[128,1280]{1,0:T(8,128)(2,1)S(1)}, bf16[128,1280]{1,0:T(8,128)(2,1)S(1)}, u32[]{:S(2)}, u32[]{:S(2)}) collective-permute-start(bf16[128,1280]{1,0:T(8,128)(2,1)S(1)} %collective-permute-done.12.refs_5_), channel_id=1, source_target_pairs={{0,1},{1,0},{2,3},{3,2},{4,5},{5,4},{6,7},{7,6},{8,9},{9,8},{10,11... | collective-permute-start | bytes 983048 | tf_op jit(solution)/shard_map/ppermute | solution.py:378
  67.2 6.6 %collective-permute-start.16 = (bf16[128,1280]{1,0:T(8,128)(2,1)S(1)}, bf16[128,1280]{1,0:T(8,128)(2,1)S(1)}, u32[]{:S(2)}, u32[]{:S(2)}) collective-permute-start(bf16[128,1280]{1,0:T(8,128)(2,1)S(1)} %collective-permute-done.7.refs_6_), channel_id=1, source_target_pairs={{0,1},{1,0},{2,3},{3,2},{4,5},{5,4},{6,7},{7,6},{8,9},{9,8},{10,11... | collective-permute-start | bytes 983048 | tf_op jit(solution)/shard_map/ppermute | solution.py:378
  73.8 1.7 %collective-permute-start.17 = (bf16[128,1280]{1,0:T(8,128)(2,1)S(1)}, bf16[128,1280]{1,0:T(8,128)(2,1)S(1)}, u32[]{:S(2)}, u32[]{:S(2)}) collective-permute-start(bf16[128,1280]{1,0:T(8,128)(2,1)S(1)} %collective-permute-done.13.refs_7_), channel_id=1, source_target_pairs={{0,1},{1,0},{2,3},{3,2},{4,5},{5,4},{6,7},{7,6},{8,9},{9,8},{10,11... | collective-permute-start | bytes 983048 | tf_op jit(solution)/shard_map/ppermute | solution.py:378
  75.4 6.8 %copy-start.3 = (s32[256]{0:T(256)S(1)}, s32[256]{0:T(256)}, u32[]{:S(2)}) copy-start(s32[256]{0:T(256)} %param.11) | copy-start | bytes 3076

commit v19 on v15

--- a/solution.py
+++ b/solution.py
@@ -414,16 +414,15 @@
         name="pick_rows",
     )(code, size_row, keep, to_core, to_y, to_both)
 
-    beside, mine_y, far = swap(mine, 4), swap(mine, 2), [swap(mine, 1)]
-    mine, far[0] = lax.optimization_barrier((mine, far[0]))
-    across = swap(mine, 8)
-    beside, mine_y = lax.optimization_barrier((beside, mine_y))
+    beside, mine_y, across = swap(mine, 4), swap(mine, 2), swap(mine, 8)
+    far = [swap(mine, 1)]
+    beside, mine_y, *panel = lax.optimization_barrier((beside, mine_y, *panel))
 
     beside_y = swap(beside, 2)
+    panel = [panel[0]] + [swap(panel[r], 4 * r) for r in range(1, Z)]
     far += [swap(mine_y, 1), swap(beside, 1)]
-    *panel, far[1], far[2] = lax.optimization_barrier((*panel, far[1], far[2]))
-    panel = [panel[0]] + [swap(panel[r], 4 * r) for r in range(1, Z)]
-    across, beside_y, *panel = lax.optimization_barrier((across, beside_y, *panel))
+    across, beside_y, *rest = lax.optimization_barrier((across, beside_y, *panel, *far))
+    panel, far = rest[:Z], rest[Z:]
 
     corner, across_y = swap(across, 4), swap(across, 2)
     near = [mine, mine_y, beside]

time: 96.5 us -> 93.7 us (0.971)
  waiting for transfers between devices: 29.8 us -> 26.8 us
    ppermute x21, waiting for transfers between devices: 29.8 us -> 26.8 us  [swap(): return lax.ppermute(array, 'shell', [(i, i ^ bit) for i in range(n)])]
  transfers between devices with their start and end apart: 21 -> 21, of which waited for: 6 -> 6; matrix products, arithmetic and copies ran while one was open for 0% -> 0% of each run, Pallas kernels for 9% -> 10%
where the time goes in v19:
time: 93.7 us; the launch traced here: 93.4 us
  waiting for transfers between devices  26.8 us (29%)
  Pallas kernels  20.1 us (21%)
  starting transfers between devices  17.4 us (19%)
  between operations  14.1 us (15%)
  blocking collectives  12.8 us (14%)
  local copies, waits for them, and re-layouts  1.58 us (2%)
    ppermute x21, waiting for transfers between devices, swap(): return lax.ppermute(array, 'shell', [(i, i ^ bit) for i in range(n)])  26.8 us
    ppermute x21, starting transfers between devices, swap(): return lax.ppermute(array, 'shell', [(i, i ^ bit) for i in range(n)])  17.4 us
    all_to_all x1, blocking collectives, short_way(): lax.all_to_all(code, 'shell', split_axis=0, concat_axis=0, tiled=True)  12.8 us
    pallas_call x1, Pallas kernels, short_way(): pl.pallas_call(functools.partial(half_kernel, here, early), out_shape=(sh...  8.79 us
    pallas_call x1, Pallas kernels, short_way(): pl.pallas_call(functools.partial(last_kernel, count, early), out_shape=sh...  7.38 us
    pallas_call x1, Pallas kernels, short_way(): pl.pallas_call(functools.partial(pick_kernel, here), out_shape=[shape(CAP...  2.16 us
  transfers between devices with their start and end apart: 21, of which 6 were waited for; matrix products, arithmetic and copies ran while one was open for 0% of the time, Pallas kernels for 10%

profile of v19, /device:TPU:0, one launch (start us, length us, event | category | flops | bytes accessed | tf_op | source)
XLA Modules:
  0.0 93.4 jit_solution(8471393944360723574)
XLA Ops:
  6.5 0.9 copy-done.1
  7.4 1.6 %pack_rows.1 = (bf16[96,1280]{1,0:T(8,128)(2,1)S(1)}, bf16[96,1280]{1,0:T(8,128)(2,1)S(1)}, bf16[96,1280]{1,0:T(8,128)(2,1)S(1)}, bf16[96,1280]{1,0:T(8,128)(2,1)S(1)}) custom-call(bf16[160,2304]{1,0:T(8,128)(2,1)} %vir_ref.1, bf16[160,256]{1,0:T(8,128)(2,1)} %occ_ref.1, bf16[8,32,256]{2,1,0:T(8,128)(2,1)S(1)} %copy-done.1), custom_call_target="tpu_custom_call" | custom-call | flops 300000000 | bytes 3000000 | tf_op jit(solution)/shard_map/pack_rows/pallas_call | solution.py:384
  9.0 0.5 collective-permute-start
  9.5 2.6 %collective-permute-start.1 = (bf16[96,1280]{1,0:T(8,128)(2,1)S(1)}, bf16[96,1280]{1,0:T(8,128)(2,1)S(1)}, u32[]{:S(2)}, u32[]{:S(2)}) collective-permute-start(bf16[96,1280]{1,0:T(8,128)(2,1)S(1)} %get-tuple-element.250), channel_id=1, source_target_pairs={{0,2},{1,3},{2,0},{3,1},{4,6},{5,7},{6,4},{7,5},{8,10},{9,11},{10,... | collective-permute-start | bytes 737288 | tf_op jit(solution)/shard_map/ppermute | solution.py:382
  12.1 0.1 collective-permute-start.2
  12.9 0.0 copy-start
  12.9 0.7 copy-done
  13.5 0.2 pack_ids.1
  13.7 12.8 %all_to_all.5.code_ref = s32[16,8,128]{2,1,0:T(8,128)S(1)} all-to-all(s32[16,8,128]{2,1,0:T(8,128)S(1)} %pack_ids.1), channel_id=1, replica_groups=mesh['groups'=2,'shell'=16] {'shell'}, dimensions={0} | all-to-all | bytes 131072 | tf_op jit(solution)/shard_map/all_to_all | solution.py:404
  26.5 0.0 collective-permute-done.refs_1_
  26.5 2.2 %pick_rows.1 = (bf16[128,1280]{1,0:T(8,128)(2,1)S(1)}, s32[1]{0:T(128)}, s32[1]{0:T(128)}, bf16[4,16,256]{2,1,0:T(8,128)(2,1)S(1)}, bf16[4,16,256]{2,1,0:T(8,128...) custom-call(s32[16,8,128]{2,1,0:T(8,128)S(1)} %all_to_all.5.code_ref, s32[1,256]{1,0:T(1,128)} %bitcast.87, ...), custom_call_target="tpu_custom_call" | custom-call | flops 300000000 | bytes 2000000 | tf_op jit(solution)/shard_map/pick_rows/pallas_call | solution.py:406
  28.7 0.2 collective-permute-start.4
  28.9 1.3 %collective-permute-start.5 = (bf16[128,1280]{1,0:T(8,128)(2,1)S(1)}, bf16[128,1280]{1,0:T(8,128)(2,1)S(1)}, u32[]{:S(2)}, u32[]{:S(2)}) collective-permute-start(bf16[128,1280]{1,0:T(8,128)(2,1)S(1)} %get-tuple-element.254.refs_4_.refs_0_), channel_id=1, source_target_pairs={{0,2},{1,3},{2,0},{3,1},{4,6},{5,7},{6,4},{7,5},{8,10},{9,11},{10,... | collective-permute-start | bytes 983048 | tf_op jit(solution)/shard_map/ppermute | solution.py:382
  30.2 2.6 %collective-permute-start.3 = (bf16[128,1280]{1,0:T(8,128)(2,1)S(1)}, bf16[128,1280]{1,0:T(8,128)(2,1)S(1)}, u32[]{:S(2)}, u32[]{:S(2)}) collective-permute-start(bf16[128,1280]{1,0:T(8,128)(2,1)S(1)} %get-tuple-element.254.refs_4_.refs_0_), channel_id=1, source_target_pairs={{0,8},{1,9},{2,10},{3,11},{4,12},{5,13},{6,14},{7,15},{8,0},{9,1},... | collective-permute-start | bytes 983048 | tf_op jit(solution)/shard_map/ppermute | solution.py:382
  32.8 11.1 %collective-permute-done.4.refs_6_.refs_2_ = bf16[128,1280]{1,0:T(8,128)(2,1)S(1)} collective-permute-done((bf16[128,1280]{1,0:T(8,128)(2,1)S(1)}, bf16[128,1280]{1,0:T(8,128)(2,1)S(1)}, u32[]{:S(2)}, u32[]{:S(2)}) %collective-permute-start.4) | collective-permute-done | bytes 327712 | tf_op jit(solution)/shard_map/ppermute | solution.py:382
  43.9 0.9 collective-permute-start.6
  44.8 0.5 collective-permute-start.12
  45.3 1.7 %collective-permute-done.3.refs_3_ = bf16[128,1280]{1,0:T(8,128)(2,1)S(1)} collective-permute-done((bf16[128,1280]{1,0:T(8,128)(2,1)S(1)}, bf16[128,1280]{1,0:T(8,128)(2,1)S(1)}, u32[]{:S(2)}, u32[]{:S(2)}) %collective-permute-start.3) | collective-permute-done | bytes 327712 | tf_op jit(solution)/shard_map/ppermute | solution.py:382
  47.0 3.0 %collective-permute-start.8 = (bf16[4,16,256]{2,1,0:T(8,128)(2,1)S(1)}, bf16[4,16,256]{2,1,0:T(8,128)(2,1)S(1)}, u32[]{:S(2)}, u32[]{:S(2)}) collective-permute-start(bf16[4,16,256]{2,1,0:T(8,128)(2,1)S(1)} %get-tuple-element.262), channel_id=1, source_target_pairs={{0,8},{1,9},{2,10},{3,11},{4,12},{5,13},{6,14},{7,15},{8,0},{9,1},... | collective-permute-start | bytes 98312 | tf_op jit(solution)/shard_map/ppermute | solution.py:382
  50.1 0.9 collective-permute-done.7.refs_1_
  50.9 2.5 %collective-permute-start.9 = (bf16[4,16,256]{2,1,0:T(8,128)(2,1)S(1)}, bf16[4,16,256]{2,1,0:T(8,128)(2,1)S(1)}, u32[]{:S(2)}, u32[]{:S(2)}) collective-permute-start(bf16[4,16,256]{2,1,0:T(8,128)(2,1)S(1)} %get-tuple-element.263), channel_id=1, source_target_pairs={{0,12},{1,13},{2,14},{3,15},{4,8},{5,9},{6,10},{7,11},{8,4},{9,5},... | collective-permute-start | bytes 98312 | tf_op jit(solution)/shard_map/ppermute | solution.py:382
  53.4 3.3 %collective-permute-done.9.refs_3_ = bf16[4,16,256]{2,1,0:T(8,128)(2,1)S(1)} collective-permute-done((bf16[4,16,256]{2,1,0:T(8,128)(2,1)S(1)}, bf16[4,16,256]{2,1,0:T(8,128)(2,1)S(1)}, u32[]{:S(2)}, u32[]{:S(2)}) %collective-permute-start.9) | collective-permute-done | bytes 32800 | tf_op jit(solution)/shard_map/ppermute | solution.py:382
  56.8 0.1 collective-permute-start.13
  56.9 1.1 %collective-permute-start.14 = (bf16[128,1280]{1,0:T(8,128)(2,1)S(1)}, bf16[128,1280]{1,0:T(8,128)(2,1)S(1)}, u32[]{:S(2)}, u32[]{:S(2)}) collective-permute-start(bf16[128,1280]{1,0:T(8,128)(2,1)S(1)} %collective-permute-done.3.refs_3_), channel_id=1, source_target_pairs={{0,2},{1,3},{2,0},{3,1},{4,6},{5,7},{6,4},{7,5},{8,10},{9,11},{10,... | collective-permute-start | bytes 983048 | tf_op jit(solution)/shard_map/ppermute | solution.py:382
  58.0 0.5 collective-permute-start.17
  58.5 8.8 %half_transform.1 = (f32[512,1024]{1,0:T(8,128)S(1)}, bf16[2,640,1024]{2,1,0:T(8,128)(2,1)S(1)}) custom-call(s32[16,8,128]{2,1,0:T(8,128)S(1)} %all_to_all.5.code_ref, s32[1,256]{1,0:T(1,128)} %bitcast.88, bf16[4,16,256]{2,1,0:T(8,128)(2,1)S(1)} %get-tuple-element.417.refs_0_, bf16[4,16,256]{2,1,0:T(8,128)(2,1)S(1)} %collective-permute-done.7.refs_1_, ...), custom_call_target="tpu_custom_call" | custom-call | flops 7000000000 | bytes 1 | tf_op jit(solution)/shard_map/half_transform/pallas_call | solution.py:431
  67.3 1.1 %collective-permute-start.15 = (bf16[128,1280]{1,0:T(8,128)(2,1)S(1)}, bf16[128,1280]{1,0:T(8,128)(2,1)S(1)}, u32[]{:S(2)}, u32[]{:S(2)}) collective-permute-start(bf16[128,1280]{1,0:T(8,128)(2,1)S(1)} %collective-permute-done.13.refs_6_), channel_id=1, source_target_pairs={{0,2},{1,3},{2,0},{3,1},{4,6},{5,7},{6,4},{7,5},{8,10},{9,11},{10,... | collective-permute-start | bytes 983048 | tf_op jit(solution)/shard_map/ppermute | solution.py:382
  68.4 0.5 collective-permute-start.19
  68.9 8.1 %collective-permute-done.15.refs_7_ = bf16[128,1280]{1,0:T(8,128)(2,1)S(1)} collective-permute-done((bf16[128,1280]{1,0:T(8,128)(2,1)S(1)}, bf16[128,1280]{1,0:T(8,128)(2,1)S(1)}, u32[]{:S(2)}, u32[]{:S(2)}) %collective-permute-start.15) | collective-permute-done | bytes 327712 | tf_op jit(solution)/shard_map/ppermute | solution.py:382
  77.0 1.6 %collective-permute-done.20.refs_15_ = bf16[128,1280]{1,0:T(8,128)(2,1)S(1)} collective-permute-done((bf16[128,1280]{1,0:T(8,128)(2,1)S(1)}, bf16[128,1280]{1,0:T(8,128)(2,1)S(1)}, u32[]{:S(2)}, u32[]{:S(2)}) %collective-permute-start.20) | collective-permute-done | bytes 327712 | tf_op jit(solution)/shard_map/ppermute | solution.py:382
  78.6 7.4 %last_product.1 = bf16[2,256,2304]{2,1,0:T(8,128)(2,1)} custom-call(s32[1]{0:T(128)} %get-tuple-element.416.me_ref, f32[512,1024]{1,0:T(8,128)S(1)} %get-tuple-element.275.part_any, bf16[2,640,1024]{2,1,0:T(8,128)(2,1)S(1)} %get-tuple-element.276.late_any, bf16[128,1280]{1,0:T(8,128)(2,1)S(1)} %get-tuple-element.254.refs_4_.refs_0_, ...), custom_call_target="tpu_custom_call" | custom-call | flops 20000000000 | bytes 1 | tf_op jit(solution)/shard_map/last_product/pallas_call | solution.py:462
  86.0 0.6 while.17
  (23 shorter events, 0.1 us)
Async XLA Ops:
  6.5 0.9 copy-start.1
  9.0 17.5 %collective-permute-start = (bf16[96,1280]{1,0:T(8,128)(2,1)S(1)}, bf16[96,1280]{1,0:T(8,128)(2,1)S(1)}, u32[]{:S(2)}, u32[]{:S(2)}) collective-permute-start(bf16[96,1280]{1,0:T(8,128)(2,1)S(1)} %get-tuple-element.249), channel_id=1, source_target_pairs={{0,1},{1,0},{2,3},{3,2},{4,5},{5,4},{6,7},{7,6},{8,9},{9,8},{10,11... | collective-permute-start | bytes 737288 | tf_op jit(solution)/shard_map/ppermute | solution.py:382
  9.5 17.0 %collective-permute-start.1 = (bf16[96,1280]{1,0:T(8,128)(2,1)S(1)}, bf16[96,1280]{1,0:T(8,128)(2,1)S(1)}, u32[]{:S(2)}, u32[]{:S(2)}) collective-permute-start(bf16[96,1280]{1,0:T(8,128)(2,1)S(1)} %get-tuple-element.250), channel_id=1, source_target_pairs={{0,2},{1,3},{2,0},{3,1},{4,6},{5,7},{6,4},{7,5},{8,10},{9,11},{10,... | collective-permute-start | bytes 737288 | tf_op jit(solution)/shard_map/ppermute | solution.py:382
  12.1 14.4 %collective-permute-start.2 = (bf16[96,1280]{1,0:T(8,128)(2,1)S(1)}, bf16[96,1280]{1,0:T(8,128)(2,1)S(1)}, u32[]{:S(2)}, u32[]{:S(2)}) collective-permute-start(bf16[96,1280]{1,0:T(8,128)(2,1)S(1)} %get-tuple-element.251), channel_id=1, source_target_pairs={{0,3},{1,2},{2,1},{3,0},{4,7},{5,6},{6,5},{7,4},{8,11},{9,10},{10,... | collective-permute-start | bytes 737288 | tf_op jit(solution)/shard_map/ppermute | solution.py:382
  12.9 0.7 copy-start
  28.7 15.2 %collective-permute-start.4 = (bf16[128,1280]{1,0:T(8,128)(2,1)S(1)}, bf16[128,1280]{1,0:T(8,128)(2,1)S(1)}, u32[]{:S(2)}, u32[]{:S(2)}) collective-permute-start(bf16[128,1280]{1,0:T(8,128)(2,1)S(1)} %get-tuple-element.254.refs_4_.refs_0_), channel_id=1, source_target_pairs={{0,4},{1,5},{2,6},{3,7},{4,0},{5,1},{6,2},{7,3},{8,12},{9,13},{10,... | collective-permute-start | bytes 983048 | tf_op jit(solution)/shard_map/ppermute | solution.py:382
  28.9 15.0 %collective-permute-start.5 = (bf16[128,1280]{1,0:T(8,128)(2,1)S(1)}, bf16[128,1280]{1,0:T(8,128)(2,1)S(1)}, u32[]{:S(2)}, u32[]{:S(2)}) collective-permute-start(bf16[128,1280]{1,0:T(8,128)(2,1)S(1)} %get-tuple-element.254.refs_4_.refs_0_), channel_id=1, source_target_pairs={{0,2},{1,3},{2,0},{3,1},{4,6},{5,7},{6,4},{7,5},{8,10},{9,11},{10,... | collective-permute-start | bytes 983048 | tf_op jit(solution)/shard_map/ppermute | solution.py:382
  30.2 16.8 %collective-permute-start.3 = (bf16[128,1280]{1,0:T(8,128)(2,1)S(1)}, bf16[128,1280]{1,0:T(8,128)(2,1)S(1)}, u32[]{:S(2)}, u32[]{:S(2)}) collective-permute-start(bf16[128,1280]{1,0:T(8,128)(2,1)S(1)} %get-tuple-element.254.refs_4_.refs_0_), channel_id=1, source_target_pairs={{0,8},{1,9},{2,10},{3,11},{4,12},{5,13},{6,14},{7,15},{8,0},{9,1},... | collective-permute-start | bytes 983048 | tf_op jit(solution)/shard_map/ppermute | solution.py:382
  32.8 14.2 %collective-permute-start.10 = (bf16[128,1280]{1,0:T(8,128)(2,1)S(1)}, bf16[128,1280]{1,0:T(8,128)(2,1)S(1)}, u32[]{:S(2)}, u32[]{:S(2)}) collective-permute-start(bf16[128,1280]{1,0:T(8,128)(2,1)S(1)} %get-tuple-element.254.refs_4_.refs_0_), channel_id=1, source_target_pairs={{0,1},{1,0},{2,3},{3,2},{4,5},{5,4},{6,7},{7,6},{8,9},{9,8},{10,11... | collective-permute-start | bytes 983048 | tf_op jit(solution)/shard_map/ppermute | solution.py:382
  43.9 12.9 %collective-permute-start.6 = (bf16[128,1280]{1,0:T(8,128)(2,1)S(1)}, bf16[128,1280]{1,0:T(8,128)(2,1)S(1)}, u32[]{:S(2)}, u32[]{:S(2)}) collective-permute-start(bf16[128,1280]{1,0:T(8,128)(2,1)S(1)} %collective-permute-done.4.refs_6_.refs_2_), channel_id=1, source_target_pairs={{0,2},{1,3},{2,0},{3,1},{4,6},{5,7},{6,4},{7,5},{8,10},{9,11},{10,... | collective-permute-start | bytes 983048 | tf_op jit(solution)/shard_map/ppermute | solution.py:382
  44.8 12.0 %collective-permute-start.11 = (bf16[128,1280]{1,0:T(8,128)(2,1)S(1)}, bf16[128,1280]{1,0:T(8,128)(2,1)S(1)}, u32[]{:S(2)}, u32[]{:S(2)}) collective-permute-start(bf16[128,1280]{1,0:T(8,128)(2,1)S(1)} %collective-permute-done.5.refs_5_.refs_1_), channel_id=1, source_target_pairs={{0,1},{1,0},{2,3},{3,2},{4,5},{5,4},{6,7},{7,6},{8,9},{9,8},{10,11... | collective-permute-start | bytes 983048 | tf_op jit(solution)/shard_map/ppermute | solution.py:382
  44.8 12.0 %collective-permute-start.12 = (bf16[128,1280]{1,0:T(8,128)(2,1)S(1)}, bf16[128,1280]{1,0:T(8,128)(2,1)S(1)}, u32[]{:S(2)}, u32[]{:S(2)}) collective-permute-start(bf16[128,1280]{1,0:T(8,128)(2,1)S(1)} %collective-permute-done.4.refs_6_.refs_2_), channel_id=1, source_target_pairs={{0,1},{1,0},{2,3},{3,2},{4,5},{5,4},{6,7},{7,6},{8,9},{9,8},{10,11... | collective-permute-start | bytes 983048 | tf_op jit(solution)/shard_map/ppermute | solution.py:382
  47.0 3.9 %collective-permute-start.7 = (bf16[4,16,256]{2,1,0:T(8,128)(2,1)S(1)}, bf16[4,16,256]{2,1,0:T(8,128)(2,1)S(1)}, u32[]{:S(2)}, u32[]{:S(2)}) collective-permute-start(bf16[4,16,256]{2,1,0:T(8,128)(2,1)S(1)} %get-tuple-element.261), channel_id=1, source_target_pairs={{0,4},{1,5},{2,6},{3,7},{4,0},{5,1},{6,2},{7,3},{8,12},{9,13},{10,... | collective-permute-start | bytes 98312 | tf_op jit(solution)/shard_map/ppermute | solution.py:382
  47.0 6.4 %collective-permute-start.8 = (bf16[4,16,256]{2,1,0:T(8,128)(2,1)S(1)}, bf16[4,16,256]{2,1,0:T(8,128)(2,1)S(1)}, u32[]{:S(2)}, u32[]{:S(2)}) collective-permute-start(bf16[4,16,256]{2,1,0:T(8,128)(2,1)S(1)} %get-tuple-element.262), channel_id=1, source_target_pairs={{0,8},{1,9},{2,10},{3,11},{4,12},{5,13},{6,14},{7,15},{8,0},{9,1},... | collective-permute-start | bytes 98312 | tf_op jit(solution)/shard_map/ppermute | solution.py:382
  50.9 5.8 %collective-permute-start.9 = (bf16[4,16,256]{2,1,0:T(8,128)(2,1)S(1)}, bf16[4,16,256]{2,1,0:T(8,128)(2,1)S(1)}, u32[]{:S(2)}, u32[]{:S(2)}) collective-permute-start(bf16[4,16,256]{2,1,0:T(8,128)(2,1)S(1)} %get-tuple-element.263), channel_id=1, source_target_pairs={{0,12},{1,13},{2,14},{3,15},{4,8},{5,9},{6,10},{7,11},{8,4},{9,5},... | collective-permute-start | bytes 98312 | tf_op jit(solution)/shard_map/ppermute | solution.py:382
  56.8 10.5 %collective-permute-start.13 = (bf16[128,1280]{1,0:T(8,128)(2,1)S(1)}, bf16[128,1280]{1,0:T(8,128)(2,1)S(1)}, u32[]{:S(2)}, u32[]{:S(2)}) collective-permute-start(bf16[128,1280]{1,0:T(8,128)(2,1)S(1)} %collective-permute-done.3.refs_3_), channel_id=1, source_target_pairs={{0,4},{1,5},{2,6},{3,7},{4,0},{5,1},{6,2},{7,3},{8,12},{9,13},{10,... | collective-permute-start | bytes 983048 | tf_op jit(solution)/shard_map/ppermute | solution.py:382
  56.9 11.5 %collective-permute-start.14 = (bf16[128,1280]{1,0:T(8,128)(2,1)S(1)}, bf16[128,1280]{1,0:T(8,128)(2,1)S(1)}, u32[]{:S(2)}, u32[]{:S(2)}) collective-permute-start(bf16[128,1280]{1,0:T(8,128)(2,1)S(1)} %collective-permute-done.3.refs_3_), channel_id=1, source_target_pairs={{0,2},{1,3},{2,0},{3,1},{4,6},{5,7},{6,4},{7,5},{8,10},{9,11},{10,... | collective-permute-start | bytes 983048 | tf_op jit(solution)/shard_map/ppermute | solution.py:382
  58.0 10.9 %collective-permute-start.16 = (bf16[128,1280]{1,0:T(8,128)(2,1)S(1)}, bf16[128,1280]{1,0:T(8,128)(2,1)S(1)}, u32[]{:S(2)}, u32[]{:S(2)}) collective-permute-start(bf16[128,1280]{1,0:T(8,128)(2,1)S(1)} %collective-permute-done.3.refs_3_), channel_id=1, source_target_pairs={{0,1},{1,0},{2,3},{3,2},{4,5},{5,4},{6,7},{7,6},{8,9},{9,8},{10,11... | collective-permute-start | bytes 983048 | tf_op jit(solution)/shard_map/ppermute | solution.py:382
  58.0 10.9 %collective-permute-start.17 = (bf16[128,1280]{1,0:T(8,128)(2,1)S(1)}, bf16[128,1280]{1,0:T(8,128)(2,1)S(1)}, u32[]{:S(2)}, u32[]{:S(2)}) collective-permute-start(bf16[128,1280]{1,0:T(8,128)(2,1)S(1)} %collective-permute-done.6.refs_4_), channel_id=1, source_target_pairs={{0,1},{1,0},{2,3},{3,2},{4,5},{5,4},{6,7},{7,6},{8,9},{9,8},{10,11... | collective-permute-start | bytes 983048 | tf_op jit(solution)/shard_map/ppermute | solution.py:382
  67.3 9.7 %collective-permute-start.15 = (bf16[128,1280]{1,0:T(8,128)(2,1)S(1)}, bf16[128,1280]{1,0:T(8,128)(2,1)S(1)}, u32[]{:S(2)}, u32[]{:S(2)}) collective-permute-start(bf16[128,1280]{1,0:T(8,128)(2,1)S(1)} %collective-permute-done.13.refs_6_), channel_id=1, source_target_pairs={{0,2},{1,3},{2,0},{3,1},{4,6},{5,7},{6,4},{7,5},{8,10},{9,11},{10,... | collective-permute-start | bytes 983048 | tf_op jit(solution)/shard_map/ppermute | solution.py:382
  68.4 8.6 %collective-permute-start.18 = (bf16[128,1280]{1,0:T(8,128)(2,1)S(1)}, bf16[128,1280]{1,0:T(8,128)(2,1)S(1)}, u32[]{:S(2)}, u32[]{:S(2)}) collective-permute-start(bf16[128,1280]{1,0:T(8,128)(2,1)S(1)} %collective-permute-done.14.refs_5_), channel_id=1, source_target_pairs={{0,1},{1,0},{2,3},{3,2},{4,5},{5,4},{6,7},{7,6},{8,9},{9,8},{10,11... | collective-permute-start | bytes 983048 | tf_op jit(solution)/shard_map/ppermute | solution.py:382
  68.4 8.6 %collective-permute-start.19 = (bf16[128,1280]{1,0:T(8,128)(2,1)S(1)}, bf16[128,1280]{1,0:T(8,128)(2,1)S(1)}, u32[]{:S(2)}, u32[]{:S(2)}) collective-permute-start(bf16[128,1280]{1,0:T(8,128)(2,1)S(1)} %collective-permute-done.13.refs_6_), channel_id=1, source_target_pairs={{0,1},{1,0},{2,3},{3,2},{4,5},{5,4},{6,7},{7,6},{8,9},{9,8},{10,11... | collective-permute-start | bytes 983048 | tf_op jit(solution)/shard_map/ppermute | solution.py:382
  77.0 1.6 %collective-permute-start.20 = (bf16[128,1280]{1,0:T(8,128)(2,1)S(1)}, bf16[128,1280]{1,0:T(8,128)(2,1)S(1)}, u32[]{:S(2)}, u32[]{:S(2)}) collective-permute-start(bf16[128,1280]{1,0:T(8,128)(2,1)S(1)} %collective-permute-done.15.refs_7_), channel_id=1, source_target_pairs={{0,1},{1,0},{2,3},{3,2},{4,5},{5,4},{6,7},{7,6},{8,9},{9,8},{10,11... | collective-permute-start | bytes 983048 | tf_op jit(solution)/shard_map/ppermute | solution.py:382
  78.6 7.4 %copy-start.3 = (s32[256]{0:T(256)S(1)}, s32[256]{0:T(256)}, u32[]{:S(2)}) copy-start(s32[256]{0:T(256)} %param.11) | copy-start | bytes 3076

commit v20 on v18

--- a/solution.py
+++ b/solution.py
@@ -208,8 +208,9 @@
 
 
 def slot_of(window, chip):
-    slot = window ^ chip
-    return jnp.where((slot == 3) | (slot == 4), slot ^ 7, slot)
+    rel = window ^ chip
+    early = jnp.where((rel == 3) | (rel == 4), rel ^ 7, rel)
+    return jnp.where((rel == 5) | (rel == 6), rel ^ 3, early)
 
 
 def half_kernel(here, early, code_ref, got_ref, size_ref, *refs):
@@ -301,49 +302,65 @@
         late_ref[p] = jnp.dot(hot_ref[...], placed_ref[p], preferred_element_type=F32).astype(BF16)
 
 
-def last_kernel(count, early, me_ref, part_any, late_any, *refs):
-    pieces, (out_any, right_ref, occ_ref, part_ref, late_ref, half_ref, tiles_ref, sems) = refs[: 2 * count], refs[2 * count :]
+def gather_kernel(early, me_ref, part_ref, late_ref, *refs):
+    count = (len(refs) - 4) // 2
+    pieces, (right_ref, half_ref, occ_ref, sems) = refs[: 2 * count], refs[2 * count :]
     width = right_ref.shape[2]
-    tile = tiles_ref.shape[3]
-    per = width // tile
     core = lax.rem(me_ref[0], CORES)
-    first, near, far, results = [], [], [], []
-
-    def copy_of(source, target):
-        at = len(first) + len(near) + len(far) + len(results)
-        return pltpu.make_async_copy(source, target, sems.at[at])
-
-    first.append(copy_of(part_any, part_ref))
-    first.append(copy_of(late_any, late_ref))
+    first, copies = [], []
     for side in range(2):
         half = lax.rem(core + side, CORES)
-        for k in range(early, count):
-            target = occ_ref.at[pl.ds((k - early) * CAP, CAP), pl.ds(pl.multiple_of(half * 128, 128), 128)]
-            first.append(copy_of(pieces[side * count + k].at[:, pl.ds(width, 128)], target))
-    for side, copies in enumerate((near, far)):
         for k in range(count):
+            at = side * count + k
+            if k >= early:
+                target = occ_ref.at[pl.ds((k - early) * CAP, CAP), pl.ds(pl.multiple_of(half * 128, 128), 128)]
+                source = pieces[at].at[:, pl.ds(width, 128)]
+                first.append(pltpu.make_async_copy(source, target, sems.at[2 * count + at]))
             target = right_ref.at[side, pl.ds(k * CAP, CAP), :]
-            copies.append(copy_of(pieces[side * count + k].at[:, pl.ds(0, width)], target))
-    for copy in (*first, *near, *far):
+            copies.append(pltpu.make_async_copy(pieces[at].at[:, pl.ds(0, width)], target, sems.at[at]))
+    for copy in (*first, *copies):
         copy.start()
     for copy in first:
         copy.wait()
     occ = occ_ref[...].T
     for p in range(2):
         rows = slice(p * NOCC, (p + 1) * NOCC)
-        late = jnp.dot(occ, late_ref[p], preferred_element_type=F32)
-        half_ref[rows, :] = (part_ref[rows, :] + late).astype(BF16)
-    for side, copies in enumerate((near, far)):
-        for copy in copies:
-            copy.wait()
+        late = jnp.dot(occ, late_ref[p, : occ_ref.shape[0], :], preferred_element_type=F32)
+        half_ref[rows, :] = part_ref[rows, :] + late
+    for copy in copies:
+        copy.wait()
+
+
+def last_kernel(me_ref, part_ref, right_ref, late_any, *refs):
+    pieces, (out_any, late_ref, half_ref, tiles_ref, sems) = (refs[:2], refs[2:4]), refs[4:]
+    width = right_ref.shape[2]
+    cut = right_ref.shape[1]
+    tile = tiles_ref.shape[3]
+    per = width // tile
+    core = lax.rem(me_ref[0], CORES)
+    rows = late_any.shape[1] - 2 * CAP
+    copy = pltpu.make_async_copy(late_any.at[:, pl.ds(rows, 2 * CAP), :], late_ref, sems.at[0])
+    copy.start()
+    copy.wait()
+    sides = [jnp.concatenate([ref[:, width:] for ref in side], axis=0).T for side in pieces]
+    for p in range(2):
+        for side, occ in enumerate(sides):
+            half = lax.rem(core + side, CORES)
+            rows = pl.ds(pl.multiple_of(p * NOCC + half * 128, 128), 128)
+            late = jnp.dot(occ, late_ref[p], preferred_element_type=F32)
+            half_ref[rows, :] = (part_ref[rows, :] + late).astype(BF16)
+    results = []
+    for side, tail in enumerate(pieces):
         base = lax.rem(core + side, CORES) * width
         for t in range(per):
-            right = right_ref[side, :, t * tile : (t + 1) * tile]
-            total = jnp.dot(half_ref[...], right, preferred_element_type=F32).astype(BF16)
+            columns = slice(t * tile, (t + 1) * tile)
+            total = jnp.dot(half_ref[:, :cut], right_ref[side, :, columns], preferred_element_type=F32)
+            below = jnp.concatenate([ref[:, columns] for ref in tail], axis=0)
+            total += jnp.dot(half_ref[:, cut:], below, preferred_element_type=F32)
             at = side * per + t
-            tiles_ref[at] = total.reshape(tiles_ref.shape[1:])
-            columns = pl.ds(pl.multiple_of(base + t * tile, 128), tile)
-            results.append(copy_of(tiles_ref.at[at], out_any.at[:, :, columns]))
+            tiles_ref[at] = total.astype(BF16).reshape(tiles_ref.shape[1:])
+            target = out_any.at[:, :, pl.ds(pl.multiple_of(base + t * tile, 128), tile)]
+            results.append(pltpu.make_async_copy(tiles_ref.at[at], target, sems.at[1 + at]))
             results[-1].start()
     for copy in results:
         copy.wait()
@@ -442,34 +459,40 @@
         cost_estimate=cost(7e9, 1),
         name="half_transform",
     )(code, got, size_row, *near, *far)
-    corner, half, late = lax.optimization_barrier((corner, half, late))
+    corner, beside_y, half, late = lax.optimization_barrier((corner, beside_y, half, late))
     corner_y = swap(corner, 2)
-    near += [beside_y, across_y, corner]
+    near += [beside_y, corner]
     far += [swap(piece, 1) for piece in near[early:]]
-    corner_y, *far = lax.optimization_barrier((corner_y, *far))
-    near.append(corner_y)
-    far.append(swap(corner_y, 1))
-
     count = len(near)
+    right, half = pl.pallas_call(
+        functools.partial(gather_kernel, early),
+        out_shape=(shape(CORES, count * CAP, width), shape(2 * NOCC, room, dtype=F32)),
+        in_specs=[SMEM] + [VMEM] * 2 + [ANY] * (2 * count),
+        out_specs=(VMEM, VMEM),
+        scratch_shapes=[pltpu.VMEM(((count - early) * CAP, NOCC), BF16), pltpu.SemaphoreType.DMA((4 * count,))],
+        compiler_params=params(20),
+        cost_estimate=cost(1, 1),
+        name="gather_pieces",
+    )(me, half, late, *near, *far)
+    corner_y, right, half = lax.optimization_barrier((corner_y, right, half))
+    tails = [across_y, corner_y, swap(across_y, 1), swap(corner_y, 1)]
+
     tile = width // 3
     out = pl.pallas_call(
-        functools.partial(last_kernel, count, early),
+        last_kernel,
         out_shape=shape(2, NOCC, nvir),
-        in_specs=[SMEM] + [ANY] * (2 + 2 * count),
+        in_specs=[SMEM] + [VMEM] * 2 + [ANY] + [VMEM] * 4,
         out_specs=ANY,
         scratch_shapes=[
-            pltpu.VMEM((CORES, room, width), BF16),
-            pltpu.VMEM((room - early * CAP, NOCC), BF16),
-            pltpu.VMEM(half.shape, F32),
-            pltpu.VMEM(late.shape, BF16),
+            pltpu.VMEM((2, 2 * CAP, room), BF16),
             pltpu.VMEM((2 * NOCC, room), BF16),
             pltpu.VMEM((nvir // tile, 2, NOCC, tile), BF16),
-            pltpu.SemaphoreType.DMA((2 + 4 * count + nvir // tile,)),
+            pltpu.SemaphoreType.DMA((1 + nvir // tile,)),
         ],
-        compiler_params=params(30),
+        compiler_params=params(24),
         cost_estimate=cost(2e10, 1),
         name="last_product",
-    )(me, half, late, *near, *far)
+    )(me, half, right, late, *tails)
     return out, over[0], code, got
 
 

time: 90 us -> 88.5 us (0.983)
  waiting for transfers between devices: 14.1 us -> 12.6 us
    ppermute x18, waiting for transfers between devices: 14.1 us -> 12.6 us  [swap(): return lax.ppermute(array, 'shell', [(i, i ^ bit) for i in range(n)])]
    pallas_call x1 -> x2, Pallas kernels: 6.76 us -> 6.96 us  [the longest x1 5.31 us: short_way(): pl.pallas_call(last_kernel, out_shape=shape(2, NOCC, nvir), in_specs=[SME...]
  transfers between devices with their start and end apart: 18 -> 18, of which waited for: 4 -> 5; matrix products, arithmetic and copies ran while one was open for 0% -> 0% of each run, Pallas kernels for 9% -> 11%
where the time goes in v20:
time: 88.5 us; the launch traced here: 88.2 us
  blocking collectives  29 us (33%)
  Pallas kernels  19.1 us (22%)
  between operations  14.2 us (16%)
  waiting for transfers between devices  12.6 us (14%)
  starting transfers between devices  11.1 us (13%)
  local copies, waits for them, and re-layouts  1.58 us (2%)
    all_to_all x1, blocking collectives, short_way(): lax.all_to_all(panel, 'shell', split_axis=0, concat_axis=0, axis_index_gr...  16.1 us
    all_to_all x1, blocking collectives, short_way(): lax.all_to_all(code, 'shell', split_axis=0, concat_axis=0, tiled=True)  12.8 us
    ppermute x18, waiting for transfers between devices, swap(): return lax.ppermute(array, 'shell', [(i, i ^ bit) for i in range(n)])  12.6 us
    ppermute x18, starting transfers between devices, swap(): return lax.ppermute(array, 'shell', [(i, i ^ bit) for i in range(n)])  11.1 us
    pallas_call x1, Pallas kernels, short_way(): pl.pallas_call(functools.partial(half_kernel, here, early), out_shape=(sh...  8.29 us
    pallas_call x1, Pallas kernels, short_way(): pl.pallas_call(last_kernel, out_shape=shape(2, NOCC, nvir), in_specs=[SME...  5.31 us
    pallas_call x1, Pallas kernels, short_way(): pl.pallas_call(functools.partial(pick_kernel, here), out_shape=[shape(CAP...  2.14 us
  transfers between devices with their start and end apart: 18, of which 5 were waited for; matrix products, arithmetic and copies ran while one was open for 0% of the time, Pallas kernels for 11%

profile of v20, /device:TPU:0, one launch (start us, length us, event | category | flops | bytes accessed | tf_op | source)
XLA Modules:
  0.0 88.2 jit_solution(8828379845933327191)
XLA Ops:
  6.5 0.9 %copy-done.1 = bf16[8,32,256]{2,1,0:T(8,128)(2,1)S(1)} copy-done((bf16[8,32,256]{2,1,0:T(8,128)(2,1)S(1)}, bf16[8,32,256]{2,1,0:T(8,128)(2,1)}, u32[]{:S(2)}) %copy-start.1) | copy-done | bytes 131096
  7.4 1.6 %pack_rows.1 = (bf16[96,1280]{1,0:T(8,128)(2,1)S(1)}, bf16[96,1280]{1,0:T(8,128)(2,1)S(1)}, bf16[96,1280]{1,0:T(8,128)(2,1)S(1)}, bf16[96,1280]{1,0:T(8,128)(2,1)S(1)}) custom-call(bf16[160,2304]{1,0:T(8,128)(2,1)} %vir_ref.1, bf16[160,256]{1,0:T(8,128)(2,1)} %occ_ref.1, bf16[8,32,256]{2,1,0:T(8,128)(2,1)S(1)} %copy-done.1), custom_call_target="tpu_custom_call" | custom-call | flops 300000000 | bytes 3000000 | tf_op jit(solution)/shard_map/pack_rows/pallas_call | solution.py:397
  9.0 0.5 collective-permute-start
  9.5 2.6 %collective-permute-start.1 = (bf16[96,1280]{1,0:T(8,128)(2,1)S(1)}, bf16[96,1280]{1,0:T(8,128)(2,1)S(1)}, u32[]{:S(2)}, u32[]{:S(2)}) collective-permute-start(bf16[96,1280]{1,0:T(8,128)(2,1)S(1)} %get-tuple-element.171), channel_id=1, source_target_pairs={{0,2},{1,3},{2,0},{3,1},{4,6},{5,7},{6,4},{7,5},{8,10},{9,11},{10,... | collective-permute-start | bytes 737288 | tf_op jit(solution)/shard_map/ppermute | solution.py:395
  12.1 0.1 collective-permute-start.2
  12.9 0.0 copy-start
  12.9 0.7 copy-done
  13.5 0.2 pack_ids.1
  13.7 12.8 %all_to_all.10.code_ref = s32[16,8,128]{2,1,0:T(8,128)S(1)} all-to-all(s32[16,8,128]{2,1,0:T(8,128)S(1)} %pack_ids.1), channel_id=1, replica_groups=mesh['groups'=2,'shell'=16] {'shell'}, dimensions={0} | all-to-all | bytes 131072 | tf_op jit(solution)/shard_map/all_to_all | solution.py:417
  26.5 0.0 collective-permute-done.refs_1_
  26.5 0.0 collective-permute-done.1.refs_2_
  26.5 2.1 %pick_rows.1 = (bf16[128,1280]{1,0:T(8,128)(2,1)S(1)}, s32[1]{0:T(128)}, s32[1]{0:T(128)}, bf16[4,4,16,256]{3,2,1,0:T(8,128)(2,1)S(1)}) custom-call(s32[16,8,128]{2,1,0:T(8,128)S(1)} %all_to_all.10.code_ref, s32[1,256]{1,0:T(1,128)} %bitcast.66, bf16[96,1280]{1,0:T(8,128)(2,1)S(1)} %get-tuple-element.169.refs_0_, ...), custom_call_target="tpu_custom_call" | custom-call | flops 300000000 | bytes 2000000 | tf_op jit(solution)/shard_map/pick_rows/pallas_call | solution.py:419
  28.7 1.0 %collective-permute-start.3 = (bf16[128,1280]{1,0:T(8,128)(2,1)S(1)}, bf16[128,1280]{1,0:T(8,128)(2,1)S(1)}, u32[]{:S(2)}, u32[]{:S(2)}) collective-permute-start(bf16[128,1280]{1,0:T(8,128)(2,1)S(1)} %get-tuple-element.175.refs_0_), channel_id=1, source_target_pairs={{0,8},{1,9},{2,10},{3,11},{4,12},{5,13},{6,14},{7,15},{8,0},{9,1},... | collective-permute-start | bytes 983048 | tf_op jit(solution)/shard_map/ppermute | solution.py:395
  29.6 1.6 %collective-permute-start.4 = (bf16[128,1280]{1,0:T(8,128)(2,1)S(1)}, bf16[128,1280]{1,0:T(8,128)(2,1)S(1)}, u32[]{:S(2)}, u32[]{:S(2)}) collective-permute-start(bf16[128,1280]{1,0:T(8,128)(2,1)S(1)} %get-tuple-element.175.refs_0_), channel_id=1, source_target_pairs={{0,2},{1,3},{2,0},{3,1},{4,6},{5,7},{6,4},{7,5},{8,10},{9,11},{10,... | collective-permute-start | bytes 983048 | tf_op jit(solution)/shard_map/ppermute | solution.py:395
  31.2 1.6 %collective-permute-start.5 = (bf16[128,1280]{1,0:T(8,128)(2,1)S(1)}, bf16[128,1280]{1,0:T(8,128)(2,1)S(1)}, u32[]{:S(2)}, u32[]{:S(2)}) collective-permute-start(bf16[128,1280]{1,0:T(8,128)(2,1)S(1)} %get-tuple-element.175.refs_0_), channel_id=1, source_target_pairs={{0,4},{1,5},{2,6},{3,7},{4,0},{5,1},{6,2},{7,3},{8,12},{9,13},{10,... | collective-permute-start | bytes 983048 | tf_op jit(solution)/shard_map/ppermute | solution.py:395
  32.8 16.1 %all_to_all.11 = bf16[4,4,16,256]{3,2,1,0:T(8,128)(2,1)S(1)} all-to-all(bf16[4,4,16,256]{3,2,1,0:T(8,128)(2,1)S(1)} %get-tuple-element.176), channel_id=1, replica_groups={{0,4,8,12},{1,5,9,13},{2,6,10,14},{3,7,11,15},{16,20,24,28},{17,21,25,2..., dimensions={0} | all-to-all | bytes 262144 | tf_op jit(solution)/shard_map/all_to_all | solution.py:432
  49.0 0.1 collective-permute-start.9
  49.1 0.5 collective-permute-start.10
  49.6 0.1 collective-permute-start.11
  49.6 0.7 collective-permute-start.8
  50.4 0.3 collective-permute-done.9.refs_5_.refs_7_
  50.7 1.0 %collective-permute-start.15 = (bf16[128,1280]{1,0:T(8,128)(2,1)S(1)}, bf16[128,1280]{1,0:T(8,128)(2,1)S(1)}, u32[]{:S(2)}, u32[]{:S(2)}) collective-permute-start(bf16[128,1280]{1,0:T(8,128)(2,1)S(1)} %collective-permute-done.3.refs_3_), channel_id=1, source_target_pairs={{0,2},{1,3},{2,0},{3,1},{4,6},{5,7},{6,4},{7,5},{8,10},{9,11},{10,... | collective-permute-start | bytes 983048 | tf_op jit(solution)/shard_map/ppermute | solution.py:395
  51.7 8.3 %half_transform.1 = (f32[512,1024]{1,0:T(8,128)S(1)}, bf16[2,512,1024]{2,1,0:T(8,128)(2,1)S(1)}) custom-call(s32[16,8,128]{2,1,0:T(8,128)S(1)} %all_to_all.10.code_ref, bf16[16,16,256]{2,1,0:T(8,128)(2,1)S(1)} %bitcast.64, s32[1,256]{1,0:T(1,128)} %bitcast.67, bf16[128,1280]{1,0:T(8,128)(2,1)S(1)} %get-tuple-element.175.refs_0_, ...), custom_call_target="tpu_custom_call" | custom-call | flops 7000000000 | bytes 1 | tf_op jit(solution)/shard_map/half_transform/pallas_call | solution.py:442
  60.0 0.2 collective-permute-done.8.refs_4_
  60.1 0.5 collective-permute-start.14
  60.7 0.9 %collective-permute-start.12 = (bf16[128,1280]{1,0:T(8,128)(2,1)S(1)}, bf16[128,1280]{1,0:T(8,128)(2,1)S(1)}, u32[]{:S(2)}, u32[]{:S(2)}) collective-permute-start(bf16[128,1280]{1,0:T(8,128)(2,1)S(1)} %collective-permute-done.7.refs_5_), channel_id=1, source_target_pairs={{0,2},{1,3},{2,0},{3,1},{4,6},{5,7},{6,4},{7,5},{8,10},{9,11},{10,... | collective-permute-start | bytes 983048 | tf_op jit(solution)/shard_map/ppermute | solution.py:395
  61.6 5.6 %collective-permute-done.15.refs_0_ = bf16[128,1280]{1,0:T(8,128)(2,1)S(1)} collective-permute-done((bf16[128,1280]{1,0:T(8,128)(2,1)S(1)}, bf16[128,1280]{1,0:T(8,128)(2,1)S(1)}, u32[]{:S(2)}, u32[]{:S(2)}) %collective-permute-start.15) | collective-permute-done | bytes 327712 | tf_op jit(solution)/shard_map/ppermute | solution.py:395
  67.2 1.6 %gather_pieces.1 = (bf16[2,768,1152]{2,1,0:T(8,128)(2,1)S(1)}, f32[512,1024]{1,0:T(8,128)S(1)}) custom-call(s32[1]{0:T(128)} %get-tuple-element.174.me_ref, f32[512,1024]{1,0:T(8,128)S(1)} %get-tuple-element.185.part_ref, bf16[2,512,1024]{2,1,0:T(8,128)(2,1)S(1)} %get-tuple-element.186.late_ref.late_any, bf16[128,1280]{1,0:T(8,128)(2,1)S(1)} %get-tuple-element.175.refs_0_, ...), custom_call_target="tpu_custom_call" | custom-call | flops 1 | bytes 1 | tf_op jit(solution)/shard_map/gather_pieces/pallas_call | solution.py:467
  68.8 4.9 %collective-permute-done.12.refs_1_ = bf16[128,1280]{1,0:T(8,128)(2,1)S(1)} collective-permute-done((bf16[128,1280]{1,0:T(8,128)(2,1)S(1)}, bf16[128,1280]{1,0:T(8,128)(2,1)S(1)}, u32[]{:S(2)}, u32[]{:S(2)}) %collective-permute-start.12) | collective-permute-done | bytes 327712 | tf_op jit(solution)/shard_map/ppermute | solution.py:395
  73.8 1.6 %collective-permute-done.17.refs_3_ = bf16[128,1280]{1,0:T(8,128)(2,1)S(1)} collective-permute-done((bf16[128,1280]{1,0:T(8,128)(2,1)S(1)}, bf16[128,1280]{1,0:T(8,128)(2,1)S(1)}, u32[]{:S(2)}, u32[]{:S(2)}) %collective-permute-start.17) | collective-permute-done | bytes 327712 | tf_op jit(solution)/shard_map/ppermute | solution.py:395
  75.4 5.3 %last_product.1 = bf16[2,256,2304]{2,1,0:T(8,128)(2,1)} custom-call(s32[1]{0:T(128)} %get-tuple-element.174.me_ref, f32[512,1024]{1,0:T(8,128)S(1)} %get-tuple-element.190.part_ref, bf16[2,768,1152]{2,1,0:T(8,128)(2,1)S(1)} %get-tuple-element.191.right_ref, bf16[2,512,1024]{2,1,0:T(8,128)(2,1)S(1)} %get-tuple-element.186.late_ref.late_any, ...), custom_call_target="tpu_custom_call" | custom-call | flops 20000000000 | bytes 1 | tf_op jit(solution)/shard_map/last_product/pallas_call | solution.py:481
  80.7 0.6 while.17
  (19 shorter events, 0.0 us)
Async XLA Ops:
  6.5 0.9 %copy-start.1 = (bf16[8,32,256]{2,1,0:T(8,128)(2,1)S(1)}, bf16[8,32,256]{2,1,0:T(8,128)(2,1)}, u32[]{:S(2)}) copy-start(bf16[8,32,256]{2,1,0:T(8,128)(2,1)} %panels_ref.1) | copy-start | bytes 393220
  9.0 17.5 %collective-permute-start = (bf16[96,1280]{1,0:T(8,128)(2,1)S(1)}, bf16[96,1280]{1,0:T(8,128)(2,1)S(1)}, u32[]{:S(2)}, u32[]{:S(2)}) collective-permute-start(bf16[96,1280]{1,0:T(8,128)(2,1)S(1)} %get-tuple-element.170), channel_id=1, source_target_pairs={{0,1},{1,0},{2,3},{3,2},{4,5},{5,4},{6,7},{7,6},{8,9},{9,8},{10,11... | collective-permute-start | bytes 737288 | tf_op jit(solution)/shard_map/ppermute | solution.py:395
  9.5 17.0 %collective-permute-start.1 = (bf16[96,1280]{1,0:T(8,128)(2,1)S(1)}, bf16[96,1280]{1,0:T(8,128)(2,1)S(1)}, u32[]{:S(2)}, u32[]{:S(2)}) collective-permute-start(bf16[96,1280]{1,0:T(8,128)(2,1)S(1)} %get-tuple-element.171), channel_id=1, source_target_pairs={{0,2},{1,3},{2,0},{3,1},{4,6},{5,7},{6,4},{7,5},{8,10},{9,11},{10,... | collective-permute-start | bytes 737288 | tf_op jit(solution)/shard_map/ppermute | solution.py:395
  12.1 14.4 %collective-permute-start.2 = (bf16[96,1280]{1,0:T(8,128)(2,1)S(1)}, bf16[96,1280]{1,0:T(8,128)(2,1)S(1)}, u32[]{:S(2)}, u32[]{:S(2)}) collective-permute-start(bf16[96,1280]{1,0:T(8,128)(2,1)S(1)} %get-tuple-element.172), channel_id=1, source_target_pairs={{0,3},{1,2},{2,1},{3,0},{4,7},{5,6},{6,5},{7,4},{8,11},{9,10},{10,... | collective-permute-start | bytes 737288 | tf_op jit(solution)/shard_map/ppermute | solution.py:395
  12.9 0.7 copy-start
  28.7 20.3 %collective-permute-start.3 = (bf16[128,1280]{1,0:T(8,128)(2,1)S(1)}, bf16[128,1280]{1,0:T(8,128)(2,1)S(1)}, u32[]{:S(2)}, u32[]{:S(2)}) collective-permute-start(bf16[128,1280]{1,0:T(8,128)(2,1)S(1)} %get-tuple-element.175.refs_0_), channel_id=1, source_target_pairs={{0,8},{1,9},{2,10},{3,11},{4,12},{5,13},{6,14},{7,15},{8,0},{9,1},... | collective-permute-start | bytes 983048 | tf_op jit(solution)/shard_map/ppermute | solution.py:395
  29.6 19.3 %collective-permute-start.4 = (bf16[128,1280]{1,0:T(8,128)(2,1)S(1)}, bf16[128,1280]{1,0:T(8,128)(2,1)S(1)}, u32[]{:S(2)}, u32[]{:S(2)}) collective-permute-start(bf16[128,1280]{1,0:T(8,128)(2,1)S(1)} %get-tuple-element.175.refs_0_), channel_id=1, source_target_pairs={{0,2},{1,3},{2,0},{3,1},{4,6},{5,7},{6,4},{7,5},{8,10},{9,11},{10,... | collective-permute-start | bytes 983048 | tf_op jit(solution)/shard_map/ppermute | solution.py:395
  31.2 17.7 %collective-permute-start.5 = (bf16[128,1280]{1,0:T(8,128)(2,1)S(1)}, bf16[128,1280]{1,0:T(8,128)(2,1)S(1)}, u32[]{:S(2)}, u32[]{:S(2)}) collective-permute-start(bf16[128,1280]{1,0:T(8,128)(2,1)S(1)} %get-tuple-element.175.refs_0_), channel_id=1, source_target_pairs={{0,4},{1,5},{2,6},{3,7},{4,0},{5,1},{6,2},{7,3},{8,12},{9,13},{10,... | collective-permute-start | bytes 983048 | tf_op jit(solution)/shard_map/ppermute | solution.py:395
  32.8 16.2 %collective-permute-start.6 = (bf16[128,1280]{1,0:T(8,128)(2,1)S(1)}, bf16[128,1280]{1,0:T(8,128)(2,1)S(1)}, u32[]{:S(2)}, u32[]{:S(2)}) collective-permute-start(bf16[128,1280]{1,0:T(8,128)(2,1)S(1)} %get-tuple-element.175.refs_0_), channel_id=1, source_target_pairs={{0,1},{1,0},{2,3},{3,2},{4,5},{5,4},{6,7},{7,6},{8,9},{9,8},{10,11... | collective-permute-start | bytes 983048 | tf_op jit(solution)/shard_map/ppermute | solution.py:395
  49.0 1.7 %collective-permute-start.9 = (bf16[128,1280]{1,0:T(8,128)(2,1)S(1)}, bf16[128,1280]{1,0:T(8,128)(2,1)S(1)}, u32[]{:S(2)}, u32[]{:S(2)}) collective-permute-start(bf16[128,1280]{1,0:T(8,128)(2,1)S(1)} %collective-permute-done.4.refs_1_), channel_id=1, source_target_pairs={{0,1},{1,0},{2,3},{3,2},{4,5},{5,4},{6,7},{7,6},{8,9},{9,8},{10,11... | collective-permute-start | bytes 983048 | tf_op jit(solution)/shard_map/ppermute | solution.py:395
  49.1 2.6 %collective-permute-start.10 = (bf16[128,1280]{1,0:T(8,128)(2,1)S(1)}, bf16[128,1280]{1,0:T(8,128)(2,1)S(1)}, u32[]{:S(2)}, u32[]{:S(2)}) collective-permute-start(bf16[128,1280]{1,0:T(8,128)(2,1)S(1)} %collective-permute-done.5.refs_2_), channel_id=1, source_target_pairs={{0,1},{1,0},{2,3},{3,2},{4,5},{5,4},{6,7},{7,6},{8,9},{9,8},{10,11... | collective-permute-start | bytes 983048 | tf_op jit(solution)/shard_map/ppermute | solution.py:395
  49.6 2.1 %collective-permute-start.11 = (bf16[128,1280]{1,0:T(8,128)(2,1)S(1)}, bf16[128,1280]{1,0:T(8,128)(2,1)S(1)}, u32[]{:S(2)}, u32[]{:S(2)}) collective-permute-start(bf16[128,1280]{1,0:T(8,128)(2,1)S(1)} %collective-permute-done.3.refs_3_), channel_id=1, source_target_pairs={{0,1},{1,0},{2,3},{3,2},{4,5},{5,4},{6,7},{7,6},{8,9},{9,8},{10,11... | collective-permute-start | bytes 983048 | tf_op jit(solution)/shard_map/ppermute | solution.py:395
  49.6 10.3 %collective-permute-start.7 = (bf16[128,1280]{1,0:T(8,128)(2,1)S(1)}, bf16[128,1280]{1,0:T(8,128)(2,1)S(1)}, u32[]{:S(2)}, u32[]{:S(2)}) collective-permute-start(bf16[128,1280]{1,0:T(8,128)(2,1)S(1)} %collective-permute-done.3.refs_3_), channel_id=1, source_target_pairs={{0,4},{1,5},{2,6},{3,7},{4,0},{5,1},{6,2},{7,3},{8,12},{9,13},{10,... | collective-permute-start | bytes 983048 | tf_op jit(solution)/shard_map/ppermute | solution.py:395
  49.6 10.5 %collective-permute-start.8 = (bf16[128,1280]{1,0:T(8,128)(2,1)S(1)}, bf16[128,1280]{1,0:T(8,128)(2,1)S(1)}, u32[]{:S(2)}, u32[]{:S(2)}) collective-permute-start(bf16[128,1280]{1,0:T(8,128)(2,1)S(1)} %collective-permute-done.5.refs_2_), channel_id=1, source_target_pairs={{0,2},{1,3},{2,0},{3,1},{4,6},{5,7},{6,4},{7,5},{8,10},{9,11},{10,... | collective-permute-start | bytes 983048 | tf_op jit(solution)/shard_map/ppermute | solution.py:395
  50.7 16.5 %collective-permute-start.15 = (bf16[128,1280]{1,0:T(8,128)(2,1)S(1)}, bf16[128,1280]{1,0:T(8,128)(2,1)S(1)}, u32[]{:S(2)}, u32[]{:S(2)}) collective-permute-start(bf16[128,1280]{1,0:T(8,128)(2,1)S(1)} %collective-permute-done.3.refs_3_), channel_id=1, source_target_pairs={{0,2},{1,3},{2,0},{3,1},{4,6},{5,7},{6,4},{7,5},{8,10},{9,11},{10,... | collective-permute-start | bytes 983048 | tf_op jit(solution)/shard_map/ppermute | solution.py:395
  60.1 7.0 %collective-permute-start.13 = (bf16[128,1280]{1,0:T(8,128)(2,1)S(1)}, bf16[128,1280]{1,0:T(8,128)(2,1)S(1)}, u32[]{:S(2)}, u32[]{:S(2)}) collective-permute-start(bf16[128,1280]{1,0:T(8,128)(2,1)S(1)} %collective-permute-done.8.refs_4_), channel_id=1, source_target_pairs={{0,1},{1,0},{2,3},{3,2},{4,5},{5,4},{6,7},{7,6},{8,9},{9,8},{10,11... | collective-permute-start | bytes 983048 | tf_op jit(solution)/shard_map/ppermute | solution.py:395
  60.1 7.0 %collective-permute-start.14 = (bf16[128,1280]{1,0:T(8,128)(2,1)S(1)}, bf16[128,1280]{1,0:T(8,128)(2,1)S(1)}, u32[]{:S(2)}, u32[]{:S(2)}) collective-permute-start(bf16[128,1280]{1,0:T(8,128)(2,1)S(1)} %collective-permute-done.7.refs_5_), channel_id=1, source_target_pairs={{0,1},{1,0},{2,3},{3,2},{4,5},{5,4},{6,7},{7,6},{8,9},{9,8},{10,11... | collective-permute-start | bytes 983048 | tf_op jit(solution)/shard_map/ppermute | solution.py:395
  60.7 13.1 %collective-permute-start.12 = (bf16[128,1280]{1,0:T(8,128)(2,1)S(1)}, bf16[128,1280]{1,0:T(8,128)(2,1)S(1)}, u32[]{:S(2)}, u32[]{:S(2)}) collective-permute-start(bf16[128,1280]{1,0:T(8,128)(2,1)S(1)} %collective-permute-done.7.refs_5_), channel_id=1, source_target_pairs={{0,2},{1,3},{2,0},{3,1},{4,6},{5,7},{6,4},{7,5},{8,10},{9,11},{10,... | collective-permute-start | bytes 983048 | tf_op jit(solution)/shard_map/ppermute | solution.py:395
  67.2 6.6 %collective-permute-start.16 = (bf16[128,1280]{1,0:T(8,128)(2,1)S(1)}, bf16[128,1280]{1,0:T(8,128)(2,1)S(1)}, u32[]{:S(2)}, u32[]{:S(2)}) collective-permute-start(bf16[128,1280]{1,0:T(8,128)(2,1)S(1)} %collective-permute-done.15.refs_0_), channel_id=1, source_target_pairs={{0,1},{1,0},{2,3},{3,2},{4,5},{5,4},{6,7},{7,6},{8,9},{9,8},{10,11... | collective-permute-start | bytes 983048 | tf_op jit(solution)/shard_map/ppermute | solution.py:395
  73.7 7.0 %copy-start.3 = (s32[256]{0:T(256)S(1)}, s32[256]{0:T(256)}, u32[]{:S(2)}) copy-start(s32[256]{0:T(256)} %param.11) | copy-start | bytes 3076
  73.7 1.6 %collective-permute-start.17 = (bf16[128,1280]{1,0:T(8,128)(2,1)S(1)}, bf16[128,1280]{1,0:T(8,128)(2,1)S(1)}, u32[]{:S(2)}, u32[]{:S(2)}) collective-permute-start(bf16[128,1280]{1,0:T(8,128)(2,1)S(1)} %collective-permute-done.12.refs_1_), channel_id=1, source_target_pairs={{0,1},{1,0},{2,3},{3,2},{4,5},{5,4},{6,7},{7,6},{8,9},{9,8},{10,11... | collective-permute-start | bytes 983048 | tf_op jit(solution)/shard_map/ppermute | solution.py:395

commit v21 on v20

--- a/solution.py
+++ b/solution.py
@@ -153,7 +153,8 @@
             out[rows:, Z * block :] = jnp.zeros((2 * BLK_DEV, out.shape[1] - Z * block), BF16)
 
 
-def ids_kernel(shells, pairs_ref, count_ref, code_ref):
+def ids_kernel(shells, pairs_ref, count_ref, size_ref, code_ref, size_out_ref):
+    size_out_ref[...] = size_ref[...]
     code = pairs_ref[1:2, :] + shells * pairs_ref[0:1, :]
     code = jnp.where(iota((1, BLK_DEV), 1) < count_ref[...], code, -1).astype(F32)
     square = (BLK_DEV, BLK_DEV)
@@ -394,6 +395,16 @@
     def swap(array, bit):
         return lax.ppermute(array, "shell", [(i, i ^ bit) for i in range(n)])
 
+    code, size_row = pl.pallas_call(
+        functools.partial(ids_kernel, size_row.shape[1]),
+        out_shape=(shape(n, BLK_DEV, 128, dtype=jnp.int32), shape(*size_row.shape, dtype=jnp.int32)),
+        in_specs=[VMEM] * 3,
+        out_specs=(VMEM, VMEM),
+        compiler_params=params(12),
+        cost_estimate=cost(1e4, 1e4),
+        name="pack_ids",
+    )(block_pairs.T, block_count.reshape(1, 1), size_row)
+    code, panels = lax.optimization_barrier((code, panels))
     keep, to_core, to_y, to_both = pl.pallas_call(
         pack_kernel,
         out_shape=[shape(here // 2 + 2 * BLK_DEV, packed)] * 4,
@@ -405,15 +416,6 @@
         name="pack_rows",
     )(vir_coef, occ_coef, panels)
     to_y, to_both, to_core = swap(to_y, 2), swap(to_both, 3), swap(to_core, 1)
-    code = pl.pallas_call(
-        functools.partial(ids_kernel, size_row.shape[1]),
-        out_shape=shape(n, BLK_DEV, 128, dtype=jnp.int32),
-        in_specs=[VMEM] * 2,
-        out_specs=VMEM,
-        compiler_params=params(12),
-        cost_estimate=cost(1e4, 1e4),
-        name="pack_ids",
-    )(block_pairs.T, block_count.reshape(1, 1))
     code = lax.all_to_all(code, "shell", split_axis=0, concat_axis=0, tiled=True)
 
     mine, over, me, panel = pl.pallas_call(

time: 88.5 us -> 89.2 us (level)
  starting transfers between devices: 11.1 us -> 13.6 us
  blocking collectives: 29 us -> 28 us
    ppermute x18, starting transfers between devices: 11.1 us -> 13.6 us  [swap(): return lax.ppermute(array, 'shell', [(i, i ^ bit) for i in range(n)])]
    all_to_all x1, blocking collectives: 16.1 us -> 15.2 us  [short_way(): lax.all_to_all(panel, 'shell', split_axis=0, concat_axis=0, axis_index_gr...]
  transfers between devices with their start and end apart: 18 -> 18, of which waited for: 5 -> 4; matrix products, arithmetic and copies ran while one was open for 0% -> 0% of each run, Pallas kernels for 11% -> 10%
where the time goes in v21:
time: 89.2 us; the launch traced here: 88.9 us
  blocking collectives  28 us (31%)
  Pallas kernels  18.5 us (21%)
  between operations  14.2 us (16%)
  starting transfers between devices  13.6 us (15%)
  waiting for transfers between devices  12.4 us (14%)
  local copies, waits for them, and re-layouts  1.58 us (2%)
    all_to_all x1, blocking collectives, short_way(): lax.all_to_all(panel, 'shell', split_axis=0, concat_axis=0, axis_index_gr...  15.2 us
    ppermute x18, starting transfers between devices, swap(): return lax.ppermute(array, 'shell', [(i, i ^ bit) for i in range(n)])  13.6 us
    all_to_all x1, blocking collectives, short_way(): lax.all_to_all(code, 'shell', split_axis=0, concat_axis=0, tiled=True)  12.8 us
    ppermute x18, waiting for transfers between devices, swap(): return lax.ppermute(array, 'shell', [(i, i ^ bit) for i in range(n)])  12.4 us
    pallas_call x1, Pallas kernels, short_way(): pl.pallas_call(functools.partial(half_kernel, here, early), out_shape=(sh...  7.63 us
    pallas_call x1, Pallas kernels, short_way(): pl.pallas_call(last_kernel, out_shape=shape(2, NOCC, nvir), in_specs=[SME...  5.32 us
  transfers between devices with their start and end apart: 18, of which 4 were waited for; matrix products, arithmetic and copies ran while one was open for 0% of the time, Pallas kernels for 10%

profile of v21, /device:TPU:0, one launch (start us, length us, event | category | flops | bytes accessed | tf_op | source)
XLA Modules:
  0.0 88.9 jit_solution(12307314478761116351)
XLA Ops:
  7.2 0.7 copy-done
  7.9 0.8 pack_ids.1
  8.7 0.9 %copy-done.1 = bf16[8,32,256]{2,1,0:T(8,128)(2,1)S(1)} copy-done((bf16[8,32,256]{2,1,0:T(8,128)(2,1)S(1)}, bf16[8,32,256]{2,1,0:T(8,128)(2,1)}, u32[]{:S(2)}) %copy-start.1) | copy-done | bytes 131096
  9.6 1.6 %pack_rows.1 = (bf16[96,1280]{1,0:T(8,128)(2,1)S(1)}, bf16[96,1280]{1,0:T(8,128)(2,1)S(1)}, bf16[96,1280]{1,0:T(8,128)(2,1)S(1)}, bf16[96,1280]{1,0:T(8,128)(2,1)S(1)}) custom-call(bf16[160,2304]{1,0:T(8,128)(2,1)} %vir_ref.1, bf16[160,256]{1,0:T(8,128)(2,1)} %occ_ref.1, bf16[8,32,256]{2,1,0:T(8,128)(2,1)S(1)} %copy-done.1), custom_call_target="tpu_custom_call" | custom-call | flops 300000000 | bytes 3000000 | tf_op jit(solution)/shard_map/pack_rows/pallas_call | solution.py:408
  11.2 0.5 collective-permute-start
  11.7 2.6 %collective-permute-start.1 = (bf16[96,1280]{1,0:T(8,128)(2,1)S(1)}, bf16[96,1280]{1,0:T(8,128)(2,1)S(1)}, u32[]{:S(2)}, u32[]{:S(2)}) collective-permute-start(bf16[96,1280]{1,0:T(8,128)(2,1)S(1)} %get-tuple-element.179), channel_id=1, source_target_pairs={{0,2},{1,3},{2,0},{3,1},{4,6},{5,7},{6,4},{7,5},{8,10},{9,11},{10,... | collective-permute-start | bytes 737288 | tf_op jit(solution)/shard_map/ppermute | solution.py:396
  14.3 0.1 collective-permute-start.2
  14.4 12.8 %all_to_all.10.code_ref = s32[16,8,128]{2,1,0:T(8,128)S(1)} all-to-all(s32[16,8,128]{2,1,0:T(8,128)S(1)} %get-tuple-element.174), channel_id=1, replica_groups=mesh['groups'=2,'shell'=16] {'shell'}, dimensions={0} | all-to-all | bytes 131072 | tf_op jit(solution)/shard_map/all_to_all | solution.py:419
  27.2 0.0 collective-permute-done.refs_1_
  27.2 1.5 %pick_rows.1 = (bf16[128,1280]{1,0:T(8,128)(2,1)S(1)}, s32[1]{0:T(128)}, s32[1]{0:T(128)}, bf16[4,4,16,256]{3,2,1,0:T(8,128)(2,1)S(1)}) custom-call(s32[16,8,128]{2,1,0:T(8,128)S(1)} %all_to_all.10.code_ref, s32[1,256]{1,0:T(1,128)S(1)} %get-tuple-element.175.size_ref, bf16[96,1280]{1,0:T(8,128)(2,1)S(1)} %get-tuple-element.177.refs_0_, ...), custom_call_target="tpu_custom_call" | custom-call | flops 300000000 | bytes 2000000 | tf_op jit(solution)/shard_map/pick_rows/pallas_call | solution.py:421
  28.7 2.5 %collective-permute-start.3 = (bf16[128,1280]{1,0:T(8,128)(2,1)S(1)}, bf16[128,1280]{1,0:T(8,128)(2,1)S(1)}, u32[]{:S(2)}, u32[]{:S(2)}) collective-permute-start(bf16[128,1280]{1,0:T(8,128)(2,1)S(1)} %get-tuple-element.183.refs_0_), channel_id=1, source_target_pairs={{0,8},{1,9},{2,10},{3,11},{4,12},{5,13},{6,14},{7,15},{8,0},{9,1},... | collective-permute-start | bytes 983048 | tf_op jit(solution)/shard_map/ppermute | solution.py:396
  31.2 1.6 %collective-permute-start.4 = (bf16[128,1280]{1,0:T(8,128)(2,1)S(1)}, bf16[128,1280]{1,0:T(8,128)(2,1)S(1)}, u32[]{:S(2)}, u32[]{:S(2)}) collective-permute-start(bf16[128,1280]{1,0:T(8,128)(2,1)S(1)} %get-tuple-element.183.refs_0_), channel_id=1, source_target_pairs={{0,2},{1,3},{2,0},{3,1},{4,6},{5,7},{6,4},{7,5},{8,10},{9,11},{10,... | collective-permute-start | bytes 983048 | tf_op jit(solution)/shard_map/ppermute | solution.py:396
  32.7 1.6 %collective-permute-start.5 = (bf16[128,1280]{1,0:T(8,128)(2,1)S(1)}, bf16[128,1280]{1,0:T(8,128)(2,1)S(1)}, u32[]{:S(2)}, u32[]{:S(2)}) collective-permute-start(bf16[128,1280]{1,0:T(8,128)(2,1)S(1)} %get-tuple-element.183.refs_0_), channel_id=1, source_target_pairs={{0,4},{1,5},{2,6},{3,7},{4,0},{5,1},{6,2},{7,3},{8,12},{9,13},{10,... | collective-permute-start | bytes 983048 | tf_op jit(solution)/shard_map/ppermute | solution.py:396
  34.3 15.2 %all_to_all.11 = bf16[4,4,16,256]{3,2,1,0:T(8,128)(2,1)S(1)} all-to-all(bf16[4,4,16,256]{3,2,1,0:T(8,128)(2,1)S(1)} %get-tuple-element.184), channel_id=1, replica_groups={{0,4,8,12},{1,5,9,13},{2,6,10,14},{3,7,11,15},{16,20,24,28},{17,21,25,2..., dimensions={0} | all-to-all | bytes 262144 | tf_op jit(solution)/shard_map/all_to_all | solution.py:434
  49.5 0.0 collective-permute-done.3.refs_3_
  49.5 0.0 collective-permute-done.4.refs_1_
  49.5 0.1 collective-permute-start.9
  49.6 0.5 collective-permute-start.10
  50.1 0.1 collective-permute-start.11
  50.2 0.5 collective-permute-start.7
  50.6 1.2 %collective-permute-start.8 = (bf16[128,1280]{1,0:T(8,128)(2,1)S(1)}, bf16[128,1280]{1,0:T(8,128)(2,1)S(1)}, u32[]{:S(2)}, u32[]{:S(2)}) collective-permute-start(bf16[128,1280]{1,0:T(8,128)(2,1)S(1)} %collective-permute-done.5.refs_2_), channel_id=1, source_target_pairs={{0,2},{1,3},{2,0},{3,1},{4,6},{5,7},{6,4},{7,5},{8,10},{9,11},{10,... | collective-permute-start | bytes 983048 | tf_op jit(solution)/shard_map/ppermute | solution.py:396
  51.9 0.8 collective-permute-start.15
  52.7 7.6 %half_transform.1 = (f32[512,1024]{1,0:T(8,128)S(1)}, bf16[2,512,1024]{2,1,0:T(8,128)(2,1)S(1)}) custom-call(s32[16,8,128]{2,1,0:T(8,128)S(1)} %all_to_all.10.code_ref, bf16[16,16,256]{2,1,0:T(8,128)(2,1)S(1)} %bitcast.64, s32[1,256]{1,0:T(1,128)S(1)} %get-tuple-element.175.size_ref, bf16[128,1280]{1,0:T(8,128)(2,1)S(1)} %get-tuple-element.183.refs_0_, ...), custom_call_target="tpu_custom_call" | custom-call | flops 7000000000 | bytes 1 | tf_op jit(solution)/shard_map/half_transform/pallas_call | solution.py:444
  60.3 0.9 collective-permute-done.8.refs_4_
  61.2 0.5 collective-permute-start.14
  61.7 1.2 %collective-permute-start.12 = (bf16[128,1280]{1,0:T(8,128)(2,1)S(1)}, bf16[128,1280]{1,0:T(8,128)(2,1)S(1)}, u32[]{:S(2)}, u32[]{:S(2)}) collective-permute-start(bf16[128,1280]{1,0:T(8,128)(2,1)S(1)} %collective-permute-done.7.refs_5_), channel_id=1, source_target_pairs={{0,2},{1,3},{2,0},{3,1},{4,6},{5,7},{6,4},{7,5},{8,10},{9,11},{10,... | collective-permute-start | bytes 983048 | tf_op jit(solution)/shard_map/ppermute | solution.py:396
  62.9 5.3 %collective-permute-done.15.refs_0_ = bf16[128,1280]{1,0:T(8,128)(2,1)S(1)} collective-permute-done((bf16[128,1280]{1,0:T(8,128)(2,1)S(1)}, bf16[128,1280]{1,0:T(8,128)(2,1)S(1)}, u32[]{:S(2)}, u32[]{:S(2)}) %collective-permute-start.15) | collective-permute-done | bytes 327712 | tf_op jit(solution)/shard_map/ppermute | solution.py:396
  68.2 1.6 %gather_pieces.1 = (bf16[2,768,1152]{2,1,0:T(8,128)(2,1)S(1)}, f32[512,1024]{1,0:T(8,128)S(1)}) custom-call(s32[1]{0:T(128)} %get-tuple-element.182.me_ref, f32[512,1024]{1,0:T(8,128)S(1)} %get-tuple-element.193.part_ref, bf16[2,512,1024]{2,1,0:T(8,128)(2,1)S(1)} %get-tuple-element.194.late_ref.late_any, bf16[128,1280]{1,0:T(8,128)(2,1)S(1)} %get-tuple-element.183.refs_0_, ...), custom_call_target="tpu_custom_call" | custom-call | flops 1 | bytes 1 | tf_op jit(solution)/shard_map/gather_pieces/pallas_call | solution.py:469
  69.9 4.6 %collective-permute-done.12.refs_1_ = bf16[128,1280]{1,0:T(8,128)(2,1)S(1)} collective-permute-done((bf16[128,1280]{1,0:T(8,128)(2,1)S(1)}, bf16[128,1280]{1,0:T(8,128)(2,1)S(1)}, u32[]{:S(2)}, u32[]{:S(2)}) %collective-permute-start.12) | collective-permute-done | bytes 327712 | tf_op jit(solution)/shard_map/ppermute | solution.py:396
  74.5 1.6 %collective-permute-done.17.refs_3_ = bf16[128,1280]{1,0:T(8,128)(2,1)S(1)} collective-permute-done((bf16[128,1280]{1,0:T(8,128)(2,1)S(1)}, bf16[128,1280]{1,0:T(8,128)(2,1)S(1)}, u32[]{:S(2)}, u32[]{:S(2)}) %collective-permute-start.17) | collective-permute-done | bytes 327712 | tf_op jit(solution)/shard_map/ppermute | solution.py:396
  76.1 5.3 %last_product.1 = bf16[2,256,2304]{2,1,0:T(8,128)(2,1)} custom-call(s32[1]{0:T(128)} %get-tuple-element.182.me_ref, f32[512,1024]{1,0:T(8,128)S(1)} %get-tuple-element.198.part_ref, bf16[2,768,1152]{2,1,0:T(8,128)(2,1)S(1)} %get-tuple-element.199.right_ref, bf16[2,512,1024]{2,1,0:T(8,128)(2,1)S(1)} %get-tuple-element.194.late_ref.late_any, ...), custom_call_target="tpu_custom_call" | custom-call | flops 20000000000 | bytes 1 | tf_op jit(solution)/shard_map/last_product/pallas_call | solution.py:483
  81.4 0.6 while.17
  (19 shorter events, 0.0 us)
Async XLA Ops:
  7.2 0.7 copy-start
  8.7 0.9 %copy-start.1 = (bf16[8,32,256]{2,1,0:T(8,128)(2,1)S(1)}, bf16[8,32,256]{2,1,0:T(8,128)(2,1)}, u32[]{:S(2)}) copy-start(bf16[8,32,256]{2,1,0:T(8,128)(2,1)} %panels_ref) | copy-start | bytes 393220
  11.2 16.0 %collective-permute-start = (bf16[96,1280]{1,0:T(8,128)(2,1)S(1)}, bf16[96,1280]{1,0:T(8,128)(2,1)S(1)}, u32[]{:S(2)}, u32[]{:S(2)}) collective-permute-start(bf16[96,1280]{1,0:T(8,128)(2,1)S(1)} %get-tuple-element.178), channel_id=1, source_target_pairs={{0,1},{1,0},{2,3},{3,2},{4,5},{5,4},{6,7},{7,6},{8,9},{9,8},{10,11... | collective-permute-start | bytes 737288 | tf_op jit(solution)/shard_map/ppermute | solution.py:396
  11.7 15.5 %collective-permute-start.1 = (bf16[96,1280]{1,0:T(8,128)(2,1)S(1)}, bf16[96,1280]{1,0:T(8,128)(2,1)S(1)}, u32[]{:S(2)}, u32[]{:S(2)}) collective-permute-start(bf16[96,1280]{1,0:T(8,128)(2,1)S(1)} %get-tuple-element.179), channel_id=1, source_target_pairs={{0,2},{1,3},{2,0},{3,1},{4,6},{5,7},{6,4},{7,5},{8,10},{9,11},{10,... | collective-permute-start | bytes 737288 | tf_op jit(solution)/shard_map/ppermute | solution.py:396
  14.3 12.9 %collective-permute-start.2 = (bf16[96,1280]{1,0:T(8,128)(2,1)S(1)}, bf16[96,1280]{1,0:T(8,128)(2,1)S(1)}, u32[]{:S(2)}, u32[]{:S(2)}) collective-permute-start(bf16[96,1280]{1,0:T(8,128)(2,1)S(1)} %get-tuple-element.180), channel_id=1, source_target_pairs={{0,3},{1,2},{2,1},{3,0},{4,7},{5,6},{6,5},{7,4},{8,11},{9,10},{10,... | collective-permute-start | bytes 737288 | tf_op jit(solution)/shard_map/ppermute | solution.py:396
  28.7 20.8 %collective-permute-start.3 = (bf16[128,1280]{1,0:T(8,128)(2,1)S(1)}, bf16[128,1280]{1,0:T(8,128)(2,1)S(1)}, u32[]{:S(2)}, u32[]{:S(2)}) collective-permute-start(bf16[128,1280]{1,0:T(8,128)(2,1)S(1)} %get-tuple-element.183.refs_0_), channel_id=1, source_target_pairs={{0,8},{1,9},{2,10},{3,11},{4,12},{5,13},{6,14},{7,15},{8,0},{9,1},... | collective-permute-start | bytes 983048 | tf_op jit(solution)/shard_map/ppermute | solution.py:396
  31.2 18.4 %collective-permute-start.4 = (bf16[128,1280]{1,0:T(8,128)(2,1)S(1)}, bf16[128,1280]{1,0:T(8,128)(2,1)S(1)}, u32[]{:S(2)}, u32[]{:S(2)}) collective-permute-start(bf16[128,1280]{1,0:T(8,128)(2,1)S(1)} %get-tuple-element.183.refs_0_), channel_id=1, source_target_pairs={{0,2},{1,3},{2,0},{3,1},{4,6},{5,7},{6,4},{7,5},{8,10},{9,11},{10,... | collective-permute-start | bytes 983048 | tf_op jit(solution)/shard_map/ppermute | solution.py:396
  32.7 16.8 %collective-permute-start.5 = (bf16[128,1280]{1,0:T(8,128)(2,1)S(1)}, bf16[128,1280]{1,0:T(8,128)(2,1)S(1)}, u32[]{:S(2)}, u32[]{:S(2)}) collective-permute-start(bf16[128,1280]{1,0:T(8,128)(2,1)S(1)} %get-tuple-element.183.refs_0_), channel_id=1, source_target_pairs={{0,4},{1,5},{2,6},{3,7},{4,0},{5,1},{6,2},{7,3},{8,12},{9,13},{10,... | collective-permute-start | bytes 983048 | tf_op jit(solution)/shard_map/ppermute | solution.py:396
  34.3 15.2 %collective-permute-start.6 = (bf16[128,1280]{1,0:T(8,128)(2,1)S(1)}, bf16[128,1280]{1,0:T(8,128)(2,1)S(1)}, u32[]{:S(2)}, u32[]{:S(2)}) collective-permute-start(bf16[128,1280]{1,0:T(8,128)(2,1)S(1)} %get-tuple-element.183.refs_0_), channel_id=1, source_target_pairs={{0,1},{1,0},{2,3},{3,2},{4,5},{5,4},{6,7},{7,6},{8,9},{9,8},{10,11... | collective-permute-start | bytes 983048 | tf_op jit(solution)/shard_map/ppermute | solution.py:396
  49.5 2.3 %collective-permute-start.9 = (bf16[128,1280]{1,0:T(8,128)(2,1)S(1)}, bf16[128,1280]{1,0:T(8,128)(2,1)S(1)}, u32[]{:S(2)}, u32[]{:S(2)}) collective-permute-start(bf16[128,1280]{1,0:T(8,128)(2,1)S(1)} %collective-permute-done.4.refs_1_), channel_id=1, source_target_pairs={{0,1},{1,0},{2,3},{3,2},{4,5},{5,4},{6,7},{7,6},{8,9},{9,8},{10,11... | collective-permute-start | bytes 983048 | tf_op jit(solution)/shard_map/ppermute | solution.py:396
  49.6 3.1 %collective-permute-start.10 = (bf16[128,1280]{1,0:T(8,128)(2,1)S(1)}, bf16[128,1280]{1,0:T(8,128)(2,1)S(1)}, u32[]{:S(2)}, u32[]{:S(2)}) collective-permute-start(bf16[128,1280]{1,0:T(8,128)(2,1)S(1)} %collective-permute-done.5.refs_2_), channel_id=1, source_target_pairs={{0,1},{1,0},{2,3},{3,2},{4,5},{5,4},{6,7},{7,6},{8,9},{9,8},{10,11... | collective-permute-start | bytes 983048 | tf_op jit(solution)/shard_map/ppermute | solution.py:396
  50.1 2.6 %collective-permute-start.11 = (bf16[128,1280]{1,0:T(8,128)(2,1)S(1)}, bf16[128,1280]{1,0:T(8,128)(2,1)S(1)}, u32[]{:S(2)}, u32[]{:S(2)}) collective-permute-start(bf16[128,1280]{1,0:T(8,128)(2,1)S(1)} %collective-permute-done.3.refs_3_), channel_id=1, source_target_pairs={{0,1},{1,0},{2,3},{3,2},{4,5},{5,4},{6,7},{7,6},{8,9},{9,8},{10,11... | collective-permute-start | bytes 983048 | tf_op jit(solution)/shard_map/ppermute | solution.py:396
  50.2 10.1 %collective-permute-start.7 = (bf16[128,1280]{1,0:T(8,128)(2,1)S(1)}, bf16[128,1280]{1,0:T(8,128)(2,1)S(1)}, u32[]{:S(2)}, u32[]{:S(2)}) collective-permute-start(bf16[128,1280]{1,0:T(8,128)(2,1)S(1)} %collective-permute-done.3.refs_3_), channel_id=1, source_target_pairs={{0,4},{1,5},{2,6},{3,7},{4,0},{5,1},{6,2},{7,3},{8,12},{9,13},{10,... | collective-permute-start | bytes 983048 | tf_op jit(solution)/shard_map/ppermute | solution.py:396
  50.6 10.6 %collective-permute-start.8 = (bf16[128,1280]{1,0:T(8,128)(2,1)S(1)}, bf16[128,1280]{1,0:T(8,128)(2,1)S(1)}, u32[]{:S(2)}, u32[]{:S(2)}) collective-permute-start(bf16[128,1280]{1,0:T(8,128)(2,1)S(1)} %collective-permute-done.5.refs_2_), channel_id=1, source_target_pairs={{0,2},{1,3},{2,0},{3,1},{4,6},{5,7},{6,4},{7,5},{8,10},{9,11},{10,... | collective-permute-start | bytes 983048 | tf_op jit(solution)/shard_map/ppermute | solution.py:396
  51.9 16.4 %collective-permute-start.15 = (bf16[128,1280]{1,0:T(8,128)(2,1)S(1)}, bf16[128,1280]{1,0:T(8,128)(2,1)S(1)}, u32[]{:S(2)}, u32[]{:S(2)}) collective-permute-start(bf16[128,1280]{1,0:T(8,128)(2,1)S(1)} %collective-permute-done.3.refs_3_), channel_id=1, source_target_pairs={{0,2},{1,3},{2,0},{3,1},{4,6},{5,7},{6,4},{7,5},{8,10},{9,11},{10,... | collective-permute-start | bytes 983048 | tf_op jit(solution)/shard_map/ppermute | solution.py:396
  61.2 7.0 %collective-permute-start.13 = (bf16[128,1280]{1,0:T(8,128)(2,1)S(1)}, bf16[128,1280]{1,0:T(8,128)(2,1)S(1)}, u32[]{:S(2)}, u32[]{:S(2)}) collective-permute-start(bf16[128,1280]{1,0:T(8,128)(2,1)S(1)} %collective-permute-done.8.refs_4_), channel_id=1, source_target_pairs={{0,1},{1,0},{2,3},{3,2},{4,5},{5,4},{6,7},{7,6},{8,9},{9,8},{10,11... | collective-permute-start | bytes 983048 | tf_op jit(solution)/shard_map/ppermute | solution.py:396
  61.2 7.0 %collective-permute-start.14 = (bf16[128,1280]{1,0:T(8,128)(2,1)S(1)}, bf16[128,1280]{1,0:T(8,128)(2,1)S(1)}, u32[]{:S(2)}, u32[]{:S(2)}) collective-permute-start(bf16[128,1280]{1,0:T(8,128)(2,1)S(1)} %collective-permute-done.7.refs_5_), channel_id=1, source_target_pairs={{0,1},{1,0},{2,3},{3,2},{4,5},{5,4},{6,7},{7,6},{8,9},{9,8},{10,11... | collective-permute-start | bytes 983048 | tf_op jit(solution)/shard_map/ppermute | solution.py:396
  61.7 12.8 %collective-permute-start.12 = (bf16[128,1280]{1,0:T(8,128)(2,1)S(1)}, bf16[128,1280]{1,0:T(8,128)(2,1)S(1)}, u32[]{:S(2)}, u32[]{:S(2)}) collective-permute-start(bf16[128,1280]{1,0:T(8,128)(2,1)S(1)} %collective-permute-done.7.refs_5_), channel_id=1, source_target_pairs={{0,2},{1,3},{2,0},{3,1},{4,6},{5,7},{6,4},{7,5},{8,10},{9,11},{10,... | collective-permute-start | bytes 983048 | tf_op jit(solution)/shard_map/ppermute | solution.py:396
  68.2 6.3 %collective-permute-start.16 = (bf16[128,1280]{1,0:T(8,128)(2,1)S(1)}, bf16[128,1280]{1,0:T(8,128)(2,1)S(1)}, u32[]{:S(2)}, u32[]{:S(2)}) collective-permute-start(bf16[128,1280]{1,0:T(8,128)(2,1)S(1)} %collective-permute-done.15.refs_0_), channel_id=1, source_target_pairs={{0,1},{1,0},{2,3},{3,2},{4,5},{5,4},{6,7},{7,6},{8,9},{9,8},{10,11... | collective-permute-start | bytes 983048 | tf_op jit(solution)/shard_map/ppermute | solution.py:396
  74.5 7.0 %copy-start.3 = (s32[256]{0:T(256)S(1)}, s32[256]{0:T(256)}, u32[]{:S(2)}) copy-start(s32[256]{0:T(256)} %param.11) | copy-start | bytes 3076
  74.5 1.6 %collective-permute-start.17 = (bf16[128,1280]{1,0:T(8,128)(2,1)S(1)}, bf16[128,1280]{1,0:T(8,128)(2,1)S(1)}, u32[]{:S(2)}, u32[]{:S(2)}) collective-permute-start(bf16[128,1280]{1,0:T(8,128)(2,1)S(1)} %collective-permute-done.12.refs_1_), channel_id=1, source_target_pairs={{0,1},{1,0},{2,3},{3,2},{4,5},{5,4},{6,7},{7,6},{8,9},{9,8},{10,11... | collective-permute-start | bytes 983048 | tf_op jit(solution)/shard_map/ppermute | solution.py:396

commit v22 on v20

--- a/solution.py
+++ b/solution.py
@@ -162,7 +162,7 @@
 
 
 def pick_kernel(here, code_ref, size_ref, *refs):
-    sources, (out_ref, over_ref, me_ref, panel_ref) = refs[:4], refs[4:]
+    sources, (out_ref, over_ref, me_ref), panel_refs = refs[:4], refs[4:7], refs[7:]
     me = lax.axis_index("shell")
     me_ref[0] = me
     core, y, z = lax.rem(me, 2), lax.rem(lax.div(me, 2), 2), lax.div(me, 4)
@@ -187,8 +187,9 @@
     for k, source in enumerate(sources):
         member = 2 * lax.rem(y + k // 2, 2) + lax.rem(core + k % 2, 2)
         device = 4 * z + member
-        for to_z in range(Z):
-            panel_ref[to_z, member] = source[rows:, to_z * EDGE * EDGE : (to_z + 1) * EDGE * EDGE]
+        for r, panel_ref in enumerate(panel_refs):
+            lanes = pl.ds(pl.multiple_of((z ^ r) * (EDGE * EDGE), 128), EDGE * EDGE)
+            panel_ref[member] = source[rows:, lanes]
         row = (2 * iota((shell_count, 128), 1) + device * here + y).astype(F32)
         where = row - shells.starts
         inside = (where >= 0.0) & (where < shells.size)
@@ -213,11 +214,12 @@
     return jnp.where((rel == 5) | (rel == 6), rel ^ 3, early)
 
 
-def half_kernel(here, early, code_ref, got_ref, size_ref, *refs):
-    pieces, refs = refs[: 2 * early], refs[2 * early :]
-    half_ref, late_ref, occ_ref, part_ref, hot_ref, placed_ref, sems = refs
+def half_kernel(here, early, code_ref, size_ref, *refs):
+    panel_refs, pieces, refs = refs[:Z], refs[Z : Z + 2 * early], refs[Z + 2 * early :]
+    half_ref, late_ref, all_ref, got_ref, occ_ref, part_ref, hot_ref, placed_ref, sems = refs
     me = lax.axis_index("shell")
     core, chip = lax.rem(me, CORES), lax.div(me, CORES)
+    z = lax.div(chip, Y)
     width = pieces[0].shape[1] - 128
     copies = []
     for far in range(2):
@@ -228,6 +230,9 @@
             copies.append(pltpu.make_async_copy(pieces[at].at[:, pl.ds(width, 128)], target, sems.at[at]))
     for copy in copies:
         copy.start()
+    for r, panel_ref in enumerate(panel_refs):
+        got_ref[pl.ds((z ^ r) * (Y * CORES), Y * CORES)] = panel_ref[...]
+    all_ref[...] = got_ref[...]
     window = CORES * Y * here
     shell_count = size_ref.shape[1]
     got = got_ref[...].astype(F32)
@@ -416,39 +421,42 @@
     )(block_pairs.T, block_count.reshape(1, 1))
     code = lax.all_to_all(code, "shell", split_axis=0, concat_axis=0, tiled=True)
 
-    mine, over, me, panel = pl.pallas_call(
+    mine, over, me, *panel = pl.pallas_call(
         functools.partial(pick_kernel, here),
         out_shape=[shape(CAP, packed), shape(1, dtype=jnp.int32), shape(1, dtype=jnp.int32)]
-        + [shape(Z, Y * CORES, 2 * BLK_DEV, EDGE * EDGE)],
+        + [shape(Y * CORES, 2 * BLK_DEV, EDGE * EDGE)] * Z,
         in_specs=[VMEM] * 6,
-        out_specs=[VMEM, SMEM, SMEM, VMEM],
+        out_specs=[VMEM, SMEM, SMEM] + [VMEM] * Z,
         compiler_params=params(12),
         cost_estimate=cost(3e8, 2e6),
         name="pick_rows",
     )(code, size_row, keep, to_core, to_y, to_both)
 
     across, mine_y, beside = swap(mine, 8), swap(mine, 2), swap(mine, 4)
-    lines = [[Y * CORES * z + k for z in range(Z)] for k in range(Y * CORES)]
-    got = lax.all_to_all(panel, "shell", split_axis=0, concat_axis=0, axis_index_groups=lines, tiled=True)
-    got = got.reshape(n, 2 * BLK_DEV, EDGE * EDGE)
-    far = [swap(mine, 1)]
-    across, mine_y, beside, got, *far = lax.optimization_barrier((across, mine_y, beside, got, *far))
+    panel = [panel[0]] + [swap(panel[r], 4 * r) for r in range(1, Z)]
+    across, mine_y, beside, *panel = lax.optimization_barrier((across, mine_y, beside, *panel))
 
     corner, beside_y, across_y = swap(across, 4), swap(beside, 2), swap(across, 2)
     near = [mine, mine_y, beside, across]
-    far += [swap(piece, 1) for piece in near[1:]]
+    far = [swap(piece, 1) for piece in near]
     early = len(near)
     slots = LIVE_DEV * n * EDGE
-    half, late = pl.pallas_call(
+    half, late, got = pl.pallas_call(
         functools.partial(half_kernel, here, early),
-        out_shape=(shape(2 * NOCC, room, dtype=F32), shape(2, room - early * CAP, room)),
+        out_shape=(
+            shape(2 * NOCC, room, dtype=F32),
+            shape(2, room - early * CAP, room),
+            shape(n, 2 * BLK_DEV, EDGE * EDGE),
+        ),
         grid=(1,),
-        in_specs=[VMEM] * 3 + [ANY] * (2 * early),
+        in_specs=[VMEM] * (2 + Z) + [ANY] * (2 * early),
         out_specs=(
             pl.BlockSpec((2 * NOCC, room), lambda i: (0, 0)),
             pl.BlockSpec((2, room - early * CAP, room), lambda i: (0, 0, 0)),
+            pl.BlockSpec((n, 2 * BLK_DEV, EDGE * EDGE), lambda i: (0, 0, 0)),
         ),
         scratch_shapes=[
+            pltpu.VMEM((n, 2 * BLK_DEV, EDGE * EDGE), BF16),
             pltpu.VMEM((early * CAP, NOCC), BF16),
             pltpu.VMEM((NOCC, slots), BF16),
             pltpu.VMEM((room - early * CAP, slots), BF16),
@@ -458,7 +466,7 @@
         compiler_params=params(30),
         cost_estimate=cost(7e9, 1),
         name="half_transform",
-    )(code, got, size_row, *near, *far)
+    )(code, size_row, *panel, *near, *far)
     corner, beside_y, half, late = lax.optimization_barrier((corner, beside_y, half, late))
     corner_y = swap(corner, 2)
     near += [beside_y, corner]

time: 88.5 us -> 93.6 us (1.058)
  waiting for transfers between devices: 12.6 us -> 31.4 us
  blocking collectives: 29 us -> 12.8 us
  starting transfers between devices: 11.1 us -> 13.5 us
    ppermute x18 -> x21, waiting for transfers between devices: 12.6 us -> 31.4 us  [swap(): return lax.ppermute(array, 'shell', [(i, i ^ bit) for i in range(n)])]
    all_to_all x1 -> x0, blocking collectives: 16.1 us -> none  [short_way(): lax.all_to_all(panel, 'shell', split_axis=0, concat_axis=0, axis_index_gr...]
    ppermute x18 -> x21, starting transfers between devices: 11.1 us -> 13.5 us  [swap(): return lax.ppermute(array, 'shell', [(i, i ^ bit) for i in range(n)])]
  transfers between devices with their start and end apart: 18 -> 21, of which waited for: 5 -> 7; matrix products, arithmetic and copies ran while one was open for 0% -> 0% of each run, Pallas kernels for 11% -> 11%
where the time goes in v22:
time: 93.6 us; the launch traced here: 93.4 us
  waiting for transfers between devices  31.4 us (34%)
  Pallas kernels  19.3 us (21%)
  between operations  14.2 us (15%)
  starting transfers between devices  13.5 us (14%)
  blocking collectives  12.8 us (14%)
  local copies, waits for them, and re-layouts  1.58 us (2%)
    ppermute x21, waiting for transfers between devices, swap(): return lax.ppermute(array, 'shell', [(i, i ^ bit) for i in range(n)])  31.4 us
    ppermute x21, starting transfers between devices, swap(): return lax.ppermute(array, 'shell', [(i, i ^ bit) for i in range(n)])  13.5 us
    all_to_all x1, blocking collectives, short_way(): lax.all_to_all(code, 'shell', split_axis=0, concat_axis=0, tiled=True)  12.8 us
    pallas_call x1, Pallas kernels, short_way(): pl.pallas_call(functools.partial(half_kernel, here, early), out_shape=(sh...  8.29 us
    pallas_call x1, Pallas kernels, short_way(): pl.pallas_call(last_kernel, out_shape=shape(2, NOCC, nvir), in_specs=[SME...  5.5 us
    pallas_call x1, Pallas kernels, short_way(): pl.pallas_call(functools.partial(pick_kernel, here), out_shape=[shape(CAP...  2.16 us
  transfers between devices with their start and end apart: 21, of which 7 were waited for; matrix products, arithmetic and copies ran while one was open for 0% of the time, Pallas kernels for 11%

profile of v22, /device:TPU:0, one launch (start us, length us, event | category | flops | bytes accessed | tf_op | source)
XLA Modules:
  0.0 93.4 jit_solution(17427408450565384399)
XLA Ops:
  6.5 0.9 copy-done.1
  7.4 1.6 %pack_rows.1 = (bf16[96,1280]{1,0:T(8,128)(2,1)S(1)}, bf16[96,1280]{1,0:T(8,128)(2,1)S(1)}, bf16[96,1280]{1,0:T(8,128)(2,1)S(1)}, bf16[96,1280]{1,0:T(8,128)(2,1)S(1)}) custom-call(bf16[160,2304]{1,0:T(8,128)(2,1)} %vir_ref.1, bf16[160,256]{1,0:T(8,128)(2,1)} %occ_ref.1, bf16[8,32,256]{2,1,0:T(8,128)(2,1)S(1)} %copy-done.1), custom_call_target="tpu_custom_call" | custom-call | flops 300000000 | bytes 3000000 | tf_op jit(solution)/shard_map/pack_rows/pallas_call | solution.py:402
  9.0 0.5 collective-permute-start
  9.5 2.6 %collective-permute-start.1 = (bf16[96,1280]{1,0:T(8,128)(2,1)S(1)}, bf16[96,1280]{1,0:T(8,128)(2,1)S(1)}, u32[]{:S(2)}, u32[]{:S(2)}) collective-permute-start(bf16[96,1280]{1,0:T(8,128)(2,1)S(1)} %get-tuple-element.177), channel_id=1, source_target_pairs={{0,2},{1,3},{2,0},{3,1},{4,6},{5,7},{6,4},{7,5},{8,10},{9,11},{10,... | collective-permute-start | bytes 737288 | tf_op jit(solution)/shard_map/ppermute | solution.py:400
  12.9 0.7 copy-done
  13.5 0.2 pack_ids.1
  13.7 12.8 %all_to_all.5.code_ref = s32[16,8,128]{2,1,0:T(8,128)S(1)} all-to-all(s32[16,8,128]{2,1,0:T(8,128)S(1)} %pack_ids.1), channel_id=1, replica_groups=mesh['groups'=2,'shell'=16] {'shell'}, dimensions={0} | all-to-all | bytes 131072 | tf_op jit(solution)/shard_map/all_to_all | solution.py:422
  26.5 2.2 %pick_rows.1 = (bf16[128,1280]{1,0:T(8,128)(2,1)S(1)}, s32[1]{0:T(128)}, s32[1]{0:T(128)}, bf16[4,16,256]{2,1,0:T(8,128)(2,1)S(1)}, bf16[4,16,256]{2,1,0:T(8,128...) custom-call(s32[16,8,128]{2,1,0:T(8,128)S(1)} %all_to_all.5.code_ref, s32[1,256]{1,0:T(1,128)} %bitcast.63, ...), custom_call_target="tpu_custom_call" | custom-call | flops 300000000 | bytes 2000000 | tf_op jit(solution)/shard_map/pick_rows/pallas_call | solution.py:424
  28.7 1.0 %collective-permute-start.3 = (bf16[128,1280]{1,0:T(8,128)(2,1)S(1)}, bf16[128,1280]{1,0:T(8,128)(2,1)S(1)}, u32[]{:S(2)}, u32[]{:S(2)}) collective-permute-start(bf16[128,1280]{1,0:T(8,128)(2,1)S(1)} %get-tuple-element.181.refs_4_.refs_0_), channel_id=1, source_target_pairs={{0,8},{1,9},{2,10},{3,11},{4,12},{5,13},{6,14},{7,15},{8,0},{9,1},... | collective-permute-start | bytes 983048 | tf_op jit(solution)/shard_map/ppermute | solution.py:400
  29.7 1.6 %collective-permute-start.4 = (bf16[128,1280]{1,0:T(8,128)(2,1)S(1)}, bf16[128,1280]{1,0:T(8,128)(2,1)S(1)}, u32[]{:S(2)}, u32[]{:S(2)}) collective-permute-start(bf16[128,1280]{1,0:T(8,128)(2,1)S(1)} %get-tuple-element.181.refs_4_.refs_0_), channel_id=1, source_target_pairs={{0,2},{1,3},{2,0},{3,1},{4,6},{5,7},{6,4},{7,5},{8,10},{9,11},{10,... | collective-permute-start | bytes 983048 | tf_op jit(solution)/shard_map/ppermute | solution.py:400
  31.2 1.6 %collective-permute-start.5 = (bf16[128,1280]{1,0:T(8,128)(2,1)S(1)}, bf16[128,1280]{1,0:T(8,128)(2,1)S(1)}, u32[]{:S(2)}, u32[]{:S(2)}) collective-permute-start(bf16[128,1280]{1,0:T(8,128)(2,1)S(1)} %get-tuple-element.181.refs_4_.refs_0_), channel_id=1, source_target_pairs={{0,4},{1,5},{2,6},{3,7},{4,0},{5,1},{6,2},{7,3},{8,12},{9,13},{10,... | collective-permute-start | bytes 983048 | tf_op jit(solution)/shard_map/ppermute | solution.py:400
  32.8 0.5 collective-permute-start.6
  33.3 0.6 collective-permute-start.7
  33.8 14.4 %collective-permute-done.6.refs_1_ = bf16[4,16,256]{2,1,0:T(8,128)(2,1)S(1)} collective-permute-done((bf16[4,16,256]{2,1,0:T(8,128)(2,1)S(1)}, bf16[4,16,256]{2,1,0:T(8,128)(2,1)S(1)}, u32[]{:S(2)}, u32[]{:S(2)}) %collective-permute-start.6) | collective-permute-done | bytes 32800 | tf_op jit(solution)/shard_map/ppermute | solution.py:400
  48.3 1.6 %collective-permute-start.8 = (bf16[4,16,256]{2,1,0:T(8,128)(2,1)S(1)}, bf16[4,16,256]{2,1,0:T(8,128)(2,1)S(1)}, u32[]{:S(2)}, u32[]{:S(2)}) collective-permute-start(bf16[4,16,256]{2,1,0:T(8,128)(2,1)S(1)} %get-tuple-element.185), channel_id=1, source_target_pairs={{0,12},{1,13},{2,14},{3,15},{4,8},{5,9},{6,10},{7,11},{8,4},{9,5},... | collective-permute-start | bytes 98312 | tf_op jit(solution)/shard_map/ppermute | solution.py:400
  49.9 4.1 %collective-permute-done.8.refs_3_ = bf16[4,16,256]{2,1,0:T(8,128)(2,1)S(1)} collective-permute-done((bf16[4,16,256]{2,1,0:T(8,128)(2,1)S(1)}, bf16[4,16,256]{2,1,0:T(8,128)(2,1)S(1)}, u32[]{:S(2)}, u32[]{:S(2)}) %collective-permute-start.8) | collective-permute-done | bytes 32800 | tf_op jit(solution)/shard_map/ppermute | solution.py:400
  54.0 0.1 collective-permute-start.12
  54.1 0.5 collective-permute-start.13
  54.6 0.1 collective-permute-start.14
  54.7 0.5 collective-permute-start.10
  55.2 0.5 collective-permute-done.12.refs_9_.refs_7_
  55.7 1.0 %collective-permute-start.18 = (bf16[128,1280]{1,0:T(8,128)(2,1)S(1)}, bf16[128,1280]{1,0:T(8,128)(2,1)S(1)}, u32[]{:S(2)}, u32[]{:S(2)}) collective-permute-start(bf16[128,1280]{1,0:T(8,128)(2,1)S(1)} %collective-permute-done.3.refs_7_.refs_3_), channel_id=1, source_target_pairs={{0,2},{1,3},{2,0},{3,1},{4,6},{5,7},{6,4},{7,5},{8,10},{9,11},{10,... | collective-permute-start | bytes 983048 | tf_op jit(solution)/shard_map/ppermute | solution.py:400
  56.7 8.3 %half_transform.1 = (f32[512,1024]{1,0:T(8,128)S(1)}, bf16[2,512,1024]{2,1,0:T(8,128)(2,1)S(1)}, bf16[16,16,256]{2,1,0:T(8,128)(2,1)S(1)}) custom-call(s32[16,8,128]{2,1,0:T(8,128)S(1)} %all_to_all.5.code_ref, s32[1,256]{1,0:T(1,128)} %bitcast.64, bf16[4,16,256]{2,1,0:T(8,128)(2,1)S(1)} %get-tuple-element.188.refs_0_, ...), custom_call_target="tpu_custom_call" | custom-call | flops 7000000000 | bytes 1 | tf_op jit(solution)/shard_map/half_transform/pallas_call | solution.py:444
  65.0 0.2 collective-permute-done.10.refs_4_
  65.2 0.5 collective-permute-start.17
  65.7 0.9 collective-permute-start.15
  66.6 5.6 %collective-permute-done.18.refs_0_ = bf16[128,1280]{1,0:T(8,128)(2,1)S(1)} collective-permute-done((bf16[128,1280]{1,0:T(8,128)(2,1)S(1)}, bf16[128,1280]{1,0:T(8,128)(2,1)S(1)}, u32[]{:S(2)}, u32[]{:S(2)}) %collective-permute-start.18) | collective-permute-done | bytes 327712 | tf_op jit(solution)/shard_map/ppermute | solution.py:400
  72.2 1.6 %gather_pieces.1 = (bf16[2,768,1152]{2,1,0:T(8,128)(2,1)S(1)}, f32[512,1024]{1,0:T(8,128)S(1)}) custom-call(s32[1]{0:T(128)} %get-tuple-element.180.me_ref, f32[512,1024]{1,0:T(8,128)S(1)} %get-tuple-element.196.part_ref, bf16[2,512,1024]{2,1,0:T(8,128)(2,1)S(1)} %get-tuple-element.197.late_ref.late_any, ...), custom_call_target="tpu_custom_call" | custom-call | flops 1 | bytes 1 | tf_op jit(solution)/shard_map/gather_pieces/pallas_call | solution.py:475
  73.9 4.9 %collective-permute-done.15.refs_1_ = bf16[128,1280]{1,0:T(8,128)(2,1)S(1)} collective-permute-done((bf16[128,1280]{1,0:T(8,128)(2,1)S(1)}, bf16[128,1280]{1,0:T(8,128)(2,1)S(1)}, u32[]{:S(2)}, u32[]{:S(2)}) %collective-permute-start.15) | collective-permute-done | bytes 327712 | tf_op jit(solution)/shard_map/ppermute | solution.py:400
  78.8 1.6 %collective-permute-done.20.refs_3_ = bf16[128,1280]{1,0:T(8,128)(2,1)S(1)} collective-permute-done((bf16[128,1280]{1,0:T(8,128)(2,1)S(1)}, bf16[128,1280]{1,0:T(8,128)(2,1)S(1)}, u32[]{:S(2)}, u32[]{:S(2)}) %collective-permute-start.20) | collective-permute-done | bytes 327712 | tf_op jit(solution)/shard_map/ppermute | solution.py:400
  80.4 5.5 %last_product.1 = bf16[2,256,2304]{2,1,0:T(8,128)(2,1)} custom-call(s32[1]{0:T(128)} %get-tuple-element.180.me_ref, f32[512,1024]{1,0:T(8,128)S(1)} %get-tuple-element.201.part_ref, bf16[2,768,1152]{2,1,0:T(8,128)(2,1)S(1)} %get-tuple-element.202.right_ref, bf16[2,512,1024]{2,1,0:T(8,128)(2,1)S(1)} %get-tuple-element.197.late_ref.late_any, ...), custom_call_target="tpu_custom_call" | custom-call | flops 20000000000 | bytes 1 | tf_op jit(solution)/shard_map/last_product/pallas_call | solution.py:489
  85.9 0.6 while.17
  (24 shorter events, 0.1 us)
Async XLA Ops:
  6.5 0.9 copy-start.1
  9.0 17.5 %collective-permute-start = (bf16[96,1280]{1,0:T(8,128)(2,1)S(1)}, bf16[96,1280]{1,0:T(8,128)(2,1)S(1)}, u32[]{:S(2)}, u32[]{:S(2)}) collective-permute-start(bf16[96,1280]{1,0:T(8,128)(2,1)S(1)} %get-tuple-element.176), channel_id=1, source_target_pairs={{0,1},{1,0},{2,3},{3,2},{4,5},{5,4},{6,7},{7,6},{8,9},{9,8},{10,11... | collective-permute-start | bytes 737288 | tf_op jit(solution)/shard_map/ppermute | solution.py:400
  9.5 17.0 %collective-permute-start.1 = (bf16[96,1280]{1,0:T(8,128)(2,1)S(1)}, bf16[96,1280]{1,0:T(8,128)(2,1)S(1)}, u32[]{:S(2)}, u32[]{:S(2)}) collective-permute-start(bf16[96,1280]{1,0:T(8,128)(2,1)S(1)} %get-tuple-element.177), channel_id=1, source_target_pairs={{0,2},{1,3},{2,0},{3,1},{4,6},{5,7},{6,4},{7,5},{8,10},{9,11},{10,... | collective-permute-start | bytes 737288 | tf_op jit(solution)/shard_map/ppermute | solution.py:400
  12.1 14.4 %collective-permute-start.2 = (bf16[96,1280]{1,0:T(8,128)(2,1)S(1)}, bf16[96,1280]{1,0:T(8,128)(2,1)S(1)}, u32[]{:S(2)}, u32[]{:S(2)}) collective-permute-start(bf16[96,1280]{1,0:T(8,128)(2,1)S(1)} %get-tuple-element.178), channel_id=1, source_target_pairs={{0,3},{1,2},{2,1},{3,0},{4,7},{5,6},{6,5},{7,4},{8,11},{9,10},{10,... | collective-permute-start | bytes 737288 | tf_op jit(solution)/shard_map/ppermute | solution.py:400
  12.9 0.7 copy-start
  28.7 25.3 %collective-permute-start.3 = (bf16[128,1280]{1,0:T(8,128)(2,1)S(1)}, bf16[128,1280]{1,0:T(8,128)(2,1)S(1)}, u32[]{:S(2)}, u32[]{:S(2)}) collective-permute-start(bf16[128,1280]{1,0:T(8,128)(2,1)S(1)} %get-tuple-element.181.refs_4_.refs_0_), channel_id=1, source_target_pairs={{0,8},{1,9},{2,10},{3,11},{4,12},{5,13},{6,14},{7,15},{8,0},{9,1},... | collective-permute-start | bytes 983048 | tf_op jit(solution)/shard_map/ppermute | solution.py:400
  29.7 24.3 %collective-permute-start.4 = (bf16[128,1280]{1,0:T(8,128)(2,1)S(1)}, bf16[128,1280]{1,0:T(8,128)(2,1)S(1)}, u32[]{:S(2)}, u32[]{:S(2)}) collective-permute-start(bf16[128,1280]{1,0:T(8,128)(2,1)S(1)} %get-tuple-element.181.refs_4_.refs_0_), channel_id=1, source_target_pairs={{0,2},{1,3},{2,0},{3,1},{4,6},{5,7},{6,4},{7,5},{8,10},{9,11},{10,... | collective-permute-start | bytes 983048 | tf_op jit(solution)/shard_map/ppermute | solution.py:400
  31.2 22.8 %collective-permute-start.5 = (bf16[128,1280]{1,0:T(8,128)(2,1)S(1)}, bf16[128,1280]{1,0:T(8,128)(2,1)S(1)}, u32[]{:S(2)}, u32[]{:S(2)}) collective-permute-start(bf16[128,1280]{1,0:T(8,128)(2,1)S(1)} %get-tuple-element.181.refs_4_.refs_0_), channel_id=1, source_target_pairs={{0,4},{1,5},{2,6},{3,7},{4,0},{5,1},{6,2},{7,3},{8,12},{9,13},{10,... | collective-permute-start | bytes 983048 | tf_op jit(solution)/shard_map/ppermute | solution.py:400
  32.8 15.5 %collective-permute-start.6 = (bf16[4,16,256]{2,1,0:T(8,128)(2,1)S(1)}, bf16[4,16,256]{2,1,0:T(8,128)(2,1)S(1)}, u32[]{:S(2)}, u32[]{:S(2)}) collective-permute-start(bf16[4,16,256]{2,1,0:T(8,128)(2,1)S(1)} %get-tuple-element.183), channel_id=1, source_target_pairs={{0,4},{1,5},{2,6},{3,7},{4,0},{5,1},{6,2},{7,3},{8,12},{9,13},{10,... | collective-permute-start | bytes 98312 | tf_op jit(solution)/shard_map/ppermute | solution.py:400
  33.3 16.6 %collective-permute-start.7 = (bf16[4,16,256]{2,1,0:T(8,128)(2,1)S(1)}, bf16[4,16,256]{2,1,0:T(8,128)(2,1)S(1)}, u32[]{:S(2)}, u32[]{:S(2)}) collective-permute-start(bf16[4,16,256]{2,1,0:T(8,128)(2,1)S(1)} %get-tuple-element.184), channel_id=1, source_target_pairs={{0,8},{1,9},{2,10},{3,11},{4,12},{5,13},{6,14},{7,15},{8,0},{9,1},... | collective-permute-start | bytes 98312 | tf_op jit(solution)/shard_map/ppermute | solution.py:400
  48.3 5.7 %collective-permute-start.8 = (bf16[4,16,256]{2,1,0:T(8,128)(2,1)S(1)}, bf16[4,16,256]{2,1,0:T(8,128)(2,1)S(1)}, u32[]{:S(2)}, u32[]{:S(2)}) collective-permute-start(bf16[4,16,256]{2,1,0:T(8,128)(2,1)S(1)} %get-tuple-element.185), channel_id=1, source_target_pairs={{0,12},{1,13},{2,14},{3,15},{4,8},{5,9},{6,10},{7,11},{8,4},{9,5},... | collective-permute-start | bytes 98312 | tf_op jit(solution)/shard_map/ppermute | solution.py:400
  49.9 4.8 %collective-permute-start.11 = (bf16[128,1280]{1,0:T(8,128)(2,1)S(1)}, bf16[128,1280]{1,0:T(8,128)(2,1)S(1)}, u32[]{:S(2)}, u32[]{:S(2)}) collective-permute-start(bf16[128,1280]{1,0:T(8,128)(2,1)S(1)} %get-tuple-element.181.refs_4_.refs_0_), channel_id=1, source_target_pairs={{0,1},{1,0},{2,3},{3,2},{4,5},{5,4},{6,7},{7,6},{8,9},{9,8},{10,11... | collective-permute-start | bytes 983048 | tf_op jit(solution)/shard_map/ppermute | solution.py:400
  54.0 1.7 %collective-permute-start.12 = (bf16[128,1280]{1,0:T(8,128)(2,1)S(1)}, bf16[128,1280]{1,0:T(8,128)(2,1)S(1)}, u32[]{:S(2)}, u32[]{:S(2)}) collective-permute-start(bf16[128,1280]{1,0:T(8,128)(2,1)S(1)} %collective-permute-done.4.refs_5_.refs_1_), channel_id=1, source_target_pairs={{0,1},{1,0},{2,3},{3,2},{4,5},{5,4},{6,7},{7,6},{8,9},{9,8},{10,11... | collective-permute-start | bytes 983048 | tf_op jit(solution)/shard_map/ppermute | solution.py:400
  54.1 2.6 %collective-permute-start.13 = (bf16[128,1280]{1,0:T(8,128)(2,1)S(1)}, bf16[128,1280]{1,0:T(8,128)(2,1)S(1)}, u32[]{:S(2)}, u32[]{:S(2)}) collective-permute-start(bf16[128,1280]{1,0:T(8,128)(2,1)S(1)} %collective-permute-done.5.refs_6_.refs_2_), channel_id=1, source_target_pairs={{0,1},{1,0},{2,3},{3,2},{4,5},{5,4},{6,7},{7,6},{8,9},{9,8},{10,11... | collective-permute-start | bytes 983048 | tf_op jit(solution)/shard_map/ppermute | solution.py:400
  54.6 2.1 %collective-permute-start.14 = (bf16[128,1280]{1,0:T(8,128)(2,1)S(1)}, bf16[128,1280]{1,0:T(8,128)(2,1)S(1)}, u32[]{:S(2)}, u32[]{:S(2)}) collective-permute-start(bf16[128,1280]{1,0:T(8,128)(2,1)S(1)} %collective-permute-done.3.refs_7_.refs_3_), channel_id=1, source_target_pairs={{0,1},{1,0},{2,3},{3,2},{4,5},{5,4},{6,7},{7,6},{8,9},{9,8},{10,11... | collective-permute-start | bytes 983048 | tf_op jit(solution)/shard_map/ppermute | solution.py:400
  54.7 10.3 %collective-permute-start.9 = (bf16[128,1280]{1,0:T(8,128)(2,1)S(1)}, bf16[128,1280]{1,0:T(8,128)(2,1)S(1)}, u32[]{:S(2)}, u32[]{:S(2)}) collective-permute-start(bf16[128,1280]{1,0:T(8,128)(2,1)S(1)} %collective-permute-done.3.refs_7_.refs_3_), channel_id=1, source_target_pairs={{0,4},{1,5},{2,6},{3,7},{4,0},{5,1},{6,2},{7,3},{8,12},{9,13},{10,... | collective-permute-start | bytes 983048 | tf_op jit(solution)/shard_map/ppermute | solution.py:400
  54.7 10.5 %collective-permute-start.10 = (bf16[128,1280]{1,0:T(8,128)(2,1)S(1)}, bf16[128,1280]{1,0:T(8,128)(2,1)S(1)}, u32[]{:S(2)}, u32[]{:S(2)}) collective-permute-start(bf16[128,1280]{1,0:T(8,128)(2,1)S(1)} %collective-permute-done.5.refs_6_.refs_2_), channel_id=1, source_target_pairs={{0,2},{1,3},{2,0},{3,1},{4,6},{5,7},{6,4},{7,5},{8,10},{9,11},{10,... | collective-permute-start | bytes 983048 | tf_op jit(solution)/shard_map/ppermute | solution.py:400
  55.7 16.5 %collective-permute-start.18 = (bf16[128,1280]{1,0:T(8,128)(2,1)S(1)}, bf16[128,1280]{1,0:T(8,128)(2,1)S(1)}, u32[]{:S(2)}, u32[]{:S(2)}) collective-permute-start(bf16[128,1280]{1,0:T(8,128)(2,1)S(1)} %collective-permute-done.3.refs_7_.refs_3_), channel_id=1, source_target_pairs={{0,2},{1,3},{2,0},{3,1},{4,6},{5,7},{6,4},{7,5},{8,10},{9,11},{10,... | collective-permute-start | bytes 983048 | tf_op jit(solution)/shard_map/ppermute | solution.py:400
  65.2 7.0 %collective-permute-start.16 = (bf16[128,1280]{1,0:T(8,128)(2,1)S(1)}, bf16[128,1280]{1,0:T(8,128)(2,1)S(1)}, u32[]{:S(2)}, u32[]{:S(2)}) collective-permute-start(bf16[128,1280]{1,0:T(8,128)(2,1)S(1)} %collective-permute-done.10.refs_4_), channel_id=1, source_target_pairs={{0,1},{1,0},{2,3},{3,2},{4,5},{5,4},{6,7},{7,6},{8,9},{9,8},{10,11... | collective-permute-start | bytes 983048 | tf_op jit(solution)/shard_map/ppermute | solution.py:400
  65.2 7.0 %collective-permute-start.17 = (bf16[128,1280]{1,0:T(8,128)(2,1)S(1)}, bf16[128,1280]{1,0:T(8,128)(2,1)S(1)}, u32[]{:S(2)}, u32[]{:S(2)}) collective-permute-start(bf16[128,1280]{1,0:T(8,128)(2,1)S(1)} %collective-permute-done.9.refs_5_), channel_id=1, source_target_pairs={{0,1},{1,0},{2,3},{3,2},{4,5},{5,4},{6,7},{7,6},{8,9},{9,8},{10,11... | collective-permute-start | bytes 983048 | tf_op jit(solution)/shard_map/ppermute | solution.py:400
  65.7 13.1 %collective-permute-start.15 = (bf16[128,1280]{1,0:T(8,128)(2,1)S(1)}, bf16[128,1280]{1,0:T(8,128)(2,1)S(1)}, u32[]{:S(2)}, u32[]{:S(2)}) collective-permute-start(bf16[128,1280]{1,0:T(8,128)(2,1)S(1)} %collective-permute-done.9.refs_5_), channel_id=1, source_target_pairs={{0,2},{1,3},{2,0},{3,1},{4,6},{5,7},{6,4},{7,5},{8,10},{9,11},{10,... | collective-permute-start | bytes 983048 | tf_op jit(solution)/shard_map/ppermute | solution.py:400
  72.2 6.6 %collective-permute-start.19 = (bf16[128,1280]{1,0:T(8,128)(2,1)S(1)}, bf16[128,1280]{1,0:T(8,128)(2,1)S(1)}, u32[]{:S(2)}, u32[]{:S(2)}) collective-permute-start(bf16[128,1280]{1,0:T(8,128)(2,1)S(1)} %collective-permute-done.18.refs_0_), channel_id=1, source_target_pairs={{0,1},{1,0},{2,3},{3,2},{4,5},{5,4},{6,7},{7,6},{8,9},{9,8},{10,11... | collective-permute-start | bytes 983048 | tf_op jit(solution)/shard_map/ppermute | solution.py:400
  78.8 7.1 %copy-start.3 = (s32[256]{0:T(256)S(1)}, s32[256]{0:T(256)}, u32[]{:S(2)}) copy-start(s32[256]{0:T(256)} %param.11) | copy-start | bytes 3076
  78.8 1.6 %collective-permute-start.20 = (bf16[128,1280]{1,0:T(8,128)(2,1)S(1)}, bf16[128,1280]{1,0:T(8,128)(2,1)S(1)}, u32[]{:S(2)}, u32[]{:S(2)}) collective-permute-start(bf16[128,1280]{1,0:T(8,128)(2,1)S(1)} %collective-permute-done.15.refs_1_), channel_id=1, source_target_pairs={{0,1},{1,0},{2,3},{3,2},{4,5},{5,4},{6,7},{7,6},{8,9},{9,8},{10,11... | collective-permute-start | bytes 983048 | tf_op jit(solution)/shard_map/ppermute | solution.py:400
